TPU v7x, 32 devices: a whole 2x2x4 slice. The times are simulated.
32 devices in a mesh: dp: 4 (over y, x), fsdp: 8 (over z, core).
Axes of the slice: x: 2, y: 2, z: 4, core: 2. Of those that a mesh axis runs over, the one named last changes fastest.
Arguments:
- pixels: bfloat16 [32768, 3072], P(('dp', 'fsdp')), may hold values from -6 to 6
- segment: int32 [32768], P(('dp', 'fsdp')), may hold values from 0 to 8, as said below
- patch_size: int32 [32, 8], P(('dp', 'fsdp')), may hold values from 8 to 48, as said below
- labels: int32 [32, 8], P(('dp', 'fsdp')), may hold values from 0 to 999
- patch_kernel: float32 [3072, 768], P('fsdp'), may hold values from -0.109375 to 0.109375
- head_weight: float32 [768, 1000], P('fsdp'), may hold values from -0.21875 to 0.21875
- input_proj: float32 [2, 768, 5376], P(None, 'fsdp'), may hold values from -0.21875 to 0.21875
- output_proj: float32 [2, 3840, 768], P(None, 'fsdp')
- layer_vector: float32 [2, 9984], P(None, 'fsdp')
- position_table: float32 [49, 768], replicated, may hold values from -0.625 to 0.625
- global_vector: float32 [3304], replicated
- patch_moment: float32 [3072, 768], P('fsdp')
- head_moment: float32 [768, 1000], P('fsdp')
- input_moment: float32 [2, 768, 5376], P(None, 'fsdp')
- output_moment: float32 [2, 3840, 768], P(None, 'fsdp')
- layer_moment: float32 [2, 9984], P(None, 'fsdp')
- position_moment: float32 [49, 768], replicated
- global_moment: float32 [3304], replicated
- patch_square: float32 [3072, 768], P('fsdp')
- head_square: float32 [768, 1000], P('fsdp')
- input_square: float32 [2, 768, 5376], P(None, 'fsdp')
- output_square: float32 [2, 3840, 768], P(None, 'fsdp')
- layer_square: float32 [2, 9984], P(None, 'fsdp')
- position_square: float32 [49, 768], replicated
- global_square: float32 [3304], replicated
Outputs:
- loss_sum: float32 [], replicated
- token_total: float32 [], replicated
- grad_norm: float32 [], replicated
- next_patch_moment: float32 [3072, 768], P('fsdp')
- next_head_moment: float32 [768, 1000], P('fsdp')
- next_input_moment: float32 [2, 768, 5376], P(None, 'fsdp')
- next_output_moment: float32 [2, 3840, 768], P(None, 'fsdp')
- next_layer_moment: float32 [2, 9984], P(None, 'fsdp')
- next_position_moment: float32 [49, 768], replicated
- next_global_moment: float32 [3304], replicated
- next_patch_square: float32 [3072, 768], P('fsdp')
- next_head_square: float32 [768, 1000], P('fsdp')
- next_input_square: float32 [2, 768, 5376], P(None, 'fsdp')
- next_output_square: float32 [2, 3840, 768], P(None, 'fsdp')
- next_layer_square: float32 [2, 9984], P(None, 'fsdp')
- next_position_square: float32 [49, 768], replicated
- next_global_square: float32 [3304], replicated
- next_patch_kernel: float32 [3072, 768], P('fsdp')
- next_head_weight: float32 [768, 1000], P('fsdp')
- next_input_proj: float32 [2, 768, 5376], P(None, 'fsdp')
- next_output_proj: float32 [2, 3840, 768], P(None, 'fsdp')
- next_layer_vector: float32 [2, 9984], P(None, 'fsdp')
- next_position_table: float32 [49, 768], replicated
- next_global_vector: float32 [3304], replicated
Inputs may be any that keep to these rules, and one draw needn't show every extreme that they name: `patch_size`: each entry is one of 8, 10, 12, 15, 16, 20, 24, 30, 40, 48, all divisors of 240. `segment`: within each row of 1024 tokens (the tokens of one device), the slots that the row holds come in increasing order from the row's first token, each as one run of (240 / its patch size)^2 tokens; slot 0 is always held; the tokens after the last run have the value 8.
All inputs are finite; a program needn't handle non-finite values.
Results may differ from a plain program's by a relative error of at most 0.035.
Values may be sent and summed in bfloat16 or wider, within the bound.
A program may use at most 384 MiB of HBM per device.

v0:
```python
import jax
import jax.numpy as jnp
from jax import lax
from jax.sharding import PartitionSpec as P

D = 768
HEADS = 12
HD = 64
CLS = 1000
GRID = 7
IMG = 240
IMGS = 8
LAYERS = 2
STEP = 3


NORM_EPS = 1e-06
CLIP_NORM = 0.01
LEARN_RATE = 0.05
VECTOR_RATE = 0.25
BETA_ONE = 0.5
BETA_TWO = 0.5
ADAM_EPS = 1e-08
WEIGHT_DECAY = 0.05
HIGHEST = lax.Precision.HIGHEST


def layer_norm(values, gain, shift):
    center = values - jnp.mean(values, -1, keepdims=True)
    spread = jnp.mean(center * center, -1, keepdims=True)
    return center * lax.rsqrt(spread + NORM_EPS) * gain + shift


def rounded(values):
    return lax.optimization_barrier(values.astype(jnp.bfloat16)).astype(jnp.float32)


def column_total(rows):
    return jnp.sum(rows.astype(jnp.float32), 0)


def matmul(left, right):
    return jnp.dot(left, right, preferred_element_type=jnp.float32)


def split_heads(rows):
    return rows.reshape(rows.shape[0], HEADS, HD)


def row_layout(seg_row, patch_row):
    row_count = seg_row.shape[0]
    slots = jnp.arange(IMGS, dtype=jnp.int32)
    member = seg_row[:, None] == slots[None, :]
    counts = jnp.sum(member.astype(jnp.int32), 0, dtype=jnp.int32)
    starts = jnp.cumsum(counts, dtype=jnp.int32) - counts
    inside = jnp.any(member, 1)
    offset = jnp.arange(row_count, dtype=jnp.int32) - jnp.sum(
        jnp.where(member, starts[None, :], 0), 1, dtype=jnp.int32
    )
    offset = jnp.where(inside, offset, 0)
    patch_tok = jnp.sum(jnp.where(member, patch_row[None, :], 0), 1, dtype=jnp.int32) + jnp.where(
        inside, 0, IMG
    )
    side = IMG // patch_tok
    nodes = jnp.arange(GRID, dtype=jnp.int32).astype(jnp.float32)

    def hat(coord):
        place = ((2 * coord + 1) * GRID).astype(jnp.float32) / (2 * side).astype(jnp.float32) - 0.5
        place = jnp.clip(place, 0.0, GRID - 1.0)
        return jnp.maximum(1.0 - jnp.abs(place[:, None] - nodes[None, :]), 0.0)

    weights = (hat(offset // side)[:, :, None] * hat(offset % side)[:, None, :]).reshape(
        row_count, GRID * GRID
    )
    return (weights, member.astype(jnp.float32), counts.astype(jnp.float32))


def attention_scores(query_block, key_rows, seg_block, seg_row):
    score_scale = query_block.shape[-1] ** (-0.5)
    scores = (
        jnp.einsum("qhd,khd->hqk", query_block, key_rows, preferred_element_type=jnp.float32)
        * score_scale
    )
    return jnp.where((seg_block[:, None] == seg_row[None, :])[None], scores, -1e30)


def attention_forward(queries, key_rows, values, seg_row):
    row_count = seg_row.shape[0]
    block_rows = min(512, row_count)

    def one_block(block_index):
        first_row = block_index * block_rows
        query_block = lax.dynamic_slice_in_dim(queries, first_row, block_rows, 0)
        seg_block = lax.dynamic_slice_in_dim(seg_row, first_row, block_rows, 0)
        scores = attention_scores(query_block, key_rows, seg_block, seg_row)
        highest = jnp.max(scores, -1, keepdims=True)
        exponent = jnp.exp(scores - highest)
        totals = jnp.sum(exponent, -1, keepdims=True)
        probabilities = (exponent / totals).astype(jnp.bfloat16)
        output = jnp.einsum(
            "hqk,khd->qhd", probabilities, values, preferred_element_type=jnp.float32
        )
        return (output.astype(jnp.bfloat16), (highest + jnp.log(totals))[:, :, 0])

    outputs, log_totals = lax.map(one_block, jnp.arange(row_count // block_rows))
    return (outputs.reshape(row_count, HEADS * HD), log_totals)


def attention_backward(queries, key_rows, values, seg_row, log_totals, attended_grad):
    row_count = seg_row.shape[0]
    block_rows = min(512, row_count)
    score_scale = queries.shape[-1] ** (-0.5)

    def one_block(running, block_index):
        key_grad, value_grad = running
        first_row = block_index * block_rows
        query_block = lax.dynamic_slice_in_dim(queries, first_row, block_rows, 0)
        seg_block = lax.dynamic_slice_in_dim(seg_row, first_row, block_rows, 0)
        grad_block = lax.dynamic_slice_in_dim(attended_grad, first_row, block_rows, 0)
        scores = attention_scores(query_block, key_rows, seg_block, seg_row)
        probabilities = jnp.exp(scores - log_totals[block_index][:, :, None])
        probs_grad = jnp.einsum(
            "qhd,khd->hqk", grad_block, values, preferred_element_type=jnp.float32
        )
        row_inner = jnp.sum(probabilities * probs_grad, -1, keepdims=True)
        scores_grad = (probabilities * (probs_grad - row_inner)).astype(jnp.bfloat16)
        query_grad = (
            jnp.einsum("hqk,khd->qhd", scores_grad, key_rows, preferred_element_type=jnp.float32)
            * score_scale
        )
        key_grad = (
            key_grad
            + jnp.einsum(
                "hqk,qhd->khd", scores_grad, query_block, preferred_element_type=jnp.float32
            )
            * score_scale
        )
        value_grad = value_grad + jnp.einsum(
            "hqk,qhd->khd",
            probabilities.astype(jnp.bfloat16),
            grad_block,
            preferred_element_type=jnp.float32,
        )
        return ((key_grad, value_grad), query_grad)

    zero_grad = jnp.zeros(key_rows.shape, jnp.float32)
    (key_grad, value_grad), query_grad = lax.scan(
        one_block, (zero_grad, zero_grad), jnp.arange(row_count // block_rows)
    )
    return (
        query_grad.reshape(row_count, -1),
        key_grad.reshape(row_count, -1),
        value_grad.reshape(row_count, -1),
    )


def layer_forward(stream, weights, seg_row):
    proj_in, proj_out, vector_low = weights
    vector = vector_low.astype(jnp.float32)
    normed = layer_norm(stream, vector[0:D], vector[D : 2 * D]).astype(jnp.bfloat16)
    qkv_rows = (matmul(normed, proj_in[:, : 3 * D]) + vector[4 * D : 7 * D]).astype(jnp.bfloat16)
    attended, log_totals = attention_forward(
        split_heads(qkv_rows[:, :D]),
        split_heads(qkv_rows[:, D : 2 * D]),
        split_heads(qkv_rows[:, 2 * D :]),
        seg_row,
    )
    residual = stream + matmul(attended, proj_out[:D]) + vector[7 * D : 8 * D]
    normed_second = layer_norm(residual, vector[2 * D : 3 * D], vector[3 * D : 4 * D]).astype(
        jnp.bfloat16
    )
    hidden = matmul(normed_second, proj_in[:, 3 * D :]) + vector[9 * D :]
    active = jax.nn.gelu(hidden).astype(jnp.bfloat16)
    output = residual + matmul(active, proj_out[D:]) + vector[8 * D : 9 * D]
    return (output, (stream, qkv_rows, attended, log_totals, residual, hidden))


def layer_backward(grad_stream, weights, layer_saved, seg_row):
    proj_in, proj_out, vector_low = weights
    vector = vector_low.astype(jnp.float32)
    stream, qkv_rows, attended, log_totals, residual, hidden = layer_saved
    grad_low = grad_stream.astype(jnp.bfloat16)
    normed_second, second_back = jax.vjp(
        layer_norm, residual, vector[2 * D : 3 * D], vector[3 * D : 4 * D]
    )
    normed_second = normed_second.astype(jnp.bfloat16)
    active, gelu_back = jax.vjp(jax.nn.gelu, hidden)
    active = active.astype(jnp.bfloat16)
    down_grad = matmul(active.T, grad_low)
    active_grad = matmul(grad_low, proj_out[D:].T)
    hidden_grad = gelu_back(active_grad)[0].astype(jnp.bfloat16)
    up_grad = matmul(normed_second.T, hidden_grad)
    second_grad = matmul(hidden_grad, proj_in[:, 3 * D :].T)
    residual_grad, gain_second, shift_second = second_back(second_grad)
    residual_grad = residual_grad + grad_stream
    residual_low = residual_grad.astype(jnp.bfloat16)
    mixing_grad = matmul(attended.T, residual_low)
    attended_grad = matmul(residual_low, proj_out[:D].T).astype(jnp.bfloat16)
    query_grad, key_grad, value_grad = attention_backward(
        split_heads(qkv_rows[:, :D]),
        split_heads(qkv_rows[:, D : 2 * D]),
        split_heads(qkv_rows[:, 2 * D :]),
        seg_row,
        log_totals,
        split_heads(attended_grad),
    )
    qkv_grad = jnp.concatenate([query_grad, key_grad, value_grad], 1).astype(jnp.bfloat16)
    normed, first_back = jax.vjp(layer_norm, stream, vector[0:D], vector[D : 2 * D])
    project_grad = matmul(normed.astype(jnp.bfloat16).T, qkv_grad)
    normed_grad = matmul(qkv_grad, proj_in[:, : 3 * D].T)
    stream_grad, gain_first, shift_first = first_back(normed_grad)
    vector_grad = jnp.concatenate(
        [
            gain_first,
            shift_first,
            gain_second,
            shift_second,
            column_total(qkv_grad),
            column_total(residual_low),
            column_total(grad_low),
            column_total(hidden_grad),
        ]
    )
    return (
        residual_grad + stream_grad,
        (
            jnp.concatenate([project_grad, up_grad], 1),
            jnp.concatenate([mixing_grad, down_grad], 0),
            vector_grad,
        ),
    )


def adam_update(gradient, moment, square, weight, factor, learn_rate):
    clipped = gradient * factor
    moment = BETA_ONE * moment + (1.0 - BETA_ONE) * clipped
    square = BETA_TWO * square + (1.0 - BETA_TWO) * clipped * clipped
    fixed_one = 1.0 - BETA_ONE**STEP
    fixed_two = 1.0 - BETA_TWO**STEP
    step_dir = (
        moment / fixed_one / (jnp.sqrt(square / fixed_two) + ADAM_EPS) + WEIGHT_DECAY * weight
    )
    return (moment, square, weight - learn_rate * step_dir)


def body(
    pixels,
    segment,
    patch_size,
    labels,
    patch_kernel,
    head_weight,
    input_proj,
    output_proj,
    layer_vector,
    position_table,
    global_vector,
    patch_moment,
    head_moment,
    input_moment,
    output_moment,
    layer_moment,
    position_moment,
    global_moment,
    patch_square,
    head_square,
    input_square,
    output_square,
    layer_square,
    position_square,
    global_square,
):
    pos_weights, member, counts = row_layout(segment, patch_size[0])
    token_total = lax.psum(jnp.sum(counts), ("dp", "fsdp"))
    kernel_full, head_full = (
        lax.all_gather(patch_kernel.astype(jnp.bfloat16), "fsdp", axis=0, tiled=True),
        lax.all_gather(head_weight.astype(jnp.bfloat16), "fsdp", axis=0, tiled=True),
    )
    global_low = rounded(global_vector)
    position_low = rounded(position_table)
    embed_pre = matmul(pixels, kernel_full) + global_low[:D]
    stream = embed_pre + jnp.dot(pos_weights, position_low, precision=HIGHEST)
    gathered = []
    saved_layers = []
    for depth_index in range(LAYERS):
        weights = (
            lax.all_gather(
                input_proj[depth_index].astype(jnp.bfloat16), "fsdp", axis=0, tiled=True
            ),
            lax.all_gather(
                output_proj[depth_index].astype(jnp.bfloat16), "fsdp", axis=0, tiled=True
            ),
            lax.all_gather(
                layer_vector[depth_index].astype(jnp.bfloat16), "fsdp", axis=0, tiled=True
            ),
        )
        stream, layer_saved = layer_forward(stream, weights, segment)
        gathered.append(weights)
        saved_layers.append(layer_saved)
    final_norm, final_back = jax.vjp(
        layer_norm, stream, global_low[D : 2 * D], global_low[2 * D : 3 * D]
    )
    image_sizes = jnp.maximum(counts, 1.0)
    pooled = (jnp.dot(member.T, final_norm, precision=HIGHEST) / image_sizes[:, None]).astype(
        jnp.bfloat16
    )
    logits = matmul(pooled, head_full) + global_low[3 * D :]
    highest = jnp.max(logits, -1, keepdims=True)
    exponent = jnp.exp(logits - highest)
    totals = jnp.sum(exponent, -1, keepdims=True)
    logsum = (highest + jnp.log(totals))[:, 0]
    onehot = labels[0][:, None] == jnp.arange(CLS, dtype=jnp.int32)[None, :]
    picked = jnp.sum(jnp.where(onehot, logits, 0.0), 1)
    loss_local = jnp.sum(counts * (logsum - picked))
    logits_grad = (
        (exponent / totals - onehot.astype(jnp.float32)) * (counts / token_total)[:, None]
    ).astype(jnp.bfloat16)
    head_grad = matmul(pooled.T, logits_grad)
    pooled_grad = matmul(logits_grad, head_full.T)
    final_grad = jnp.dot(member, pooled_grad / image_sizes[:, None], precision=HIGHEST)
    stream_grad, final_gain, final_shift = final_back(final_grad)
    layer_parts = []
    for depth_index in reversed(range(LAYERS)):
        weights = (
            lax.all_gather(
                input_proj[depth_index].astype(jnp.bfloat16), "fsdp", axis=0, tiled=True
            ),
            lax.all_gather(
                output_proj[depth_index].astype(jnp.bfloat16), "fsdp", axis=0, tiled=True
            ),
            lax.all_gather(
                layer_vector[depth_index].astype(jnp.bfloat16), "fsdp", axis=0, tiled=True
            ),
        )
        stream_grad, partial_value = layer_backward(
            stream_grad, weights, saved_layers[depth_index], segment
        )
        shards = (
            lax.psum_scatter(
                partial_value[0].astype(jnp.bfloat16), "fsdp", scatter_dimension=0, tiled=True
            ).astype(jnp.float32),
            lax.psum_scatter(
                partial_value[1].astype(jnp.bfloat16), "fsdp", scatter_dimension=0, tiled=True
            ).astype(jnp.float32),
            lax.psum_scatter(
                partial_value[2].astype(jnp.bfloat16), "fsdp", scatter_dimension=0, tiled=True
            ).astype(jnp.float32),
        )
        shards = (
            lax.psum(shards[0].astype(jnp.bfloat16), "dp").astype(jnp.float32),
            lax.psum(shards[1].astype(jnp.bfloat16), "dp").astype(jnp.float32),
            lax.psum(shards[2].astype(jnp.bfloat16), "dp").astype(jnp.float32),
        )
        layer_parts.insert(0, shards)
    embed_low = stream_grad.astype(jnp.bfloat16)
    kernel_grad = matmul(pixels.T, embed_low)
    position_grad = jnp.dot(pos_weights.T, stream_grad, precision=HIGHEST)
    input_part = jnp.stack([item[0] for item in layer_parts])
    output_part = jnp.stack([item[1] for item in layer_parts])
    vector_part = jnp.stack([item[2] for item in layer_parts])
    kernel_sum, head_sum = (
        lax.psum_scatter(
            kernel_grad.astype(jnp.bfloat16), "fsdp", scatter_dimension=0, tiled=True
        ).astype(jnp.float32),
        lax.psum_scatter(
            head_grad.astype(jnp.bfloat16), "fsdp", scatter_dimension=0, tiled=True
        ).astype(jnp.float32),
    )
    kernel_sum, head_sum = (
        lax.psum(kernel_sum.astype(jnp.bfloat16), "dp").astype(jnp.float32),
        lax.psum(head_sum.astype(jnp.bfloat16), "dp").astype(jnp.float32),
    )
    input_sum, output_sum, vector_sum = (input_part, output_part, vector_part)
    global_grad = jnp.concatenate(
        [column_total(embed_low), final_gain, final_shift, column_total(logits_grad)]
    )
    position_sum, global_sum, loss_sum = lax.psum(
        (position_grad, global_grad, loss_local), ("dp", "fsdp")
    )
    local_squares = sum(
        (jnp.sum(item * item) for item in (kernel_sum, head_sum, input_sum, output_sum, vector_sum))
    )
    shard_squares = lax.psum(local_squares, "fsdp")
    grad_norm = jnp.sqrt(
        shard_squares + jnp.sum(position_sum * position_sum) + jnp.sum(global_sum * global_sum)
    )
    factor = jnp.minimum(1.0, CLIP_NORM / grad_norm)
    patch_next = adam_update(
        kernel_sum, patch_moment, patch_square, patch_kernel, factor, LEARN_RATE
    )
    head_next = adam_update(head_sum, head_moment, head_square, head_weight, factor, LEARN_RATE)
    input_next = adam_update(input_sum, input_moment, input_square, input_proj, factor, LEARN_RATE)
    output_next = adam_update(
        output_sum, output_moment, output_square, output_proj, factor, LEARN_RATE
    )
    layer_next = adam_update(
        vector_sum, layer_moment, layer_square, layer_vector, factor, VECTOR_RATE
    )
    position_next = adam_update(
        position_sum, position_moment, position_square, position_table, factor, LEARN_RATE
    )
    global_next = adam_update(
        global_sum, global_moment, global_square, global_vector, factor, VECTOR_RATE
    )
    return (
        loss_sum,
        token_total,
        grad_norm,
        patch_next[0],
        head_next[0],
        input_next[0],
        output_next[0],
        layer_next[0],
        position_next[0],
        global_next[0],
        patch_next[1],
        head_next[1],
        input_next[1],
        output_next[1],
        layer_next[1],
        position_next[1],
        global_next[1],
        patch_next[2],
        head_next[2],
        input_next[2],
        output_next[2],
        layer_next[2],
        position_next[2],
        global_next[2],
    )


def solution(mesh):
    in_specs = (
        P(("dp", "fsdp"), None),
        P(("dp", "fsdp")),
        P(("dp", "fsdp"), None),
        P(("dp", "fsdp"), None),
        P("fsdp", None),
        P("fsdp", None),
        P(None, "fsdp", None),
        P(None, "fsdp", None),
        P(None, "fsdp"),
        P(),
        P(),
        P("fsdp", None),
        P("fsdp", None),
        P(None, "fsdp", None),
        P(None, "fsdp", None),
        P(None, "fsdp"),
        P(),
        P(),
        P("fsdp", None),
        P("fsdp", None),
        P(None, "fsdp", None),
        P(None, "fsdp", None),
        P(None, "fsdp"),
        P(),
        P(),
    )
    out_specs = (
        P(),
        P(),
        P(),
        P("fsdp", None),
        P("fsdp", None),
        P(None, "fsdp", None),
        P(None, "fsdp", None),
        P(None, "fsdp"),
        P(),
        P(),
        P("fsdp", None),
        P("fsdp", None),
        P(None, "fsdp", None),
        P(None, "fsdp", None),
        P(None, "fsdp"),
        P(),
        P(),
        P("fsdp", None),
        P("fsdp", None),
        P(None, "fsdp", None),
        P(None, "fsdp", None),
        P(None, "fsdp"),
        P(),
        P(),
    )
    return jax.shard_map(body, mesh=mesh, in_specs=in_specs, out_specs=out_specs, check_vma=False)
```

profile of v0, /device:TPU:0, one launch (start us, length us, event | category | flops | bytes accessed | tf_op | source)
XLA Modules:
  0.0 1684.8 jit_solution(4344751197061849298)
XLA Ops:
  21.2 32.3 %all-reduce.6 = (bf16[9984]{0:T(1024)(128)(2,1)S(1)}, bf16[9984]{0:T(1024)(128)(2,1)S(1)}) all-reduce(bf16[9984]{0:T(1024)(128)(2,1)S(1)} %dynamic-update-slice, bf16[9984]{0:T(1024)(128)(2,1)S(1)} %dynamic-update-slice.1), channel_id=2, replica_groups=mesh['dp'=4,'fsdp'=8] {'fsdp'}, use_global_device_ids=true, to_apply=%add | all-reduce | flops 19968 | bytes 79872
  65.7 8.6 fusion.190
  76.5 71.4 %all-gather.17.cloned.1.call-done = bf16[1,768,5376]{2,1,0:T(8,128)(2,1)} async-done(((bf16[1,96,5376]{2,1,0:T(8,128)(2,1)}), bf16[1,768,5376]{2,1,0:T(8,128)(2,1)}) %all-gather.17.cloned.1.call-update) | async-done | bytes 8257552 | tf_op jit(solution)/shard_map/all_gather | solution.py:287
  163.3 75.0 %while.54 = (s32[]{:T(128)}, bf16[2,512,12,64]{1,3,2,0:T(8,128)(2,1)}, f32[2,12,512]{2,1,0:T(8,128)S(1)}, s32[2]{0:T(128)S(1)}, s32[1024]{0:T(1024)S(1)}, /*inde...) while((s32[]{:T(128)}, ...), condition=%wide.region_10.11_spmd, body=%wide.region_7.10_spmd.sunk | while | flops 1687021568 | bytes 189499632 | solution.py:105
  165.2 10.9 fusion.263
  176.1 12.4 fusion.264
  202.2 10.7 fusion.263
  212.9 13.0 fusion.264
  249.6 9.0 fusion.83
  258.6 11.2 fusion.181
  270.3 21.6 %all-gather.21.cloned.1.call-done = bf16[1,768,5376]{2,1,0:T(8,128)(2,1)} async-done(((bf16[1,96,5376]{2,1,0:T(8,128)(2,1)}), bf16[1,768,5376]{2,1,0:T(8,128)(2,1)}) %all-gather.21.cloned.1.call-update) | async-done | bytes 8257552 | tf_op jit(solution)/shard_map/all_gather | solution.py:287
  307.5 73.9 %while.55 = (s32[]{:T(128)}, bf16[2,512,12,64]{1,3,2,0:T(8,128)(2,1)}, f32[2,12,512]{2,1,0:T(8,128)S(1)}, s32[2]{0:T(128)S(1)}, s32[1024]{0:T(1024)S(1)}, /*inde...) while((s32[]{:T(128)}, ...), condition=%wide.region_18.19_spmd, body=%wide.region_15.18_spmd.sunk | while | flops 1687021568 | bytes 189499632 | solution.py:105
  309.3 10.9 fusion.268
  320.2 12.4 fusion.269
  346.3 10.7 fusion.268
  357.1 12.4 fusion.269
  391.4 8.9 fusion.79
  400.4 11.1 fusion.183
  417.9 39.1 %psum.92 = f32[]{:T(128)} all-reduce(f32[]{:T(128)} %get-tuple-element.472), channel_id=1, replica_groups=mesh['dp'=4,'fsdp'=8] {'dp','fsdp'}, use_global_device_ids=true, to_apply=%region_29.30 | all-reduce | flops 1 | bytes 8 | tf_op jit(solution)/shard_map/psum | solution.py:274
  476.5 17.9 %fusion.166 = (bf16[3072]{0:T(1024)(128)(2,1)}, bf16[1024,3072]{1,0:T(8,128)(2,1)}) fusion(f32[1024,3072]{1,0:T(8,128)} %fusion.79, f32[3072]{0:T(1024)S(1)} %bitcast.266, bf16[1024,768]{0,1:T(8,128)(2,1)S(1)} %get-tuple-element.596, bf16[1,3840,768]{2,1,0:T(8,128)(2,1)S(1)} %bitcast.293), kind=kOutput, calls=%fused_computation.343 | convolution fusion | flops 4901041152 | bytes 25184256 | tf_op jit(solution)/shard_map/dot_general | solution.py:43
  494.3 9.0 fusion.187
  521.4 174.3 %while.56 = (s32[]{:T(128)}, f32[1024,12,64]{0,2,1:T(8,128)}, f32[1024,12,64]{0,2,1:T(8,128)}, bf16[2,512,12,64]{1,3,2,0:T(8,128)(2,1)}, s32[2]{0:T(128)S(1)}, /...) while((s32[]{:T(128)}, f32[1024,12,64]{0,2,1:T(8,128)}, ...), condition=%wide.region_36.37_spmd.clone, body=%wide.region_34.36_spmd.clone.sunk | while | flops 4125747200 | bytes 231926128 | solution.py:147
  525.3 11.5 fusion.280
  536.8 13.3 bitcast_add_fusion.9
  550.1 18.1 %multiply_reduce_fusion.22 = (f32[12,512]{1,0:T(8,128)S(1)}, f32[12,512,1024]{2,1,0:T(8,128)}) fusion(f32[12,512,1024]{2,1,0:T(8,128)} %fusion.280, f32[12,512]{1,0:T(8,128)S(1)} %dynamic-slice_bitcast_fusion.4, pred[512,1024]{1,0:T(8,128)(4,1)S(1)} %broadcast_compare_fusion.10, bf16[1024,12,64]{0,2,1:T(8,128)(2,1)} %get-tuple-element.1020, ...), kind=kOutput, calls=%fused_computation.33.clone.1 | convolution fusion | flops 836757504 | bytes 53264388 | tf_op jit(solution)/shard_map/while/body/eval_jaxpr/qhd,khd->hqk/dot_general | solution.py:122
  568.2 21.2 %multiply_convert_fusion.12 = bf16[12,512,1024]{2,1,0:T(8,128)(2,1)} fusion(f32[12,512,1024]{2,1,0:T(8,128)} %get-tuple-element.891, f32[12,512,1024]{2,1,0:T(8,128)} %fusion.280, f32[12,512]{1,0:T(8,128)S(1)} %get-tuple-element.892, f32[12,512]{1,0:T(8,128)S(1)} %dynamic-slice_bitcast_fusion.4, pred[512,1024]{1,0:T(8,128)(4,1)S(1)} %broadcast_compare_fusion.10), kind=kLoop, calls=%fused_computation.32.clone.1 | loop fusion | flops 37748736 | bytes 63488000 | tf_op jit(solution)/shard_map/while/body/eval_jaxpr/convert_element_type | solution.py:126
  589.4 9.5 bitcast_dynamic-update-slice_fusion.10
  598.9 8.6 bitcast_add_fusion.8
  611.3 11.5 fusion.280
  622.7 14.3 bitcast_add_fusion.9
  637.0 18.1 %multiply_reduce_fusion.22 = (f32[12,512]{1,0:T(8,128)S(1)}, f32[12,512,1024]{2,1,0:T(8,128)}) fusion(f32[12,512,1024]{2,1,0:T(8,128)} %fusion.280, f32[12,512]{1,0:T(8,128)S(1)} %dynamic-slice_bitcast_fusion.4, pred[512,1024]{1,0:T(8,128)(4,1)S(1)} %broadcast_compare_fusion.10, bf16[1024,12,64]{0,2,1:T(8,128)(2,1)} %get-tuple-element.1020, ...), kind=kOutput, calls=%fused_computation.33.clone.1 | convolution fusion | flops 836757504 | bytes 53264388 | tf_op jit(solution)/shard_map/while/body/eval_jaxpr/qhd,khd->hqk/dot_general | solution.py:122
  655.1 21.2 %multiply_convert_fusion.12 = bf16[12,512,1024]{2,1,0:T(8,128)(2,1)} fusion(f32[12,512,1024]{2,1,0:T(8,128)} %get-tuple-element.891, f32[12,512,1024]{2,1,0:T(8,128)} %fusion.280, f32[12,512]{1,0:T(8,128)S(1)} %get-tuple-element.892, f32[12,512]{1,0:T(8,128)S(1)} %dynamic-slice_bitcast_fusion.4, pred[512,1024]{1,0:T(8,128)(4,1)S(1)} %broadcast_compare_fusion.10), kind=kLoop, calls=%fused_computation.32.clone.1 | loop fusion | flops 37748736 | bytes 63488000 | tf_op jit(solution)/shard_map/while/body/eval_jaxpr/convert_element_type | solution.py:126
  676.3 9.5 bitcast_dynamic-update-slice_fusion.10
  685.8 9.5 bitcast_add_fusion.8
  702.6 8.7 fusion.186
  722.3 17.7 %fusion.162 = (bf16[3072]{0:T(1024)(128)(2,1)}, bf16[1024,3072]{1,0:T(8,128)(2,1)}) fusion(f32[1024,3072]{1,0:T(8,128)} %fusion.83, f32[3072]{0:T(1024)S(1)} %bitcast.263, bf16[1024,768]{0,1:T(8,128)(2,1)S(1)} %get-tuple-element.590, bf16[1,3840,768]{2,1,0:T(8,128)(2,1)S(1)} %bitcast.291), kind=kOutput, calls=%fused_computation.341 | convolution fusion | flops 4901041152 | bytes 25184256 | tf_op jit(solution)/shard_map/dot_general | solution.py:43
  740.0 8.9 fusion.189
  766.7 174.0 %while.57 = (s32[]{:T(128)}, f32[1024,12,64]{0,2,1:T(8,128)}, f32[1024,12,64]{0,2,1:T(8,128)}, bf16[2,512,12,64]{1,3,2,0:T(8,128)(2,1)}, s32[2]{0:T(128)S(1)}, /...) while((s32[]{:T(128)}, f32[1024,12,64]{0,2,1:T(8,128)}, ...), condition=%wide.region_43.44_spmd.clone, body=%wide.region_41.43_spmd.clone.sunk | while | flops 4125747200 | bytes 225634640 | solution.py:147
  770.5 11.5 fusion.290
  782.0 13.3 bitcast_add_fusion.11
  795.3 18.1 %multiply_reduce_fusion.23 = (f32[12,512]{1,0:T(8,128)S(1)}, f32[12,512,1024]{2,1,0:T(8,128)}) fusion(f32[12,512,1024]{2,1,0:T(8,128)} %fusion.290, f32[12,512]{1,0:T(8,128)S(1)} %dynamic-slice_bitcast_fusion.5, pred[512,1024]{1,0:T(8,128)(4,1)S(1)} %broadcast_compare_fusion.11, bf16[1024,12,64]{0,2,1:T(8,128)(2,1)} %get-tuple-element.1068, ...), kind=kOutput, calls=%fused_computation.56.clone.1 | convolution fusion | flops 836757504 | bytes 53264388 | tf_op jit(solution)/shard_map/while/body/eval_jaxpr/qhd,khd->hqk/dot_general | solution.py:122
  813.4 21.2 %multiply_convert_fusion.13 = bf16[12,512,1024]{2,1,0:T(8,128)(2,1)} fusion(f32[12,512,1024]{2,1,0:T(8,128)} %get-tuple-element.904, f32[12,512,1024]{2,1,0:T(8,128)} %fusion.290, f32[12,512]{1,0:T(8,128)S(1)} %get-tuple-element.905, f32[12,512]{1,0:T(8,128)S(1)} %dynamic-slice_bitcast_fusion.5, pred[512,1024]{1,0:T(8,128)(4,1)S(1)} %broadcast_compare_fusion.11), kind=kLoop, calls=%fused_computation.55.clone.1 | loop fusion | flops 37748736 | bytes 63488000 | tf_op jit(solution)/shard_map/while/body/eval_jaxpr/convert_element_type | solution.py:126
  834.6 9.5 bitcast_dynamic-update-slice_fusion.11
  856.3 11.5 fusion.290
  867.8 14.2 bitcast_add_fusion.11
  882.0 18.1 %multiply_reduce_fusion.23 = (f32[12,512]{1,0:T(8,128)S(1)}, f32[12,512,1024]{2,1,0:T(8,128)}) fusion(f32[12,512,1024]{2,1,0:T(8,128)} %fusion.290, f32[12,512]{1,0:T(8,128)S(1)} %dynamic-slice_bitcast_fusion.5, pred[512,1024]{1,0:T(8,128)(4,1)S(1)} %broadcast_compare_fusion.11, bf16[1024,12,64]{0,2,1:T(8,128)(2,1)} %get-tuple-element.1068, ...), kind=kOutput, calls=%fused_computation.56.clone.1 | convolution fusion | flops 836757504 | bytes 53264388 | tf_op jit(solution)/shard_map/while/body/eval_jaxpr/qhd,khd->hqk/dot_general | solution.py:122
  900.1 21.2 %multiply_convert_fusion.13 = bf16[12,512,1024]{2,1,0:T(8,128)(2,1)} fusion(f32[12,512,1024]{2,1,0:T(8,128)} %get-tuple-element.904, f32[12,512,1024]{2,1,0:T(8,128)} %fusion.290, f32[12,512]{1,0:T(8,128)S(1)} %get-tuple-element.905, f32[12,512]{1,0:T(8,128)S(1)} %dynamic-slice_bitcast_fusion.5, pred[512,1024]{1,0:T(8,128)(4,1)S(1)} %broadcast_compare_fusion.11), kind=kLoop, calls=%fused_computation.55.clone.1 | loop fusion | flops 37748736 | bytes 63488000 | tf_op jit(solution)/shard_map/while/body/eval_jaxpr/convert_element_type | solution.py:126
  921.4 9.5 bitcast_dynamic-update-slice_fusion.11
  930.9 9.5 bitcast_add_fusion.10
  947.6 8.7 fusion.188
  988.3 12.2 convolution_convert_fusion
  1007.6 11.7 convolution_convert_fusion.1
  1022.8 9.3 convolution_convert_fusion.5
  1032.2 9.9 convolution_convert_fusion.2
  1058.5 10.0 convolution_convert_fusion.3
  1076.8 61.0 %reduce-scatter.17.cloned.1.call-done = bf16[480,768]{1,0:T(8,128)(2,1)} async-done(((bf16[3840,768]{1,0:T(8,128)(2,1)}), bf16[480,768]{1,0:T(8,128)(2,1)}) %reduce-scatter.17.cloned.1.call-update) | async-done | bytes 737296 | tf_op jit(solution)/shard_map/reduce_scatter | solution.py:342
  1137.8 66.7 %reduce-scatter.15.cloned.1.call-done = bf16[480,768]{1,0:T(8,128)(2,1)} async-done(((bf16[3840,768]{1,0:T(8,128)(2,1)}), bf16[480,768]{1,0:T(8,128)(2,1)}) %reduce-scatter.15.cloned.1.call-update) | async-done | bytes 737296 | tf_op jit(solution)/shard_map/reduce_scatter | solution.py:342
  1204.6 89.1 %reduce-scatter.13.cloned.1.call-done = bf16[96,5376]{1,0:T(8,128)(2,1)} async-done(((bf16[768,5376]{1,0:T(8,128)(2,1)}), bf16[96,5376]{1,0:T(8,128)(2,1)}) %reduce-scatter.13.cloned.1.call-update) | async-done | bytes 1032208 | tf_op jit(solution)/shard_map/reduce_scatter | solution.py:339
  1293.6 89.0 %reduce-scatter.11.cloned.1.call-done = bf16[96,5376]{1,0:T(8,128)(2,1)} async-done(((bf16[768,5376]{1,0:T(8,128)(2,1)}), bf16[96,5376]{1,0:T(8,128)(2,1)}) %reduce-scatter.11.cloned.1.call-update) | async-done | bytes 1032208 | tf_op jit(solution)/shard_map/reduce_scatter | solution.py:339
  1391.8 38.8 %all-reduce.4 = (f32[]{:T(128)}, f32[3304]{0:T(1024)S(1)}) all-reduce(f32[]{:T(128)} %get-tuple-element.473, f32[3304]{0:T(1024)S(1)} %pad_maximum_fusion.8), channel_id=1, replica_groups=mesh['dp'=4,'fsdp'=8] {'dp','fsdp'}, use_global_device_ids=true, to_apply=%region_27.28 | all-reduce | flops 3305 | bytes 26440 | tf_op jit(solution)/shard_map/psum | solution.py:377
  1439.2 27.6 %all-reduce.5 = (bf16[9984]{0:T(1024)(128)(2,1)S(1)}, bf16[9984]{0:T(1024)(128)(2,1)S(1)}) all-reduce(bf16[9984]{0:T(1024)(128)(2,1)S(1)} %dynamic-update-slice.9, bf16[9984]{0:T(1024)(128)(2,1)S(1)} %dynamic-update-slice.17), channel_id=15, replica_groups=mesh['dp'=4,'fsdp'=8] {'fsdp'}, use_global_device_ids=true, to_apply=%region_80.81.clone | all-reduce | flops 19968 | bytes 79872
  1474.2 16.8 all-reduce.7
  1508.2 115.0 %all-reduce.12.cloned.1.call-done = f32[49,768]{1,0:T(8,128)} async-done(((f32[49,768]{1,0:T(8,128)}), f32[49,768]{1,0:T(8,128)}) %all-reduce.12.cloned.1.call-update) | async-done | bytes 150544 | tf_op jit(solution)/shard_map/psum | solution.py:377
  1624.8 16.3 psum.101
  (662 shorter events, 371.0 us)
Async XLA Ops:
  7.2 58.5 %all-gather.13.cloned.1.call-start = ((), (), s32[]{:S(2)}) async-start(), calls=%async_computation.6 | async-start | bytes 5308416 | tf_op jit(solution)/shard_map/all_gather | solution.py:276
  9.4 138.4 %all-gather.17.cloned.1.call-start = ((), (), s32[]{:S(2)}) async-start(), calls=%async_computation.14 | async-start | bytes 9289728 | tf_op jit(solution)/shard_map/all_gather | solution.py:287
  13.3 230.8 %all-gather.19.cloned.1.call-start = ((), (), s32[]{:S(2)}) async-start(), calls=%async_computation.15 | async-start | bytes 6635520 | tf_op jit(solution)/shard_map/all_gather | solution.py:290
  14.6 42.8 %copy-start.77 = (f32[49,768]{1,0:T(8,128)S(1)}, f32[49,768]{1,0:T(8,128)}, u32[]{:S(2)}) copy-start(f32[49,768]{1,0:T(8,128)} %param.42) | copy-start | bytes 451588
  14.6 42.8 %copy-start.174 = (s32[1,8]{1,0:T(1,128)S(1)}, s32[1,8]{1,0:T(1,128)}, u32[]{:S(2)}) copy-start(s32[1,8]{1,0:T(1,128)} %param.35) | copy-start | bytes 100
  15.9 276.0 %all-gather.21.cloned.1.call-start = ((), (), s32[]{:S(2)}) async-start(), calls=%async_computation.16 | async-start | bytes 9289728 | tf_op jit(solution)/shard_map/all_gather | solution.py:287
  16.5 369.5 %all-gather.23.cloned.1.call-start = ((), (), s32[]{:S(2)}) async-start(), calls=%async_computation.17 | async-start | bytes 6635520 | tf_op jit(solution)/shard_map/all_gather | solution.py:290
  17.0 398.1 %all-gather.15.cloned.1.call-start = ((), (), s32[]{:S(2)}) async-start(), calls=%async_computation.7 | async-start | bytes 1769472 | tf_op jit(solution)/shard_map/all_gather | solution.py:277
  17.8 1056.8 %reduce-scatter.19.cloned.1.call-start = ((), (), s32[]{:S(2)}) async-start(), calls=%async_computation.18 | async-start | bytes 5308416
  18.0 39.5 %copy-start.167 = (s32[8]{0:T(128)}, s32[8]{0:T(128)S(1)}, u32[]{:S(2)}) copy-start(s32[8]{0:T(128)S(1)} %convert_reduce_fusion.2) | copy-start | bytes 100
  54.8 93.1 %copy-start.123 = (f32[768]{0:T(1024)}, f32[768]{0:T(1024)S(1)}, u32[]{:S(2)}) copy-start(f32[768]{0:T(1024)S(1)} %get-tuple-element.464) | copy-start | bytes 9220
  54.8 93.1 %copy-start.155 = (f32[768]{0:T(1024)}, f32[768]{0:T(1024)S(1)}, u32[]{:S(2)}) copy-start(f32[768]{0:T(1024)S(1)} %get-tuple-element.463) | copy-start | bytes 9220
  57.9 16.4 copy-start.66
  76.0 78.2 %copy-start.12 = (f32[1024,768]{0,1:T(8,128)}, f32[1024,768]{0,1:T(8,128)S(1)}, u32[]{:S(2)}) copy-start(f32[1024,768]{0,1:T(8,128)S(1)} %get-tuple-element.637) | copy-start | bytes 9437188
  76.1 78.2 %copy-start.94 = (f32[1024]{0:T(1024)}, f32[1024]{0:T(1024)S(1)}, u32[]{:S(2)}) copy-start(f32[1024]{0:T(1024)S(1)} %broadcast_multiply_fusion.5) | copy-start | bytes 12292
  76.4 77.8 %copy-start.112 = (f32[1024]{0:T(1024)}, f32[1024]{0:T(1024)S(1)}, u32[]{:S(2)}) copy-start(f32[1024]{0:T(1024)S(1)} %multiply_reduce_fusion.16) | copy-start | bytes 12292
  76.5 77.8 %copy-start.118 = (f32[1024]{0:T(1024)}, f32[1024]{0:T(1024)S(1)}, u32[]{:S(2)}) copy-start(f32[1024]{0:T(1024)S(1)} %fusion.142) | copy-start | bytes 12292
  165.2 23.3 %copy-start.10 = (bf16[1024,12,64]{0,2,1:T(8,128)(2,1)S(1)}, bf16[1024,12,64]{0,2,1:T(8,128)(2,1)}, u32[]{:S(2)}) copy-start(bf16[1024,12,64]{0,2,1:T(8,128)(2,1)} %get-tuple-element.937) | copy-start | bytes 4718596 | tf_op jit(solution)/shard_map/while
  176.1 15.9 copy-start
  202.2 23.8 %copy-start.10 = (bf16[1024,12,64]{0,2,1:T(8,128)(2,1)S(1)}, bf16[1024,12,64]{0,2,1:T(8,128)(2,1)}, u32[]{:S(2)}) copy-start(bf16[1024,12,64]{0,2,1:T(8,128)(2,1)} %get-tuple-element.937) | copy-start | bytes 4718596 | tf_op jit(solution)/shard_map/while
  212.9 16.9 %copy-start = (f32[12,512,1024]{2,1,0:T(8,128)S(1)}, f32[12,512,1024]{2,1,0:T(8,128)}, u32[]{:S(2)}) copy-start(f32[12,512,1024]{2,1,0:T(8,128)} %get-tuple-element.868) | copy-start | bytes 75497472 | tf_op jit(solution)/shard_map/while
  269.8 28.5 %copy-start.24 = (f32[1024,768]{0,1:T(8,128)}, f32[1024,768]{0,1:T(8,128)S(1)}, u32[]{:S(2)}) copy-start(f32[1024,768]{0,1:T(8,128)S(1)} %get-tuple-element.641) | copy-start | bytes 9437188
  269.8 22.1 %copy-start.125 = (f32[768]{0:T(1024)S(1)}, f32[768]{0:T(1024)}, u32[]{:S(2)}) copy-start(f32[768]{0:T(1024)} %get-tuple-element.458) | copy-start | bytes 9220
  269.8 22.1 %copy-start.140 = (f32[2304]{0:T(1024)S(1)}, f32[2304]{0:T(1024)}, u32[]{:S(2)}) copy-start(f32[2304]{0:T(1024)} %slice_reduce_fusion) | copy-start | bytes 27652
  269.8 22.1 %copy-start.159 = (f32[768]{0:T(1024)S(1)}, f32[768]{0:T(1024)}, u32[]{:S(2)}) copy-start(f32[768]{0:T(1024)} %get-tuple-element.457) | copy-start | bytes 9220
  269.9 28.4 %copy-start.96 = (f32[1024]{0:T(1024)}, f32[1024]{0:T(1024)S(1)}, u32[]{:S(2)}) copy-start(f32[1024]{0:T(1024)S(1)} %broadcast_multiply_fusion.3) | copy-start | bytes 12292
  270.3 28.0 %copy-start.116 = (f32[1024]{0:T(1024)}, f32[1024]{0:T(1024)S(1)}, u32[]{:S(2)}) copy-start(f32[1024]{0:T(1024)S(1)} %multiply_reduce_fusion.14) | copy-start | bytes 12292
  270.3 28.0 %copy-start.120 = (f32[1024]{0:T(1024)}, f32[1024]{0:T(1024)S(1)}, u32[]{:S(2)}) copy-start(f32[1024]{0:T(1024)S(1)} %fusion.144) | copy-start | bytes 12292
  309.3 23.3 %copy-start.11 = (bf16[1024,12,64]{0,2,1:T(8,128)(2,1)S(1)}, bf16[1024,12,64]{0,2,1:T(8,128)(2,1)}, u32[]{:S(2)}) copy-start(bf16[1024,12,64]{0,2,1:T(8,128)(2,1)} %get-tuple-element.973) | copy-start | bytes 4718596 | tf_op jit(solution)/shard_map/while
  320.2 15.9 copy-start.1
  346.3 23.2 %copy-start.11 = (bf16[1024,12,64]{0,2,1:T(8,128)(2,1)S(1)}, bf16[1024,12,64]{0,2,1:T(8,128)(2,1)}, u32[]{:S(2)}) copy-start(bf16[1024,12,64]{0,2,1:T(8,128)(2,1)} %get-tuple-element.973) | copy-start | bytes 4718596 | tf_op jit(solution)/shard_map/while
  357.1 15.8 copy-start.1
  390.5 122.8 %copy-start.89 = (f32[1024]{0:T(1024)}, f32[1024]{0:T(1024)S(1)}, u32[]{:S(2)}) copy-start(f32[1024]{0:T(1024)S(1)} %broadcast_multiply_fusion.2) | copy-start | bytes 12292
  390.9 122.4 %copy-start.110 = (f32[1024]{0:T(1024)}, f32[1024]{0:T(1024)S(1)}, u32[]{:S(2)}) copy-start(f32[1024]{0:T(1024)S(1)} %fusion.145) | copy-start | bytes 12292
  415.1 49.5 %copy-start.84 = (bf16[8,768]{1,0:T(8,128)(2,1)}, bf16[8,768]{1,0:T(8,128)(2,1)S(1)}, u32[]{:S(2)}) copy-start(bf16[8,768]{1,0:T(8,128)(2,1)S(1)} %fusion.112) | copy-start | bytes 36868
  475.3 19.0 %slice-start.6 = ((s8[8257536]{0:T(1024)(128)(4,1)}), s8[4194304]{0:T(1024)(128)(4,1)S(1)}, s32[]{:S(2)}) async-start(s8[8257536]{0:T(1024)(128)(4,1)} %bitcast.285), calls=%async_computation.26 | async-start | bytes 8388608
  476.3 18.1 %copy-start.68 = (bf16[1024,768]{0,1:T(8,128)(2,1)}, bf16[1024,768]{0,1:T(8,128)(2,1)S(1)}, u32[]{:S(2)}) copy-start(bf16[1024,768]{0,1:T(8,128)(2,1)S(1)} %get-tuple-element.596) | copy-start | bytes 4718596
  476.5 17.9 %slice-start.7 = ((s8[8257536]{0:T(1024)(128)(4,1)}), s8[4063232]{0:T(1024)(128)(4,1)S(1)}, s32[]{:S(2)}) async-start(s8[8257536]{0:T(1024)(128)(4,1)} %bitcast.285), calls=%async_computation.27 | async-start | bytes 8126464
  720.6 19.4 %slice-start.2 = ((s8[8257536]{0:T(1024)(128)(4,1)}), s8[4194304]{0:T(1024)(128)(4,1)S(1)}, s32[]{:S(2)}) async-start(s8[8257536]{0:T(1024)(128)(4,1)} %bitcast.277), calls=%async_computation.22 | async-start | bytes 8388608
  721.7 18.4 %copy-start.71 = (bf16[1024,768]{0,1:T(8,128)(2,1)}, bf16[1024,768]{0,1:T(8,128)(2,1)S(1)}, u32[]{:S(2)}) copy-start(bf16[1024,768]{0,1:T(8,128)(2,1)S(1)} %get-tuple-element.590) | copy-start | bytes 4718596
  722.3 17.7 %slice-start.3 = ((s8[8257536]{0:T(1024)(128)(4,1)}), s8[4063232]{0:T(1024)(128)(4,1)S(1)}, s32[]{:S(2)}) async-start(s8[8257536]{0:T(1024)(128)(4,1)} %bitcast.277), calls=%async_computation.23 | async-start | bytes 8126464
  980.9 95.9 %reduce-scatter.9.cloned.1.call-start = ((), (), s32[]{:S(2)}) async-start(), calls=%async_computation.8 | async-start | bytes 1769472 | tf_op jit(solution)/shard_map/reduce_scatter | solution.py:365
  988.2 149.6 %reduce-scatter.17.cloned.1.call-start = ((), (), s32[]{:S(2)}) async-start(), calls=%async_computation.12 | async-start | bytes 6635520 | tf_op jit(solution)/shard_map/reduce_scatter | solution.py:342
  1003.3 201.2 %reduce-scatter.15.cloned.1.call-start = ((), (), s32[]{:S(2)}) async-start(), calls=%async_computation.11 | async-start | bytes 6635520 | tf_op jit(solution)/shard_map/reduce_scatter | solution.py:342
  1022.2 271.5 %reduce-scatter.13.cloned.1.call-start = ((), (), s32[]{:S(2)}) async-start(), calls=%async_computation.10 | async-start | bytes 9289728 | tf_op jit(solution)/shard_map/reduce_scatter | solution.py:339
  1049.4 333.2 %reduce-scatter.11.cloned.1.call-start = ((), (), s32[]{:S(2)}) async-start(), calls=%async_computation.9 | async-start | bytes 9289728 | tf_op jit(solution)/shard_map/reduce_scatter | solution.py:339
  1074.6 420.9 %all-reduce.14.cloned.1.call-start = ((), (), s32[]{:S(2)}) async-start(), calls=%async_computation.19 | async-start | bytes 8650752 | tf_op jit(solution)/shard_map/psum | solution.py:370
  1382.7 240.5 %all-reduce.12.cloned.1.call-start = ((), (), s32[]{:S(2)}) async-start(), calls=%async_computation.13 | async-start | bytes 344064 | tf_op jit(solution)/shard_map/psum | solution.py:377
  1382.8 47.7 %copy-start.148 = (bf16[768]{0:T(1024)(128)(2,1)S(1)}, bf16[768]{0:T(1024)(128)(2,1)}, u32[]{:S(2)}) copy-start(bf16[768]{0:T(1024)(128)(2,1)} %get-tuple-element.452) | copy-start | bytes 4612
  1382.8 47.9 %copy-start.149 = (bf16[768]{0:T(1024)(128)(2,1)S(1)}, bf16[768]{0:T(1024)(128)(2,1)}, u32[]{:S(2)}) copy-start(bf16[768]{0:T(1024)(128)(2,1)} %get-tuple-element.450) | copy-start | bytes 4612
  1382.8 48.1 %copy-start.170 = (bf16[768]{0:T(1024)(128)(2,1)S(1)}, bf16[768]{0:T(1024)(128)(2,1)}, u32[]{:S(2)}) copy-start(bf16[768]{0:T(1024)(128)(2,1)} %get-tuple-element.650) | copy-start | bytes 4612
  1382.8 48.3 %copy-start.172 = (bf16[768]{0:T(1024)(128)(2,1)S(1)}, bf16[768]{0:T(1024)(128)(2,1)}, u32[]{:S(2)}) copy-start(bf16[768]{0:T(1024)(128)(2,1)} %get-tuple-element.654) | copy-start | bytes 4612
  1382.9 48.5 %copy-start.144 = (bf16[768]{0:T(1024)(128)(2,1)S(1)}, bf16[768]{0:T(1024)(128)(2,1)}, u32[]{:S(2)}) copy-start(bf16[768]{0:T(1024)(128)(2,1)} %get-tuple-element.446) | copy-start | bytes 4612
  1382.9 48.7 %copy-start.145 = (bf16[768]{0:T(1024)(128)(2,1)S(1)}, bf16[768]{0:T(1024)(128)(2,1)}, u32[]{:S(2)}) copy-start(bf16[768]{0:T(1024)(128)(2,1)} %get-tuple-element.444) | copy-start | bytes 4612
  1382.9 48.9 %copy-start.169 = (bf16[768]{0:T(1024)(128)(2,1)S(1)}, bf16[768]{0:T(1024)(128)(2,1)}, u32[]{:S(2)}) copy-start(bf16[768]{0:T(1024)(128)(2,1)} %get-tuple-element.652) | copy-start | bytes 4612
  1382.9 49.1 %copy-start.171 = (bf16[768]{0:T(1024)(128)(2,1)S(1)}, bf16[768]{0:T(1024)(128)(2,1)}, u32[]{:S(2)}) copy-start(bf16[768]{0:T(1024)(128)(2,1)} %get-tuple-element.656) | copy-start | bytes 4612
  1382.9 49.3 %copy-start.46 = (bf16[96,8,2,512]{3,1,2,0:T(8,128)(2,1)S(1)}, bf16[96,8,2,512]{3,1,2,0:T(8,128)(2,1)}, u32[]{:S(2)}) copy-start(bf16[96,8,2,512]{3,1,2,0:T(8,128)(2,1)} %copy-done.45) | copy-start | bytes 4718596
  1382.9 49.3 %copy-start.48 = (bf16[1024,12,64]{0,2,1:T(8,128)(2,1)S(1)}, bf16[1024,12,64]{0,2,1:T(8,128)(2,1)}, u32[]{:S(2)}) copy-start(bf16[1024,12,64]{0,2,1:T(8,128)(2,1)} %copy-done.47) | copy-start | bytes 4718596
  1430.6 37.0 %copy-start.93 = (f32[3304]{0:T(1024)}, f32[3304]{0:T(1024)S(1)}, u32[]{:S(2)}) copy-start(f32[3304]{0:T(1024)S(1)} %get-tuple-element.551) | copy-start | bytes 39652
  1434.2 34.0 %copy-start.28 = (f32[1024,768]{0,1:T(8,128)S(1)}, f32[1024,768]{0,1:T(8,128)}, u32[]{:S(2)}) copy-start(f32[1024,768]{0,1:T(8,128)} %copy-done.26) | copy-start | bytes 9437188
  1434.2 34.0 %copy-start.67 = (f32[1024,49]{0,1:T(8,128)S(1)}, f32[1024,49]{0,1:T(8,128)}, u32[]{:S(2)}) copy-start(f32[1024,49]{0,1:T(8,128)} %copy-done.66) | copy-start | bytes 602116
  1474.1 169.0 %copy-start.56 = (f32[384,768]{0,1:T(8,128)S(1)}, f32[384,768]{0,1:T(8,128)}, u32[]{:S(2)}) copy-start(f32[384,768]{0,1:T(8,128)} %copy.159) | copy-start | bytes 3538948
  1474.1 169.0 %copy-start.57 = (f32[384,768]{0,1:T(8,128)S(1)}, f32[384,768]{0,1:T(8,128)}, u32[]{:S(2)}) copy-start(f32[384,768]{0,1:T(8,128)} %copy.156) | copy-start | bytes 3538948
  1474.1 169.0 %copy-start.58 = (f32[384,768]{0,1:T(8,128)S(1)}, f32[384,768]{0,1:T(8,128)}, u32[]{:S(2)}) copy-start(f32[384,768]{0,1:T(8,128)} %copy.157) | copy-start | bytes 3538948
  (148 other events, 812.4 us)
Sparse Core Ops, SparseCore 0:
  10.2 55.4 all-gather.12
  67.9 79.8 all-gather.16
  150.1 60.0 all-gather.18
  212.2 79.6 all-gather.20
  294.0 60.0 all-gather.22
  356.1 23.7 all-gather.14
  981.0 54.9 reduce-scatter.18
  1038.8 32.3 reduce-scatter.8
  1073.6 64.1 reduce-scatter.16
  1140.1 64.4 reduce-scatter.14
  1206.9 86.7 reduce-scatter.12
  1295.9 86.7 reduce-scatter.10
  1387.6 107.7 all-reduce.13
  1501.4 121.7 all-reduce.11
where the time goes:
time: 1700 us; the launch traced here: 1680 us
  matrix products  571 us (34%)
  waiting for transfers between devices  526 us (31%)
  other arithmetic  247 us (15%)
  blocking collectives  171 us (10%)
  local copies, waits for them, and re-layouts  131 us (8%)
  between operations  24.2 us (1%)
    dot_general x29, matrix products, matmul(): return jnp.dot(left, right, preferred_element_type=jnp.float32)  233 us
    reduce_scatter x2, waiting for transfers between devices, body(): lax.psum_scatter(partial_value[0].astype(jnp.bfloat16), 'fsdp', scatter_d...  178 us
    reduce_scatter x2, waiting for transfers between devices, body(): lax.psum_scatter(partial_value[1].astype(jnp.bfloat16), 'fsdp', scatter_d...  128 us
    psum x1, waiting for transfers between devices, body(): lax.psum((position_grad, global_grad, loss_local), ('dp', 'fsdp'))  115 us
    all_gather x2, waiting for transfers between devices, body(): lax.all_gather(input_proj[depth_index].astype(jnp.bfloat16), 'fsdp', axis...  93 us
    dot_general x8, matrix products, attention_scores(): jnp.einsum('qhd,khd->hqk', query_block, key_rows, preferred_element_type=...  89 us
    convert_element_type x4, other arithmetic, one_block(): (probabilities * (probs_grad - row_inner)).astype(jnp.bfloat16)  85 us
    dot_general x4, matrix products, one_block(): jnp.einsum('qhd,khd->hqk', grad_block, values, preferred_element_type=jnp...  72.4 us
  transfers between devices with their start and end apart: 14, of which 9 were waited for; matrix products, arithmetic and copies ran while one was open for 22% of the time, Pallas kernels for 0%

commit v1 on v0

v1 whole, which is shorter than its diff:
```python
import functools

import jax
import jax.numpy as jnp
from jax import lax
from jax.experimental import pallas as pl
from jax.experimental.pallas import tpu as pltpu
from jax.sharding import PartitionSpec as P

D = 768
HEADS = 12
HD = 64
CLS = 1000
GRID = 7
IMG = 240
IMGS = 8
LAYERS = 2
STEP = 3


NORM_EPS = 1e-06
CLIP_NORM = 0.01
LEARN_RATE = 0.05
VECTOR_RATE = 0.25
BETA_ONE = 0.5
BETA_TWO = 0.5
ADAM_EPS = 1e-08
WEIGHT_DECAY = 0.05
HIGHEST = lax.Precision.HIGHEST

PAIR = 2 * HD
MASKED = -1e30
VMEM_LIMIT = 56 * 1024 * 1024
AXES = ("fsdp", "dp")
LANES = 128


def layer_norm(values, gain, shift):
    center = values - jnp.mean(values, -1, keepdims=True)
    spread = jnp.mean(center * center, -1, keepdims=True)
    return center * lax.rsqrt(spread + NORM_EPS) * gain + shift


def rounded(values):
    return lax.optimization_barrier(values.astype(jnp.bfloat16)).astype(jnp.float32)


def column_total(rows):
    return jnp.sum(rows.astype(jnp.float32), 0)


def matmul(left, right):
    return jnp.dot(left, right, preferred_element_type=jnp.float32)


def gather_rows(shard):
    share = shard.shape[0] // lax.axis_size("dp")
    mine = lax.dynamic_slice_in_dim(shard, lax.axis_index("dp") * share, share, 0)
    return lax.all_gather(mine.astype(jnp.bfloat16), AXES, axis=0, tiled=True)


def scatter_rows(partial_sum):
    return lax.psum_scatter(
        partial_sum.astype(jnp.bfloat16), AXES, scatter_dimension=0, tiled=True
    )


def regather(shares):
    return lax.all_gather(shares, "dp", axis=0, tiled=True).astype(jnp.float32)


def padded_rows(flat, multiple):
    extra = -flat.shape[0] % (multiple * LANES)
    return jnp.pad(flat, (0, extra)).reshape(-1, LANES)


def gather_vectors(shard):
    size = shard.size
    full = lax.all_gather(
        padded_rows(shard.astype(jnp.bfloat16).reshape(-1), 16), "fsdp", axis=0, tiled=True
    )
    owners = lax.axis_size("fsdp")
    full = full.reshape(owners, -1)[:, :size].reshape(owners, *shard.shape)
    return jnp.swapaxes(full, 0, 1).reshape(shard.shape[0], -1)


def total_flat(flat):
    rows = padded_rows(flat, 16 * lax.axis_size("dp") * lax.axis_size("fsdp"))
    share = lax.psum_scatter(rows, AXES, scatter_dimension=0, tiled=True)
    return lax.all_gather(share, AXES, axis=0, tiled=True).reshape(-1)[: flat.shape[0]]


def row_layout(seg_row, patch_row):
    row_count = seg_row.shape[0]
    slots = jnp.arange(IMGS, dtype=jnp.int32)
    member = seg_row[:, None] == slots[None, :]
    counts = jnp.sum(member.astype(jnp.int32), 0, dtype=jnp.int32)
    starts = jnp.cumsum(counts, dtype=jnp.int32) - counts
    inside = jnp.any(member, 1)
    offset = jnp.arange(row_count, dtype=jnp.int32) - jnp.sum(
        jnp.where(member, starts[None, :], 0), 1, dtype=jnp.int32
    )
    offset = jnp.where(inside, offset, 0)
    patch_tok = jnp.sum(jnp.where(member, patch_row[None, :], 0), 1, dtype=jnp.int32) + jnp.where(
        inside, 0, IMG
    )
    side = IMG // patch_tok
    nodes = jnp.arange(GRID, dtype=jnp.int32).astype(jnp.float32)

    def hat(coord):
        place = ((2 * coord + 1) * GRID).astype(jnp.float32) / (2 * side).astype(jnp.float32) - 0.5
        place = jnp.clip(place, 0.0, GRID - 1.0)
        return jnp.maximum(1.0 - jnp.abs(place[:, None] - nodes[None, :]), 0.0)

    weights = (hat(offset // side)[:, :, None] * hat(offset % side)[:, None, :]).reshape(
        row_count, GRID * GRID
    )
    return (weights, member.astype(jnp.float32), counts.astype(jnp.float32))


def attention_forward_kernel(q_ref, k_ref, v_ref, seg_col_ref, seg_row_ref, out_ref, expo_ref, inv_ref, *, block):
    rows = q_ref.shape[0]
    lower = lax.broadcasted_iota(jnp.int32, (block, PAIR), 1) < HD
    keys = k_ref[...]
    values = v_ref[...]
    seg_row = seg_row_ref[...]

    def one_block(step, carry):
        at = pl.ds(pl.multiple_of(step * block, block), block)
        query = q_ref[at, :] * jnp.bfloat16(HD**-0.5)
        same = seg_col_ref[at, :] == seg_row
        outs, invs = [], []
        for head in range(2):
            keep = lower if head == 0 else jnp.logical_not(lower)
            mine = jnp.where(keep, query, jnp.bfloat16(0))
            scores = lax.dot_general(
                mine, keys, (((1,), (1,)), ((), ())), preferred_element_type=jnp.float32
            )
            scores = jnp.where(same, scores, MASKED)
            highest = jnp.max(scores, -1, keepdims=True)
            exponent = jnp.exp(scores - highest)
            total = jnp.sum(exponent, -1, keepdims=True)
            low = exponent.astype(jnp.bfloat16)
            expo_ref[head, at, :] = low
            outs.append(jnp.dot(low, values, preferred_element_type=jnp.float32))
            invs.append(1.0 / total)
        inverse = jnp.where(lower, invs[0], invs[1])
        out_ref[at, :] = (jnp.where(lower, outs[0], outs[1]) * inverse).astype(jnp.bfloat16)
        inv_ref[at, :] = inverse
        return carry

    lax.fori_loop(0, rows // block, one_block, 0, unroll=True)


def attention_forward(qkv_rows, segment):
    rows = qkv_rows.shape[0]
    pairs = HEADS // 2
    block = min(256, rows)
    wide = lambda base: pl.BlockSpec((rows, PAIR), lambda j, base=base: (0, base + j))
    return pl.pallas_call(
        functools.partial(attention_forward_kernel, block=block),
        grid=(pairs,),
        in_specs=[
            wide(0),
            wide(pairs),
            wide(2 * pairs),
            pl.BlockSpec((rows, 1), lambda j: (0, 0)),
            pl.BlockSpec((1, rows), lambda j: (0, 0)),
        ],
        out_specs=[
            wide(0),
            pl.BlockSpec((2, rows, rows), lambda j: (j, 0, 0)),
            wide(0),
        ],
        out_shape=[
            jax.ShapeDtypeStruct((rows, D), jnp.bfloat16),
            jax.ShapeDtypeStruct((HEADS, rows, rows), jnp.bfloat16),
            jax.ShapeDtypeStruct((rows, D), jnp.float32),
        ],
        compiler_params=pltpu.CompilerParams(vmem_limit_bytes=VMEM_LIMIT),
        cost_estimate=pl.CostEstimate(
            flops=4 * HEADS * rows * rows * HD * 4,
            bytes_accessed=2 * HEADS * rows * rows + 12 * rows * D,
            transcendentals=HEADS * rows * rows,
        ),
        name="attention_forward",
    )(qkv_rows, qkv_rows, qkv_rows, segment[:, None], segment[None, :])


def attention_backward_kernel(q_ref, k_ref, v_ref, expo_ref, inv_ref, out_ref, grad_ref, dqkv_ref, *, block):
    rows = q_ref.shape[0]
    pair = pl.program_id(0)
    lower = lax.broadcasted_iota(jnp.int32, (block, PAIR), 1) < HD
    keys = k_ref[...]
    values = v_ref[...]
    scale = HD**-0.5
    scaled_grad = (grad_ref[...].astype(jnp.float32) * inv_ref[...]).astype(jnp.bfloat16)
    query = q_ref[...]
    query_t = query.T
    grad_t = scaled_grad.T
    product = scaled_grad.astype(jnp.float32) * out_ref[...].astype(jnp.float32)
    key_t = [None, None]
    value_t = [None, None]
    for step in range(rows // block):
        at = slice(step * block, (step + 1) * block)
        query_parts = []
        for head in range(2):
            lanes = slice(head * HD, (head + 1) * HD)
            keep = lower if head == 0 else jnp.logical_not(lower)
            mine = jnp.where(keep, scaled_grad[at], jnp.bfloat16(0))
            inner = jnp.sum(jnp.where(keep, product[at], 0.0), -1, keepdims=True)
            low = expo_ref[head, at, :]
            probs_grad = lax.dot_general(
                mine, values, (((1,), (1,)), ((), ())), preferred_element_type=jnp.float32
            )
            scores_grad = (low.astype(jnp.float32) * (probs_grad - inner)).astype(jnp.bfloat16)
            query_parts.append(jnp.dot(scores_grad, keys, preferred_element_type=jnp.float32))
            key_part = jnp.dot(query_t[lanes, at], scores_grad, preferred_element_type=jnp.float32)
            value_part = jnp.dot(grad_t[lanes, at], low, preferred_element_type=jnp.float32)
            key_t[head] = key_part if step == 0 else key_t[head] + key_part
            value_t[head] = value_part if step == 0 else value_t[head] + value_part
        query_grad = jnp.where(lower, query_parts[0], query_parts[1]) * scale
        dqkv_ref[at, pl.ds(pl.multiple_of(pair * PAIR, PAIR), PAIR)] = query_grad.astype(jnp.bfloat16)
    key_grad = (jnp.concatenate(key_t, 0) * scale).T
    value_grad = jnp.concatenate(value_t, 0).T
    dqkv_ref[:, pl.ds(pl.multiple_of(D + pair * PAIR, PAIR), PAIR)] = key_grad.astype(jnp.bfloat16)
    dqkv_ref[:, pl.ds(pl.multiple_of(2 * D + pair * PAIR, PAIR), PAIR)] = value_grad.astype(jnp.bfloat16)


def attention_backward(qkv_rows, expo, inverse, attended, attended_grad):
    rows = qkv_rows.shape[0]
    pairs = HEADS // 2
    block = min(256, rows)
    wide = lambda base: pl.BlockSpec((rows, PAIR), lambda j, base=base: (0, base + j))
    return pl.pallas_call(
        functools.partial(attention_backward_kernel, block=block),
        grid=(pairs,),
        in_specs=[
            wide(0),
            wide(pairs),
            wide(2 * pairs),
            pl.BlockSpec((2, rows, rows), lambda j: (j, 0, 0)),
            wide(0),
            wide(0),
            wide(0),
        ],
        out_specs=pl.BlockSpec((rows, 3 * D), lambda j: (0, 0)),
        out_shape=jax.ShapeDtypeStruct((rows, 3 * D), jnp.bfloat16),
        compiler_params=pltpu.CompilerParams(vmem_limit_bytes=VMEM_LIMIT),
        cost_estimate=pl.CostEstimate(
            flops=8 * HEADS * rows * rows * HD * 4,
            bytes_accessed=2 * HEADS * rows * rows + 20 * rows * D,
            transcendentals=0,
        ),
        name="attention_backward",
    )(qkv_rows, qkv_rows, qkv_rows, expo, inverse, attended, attended_grad)


def layer_forward(stream, weights, seg_row):
    proj_in, proj_out, vector_low = weights
    vector = vector_low.astype(jnp.float32)
    normed = layer_norm(stream, vector[0:D], vector[D : 2 * D]).astype(jnp.bfloat16)
    qkv_rows = (matmul(normed, proj_in[:, : 3 * D]) + vector[4 * D : 7 * D]).astype(jnp.bfloat16)
    attended, expo, inverse = attention_forward(qkv_rows, seg_row)
    residual = stream + matmul(attended, proj_out[:D]) + vector[7 * D : 8 * D]
    normed_second = layer_norm(residual, vector[2 * D : 3 * D], vector[3 * D : 4 * D]).astype(
        jnp.bfloat16
    )
    hidden = matmul(normed_second, proj_in[:, 3 * D :]) + vector[9 * D :]
    active = jax.nn.gelu(hidden).astype(jnp.bfloat16)
    output = residual + matmul(active, proj_out[D:]) + vector[8 * D : 9 * D]
    return (output, (stream, qkv_rows, attended, expo, inverse, residual, hidden))


def layer_backward(grad_stream, weights, layer_saved):
    proj_in, proj_out, vector_low = weights
    vector = vector_low.astype(jnp.float32)
    stream, qkv_rows, attended, expo, inverse, residual, hidden = layer_saved
    grad_low = grad_stream.astype(jnp.bfloat16)
    normed_second, second_back = jax.vjp(
        layer_norm, residual, vector[2 * D : 3 * D], vector[3 * D : 4 * D]
    )
    normed_second = normed_second.astype(jnp.bfloat16)
    active, gelu_back = jax.vjp(jax.nn.gelu, hidden)
    active = active.astype(jnp.bfloat16)
    down_grad = matmul(active.T, grad_low)
    active_grad = matmul(grad_low, proj_out[D:].T)
    hidden_grad = gelu_back(active_grad)[0].astype(jnp.bfloat16)
    up_grad = matmul(normed_second.T, hidden_grad)
    second_grad = matmul(hidden_grad, proj_in[:, 3 * D :].T)
    residual_grad, gain_second, shift_second = second_back(second_grad)
    residual_grad = residual_grad + grad_stream
    residual_low = residual_grad.astype(jnp.bfloat16)
    mixing_grad = matmul(attended.T, residual_low)
    attended_grad = matmul(residual_low, proj_out[:D].T).astype(jnp.bfloat16)
    qkv_grad = attention_backward(qkv_rows, expo, inverse, attended, attended_grad)
    normed, first_back = jax.vjp(layer_norm, stream, vector[0:D], vector[D : 2 * D])
    project_grad = matmul(normed.astype(jnp.bfloat16).T, qkv_grad)
    normed_grad = matmul(qkv_grad, proj_in[:, : 3 * D].T)
    stream_grad, gain_first, shift_first = first_back(normed_grad)
    vector_grad = jnp.concatenate(
        [
            gain_first,
            shift_first,
            gain_second,
            shift_second,
            column_total(qkv_grad),
            column_total(residual_low),
            column_total(grad_low),
            column_total(hidden_grad),
        ]
    )
    return (
        residual_grad + stream_grad,
        (
            jnp.concatenate([project_grad, up_grad], 1),
            jnp.concatenate([mixing_grad, down_grad], 0),
            vector_grad,
        ),
    )


def adam_update(gradient, moment, square, weight, factor, learn_rate):
    clipped = gradient * factor
    moment = BETA_ONE * moment + (1.0 - BETA_ONE) * clipped
    square = BETA_TWO * square + (1.0 - BETA_TWO) * clipped * clipped
    fixed_one = 1.0 - BETA_ONE**STEP
    fixed_two = 1.0 - BETA_TWO**STEP
    step_dir = (
        moment / fixed_one / (jnp.sqrt(square / fixed_two) + ADAM_EPS) + WEIGHT_DECAY * weight
    )
    return (moment, square, weight - learn_rate * step_dir)


def body(
    pixels,
    segment,
    patch_size,
    labels,
    patch_kernel,
    head_weight,
    input_proj,
    output_proj,
    layer_vector,
    position_table,
    global_vector,
    patch_moment,
    head_moment,
    input_moment,
    output_moment,
    layer_moment,
    position_moment,
    global_moment,
    patch_square,
    head_square,
    input_square,
    output_square,
    layer_square,
    position_square,
    global_square,
):
    pos_weights, member, counts = row_layout(segment, patch_size[0])
    kernel_full = gather_rows(patch_kernel)
    vectors = gather_vectors(layer_vector)
    layer_weights = [
        (gather_rows(input_proj[index]), gather_rows(output_proj[index]), vectors[index])
        for index in range(LAYERS)
    ]
    head_full = gather_rows(head_weight)
    global_low = rounded(global_vector)
    position_low = rounded(position_table)
    embed_pre = matmul(pixels, kernel_full) + global_low[:D]
    stream = embed_pre + jnp.dot(pos_weights, position_low, precision=HIGHEST)
    saved_layers = []
    for weights in layer_weights:
        stream, layer_saved = layer_forward(stream, weights, segment)
        saved_layers.append(layer_saved)
    final_norm, final_back = jax.vjp(
        layer_norm, stream, global_low[D : 2 * D], global_low[2 * D : 3 * D]
    )
    image_sizes = jnp.maximum(counts, 1.0)
    pooled = (jnp.dot(member.T, final_norm, precision=HIGHEST) / image_sizes[:, None]).astype(
        jnp.bfloat16
    )
    logits = matmul(pooled, head_full) + global_low[3 * D :]
    highest = jnp.max(logits, -1, keepdims=True)
    exponent = jnp.exp(logits - highest)
    totals = jnp.sum(exponent, -1, keepdims=True)
    logsum = (highest + jnp.log(totals))[:, 0]
    onehot = labels[0][:, None] == jnp.arange(CLS, dtype=jnp.int32)[None, :]
    picked = jnp.sum(jnp.where(onehot, logits, 0.0), 1)
    loss_local = jnp.sum(counts * (logsum - picked))
    logits_grad = ((exponent / totals - onehot.astype(jnp.float32)) * counts[:, None]).astype(
        jnp.bfloat16
    )
    head_share = scatter_rows(matmul(pooled.T, logits_grad))
    pooled_grad = matmul(logits_grad, head_full.T)
    final_grad = jnp.dot(member, pooled_grad / image_sizes[:, None], precision=HIGHEST)
    stream_grad, final_gain, final_shift = final_back(final_grad)
    layer_shares = [None] * LAYERS
    vector_grads = [None] * LAYERS
    for index in reversed(range(LAYERS)):
        stream_grad, grads = layer_backward(stream_grad, layer_weights[index], saved_layers[index])
        layer_shares[index] = (scatter_rows(grads[0]), scatter_rows(grads[1]))
        vector_grads[index] = grads[2]
    embed_low = stream_grad.astype(jnp.bfloat16)
    kernel_share = scatter_rows(matmul(pixels.T, embed_low))
    position_grad = jnp.dot(pos_weights.T, stream_grad, precision=HIGHEST)
    pieces = [
        position_grad.reshape(-1),
        column_total(embed_low),
        final_gain,
        final_shift,
        column_total(logits_grad),
        *vector_grads,
        loss_local[None],
        jnp.sum(counts)[None],
    ]
    small = total_flat(jnp.concatenate(pieces))
    position_sum = small[: position_grad.size].reshape(position_grad.shape)
    global_sum = small[position_grad.size :][: global_vector.shape[0]]
    vector_total = small[position_grad.size + global_vector.shape[0] :][
        : LAYERS * vectors.shape[1]
    ].reshape(vectors.shape)
    loss_sum = small[-2]
    token_total = small[-1]
    shares = [kernel_share, head_share]
    for pair in layer_shares:
        shares.extend(pair)
    local_squares = sum(jnp.sum(jnp.square(item.astype(jnp.float32))) for item in shares)
    share_squares = lax.psum(local_squares, ("dp", "fsdp"))
    kernel_sum = regather(kernel_share)
    head_sum = regather(head_share)
    input_sum = jnp.stack([regather(pair[0]) for pair in layer_shares])
    output_sum = jnp.stack([regather(pair[1]) for pair in layer_shares])
    vector_sum = lax.dynamic_slice_in_dim(
        vector_total, lax.axis_index("fsdp") * layer_vector.shape[1], layer_vector.shape[1], 1
    )
    grad_norm = (
        jnp.sqrt(
            share_squares
            + jnp.sum(vector_total * vector_total)
            + jnp.sum(position_sum * position_sum)
            + jnp.sum(global_sum * global_sum)
        )
        / token_total
    )
    factor = jnp.minimum(1.0, CLIP_NORM / grad_norm) / token_total
    patch_next = adam_update(
        kernel_sum, patch_moment, patch_square, patch_kernel, factor, LEARN_RATE
    )
    head_next = adam_update(head_sum, head_moment, head_square, head_weight, factor, LEARN_RATE)
    input_next = adam_update(input_sum, input_moment, input_square, input_proj, factor, LEARN_RATE)
    output_next = adam_update(
        output_sum, output_moment, output_square, output_proj, factor, LEARN_RATE
    )
    layer_next = adam_update(
        vector_sum, layer_moment, layer_square, layer_vector, factor, VECTOR_RATE
    )
    position_next = adam_update(
        position_sum, position_moment, position_square, position_table, factor, LEARN_RATE
    )
    global_next = adam_update(
        global_sum, global_moment, global_square, global_vector, factor, VECTOR_RATE
    )
    return (
        loss_sum,
        token_total,
        grad_norm,
        patch_next[0],
        head_next[0],
        input_next[0],
        output_next[0],
        layer_next[0],
        position_next[0],
        global_next[0],
        patch_next[1],
        head_next[1],
        input_next[1],
        output_next[1],
        layer_next[1],
        position_next[1],
        global_next[1],
        patch_next[2],
        head_next[2],
        input_next[2],
        output_next[2],
        layer_next[2],
        position_next[2],
        global_next[2],
    )


def solution(mesh):
    in_specs = (
        P(("dp", "fsdp"), None),
        P(("dp", "fsdp")),
        P(("dp", "fsdp"), None),
        P(("dp", "fsdp"), None),
        P("fsdp", None),
        P("fsdp", None),
        P(None, "fsdp", None),
        P(None, "fsdp", None),
        P(None, "fsdp"),
        P(),
        P(),
        P("fsdp", None),
        P("fsdp", None),
        P(None, "fsdp", None),
        P(None, "fsdp", None),
        P(None, "fsdp"),
        P(),
        P(),
        P("fsdp", None),
        P("fsdp", None),
        P(None, "fsdp", None),
        P(None, "fsdp", None),
        P(None, "fsdp"),
        P(),
        P(),
    )
    out_specs = (
        P(),
        P(),
        P(),
        P("fsdp", None),
        P("fsdp", None),
        P(None, "fsdp", None),
        P(None, "fsdp", None),
        P(None, "fsdp"),
        P(),
        P(),
        P("fsdp", None),
        P("fsdp", None),
        P(None, "fsdp", None),
        P(None, "fsdp", None),
        P(None, "fsdp"),
        P(),
        P(),
        P("fsdp", None),
        P("fsdp", None),
        P(None, "fsdp", None),
        P(None, "fsdp", None),
        P(None, "fsdp"),
        P(),
        P(),
    )
    return jax.shard_map(body, mesh=mesh, in_specs=in_specs, out_specs=out_specs, check_vma=False)
```

time: 1700 us -> 1640 us (0.965)
  waiting for transfers between devices: 526 us -> 879 us
  matrix products: 571 us -> 248 us
  other arithmetic: 247 us -> 91.8 us
  Pallas kernels: 0 us -> 120 us
  local copies, waits for them, and re-layouts: 131 us -> 76.2 us
  blocking collectives: 171 us -> 193 us
    dot_general x28 -> x0, matrix products: 325 us -> none  [the longest x8 89 us: attention_scores(): jnp.einsum('qhd,khd->hqk', query_block, key_rows, preferred_element_type=...]
    reduce_scatter x5 -> x7, waiting for transfers between devices: 306 us -> 629 us  [the longest x6 605 us: scatter_rows(): lax.psum_scatter(partial_sum.astype(jnp.bfloat16), AXES, scatter_dimensio...]
    all_gather x0 -> x8, blocking collectives: none -> 154 us  [the longest x6 72.6 us: regather(): return lax.all_gather(shares, 'dp', axis=0, tiled=True).astype(jnp.float32)]
    all_gather x6, waiting for transfers between devices: 101 us -> 249 us  [gather_rows(): return lax.all_gather(mine.astype(jnp.bfloat16), AXES, axis=0, tiled=True)]
    pallas_call x0 -> x4, Pallas kernels: none -> 120 us  [the longest x2 62.2 us: attention_forward(): pl.pallas_call(functools.partial(attention_forward_kernel, block=block),...]
    psum x2 -> x0, waiting for transfers between devices: 118 us -> none  [the longest x1 115 us: body(): lax.psum((position_grad, global_grad, loss_local), ('dp', 'fsdp'))]
    convert_element_type x6 -> x3, other arithmetic: 87.8 us -> 0.73 us  [the longest x1 0.51 us: row_layout(): return (weights, member.astype(jnp.float32), counts.astype(jnp.float32))]
    psum x4 -> x1, blocking collectives: 111 us -> 39.3 us  [body(): share_squares = lax.psum(local_squares, ('dp', 'fsdp'))]
  transfers between devices with their start and end apart: 14 -> 13, of which waited for: 9 -> 13; matrix products, arithmetic and copies ran while one was open for 22% -> 13% of each run, Pallas kernels for 0% -> 4%
where the time goes in v1:
time: 1640 us; the launch traced here: 1630 us
  waiting for transfers between devices  879 us (54%)
  matrix products  248 us (15%)
  blocking collectives  193 us (12%)
  Pallas kernels  120 us (7%)
  other arithmetic  91.8 us (6%)
  local copies, waits for them, and re-layouts  76.2 us (5%)
  between operations  25.3 us (2%)
    reduce_scatter x6, waiting for transfers between devices, scatter_rows(): lax.psum_scatter(partial_sum.astype(jnp.bfloat16), AXES, scatter_dimensio...  605 us
    all_gather x6, waiting for transfers between devices, gather_rows(): return lax.all_gather(mine.astype(jnp.bfloat16), AXES, axis=0, tiled=True)  249 us
    dot_general x29, matrix products, matmul(): return jnp.dot(left, right, preferred_element_type=jnp.float32)  237 us
    all_gather x6, blocking collectives, regather(): return lax.all_gather(shares, 'dp', axis=0, tiled=True).astype(jnp.float32)  72.6 us
    all_gather x1, blocking collectives, total_flat(): lax.all_gather(share, AXES, axis=0, tiled=True).reshape(-1)[:flat.shape[0]]  65.4 us
    pallas_call x2, Pallas kernels, attention_forward(): pl.pallas_call(functools.partial(attention_forward_kernel, block=block),...  62.2 us
    pallas_call x2, Pallas kernels, attention_backward(): pl.pallas_call(functools.partial(attention_backward_kernel, block=block),...  57.7 us
    psum x1, blocking collectives, body(): share_squares = lax.psum(local_squares, ('dp', 'fsdp'))  39.3 us
  transfers between devices with their start and end apart: 13, of which 13 were waited for; matrix products, arithmetic and copies ran while one was open for 13% of the time, Pallas kernels for 4%

profile of v1, /device:TPU:0, one launch (start us, length us, event | category | flops | bytes accessed | tf_op | source)
XLA Modules:
  0.0 1633.4 jit_solution(18098145265348547165)
XLA Ops:
  20.4 15.7 all_gather.43
  43.1 34.7 %all-gather.11.cloned.1.call-done = bf16[3072,768]{1,0:T(8,128)(2,1)} async-done(((bf16[96,768]{1,0:T(8,128)(2,1)}), bf16[3072,768]{1,0:T(8,128)(2,1)}) %all-gather.11.cloned.1.call-update) | async-done | bytes 4718608 | tf_op jit(solution)/shard_map/all_gather | solution.py:59
  77.8 8.8 fusion.125
  88.9 68.3 %all-gather.15.cloned.1.call-done = bf16[1,768,5376]{2,1,0:T(8,128)(2,1)} async-done(((bf16[1,24,5376]{2,1,0:T(8,128)(2,1)}), bf16[1,768,5376]{2,1,0:T(8,128)(2,1)}) %all-gather.15.cloned.1.call-update) | async-done | bytes 8257552 | tf_op jit(solution)/shard_map/all_gather | solution.py:59
  157.2 7.8 add_convert_fusion.1.q_ref.k_ref.v_ref
  165.0 31.0 %attention_forward.2 = (bf16[1024,768]{1,0:T(8,128)(2,1)}, bf16[12,1024,1024]{2,1,0:T(8,128)(2,1)}, f32[1024,768]{1,0:T(8,128)}) custom-call(bf16[1024,2304]{1,0:T(8,128)(2,1)} %add_convert_fusion.1.q_ref.k_ref.v_ref, bf16[1024,2304]{1,0:T(8,128)(2,1)} %add_convert_fusion.1.q_ref.k_ref.v_ref, bf16[1024,2304]{1,0:T(8,128)(2,1)} %add_convert_fusion.1.q_ref.k_ref.v_ref, ...), custom_call_target="tpu_custom_call" | custom-call | flops 12884901888 | bytes 34603008 | tf_op jit(solution)/shard_map/attention_forward/pallas_call | solution.py:160
  196.0 30.9 %all-gather.17.cloned.1.call-done = bf16[1,3840,768]{2,1,0:T(8,128)(2,1)} async-done(((bf16[1,120,768]{2,1,0:T(8,128)(2,1)}), bf16[1,3840,768]{2,1,0:T(8,128)(2,1)}) %all-gather.17.cloned.1.call-update) | async-done | bytes 5898256 | tf_op jit(solution)/shard_map/all_gather | solution.py:59
  231.3 8.6 fusion.25
  240.0 11.1 fusion.116
  251.5 54.8 %all-gather.19.cloned.1.call-done = bf16[1,768,5376]{2,1,0:T(8,128)(2,1)} async-done(((bf16[1,24,5376]{2,1,0:T(8,128)(2,1)}), bf16[1,768,5376]{2,1,0:T(8,128)(2,1)}) %all-gather.19.cloned.1.call-update) | async-done | bytes 8257552 | tf_op jit(solution)/shard_map/all_gather | solution.py:59
  306.4 7.8 add_convert_fusion.q_ref.k_ref.v_ref
  314.1 31.2 %attention_forward.3 = (bf16[1024,768]{1,0:T(8,128)(2,1)}, bf16[12,1024,1024]{2,1,0:T(8,128)(2,1)}, f32[1024,768]{1,0:T(8,128)}) custom-call(bf16[1024,2304]{1,0:T(8,128)(2,1)} %add_convert_fusion.q_ref.k_ref.v_ref, bf16[1024,2304]{1,0:T(8,128)(2,1)} %add_convert_fusion.q_ref.k_ref.v_ref, bf16[1024,2304]{1,0:T(8,128)(2,1)} %add_convert_fusion.q_ref.k_ref.v_ref, ...), custom_call_target="tpu_custom_call" | custom-call | flops 12884901888 | bytes 34603008 | tf_op jit(solution)/shard_map/attention_forward/pallas_call | solution.py:160
  345.3 30.6 %all-gather.21.cloned.1.call-done = bf16[1,3840,768]{2,1,0:T(8,128)(2,1)} async-done(((bf16[1,120,768]{2,1,0:T(8,128)(2,1)}), bf16[1,3840,768]{2,1,0:T(8,128)(2,1)}) %all-gather.21.cloned.1.call-update) | async-done | bytes 5898256 | tf_op jit(solution)/shard_map/all_gather | solution.py:59
  375.9 4.4 fusion.117
  381.2 8.5 fusion.21
  389.8 10.0 fusion.118
  403.4 30.0 %all-gather.13.cloned.1.call-done = bf16[768,1000]{1,0:T(8,128)(2,1)} async-done(((bf16[24,1000]{1,0:T(8,128)(2,1)}), bf16[768,1000]{1,0:T(8,128)(2,1)}) %all-gather.13.cloned.1.call-update) | async-done | bytes 1536016 | tf_op jit(solution)/shard_map/all_gather | solution.py:59
  439.1 3.8 fusion.120
  442.9 3.7 copy.104
  446.5 4.5 multiply_reduce_fusion.4
  454.9 18.2 %convert_reduce_fusion = (f32[3072]{0:T(1024)}, bf16[1024,3072]{1,0:T(8,128)(2,1)}) fusion(f32[1024,3072]{1,0:T(8,128)} %fusion.21, f32[3072]{0:T(1024)S(1)} %copy-done.99, bf16[1024,768]{0,1:T(8,128)(2,1)S(1)} %get-tuple-element.126, bf16[1,3840,768]{2,1,0:T(8,128)(2,1)S(1)} %bitcast.129), kind=kOutput, calls=%fused_computation.18 | convolution fusion | flops 4904186880 | bytes 25190400 | tf_op jit(solution)/shard_map/dot_general | solution.py:53
  473.0 9.0 fusion.124
  492.3 4.7 convolution_convert_fusion.9.grad_ref
  497.0 29.0 %attention_backward.2 = bf16[1024,2304]{1,0:T(8,128)(2,1)} custom-call(bf16[1024,2304]{1,0:T(8,128)(2,1)} %add_convert_fusion.q_ref.k_ref.v_ref, bf16[1024,2304]{1,0:T(8,128)(2,1)} %add_convert_fusion.q_ref.k_ref.v_ref, bf16[1024,2304]{1,0:T(8,128)(2,1)} %add_convert_fusion.q_ref.k_ref.v_ref, bf16[12,1024,1024]{2,1,0:T(8,128)(2,1)} %get-tuple-element.32.expo_ref, ...), custom_call_target="tpu_custom_call" | custom-call | flops 25769803776 | bytes 40894464 | tf_op jit(solution)/shard_map/attention_backward/pallas_call | solution.py:235
  526.0 9.5 fusion.123
  535.5 3.7 copy.106
  539.2 3.5 multiply_reduce_fusion.1
  546.4 18.1 %convert_reduce_fusion.1 = (f32[3072]{0:T(1024)}, bf16[1024,3072]{1,0:T(8,128)(2,1)}) fusion(f32[1024,3072]{1,0:T(8,128)} %fusion.25, f32[3072]{0:T(1024)S(1)} %copy-done.97, bf16[1024,768]{0,1:T(8,128)(2,1)S(1)} %get-tuple-element.132, bf16[1,3840,768]{2,1,0:T(8,128)(2,1)S(1)} %bitcast.125), kind=kOutput, calls=%fused_computation.19 | convolution fusion | flops 4904186880 | bytes 25190400 | tf_op jit(solution)/shard_map/dot_general | solution.py:53
  564.5 8.9 fusion.122
  573.4 3.7 copy.107
  584.9 4.7 convolution_convert_fusion.8.grad_ref
  589.7 28.8 %attention_backward.3 = bf16[1024,2304]{1,0:T(8,128)(2,1)} custom-call(bf16[1024,2304]{1,0:T(8,128)(2,1)} %add_convert_fusion.1.q_ref.k_ref.v_ref, bf16[1024,2304]{1,0:T(8,128)(2,1)} %add_convert_fusion.1.q_ref.k_ref.v_ref, bf16[1024,2304]{1,0:T(8,128)(2,1)} %add_convert_fusion.1.q_ref.k_ref.v_ref, bf16[12,1024,1024]{2,1,0:T(8,128)(2,1)} %get-tuple-element.34.expo_ref, ...), custom_call_target="tpu_custom_call" | custom-call | flops 25769803776 | bytes 40894464 | tf_op jit(solution)/shard_map/attention_backward/pallas_call | solution.py:235
  618.5 9.5 fusion.121
  628.0 3.7 copy.108
  645.6 18.6 %concatenate.19 = f32[60906]{0:T(1024)S(1)} concatenate(f32[37632]{0:T(1024)S(1)} %reshape.441, f32[768]{0:T(1024)} %get-tuple-element.137, f32[768]{0:T(1024)} %get-tuple-element.92, f32[768]{0:T(1024)} %get-tuple-element.186, f32[1000]{0:T(1024)} %get-tuple-element.135, f32[768]{0:T(1024)} %get-tuple-element.90, f32[768]{0:T(1024)} %get-tuple-element.188, ...), dimensions={0} | concatenate | bytes 487248 | tf_op jit(solution)/shard_map/concatenate | solution.py:419
  667.6 9.1 fusion.14
  676.7 6.7 copy.116
  683.5 3.9 convolution_convert_fusion.10
  687.5 11.6 convolution_convert_fusion
  702.1 3.9 convolution_convert_fusion.11
  706.0 11.8 convolution_convert_fusion.2
  721.4 8.1 convolution_convert_fusion.6
  729.5 10.0 convolution_convert_fusion.3
  739.5 6.1 pad_maximum_fusion
  746.3 9.4 convolution_convert_fusion.5
  755.7 10.0 convolution_convert_fusion.1
  765.8 7.2 pad_maximum_fusion.1
  773.0 24.4 %reduce-scatter.10.cloned.1.call-done = f32[16,128]{1,0:T(8,128)} async-done(((f32[512,128]{1,0:T(8,128)}), f32[16,128]{1,0:T(8,128)}) %reduce-scatter.10.cloned.1.call-update) | async-done | bytes 8208 | tf_op jit(solution)/shard_map/reduce_scatter | solution.py:89
  797.4 65.4 %all_gather.49 = f32[512,128]{1,0:T(8,128)S(1)} all-gather(f32[16,128]{1,0:T(8,128)} %reduce-scatter.10.cloned.1.call-done), channel_id=1, replica_groups=mesh['dp'=4,'fsdp'=8] {'fsdp','dp'}, dimensions={0}, use_global_device_ids=true | all-gather | bytes 270336 | tf_op jit(solution)/shard_map/all_gather | solution.py:90
  866.7 30.1 %reduce-scatter.12.cloned.1.call-done = bf16[24,1000]{1,0:T(8,128)(2,1)} async-done(((bf16[768,1000]{1,0:T(8,128)(2,1)}), bf16[24,1000]{1,0:T(8,128)(2,1)}) %reduce-scatter.12.cloned.1.call-update) | async-done | bytes 48016 | tf_op jit(solution)/shard_map/reduce_scatter | solution.py:63
  896.8 10.0 all_gather.51
  908.2 101.0 %reduce-scatter.22.cloned.1.call-done = bf16[96,768]{1,0:T(8,128)(2,1)} async-done(((bf16[3072,768]{1,0:T(8,128)(2,1)}), bf16[96,768]{1,0:T(8,128)(2,1)}) %reduce-scatter.22.cloned.1.call-update) | async-done | bytes 147472 | tf_op jit(solution)/shard_map/reduce_scatter | solution.py:63
  1012.3 11.2 all_gather.50
  1023.5 103.1 %reduce-scatter.20.cloned.1.call-done = bf16[120,768]{1,0:T(8,128)(2,1)} async-done(((bf16[3840,768]{1,0:T(8,128)(2,1)}), bf16[120,768]{1,0:T(8,128)(2,1)}) %reduce-scatter.20.cloned.1.call-update) | async-done | bytes 184336 | tf_op jit(solution)/shard_map/reduce_scatter | solution.py:63
  1128.2 116.0 %reduce-scatter.16.cloned.1.call-done = bf16[120,768]{1,0:T(8,128)(2,1)} async-done(((bf16[3840,768]{1,0:T(8,128)(2,1)}), bf16[120,768]{1,0:T(8,128)(2,1)}) %reduce-scatter.16.cloned.1.call-update) | async-done | bytes 184336 | tf_op jit(solution)/shard_map/reduce_scatter | solution.py:63
  1245.8 12.1 all_gather.55
  1257.9 121.4 %reduce-scatter.14.cloned.1.call-done = bf16[24,5376]{1,0:T(8,128)(2,1)} async-done(((bf16[768,5376]{1,0:T(8,128)(2,1)}), bf16[24,5376]{1,0:T(8,128)(2,1)}) %reduce-scatter.14.cloned.1.call-update) | async-done | bytes 258064 | tf_op jit(solution)/shard_map/reduce_scatter | solution.py:63
  1382.3 133.4 %reduce-scatter.18.cloned.1.call-done = bf16[24,5376]{1,0:T(8,128)(2,1)} async-done(((bf16[768,5376]{1,0:T(8,128)(2,1)}), bf16[24,5376]{1,0:T(8,128)(2,1)}) %reduce-scatter.18.cloned.1.call-update) | async-done | bytes 258064 | tf_op jit(solution)/shard_map/reduce_scatter | solution.py:63
  1518.7 12.1 all_gather.54
  1530.8 39.3 %psum.7 = f32[]{:T(128)} all-reduce(f32[]{:T(128)S(6)} %add.524), channel_id=1, replica_groups=mesh['dp'=4,'fsdp'=8] {'dp','fsdp'}, use_global_device_ids=true, to_apply=%region_63.64 | all-reduce | flops 1 | bytes 8 | tf_op jit(solution)/shard_map/psum | solution.py:431
  1586.5 5.6 multiply_subtract_fusion.1
  1592.0 14.1 all_gather.53
  1606.1 13.1 all_gather.52
  1619.3 6.2 multiply_subtract_fusion
  (432 shorter events, 112.2 us)
Async XLA Ops:
  7.2 70.6 %all-gather.11.cloned.1.call-start = ((), (), s32[]{:S(2)}) async-start(), calls=%async_computation.7 | async-start | bytes 4866048 | tf_op jit(solution)/shard_map/all_gather | solution.py:59
  9.1 148.1 %all-gather.15.cloned.1.call-start = ((), (), s32[]{:S(2)}) async-start(), calls=%async_computation.15 | async-start | bytes 8515584 | tf_op jit(solution)/shard_map/all_gather | solution.py:59
  13.2 25.9 %copy-start.59 = (f32[3304]{0:T(1024)S(1)}, f32[3304]{0:T(1024)}, u32[]{:S(2)}) copy-start(f32[3304]{0:T(1024)} %param.35) | copy-start | bytes 39652
  13.2 28.3 %copy-start.125 = (s32[1,8]{1,0:T(1,128)S(1)}, s32[1,8]{1,0:T(1,128)}, u32[]{:S(2)}) copy-start(s32[1,8]{1,0:T(1,128)} %param.27) | copy-start | bytes 100
  13.2 213.7 %all-gather.17.cloned.1.call-start = ((), (), s32[]{:S(2)}) async-start(), calls=%async_computation.16 | async-start | bytes 6082560 | tf_op jit(solution)/shard_map/all_gather | solution.py:59
  13.3 28.7 %copy-start.44 = (f32[49,768]{1,0:T(8,128)S(1)}, f32[49,768]{1,0:T(8,128)}, u32[]{:S(2)}) copy-start(f32[49,768]{1,0:T(8,128)} %param.34) | copy-start | bytes 451588
  15.0 291.3 %all-gather.19.cloned.1.call-start = ((), (), s32[]{:S(2)}) async-start(), calls=%async_computation.17 | async-start | bytes 8515584 | tf_op jit(solution)/shard_map/all_gather | solution.py:59
  16.8 359.2 %all-gather.21.cloned.1.call-start = ((), (), s32[]{:S(2)}) async-start(), calls=%async_computation.18 | async-start | bytes 6082560 | tf_op jit(solution)/shard_map/all_gather | solution.py:59
  18.5 414.9 %all-gather.13.cloned.1.call-start = ((), (), s32[]{:S(2)}) async-start(), calls=%async_computation.8 | async-start | bytes 1622016 | tf_op jit(solution)/shard_map/all_gather | solution.py:59
  20.1 777.3 %reduce-scatter.10.cloned.1.call-start = ((), (), s32[]{:S(2)}) async-start(), calls=%async_computation.9 | async-start | bytes 270336 | tf_op jit(solution)/shard_map/reduce_scatter | solution.py:89
  20.3 21.7 %copy-start.107 = (s32[8]{0:T(128)}, s32[8]{0:T(128)S(1)}, u32[]{:S(2)}) copy-start(s32[8]{0:T(128)S(1)} %convert_reduce_fusion.10) | copy-start | bytes 100
  36.5 50.1 %copy-start.45 = (f32[9984]{0:T(1024)}, f32[9984]{0:T(1024)S(1)}, u32[]{:S(2)}) copy-start(f32[9984]{0:T(1024)S(1)} %reshape.445) | copy-start | bytes 119812
  37.2 193.7 %copy-start.61 = (f32[768]{0:T(1024)}, f32[768]{0:T(1024)S(1)}, u32[]{:S(2)}) copy-start(f32[768]{0:T(1024)S(1)} %get-tuple-element.159) | copy-start | bytes 9220
  37.9 48.8 %copy-start.46 = (f32[9984]{0:T(1024)}, f32[9984]{0:T(1024)S(1)}, u32[]{:S(2)}) copy-start(f32[9984]{0:T(1024)S(1)} %reshape.446) | copy-start | bytes 119812
  38.5 451.8 %copy-start.57 = (f32[768]{0:T(1024)}, f32[768]{0:T(1024)S(1)}, u32[]{:S(2)}) copy-start(f32[768]{0:T(1024)S(1)} %get-tuple-element.153) | copy-start | bytes 9220
  42.1 44.6 %copy-start.33 = (f32[1024,49]{0,1:T(8,128)}, f32[1024,49]{0,1:T(8,128)S(1)}, u32[]{:S(2)}) copy-start(f32[1024,49]{0,1:T(8,128)S(1)} %mul.681) | copy-start | bytes 602116
  43.1 43.5 %copy-start.95 = (f32[768]{0:T(1024)S(1)}, f32[768]{0:T(1024)}, u32[]{:S(2)}) copy-start(f32[768]{0:T(1024)} %get-tuple-element.169) | copy-start | bytes 9220
  88.4 138.5 %copy-start = (f32[1024,768]{0,1:T(8,128)}, f32[1024,768]{0,1:T(8,128)S(1)}, u32[]{:S(2)}) copy-start(f32[1024,768]{0,1:T(8,128)S(1)} %get-tuple-element.175) | copy-start | bytes 9437188
  88.4 68.8 %slice-start.4 = ((f32[9984]{0:T(1024)}), f32[2304]{0:T(1024)S(1)}, s32[]{:S(2)}) async-start(f32[9984]{0:T(1024)} %copy-done.45), calls=%async_computation.24 | async-start | bytes 24576 | tf_op jit(solution)/shard_map/slice | solution.py:263
  88.5 68.8 %copy-start.83 = (f32[768]{0:T(1024)S(1)}, f32[768]{0:T(1024)}, u32[]{:S(2)}) copy-start(f32[768]{0:T(1024)} %get-tuple-element.164) | copy-start | bytes 9220
  88.5 68.7 %copy-start.115 = (f32[768]{0:T(1024)S(1)}, f32[768]{0:T(1024)}, u32[]{:S(2)}) copy-start(f32[768]{0:T(1024)} %get-tuple-element.163) | copy-start | bytes 9220
  88.5 76.5 %copy-start.64 = (f32[1024]{0:T(1024)}, f32[1024]{0:T(1024)S(1)}, u32[]{:S(2)}) copy-start(f32[1024]{0:T(1024)S(1)} %broadcast_multiply_fusion.5) | copy-start | bytes 12292
  88.9 76.1 %copy-start.77 = (f32[1024]{0:T(1024)}, f32[1024]{0:T(1024)S(1)}, u32[]{:S(2)}) copy-start(f32[1024]{0:T(1024)S(1)} %multiply_reduce_fusion.14) | copy-start | bytes 12292
  88.9 76.1 %copy-start.86 = (f32[1024]{0:T(1024)}, f32[1024]{0:T(1024)S(1)}, u32[]{:S(2)}) copy-start(f32[1024]{0:T(1024)S(1)} %fusion.81) | copy-start | bytes 12292
  165.0 61.9 %copy-start.120 = (f32[768]{0:T(1024)S(1)}, f32[768]{0:T(1024)}, u32[]{:S(2)}) copy-start(f32[768]{0:T(1024)} %get-tuple-element.162) | copy-start | bytes 9220
  251.1 63.1 %copy-start.13 = (f32[1024,768]{0,1:T(8,128)}, f32[1024,768]{0,1:T(8,128)S(1)}, u32[]{:S(2)}) copy-start(f32[1024,768]{0,1:T(8,128)S(1)} %get-tuple-element.179) | copy-start | bytes 9437188
  251.1 55.3 %slice-start.5 = ((f32[9984]{0:T(1024)}), f32[2304]{0:T(1024)S(1)}, s32[]{:S(2)}) async-start(f32[9984]{0:T(1024)} %copy-done.46), calls=%async_computation.25 | async-start | bytes 24576 | tf_op jit(solution)/shard_map/slice | solution.py:263
  251.1 55.3 %copy-start.81 = (f32[768]{0:T(1024)S(1)}, f32[768]{0:T(1024)}, u32[]{:S(2)}) copy-start(f32[768]{0:T(1024)} %get-tuple-element.158) | copy-start | bytes 9220
  251.1 55.3 %copy-start.111 = (f32[768]{0:T(1024)S(1)}, f32[768]{0:T(1024)}, u32[]{:S(2)}) copy-start(f32[768]{0:T(1024)} %get-tuple-element.157) | copy-start | bytes 9220
  251.1 291.6 %copy-start.67 = (f32[1024]{0:T(1024)}, f32[1024]{0:T(1024)S(1)}, u32[]{:S(2)}) copy-start(f32[1024]{0:T(1024)S(1)} %broadcast_multiply_fusion.3) | copy-start | bytes 12292
  251.5 291.2 %copy-start.89 = (f32[1024]{0:T(1024)}, f32[1024]{0:T(1024)S(1)}, u32[]{:S(2)}) copy-start(f32[1024]{0:T(1024)S(1)} %fusion.83) | copy-start | bytes 12292
  314.1 61.8 %copy-start.118 = (f32[768]{0:T(1024)S(1)}, f32[768]{0:T(1024)}, u32[]{:S(2)}) copy-start(f32[768]{0:T(1024)} %get-tuple-element.156) | copy-start | bytes 9220
  380.3 110.0 %copy-start.5 = (f32[1024,768]{0,1:T(8,128)}, f32[1024,768]{0,1:T(8,128)S(1)}, u32[]{:S(2)}) copy-start(f32[1024,768]{0,1:T(8,128)S(1)} %get-tuple-element.181) | copy-start | bytes 9437188
  380.3 109.9 %copy-start.52 = (f32[1024]{0:T(1024)}, f32[1024]{0:T(1024)S(1)}, u32[]{:S(2)}) copy-start(f32[1024]{0:T(1024)S(1)} %broadcast_multiply_fusion.2) | copy-start | bytes 12292
  380.8 109.5 %copy-start.72 = (f32[1024]{0:T(1024)}, f32[1024]{0:T(1024)S(1)}, u32[]{:S(2)}) copy-start(f32[1024]{0:T(1024)S(1)} %fusion.84) | copy-start | bytes 12292
  399.8 33.5 %copy-start.91 = (f32[1000]{0:T(1024)S(1)}, f32[1000]{0:T(1024)}, u32[]{:S(2)}) copy-start(f32[1000]{0:T(1024)} %slice.223) | copy-start | bytes 12004
  400.2 35.0 %copy-start.121 = (s32[1,8]{1,0:T(1,128)S(1)}, s32[1,8]{1,0:T(1,128)}, u32[]{:S(2)}) copy-start(s32[1,8]{1,0:T(1,128)} %param.28) | copy-start | bytes 100
  400.2 35.7 %copy-start.123 = (f32[8]{0:T(128)S(1)}, f32[8]{0:T(128)}, u32[]{:S(2)}) copy-start(f32[8]{0:T(128)} %get-tuple-element.170) | copy-start | bytes 100
  403.4 39.5 %copy-start.50 = (bf16[8,768]{1,0:T(8,128)(2,1)}, bf16[8,768]{1,0:T(8,128)(2,1)S(1)}, u32[]{:S(2)}) copy-start(bf16[8,768]{1,0:T(8,128)(2,1)S(1)} %fusion.51) | copy-start | bytes 36868
  435.2 11.3 copy-start.103
  435.9 10.6 copy-start.105
  453.7 19.3 %slice-start.8 = ((s8[8257536]{0:T(1024)(128)(4,1)}), s8[4194304]{0:T(1024)(128)(4,1)S(1)}, s32[]{:S(2)}) async-start(s8[8257536]{0:T(1024)(128)(4,1)} %bitcast.121), calls=%async_computation.28 | async-start | bytes 8388608
  454.6 18.4 %copy-start.35 = (bf16[1024,768]{0,1:T(8,128)(2,1)}, bf16[1024,768]{0,1:T(8,128)(2,1)S(1)}, u32[]{:S(2)}) copy-start(bf16[1024,768]{0,1:T(8,128)(2,1)S(1)} %get-tuple-element.126) | copy-start | bytes 4718596
  454.9 18.2 %slice-start.9 = ((s8[8257536]{0:T(1024)(128)(4,1)}), s8[4063232]{0:T(1024)(128)(4,1)S(1)}, s32[]{:S(2)}) async-start(s8[8257536]{0:T(1024)(128)(4,1)} %bitcast.121), calls=%async_computation.29 | async-start | bytes 8126464
  544.7 19.8 %slice-start.6 = ((s8[8257536]{0:T(1024)(128)(4,1)}), s8[4194304]{0:T(1024)(128)(4,1)S(1)}, s32[]{:S(2)}) async-start(s8[8257536]{0:T(1024)(128)(4,1)} %bitcast.115), calls=%async_computation.26 | async-start | bytes 8388608
  545.7 18.7 %copy-start.37 = (bf16[1024,768]{0,1:T(8,128)(2,1)}, bf16[1024,768]{0,1:T(8,128)(2,1)S(1)}, u32[]{:S(2)}) copy-start(bf16[1024,768]{0,1:T(8,128)(2,1)S(1)} %get-tuple-element.132) | copy-start | bytes 4718596
  546.4 18.1 %slice-start.7 = ((s8[8257536]{0:T(1024)(128)(4,1)}), s8[4063232]{0:T(1024)(128)(4,1)S(1)}, s32[]{:S(2)}) async-start(s8[8257536]{0:T(1024)(128)(4,1)} %bitcast.115), calls=%async_computation.27 | async-start | bytes 8126464
  643.7 21.3 %copy-start.51 = (bf16[8,768]{1,0:T(8,128)(2,1)S(1)}, bf16[8,768]{1,0:T(8,128)(2,1)}, u32[]{:S(2)}) copy-start(bf16[8,768]{1,0:T(8,128)(2,1)} %copy-done.50) | copy-start | bytes 36868
  665.0 231.8 %reduce-scatter.12.cloned.1.call-start = ((), (), s32[]{:S(2)}) async-start(), calls=%async_computation.10 | async-start | bytes 1622016 | tf_op jit(solution)/shard_map/reduce_scatter | solution.py:63
  667.5 341.7 %reduce-scatter.22.cloned.1.call-start = ((), (), s32[]{:S(2)}) async-start(), calls=%async_computation.19 | async-start | bytes 4866048 | tf_op jit(solution)/shard_map/reduce_scatter | solution.py:63
  683.4 443.1 %reduce-scatter.20.cloned.1.call-start = ((), (), s32[]{:S(2)}) async-start(), calls=%async_computation.14 | async-start | bytes 6082560 | tf_op jit(solution)/shard_map/reduce_scatter | solution.py:63
  702.0 542.2 %reduce-scatter.16.cloned.1.call-start = ((), (), s32[]{:S(2)}) async-start(), calls=%async_computation.12 | async-start | bytes 6082560 | tf_op jit(solution)/shard_map/reduce_scatter | solution.py:63
  720.8 658.6 %reduce-scatter.14.cloned.1.call-start = ((), (), s32[]{:S(2)}) async-start(), calls=%async_computation.11 | async-start | bytes 8515584 | tf_op jit(solution)/shard_map/reduce_scatter | solution.py:63
  745.6 10.1 copy-start.6
  745.6 10.1 copy-start.53
  745.7 770.0 %reduce-scatter.18.cloned.1.call-start = ((), (), s32[]{:S(2)}) async-start(), calls=%async_computation.13 | async-start | bytes 8515584 | tf_op jit(solution)/shard_map/reduce_scatter | solution.py:63
  773.0 803.4 %copy-start.60 = (f32[3304]{0:T(1024)S(1)}, f32[3304]{0:T(1024)}, u32[]{:S(2)}) copy-start(f32[3304]{0:T(1024)} %param.35) | copy-start | bytes 39652
  773.0 803.4 %copy-start.93 = (f32[3304]{0:T(1024)S(1)}, f32[3304]{0:T(1024)}, u32[]{:S(2)}) copy-start(f32[3304]{0:T(1024)} %param.49) | copy-start | bytes 39652
  773.0 803.4 %copy-start.94 = (f32[3304]{0:T(1024)S(1)}, f32[3304]{0:T(1024)}, u32[]{:S(2)}) copy-start(f32[3304]{0:T(1024)} %param.42) | copy-start | bytes 39652
  1257.9 324.0 %copy-start.39 = (f32[384,768]{1,0:T(8,128)S(1)}, f32[384,768]{1,0:T(8,128)}, u32[]{:S(2)}) copy-start(f32[384,768]{1,0:T(8,128)} %param.29) | copy-start | bytes 3538948
  1586.4 19.7 %copy-start.42 = (bf16[24,5376]{1,0:T(8,128)(2,1)S(1)}, bf16[24,5376]{1,0:T(8,128)(2,1)}, u32[]{:S(2)}) copy-start(bf16[24,5376]{1,0:T(8,128)(2,1)} %reduce-scatter.14.cloned.1.call-done) | copy-start | bytes 774148
  1586.4 32.8 %copy-start.25 = (f32[2,96,5376]{2,1,0:T(8,128)S(1)}, f32[2,96,5376]{2,1,0:T(8,128)}, u32[]{:S(2)}) copy-start(f32[2,96,5376]{2,1,0:T(8,128)} %param.31) | copy-start | bytes 12386308
  1586.4 32.8 %copy-start.28 = (f32[2,96,5376]{2,1,0:T(8,128)S(1)}, f32[2,96,5376]{2,1,0:T(8,128)}, u32[]{:S(2)}) copy-start(f32[2,96,5376]{2,1,0:T(8,128)} %param.45) | copy-start | bytes 12386308
  1586.4 32.8 %copy-start.29 = (f32[2,96,5376]{2,1,0:T(8,128)S(1)}, f32[2,96,5376]{2,1,0:T(8,128)}, u32[]{:S(2)}) copy-start(f32[2,96,5376]{2,1,0:T(8,128)} %param.38) | copy-start | bytes 12386308
  (93 other events, 409.6 us)
Sparse Core Ops, SparseCore 0:
  11.5 66.2 all-gather.10
  81.3 75.8 all-gather.14
  160.7 66.2 all-gather.16
  230.3 76.0 all-gather.18
  309.7 66.2 all-gather.20
  379.2 54.0 all-gather.12
  665.1 132.2 reduce-scatter.9
  803.5 93.2 reduce-scatter.11
  903.2 106.0 reduce-scatter.21
  1014.7 111.8 reduce-scatter.19
  1132.2 111.9 reduce-scatter.15
  1249.9 129.3 reduce-scatter.13
  1386.2 129.4 reduce-scatter.17

commit v2 on v1

--- a/solution.py
+++ b/solution.py
@@ -31,7 +31,7 @@
 PAIR = 2 * HD
 MASKED = -1e30
 VMEM_LIMIT = 56 * 1024 * 1024
-AXES = ("fsdp", "dp")
+MESH = pl.DeviceIdType.MESH
 LANES = 128
 
 
@@ -53,41 +53,9 @@
     return jnp.dot(left, right, preferred_element_type=jnp.float32)
 
 
-def gather_rows(shard):
-    share = shard.shape[0] // lax.axis_size("dp")
-    mine = lax.dynamic_slice_in_dim(shard, lax.axis_index("dp") * share, share, 0)
-    return lax.all_gather(mine.astype(jnp.bfloat16), AXES, axis=0, tiled=True)
-
-
-def scatter_rows(partial_sum):
-    return lax.psum_scatter(
-        partial_sum.astype(jnp.bfloat16), AXES, scatter_dimension=0, tiled=True
-    )
-
-
-def regather(shares):
-    return lax.all_gather(shares, "dp", axis=0, tiled=True).astype(jnp.float32)
-
-
 def padded_rows(flat, multiple):
     extra = -flat.shape[0] % (multiple * LANES)
     return jnp.pad(flat, (0, extra)).reshape(-1, LANES)
-
-
-def gather_vectors(shard):
-    size = shard.size
-    full = lax.all_gather(
-        padded_rows(shard.astype(jnp.bfloat16).reshape(-1), 16), "fsdp", axis=0, tiled=True
-    )
-    owners = lax.axis_size("fsdp")
-    full = full.reshape(owners, -1)[:, :size].reshape(owners, *shard.shape)
-    return jnp.swapaxes(full, 0, 1).reshape(shard.shape[0], -1)
-
-
-def total_flat(flat):
-    rows = padded_rows(flat, 16 * lax.axis_size("dp") * lax.axis_size("fsdp"))
-    share = lax.psum_scatter(rows, AXES, scatter_dimension=0, tiled=True)
-    return lax.all_gather(share, AXES, axis=0, tiled=True).reshape(-1)[: flat.shape[0]]
 
 
 def row_layout(seg_row, patch_row):
@@ -116,6 +84,443 @@
         row_count, GRID * GRID
     )
     return (weights, member.astype(jnp.float32), counts.astype(jnp.float32))
+
+
+TURNS = (1, 2, 3)
+
+
+def place():
+    slot = lax.axis_index("fsdp")
+    return lax.axis_index("dp"), lax.div(slot, 2), lax.rem(slot, 2)
+
+
+def partner(index, turn):
+    if turn == 0:
+        return index
+    if turn == 1:
+        return index + 1 - 2 * lax.rem(index, 2)
+    if turn == 2:
+        return lax.rem(index + 2, 4)
+    return 3 - index
+
+
+def greet():
+    group, level, core = place()
+    barrier = pltpu.get_barrier_semaphore()
+    peers = [(group, 2 * level + 1 - core)]
+    for turn in TURNS:
+        peers.append((group, 2 * partner(level, turn) + core))
+        peers.append((partner(group, turn), 2 * level + core))
+    for peer in peers:
+        pl.semaphore_signal(barrier, inc=1, device_id=peer, device_id_type=MESH)
+    pl.semaphore_wait(barrier, len(peers))
+
+
+def quarter_shape(rows, columns):
+    if columns % (2 * LANES) == 0:
+        return rows // 2, columns // 2
+    return rows // 4, columns
+
+
+def quarter(index, rows, columns):
+    high, wide = quarter_shape(rows, columns)
+    if wide == columns:
+        return pl.ds(pl.multiple_of(index * high, high), high), pl.ds(0, columns)
+    return (
+        pl.ds(pl.multiple_of(lax.div(index, 2) * high, high), high),
+        pl.ds(pl.multiple_of(lax.rem(index, 2) * wide, wide), wide),
+    )
+
+
+def remote(source, target, send, receive, device):
+    return pltpu.make_async_remote_copy(
+        src_ref=source,
+        dst_ref=target,
+        send_sem=send,
+        recv_sem=receive,
+        device_id=device,
+        device_id_type=MESH,
+    )
+
+
+GATHER_SEMS = 33
+
+
+class Gather:
+    def __init__(self, shard, out, sems, split):
+        self.shard, self.out, self.sems, self.split = shard, out, sems, split
+        self.rows, self.columns = shard.shape
+
+    def level_copy(self, turn):
+        group, level, core = place()
+        block = self.out.at[2 * level + core]
+        source = self.shard
+        if self.split:
+            part = quarter(group, self.rows, self.columns)
+            source, block = source.at[part], block.at[part]
+        sems = self.sems
+        peer = (group, 2 * partner(level, turn) + core)
+        return remote(source, block, sems.at[turn], sems.at[3 + turn], peer)
+
+    def group_copy(self, turn, other):
+        group, level, core = place()
+        part = quarter(group, self.rows, self.columns)
+        block = self.out.at[2 * partner(level, turn) + core].at[part]
+        index = 3 * (turn - 1) + other - 1
+        peer = (partner(group, other), 2 * level + core)
+        return remote(block, block, self.sems.at[7 + index], self.sems.at[16 + index], peer)
+
+    def core_copy(self, turn):
+        group, level, core = place()
+        slot = 2 * partner(level, turn) + core
+        source = self.shard if turn == 0 else self.out.at[slot]
+        peer = (group, 2 * level + 1 - core)
+        return remote(source, self.out.at[slot], self.sems.at[25 + turn], self.sems.at[29 + turn], peer)
+
+    def own_copy(self):
+        _, level, core = place()
+        return pltpu.make_async_copy(self.shard, self.out.at[2 * level + core], self.sems.at[0])
+
+    def first(self):
+        for turn in TURNS:
+            self.level_copy(turn).start()
+        self.core_copy(0).start()
+        self.own_copy().start()
+
+    def second(self):
+        for turn in TURNS:
+            self.level_copy(turn).wait_recv()
+            if self.split:
+                for other in TURNS:
+                    self.group_copy(turn, other).start()
+            else:
+                self.core_copy(turn).start()
+
+    def third(self):
+        if not self.split:
+            return
+        for turn in TURNS:
+            for other in TURNS:
+                self.group_copy(turn, other).wait_recv()
+            self.core_copy(turn).start()
+
+    def fourth(self):
+        for turn in (0, *TURNS):
+            self.core_copy(turn).wait_recv()
+        for turn in TURNS:
+            self.level_copy(turn).wait_send()
+            if self.split:
+                for other in TURNS:
+                    self.group_copy(turn, other).wait_send()
+        for turn in (0, *TURNS):
+            self.core_copy(turn).wait_send()
+        self.own_copy().wait()
+
+
+def gather_kernel(*refs, split):
+    count = len(split)
+    sems = refs[2 * count]
+    jobs = [
+        Gather(refs[i], refs[count + i], sems.at[i], split[i]) for i in range(count)
+    ]
+    greet()
+    for stage in ("first", "second", "third", "fourth"):
+        for job in jobs:
+            getattr(job, stage)()
+
+
+def gather_call(shards, split, collective_id):
+    count = len(shards)
+    owners = lax.axis_size("fsdp")
+    anywhere = pl.BlockSpec(memory_space=pl.ANY)
+    full = pl.pallas_call(
+        functools.partial(gather_kernel, split=split),
+        in_specs=[anywhere] * count,
+        out_specs=[anywhere] * count,
+        out_shape=[jax.ShapeDtypeStruct((owners, *s.shape), s.dtype) for s in shards],
+        scratch_shapes=[pltpu.SemaphoreType.DMA((count, GATHER_SEMS))],
+        compiler_params=pltpu.CompilerParams(
+            collective_id=collective_id, has_side_effects=True, vmem_limit_bytes=VMEM_LIMIT
+        ),
+        name="gather_weights",
+    )(*shards)
+    return [f.reshape(owners * f.shape[1], f.shape[2]) for f in full]
+
+
+REDUCE_SEMS = 48
+
+
+class Reduce:
+    def __init__(self, grad, out, scratch, sems):
+        self.grad, self.out, self.sems = grad, out, sems
+        self.own, self.got_core, self.got_group, self.part, self.got_level = scratch
+        self.rows, self.columns = out.shape
+        self.chunk = 16
+
+    def load(self, level):
+        _, _, core = place()
+        return pltpu.make_async_copy(
+            self.grad.at[2 * level + core], self.own.at[level], self.sems.at[level]
+        )
+
+    def core_copy(self, target_level):
+        group, level, core = place()
+        return remote(
+            self.grad.at[2 * target_level + 1 - core],
+            self.got_core.at[target_level],
+            self.sems.at[4 + target_level],
+            self.sems.at[8 + target_level],
+            (group, 2 * level + 1 - core),
+        )
+
+    def group_copy(self, turn, other):
+        group, level, core = place()
+        target = partner(level, turn)
+        peer = partner(group, other)
+        part = quarter(peer, self.rows, self.columns)
+        index = 3 * turn + other - 1
+        return remote(
+            self.own.at[target].at[part],
+            self.got_group.at[other - 1, target],
+            self.sems.at[12 + index],
+            self.sems.at[24 + index],
+            (peer, 2 * level + core),
+        )
+
+    def level_copy(self, turn):
+        group, level, core = place()
+        target = partner(level, turn)
+        return remote(
+            self.part.at[target],
+            self.got_level.at[turn - 1],
+            self.sems.at[35 + turn],
+            self.sems.at[38 + turn],
+            (group, 2 * target + core),
+        )
+
+    def share_copy(self, other):
+        group, level, core = place()
+        mine = self.out.at[quarter(group, self.rows, self.columns)]
+        return remote(
+            mine,
+            mine,
+            self.sems.at[41 + other],
+            self.sems.at[44 + other],
+            (partner(group, other), 2 * level + core),
+        )
+
+    def first(self):
+        _, level, _ = place()
+        for turn in (*TURNS, 0):
+            self.core_copy(partner(level, turn)).start()
+            self.load(partner(level, turn)).start()
+
+    def second(self):
+        _, level, _ = place()
+        for turn in (*TURNS, 0):
+            target = partner(level, turn)
+            self.load(target).wait()
+            self.core_copy(target).wait_recv()
+
+            def add(step, carry):
+                rows = pl.ds(pl.multiple_of(step * self.chunk, self.chunk), self.chunk)
+                total = self.own[target, rows, :].astype(jnp.float32)
+                total = total + self.got_core[target, rows, :].astype(jnp.float32)
+                self.own[target, rows, :] = total.astype(self.own.dtype)
+                return carry
+
+            lax.fori_loop(0, self.rows // self.chunk, add, 0)
+            for other in TURNS:
+                self.group_copy(turn, other).start()
+
+    def third(self):
+        group, level, _ = place()
+        high, wide = quarter_shape(self.rows, self.columns)
+        row_part, column_part = quarter(group, self.rows, self.columns)
+        for turn in (*TURNS, 0):
+            target = partner(level, turn)
+            for other in TURNS:
+                self.group_copy(turn, other).wait_recv()
+
+            def add(step, carry):
+                at = pl.multiple_of(step * self.chunk, self.chunk)
+                rows = pl.ds(at, self.chunk)
+                mine = pl.ds(pl.multiple_of(row_part.start + at, self.chunk), self.chunk)
+                total = self.own[target, mine, column_part].astype(jnp.float32)
+                for slot in range(3):
+                    total = total + self.got_group[slot, target, rows, :].astype(jnp.float32)
+                self.part[target, rows, :] = total.astype(self.part.dtype)
+                return carry
+
+            lax.fori_loop(0, high // self.chunk, add, 0)
+            if turn:
+                self.level_copy(turn).start()
+
+    def fourth(self):
+        group, level, _ = place()
+        high, wide = quarter_shape(self.rows, self.columns)
+        row_part, column_part = quarter(group, self.rows, self.columns)
+        for turn in TURNS:
+            self.level_copy(turn).wait_recv()
+
+        def add(step, carry):
+            at = pl.multiple_of(step * self.chunk, self.chunk)
+            rows = pl.ds(at, self.chunk)
+            mine = pl.ds(pl.multiple_of(row_part.start + at, self.chunk), self.chunk)
+            total = self.part[level, rows, :].astype(jnp.float32)
+            for slot in range(3):
+                total = total + self.got_level[slot, rows, :].astype(jnp.float32)
+            self.out[mine, column_part] = total.astype(self.out.dtype)
+            return carry
+
+        lax.fori_loop(0, high // self.chunk, add, 0)
+        for other in TURNS:
+            self.share_copy(other).start()
+
+    def fifth(self):
+        for other in TURNS:
+            self.share_copy(other).wait_recv()
+
+    def sixth(self):
+        _, level, _ = place()
+        for turn in (*TURNS, 0):
+            self.core_copy(partner(level, turn)).wait_send()
+            for other in TURNS:
+                self.group_copy(turn, other).wait_send()
+            if turn:
+                self.level_copy(turn).wait_send()
+                self.share_copy(turn).wait_send()
+
+
+class Spread:
+    def __init__(self, full, sems):
+        self.full, self.sems = full, sems
+
+    def level_copy(self, turn):
+        group, level, core = place()
+        block = self.full.at[2 * level + core]
+        peer = (group, 2 * partner(level, turn) + core)
+        return remote(block, block, self.sems.at[turn - 1], self.sems.at[2 + turn], peer)
+
+    def core_copy(self, turn):
+        group, level, core = place()
+        block = self.full.at[2 * partner(level, turn) + core]
+        peer = (group, 2 * level + 1 - core)
+        return remote(block, block, self.sems.at[6 + turn], self.sems.at[10 + turn], peer)
+
+    def run(self):
+        for turn in TURNS:
+            self.level_copy(turn).start()
+        self.core_copy(0).start()
+        for turn in TURNS:
+            self.level_copy(turn).wait_recv()
+            self.core_copy(turn).start()
+        for turn in (0, *TURNS):
+            self.core_copy(turn).wait_recv()
+        for turn in (0, *TURNS):
+            self.core_copy(turn).wait_send()
+            if turn:
+                self.level_copy(turn).wait_send()
+
+
+def reduce_kernel(*refs, count, spread):
+    grads, refs = refs[:count], refs[count:]
+    squares = None
+    if spread:
+        squares, refs = refs[0], refs[1:]
+    outs, refs = refs[:count], refs[count:]
+    if spread:
+        full, refs = refs[0], refs[1:]
+    sems, refs = refs[0], refs[1:]
+    if spread:
+        spread_sems, refs = refs[0], refs[1:]
+    jobs = [
+        Reduce(grads[i], outs[i], refs[5 * i : 5 * i + 5], sems.at[i]) for i in range(count)
+    ]
+    greet()
+    for stage in ("first", "second", "third", "fourth", "fifth"):
+        for job in jobs:
+            getattr(job, stage)()
+    if spread:
+        _, level, core = place()
+        total = squares[...]
+        for out in outs[:-1]:
+            for step in range(out.shape[0] // 16):
+                piece = out[step * 16 : step * 16 + 16, :].astype(jnp.float32)
+                piece = jnp.sum(piece * piece, 0, keepdims=True)
+                for lane in range(0, out.shape[1], LANES):
+                    total = total + piece[:, lane : lane + LANES]
+        mine = 2 * level + core
+        last = outs[-1].shape[0] - 1
+        full[mine] = outs[-1][...]
+        full[mine, last : last + 1, :] = total
+        Spread(full, spread_sems).run()
+    for job in jobs:
+        job.sixth()
+
+
+def reduce_call(grads, collective_id, squares=None):
+    count = len(grads)
+    spread = squares is not None
+    anywhere = pl.BlockSpec(memory_space=pl.ANY)
+    in_vmem = pl.BlockSpec(memory_space=pltpu.VMEM)
+    scratch = [pltpu.SemaphoreType.DMA((count, REDUCE_SEMS))]
+    if spread:
+        scratch.append(pltpu.SemaphoreType.DMA((14,)))
+    for grad in grads:
+        _, rows, columns = grad.shape
+        high, wide = quarter_shape(rows, columns)
+        for shape in ((4, rows, columns), (4, rows, columns), (3, 4, high, wide), (4, high, wide), (3, high, wide)):
+            scratch.append(pltpu.VMEM(shape, grad.dtype))
+    out_shape = [jax.ShapeDtypeStruct(g.shape[1:], g.dtype) for g in grads]
+    operands = list(grads)
+    if spread:
+        out_shape.append(jax.ShapeDtypeStruct(grads[-1].shape, grads[-1].dtype))
+        operands.append(squares)
+    return pl.pallas_call(
+        functools.partial(reduce_kernel, count=count, spread=spread),
+        in_specs=[anywhere] * count + [in_vmem] * spread,
+        out_specs=[in_vmem] * len(out_shape),
+        out_shape=out_shape,
+        scratch_shapes=scratch,
+        compiler_params=pltpu.CompilerParams(
+            collective_id=collective_id, has_side_effects=True, vmem_limit_bytes=VMEM_LIMIT
+        ),
+        name="reduce_gradients",
+    )(*operands)
+
+
+def with_kernels():
+    return lax.axis_size("dp") == 4 and lax.axis_size("fsdp") == 8
+
+
+def gather_all(shards, split, collective_id):
+    if with_kernels():
+        return gather_call(shards, split, collective_id)
+    return [lax.all_gather(shard, "fsdp", axis=0, tiled=True) for shard in shards]
+
+
+def reduce_all(grads, collective_id, squares=None):
+    if with_kernels():
+        return reduce_call(grads, collective_id, squares)
+    outs = [
+        lax.psum(lax.psum_scatter(grad, "fsdp", scatter_dimension=0), "dp") for grad in grads
+    ]
+    if squares is not None:
+        for out in outs[:-1]:
+            squares = squares + squares_of(out)
+        outs.append(lax.all_gather(outs[-1].at[-1:].set(squares), "fsdp", axis=0))
+    return outs
+
+
+def squares_of(item):
+    total = jnp.sum(jnp.square(item.astype(jnp.float32)))
+    return jnp.full((1, LANES), 1.0 / LANES, jnp.float32) * total
+
+
+def by_owner(grad, low=jnp.bfloat16):
+    owners = lax.axis_size("fsdp")
+    return grad.astype(low).reshape(owners, grad.shape[0] // owners, grad.shape[1])
 
 
 def attention_forward_kernel(q_ref, k_ref, v_ref, seg_col_ref, seg_row_ref, out_ref, expo_ref, inv_ref, *, block):
@@ -313,7 +718,8 @@
     return (
         residual_grad + stream_grad,
         (
-            jnp.concatenate([project_grad, up_grad], 1),
+            project_grad,
+            up_grad,
             jnp.concatenate([mixing_grad, down_grad], 0),
             vector_grad,
         ),
@@ -360,13 +766,25 @@
     global_square,
 ):
     pos_weights, member, counts = row_layout(segment, patch_size[0])
-    kernel_full = gather_rows(patch_kernel)
-    vectors = gather_vectors(layer_vector)
-    layer_weights = [
-        (gather_rows(input_proj[index]), gather_rows(output_proj[index]), vectors[index])
-        for index in range(LAYERS)
-    ]
-    head_full = gather_rows(head_weight)
+    owners = lax.axis_size("fsdp")
+    low = jnp.bfloat16
+    vector_size = layer_vector.size
+    kernel_full, vectors = gather_all(
+        [patch_kernel.astype(low), padded_rows(layer_vector.astype(low).reshape(-1), 32)],
+        (True, False),
+        1,
+    )
+    vectors = vectors.reshape(owners, -1)[:, :vector_size].reshape(owners, *layer_vector.shape)
+    vectors = jnp.swapaxes(vectors, 0, 1).reshape(LAYERS, -1)
+    head_shard = jnp.pad(head_weight.astype(low), ((0, 0), (0, -CLS % LANES)))
+    full_zero = gather_all(
+        [input_proj[0].astype(low), output_proj[0].astype(low)], (True, True), 2
+    )
+    full_one = gather_all(
+        [input_proj[1].astype(low), output_proj[1].astype(low), head_shard], (True,) * 3, 3
+    )
+    layer_weights = [(*full_zero, vectors[0]), (*full_one[:2], vectors[1])]
+    head_full = full_one[2][:, :CLS]
     global_low = rounded(global_vector)
     position_low = rounded(position_table)
     embed_pre = matmul(pixels, kernel_full) + global_low[:D]
@@ -393,53 +811,57 @@
     logits_grad = ((exponent / totals - onehot.astype(jnp.float32)) * counts[:, None]).astype(
         jnp.bfloat16
     )
-    head_share = scatter_rows(matmul(pooled.T, logits_grad))
+    head_grad = jnp.pad(matmul(pooled.T, logits_grad), ((0, 0), (0, -CLS % LANES)))
     pooled_grad = matmul(logits_grad, head_full.T)
     final_grad = jnp.dot(member, pooled_grad / image_sizes[:, None], precision=HIGHEST)
     stream_grad, final_gain, final_shift = final_back(final_grad)
-    layer_shares = [None] * LAYERS
-    vector_grads = [None] * LAYERS
-    for index in reversed(range(LAYERS)):
-        stream_grad, grads = layer_backward(stream_grad, layer_weights[index], saved_layers[index])
-        layer_shares[index] = (scatter_rows(grads[0]), scatter_rows(grads[1]))
-        vector_grads[index] = grads[2]
+    stream_grad, grads_one = layer_backward(stream_grad, layer_weights[1], saved_layers[1])
+    shares_one = reduce_all([by_owner(grad) for grad in (*grads_one[:3], head_grad)], 4)
+    stream_grad, grads_zero = layer_backward(stream_grad, layer_weights[0], saved_layers[0])
+    shares_zero = reduce_all([by_owner(grad) for grad in grads_zero[:3]], 5)
     embed_low = stream_grad.astype(jnp.bfloat16)
-    kernel_share = scatter_rows(matmul(pixels.T, embed_low))
     position_grad = jnp.dot(pos_weights.T, stream_grad, precision=HIGHEST)
-    pieces = [
-        position_grad.reshape(-1),
-        column_total(embed_low),
-        final_gain,
-        final_shift,
-        column_total(logits_grad),
-        *vector_grads,
-        loss_local[None],
-        jnp.sum(counts)[None],
-    ]
-    small = total_flat(jnp.concatenate(pieces))
-    position_sum = small[: position_grad.size].reshape(position_grad.shape)
-    global_sum = small[position_grad.size :][: global_vector.shape[0]]
-    vector_total = small[position_grad.size + global_vector.shape[0] :][
-        : LAYERS * vectors.shape[1]
-    ].reshape(vectors.shape)
-    loss_sum = small[-2]
-    token_total = small[-1]
-    shares = [kernel_share, head_share]
-    for pair in layer_shares:
-        shares.extend(pair)
-    local_squares = sum(jnp.sum(jnp.square(item.astype(jnp.float32))) for item in shares)
-    share_squares = lax.psum(local_squares, ("dp", "fsdp"))
-    kernel_sum = regather(kernel_share)
-    head_sum = regather(head_share)
-    input_sum = jnp.stack([regather(pair[0]) for pair in layer_shares])
-    output_sum = jnp.stack([regather(pair[1]) for pair in layer_shares])
-    vector_sum = lax.dynamic_slice_in_dim(
-        vector_total, lax.axis_index("fsdp") * layer_vector.shape[1], layer_vector.shape[1], 1
-    )
+    vector_part = jnp.stack([grads_zero[3], grads_one[3]]).reshape(LAYERS, owners, -1)
+    vector_part = jnp.swapaxes(vector_part, 0, 1).reshape(owners, vector_size)
+    vector_rows = -(-vector_size // LANES)
+    vector_part = jnp.pad(vector_part, ((0, 0), (0, vector_rows * LANES - vector_size)))
+    rest = jnp.concatenate(
+        [
+            position_grad.reshape(-1),
+            column_total(embed_low),
+            final_gain,
+            final_shift,
+            column_total(logits_grad),
+            loss_local[None],
+            jnp.sum(counts)[None],
+        ]
+    )
+    rest_rows = -(-rest.shape[0] // (owners * LANES))
+    rest_part = jnp.pad(rest, (0, rest_rows * owners * LANES - rest.shape[0]))
+    small = jnp.concatenate([vector_part, rest_part.reshape(owners, -1)], 1)
+    used = vector_rows + rest_rows
+    block_rows = (used // 64 + 1) * 64
+    small = jnp.pad(small.reshape(owners, used, LANES), ((0, 0), (0, block_rows - used), (0, 0)))
+    squares = sum(squares_of(item) for item in (*shares_zero, *shares_one))
+    kernel_sum, small_share, small_full = reduce_all(
+        [by_owner(matmul(pixels.T, embed_low)), small], 6, squares
+    )
+    rest_sum = small_full[:, vector_rows:used].reshape(-1)
+    position_sum = rest_sum[: position_grad.size].reshape(position_grad.shape)
+    global_sum = rest_sum[position_grad.size :][: global_vector.shape[0]]
+    loss_sum = rest_sum[rest.shape[0] - 2]
+    token_total = rest_sum[rest.shape[0] - 1]
+    kernel_sum = kernel_sum.astype(jnp.float32)
+    head_sum = shares_one[3][:, :CLS].astype(jnp.float32)
+    input_sum = jnp.stack(
+        [jnp.concatenate(pair[:2], 1) for pair in (shares_zero, shares_one)]
+    ).astype(jnp.float32)
+    output_sum = jnp.stack([shares_zero[2], shares_one[2]]).astype(jnp.float32)
+    vector_sum = small_share[:vector_rows].reshape(-1)[:vector_size].reshape(layer_vector.shape)
     grad_norm = (
         jnp.sqrt(
-            share_squares
-            + jnp.sum(vector_total * vector_total)
+            jnp.sum(small_full[:, -1])
+            + jnp.sum(jnp.square(small_full[:, :vector_rows]))
             + jnp.sum(position_sum * position_sum)
             + jnp.sum(global_sum * global_sum)
         )

time: 1640 us -> 993 us (0.61)
  waiting for transfers between devices: 879 us -> 0 us
  Pallas kernels: 120 us -> 592 us
  blocking collectives: 193 us -> 0 us
  local copies, waits for them, and re-layouts: 76.2 us -> 58.5 us
    reduce_scatter x7 -> x0, waiting for transfers between devices: 629 us -> none  [the longest x6 605 us: scatter_rows(): lax.psum_scatter(partial_sum.astype(jnp.bfloat16), AXES, scatter_dimensio...]
    pallas_call x0 -> x6, Pallas kernels: none -> 473 us  [the longest x3 275 us: reduce_call(): pl.pallas_call(functools.partial(reduce_kernel, count=count, spread=sprea...]
    all_gather x6 -> x0, waiting for transfers between devices: 249 us -> none  [gather_rows(): return lax.all_gather(mine.astype(jnp.bfloat16), AXES, axis=0, tiled=True)]
    all_gather x8 -> x0, blocking collectives: 154 us -> none  [the longest x6 72.6 us: regather(): return lax.all_gather(shares, 'dp', axis=0, tiled=True).astype(jnp.float32)]
    psum x1 -> x0, blocking collectives: 39.3 us -> none  [body(): share_squares = lax.psum(local_squares, ('dp', 'fsdp'))]
    dot_general x29, matrix products: 237 us -> 219 us  [matmul(): return jnp.dot(left, right, preferred_element_type=jnp.float32)]
  transfers between devices with their start and end apart: 13 -> 0, of which waited for: 13 -> 0; matrix products, arithmetic and copies ran while one was open for 13% -> 0% of each run, Pallas kernels for 4% -> 0%
where the time goes in v2:
time: 993 us; the launch traced here: 984 us
  Pallas kernels  592 us (60%)
  matrix products  232 us (23%)
  other arithmetic  88.1 us (9%)
  local copies, waits for them, and re-layouts  58.5 us (6%)
  between operations  13.7 us (1%)
    pallas_call x3, Pallas kernels, reduce_call(): pl.pallas_call(functools.partial(reduce_kernel, count=count, spread=sprea...  275 us
    dot_general x29, matrix products, matmul(): return jnp.dot(left, right, preferred_element_type=jnp.float32)  219 us
    pallas_call x3, Pallas kernels, gather_call(): pl.pallas_call(functools.partial(gather_kernel, split=split), in_specs=[a...  198 us
    pallas_call x2, Pallas kernels, attention_forward(): pl.pallas_call(functools.partial(attention_forward_kernel, block=block),...  61.9 us
    pallas_call x2, Pallas kernels, attention_backward(): pl.pallas_call(functools.partial(attention_backward_kernel, block=block),...  57.2 us
    sub x7, other arithmetic, adam_update(): return (moment, square, weight - learn_rate * step_dir)  20.9 us

profile of v2, /device:TPU:0, one launch (start us, length us, event | category | flops | bytes accessed | tf_op | source)
XLA Modules:
  0.0 984.4 jit_solution(14013045212832817735)
XLA Ops:
  2.5 2.1 convert_element_type.263.refs_0_
  6.0 37.5 %gather_weights.3 = (bf16[8,384,768]{2,1,0:T(8,128)(2,1)}, bf16[8,32,128]{2,1,0:T(8,128)(2,1)}) custom-call(bf16[384,768]{1,0:T(8,128)(2,1)} %convert_element_type.263.refs_0_, bf16[32,128]{1,0:T(8,128)(2,1)} %pad_bitcast_fusion.refs_1_), custom_call_target="tpu_custom_call" | custom-call | tf_op jit(solution)/shard_map/gather_weights/pallas_call | solution.py:236
  45.7 8.7 fusion.144
  61.2 76.9 %gather_weights.4 = (bf16[8,96,5376]{2,1,0:T(8,128)(2,1)}, bf16[8,480,768]{2,1,0:T(8,128)(2,1)}) custom-call(bf16[96,5376]{1,0:T(8,128)(2,1)} %get-tuple-element.132.refs_0_, bf16[480,768]{1,0:T(8,128)(2,1)} %get-tuple-element.134.refs_1_), custom_call_target="tpu_custom_call" | custom-call | tf_op jit(solution)/shard_map/gather_weights/pallas_call | solution.py:236
  138.6 7.8 add_convert_fusion.1.q_ref.k_ref.v_ref
  147.4 31.0 %attention_forward.2 = (bf16[1024,768]{1,0:T(8,128)(2,1)}, bf16[12,1024,1024]{2,1,0:T(8,128)(2,1)}, f32[1024,768]{1,0:T(8,128)}) custom-call(bf16[1024,2304]{1,0:T(8,128)(2,1)} %add_convert_fusion.1.q_ref.k_ref.v_ref, bf16[1024,2304]{1,0:T(8,128)(2,1)} %add_convert_fusion.1.q_ref.k_ref.v_ref, bf16[1024,2304]{1,0:T(8,128)(2,1)} %add_convert_fusion.1.q_ref.k_ref.v_ref, ...), custom_call_target="tpu_custom_call" | custom-call | flops 12884901888 | bytes 34603008 | tf_op jit(solution)/shard_map/attention_forward/pallas_call | solution.py:565
  178.4 3.3 fusion.134
  183.4 10.7 %fusion.29 = f32[1024,3072]{1,0:T(8,128)} fusion(bf16[768,5376]{1,0:T(8,128)(2,1)} %bitcast.115, f32[1024,768]{0,1:T(8,128)S(1)} %get-tuple-element.161, f32[768]{0:T(1024)S(1)} %get-tuple-element.145, f32[768]{0:T(1024)S(1)} %get-tuple-element.143, f32[1024]{0:T(1024)S(1)} %fusion.105, f32[1024]{0:T(1024)S(1)} %broadcast_multiply_fusion.4), kind=kOutput, calls=%fused_computation.59 | convolution fusion | flops 4835770368 | bytes 20461568 | tf_op jit(solution)/shard_map/dot_general | solution.py:53
  194.1 11.5 %fusion.135 = (f32[1024]{0:T(1024)S(1)}, f32[1024,768]{0,1:T(8,128)S(1)}) fusion(f32[768]{0:T(1024)S(1)} %get-tuple-element.144, f32[1024,768]{0,1:T(8,128)S(1)} %get-tuple-element.161, bf16[3840,768]{1,0:T(8,128)(2,1)} %bitcast.129, f32[1024,3072]{1,0:T(8,128)} %fusion.29, f32[3072]{0:T(1024)S(1)} %slice.222), kind=kOutput, calls=%fused_computation.295 | convolution fusion | flops 4865653760 | bytes 23612416 | tf_op jit(solution)/shard_map/dot_general | solution.py:53
  206.5 83.5 %gather_weights.5 = (bf16[8,96,5376]{2,1,0:T(8,128)(2,1)}, bf16[8,480,768]{2,1,0:T(8,128)(2,1)}, bf16[8,96,1024]{2,1,0:T(8,128)(2,1)}) custom-call(bf16[96,5376]{1,0:T(8,128)(2,1)} %get-tuple-element.131.refs_0_, bf16[480,768]{1,0:T(8,128)(2,1)} %get-tuple-element.133.refs_1_, bf16[96,1024]{1,0:T(8,128)(2,1)} %pad.26.refs_2_), custom_call_target="tpu_custom_call" | custom-call | tf_op jit(solution)/shard_map/gather_weights/pallas_call | solution.py:236
  290.5 7.8 add_convert_fusion.q_ref.k_ref.v_ref
  298.3 30.9 %attention_forward.3 = (bf16[1024,768]{1,0:T(8,128)(2,1)}, bf16[12,1024,1024]{2,1,0:T(8,128)(2,1)}, f32[1024,768]{1,0:T(8,128)}) custom-call(bf16[1024,2304]{1,0:T(8,128)(2,1)} %add_convert_fusion.q_ref.k_ref.v_ref, bf16[1024,2304]{1,0:T(8,128)(2,1)} %add_convert_fusion.q_ref.k_ref.v_ref, bf16[1024,2304]{1,0:T(8,128)(2,1)} %add_convert_fusion.q_ref.k_ref.v_ref, ...), custom_call_target="tpu_custom_call" | custom-call | flops 12884901888 | bytes 34603008 | tf_op jit(solution)/shard_map/attention_forward/pallas_call | solution.py:565
  329.2 3.2 fusion.136
  332.9 11.9 %fusion.21 = f32[1024,3072]{1,0:T(8,128)} fusion(bf16[768,5376]{1,0:T(8,128)(2,1)} %bitcast.121, f32[1024,768]{0,1:T(8,128)S(1)} %get-tuple-element.165, f32[768]{0:T(1024)S(1)} %get-tuple-element.139, f32[768]{0:T(1024)S(1)} %get-tuple-element.137, f32[1024]{0:T(1024)S(1)} %fusion.107, f32[1024]{0:T(1024)S(1)} %broadcast_multiply_fusion.2), kind=kOutput, calls=%fused_computation.51 | convolution fusion | flops 4835770368 | bytes 20461568 | tf_op jit(solution)/shard_map/dot_general | solution.py:53
  344.9 10.0 %fusion.137 = (f32[1024]{0:T(1024)S(1)}, f32[1024,768]{0,1:T(8,128)S(1)}) fusion(f32[768]{0:T(1024)S(1)} %get-tuple-element.138, f32[1024,768]{0,1:T(8,128)S(1)} %get-tuple-element.165, bf16[3840,768]{1,0:T(8,128)(2,1)S(1)} %bitcast.138, f32[1024,3072]{1,0:T(8,128)} %fusion.21, f32[3072]{0:T(1024)S(1)} %slice.237), kind=kOutput, calls=%fused_computation.297 | convolution fusion | flops 4865653760 | bytes 23613440 | tf_op jit(solution)/shard_map/dot_general | solution.py:53
  355.6 2.0 fusion.69
  360.0 3.7 fusion.143
  363.7 3.7 copy.81
  367.4 4.5 multiply_reduce_fusion
  375.7 17.9 %convert_reduce_fusion = (f32[3072]{0:T(1024)}, bf16[1024,3072]{1,0:T(8,128)(2,1)}) fusion(f32[1024,3072]{1,0:T(8,128)} %fusion.21, f32[3072]{0:T(1024)S(1)} %slice.237, bf16[1024,768]{0,1:T(8,128)(2,1)S(1)} %get-tuple-element.122, bf16[3840,768]{1,0:T(8,128)(2,1)S(1)} %bitcast.141), kind=kOutput, calls=%fused_computation.18 | convolution fusion | flops 4904186880 | bytes 25190400 | tf_op jit(solution)/shard_map/dot_general | solution.py:53
  393.6 9.4 fusion.140
  403.0 3.5 copy.82
  406.5 2.5 multiply_reduce_fusion.8
  414.4 3.9 convolution_convert_fusion.8.grad_ref
  418.2 28.7 %attention_backward.2 = bf16[1024,2304]{1,0:T(8,128)(2,1)} custom-call(bf16[1024,2304]{1,0:T(8,128)(2,1)} %add_convert_fusion.q_ref.k_ref.v_ref, bf16[1024,2304]{1,0:T(8,128)(2,1)} %add_convert_fusion.q_ref.k_ref.v_ref, bf16[1024,2304]{1,0:T(8,128)(2,1)} %add_convert_fusion.q_ref.k_ref.v_ref, bf16[12,1024,1024]{2,1,0:T(8,128)(2,1)} %get-tuple-element.56.expo_ref, ...), custom_call_target="tpu_custom_call" | custom-call | flops 25769803776 | bytes 40894464 | tf_op jit(solution)/shard_map/attention_backward/pallas_call | solution.py:640
  446.9 8.9 fusion.139
  455.9 3.7 copy.83
  459.5 3.0 multiply_reduce_fusion.2
  466.5 17.1 %convert_reduce_fusion.1 = (f32[3072]{0:T(1024)S(1)}, bf16[1024,3072]{1,0:T(8,128)(2,1)}) fusion(f32[1024,3072]{1,0:T(8,128)} %fusion.29, f32[3072]{0:T(1024)S(1)} %copy-done.105, bf16[1024,768]{0,1:T(8,128)(2,1)S(1)} %get-tuple-element.116, bf16[3840,768]{1,0:T(8,128)(2,1)S(1)} %bitcast.133), kind=kOutput, calls=%fused_computation.19 | convolution fusion | flops 4904186880 | bytes 25190400 | tf_op jit(solution)/shard_map/dot_general | solution.py:53
  483.5 8.4 fusion.142
  491.9 3.9 copy.84
  495.8 2.5 multiply_reduce_fusion.6
  504.7 3.9 convolution_convert_fusion.7.grad_ref
  508.6 28.5 %attention_backward.3 = bf16[1024,2304]{1,0:T(8,128)(2,1)} custom-call(bf16[1024,2304]{1,0:T(8,128)(2,1)} %add_convert_fusion.1.q_ref.k_ref.v_ref, bf16[1024,2304]{1,0:T(8,128)(2,1)} %add_convert_fusion.1.q_ref.k_ref.v_ref, bf16[1024,2304]{1,0:T(8,128)(2,1)} %add_convert_fusion.1.q_ref.k_ref.v_ref, bf16[12,1024,1024]{2,1,0:T(8,128)(2,1)} %get-tuple-element.58.expo_ref, ...), custom_call_target="tpu_custom_call" | custom-call | flops 25769803776 | bytes 40894464 | tf_op jit(solution)/shard_map/attention_backward/pallas_call | solution.py:640
  537.1 8.9 fusion.141
  546.1 4.1 copy.85
  550.2 3.0 multiply_reduce_fusion.4
  557.2 6.7 fusion.14
  564.0 6.7 copy.86
  570.7 3.0 convert_reduce_fusion.2
  574.0 3.0 convert_reduce_fusion.3
  578.1 5.8 fusion.57
  585.9 2.3 concatenate.29
  590.0 8.1 convolution_convert_fusion.6
  598.1 10.3 %convolution_convert_fusion.3 = bf16[768,3072]{1,0:T(8,128)(2,1)} fusion(bf16[1024,3072]{1,0:T(8,128)(2,1)} %get-tuple-element.114, f32[1024,768]{0,1:T(8,128)S(1)} %copy-done.4, f32[768]{0:T(1024)S(1)} %copy-done.120, f32[768]{0:T(1024)S(1)} %copy-done.77, f32[1024]{0:T(1024)S(1)} %copy-done.87, f32[1024]{0:T(1024)S(1)} %copy-done.70), kind=kOutput, calls=%fused_computation.33 | convolution fusion | flops 4838129664 | bytes 14170112 | tf_op jit(solution)/shard_map/dot_general | solution.py:53
  608.4 8.9 convolution_convert_fusion.2
  618.8 2.9 pad_maximum_fusion
  621.7 105.8 %reduce_gradients.3 = (bf16[96,2304]{1,0:T(8,128)(2,1)}, bf16[96,3072]{1,0:T(8,128)(2,1)}, bf16[480,768]{1,0:T(8,128)(2,1)}) custom-call(bf16[8,96,2304]{2,1,0:T(8,128)(2,1)} %bitcast.93, bf16[8,96,3072]{2,1,0:T(8,128)(2,1)} %bitcast.91, bf16[8,480,768]{2,1,0:T(8,128)(2,1)} %bitcast.87), custom_call_target="tpu_custom_call" | custom-call | tf_op jit(solution)/shard_map/reduce_gradients/pallas_call | solution.py:480
  727.5 1.8 multiply_reduce_fusion.20
  729.3 2.0 multiply_reduce_fusion.18
  732.6 2.1 multiply_reduce_fusion.16
  735.5 8.1 convolution_convert_fusion.5
  743.6 10.1 %convolution_convert_fusion.1 = bf16[768,3072]{1,0:T(8,128)(2,1)} fusion(bf16[1024,3072]{1,0:T(8,128)(2,1)} %get-tuple-element.120, f32[1024,768]{0,1:T(8,128)S(1)} %copy-done.6, f32[768]{0:T(1024)S(1)} %copy-done.116, f32[768]{0:T(1024)S(1)} %copy-done.72, f32[1024]{0:T(1024)S(1)} %copy-done.84, f32[1024]{0:T(1024)S(1)} %copy-done.68), kind=kOutput, calls=%fused_computation.31 | convolution fusion | flops 4838129664 | bytes 14170112 | tf_op jit(solution)/shard_map/dot_general | solution.py:53
  753.8 8.9 convolution_convert_fusion
  764.2 2.9 pad_maximum_fusion.1
  769.8 118.5 %reduce_gradients.4 = (bf16[96,2304]{1,0:T(8,128)(2,1)}, bf16[96,3072]{1,0:T(8,128)(2,1)}, bf16[480,768]{1,0:T(8,128)(2,1)}, bf16[96,1024]{1,0:T(8,128)(2,1)}) custom-call(bf16[8,96,2304]{2,1,0:T(8,128)(2,1)} %bitcast.94, bf16[8,96,3072]{2,1,0:T(8,128)(2,1)} %bitcast.92, bf16[8,480,768]{2,1,0:T(8,128)(2,1)} %bitcast.88, bf16[8,96,1024]{2,1,0:T(8,128)(2,1)} %bitcast.90), custom_call_target="tpu_custom_call" | custom-call | tf_op jit(solution)/shard_map/reduce_gradients/pallas_call | solution.py:480
  888.4 1.8 multiply_reduce_fusion.19
  890.9 2.0 multiply_reduce_fusion.17
  893.5 2.3 multiply_reduce_fusion.15
  899.2 50.6 %reduce_gradients.5 = (bf16[384,768]{1,0:T(8,128)(2,1)}, f32[64,128]{1,0:T(8,128)}, f32[8,64,128]{2,1,0:T(8,128)}) custom-call(bf16[8,384,768]{2,1,0:T(8,128)(2,1)} %bitcast.89, f32[8,64,128]{2,1,0:T(8,128)} %pad.29.refs_1_, f32[1,128]{1,0:T(1,128)} %broadcast.587.refs_2_), custom_call_target="tpu_custom_call" | custom-call | tf_op jit(solution)/shard_map/reduce_gradients/pallas_call | solution.py:480
  960.4 4.1 multiply_subtract_fusion.2
  964.5 2.9 multiply_subtract_fusion.3
  967.8 7.2 multiply_subtract_fusion
  975.2 4.6 multiply_subtract_fusion.1
  (428 shorter events, 64.8 us)
Async XLA Ops:
  0.7 44.4 %copy-start.63 = (s32[1024]{0:T(1024)S(1)}, s32[1024]{0:T(1024)}, u32[]{:S(2)}) copy-start(s32[1024]{0:T(1024)} %param.26) | copy-start | bytes 12292
  0.7 44.5 %copy-start.124 = (s32[1,8]{1,0:T(1,128)S(1)}, s32[1,8]{1,0:T(1,128)}, u32[]{:S(2)}) copy-start(s32[1,8]{1,0:T(1,128)} %param.27) | copy-start | bytes 100
  0.7 45.0 %copy-start.55 = (f32[49,768]{1,0:T(8,128)S(1)}, f32[49,768]{1,0:T(8,128)}, u32[]{:S(2)}) copy-start(f32[49,768]{1,0:T(8,128)} %param.34) | copy-start | bytes 451588
  1.5 353.8 %copy-start.114 = (s32[8]{0:T(128)}, s32[8]{0:T(128)S(1)}, u32[]{:S(2)}) copy-start(s32[8]{0:T(128)S(1)} %convert_reduce_fusion.10) | copy-start | bytes 100
  44.9 160.8 %copy-start.57 = (f32[9984]{0:T(1024)}, f32[9984]{0:T(1024)S(1)}, u32[]{:S(2)}) copy-start(f32[9984]{0:T(1024)S(1)} %reshape.512) | copy-start | bytes 119812
  44.9 245.6 %copy-start.117 = (f32[768]{0:T(1024)}, f32[768]{0:T(1024)S(1)}, u32[]{:S(2)}) copy-start(f32[768]{0:T(1024)S(1)} %get-tuple-element.141) | copy-start | bytes 9220
  44.9 288.0 %copy-start.115 = (f32[768]{0:T(1024)}, f32[768]{0:T(1024)S(1)}, u32[]{:S(2)}) copy-start(f32[768]{0:T(1024)S(1)} %get-tuple-element.139) | copy-start | bytes 9220
  44.9 365.8 %copy-start.71 = (f32[768]{0:T(1024)}, f32[768]{0:T(1024)S(1)}, u32[]{:S(2)}) copy-start(f32[768]{0:T(1024)S(1)} %get-tuple-element.137) | copy-start | bytes 9220
  44.9 417.6 %copy-start.92 = (f32[768]{0:T(1024)}, f32[768]{0:T(1024)S(1)}, u32[]{:S(2)}) copy-start(f32[768]{0:T(1024)S(1)} %get-tuple-element.142) | copy-start | bytes 9220
  45.0 11.2 %copy-start.59 = (f32[9984]{0:T(1024)}, f32[9984]{0:T(1024)S(1)}, u32[]{:S(2)}) copy-start(f32[9984]{0:T(1024)S(1)} %reshape.511) | copy-start | bytes 119812
  45.0 93.5 %copy-start.94 = (f32[768]{0:T(1024)}, f32[768]{0:T(1024)S(1)}, u32[]{:S(2)}) copy-start(f32[768]{0:T(1024)S(1)} %get-tuple-element.148) | copy-start | bytes 9220
  45.0 93.5 %copy-start.121 = (f32[768]{0:T(1024)}, f32[768]{0:T(1024)S(1)}, u32[]{:S(2)}) copy-start(f32[768]{0:T(1024)S(1)} %get-tuple-element.147) | copy-start | bytes 9220
  45.1 138.3 %copy-start.76 = (f32[768]{0:T(1024)}, f32[768]{0:T(1024)S(1)}, u32[]{:S(2)}) copy-start(f32[768]{0:T(1024)S(1)} %get-tuple-element.143) | copy-start | bytes 9220
  45.1 138.3 %copy-start.119 = (f32[768]{0:T(1024)}, f32[768]{0:T(1024)S(1)}, u32[]{:S(2)}) copy-start(f32[768]{0:T(1024)S(1)} %get-tuple-element.145) | copy-start | bytes 9220
  45.6 8.7 copy-start.42
  56.2 122.3 %copy-start = (f32[1024,768]{0,1:T(8,128)}, f32[1024,768]{0,1:T(8,128)S(1)}, u32[]{:S(2)}) copy-start(f32[1024,768]{0,1:T(8,128)S(1)} %get-tuple-element.159) | copy-start | bytes 9437188
  61.2 77.4 %slice-start.1 = ((f32[9984]{0:T(1024)}), f32[2304]{0:T(1024)S(1)}, s32[]{:S(2)}) async-start(f32[9984]{0:T(1024)} %copy-done.59), calls=%async_computation.1 | async-start | bytes 24576 | tf_op jit(solution)/shard_map/slice | solution.py:668
  181.8 12.3 %copy-start.2 = (f32[1024,768]{0,1:T(8,128)}, f32[1024,768]{0,1:T(8,128)S(1)}, u32[]{:S(2)}) copy-start(f32[1024,768]{0,1:T(8,128)S(1)} %get-tuple-element.161) | copy-start | bytes 9437188
  181.8 12.3 %copy-start.69 = (f32[1024]{0:T(1024)}, f32[1024]{0:T(1024)S(1)}, u32[]{:S(2)}) copy-start(f32[1024]{0:T(1024)S(1)} %broadcast_multiply_fusion.4) | copy-start | bytes 12292
  183.4 10.7 %copy-start.85 = (f32[1024]{0:T(1024)}, f32[1024]{0:T(1024)S(1)}, u32[]{:S(2)}) copy-start(f32[1024]{0:T(1024)S(1)} %fusion.105) | copy-start | bytes 12292
  183.4 10.7 %copy-start.60 = (f32[9984]{0:T(1024)S(1)}, f32[9984]{0:T(1024)}, u32[]{:S(2)}) copy-start(f32[9984]{0:T(1024)} %copy-done.59) | copy-start | bytes 119812
  194.1 11.5 %copy-start.104 = (f32[3072]{0:T(1024)}, f32[3072]{0:T(1024)S(1)}, u32[]{:S(2)}) copy-start(f32[3072]{0:T(1024)S(1)} %slice.222) | copy-start | bytes 36868
  194.1 11.6 %copy-start.51 = (f32[96,1000]{1,0:T(8,128)S(1)}, f32[96,1000]{1,0:T(8,128)}, u32[]{:S(2)}) copy-start(f32[96,1000]{1,0:T(8,128)} %param.30) | copy-start | bytes 1152004
  205.6 123.6 %copy-start.15 = (f32[1024,768]{0,1:T(8,128)}, f32[1024,768]{0,1:T(8,128)S(1)}, u32[]{:S(2)}) copy-start(f32[1024,768]{0,1:T(8,128)S(1)} %get-tuple-element.163) | copy-start | bytes 9437188
  205.7 84.8 %slice-start = ((f32[9984]{0:T(1024)}), f32[2304]{0:T(1024)S(1)}, s32[]{:S(2)}) async-start(f32[9984]{0:T(1024)} %copy-done.57), calls=%async_computation | async-start | bytes 24576 | tf_op jit(solution)/shard_map/slice | solution.py:668
  290.1 172.5 %copy-start.80 = (f32[1024]{0:T(1024)}, f32[1024]{0:T(1024)S(1)}, u32[]{:S(2)}) copy-start(f32[1024]{0:T(1024)S(1)} %broadcast_multiply_fusion.3) | copy-start | bytes 12292
  290.5 172.1 %copy-start.98 = (f32[1024]{0:T(1024)}, f32[1024]{0:T(1024)S(1)}, u32[]{:S(2)}) copy-start(f32[1024]{0:T(1024)S(1)} %fusion.106) | copy-start | bytes 12292
  332.5 78.2 %copy-start.5 = (f32[1024,768]{0,1:T(8,128)}, f32[1024,768]{0,1:T(8,128)S(1)}, u32[]{:S(2)}) copy-start(f32[1024,768]{0,1:T(8,128)S(1)} %get-tuple-element.165) | copy-start | bytes 9437188
  332.5 78.2 %copy-start.67 = (f32[1024]{0:T(1024)}, f32[1024]{0:T(1024)S(1)}, u32[]{:S(2)}) copy-start(f32[1024]{0:T(1024)S(1)} %broadcast_multiply_fusion.2) | copy-start | bytes 12292
  332.5 12.4 %slice-start.10 = ((s8[5898240]{0:T(1024)(128)(4,1)}), s8[4194304]{0:T(1024)(128)(4,1)S(1)}, s32[]{:S(2)}) async-start(s8[5898240]{0:T(1024)(128)(4,1)} %bitcast.136), calls=%async_computation.10 | async-start | bytes 8388608
  332.9 77.8 %copy-start.83 = (f32[1024]{0:T(1024)}, f32[1024]{0:T(1024)S(1)}, u32[]{:S(2)}) copy-start(f32[1024]{0:T(1024)S(1)} %fusion.107) | copy-start | bytes 12292
  332.9 11.9 %copy-start.58 = (f32[9984]{0:T(1024)S(1)}, f32[9984]{0:T(1024)}, u32[]{:S(2)}) copy-start(f32[9984]{0:T(1024)} %copy-done.57) | copy-start | bytes 119812
  332.9 11.9 %slice-start.11 = ((s8[5898240]{0:T(1024)(128)(4,1)}), s8[1703936]{0:T(1024)(128)(4,1)S(1)}, s32[]{:S(2)}) async-start(s8[5898240]{0:T(1024)(128)(4,1)} %bitcast.136), calls=%async_computation.11 | async-start | bytes 3407872
  344.9 30.6 %copy-start.107 = (f32[3072]{0:T(1024)}, f32[3072]{0:T(1024)S(1)}, u32[]{:S(2)}) copy-start(f32[3072]{0:T(1024)S(1)} %slice.237) | copy-start | bytes 36868
  374.6 19.0 %slice-start.4 = ((s8[8257536]{0:T(1024)(128)(4,1)}), s8[4194304]{0:T(1024)(128)(4,1)S(1)}, s32[]{:S(2)}) async-start(s8[8257536]{0:T(1024)(128)(4,1)} %bitcast.123), calls=%async_computation.4 | async-start | bytes 8388608
  375.5 18.1 %copy-start.47 = (bf16[1024,768]{0,1:T(8,128)(2,1)}, bf16[1024,768]{0,1:T(8,128)(2,1)S(1)}, u32[]{:S(2)}) copy-start(bf16[1024,768]{0,1:T(8,128)(2,1)S(1)} %get-tuple-element.122) | copy-start | bytes 4718596
  375.7 17.9 %slice-start.5 = ((s8[8257536]{0:T(1024)(128)(4,1)}), s8[4063232]{0:T(1024)(128)(4,1)S(1)}, s32[]{:S(2)}) async-start(s8[8257536]{0:T(1024)(128)(4,1)} %bitcast.123), calls=%async_computation.5 | async-start | bytes 8126464
  464.7 18.8 %slice-start.2 = ((s8[8257536]{0:T(1024)(128)(4,1)}), s8[4194304]{0:T(1024)(128)(4,1)S(1)}, s32[]{:S(2)}) async-start(s8[8257536]{0:T(1024)(128)(4,1)} %bitcast.117), calls=%async_computation.2 | async-start | bytes 8388608
  465.2 18.3 %copy-start.49 = (bf16[1024,768]{0,1:T(8,128)(2,1)}, bf16[1024,768]{0,1:T(8,128)(2,1)S(1)}, u32[]{:S(2)}) copy-start(bf16[1024,768]{0,1:T(8,128)(2,1)S(1)} %get-tuple-element.116) | copy-start | bytes 4718596
  466.5 17.1 %slice-start.3 = ((s8[8257536]{0:T(1024)(128)(4,1)}), s8[4063232]{0:T(1024)(128)(4,1)S(1)}, s32[]{:S(2)}) async-start(s8[8257536]{0:T(1024)(128)(4,1)} %bitcast.117), calls=%async_computation.3 | async-start | bytes 8126464
  589.9 18.4 %slice-start.14 = ((s8[12582912]{0:T(1024)(128)(4,1)}), s8[4194304]{0:T(1024)(128)(4,1)S(1)}, s32[]{:S(2)}) async-start(s8[12582912]{0:T(1024)(128)(4,1)} %bitcast.143), calls=%async_computation.14 | async-start | bytes 8388608
  589.9 18.4 %slice-start.15 = ((s8[12582912]{0:T(1024)(128)(4,1)}), s8[4194304]{0:T(1024)(128)(4,1)S(1)}, s32[]{:S(2)}) async-start(s8[12582912]{0:T(1024)(128)(4,1)} %bitcast.143), calls=%async_computation.15 | async-start | bytes 8388608
  598.0 10.3 %copy-start.50 = (bf16[1024,768]{0,1:T(8,128)(2,1)S(1)}, bf16[1024,768]{0,1:T(8,128)(2,1)}, u32[]{:S(2)}) copy-start(bf16[1024,768]{0,1:T(8,128)(2,1)} %copy-done.49) | copy-start | bytes 4718596
  598.0 10.3 %copy-start.106 = (f32[3072]{0:T(1024)S(1)}, f32[3072]{0:T(1024)}, u32[]{:S(2)}) copy-start(f32[3072]{0:T(1024)} %copy-done.104) | copy-start | bytes 36868
  598.1 10.3 %slice-start.16 = ((s8[12582912]{0:T(1024)(128)(4,1)}), s8[4194304]{0:T(1024)(128)(4,1)S(1)}, s32[]{:S(2)}) async-start(s8[12582912]{0:T(1024)(128)(4,1)} %bitcast.143), calls=%async_computation.16 | async-start | bytes 8388608
  608.4 8.9 copy-start.13
  608.4 8.9 copy-start.125
  621.6 113.7 %copy-start.17 = (f32[1024,768]{0,1:T(8,128)S(1)}, f32[1024,768]{0,1:T(8,128)}, u32[]{:S(2)}) copy-start(f32[1024,768]{0,1:T(8,128)} %copy-done.15) | copy-start | bytes 9437188
  621.6 113.7 %copy-start.81 = (f32[1024]{0:T(1024)S(1)}, f32[1024]{0:T(1024)}, u32[]{:S(2)}) copy-start(f32[1024]{0:T(1024)} %copy-done.80) | copy-start | bytes 12292
  621.6 113.7 %copy-start.93 = (f32[768]{0:T(1024)S(1)}, f32[768]{0:T(1024)}, u32[]{:S(2)}) copy-start(f32[768]{0:T(1024)} %copy-done.92) | copy-start | bytes 9220
  621.6 113.7 %copy-start.99 = (f32[1024]{0:T(1024)S(1)}, f32[1024]{0:T(1024)}, u32[]{:S(2)}) copy-start(f32[1024]{0:T(1024)} %copy-done.98) | copy-start | bytes 12292
  621.6 113.8 %copy-start.118 = (f32[768]{0:T(1024)S(1)}, f32[768]{0:T(1024)}, u32[]{:S(2)}) copy-start(f32[768]{0:T(1024)} %copy-done.117) | copy-start | bytes 9220
  735.5 18.3 %slice-start.17 = ((s8[12582912]{0:T(1024)(128)(4,1)}), s8[4194304]{0:T(1024)(128)(4,1)S(1)}, s32[]{:S(2)}) async-start(s8[12582912]{0:T(1024)(128)(4,1)} %bitcast.145), calls=%async_computation.17 | async-start | bytes 8388608
  735.5 18.3 %slice-start.18 = ((s8[12582912]{0:T(1024)(128)(4,1)}), s8[4194304]{0:T(1024)(128)(4,1)S(1)}, s32[]{:S(2)}) async-start(s8[12582912]{0:T(1024)(128)(4,1)} %bitcast.145), calls=%async_computation.18 | async-start | bytes 8388608
  743.6 10.2 %copy-start.48 = (bf16[1024,768]{0,1:T(8,128)(2,1)S(1)}, bf16[1024,768]{0,1:T(8,128)(2,1)}, u32[]{:S(2)}) copy-start(bf16[1024,768]{0,1:T(8,128)(2,1)} %copy-done.47) | copy-start | bytes 4718596
  743.6 10.2 %copy-start.108 = (f32[3072]{0:T(1024)S(1)}, f32[3072]{0:T(1024)}, u32[]{:S(2)}) copy-start(f32[3072]{0:T(1024)} %copy-done.107) | copy-start | bytes 36868
  743.6 10.2 %slice-start.19 = ((s8[12582912]{0:T(1024)(128)(4,1)}), s8[4194304]{0:T(1024)(128)(4,1)S(1)}, s32[]{:S(2)}) async-start(s8[12582912]{0:T(1024)(128)(4,1)} %bitcast.145), calls=%async_computation.19 | async-start | bytes 8388608
  753.8 8.9 copy-start.21
  753.8 8.9 copy-start.126
  893.5 66.8 %copy-start.33 = (f32[384,768]{1,0:T(8,128)S(1)}, f32[384,768]{1,0:T(8,128)}, u32[]{:S(2)}) copy-start(f32[384,768]{1,0:T(8,128)} %param.29) | copy-start | bytes 3538948
  893.5 66.8 %copy-start.53 = (f32[384,768]{1,0:T(8,128)S(1)}, f32[384,768]{1,0:T(8,128)}, u32[]{:S(2)}) copy-start(f32[384,768]{1,0:T(8,128)} %param.43) | copy-start | bytes 3538948
  899.2 65.3 %copy-start.52 = (f32[96,1000]{1,0:T(8,128)S(1)}, f32[96,1000]{1,0:T(8,128)}, u32[]{:S(2)}) copy-start(f32[96,1000]{1,0:T(8,128)} %param.30) | copy-start | bytes 1152004
  949.9 14.6 %copy-start.54 = (bf16[96,1024]{1,0:T(8,128)(2,1)S(1)}, bf16[96,1024]{1,0:T(8,128)(2,1)}, u32[]{:S(2)}) copy-start(bf16[96,1024]{1,0:T(8,128)(2,1)} %get-tuple-element.66) | copy-start | bytes 589828
  955.7 11.7 %copy-start.45 = (bf16[96,2304]{1,0:T(8,128)(2,1)S(1)}, bf16[96,2304]{1,0:T(8,128)(2,1)}, u32[]{:S(2)}) copy-start(bf16[96,2304]{1,0:T(8,128)(2,1)} %get-tuple-element.63) | copy-start | bytes 1327108
  (83 other events, 397.9 us)

commit v3 on v2

--- a/solution.py
+++ b/solution.py
@@ -239,6 +239,7 @@
         out_specs=[anywhere] * count,
         out_shape=[jax.ShapeDtypeStruct((owners, *s.shape), s.dtype) for s in shards],
         scratch_shapes=[pltpu.SemaphoreType.DMA((count, GATHER_SEMS))],
+        cost_estimate=transfer_cost(sum(shard.size for shard in shards) * owners),
         compiler_params=pltpu.CompilerParams(
             collective_id=collective_id, has_side_effects=True, vmem_limit_bytes=VMEM_LIMIT
         ),
@@ -392,6 +393,83 @@
                 self.share_copy(turn).wait_send()
 
 
+GROUP_SEMS = 13
+
+
+class GroupReduce:
+    def __init__(self, share, out, scratch, sems):
+        self.share, self.out, self.sems = share, out, sems
+        self.own, self.got = scratch
+        self.rows, self.columns = out.shape
+        self.chunk = 16
+
+    def load(self):
+        return pltpu.make_async_copy(self.share, self.own, self.sems.at[0])
+
+    def group_copy(self, other):
+        group, level, core = place()
+        peer = partner(group, other)
+        return remote(
+            self.own.at[quarter(peer, self.rows, self.columns)],
+            self.got.at[other - 1],
+            self.sems.at[other],
+            self.sems.at[3 + other],
+            (peer, 2 * level + core),
+        )
+
+    def share_copy(self, other):
+        group, level, core = place()
+        mine = self.out.at[quarter(group, self.rows, self.columns)]
+        return remote(
+            mine,
+            mine,
+            self.sems.at[6 + other],
+            self.sems.at[9 + other],
+            (partner(group, other), 2 * level + core),
+        )
+
+    def first(self):
+        self.load().start()
+
+    def second(self):
+        self.load().wait()
+        for other in TURNS:
+            self.group_copy(other).start()
+
+    def third(self):
+        group, _, _ = place()
+        high, wide = quarter_shape(self.rows, self.columns)
+        row_part, column_part = quarter(group, self.rows, self.columns)
+        for other in TURNS:
+            self.group_copy(other).wait_recv()
+
+        def add(step, carry):
+            at = pl.multiple_of(step * self.chunk, self.chunk)
+            rows = pl.ds(at, self.chunk)
+            mine = pl.ds(pl.multiple_of(row_part.start + at, self.chunk), self.chunk)
+            total = self.own[mine, column_part].astype(jnp.float32)
+            for slot in range(3):
+                total = total + self.got[slot, rows, :].astype(jnp.float32)
+            self.out[mine, column_part] = total.astype(self.out.dtype)
+            return carry
+
+        lax.fori_loop(0, high // self.chunk, add, 0)
+        for other in TURNS:
+            self.share_copy(other).start()
+
+    def fourth(self):
+        pass
+
+    def fifth(self):
+        for other in TURNS:
+            self.share_copy(other).wait_recv()
+
+    def sixth(self):
+        for other in TURNS:
+            self.group_copy(other).wait_send()
+            self.share_copy(other).wait_send()
+
+
 class Spread:
     def __init__(self, full, sems):
         self.full, self.sems = full, sems
@@ -423,71 +501,119 @@
                 self.level_copy(turn).wait_send()
 
 
-def reduce_kernel(*refs, count, spread):
-    grads, refs = refs[:count], refs[count:]
-    squares = None
-    if spread:
-        squares, refs = refs[0], refs[1:]
-    outs, refs = refs[:count], refs[count:]
-    if spread:
-        full, refs = refs[0], refs[1:]
-    sems, refs = refs[0], refs[1:]
-    if spread:
-        spread_sems, refs = refs[0], refs[1:]
+def squares_in(out):
+    def add(step, total):
+        piece = out[pl.ds(pl.multiple_of(step * 16, 16), 16), :].astype(jnp.float32)
+        piece = piece * piece
+        for lane in range(0, out.shape[1], LANES):
+            total = total + piece[:, lane : lane + LANES]
+        return total
+
+    total = lax.fori_loop(0, out.shape[0] // 16, add, jnp.zeros((16, LANES), jnp.float32))
+    return jnp.sum(total, 0, keepdims=True)
+
+
+def run_stages(jobs, stages):
+    for stage in stages:
+        for job in jobs:
+            getattr(job, stage)()
+
+
+STAGES = ("first", "second", "third", "fourth", "fifth", "sixth")
+
+
+def whole_scratch(grad):
+    _, rows, columns = grad.shape
+    high, wide = quarter_shape(rows, columns)
+    shapes = ((4, rows, columns), (4, rows, columns), (3, 4, high, wide), (4, high, wide))
+    return [pltpu.VMEM(shape, grad.dtype) for shape in (*shapes, (3, high, wide))]
+
+
+def reduce_kernel(*refs):
+    count = (len(refs) - 1) // 7
+    grads, outs, sems, refs = refs[:count], refs[count : 2 * count], refs[2 * count], refs[2 * count + 1 :]
     jobs = [
         Reduce(grads[i], outs[i], refs[5 * i : 5 * i + 5], sems.at[i]) for i in range(count)
     ]
     greet()
-    for stage in ("first", "second", "third", "fourth", "fifth"):
-        for job in jobs:
-            getattr(job, stage)()
-    if spread:
-        _, level, core = place()
-        total = squares[...]
-        for out in outs[:-1]:
-            for step in range(out.shape[0] // 16):
-                piece = out[step * 16 : step * 16 + 16, :].astype(jnp.float32)
-                piece = jnp.sum(piece * piece, 0, keepdims=True)
-                for lane in range(0, out.shape[1], LANES):
-                    total = total + piece[:, lane : lane + LANES]
-        mine = 2 * level + core
-        last = outs[-1].shape[0] - 1
-        full[mine] = outs[-1][...]
-        full[mine, last : last + 1, :] = total
-        Spread(full, spread_sems).run()
-    for job in jobs:
-        job.sixth()
-
-
-def reduce_call(grads, collective_id, squares=None):
-    count = len(grads)
-    spread = squares is not None
+    run_stages(jobs, STAGES)
+
+
+def transfer_cost(size):
+    return pl.CostEstimate(flops=4000 * size, bytes_accessed=2 * size, transcendentals=0)
+
+
+def reduce_call(grads, collective_id):
+    in_vmem = pl.BlockSpec(memory_space=pltpu.VMEM)
+    scratch = [pltpu.SemaphoreType.DMA((len(grads), REDUCE_SEMS))]
+    for grad in grads:
+        scratch.extend(whole_scratch(grad))
+    return pl.pallas_call(
+        reduce_kernel,
+        in_specs=[pl.BlockSpec(memory_space=pl.ANY)] * len(grads),
+        out_specs=[in_vmem] * len(grads),
+        out_shape=[jax.ShapeDtypeStruct(g.shape[1:], g.dtype) for g in grads],
+        scratch_shapes=scratch,
+        compiler_params=pltpu.CompilerParams(
+            collective_id=collective_id, has_side_effects=True, vmem_limit_bytes=VMEM_LIMIT
+        ),
+        cost_estimate=pl.CostEstimate(flops=0, bytes_accessed=0, transcendentals=0),
+        name="reduce_gradients",
+    )(*grads)
+
+
+def finish_kernel(*refs, done, partly):
+    finished, refs = refs[:done], refs[done:]
+    shares, small, refs = refs[:partly], refs[partly], refs[partly + 1 :]
+    outs, small_out, full, refs = refs[:partly], refs[partly], refs[partly + 1], refs[partly + 2 :]
+    sems, group_sems, spread_sems, refs = refs[0], refs[1], refs[2], refs[3:]
+    job = Reduce(small, small_out, refs[:5], sems)
+    refs = refs[5:]
+    jobs = [
+        GroupReduce(shares[i], outs[i], refs[2 * i : 2 * i + 2], group_sems.at[i])
+        for i in range(partly)
+    ]
+    greet()
+    run_stages([job, *jobs], STAGES[:2])
+    total = sum(squares_in(out) for out in finished)
+    run_stages([*jobs, job], STAGES[2:5])
+    total = total + sum(squares_in(out) for out in outs)
+    _, level, core = place()
+    mine = 2 * level + core
+    last = small_out.shape[0] - 1
+    full[mine] = small_out[...]
+    full[mine, last : last + 1, :] = total
+    Spread(full, spread_sems).run()
+    run_stages([job, *jobs], STAGES[5:])
+
+
+def finish_call(finished, shares, small, collective_id):
+    done, partly = len(finished), len(shares)
     anywhere = pl.BlockSpec(memory_space=pl.ANY)
     in_vmem = pl.BlockSpec(memory_space=pltpu.VMEM)
-    scratch = [pltpu.SemaphoreType.DMA((count, REDUCE_SEMS))]
-    if spread:
-        scratch.append(pltpu.SemaphoreType.DMA((14,)))
-    for grad in grads:
-        _, rows, columns = grad.shape
-        high, wide = quarter_shape(rows, columns)
-        for shape in ((4, rows, columns), (4, rows, columns), (3, 4, high, wide), (4, high, wide), (3, high, wide)):
-            scratch.append(pltpu.VMEM(shape, grad.dtype))
-    out_shape = [jax.ShapeDtypeStruct(g.shape[1:], g.dtype) for g in grads]
-    operands = list(grads)
-    if spread:
-        out_shape.append(jax.ShapeDtypeStruct(grads[-1].shape, grads[-1].dtype))
-        operands.append(squares)
+    scratch = [
+        pltpu.SemaphoreType.DMA((REDUCE_SEMS,)),
+        pltpu.SemaphoreType.DMA((partly, GROUP_SEMS)),
+        pltpu.SemaphoreType.DMA((14,)),
+        *whole_scratch(small),
+    ]
+    for share in shares:
+        scratch.append(pltpu.VMEM(share.shape, share.dtype))
+        scratch.append(pltpu.VMEM((3, *quarter_shape(*share.shape)), share.dtype))
+    out_shape = [jax.ShapeDtypeStruct(s.shape, s.dtype) for s in shares]
+    out_shape.append(jax.ShapeDtypeStruct(small.shape[1:], small.dtype))
+    out_shape.append(jax.ShapeDtypeStruct(small.shape, small.dtype))
     return pl.pallas_call(
-        functools.partial(reduce_kernel, count=count, spread=spread),
-        in_specs=[anywhere] * count + [in_vmem] * spread,
+        functools.partial(finish_kernel, done=done, partly=partly),
+        in_specs=[in_vmem] * done + [anywhere] * (partly + 1),
         out_specs=[in_vmem] * len(out_shape),
         out_shape=out_shape,
         scratch_shapes=scratch,
         compiler_params=pltpu.CompilerParams(
             collective_id=collective_id, has_side_effects=True, vmem_limit_bytes=VMEM_LIMIT
         ),
-        name="reduce_gradients",
-    )(*operands)
+        name="finish_gradients",
+    )(*finished, *shares, small)
 
 
 def with_kernels():
@@ -500,22 +626,24 @@
     return [lax.all_gather(shard, "fsdp", axis=0, tiled=True) for shard in shards]
 
 
-def reduce_all(grads, collective_id, squares=None):
+def reduce_all(grads, collective_id):
     if with_kernels():
-        return reduce_call(grads, collective_id, squares)
-    outs = [
-        lax.psum(lax.psum_scatter(grad, "fsdp", scatter_dimension=0), "dp") for grad in grads
-    ]
-    if squares is not None:
-        for out in outs[:-1]:
-            squares = squares + squares_of(out)
-        outs.append(lax.all_gather(outs[-1].at[-1:].set(squares), "fsdp", axis=0))
-    return outs
-
-
-def squares_of(item):
-    total = jnp.sum(jnp.square(item.astype(jnp.float32)))
-    return jnp.full((1, LANES), 1.0 / LANES, jnp.float32) * total
+        return reduce_call(grads, collective_id)
+    return [lax.psum(scatter(grad), "dp") for grad in grads]
+
+
+def finish_all(finished, shares, small, collective_id):
+    if with_kernels():
+        return finish_call(finished, shares, small, collective_id)
+    outs = [lax.psum(share, "dp") for share in shares]
+    own = lax.psum(scatter(small), "dp")
+    total = sum(jnp.sum(jnp.square(out.astype(jnp.float32))) for out in (*finished, *outs))
+    row = jnp.full((1, LANES), 1.0 / LANES, jnp.float32) * total
+    return [*outs, own, lax.all_gather(own.at[-1:].set(row), "fsdp", axis=0)]
+
+
+def scatter(grad):
+    return lax.psum_scatter(grad, "fsdp", scatter_dimension=0)
 
 
 def by_owner(grad, low=jnp.bfloat16):
@@ -769,22 +897,22 @@
     owners = lax.axis_size("fsdp")
     low = jnp.bfloat16
     vector_size = layer_vector.size
-    kernel_full, vectors = gather_all(
-        [patch_kernel.astype(low), padded_rows(layer_vector.astype(low).reshape(-1), 32)],
-        (True, False),
+    kernel_full, vectors, input_zero = gather_all(
+        [
+            patch_kernel.astype(low),
+            padded_rows(layer_vector.astype(low).reshape(-1), 32),
+            input_proj[0].astype(low),
+        ],
+        (True, False, True),
         1,
     )
     vectors = vectors.reshape(owners, -1)[:, :vector_size].reshape(owners, *layer_vector.shape)
     vectors = jnp.swapaxes(vectors, 0, 1).reshape(LAYERS, -1)
-    head_shard = jnp.pad(head_weight.astype(low), ((0, 0), (0, -CLS % LANES)))
-    full_zero = gather_all(
-        [input_proj[0].astype(low), output_proj[0].astype(low)], (True, True), 2
-    )
-    full_one = gather_all(
-        [input_proj[1].astype(low), output_proj[1].astype(low), head_shard], (True,) * 3, 3
-    )
-    layer_weights = [(*full_zero, vectors[0]), (*full_one[:2], vectors[1])]
-    head_full = full_one[2][:, :CLS]
+    output_zero, input_one, output_one, head_full = (
+        lax.all_gather(shard.astype(low), "fsdp", axis=0, tiled=True)
+        for shard in (output_proj[0], input_proj[1], output_proj[1], head_weight)
+    )
+    layer_weights = [(input_zero, output_zero, vectors[0]), (input_one, output_one, vectors[1])]
     global_low = rounded(global_vector)
     position_low = rounded(position_table)
     embed_pre = matmul(pixels, kernel_full) + global_low[:D]
@@ -816,9 +944,11 @@
     final_grad = jnp.dot(member, pooled_grad / image_sizes[:, None], precision=HIGHEST)
     stream_grad, final_gain, final_shift = final_back(final_grad)
     stream_grad, grads_one = layer_backward(stream_grad, layer_weights[1], saved_layers[1])
-    shares_one = reduce_all([by_owner(grad) for grad in (*grads_one[:3], head_grad)], 4)
+    stream_grad, *parts_one = lax.optimization_barrier(
+        (stream_grad, *(by_owner(grad) for grad in (*grads_one[:3], head_grad)))
+    )
+    parts_one = [scatter(part) for part in parts_one]
     stream_grad, grads_zero = layer_backward(stream_grad, layer_weights[0], saved_layers[0])
-    shares_zero = reduce_all([by_owner(grad) for grad in grads_zero[:3]], 5)
     embed_low = stream_grad.astype(jnp.bfloat16)
     position_grad = jnp.dot(pos_weights.T, stream_grad, precision=HIGHEST)
     vector_part = jnp.stack([grads_zero[3], grads_one[3]]).reshape(LAYERS, owners, -1)
@@ -842,10 +972,11 @@
     used = vector_rows + rest_rows
     block_rows = (used // 64 + 1) * 64
     small = jnp.pad(small.reshape(owners, used, LANES), ((0, 0), (0, block_rows - used), (0, 0)))
-    squares = sum(squares_of(item) for item in (*shares_zero, *shares_one))
-    kernel_sum, small_share, small_full = reduce_all(
-        [by_owner(matmul(pixels.T, embed_low)), small], 6, squares
-    )
+    summed = reduce_all(
+        [by_owner(grad) for grad in (*grads_zero[:3], matmul(pixels.T, embed_low))], 2
+    )
+    shares_zero, kernel_sum = summed[:3], summed[3]
+    *shares_one, small_share, small_full = finish_all(summed, parts_one, small, 3)
     rest_sum = small_full[:, vector_rows:used].reshape(-1)
     position_sum = rest_sum[: position_grad.size].reshape(position_grad.shape)
     global_sum = rest_sum[position_grad.size :][: global_vector.shape[0]]

time: 993 us -> 847 us (0.85)
  Pallas kernels: 592 us -> 406 us
  waiting for transfers between devices: 0 us -> 31.9 us
    pallas_call x3 -> x1, Pallas kernels: 198 us -> 86.2 us  [gather_call(): pl.pallas_call(functools.partial(gather_kernel, split=split), in_specs=[a...]
    pallas_call x3 -> x2, Pallas kernels: 275 us -> 200 us  [the longest x1 139 us: reduce_call(): pl.pallas_call(reduce_kernel, in_specs=[pl.BlockSpec(memory_space=pl.ANY)...]
    all_gather x0 -> x4, waiting for transfers between devices: none -> 29.9 us  [body(): lax.all_gather(shard.astype(low), 'fsdp', axis=0, tiled=True)]
    reduce_sum x7 -> x0, other arithmetic: 13.6 us -> none  [squares_of(): total = jnp.sum(jnp.square(item.astype(jnp.float32)))]
  transfers between devices with their start and end apart: 0 -> 8, of which waited for: 0 -> 2; matrix products, arithmetic and copies ran while one was open for 0% -> 26% of each run, Pallas kernels for 0% -> 38%
where the time goes in v3:
time: 847 us; the launch traced here: 842 us
  Pallas kernels  406 us (48%)
  matrix products  238 us (28%)
  other arithmetic  88.3 us (10%)
  local copies, waits for them, and re-layouts  55.9 us (7%)
  waiting for transfers between devices  31.9 us (4%)
  between operations  22 us (3%)
    dot_general x29, matrix products, matmul(): return jnp.dot(left, right, preferred_element_type=jnp.float32)  226 us
    pallas_call x1, Pallas kernels, reduce_call(): pl.pallas_call(reduce_kernel, in_specs=[pl.BlockSpec(memory_space=pl.ANY)...  139 us
    pallas_call x1, Pallas kernels, gather_call(): pl.pallas_call(functools.partial(gather_kernel, split=split), in_specs=[a...  86.2 us
    pallas_call x2, Pallas kernels, attention_forward(): pl.pallas_call(functools.partial(attention_forward_kernel, block=block),...  62.3 us
    pallas_call x1, Pallas kernels, finish_call(): pl.pallas_call(functools.partial(finish_kernel, done=done, partly=partly)...  60.5 us
    pallas_call x2, Pallas kernels, attention_backward(): pl.pallas_call(functools.partial(attention_backward_kernel, block=block),...  57.5 us
    all_gather x4, waiting for transfers between devices, body(): lax.all_gather(shard.astype(low), 'fsdp', axis=0, tiled=True)  29.9 us
    reduce_sum x7, other arithmetic, layer_norm(): return center * lax.rsqrt(spread + NORM_EPS) * gain + shift  21.4 us
  transfers between devices with their start and end apart: 8, of which 2 were waited for; matrix products, arithmetic and copies ran while one was open for 26% of the time, Pallas kernels for 38%

profile of v3, /device:TPU:0, one launch (start us, length us, event | category | flops | bytes accessed | tf_op | source)
XLA Modules:
  0.0 842.4 jit_solution(8000775047805969565)
XLA Ops:
  7.2 2.0 convert.27
  10.5 2.4 convert.26
  17.7 86.2 %gather_weights.1 = (bf16[8,384,768]{2,1,0:T(8,128)(2,1)}, bf16[8,32,128]{2,1,0:T(8,128)(2,1)}, bf16[8,96,5376]{2,1,0:T(8,128)(2,1)}) custom-call(bf16[384,768]{1,0:T(8,128)(2,1)} %convert_element_type.243.refs_0_, bf16[32,128]{1,0:T(8,128)(2,1)} %pad_bitcast_fusion.refs_1_, bf16[96,5376]{1,0:T(8,128)(2,1)} %get-tuple-element.133.refs_2_), custom_call_target="tpu_custom_call" | custom-call | flops 26083328000 | bytes 13041664 | tf_op jit(solution)/shard_map/gather_weights/pallas_call | solution.py:236
  106.8 8.8 %fusion.123 = f32[768,1024]{1,0:T(8,128)S(1)} fusion(bf16[3072,768]{1,0:T(8,128)(2,1)} %bitcast.167, bf16[1024,3072]{1,0:T(8,128)(2,1)} %param.25), kind=kOutput, calls=%fused_computation.287 | convolution fusion | flops 4831838208 | bytes 14155776 | tf_op jit(solution)/shard_map/dot_general | solution.py:53
  119.3 8.5 %add_convert_fusion.1.q_ref.k_ref.v_ref = bf16[1024,2304]{1,0:T(8,128)(2,1)} fusion(f32[2304]{0:T(1024)S(1)} %slice-done.3, bf16[768,5376]{1,0:T(8,128)(2,1)} %bitcast.163, f32[1024,768]{0,1:T(8,128)S(1)} %get-tuple-element.160, f32[768]{0:T(1024)S(1)} %get-tuple-element.148, f32[768]{0:T(1024)S(1)} %get-tuple-element.149, f32[1024]{0:T(1024)S(1)} %fusion.82, ...), kind=kOutput, calls=%fused_computation.25 | convolution fusion | flops 3632529408 | bytes 11426816 | tf_op jit(solution)/shard_map/dot_general | solution.py:53
  127.7 31.0 %attention_forward.2 = (bf16[1024,768]{1,0:T(8,128)(2,1)}, bf16[12,1024,1024]{2,1,0:T(8,128)(2,1)}, f32[1024,768]{1,0:T(8,128)}) custom-call(bf16[1024,2304]{1,0:T(8,128)(2,1)} %add_convert_fusion.1.q_ref.k_ref.v_ref, bf16[1024,2304]{1,0:T(8,128)(2,1)} %add_convert_fusion.1.q_ref.k_ref.v_ref, bf16[1024,2304]{1,0:T(8,128)(2,1)} %add_convert_fusion.1.q_ref.k_ref.v_ref, ...), custom_call_target="tpu_custom_call" | custom-call | flops 12884901888 | bytes 34603008 | tf_op jit(solution)/shard_map/attention_forward/pallas_call | solution.py:693
  158.8 3.4 fusion.113
  162.7 12.1 %fusion.25 = f32[1024,3072]{1,0:T(8,128)} fusion(bf16[768,5376]{1,0:T(8,128)(2,1)} %bitcast.164, f32[1024,768]{0,1:T(8,128)S(1)} %get-tuple-element.162, f32[768]{0:T(1024)S(1)} %get-tuple-element.146, f32[768]{0:T(1024)S(1)} %get-tuple-element.144, f32[1024]{0:T(1024)S(1)} %fusion.83, f32[1024]{0:T(1024)S(1)} %broadcast_multiply_fusion.4), kind=kOutput, calls=%fused_computation.57 | convolution fusion | flops 4835770368 | bytes 20461568 | tf_op jit(solution)/shard_map/dot_general | solution.py:53
  174.9 9.9 %fusion.114 = (f32[1024]{0:T(1024)S(1)}, f32[1024,768]{0,1:T(8,128)S(1)}) fusion(f32[768]{0:T(1024)S(1)} %get-tuple-element.145, f32[1024,768]{0,1:T(8,128)S(1)} %get-tuple-element.162, bf16[1,3840,768]{2,1,0:T(8,128)(2,1)S(1)} %bitcast.158, f32[1024,3072]{1,0:T(8,128)} %fusion.25, f32[3072]{0:T(1024)S(1)} %slice.222), kind=kOutput, calls=%fused_computation.278 | convolution fusion | flops 4865653760 | bytes 23613440 | tf_op jit(solution)/shard_map/dot_general | solution.py:53
  185.2 6.6 all-gather.12.cloned.1.call-done
  191.8 7.7 add_convert_fusion.q_ref.k_ref.v_ref
  199.5 31.3 %attention_forward.3 = (bf16[1024,768]{1,0:T(8,128)(2,1)}, bf16[12,1024,1024]{2,1,0:T(8,128)(2,1)}, f32[1024,768]{1,0:T(8,128)}) custom-call(bf16[1024,2304]{1,0:T(8,128)(2,1)} %add_convert_fusion.q_ref.k_ref.v_ref, bf16[1024,2304]{1,0:T(8,128)(2,1)} %add_convert_fusion.q_ref.k_ref.v_ref, bf16[1024,2304]{1,0:T(8,128)(2,1)} %add_convert_fusion.q_ref.k_ref.v_ref, ...), custom_call_target="tpu_custom_call" | custom-call | flops 12884901888 | bytes 34603008 | tf_op jit(solution)/shard_map/attention_forward/pallas_call | solution.py:693
  230.8 23.3 %all-gather.14.cloned.1.call-done = bf16[1,3840,768]{2,1,0:T(8,128)(2,1)} async-done(((bf16[1,480,768]{2,1,0:T(8,128)(2,1)}), bf16[1,3840,768]{2,1,0:T(8,128)(2,1)}) %all-gather.14.cloned.1.call-update) | async-done | bytes 5898256 | tf_op jit(solution)/shard_map/all_gather | solution.py:912
  254.1 3.5 fusion.115
  258.3 8.8 %fusion.21 = f32[1024,3072]{1,0:T(8,128)} fusion(bf16[768,5376]{1,0:T(8,128)(2,1)S(1)} %bitcast.151, f32[1024,768]{0,1:T(8,128)S(1)} %get-tuple-element.166, f32[768]{0:T(1024)S(1)} %get-tuple-element.140, f32[768]{0:T(1024)S(1)} %get-tuple-element.138, f32[1024]{0:T(1024)S(1)} %fusion.85, f32[1024]{0:T(1024)S(1)} %broadcast_multiply_fusion.2), kind=kOutput, calls=%fused_computation.53 | convolution fusion | flops 4835770368 | bytes 20463616 | tf_op jit(solution)/shard_map/dot_general | solution.py:53
  267.0 10.0 %fusion.116 = (f32[1024]{0:T(1024)S(1)}, f32[1024,768]{0,1:T(8,128)S(1)}) fusion(f32[768]{0:T(1024)S(1)} %get-tuple-element.139, f32[1024,768]{0,1:T(8,128)S(1)} %get-tuple-element.166, bf16[1,3840,768]{2,1,0:T(8,128)(2,1)S(1)} %bitcast.160, f32[1024,3072]{1,0:T(8,128)} %fusion.21, f32[3072]{0:T(1024)S(1)} %slice.237), kind=kOutput, calls=%fused_computation.280 | convolution fusion | flops 4865653760 | bytes 23613440 | tf_op jit(solution)/shard_map/dot_general | solution.py:53
  278.7 2.0 fusion.49
  283.9 1.9 convolution_divide_fusion
  285.9 3.7 fusion.122
  289.6 3.6 copy.78
  293.2 4.5 multiply_reduce_fusion
  301.6 18.1 %convert_reduce_fusion = (f32[3072]{0:T(1024)}, bf16[1024,3072]{1,0:T(8,128)(2,1)}) fusion(f32[1024,3072]{1,0:T(8,128)} %fusion.21, f32[3072]{0:T(1024)S(1)} %slice.237, bf16[1024,768]{0,1:T(8,128)(2,1)S(1)} %get-tuple-element.122, bf16[1,3840,768]{2,1,0:T(8,128)(2,1)S(1)} %bitcast.162), kind=kOutput, calls=%fused_computation.18 | convolution fusion | flops 4904186880 | bytes 25190400 | tf_op jit(solution)/shard_map/dot_general | solution.py:53
  319.7 9.0 %fusion.119 = (f32[768]{0:T(1024)}, f32[1024,768]{1,0:T(8,128)}) fusion(bf16[1024,3072]{1,0:T(8,128)(2,1)} %get-tuple-element.120, bf16[768,5376]{1,0:T(8,128)(2,1)S(1)} %bitcast.154), kind=kOutput, calls=%fused_computation.283 | convolution fusion | flops 4832623616 | bytes 14158848 | tf_op jit(solution)/shard_map/dot_general | solution.py:53
  328.7 3.6 copy.79
  332.2 4.5 multiply_reduce_fusion.1
  340.1 4.4 convolution_convert_fusion.8.grad_ref
  344.5 29.0 %attention_backward.2 = bf16[1024,2304]{1,0:T(8,128)(2,1)} custom-call(bf16[1024,2304]{1,0:T(8,128)(2,1)} %add_convert_fusion.q_ref.k_ref.v_ref, bf16[1024,2304]{1,0:T(8,128)(2,1)} %add_convert_fusion.q_ref.k_ref.v_ref, bf16[1024,2304]{1,0:T(8,128)(2,1)} %add_convert_fusion.q_ref.k_ref.v_ref, bf16[12,1024,1024]{2,1,0:T(8,128)(2,1)} %get-tuple-element.55.expo_ref, ...), custom_call_target="tpu_custom_call" | custom-call | flops 25769803776 | bytes 40894464 | tf_op jit(solution)/shard_map/attention_backward/pallas_call | solution.py:768
  373.5 9.1 %fusion.118 = (f32[768]{0:T(1024)S(1)}, f32[1024,768]{1,0:T(8,128)}) fusion(bf16[1024,2304]{1,0:T(8,128)(2,1)} %attention_backward.2, bf16[768,5376]{1,0:T(8,128)(2,1)} %bitcast.150), kind=kOutput, calls=%fused_computation.282 | convolution fusion | flops 3624664320 | bytes 11406336 | tf_op jit(solution)/shard_map/dot_general | solution.py:53
  382.5 5.6 convolution_convert_fusion.6
  388.2 9.9 %convolution_convert_fusion.4 = bf16[768,3072]{1,0:T(8,128)(2,1)} fusion(bf16[1024,3072]{1,0:T(8,128)(2,1)} %get-tuple-element.120, f32[1024,768]{0,1:T(8,128)S(1)} %copy-done.13, f32[768]{0:T(1024)S(1)} %get-tuple-element.140, f32[768]{0:T(1024)S(1)} %get-tuple-element.138, f32[1024]{0:T(1024)S(1)} %fusion.85, f32[1024]{0:T(1024)S(1)} %broadcast_multiply_fusion.2), kind=kOutput, calls=%fused_computation.34 | convolution fusion | flops 4838129664 | bytes 14170112 | tf_op jit(solution)/shard_map/dot_general | solution.py:53
  398.2 10.4 %convolution_convert_fusion.3 = bf16[3072,768]{1,0:T(8,128)(2,1)} fusion(bf16[1024,768]{0,1:T(8,128)(2,1)S(1)} %copy-done.42, f32[1024,3072]{1,0:T(8,128)S(1)} %bitcast.169, f32[3072]{0:T(1024)S(1)} %slice.237), kind=kOutput, calls=%fused_computation.33 | convolution fusion | flops 4865654784 | bytes 18886656 | tf_op jit(solution)/shard_map/dot_general | solution.py:53
  408.6 2.4 convolution_convert_fusion.11
  412.8 3.6 copy.80
  416.3 2.5 multiply_reduce_fusion.7
  422.0 3.4 add_add_fusion.7
  427.3 5.2 pad_maximum_fusion
  436.3 17.0 %convert_reduce_fusion.1 = (f32[3072]{0:T(1024)}, bf16[1024,3072]{1,0:T(8,128)(2,1)S(1)}) fusion(f32[1024,3072]{1,0:T(8,128)} %fusion.25, f32[3072]{0:T(1024)S(1)} %copy-done.90, bf16[1,3840,768]{2,1,0:T(8,128)(2,1)} %all-gather.10.cloned.1.call-done, f32[1024,768]{0,1:T(8,128)S(1)} %copy-done.19), kind=kOutput, calls=%fused_computation.19 | convolution fusion | flops 4904973312 | bytes 26763264 | tf_op jit(solution)/shard_map/dot_general | solution.py:53
  453.4 11.9 %fusion.121 = (f32[768]{0:T(1024)}, f32[1024,768]{1,0:T(8,128)}) fusion(bf16[1024,3072]{1,0:T(8,128)(2,1)S(1)} %get-tuple-element.116, bf16[768,5376]{1,0:T(8,128)(2,1)} %bitcast.165), kind=kOutput, calls=%fused_computation.285 | convolution fusion | flops 4832623616 | bytes 14158848 | tf_op jit(solution)/shard_map/dot_general | solution.py:53
  465.3 4.1 copy.82
  469.4 3.0 multiply_reduce_fusion.3
  473.4 1.9 copy-done.20
  475.7 4.4 convolution_convert_fusion.7.grad_ref
  480.2 28.6 %attention_backward.3 = bf16[1024,2304]{1,0:T(8,128)(2,1)} custom-call(bf16[1024,2304]{1,0:T(8,128)(2,1)} %add_convert_fusion.1.q_ref.k_ref.v_ref, bf16[1024,2304]{1,0:T(8,128)(2,1)} %add_convert_fusion.1.q_ref.k_ref.v_ref, bf16[1024,2304]{1,0:T(8,128)(2,1)} %add_convert_fusion.1.q_ref.k_ref.v_ref, bf16[12,1024,1024]{2,1,0:T(8,128)(2,1)} %get-tuple-element.51.expo_ref, ...), custom_call_target="tpu_custom_call" | custom-call | flops 25769803776 | bytes 40894464 | tf_op jit(solution)/shard_map/attention_backward/pallas_call | solution.py:768
  508.7 9.6 %fusion.120 = (f32[768]{0:T(1024)}, f32[1024,768]{1,0:T(8,128)}) fusion(bf16[1024,2304]{1,0:T(8,128)(2,1)} %attention_backward.3, bf16[768,5376]{1,0:T(8,128)(2,1)} %bitcast.166), kind=kOutput, calls=%fused_computation.284 | convolution fusion | flops 3624664320 | bytes 11406336 | tf_op jit(solution)/shard_map/dot_general | solution.py:53
  518.4 3.7 copy.83
  522.1 2.4 multiply_reduce_fusion.5
  525.1 3.3 multiply_reduce_fusion.4
  529.0 4.4 convert_reduce_fusion.4
  535.1 6.7 fusion.14
  541.9 6.7 copy.84
  548.7 3.1 convert_reduce_fusion.2
  553.4 3.1 convert_reduce_fusion.3
  557.5 5.0 fusion.124
  564.5 2.3 concatenate.31
  568.5 3.5 convolution_convert_fusion.10
  572.0 12.3 %convolution_convert_fusion.1 = bf16[3072,768]{1,0:T(8,128)(2,1)S(1)} fusion(f32[1024,768]{0,1:T(8,128)S(1)} %copy-done.22, f32[1024,3072]{1,0:T(8,128)} %fusion.25, f32[3072]{0:T(1024)S(1)} %copy-done.91), kind=kOutput, calls=%fused_computation.31 | convolution fusion | flops 4866441216 | bytes 20459520 | tf_op jit(solution)/shard_map/dot_general | solution.py:53
  584.4 2.9 pad_maximum_fusion.1
  587.4 5.7 convolution_convert_fusion.5
  593.1 7.1 convolution_convert_fusion.2
  600.3 139.4 %reduce_gradients.1 = (bf16[96,2304]{1,0:T(8,128)(2,1)}, bf16[96,3072]{1,0:T(8,128)(2,1)}, bf16[480,768]{1,0:T(8,128)(2,1)}, bf16[384,768]{1,0:T(8,128)(2,1)}) custom-call(bf16[8,96,2304]{2,1,0:T(8,128)(2,1)} %bitcast.127, bf16[8,96,3072]{2,1,0:T(8,128)(2,1)} %bitcast.125, bf16[8,480,768]{2,1,0:T(8,128)(2,1)} %bitcast.119, bf16[8,384,768]{2,1,0:T(8,128)(2,1)} %bitcast.120), custom_call_target="tpu_custom_call" | custom-call | tf_op jit(solution)/shard_map/reduce_gradients/pallas_call | solution.py:551
  739.8 60.5 %finish_gradients.1 = (bf16[96,2304]{1,0:T(8,128)(2,1)}, bf16[96,3072]{1,0:T(8,128)(2,1)}, bf16[480,768]{1,0:T(8,128)(2,1)}, bf16[96,1024]{1,0:T(8,128)(2,1)}, f32[64,128]{1,0:T(8,128)}, /*index=5*/f32[8,64,128]{2,1,0:T(8,128)}) custom-call(bf16[96,2304]{1,0:T(8,128)(2,1)} %get-tuple-element.58.refs_0_, bf16[96,3072]{1,0:T(8,128)(2,1)} %get-tuple-element.59.refs_1_, ...), custom_call_target="tpu_custom_call" | custom-call | tf_op jit(solution)/shard_map/finish_gradients/pallas_call | solution.py:606
  811.6 4.3 multiply_subtract_fusion.2
  822.3 7.1 multiply_subtract_fusion
  829.5 4.6 multiply_subtract_fusion.1
  (404 shorter events, 59.8 us)
Async XLA Ops:
  7.2 151.6 %all-gather.10.cloned.1.call-start = ((), (), s32[]{:S(2)}) async-start(), calls=%async_computation.9 | async-start | bytes 6635520 | tf_op jit(solution)/shard_map/all_gather | solution.py:912
  10.4 181.3 %all-gather.12.cloned.1.call-start = ((), (), s32[]{:S(2)}) async-start(), calls=%async_computation.10 | async-start | bytes 9289728 | tf_op jit(solution)/shard_map/all_gather | solution.py:912
  14.4 239.7 %all-gather.14.cloned.1.call-start = ((), (), s32[]{:S(2)}) async-start(), calls=%async_computation.11 | async-start | bytes 6635520 | tf_op jit(solution)/shard_map/all_gather | solution.py:912
  15.1 265.6 %all-gather.8.cloned.1.call-start = ((), (), s32[]{:S(2)}) async-start(), calls=%async_computation.4 | async-start | bytes 1769472 | tf_op jit(solution)/shard_map/all_gather | solution.py:912
  15.9 723.8 %reduce-scatter.11.cloned.1.call-start = ((), (), s32[]{:S(2)}) async-start(), calls=%async_computation.8 | async-start | bytes 1769472 | tf_op jit(solution)/shard_map/reduce_scatter | solution.py:646
  16.1 90.1 %copy-start.98 = (s32[8]{0:T(128)}, s32[8]{0:T(128)S(1)}, u32[]{:S(2)}) copy-start(s32[8]{0:T(128)S(1)} %convert_reduce_fusion.10) | copy-start | bytes 100
  17.7 87.8 %copy-start.60 = (f32[3304]{0:T(1024)S(1)}, f32[3304]{0:T(1024)}, u32[]{:S(2)}) copy-start(f32[3304]{0:T(1024)} %param.35) | copy-start | bytes 39652
  17.7 88.5 %copy-start.106 = (s32[1,8]{1,0:T(1,128)S(1)}, s32[1,8]{1,0:T(1,128)}, u32[]{:S(2)}) copy-start(s32[1,8]{1,0:T(1,128)} %param.27) | copy-start | bytes 100
  17.7 89.0 %copy-start.49 = (f32[49,768]{1,0:T(8,128)S(1)}, f32[49,768]{1,0:T(8,128)}, u32[]{:S(2)}) copy-start(f32[49,768]{1,0:T(8,128)} %param.34) | copy-start | bytes 451588
  105.3 10.4 %copy-start.54 = (f32[9984]{0:T(1024)}, f32[9984]{0:T(1024)S(1)}, u32[]{:S(2)}) copy-start(f32[9984]{0:T(1024)S(1)} %reshape.489) | copy-start | bytes 119812
  105.3 14.0 %copy-start.64 = (f32[768]{0:T(1024)}, f32[768]{0:T(1024)S(1)}, u32[]{:S(2)}) copy-start(f32[768]{0:T(1024)S(1)} %get-tuple-element.149) | copy-start | bytes 9220
  105.3 14.0 %copy-start.101 = (f32[768]{0:T(1024)}, f32[768]{0:T(1024)S(1)}, u32[]{:S(2)}) copy-start(f32[768]{0:T(1024)S(1)} %get-tuple-element.148) | copy-start | bytes 9220
  105.3 57.3 %copy-start.75 = (f32[768]{0:T(1024)}, f32[768]{0:T(1024)S(1)}, u32[]{:S(2)}) copy-start(f32[768]{0:T(1024)S(1)} %get-tuple-element.144) | copy-start | bytes 9220
  105.3 57.3 %copy-start.99 = (f32[768]{0:T(1024)}, f32[768]{0:T(1024)S(1)}, u32[]{:S(2)}) copy-start(f32[768]{0:T(1024)S(1)} %get-tuple-element.146) | copy-start | bytes 9220
  105.4 69.5 %copy-start.89 = (f32[3072]{0:T(1024)}, f32[3072]{0:T(1024)S(1)}, u32[]{:S(2)}) copy-start(f32[3072]{0:T(1024)S(1)} %slice.222) | copy-start | bytes 36868
  105.5 10.2 %copy-start.53 = (f32[9984]{0:T(1024)}, f32[9984]{0:T(1024)S(1)}, u32[]{:S(2)}) copy-start(f32[9984]{0:T(1024)S(1)} %reshape.490) | copy-start | bytes 119812
  106.8 8.9 %copy-start.37 = (f32[1024,49]{0,1:T(8,128)}, f32[1024,49]{0,1:T(8,128)S(1)}, u32[]{:S(2)}) copy-start(f32[1024,49]{0,1:T(8,128)S(1)} %mul.664) | copy-start | bytes 602116
  117.4 41.4 %copy-start = (f32[1024,768]{0,1:T(8,128)}, f32[1024,768]{0,1:T(8,128)S(1)}, u32[]{:S(2)}) copy-start(f32[1024,768]{0,1:T(8,128)S(1)} %get-tuple-element.160) | copy-start | bytes 9437188
  117.5 10.3 %copy-start.58 = (f32[1024]{0:T(1024)}, f32[1024]{0:T(1024)S(1)}, u32[]{:S(2)}) copy-start(f32[1024]{0:T(1024)S(1)} %broadcast_multiply_fusion.5) | copy-start | bytes 12292
  117.9 9.9 %copy-start.69 = (f32[1024]{0:T(1024)}, f32[1024]{0:T(1024)S(1)}, u32[]{:S(2)}) copy-start(f32[1024]{0:T(1024)S(1)} %multiply_reduce_fusion.14) | copy-start | bytes 12292
  117.9 9.9 %copy-start.81 = (f32[1024]{0:T(1024)}, f32[1024]{0:T(1024)S(1)}, u32[]{:S(2)}) copy-start(f32[1024]{0:T(1024)S(1)} %fusion.82) | copy-start | bytes 12292
  162.2 12.6 %copy-start.9 = (f32[1024,768]{0,1:T(8,128)}, f32[1024,768]{0,1:T(8,128)S(1)}, u32[]{:S(2)}) copy-start(f32[1024,768]{0,1:T(8,128)S(1)} %get-tuple-element.162) | copy-start | bytes 9437188
  162.2 12.6 %copy-start.62 = (f32[1024]{0:T(1024)}, f32[1024]{0:T(1024)S(1)}, u32[]{:S(2)}) copy-start(f32[1024]{0:T(1024)S(1)} %broadcast_multiply_fusion.4) | copy-start | bytes 12292
  162.2 12.6 %slice-start.8 = ((s8[5898240]{0:T(1024)(128)(4,1)}), s8[4194304]{0:T(1024)(128)(4,1)S(1)}, s32[]{:S(2)}) async-start(s8[5898240]{0:T(1024)(128)(4,1)} %bitcast.157), calls=%async_computation.20 | async-start | bytes 8388608
  162.6 12.2 %copy-start.71 = (f32[1024]{0:T(1024)}, f32[1024]{0:T(1024)S(1)}, u32[]{:S(2)}) copy-start(f32[1024]{0:T(1024)S(1)} %multiply_reduce_fusion.13) | copy-start | bytes 12292
  162.6 12.2 %copy-start.78 = (f32[1024]{0:T(1024)}, f32[1024]{0:T(1024)S(1)}, u32[]{:S(2)}) copy-start(f32[1024]{0:T(1024)S(1)} %fusion.83) | copy-start | bytes 12292
  162.7 12.2 %slice-start.9 = ((s8[5898240]{0:T(1024)(128)(4,1)}), s8[1703936]{0:T(1024)(128)(4,1)S(1)}, s32[]{:S(2)}) async-start(s8[5898240]{0:T(1024)(128)(4,1)} %bitcast.157), calls=%async_computation.21 | async-start | bytes 3407872
  185.2 14.4 %copy-start.73 = (f32[1024]{0:T(1024)}, f32[1024]{0:T(1024)S(1)}, u32[]{:S(2)}) copy-start(f32[1024]{0:T(1024)S(1)} %multiply_reduce_fusion.12) | copy-start | bytes 12292
  257.6 9.4 %copy-start.12 = (f32[1024,768]{0,1:T(8,128)}, f32[1024,768]{0,1:T(8,128)S(1)}, u32[]{:S(2)}) copy-start(f32[1024,768]{0,1:T(8,128)S(1)} %get-tuple-element.166) | copy-start | bytes 9437188
  257.6 9.4 %slice-start.10 = ((s8[5898240]{0:T(1024)(128)(4,1)}), s8[4194304]{0:T(1024)(128)(4,1)S(1)}, s32[]{:S(2)}) async-start(s8[5898240]{0:T(1024)(128)(4,1)} %bitcast.159), calls=%async_computation.22 | async-start | bytes 8388608
  258.3 8.8 %slice-start.11 = ((s8[5898240]{0:T(1024)(128)(4,1)}), s8[1703936]{0:T(1024)(128)(4,1)S(1)}, s32[]{:S(2)}) async-start(s8[5898240]{0:T(1024)(128)(4,1)} %bitcast.159), calls=%async_computation.23 | async-start | bytes 3407872
  283.3 10.0 %copy-start.97 = (f32[8]{0:T(128)}, f32[8]{0:T(128)S(1)}, u32[]{:S(2)}) copy-start(f32[8]{0:T(128)S(1)} %get-tuple-element.85) | copy-start | bytes 100
  300.4 19.3 %slice-start.4 = ((s8[8257536]{0:T(1024)(128)(4,1)}), s8[4194304]{0:T(1024)(128)(4,1)S(1)}, s32[]{:S(2)}) async-start(s8[8257536]{0:T(1024)(128)(4,1)} %bitcast.152), calls=%async_computation.16 | async-start | bytes 8388608
  301.3 18.3 %copy-start.41 = (bf16[1024,768]{0,1:T(8,128)(2,1)}, bf16[1024,768]{0,1:T(8,128)(2,1)S(1)}, u32[]{:S(2)}) copy-start(bf16[1024,768]{0,1:T(8,128)(2,1)S(1)} %get-tuple-element.122) | copy-start | bytes 4718596
  301.6 18.1 %slice-start.5 = ((s8[8257536]{0:T(1024)(128)(4,1)}), s8[4063232]{0:T(1024)(128)(4,1)S(1)}, s32[]{:S(2)}) async-start(s8[8257536]{0:T(1024)(128)(4,1)} %bitcast.152), calls=%async_computation.17 | async-start | bytes 8126464
  373.5 9.1 %copy-start.27 = (bf16[1024,2304]{1,0:T(8,128)(2,1)S(1)}, bf16[1024,2304]{1,0:T(8,128)(2,1)}, u32[]{:S(2)}) copy-start(bf16[1024,2304]{1,0:T(8,128)(2,1)} %attention_backward.2) | copy-start | bytes 14155780
  382.5 15.6 %slice-start.14 = ((s8[12582912]{0:T(1024)(128)(4,1)}), s8[4194304]{0:T(1024)(128)(4,1)S(1)}, s32[]{:S(2)}) async-start(s8[12582912]{0:T(1024)(128)(4,1)} %bitcast.168), calls=%async_computation.26 | async-start | bytes 8388608
  382.5 15.6 %slice-start.15 = ((s8[12582912]{0:T(1024)(128)(4,1)}), s8[4194304]{0:T(1024)(128)(4,1)S(1)}, s32[]{:S(2)}) async-start(s8[12582912]{0:T(1024)(128)(4,1)} %bitcast.168), calls=%async_computation.27 | async-start | bytes 8388608
  388.2 9.9 %copy-start.42 = (bf16[1024,768]{0,1:T(8,128)(2,1)S(1)}, bf16[1024,768]{0,1:T(8,128)(2,1)}, u32[]{:S(2)}) copy-start(bf16[1024,768]{0,1:T(8,128)(2,1)} %copy-done.41) | copy-start | bytes 4718596
  388.2 10.0 %slice-start.16 = ((s8[12582912]{0:T(1024)(128)(4,1)}), s8[4194304]{0:T(1024)(128)(4,1)S(1)}, s32[]{:S(2)}) async-start(s8[12582912]{0:T(1024)(128)(4,1)} %bitcast.168), calls=%async_computation.28 | async-start | bytes 8388608
  398.1 10.4 %copy-start.44 = (bf16[1024,768]{0,1:T(8,128)(2,1)S(1)}, bf16[1024,768]{0,1:T(8,128)(2,1)}, u32[]{:S(2)}) copy-start(bf16[1024,768]{0,1:T(8,128)(2,1)} %copy-done.43) | copy-start | bytes 4718596
  398.2 10.4 %copy-start.108 = (bf16[1024,768]{1,0:T(8,128)(2,1)S(1)}, bf16[1024,768]{1,0:T(8,128)(2,1)}, u32[]{:S(2)}) copy-start(bf16[1024,768]{1,0:T(8,128)(2,1)} %get-tuple-element.54.out_ref) | copy-start | bytes 4718596
  433.8 305.9 %reduce-scatter.5.cloned.1.call-start = ((), (), s32[]{:S(2)}) async-start(), calls=%async_computation.5 | async-start | bytes 3981312 | tf_op jit(solution)/shard_map/reduce_scatter | solution.py:646
  434.4 305.3 %reduce-scatter.7.cloned.1.call-start = ((), (), s32[]{:S(2)}) async-start(), calls=%async_computation.6 | async-start | bytes 5308416 | tf_op jit(solution)/shard_map/reduce_scatter | solution.py:646
  435.2 304.6 %reduce-scatter.9.cloned.1.call-start = ((), (), s32[]{:S(2)}) async-start(), calls=%async_computation.7 | async-start | bytes 6635520 | tf_op jit(solution)/shard_map/reduce_scatter | solution.py:646
  453.4 11.9 %copy-start.109 = (bf16[1024,3072]{1,0:T(8,128)(2,1)}, bf16[1024,3072]{1,0:T(8,128)(2,1)S(1)}, u32[]{:S(2)}) copy-start(bf16[1024,3072]{1,0:T(8,128)(2,1)S(1)} %get-tuple-element.116) | copy-start | bytes 18874372
  525.1 10.0 %slice-start.6 = ((s8[6291456]{0:T(1024)(128)(4,1)}), s8[4194304]{0:T(1024)(128)(4,1)S(1)}, s32[]{:S(2)}) async-start(s8[6291456]{0:T(1024)(128)(4,1)} %bitcast.155), calls=%async_computation.18 | async-start | bytes 8388608
  568.5 18.8 %slice-start = ((s8[4718592]{0:T(1024)(128)(4,1)}), s8[4194304]{0:T(1024)(128)(4,1)S(1)}, s32[]{:S(2)}) async-start(s8[4718592]{0:T(1024)(128)(4,1)} %bitcast.123), calls=%async_computation.12 | async-start | bytes 8388608
  572.0 15.3 %slice-start.1 = ((s8[4718592]{0:T(1024)(128)(4,1)}), s8[524288]{0:T(1024)(128)(4,1)S(1)}, s32[]{:S(2)}) async-start(s8[4718592]{0:T(1024)(128)(4,1)} %bitcast.123), calls=%async_computation.13 | async-start | bytes 1048576
  584.4 8.7 %slice-start.17 = ((s8[6291456]{0:T(1024)(128)(4,1)}), s8[2097152]{0:T(1024)(128)(4,1)S(1)}, s32[]{:S(2)}) async-start(s8[6291456]{0:T(1024)(128)(4,1)} %bitcast.170), calls=%async_computation.29 | async-start | bytes 4194304
  739.6 71.9 %copy-start.29 = (f32[384,768]{1,0:T(8,128)S(1)}, f32[384,768]{1,0:T(8,128)}, u32[]{:S(2)}) copy-start(f32[384,768]{1,0:T(8,128)} %param.29) | copy-start | bytes 3538948
  739.7 71.9 %copy-start.36 = (bf16[384,768]{1,0:T(8,128)(2,1)S(1)}, bf16[384,768]{1,0:T(8,128)(2,1)}, u32[]{:S(2)}) copy-start(bf16[384,768]{1,0:T(8,128)(2,1)} %get-tuple-element.61.refs_3_) | copy-start | bytes 1769476
  739.8 78.0 %copy-start.86 = (f32[3304]{0:T(1024)S(1)}, f32[3304]{0:T(1024)}, u32[]{:S(2)}) copy-start(f32[3304]{0:T(1024)} %param.49) | copy-start | bytes 39652
  739.8 78.0 %copy-start.87 = (f32[3304]{0:T(1024)S(1)}, f32[3304]{0:T(1024)}, u32[]{:S(2)}) copy-start(f32[3304]{0:T(1024)} %param.42) | copy-start | bytes 39652
  739.8 79.9 %copy-start.94 = (f32[2,1248]{1,0:T(2,128)S(1)}, f32[2,1248]{1,0:T(2,128)}, u32[]{:S(2)}) copy-start(f32[2,1248]{1,0:T(2,128)} %param.47) | copy-start | bytes 29956
  739.8 79.9 %copy-start.95 = (f32[2,1248]{1,0:T(2,128)S(1)}, f32[2,1248]{1,0:T(2,128)}, u32[]{:S(2)}) copy-start(f32[2,1248]{1,0:T(2,128)} %param.40) | copy-start | bytes 29956
  811.4 7.1 copy-start.55
  811.6 10.7 %copy-start.30 = (f32[2,96,5376]{2,1,0:T(8,128)S(1)}, f32[2,96,5376]{2,1,0:T(8,128)}, u32[]{:S(2)}) copy-start(f32[2,96,5376]{2,1,0:T(8,128)} %param.45) | copy-start | bytes 12386308
  811.6 10.7 %copy-start.31 = (f32[2,96,5376]{2,1,0:T(8,128)S(1)}, f32[2,96,5376]{2,1,0:T(8,128)}, u32[]{:S(2)}) copy-start(f32[2,96,5376]{2,1,0:T(8,128)} %param.38) | copy-start | bytes 12386308
  822.3 7.2 copy-start.26
  822.3 7.2 copy-start.32
  822.3 7.2 copy-start.33
  822.3 7.2 copy-start.34
  822.3 7.2 copy-start.48
  (73 other events, 265.4 us)
Sparse Core Ops, SparseCore 0:
  10.6 98.7 all-gather.9
  111.6 80.1 all-gather.11
  194.0 60.0 all-gather.13
  256.2 23.7 all-gather.7
  434.0 33.0 reduce-scatter.10
  469.8 41.7 reduce-scatter.4
  514.0 53.4 reduce-scatter.6
  569.9 75.8 reduce-scatter.8

commit v4 on v3

--- a/solution.py
+++ b/solution.py
@@ -33,6 +33,12 @@
 VMEM_LIMIT = 56 * 1024 * 1024
 MESH = pl.DeviceIdType.MESH
 LANES = 128
+LOW = jnp.bfloat16
+ANYWHERE = pl.BlockSpec(memory_space=pl.ANY)
+NO_COST = pl.CostEstimate(flops=0, bytes_accessed=0, transcendentals=0)
+ROOT = 0.7978845608028654
+CUBE = 0.044715
+NT = (((1,), (1,)), ((), ()))
 
 
 def layer_norm(values, gain, shift):
@@ -43,10 +49,6 @@
 
 def rounded(values):
     return lax.optimization_barrier(values.astype(jnp.bfloat16)).astype(jnp.float32)
-
-
-def column_total(rows):
-    return jnp.sum(rows.astype(jnp.float32), 0)
 
 
 def matmul(left, right):
@@ -217,6 +219,18 @@
         self.own_copy().wait()
 
 
+def beside(jobs, plan):
+    for step, stages in plan.items():
+
+        @pl.when(pl.program_id(0) == step)
+        def _(stages=stages):
+            for stage in stages:
+                if stage == "greet":
+                    greet()
+                else:
+                    run_stages(jobs, (stage,))
+
+
 def gather_kernel(*refs, split):
     count = len(split)
     sems = refs[2 * count]
@@ -232,11 +246,10 @@
 def gather_call(shards, split, collective_id):
     count = len(shards)
     owners = lax.axis_size("fsdp")
-    anywhere = pl.BlockSpec(memory_space=pl.ANY)
     full = pl.pallas_call(
         functools.partial(gather_kernel, split=split),
-        in_specs=[anywhere] * count,
-        out_specs=[anywhere] * count,
+        in_specs=[ANYWHERE] * count,
+        out_specs=[ANYWHERE] * count,
         out_shape=[jax.ShapeDtypeStruct((owners, *s.shape), s.dtype) for s in shards],
         scratch_shapes=[pltpu.SemaphoreType.DMA((count, GATHER_SEMS))],
         cost_estimate=transfer_cost(sum(shard.size for shard in shards) * owners),
@@ -550,14 +563,14 @@
         scratch.extend(whole_scratch(grad))
     return pl.pallas_call(
         reduce_kernel,
-        in_specs=[pl.BlockSpec(memory_space=pl.ANY)] * len(grads),
+        in_specs=[ANYWHERE] * len(grads),
         out_specs=[in_vmem] * len(grads),
         out_shape=[jax.ShapeDtypeStruct(g.shape[1:], g.dtype) for g in grads],
         scratch_shapes=scratch,
         compiler_params=pltpu.CompilerParams(
             collective_id=collective_id, has_side_effects=True, vmem_limit_bytes=VMEM_LIMIT
         ),
-        cost_estimate=pl.CostEstimate(flops=0, bytes_accessed=0, transcendentals=0),
+        cost_estimate=NO_COST,
         name="reduce_gradients",
     )(*grads)
 
@@ -589,7 +602,6 @@
 
 def finish_call(finished, shares, small, collective_id):
     done, partly = len(finished), len(shares)
-    anywhere = pl.BlockSpec(memory_space=pl.ANY)
     in_vmem = pl.BlockSpec(memory_space=pltpu.VMEM)
     scratch = [
         pltpu.SemaphoreType.DMA((REDUCE_SEMS,)),
@@ -605,7 +617,7 @@
     out_shape.append(jax.ShapeDtypeStruct(small.shape, small.dtype))
     return pl.pallas_call(
         functools.partial(finish_kernel, done=done, partly=partly),
-        in_specs=[in_vmem] * done + [anywhere] * (partly + 1),
+        in_specs=[in_vmem] * done + [ANYWHERE] * (partly + 1),
         out_specs=[in_vmem] * len(out_shape),
         out_shape=out_shape,
         scratch_shapes=scratch,
@@ -651,7 +663,14 @@
     return grad.astype(low).reshape(owners, grad.shape[0] // owners, grad.shape[1])
 
 
-def attention_forward_kernel(q_ref, k_ref, v_ref, seg_col_ref, seg_row_ref, out_ref, expo_ref, inv_ref, *, block):
+def attention_forward_kernel(*refs, block, fetched):
+    q_ref, k_ref, v_ref, seg_col_ref, seg_row_ref = refs[:5]
+    shards, refs = refs[5 : 5 + fetched], refs[5 + fetched :]
+    out_ref, expo_ref, inv_ref = refs[:3]
+    fulls, refs = refs[3 : 3 + fetched], refs[3 + fetched :]
+    jobs = [Gather(shards[i], fulls[i], refs[0].at[i], True) for i in range(fetched)]
+    if jobs:
+        beside(jobs, {0: ("greet", "first"), 1: ("second",), 3: ("third",)})
     rows = q_ref.shape[0]
     lower = lax.broadcasted_iota(jnp.int32, (block, PAIR), 1) < HD
     keys = k_ref[...]
@@ -683,15 +702,25 @@
         return carry
 
     lax.fori_loop(0, rows // block, one_block, 0, unroll=True)
-
-
-def attention_forward(qkv_rows, segment):
+    if jobs:
+        beside(jobs, {pl.num_programs(0) - 1: ("fourth",)})
+
+
+def attention_forward(qkv_rows, segment, shards, collective_id):
+    gathered = []
+    if not with_kernels():
+        gathered, shards = gather_all(shards, (True,) * len(shards), collective_id), []
     rows = qkv_rows.shape[0]
+    fetched = len(shards)
+    owners = lax.axis_size("fsdp")
+    transfer = {}
+    if fetched:
+        transfer = {"collective_id": collective_id, "has_side_effects": True}
     pairs = HEADS // 2
     block = min(256, rows)
     wide = lambda base: pl.BlockSpec((rows, PAIR), lambda j, base=base: (0, base + j))
-    return pl.pallas_call(
-        functools.partial(attention_forward_kernel, block=block),
+    attended, expo, inverse, *full = pl.pallas_call(
+        functools.partial(attention_forward_kernel, block=block, fetched=fetched),
         grid=(pairs,),
         in_specs=[
             wide(0),
@@ -699,28 +728,43 @@
             wide(2 * pairs),
             pl.BlockSpec((rows, 1), lambda j: (0, 0)),
             pl.BlockSpec((1, rows), lambda j: (0, 0)),
+            *[ANYWHERE] * fetched,
         ],
         out_specs=[
             wide(0),
             pl.BlockSpec((2, rows, rows), lambda j: (j, 0, 0)),
             wide(0),
+            *[ANYWHERE] * fetched,
         ],
         out_shape=[
             jax.ShapeDtypeStruct((rows, D), jnp.bfloat16),
             jax.ShapeDtypeStruct((HEADS, rows, rows), jnp.bfloat16),
             jax.ShapeDtypeStruct((rows, D), jnp.float32),
+            *[jax.ShapeDtypeStruct((owners, *s.shape), s.dtype) for s in shards],
         ],
-        compiler_params=pltpu.CompilerParams(vmem_limit_bytes=VMEM_LIMIT),
+        scratch_shapes=[pltpu.SemaphoreType.DMA((fetched, GATHER_SEMS))] * (fetched > 0),
+        compiler_params=pltpu.CompilerParams(vmem_limit_bytes=VMEM_LIMIT, **transfer),
         cost_estimate=pl.CostEstimate(
             flops=4 * HEADS * rows * rows * HD * 4,
             bytes_accessed=2 * HEADS * rows * rows + 12 * rows * D,
             transcendentals=HEADS * rows * rows,
         ),
         name="attention_forward",
-    )(qkv_rows, qkv_rows, qkv_rows, segment[:, None], segment[None, :])
-
-
-def attention_backward_kernel(q_ref, k_ref, v_ref, expo_ref, inv_ref, out_ref, grad_ref, dqkv_ref, *, block):
+    )(qkv_rows, qkv_rows, qkv_rows, segment[:, None], segment[None, :], *shards)
+    gathered += [f.reshape(owners * f.shape[1], f.shape[2]) for f in full]
+    return attended, expo, inverse, gathered
+
+
+def attention_backward_kernel(*refs, block, reduced):
+    q_ref, k_ref, v_ref, expo_ref, inv_ref, out_ref, grad_ref = refs[:7]
+    sources, refs = refs[7 : 7 + reduced], refs[7 + reduced :]
+    dqkv_ref, sums, refs = refs[0], refs[1 : 1 + reduced], refs[1 + reduced :]
+    jobs = [
+        Reduce(sources[i], refs[6 * i + 1], refs[6 * i + 2 : 6 * i + 7], refs[0].at[i])
+        for i in range(reduced)
+    ]
+    if jobs:
+        beside(jobs, {0: ("greet", "first"), 1: ("second",)})
     rows = q_ref.shape[0]
     pair = pl.program_id(0)
     lower = lax.broadcasted_iota(jnp.int32, (block, PAIR), 1) < HD
@@ -758,15 +802,33 @@
     value_grad = jnp.concatenate(value_t, 0).T
     dqkv_ref[:, pl.ds(pl.multiple_of(D + pair * PAIR, PAIR), PAIR)] = key_grad.astype(jnp.bfloat16)
     dqkv_ref[:, pl.ds(pl.multiple_of(2 * D + pair * PAIR, PAIR), PAIR)] = value_grad.astype(jnp.bfloat16)
-
-
-def attention_backward(qkv_rows, expo, inverse, attended, attended_grad):
+    if jobs:
+        beside(jobs, {pl.num_programs(0) - 1: STAGES[2:]})
+
+        @pl.when(pair == pl.num_programs(0) - 1)
+        def _():
+            for job, total in zip(jobs, sums):
+                total[...] = job.out[...]
+
+
+def attention_backward(qkv_rows, expo, inverse, attended, attended_grad, grads, collective_id):
+    plain = []
+    if not with_kernels():
+        plain, grads = reduce_all(grads, collective_id), []
+    reduced = len(grads)
+    transfer, scratch = {}, []
+    if reduced:
+        transfer = {"collective_id": collective_id, "has_side_effects": True}
+        scratch.append(pltpu.SemaphoreType.DMA((reduced, REDUCE_SEMS)))
+    for grad in grads:
+        scratch.append(pltpu.VMEM(grad.shape[1:], grad.dtype))
+        scratch.extend(whole_scratch(grad))
     rows = qkv_rows.shape[0]
     pairs = HEADS // 2
     block = min(256, rows)
     wide = lambda base: pl.BlockSpec((rows, PAIR), lambda j, base=base: (0, base + j))
-    return pl.pallas_call(
-        functools.partial(attention_backward_kernel, block=block),
+    qkv_grad, *sums = pl.pallas_call(
+        functools.partial(attention_backward_kernel, block=block, reduced=reduced),
         grid=(pairs,),
         in_specs=[
             wide(0),
@@ -776,82 +838,427 @@
             wide(0),
             wide(0),
             wide(0),
+            *[ANYWHERE] * reduced,
         ],
-        out_specs=pl.BlockSpec((rows, 3 * D), lambda j: (0, 0)),
-        out_shape=jax.ShapeDtypeStruct((rows, 3 * D), jnp.bfloat16),
+        out_specs=[fixed(rows, 3 * D), *[fixed(*g.shape[1:]) for g in grads]],
+        out_shape=[
+            jax.ShapeDtypeStruct((rows, 3 * D), jnp.bfloat16),
+            *[jax.ShapeDtypeStruct(g.shape[1:], g.dtype) for g in grads],
+        ],
+        scratch_shapes=scratch,
+        compiler_params=pltpu.CompilerParams(vmem_limit_bytes=VMEM_LIMIT, **transfer),
+        cost_estimate=NO_COST,
+        name="attention_backward",
+    )(qkv_rows, qkv_rows, qkv_rows, expo, inverse, attended, attended_grad, *grads)
+    return qkv_grad, plain + sums
+
+
+def mul(left, right):
+    return jnp.dot(left, right, preferred_element_type=jnp.float32)
+
+
+def mul_nt(left, right):
+    return lax.dot_general(left, right, NT, preferred_element_type=jnp.float32)
+
+
+def normalized(values):
+    center = values - jnp.mean(values, -1, keepdims=True)
+    inverse = lax.rsqrt(jnp.mean(center * center, -1, keepdims=True) + NORM_EPS)
+    return center * inverse, inverse
+
+
+def norm_backward(grad, values, gain):
+    unit, inverse = normalized(values)
+    inner = grad * gain
+    mean_inner = jnp.mean(inner, -1, keepdims=True)
+    mean_cross = jnp.mean(inner * unit, -1, keepdims=True)
+    value_grad = inverse * (inner - mean_inner - unit * mean_cross)
+    return value_grad, column_sum(grad * unit), column_sum(grad)
+
+
+def column_sum(rows):
+    return jnp.sum(rows.astype(jnp.float32), 0, keepdims=True)
+
+
+def at_first(action):
+    pl.when(pl.program_id(0) == 0)(action)
+
+
+def accumulate(out_ref, parts):
+    value = jnp.concatenate(parts, 1)
+
+    @pl.when(pl.program_id(0) == 0)
+    def _():
+        out_ref[...] = value
+
+    @pl.when(pl.program_id(0) > 0)
+    def _():
+        out_ref[...] += value
+
+
+def rows_of(block, columns):
+    return pl.BlockSpec((block, columns), lambda i: (i, 0))
+
+
+def fixed(*shape):
+    return pl.BlockSpec(shape, lambda i: (0,) * len(shape))
+
+
+def loads(sources, targets, sems):
+    return [
+        pltpu.make_async_copy(source, target, sems.at[index])
+        for index, (source, target) in enumerate(zip(sources, targets))
+    ]
+
+
+def shape_of(*shape, dtype=jnp.float32):
+    return jax.ShapeDtypeStruct(shape, dtype)
+
+
+def block_call(body, grid, in_specs, out_specs, out_shape, scratch, flops, size, name, early=False):
+    return pl.pallas_call(
+        body,
+        grid=(grid,),
+        in_specs=in_specs,
+        out_specs=out_specs,
+        out_shape=out_shape,
+        scratch_shapes=scratch,
         compiler_params=pltpu.CompilerParams(vmem_limit_bytes=VMEM_LIMIT),
-        cost_estimate=pl.CostEstimate(
-            flops=8 * HEADS * rows * rows * HD * 4,
-            bytes_accessed=2 * HEADS * rows * rows + 20 * rows * D,
-            transcendentals=0,
-        ),
-        name="attention_backward",
-    )(qkv_rows, qkv_rows, qkv_rows, expo, inverse, attended, attended_grad)
-
-
-def layer_forward(stream, weights, seg_row):
-    proj_in, proj_out, vector_low = weights
-    vector = vector_low.astype(jnp.float32)
-    normed = layer_norm(stream, vector[0:D], vector[D : 2 * D]).astype(jnp.bfloat16)
-    qkv_rows = (matmul(normed, proj_in[:, : 3 * D]) + vector[4 * D : 7 * D]).astype(jnp.bfloat16)
-    attended, expo, inverse = attention_forward(qkv_rows, seg_row)
-    residual = stream + matmul(attended, proj_out[:D]) + vector[7 * D : 8 * D]
-    normed_second = layer_norm(residual, vector[2 * D : 3 * D], vector[3 * D : 4 * D]).astype(
-        jnp.bfloat16
-    )
-    hidden = matmul(normed_second, proj_in[:, 3 * D :]) + vector[9 * D :]
-    active = jax.nn.gelu(hidden).astype(jnp.bfloat16)
-    output = residual + matmul(active, proj_out[D:]) + vector[8 * D : 9 * D]
-    return (output, (stream, qkv_rows, attended, expo, inverse, residual, hidden))
-
-
-def layer_backward(grad_stream, weights, layer_saved):
-    proj_in, proj_out, vector_low = weights
-    vector = vector_low.astype(jnp.float32)
-    stream, qkv_rows, attended, expo, inverse, residual, hidden = layer_saved
-    grad_low = grad_stream.astype(jnp.bfloat16)
-    normed_second, second_back = jax.vjp(
-        layer_norm, residual, vector[2 * D : 3 * D], vector[3 * D : 4 * D]
-    )
-    normed_second = normed_second.astype(jnp.bfloat16)
-    active, gelu_back = jax.vjp(jax.nn.gelu, hidden)
-    active = active.astype(jnp.bfloat16)
-    down_grad = matmul(active.T, grad_low)
-    active_grad = matmul(grad_low, proj_out[D:].T)
-    hidden_grad = gelu_back(active_grad)[0].astype(jnp.bfloat16)
-    up_grad = matmul(normed_second.T, hidden_grad)
-    second_grad = matmul(hidden_grad, proj_in[:, 3 * D :].T)
-    residual_grad, gain_second, shift_second = second_back(second_grad)
-    residual_grad = residual_grad + grad_stream
-    residual_low = residual_grad.astype(jnp.bfloat16)
-    mixing_grad = matmul(attended.T, residual_low)
-    attended_grad = matmul(residual_low, proj_out[:D].T).astype(jnp.bfloat16)
-    qkv_grad = attention_backward(qkv_rows, expo, inverse, attended, attended_grad)
-    normed, first_back = jax.vjp(layer_norm, stream, vector[0:D], vector[D : 2 * D])
-    project_grad = matmul(normed.astype(jnp.bfloat16).T, qkv_grad)
-    normed_grad = matmul(qkv_grad, proj_in[:, : 3 * D].T)
-    stream_grad, gain_first, shift_first = first_back(normed_grad)
-    vector_grad = jnp.concatenate(
+        cost_estimate=NO_COST if early else pl.CostEstimate(flops=flops, bytes_accessed=size, transcendentals=0),
+        name=name,
+    )
+
+
+def embed_kernel(pixel_ref, weight_ref, pos_ref, table_ref, bias_ref, out_ref):
+    position = jnp.dot(
+        pos_ref[...], table_ref[...], precision=HIGHEST, preferred_element_type=jnp.float32
+    )
+    out_ref[...] = mul(pixel_ref[...], weight_ref[...]) + bias_ref[...] + position
+
+
+def embed(pixels, weight, pos_weights, table, bias):
+    rows, depth = pixels.shape
+    block = 256
+    nodes = pos_weights.shape[1]
+    return block_call(
+        embed_kernel,
+        rows // block,
+        [rows_of(block, depth), fixed(depth, D), rows_of(block, nodes), fixed(nodes, D), fixed(1, D)],
+        rows_of(block, D),
+        shape_of(rows, D),
+        [],
+        2 * rows * depth * D,
+        2 * rows * depth + 2 * depth * D + 4 * rows * D,
+        "embed",
+    )(pixels, weight, pos_weights, table, bias)
+
+
+def qkv_kernel(stream_ref, weight_ref, vector_ref, normed_ref, qkv_ref):
+    unit, _ = normalized(stream_ref[...])
+    normed = (unit * vector_ref[:, :D] + vector_ref[:, D : 2 * D]).astype(jnp.bfloat16)
+    normed_ref[...] = normed
+    bias = vector_ref[:, 4 * D : 7 * D]
+    qkv_ref[...] = (mul(normed, weight_ref[...]) + bias).astype(jnp.bfloat16)
+
+
+def qkv_forward(stream, weight, vector):
+    rows = stream.shape[0]
+    block = 256
+    low = jnp.bfloat16
+    return block_call(
+        qkv_kernel,
+        rows // block,
+        [rows_of(block, D), fixed(D, 3 * D), fixed(1, vector.shape[1])],
+        [rows_of(block, D), rows_of(block, 3 * D)],
+        [shape_of(rows, D, dtype=low), shape_of(rows, 3 * D, dtype=low)],
+        [],
+        6 * rows * D * D,
+        14 * rows * D + 6 * D * D,
+        "qkv_forward",
+    )(stream, weight, vector)
+
+
+def mlp_kernel(
+    stream_ref, attended_ref, up_full, proj_out, vector_ref,
+    residual_ref, normed_ref, active_ref, slope_ref, out_ref,
+    mix_ref, up_ref, down_ref, sems,
+):
+    width = up_ref.shape[1]
+    copies = loads(
+        (proj_out.at[pl.ds(0, D)], up_full, proj_out.at[pl.ds(D, width)]),
+        (mix_ref, up_ref, down_ref),
+        sems,
+    )
+
+    @at_first
+    def _():
+        for copy in copies:
+            copy.start()
+        copies[0].wait()
+
+    residual = stream_ref[...] + mul(attended_ref[...], mix_ref[...]) + vector_ref[:, 7 * D : 8 * D]
+    residual_ref[...] = residual
+    unit, _ = normalized(residual)
+    normed = (unit * vector_ref[:, 2 * D : 3 * D] + vector_ref[:, 3 * D : 4 * D]).astype(jnp.bfloat16)
+    normed_ref[...] = normed
+    at_first(copies[1].wait)
+    part = 768
+    for base in range(0, width, part):
+        columns = slice(base, base + part)
+        bias = vector_ref[:, 9 * D + base : 9 * D + base + part]
+        hidden = mul(normed, up_ref[:, columns]) + bias
+        square = hidden * hidden
+        bend = jnp.tanh(hidden * (ROOT + (ROOT * CUBE) * square))
+        half = 0.5 * (1.0 + bend)
+        active_ref[:, columns] = (hidden * half).astype(jnp.bfloat16)
+        rise = (0.5 * ROOT) + (1.5 * ROOT * CUBE) * square
+        slope_ref[:, columns] = (half + hidden * (1.0 - bend * bend) * rise).astype(jnp.bfloat16)
+    at_first(copies[2].wait)
+    out_ref[...] = residual + mul(active_ref[...], down_ref[...]) + vector_ref[:, 8 * D : 9 * D]
+
+
+def mlp_forward(stream, attended, up, proj_out, vector):
+    rows = stream.shape[0]
+    width = up.shape[1]
+    block = 256
+    low = jnp.bfloat16
+    return block_call(
+        mlp_kernel,
+        rows // block,
+        [rows_of(block, D), rows_of(block, D), ANYWHERE, ANYWHERE, fixed(1, vector.shape[1])],
+        [rows_of(block, D), rows_of(block, D), rows_of(block, width), rows_of(block, width), rows_of(block, D)],
         [
-            gain_first,
-            shift_first,
-            gain_second,
-            shift_second,
-            column_total(qkv_grad),
-            column_total(residual_low),
-            column_total(grad_low),
-            column_total(hidden_grad),
-        ]
-    )
-    return (
-        residual_grad + stream_grad,
-        (
-            project_grad,
-            up_grad,
-            jnp.concatenate([mixing_grad, down_grad], 0),
-            vector_grad,
-        ),
-    )
+            shape_of(rows, D),
+            shape_of(rows, D, dtype=low),
+            shape_of(rows, width, dtype=low),
+            shape_of(rows, width, dtype=low),
+            shape_of(rows, D),
+        ],
+        [
+            pltpu.VMEM((D, D), low),
+            pltpu.VMEM((D, width), low),
+            pltpu.VMEM((width, D), low),
+            pltpu.SemaphoreType.DMA((3,)),
+        ],
+        2 * rows * D * (D + 2 * width),
+        rows * (16 * D + 4 * width) + 2 * D * (D + 2 * width),
+        "mlp_forward",
+    )(stream, attended, up, proj_out, vector)
+
+
+def mlp_back_kernel(
+    grad_ref, slope_ref, residual_ref, up_full, proj_out, vector_ref,
+    low_ref, hidden_ref, out_ref, out_low_ref, attended_ref, sums_ref,
+    mix_ref, up_ref, down_ref, sems,
+):
+    width = up_ref.shape[1]
+    copies = loads(
+        (proj_out.at[pl.ds(D, width)], up_full, proj_out.at[pl.ds(0, D)]),
+        (down_ref, up_ref, mix_ref),
+        sems,
+    )
+
+    @at_first
+    def _():
+        for copy in copies:
+            copy.start()
+        copies[0].wait()
+
+    grad = grad_ref[...]
+    grad_low = grad.astype(jnp.bfloat16)
+    low_ref[...] = grad_low
+    part = 768
+    hidden_sums = []
+    for base in range(0, width, part):
+        columns = slice(base, base + part)
+        active_grad = mul_nt(grad_low, down_ref[columns, :])
+        hidden_grad = (active_grad * slope_ref[:, columns].astype(jnp.float32)).astype(jnp.bfloat16)
+        hidden_ref[:, columns] = hidden_grad
+        hidden_sums.append(column_sum(hidden_grad))
+    at_first(copies[1].wait)
+    second_grad = mul_nt(hidden_ref[...], up_ref[...])
+    value_grad, gain_grad, shift_grad = norm_backward(
+        second_grad, residual_ref[...], vector_ref[:, 2 * D : 3 * D]
+    )
+    total = value_grad + grad
+    out_ref[...] = total
+    total_low = total.astype(jnp.bfloat16)
+    out_low_ref[...] = total_low
+    at_first(copies[2].wait)
+    attended_ref[...] = mul_nt(total_low, mix_ref[...]).astype(jnp.bfloat16)
+    accumulate(
+        sums_ref,
+        [gain_grad, shift_grad, column_sum(total_low), column_sum(grad_low), *hidden_sums],
+    )
+
+
+def mlp_backward(grad, slope, residual, up, proj_out, vector):
+    rows = grad.shape[0]
+    width = up.shape[1]
+    block = 256
+    low = jnp.bfloat16
+    narrow = rows_of(block, D)
+    return block_call(
+        mlp_back_kernel,
+        rows // block,
+        [narrow, rows_of(block, width), narrow, ANYWHERE, ANYWHERE, fixed(1, vector.shape[1])],
+        [narrow, rows_of(block, width), narrow, narrow, narrow, fixed(1, 4 * D + width)],
+        [
+            shape_of(rows, D, dtype=low),
+            shape_of(rows, width, dtype=low),
+            shape_of(rows, D),
+            shape_of(rows, D, dtype=low),
+            shape_of(rows, D, dtype=low),
+            shape_of(1, 4 * D + width),
+        ],
+        [
+            pltpu.VMEM((D, D), low),
+            pltpu.VMEM((D, width), low),
+            pltpu.VMEM((width, D), low),
+            pltpu.SemaphoreType.DMA((3,)),
+        ],
+        2 * rows * D * (D + 2 * width),
+        rows * (18 * D + 4 * width) + 2 * D * (D + 2 * width),
+        "mlp_backward",
+        early=True,
+    )(grad, slope, residual, up, proj_out, vector)
+
+
+def qkv_back_kernel(grad_ref, residual_ref, stream_ref, weight_ref, vector_ref, out_ref, sums_ref):
+    grad = grad_ref[...]
+    normed_grad = mul_nt(grad, weight_ref[...])
+    value_grad, gain_grad, shift_grad = norm_backward(normed_grad, stream_ref[...], vector_ref[:, :D])
+    out_ref[...] = residual_ref[...] + value_grad
+    accumulate(sums_ref, [gain_grad, shift_grad, column_sum(grad)])
+
+
+def qkv_backward(grad, residual_grad, stream, weight, vector):
+    rows = stream.shape[0]
+    block = 256
+    narrow = rows_of(block, D)
+    return block_call(
+        qkv_back_kernel,
+        rows // block,
+        [rows_of(block, 3 * D), narrow, narrow, fixed(D, 3 * D), fixed(1, vector.shape[1])],
+        [narrow, fixed(1, 5 * D)],
+        [shape_of(rows, D), shape_of(1, 5 * D)],
+        [],
+        6 * rows * D * D,
+        18 * rows * D + 6 * D * D,
+        "qkv_backward",
+        early=True,
+    )(grad, residual_grad, stream, weight, vector)
+
+
+def input_grad_kernel(first_ref, second_ref, qkv_ref, hidden_ref, out_ref, left_ref, *, cut):
+    step = pl.program_id(0)
+
+    @pl.when(step == 0)
+    def _():
+        left_ref[...] = first_ref[...].T
+
+    @pl.when(step == cut)
+    def _():
+        left_ref[...] = second_ref[...].T
+
+    @pl.when(step < cut)
+    def _():
+        out_ref[...] = mul(left_ref[...], qkv_ref[...]).astype(jnp.bfloat16)
+
+    @pl.when(step >= cut)
+    def _():
+        out_ref[...] = mul(left_ref[...], hidden_ref[...]).astype(jnp.bfloat16)
+
+
+def input_weight_grad(first, second, qkv_grad, hidden_grad):
+    rows = first.shape[0]
+    cut = qkv_grad.shape[1] // D
+    steps = cut + hidden_grad.shape[1] // D
+    return block_call(
+        functools.partial(input_grad_kernel, cut=cut),
+        steps,
+        [
+            fixed(rows, D),
+            fixed(rows, D),
+            pl.BlockSpec((rows, D), lambda i: (0, jnp.minimum(i, cut - 1))),
+            pl.BlockSpec((rows, D), lambda i: (0, jnp.maximum(i - cut, 0))),
+        ],
+        pl.BlockSpec((D, D), lambda i: (0, i)),
+        shape_of(D, steps * D, dtype=jnp.bfloat16),
+        [pltpu.VMEM((D, rows), jnp.bfloat16)],
+        2 * rows * D * D * steps,
+        2 * rows * D * (steps + 2) + 2 * D * D * steps,
+        "input_weight_grad",
+        early=True,
+    )(first, second, qkv_grad, hidden_grad)
+
+
+def output_grad_kernel(attended_ref, active_ref, residual_ref, grad_ref, out_ref, *, cut):
+    step = pl.program_id(0)
+
+    @pl.when(step < cut)
+    def _():
+        out_ref[...] = mul(attended_ref[...].T, residual_ref[...]).astype(jnp.bfloat16)
+
+    @pl.when(step >= cut)
+    def _():
+        out_ref[...] = mul(active_ref[...].T, grad_ref[...]).astype(jnp.bfloat16)
+
+
+def output_weight_grad(attended, active, residual_low, grad_low):
+    rows = attended.shape[0]
+    block = 768
+    cut = attended.shape[1] // block
+    steps = cut + active.shape[1] // block
+    return block_call(
+        functools.partial(output_grad_kernel, cut=cut),
+        steps,
+        [
+            pl.BlockSpec((rows, block), lambda i: (0, jnp.minimum(i, cut - 1))),
+            pl.BlockSpec((rows, block), lambda i: (0, jnp.maximum(i - cut, 0))),
+            fixed(rows, D),
+            fixed(rows, D),
+        ],
+        rows_of(block, D),
+        shape_of(steps * block, D, dtype=jnp.bfloat16),
+        [],
+        2 * rows * D * block * steps,
+        2 * rows * (block * steps + 2 * D) + 2 * D * block * steps,
+        "output_weight_grad",
+        early=True,
+    )(attended, active, residual_low, grad_low)
+
+
+def embed_back_kernel(pixel_ref, grad_ref, pos_ref, out_ref, table_ref, bias_ref, low_ref):
+    @at_first
+    def _():
+        grad = grad_ref[...]
+        low = grad.astype(jnp.bfloat16)
+        low_ref[...] = low
+        bias_ref[...] = column_sum(low)
+        table_ref[...] = jnp.dot(
+            pos_ref[...], grad, precision=HIGHEST, preferred_element_type=jnp.float32
+        )
+
+    out_ref[...] = mul(pixel_ref[...].T, low_ref[...]).astype(jnp.bfloat16)
+
+
+def embed_backward(pixels, grad, pos_weights_t):
+    rows, depth = pixels.shape
+    block = 768
+    nodes = pos_weights_t.shape[0]
+    return block_call(
+        embed_back_kernel,
+        depth // block,
+        [pl.BlockSpec((rows, block), lambda i: (0, i)), fixed(rows, D), fixed(nodes, rows)],
+        [rows_of(block, D), fixed(nodes, D), fixed(1, D)],
+        [shape_of(depth, D, dtype=jnp.bfloat16), shape_of(nodes, D), shape_of(1, D)],
+        [pltpu.VMEM((rows, D), jnp.bfloat16)],
+        2 * rows * depth * D,
+        2 * rows * depth + 2 * depth * D + 4 * rows * D,
+        "embed_backward",
+        early=True,
+    )(pixels, grad, pos_weights_t)
 
 
 def adam_update(gradient, moment, square, weight, factor, learn_rate):
@@ -895,32 +1302,52 @@
 ):
     pos_weights, member, counts = row_layout(segment, patch_size[0])
     owners = lax.axis_size("fsdp")
-    low = jnp.bfloat16
+    nodes = pos_weights.shape[1]
+    pos_weights = jnp.pad(pos_weights, ((0, 0), (0, -nodes % 64)))
     vector_size = layer_vector.size
-    kernel_full, vectors, input_zero = gather_all(
+    inputs = [
+        (input_proj[index, :, : 3 * D].astype(LOW), input_proj[index, :, 3 * D :].astype(LOW))
+        for index in range(LAYERS)
+    ]
+    outputs = [output_proj[index].astype(LOW) for index in range(LAYERS)]
+    kernel_full, vectors, qkv_zero = gather_all(
         [
-            patch_kernel.astype(low),
-            padded_rows(layer_vector.astype(low).reshape(-1), 32),
-            input_proj[0].astype(low),
+            patch_kernel.astype(LOW),
+            padded_rows(layer_vector.astype(LOW).reshape(-1), 32),
+            inputs[0][0],
         ],
         (True, False, True),
         1,
     )
     vectors = vectors.reshape(owners, -1)[:, :vector_size].reshape(owners, *layer_vector.shape)
-    vectors = jnp.swapaxes(vectors, 0, 1).reshape(LAYERS, -1)
-    output_zero, input_one, output_one, head_full = (
-        lax.all_gather(shard.astype(low), "fsdp", axis=0, tiled=True)
-        for shard in (output_proj[0], input_proj[1], output_proj[1], head_weight)
-    )
-    layer_weights = [(input_zero, output_zero, vectors[0]), (input_one, output_one, vectors[1])]
+    vectors = jnp.swapaxes(vectors, 0, 1).reshape(LAYERS, 1, -1).astype(jnp.float32)
+    output_zero, qkv_one, up_one, head_full = (
+        lax.all_gather(shard, "fsdp", axis=0, tiled=True)
+        for shard in (outputs[0], *inputs[1], head_weight.astype(LOW))
+    )
     global_low = rounded(global_vector)
-    position_low = rounded(position_table)
-    embed_pre = matmul(pixels, kernel_full) + global_low[:D]
-    stream = embed_pre + jnp.dot(pos_weights, position_low, precision=HIGHEST)
+    position_low = jnp.pad(rounded(position_table), ((0, -nodes % 64), (0, 0)))
+    stream = embed(pixels, kernel_full, pos_weights, position_low, global_low[None, :D])
     saved_layers = []
-    for weights in layer_weights:
-        stream, layer_saved = layer_forward(stream, weights, segment)
-        saved_layers.append(layer_saved)
+    for index, qkv_weight in enumerate((qkv_zero, qkv_one)):
+        vector = vectors[index]
+        normed, qkv_rows = qkv_forward(stream, qkv_weight, vector)
+        fetch = inputs[0][1] if index == 0 else outputs[1]
+        attended, expo, inverse, (fetched,) = attention_forward(
+            qkv_rows, segment, [fetch], 4 + index
+        )
+        up, output = (fetched, output_zero) if index == 0 else (up_one, fetched)
+        residual, normed_second, active, slope, following = mlp_forward(
+            stream, attended, up, output, vector
+        )
+        saved_layers.append(
+            (
+                (qkv_weight, up, output, vector),
+                (stream, normed, qkv_rows, attended, expo, inverse),
+                (residual, normed_second, active, slope),
+            )
+        )
+        stream = following
     final_norm, final_back = jax.vjp(
         layer_norm, stream, global_low[D : 2 * D], global_low[2 * D : 3 * D]
     )
@@ -939,29 +1366,56 @@
     logits_grad = ((exponent / totals - onehot.astype(jnp.float32)) * counts[:, None]).astype(
         jnp.bfloat16
     )
-    head_grad = jnp.pad(matmul(pooled.T, logits_grad), ((0, 0), (0, -CLS % LANES)))
+    head_grad = matmul(pooled.T, logits_grad).astype(LOW)
+    head_part = scatter(by_owner(jnp.pad(head_grad, ((0, 0), (0, -CLS % LANES)))))
     pooled_grad = matmul(logits_grad, head_full.T)
     final_grad = jnp.dot(member, pooled_grad / image_sizes[:, None], precision=HIGHEST)
     stream_grad, final_gain, final_shift = final_back(final_grad)
-    stream_grad, grads_one = layer_backward(stream_grad, layer_weights[1], saved_layers[1])
-    stream_grad, *parts_one = lax.optimization_barrier(
-        (stream_grad, *(by_owner(grad) for grad in (*grads_one[:3], head_grad)))
-    )
-    parts_one = [scatter(part) for part in parts_one]
-    stream_grad, grads_zero = layer_backward(stream_grad, layer_weights[0], saved_layers[0])
-    embed_low = stream_grad.astype(jnp.bfloat16)
-    position_grad = jnp.dot(pos_weights.T, stream_grad, precision=HIGHEST)
-    vector_part = jnp.stack([grads_zero[3], grads_one[3]]).reshape(LAYERS, owners, -1)
+    vector_grads = [None] * LAYERS
+    parts = [head_part]
+    for index in reversed(range(LAYERS)):
+        (qkv_weight, up, output, vector), first, second = saved_layers[index]
+        entering, normed, qkv_rows, attended, expo, inverse = first
+        residual, normed_second, active, slope = second
+        grad_low, hidden_grad, residual_grad, residual_low, attended_grad, mlp_sums = mlp_backward(
+            stream_grad, slope, residual, up, output, vector
+        )
+        output_grad = output_weight_grad(attended, active, residual_low, grad_low)
+        attended_grad, output_grad = lax.optimization_barrier((attended_grad, output_grad))
+        beside_attention = []
+        if index:
+            parts.append(scatter(by_owner(output_grad)))
+        else:
+            beside_attention.append(by_owner(output_grad))
+        qkv_grad, output_sums = attention_backward(
+            qkv_rows, expo, inverse, attended, attended_grad, beside_attention, 6
+        )
+        stream_grad, qkv_sums = qkv_backward(qkv_grad, residual_grad, entering, qkv_weight, vector)
+        input_grad = input_weight_grad(normed, normed_second, qkv_grad, hidden_grad)
+        if index:
+            stream_grad, input_grad = lax.optimization_barrier((stream_grad, input_grad))
+            parts.append(scatter(by_owner(input_grad)))
+        vector_grads[index] = jnp.concatenate(
+            [
+                qkv_sums[0, : 2 * D],
+                mlp_sums[0, : 2 * D],
+                qkv_sums[0, 2 * D :],
+                mlp_sums[0, 2 * D :],
+            ]
+        )
+    kernel_grad, position_grad, bias_grad = embed_backward(pixels, stream_grad, pos_weights.T)
+    position_grad = position_grad[:nodes]
+    vector_part = jnp.stack(vector_grads).reshape(LAYERS, owners, -1)
     vector_part = jnp.swapaxes(vector_part, 0, 1).reshape(owners, vector_size)
     vector_rows = -(-vector_size // LANES)
     vector_part = jnp.pad(vector_part, ((0, 0), (0, vector_rows * LANES - vector_size)))
     rest = jnp.concatenate(
         [
             position_grad.reshape(-1),
-            column_total(embed_low),
+            bias_grad[0],
             final_gain,
             final_shift,
-            column_total(logits_grad),
+            jnp.sum(logits_grad.astype(jnp.float32), 0),
             loss_local[None],
             jnp.sum(counts)[None],
         ]
@@ -972,22 +1426,20 @@
     used = vector_rows + rest_rows
     block_rows = (used // 64 + 1) * 64
     small = jnp.pad(small.reshape(owners, used, LANES), ((0, 0), (0, block_rows - used), (0, 0)))
-    summed = reduce_all(
-        [by_owner(grad) for grad in (*grads_zero[:3], matmul(pixels.T, embed_low))], 2
-    )
-    shares_zero, kernel_sum = summed[:3], summed[3]
-    *shares_one, small_share, small_full = finish_all(summed, parts_one, small, 3)
+    summed = reduce_all([by_owner(input_grad), by_owner(kernel_grad)], 2)
+    (output_zero_sum,) = output_sums
+    head_sum, output_one_sum, input_one_sum, small_share, small_full = finish_all(
+        [*summed, output_zero_sum], parts, small, 3
+    )
     rest_sum = small_full[:, vector_rows:used].reshape(-1)
     position_sum = rest_sum[: position_grad.size].reshape(position_grad.shape)
     global_sum = rest_sum[position_grad.size :][: global_vector.shape[0]]
     loss_sum = rest_sum[rest.shape[0] - 2]
     token_total = rest_sum[rest.shape[0] - 1]
-    kernel_sum = kernel_sum.astype(jnp.float32)
-    head_sum = shares_one[3][:, :CLS].astype(jnp.float32)
-    input_sum = jnp.stack(
-        [jnp.concatenate(pair[:2], 1) for pair in (shares_zero, shares_one)]
-    ).astype(jnp.float32)
-    output_sum = jnp.stack([shares_zero[2], shares_one[2]]).astype(jnp.float32)
+    kernel_sum = summed[1].astype(jnp.float32)
+    head_sum = head_sum[:, :CLS].astype(jnp.float32)
+    input_sum = jnp.stack([summed[0], input_one_sum]).astype(jnp.float32)
+    output_sum = jnp.stack([output_zero_sum, output_one_sum]).astype(jnp.float32)
     vector_sum = small_share[:vector_rows].reshape(-1)[:vector_size].reshape(layer_vector.shape)
     grad_norm = (
         jnp.sqrt(

time: 847 us -> 780 us (0.921)
  Pallas kernels: 406 us -> 671 us
  matrix products: 238 us -> 9.52 us
  other arithmetic: 88.3 us -> 43.1 us
  waiting for transfers between devices: 31.9 us -> 0.24 us
  local copies, waits for them, and re-layouts: 55.9 us -> 24.7 us
    pallas_call x6 -> x20, Pallas kernels: 345 us -> 610 us  [the longest x2 126 us: attention_forward(): pl.pallas_call(functools.partial(attention_forward_kernel, block=block, f...]
    dot_general x29 -> x3, matrix products: 226 us -> 5.51 us  [matmul(): return jnp.dot(left, right, preferred_element_type=jnp.float32)]
    reduce_sum x14 -> x1, other arithmetic: 35.2 us -> 0.1 us  [body(): jnp.sum(logits_grad.astype(jnp.float32), 0)]
    all_gather x4, waiting for transfers between devices: 29.9 us -> 0.06 us  [body(): lax.all_gather(shard, 'fsdp', axis=0, tiled=True)]
    dot_general x5 -> x0, local copies, waits for them, and re-layouts: 18.5 us -> none  [the longest x4 14.9 us: matmul(): return jnp.dot(left, right, preferred_element_type=jnp.float32)]
    unnamed x270 -> x77, local copies, waits for them, and re-layouts: 17.1 us -> 6.98 us
  transfers between devices with their start and end apart: 8 -> 7, of which waited for: 2 -> 0; matrix products, arithmetic and copies ran while one was open for 26% -> 4% of each run, Pallas kernels for 38% -> 79%
where the time goes in v4:
time: 780 us; the launch traced here: 770 us
  Pallas kernels  671 us (86%)
  other arithmetic  43.1 us (6%)
  local copies, waits for them, and re-layouts  24.7 us (3%)
  between operations  21.2 us (3%)
  matrix products  9.52 us (1%)
    pallas_call x2, Pallas kernels, attention_forward(): pl.pallas_call(functools.partial(attention_forward_kernel, block=block, f...  126 us
    pallas_call x1, Pallas kernels, reduce_call(): pl.pallas_call(reduce_kernel, in_specs=[ANYWHERE] * len(grads), out_specs...  101 us
    pallas_call x2, Pallas kernels, attention_backward(): pl.pallas_call(functools.partial(attention_backward_kernel, block=block,...  101 us
    pallas_call x1, Pallas kernels, gather_call(): pl.pallas_call(functools.partial(gather_kernel, split=split), in_specs=[A...  63.4 us
    pallas_call x1, Pallas kernels, finish_call(): pl.pallas_call(functools.partial(finish_kernel, done=done, partly=partly)...  60.3 us
    pallas_call x2, Pallas kernels, mlp_forward(): block_call(mlp_kernel, rows // block, [rows_of(block, D), rows_of(block,...  51.3 us
    pallas_call x2, Pallas kernels, mlp_backward(): block_call(mlp_back_kernel, rows // block, [narrow, rows_of(block, width)...  49.5 us
    pallas_call x2, Pallas kernels, input_weight_grad(): block_call(functools.partial(input_grad_kernel, cut=cut), steps, [fixed(r...  31.9 us
  transfers between devices with their start and end apart: 7, of which 0 were waited for; matrix products, arithmetic and copies ran while one was open for 4% of the time, Pallas kernels for 79%

profile of v4, /device:TPU:0, one launch (start us, length us, event | category | flops | bytes accessed | tf_op | source)
XLA Modules:
  0.0 769.9 jit_solution(1110073679715687586)
XLA Ops:
  7.2 2.0 convert.15
  9.2 1.2 slice_bitcast_fusion
  10.5 2.4 convert.14
  12.9 1.0 fusion.54
  14.0 1.1 fusion.53
  15.2 1.7 convert_element_type.168
  18.1 0.9 convert_element_type.147.refs_0_
  20.3 1.0 convert_element_type.155
  21.3 0.7 pad_convert_fusion.table_ref
  22.0 63.4 %gather_weights.1 = (bf16[8,384,768]{2,1,0:T(8,128)(2,1)}, bf16[8,32,128]{2,1,0:T(8,128)(2,1)}, bf16[8,96,2304]{2,1,0:T(8,128)(2,1)}) custom-call(bf16[384,768]{1,0:T(8,128)(2,1)} %convert_element_type.147.refs_0_, bf16[32,128]{1,0:T(8,128)(2,1)} %pad_bitcast_fusion.refs_1_, bf16[96,2304]{1,0:T(8,128)(2,1)} %get-tuple-element.181.refs_2_), custom_call_target="tpu_custom_call" | custom-call | flops 16646144000 | bytes 8323072 | tf_op jit(solution)/shard_map/gather_weights/pallas_call | solution.py:249
  85.3 0.9 copy.65
  86.6 0.7 squeeze.47.vector_ref
  87.3 1.0 copy.57.refs_3_
  88.3 0.7 squeeze.48.vector_ref
  89.0 0.8 pad.31.clone.pos_ref
  89.9 11.9 %embed.1.stream_ref = f32[1024,768]{1,0:T(8,128)} custom-call(bf16[1024,3072]{1,0:T(8,128)(2,1)} %pixel_ref.3, bf16[3072,768]{1,0:T(8,128)(2,1)} %bitcast.102, f32[1024,64]{1,0:T(8,128)} %pad.31.clone.pos_ref, f32[64,768]{1,0:T(8,128)} %pad_convert_fusion.table_ref, f32[1,768]{1,0:T(1,128)} %broadcast_in_dim.85.bias_ref), custom_call_target="tpu_custom_call" | custom-call | flops 4831838208 | bytes 14155776 | tf_op jit(solution)/shard_map/embed/pallas_call | solution.py:943
  101.8 9.0 %qkv_forward.2 = (bf16[1024,768]{1,0:T(8,128)(2,1)}, bf16[1024,2304]{1,0:T(8,128)(2,1)}) custom-call(f32[1024,768]{1,0:T(8,128)} %embed.1.stream_ref, bf16[768,2304]{1,0:T(8,128)(2,1)} %bitcast.79, f32[1,9984]{1,0:T(1,128)} %squeeze.47.vector_ref), custom_call_target="tpu_custom_call" | custom-call | flops 3623878656 | bytes 14548992 | tf_op jit(solution)/shard_map/qkv_forward/pallas_call | solution.py:968
  110.7 61.2 %attention_forward.2 = (bf16[1024,768]{1,0:T(8,128)(2,1)}, bf16[12,1024,1024]{2,1,0:T(8,128)(2,1)}, f32[1024,768]{1,0:T(8,128)}, bf16[8,96,3072]{2,1,0:T(8,128)(2,1)}) custom-call(bf16[1024,2304]{1,0:T(8,128)(2,1)} %get-tuple-element.87.refs_0_.refs_1_.refs_2_, bf16[1024,2304]{1,0:T(8,128)(2,1)} %get-tuple-element.87.refs_0_.refs_1_.refs_2_, ...), custom_call_target="tpu_custom_call" | custom-call | flops 12884901888 | bytes 34603008 | tf_op jit(solution)/shard_map/attention_forward/pallas_call | solution.py:722
  171.9 25.7 %mlp_forward.2 = (f32[1024,768]{1,0:T(8,128)}, bf16[1024,768]{1,0:T(8,128)(2,1)}, bf16[1024,3072]{1,0:T(8,128)(2,1)}, bf16[1024,3072]{1,0:T(8,128)(2,1)}, f32[1024,768]{1,0:T(8,128)}) custom-call(f32[1024,768]{1,0:T(8,128)} %embed.1.stream_ref, bf16[1024,768]{1,0:T(8,128)(2,1)} %get-tuple-element.88.attended_ref.refs_5_, bf16[768,3072]{1,0:T(8,128)(2,1)} %bitcast.73, ...), custom_call_target="tpu_custom_call" | custom-call | flops 10871635968 | bytes 35782656 | tf_op jit(solution)/shard_map/mlp_forward/pallas_call | solution.py:1025
  197.6 9.0 %qkv_forward.3 = (bf16[1024,768]{1,0:T(8,128)(2,1)}, bf16[1024,2304]{1,0:T(8,128)(2,1)}) custom-call(f32[1024,768]{1,0:T(8,128)} %get-tuple-element.93.stream_ref, bf16[768,2304]{1,0:T(8,128)(2,1)} %bitcast.77, f32[1,9984]{1,0:T(1,128)} %squeeze.48.vector_ref), custom_call_target="tpu_custom_call" | custom-call | flops 3623878656 | bytes 14548992 | tf_op jit(solution)/shard_map/qkv_forward/pallas_call | solution.py:968
  206.6 64.6 %attention_forward.3 = (bf16[1024,768]{1,0:T(8,128)(2,1)}, bf16[12,1024,1024]{2,1,0:T(8,128)(2,1)}, f32[1024,768]{1,0:T(8,128)}, bf16[8,480,768]{2,1,0:T(8,128)(2,1)}) custom-call(bf16[1024,2304]{1,0:T(8,128)(2,1)} %get-tuple-element.94.refs_0_.refs_1_.refs_2_, bf16[1024,2304]{1,0:T(8,128)(2,1)} %get-tuple-element.94.refs_0_.refs_1_.refs_2_, ...), custom_call_target="tpu_custom_call" | custom-call | flops 12884901888 | bytes 34603008 | tf_op jit(solution)/shard_map/attention_forward/pallas_call | solution.py:722
  271.2 25.7 %mlp_forward.3 = (f32[1024,768]{1,0:T(8,128)}, bf16[1024,768]{1,0:T(8,128)(2,1)}, bf16[1024,3072]{1,0:T(8,128)(2,1)}, bf16[1024,3072]{1,0:T(8,128)(2,1)}, f32[1024,768]{1,0:T(8,128)}) custom-call(f32[1024,768]{1,0:T(8,128)} %get-tuple-element.93.stream_ref, bf16[1024,768]{1,0:T(8,128)(2,1)} %get-tuple-element.97.attended_ref.refs_5_, ...), custom_call_target="tpu_custom_call" | custom-call | flops 10871635968 | bytes 35782656 | tf_op jit(solution)/shard_map/mlp_forward/pallas_call | solution.py:1025
  296.9 2.3 reduce_sum.181
  300.3 1.7 fusion.15
  301.9 1.8 fusion.58
  304.1 1.8 convolution_convert_fusion
  305.9 2.6 copy.61
  308.5 2.7 pad.34.clone
  311.3 1.9 convolution_divide_fusion
  313.2 2.3 multiply_reduce_fusion
  315.5 1.9 fusion.52
  317.4 1.9 broadcast_add_fusion.grad_ref
  319.4 24.8 %mlp_backward.2 = (bf16[1024,768]{1,0:T(8,128)(2,1)}, bf16[1024,3072]{1,0:T(8,128)(2,1)}, f32[1024,768]{1,0:T(8,128)}, bf16[1024,768]{1,0:T(8,128)(2,1)}, bf16[1024,768]{1,0:T(8,128)(2,1)}, /*index=5*/f32[1,6144]{1,0:T(1,128)}) custom-call(f32[1024,768]{1,0:T(8,128)} %broadcast_add_fusion.grad_ref, bf16[1024,3072]{1,0:T(8,128)(2,1)} %get-tuple-element.100.slope_ref, ...), custom_call_target="tpu_custom_call" | custom-call | tf_op jit(solution)/shard_map/mlp_backward/pallas_call | solution.py:1101
  344.2 12.0 %output_weight_grad.2 = bf16[3840,768]{1,0:T(8,128)(2,1)} custom-call(bf16[1024,768]{1,0:T(8,128)(2,1)} %get-tuple-element.97.attended_ref.refs_5_, bf16[1024,3072]{1,0:T(8,128)(2,1)} %get-tuple-element.103.active_ref, bf16[1024,768]{1,0:T(8,128)(2,1)} %get-tuple-element.104.residual_ref, bf16[1024,768]{1,0:T(8,128)(2,1)} %get-tuple-element.105.grad_ref), custom_call_target="tpu_custom_call" | custom-call | tf_op jit(solution)/shard_map/output_weight_grad/pallas_call | solution.py:1213
  356.2 28.6 %attention_backward.2.grad_ref.qkv_ref = bf16[1024,2304]{1,0:T(8,128)(2,1)} custom-call(bf16[1024,2304]{1,0:T(8,128)(2,1)} %get-tuple-element.94.refs_0_.refs_1_.refs_2_, bf16[1024,2304]{1,0:T(8,128)(2,1)} %get-tuple-element.94.refs_0_.refs_1_.refs_2_, bf16[1024,2304]{1,0:T(8,128)(2,1)} %get-tuple-element.94.refs_0_.refs_1_.refs_2_, ...), custom_call_target="tpu_custom_call" | custom-call | tf_op jit(solution)/shard_map/attention_backward/pallas_call | solution.py:830
  384.9 10.5 %qkv_backward.2 = (f32[1024,768]{1,0:T(8,128)}, f32[1,3840]{1,0:T(1,128)}) custom-call(bf16[1024,2304]{1,0:T(8,128)(2,1)} %attention_backward.2.grad_ref.qkv_ref, f32[1024,768]{1,0:T(8,128)} %get-tuple-element.107.residual_ref, f32[1024,768]{1,0:T(8,128)} %get-tuple-element.93.stream_ref, bf16[768,2304]{1,0:T(8,128)(2,1)} %bitcast.78, ...), custom_call_target="tpu_custom_call" | custom-call | tf_op jit(solution)/shard_map/qkv_backward/pallas_call | solution.py:1139
  395.3 15.9 %input_weight_grad.2 = bf16[768,5376]{1,0:T(8,128)(2,1)} custom-call(bf16[1024,768]{1,0:T(8,128)(2,1)} %get-tuple-element.109.first_ref, bf16[1024,768]{1,0:T(8,128)(2,1)} %get-tuple-element.110.second_ref, bf16[1024,2304]{1,0:T(8,128)(2,1)} %attention_backward.2.grad_ref.qkv_ref, bf16[1024,3072]{1,0:T(8,128)(2,1)} %get-tuple-element.111.hidden_ref), custom_call_target="tpu_custom_call" | custom-call | tf_op jit(solution)/shard_map/input_weight_grad/pallas_call | solution.py:1177
  411.2 0.7 pad_bitcast_fusion.1.pos_ref
  412.0 24.7 %mlp_backward.3 = (bf16[1024,768]{1,0:T(8,128)(2,1)}, bf16[1024,3072]{1,0:T(8,128)(2,1)}, f32[1024,768]{1,0:T(8,128)}, bf16[1024,768]{1,0:T(8,128)(2,1)}, bf16[1024,768]{1,0:T(8,128)(2,1)}, /*index=5*/f32[1,6144]{1,0:T(1,128)}) custom-call(f32[1024,768]{1,0:T(8,128)} %get-tuple-element.112.grad_ref, bf16[1024,3072]{1,0:T(8,128)(2,1)} %get-tuple-element.113.slope_ref, ...), custom_call_target="tpu_custom_call" | custom-call | tf_op jit(solution)/shard_map/mlp_backward/pallas_call | solution.py:1101
  436.7 12.2 %output_weight_grad.3 = bf16[3840,768]{1,0:T(8,128)(2,1)} custom-call(bf16[1024,768]{1,0:T(8,128)(2,1)} %get-tuple-element.88.attended_ref.refs_5_, bf16[1024,3072]{1,0:T(8,128)(2,1)} %get-tuple-element.116.active_ref, bf16[1024,768]{1,0:T(8,128)(2,1)} %get-tuple-element.117.residual_ref, bf16[1024,768]{1,0:T(8,128)(2,1)} %get-tuple-element.118.grad_ref), custom_call_target="tpu_custom_call" | custom-call | tf_op jit(solution)/shard_map/output_weight_grad/pallas_call | solution.py:1213
  448.9 72.2 %attention_backward.3 = (bf16[1024,2304]{1,0:T(8,128)(2,1)}, bf16[480,768]{1,0:T(8,128)(2,1)}) custom-call(bf16[1024,2304]{1,0:T(8,128)(2,1)} %get-tuple-element.87.refs_0_.refs_1_.refs_2_, bf16[1024,2304]{1,0:T(8,128)(2,1)} %get-tuple-element.87.refs_0_.refs_1_.refs_2_, bf16[1024,2304]{1,0:T(8,128)(2,1)} %get-tuple-element.87.refs_0_.refs_1_.refs_2_, ...), custom_call_target="tpu_custom_call" | custom-call | tf_op jit(solution)/shard_map/attention_backward/pallas_call | solution.py:830
  521.0 10.4 %qkv_backward.3 = (f32[1024,768]{1,0:T(8,128)}, f32[1,3840]{1,0:T(1,128)}) custom-call(bf16[1024,2304]{1,0:T(8,128)(2,1)} %get-tuple-element.121.qkv_ref.grad_ref, f32[1024,768]{1,0:T(8,128)} %get-tuple-element.123.residual_ref, f32[1024,768]{1,0:T(8,128)} %embed.1.stream_ref, bf16[768,2304]{1,0:T(8,128)(2,1)} %bitcast.80, f32[1,9984]{1,0:T(1,128)} %squeeze.47.vector_ref), custom_call_target="tpu_custom_call" | custom-call | tf_op jit(solution)/shard_map/qkv_backward/pallas_call | solution.py:1139
  531.5 11.9 %embed_backward.1 = (bf16[3072,768]{1,0:T(8,128)(2,1)}, f32[64,768]{1,0:T(8,128)}, f32[1,768]{1,0:T(1,128)}) custom-call(bf16[1024,3072]{1,0:T(8,128)(2,1)} %pixel_ref.3, f32[1024,768]{1,0:T(8,128)} %get-tuple-element.124.grad_ref, f32[64,1024]{1,0:T(8,128)} %pad_bitcast_fusion.1.pos_ref), custom_call_target="tpu_custom_call" | custom-call | tf_op jit(solution)/shard_map/embed_backward/pallas_call | solution.py:1250
  543.4 0.9 slice.127
  544.3 0.7 reduce.12
  545.7 1.4 concatenate.15
  548.0 0.7 pad.37.refs_6_
  548.7 16.0 %input_weight_grad.3 = bf16[768,5376]{1,0:T(8,128)(2,1)} custom-call(bf16[1024,768]{1,0:T(8,128)(2,1)} %get-tuple-element.86.first_ref, bf16[1024,768]{1,0:T(8,128)(2,1)} %get-tuple-element.90.second_ref, bf16[1024,2304]{1,0:T(8,128)(2,1)} %get-tuple-element.121.qkv_ref.grad_ref, bf16[1024,3072]{1,0:T(8,128)(2,1)} %get-tuple-element.122.hidden_ref), custom_call_target="tpu_custom_call" | custom-call | tf_op jit(solution)/shard_map/input_weight_grad/pallas_call | solution.py:1177
  564.7 101.1 %reduce_gradients.1 = (bf16[96,5376]{1,0:T(8,128)(2,1)}, bf16[384,768]{1,0:T(8,128)(2,1)}) custom-call(bf16[8,96,5376]{2,1,0:T(8,128)(2,1)} %bitcast.63, bf16[8,384,768]{2,1,0:T(8,128)(2,1)} %bitcast.75), custom_call_target="tpu_custom_call" | custom-call | tf_op jit(solution)/shard_map/reduce_gradients/pallas_call | solution.py:564
  665.9 60.3 %finish_gradients.1 = (bf16[96,1024]{1,0:T(8,128)(2,1)}, bf16[480,768]{1,0:T(8,128)(2,1)}, bf16[96,5376]{1,0:T(8,128)(2,1)}, f32[64,128]{1,0:T(8,128)}, f32[8,64,128]{2,1,0:T(8,128)}) custom-call(bf16[96,5376]{1,0:T(8,128)(2,1)} %get-tuple-element.126.refs_0_, bf16[384,768]{1,0:T(8,128)(2,1)} %get-tuple-element.127.refs_1_, ...), custom_call_target="tpu_custom_call" | custom-call | tf_op jit(solution)/shard_map/finish_gradients/pallas_call | solution.py:618
  726.2 1.5 multiply_reduce_fusion.4
  727.8 1.4 slice_reduce_fusion.10
  729.1 0.9 slice.128
  730.1 0.6 multiply_reduce_fusion.3
  736.7 0.7 slice_bitcast_fusion.3
  737.5 0.6 multiply_subtract_fusion.5
  738.2 3.9 multiply_subtract_fusion.2
  742.2 2.0 multiply_subtract_fusion.4
  744.2 0.6 multiply_subtract_fusion.6
  744.9 2.2 multiply_subtract_fusion.3
  747.2 5.6 multiply_subtract_fusion.1
  752.8 1.2 copy-done.6
  754.0 1.2 copy-done.7
  755.3 6.2 multiply_subtract_fusion
  (146 shorter events, 7.7 us)
Async XLA Ops:
  7.2 164.7 %all-gather.10.cloned.1.call-start = ((), (), s32[]{:S(2)}) async-start(), calls=%async_computation.7 | async-start | bytes 6635520 | tf_op jit(solution)/shard_map/all_gather | solution.py:1325
  10.4 187.2 %all-gather.12.cloned.1.call-start = ((), (), s32[]{:S(2)}) async-start(), calls=%async_computation.8 | async-start | bytes 3981312 | tf_op jit(solution)/shard_map/all_gather | solution.py:1325
  12.9 4.1 copy-start.19
  12.9 4.3 copy-start.21
  12.9 4.5 copy-start.36
  13.9 4.3 copy-start.3
  13.9 5.1 copy-start.23
  13.9 257.3 %all-gather.14.cloned.1.call-start = ((), (), s32[]{:S(2)}) async-start(), calls=%async_computation.9 | async-start | bytes 5308416 | tf_op jit(solution)/shard_map/all_gather | solution.py:1325
  15.1 286.8 %all-gather.8.cloned.1.call-start = ((), (), s32[]{:S(2)}) async-start(), calls=%async_computation.3 | async-start | bytes 1769472 | tf_op jit(solution)/shard_map/all_gather | solution.py:1325
  16.9 648.9 %reduce-scatter.4.cloned.1.call-start = ((), (), s32[]{:S(2)}) async-start(), calls=%async_computation.4 | async-start | bytes 1769472 | tf_op jit(solution)/shard_map/reduce_scatter | solution.py:658
  17.1 0.7 copy-start.33
  296.9 2.8 copy-start
  296.9 3.3 copy-start.20
  300.2 3.5 copy-start.35
  311.2 354.6 %reduce-scatter.6.cloned.1.call-start = ((), (), s32[]{:S(2)}) async-start(), calls=%async_computation.5 | async-start | bytes 6635520 | tf_op jit(solution)/shard_map/reduce_scatter | solution.py:658
  356.2 309.7 %reduce-scatter.8.cloned.1.call-start = ((), (), s32[]{:S(2)}) async-start(), calls=%async_computation.6 | async-start | bytes 9289728 | tf_op jit(solution)/shard_map/reduce_scatter | solution.py:658
  531.4 13.6 %copy-start.34 = (s32[8]{0:T(128)S(1)}, s32[8]{0:T(128)}, u32[]{:S(2)}) copy-start(s32[8]{0:T(128)} %copy-done.33) | copy-start | bytes 100
  531.4 15.7 %copy-start.30 = (f32[1,3840]{1,0:T(1,128)S(1)}, f32[1,3840]{1,0:T(1,128)}, u32[]{:S(2)}) copy-start(f32[1,3840]{1,0:T(1,128)} %get-tuple-element.131) | copy-start | bytes 46084
  531.4 15.7 %copy-start.26 = (f32[1,6144]{1,0:T(1,128)S(1)}, f32[1,6144]{1,0:T(1,128)}, u32[]{:S(2)}) copy-start(f32[1,6144]{1,0:T(1,128)} %get-tuple-element.132) | copy-start | bytes 73732
  531.5 15.9 %copy-start.29 = (f32[1,3840]{1,0:T(1,128)S(1)}, f32[1,3840]{1,0:T(1,128)}, u32[]{:S(2)}) copy-start(f32[1,3840]{1,0:T(1,128)} %get-tuple-element.133) | copy-start | bytes 46084
  531.5 16.0 %copy-start.25 = (f32[1,6144]{1,0:T(1,128)S(1)}, f32[1,6144]{1,0:T(1,128)}, u32[]{:S(2)}) copy-start(f32[1,6144]{1,0:T(1,128)} %get-tuple-element.134) | copy-start | bytes 73732
  665.7 71.7 %copy-start.22 = (f32[3304]{0:T(1024)S(1)}, f32[3304]{0:T(1024)}, u32[]{:S(2)}) copy-start(f32[3304]{0:T(1024)} %param.35) | copy-start | bytes 39652
  665.7 71.7 %copy-start.27 = (f32[3304]{0:T(1024)S(1)}, f32[3304]{0:T(1024)}, u32[]{:S(2)}) copy-start(f32[3304]{0:T(1024)} %param.49) | copy-start | bytes 39652
  665.8 71.7 %copy-start.28 = (f32[3304]{0:T(1024)S(1)}, f32[3304]{0:T(1024)}, u32[]{:S(2)}) copy-start(f32[3304]{0:T(1024)} %param.42) | copy-start | bytes 39652
  665.8 72.4 %copy-start.4 = (f32[384,768]{1,0:T(8,128)S(1)}, f32[384,768]{1,0:T(8,128)}, u32[]{:S(2)}) copy-start(f32[384,768]{1,0:T(8,128)} %param.29) | copy-start | bytes 3538948
  665.8 72.3 %copy-start.11 = (bf16[384,768]{1,0:T(8,128)(2,1)S(1)}, bf16[384,768]{1,0:T(8,128)(2,1)}, u32[]{:S(2)}) copy-start(bf16[384,768]{1,0:T(8,128)(2,1)} %get-tuple-element.127.refs_1_) | copy-start | bytes 1769476
  665.8 72.3 %copy-start.13 = (f32[384,768]{1,0:T(8,128)S(1)}, f32[384,768]{1,0:T(8,128)}, u32[]{:S(2)}) copy-start(f32[384,768]{1,0:T(8,128)} %param.43) | copy-start | bytes 3538948
  738.1 4.0 copy-start.16
  738.1 6.1 copy-start.24
  738.2 6.0 copy-start.31
  738.2 6.0 copy-start.32
  738.2 6.7 copy-start.12
  738.2 6.7 copy-start.17
  738.2 6.7 copy-start.18
  738.2 8.9 %copy-start.8 = (f32[2,480,768]{2,1,0:T(8,128)S(1)}, f32[2,480,768]{2,1,0:T(8,128)}, u32[]{:S(2)}) copy-start(f32[2,480,768]{2,1,0:T(8,128)} %param.46) | copy-start | bytes 8847364
  738.2 8.9 %copy-start.9 = (f32[2,480,768]{2,1,0:T(8,128)S(1)}, f32[2,480,768]{2,1,0:T(8,128)}, u32[]{:S(2)}) copy-start(f32[2,480,768]{2,1,0:T(8,128)} %param.39) | copy-start | bytes 8847364
  738.2 8.9 %copy-start.15 = (bf16[480,768]{1,0:T(8,128)(2,1)S(1)}, bf16[480,768]{1,0:T(8,128)(2,1)}, u32[]{:S(2)}) copy-start(bf16[480,768]{1,0:T(8,128)(2,1)} %get-tuple-element.140) | copy-start | bytes 2211844
  742.2 4.9 copy-start.2
  742.2 5.0 copy-start.10
  747.1 5.6 copy-start.1
  747.2 5.6 copy-start.5
  747.2 6.8 copy-start.6
  747.2 8.0 %copy-start.7 = (f32[2,96,5376]{2,1,0:T(8,128)S(1)}, f32[2,96,5376]{2,1,0:T(8,128)}, u32[]{:S(2)}) copy-start(f32[2,96,5376]{2,1,0:T(8,128)} %param.38) | copy-start | bytes 12386308
  747.2 8.1 %copy-start.14 = (bf16[96,5376]{1,0:T(8,128)(2,1)S(1)}, bf16[96,5376]{1,0:T(8,128)(2,1)}, u32[]{:S(2)}) copy-start(bf16[96,5376]{1,0:T(8,128)(2,1)} %get-tuple-element.139) | copy-start | bytes 3096580
Sparse Core Ops, SparseCore 0:
  10.6 86.6 all-gather.9
  99.4 52.6 all-gather.11
  153.8 51.1 all-gather.13
  207.1 37.0 all-gather.7
  311.3 32.2 reduce-scatter.3
  356.3 64.1 reduce-scatter.5
  422.9 98.5 reduce-scatter.7

commit v5 on v4

--- a/solution.py
+++ b/solution.py
@@ -347,6 +347,9 @@
             for other in TURNS:
                 self.group_copy(turn, other).start()
 
+    def between(self):
+        pass
+
     def third(self):
         group, level, _ = place()
         high, wide = quarter_shape(self.rows, self.columns)
@@ -406,6 +409,195 @@
                 self.share_copy(turn).wait_send()
 
 
+WHOLE_SEMS = 40
+
+
+def add_rows(target, row, columns, source, count, wide):
+    chunk = 16 if wide > 1536 else 48
+
+    def add(step, carry):
+        at = pl.multiple_of(step * chunk, chunk)
+        mine = pl.ds(pl.multiple_of(row + at, 16), chunk)
+        total = target[mine, columns].astype(jnp.float32)
+        total = total + source[pl.ds(at, chunk), :].astype(jnp.float32)
+        target[mine, columns] = total.astype(target.dtype)
+        return carry
+
+    lax.fori_loop(0, count // chunk, add, 0)
+
+
+class Whole:
+    FIRST_X = (1, 0)
+
+    def __init__(self, grad, out, scratch, sems):
+        self.grad, self.out, self.sems = grad, out, sems
+        self.own, self.got_core, self.got_x, self.got_y, self.got_last, self.part, self.got_level = scratch
+        self.rows, self.columns = out.shape
+        self.high, self.wide = self.rows // 2, self.columns // 2
+
+    def row_half(self, index):
+        return pl.ds(pl.multiple_of(lax.div(index, 2) * self.high, self.high), self.high)
+
+    def column_half(self, index):
+        return pl.ds(pl.multiple_of(lax.rem(index, 2) * self.wide, self.wide), self.wide)
+
+    def load(self, level):
+        _, _, core = place()
+        return pltpu.make_async_copy(
+            self.grad.at[2 * level + core], self.own.at[level], self.sems.at[level]
+        )
+
+    def core_copy(self, target_level):
+        group, level, core = place()
+        return remote(
+            self.grad.at[2 * target_level + 1 - core],
+            self.got_core.at[target_level],
+            self.sems.at[4 + target_level],
+            self.sems.at[8 + target_level],
+            (group, 2 * level + 1 - core),
+        )
+
+    def step_copy(self, turn):
+        group, level, core = place()
+        block = self.own.at[partner(level, turn)]
+        if turn in self.FIRST_X:
+            peer = partner(group, 1)
+            source = block.at[:, self.column_half(peer)]
+            target = self.got_x.at[self.FIRST_X.index(turn)]
+        else:
+            peer = partner(group, 2)
+            source = block.at[self.row_half(peer), :]
+            target = self.got_y.at[turn - 2]
+        return remote(
+            source, target, self.sems.at[12 + turn], self.sems.at[16 + turn], (peer, 2 * level + core)
+        )
+
+    def last_copy(self, turn):
+        group, level, core = place()
+        block = self.own.at[partner(level, turn)]
+        peer = partner(group, 2 if turn in self.FIRST_X else 1)
+        rows = self.row_half(peer)
+        columns = self.column_half(peer)
+        return remote(
+            block.at[rows, columns],
+            self.got_last.at[turn],
+            self.sems.at[20 + turn],
+            self.sems.at[24 + turn],
+            (peer, 2 * level + core),
+        )
+
+    def level_copy(self, turn):
+        group, level, core = place()
+        target = partner(level, turn)
+        return remote(
+            self.part.at[target],
+            self.got_level.at[turn - 1],
+            self.sems.at[27 + turn],
+            self.sems.at[30 + turn],
+            (group, 2 * target + core),
+        )
+
+    def share_copy(self, other):
+        group, level, core = place()
+        mine = self.out.at[self.row_half(group), self.column_half(group)]
+        return remote(
+            mine,
+            mine,
+            self.sems.at[33 + other],
+            self.sems.at[36 + other],
+            (partner(group, other), 2 * level + core),
+        )
+
+    def first(self):
+        _, level, _ = place()
+        for turn in (*TURNS, 0):
+            self.core_copy(partner(level, turn)).start()
+            self.load(partner(level, turn)).start()
+
+    def second(self):
+        _, level, _ = place()
+        for turn in (*TURNS, 0):
+            target = partner(level, turn)
+            self.load(target).wait()
+            self.core_copy(target).wait_recv()
+            add_rows(
+                self.own.at[target], 0, slice(None), self.got_core.at[target], self.rows, self.columns
+            )
+            self.step_copy(turn).start()
+
+    def between(self):
+        group, level, _ = place()
+        for turn in (*TURNS, 0):
+            block = self.own.at[partner(level, turn)]
+            self.step_copy(turn).wait_recv()
+            if turn in self.FIRST_X:
+                source = self.got_x.at[self.FIRST_X.index(turn)]
+                add_rows(block, 0, self.column_half(group), source, self.rows, self.wide)
+            else:
+                source = self.got_y.at[turn - 2]
+                start = lax.div(group, 2) * self.high
+                add_rows(block, start, slice(None), source, self.high, self.columns)
+            self.last_copy(turn).start()
+
+    def third(self):
+        group, level, _ = place()
+        start = lax.div(group, 2) * self.high
+        columns = self.column_half(group)
+        chunk = 16 if self.wide > 1536 else 48
+        for turn in (*TURNS, 0):
+            target = partner(level, turn)
+            self.last_copy(turn).wait_recv()
+
+            def add(step, carry):
+                at = pl.multiple_of(step * chunk, chunk)
+                rows = pl.ds(at, chunk)
+                mine = pl.ds(pl.multiple_of(start + at, 16), chunk)
+                total = self.own[target, mine, columns].astype(jnp.float32)
+                total = total + self.got_last[turn, rows, :].astype(jnp.float32)
+                self.part[target, rows, :] = total.astype(self.part.dtype)
+                return carry
+
+            lax.fori_loop(0, self.high // chunk, add, 0)
+            if turn:
+                self.level_copy(turn).start()
+
+    def fourth(self):
+        group, level, _ = place()
+        start = lax.div(group, 2) * self.high
+        columns = self.column_half(group)
+        chunk = 16 if self.wide > 1536 else 48
+        for turn in TURNS:
+            self.level_copy(turn).wait_recv()
+
+        def add(step, carry):
+            at = pl.multiple_of(step * chunk, chunk)
+            rows = pl.ds(at, chunk)
+            mine = pl.ds(pl.multiple_of(start + at, 16), chunk)
+            total = self.part[level, rows, :].astype(jnp.float32)
+            for slot in range(3):
+                total = total + self.got_level[slot, rows, :].astype(jnp.float32)
+            self.out[mine, columns] = total.astype(self.out.dtype)
+            return carry
+
+        lax.fori_loop(0, self.high // chunk, add, 0)
+        for other in TURNS:
+            self.share_copy(other).start()
+
+    def fifth(self):
+        for other in TURNS:
+            self.share_copy(other).wait_recv()
+
+    def sixth(self):
+        _, level, _ = place()
+        for turn in (*TURNS, 0):
+            self.core_copy(partner(level, turn)).wait_send()
+            self.step_copy(turn).wait_send()
+            self.last_copy(turn).wait_send()
+            if turn:
+                self.level_copy(turn).wait_send()
+                self.share_copy(turn).wait_send()
+
+
 GROUP_SEMS = 13
 
 
@@ -448,6 +640,9 @@
         self.load().wait()
         for other in TURNS:
             self.group_copy(other).start()
+
+    def between(self):
+        pass
 
     def third(self):
         group, _, _ = place()
@@ -532,7 +727,7 @@
             getattr(job, stage)()
 
 
-STAGES = ("first", "second", "third", "fourth", "fifth", "sixth")
+STAGES = ("first", "second", "between", "third", "fourth", "fifth", "sixth")
 
 
 def whole_scratch(grad):
@@ -542,37 +737,78 @@
     return [pltpu.VMEM(shape, grad.dtype) for shape in (*shapes, (3, high, wide))]
 
 
-def reduce_kernel(*refs):
-    count = (len(refs) - 1) // 7
-    grads, outs, sems, refs = refs[:count], refs[count : 2 * count], refs[2 * count], refs[2 * count + 1 :]
+def stepped_scratch(grad):
+    _, rows, columns = grad.shape
+    high, wide = rows // 2, columns // 2
+    shapes = (
+        (4, rows, columns),
+        (4, rows, columns),
+        (2, rows, wide),
+        (2, high, columns),
+        (4, high, wide),
+        (4, high, wide),
+        (3, high, wide),
+    )
+    return [pltpu.VMEM(shape, grad.dtype) for shape in shapes]
+
+
+def share_scratch(share):
+    return [
+        pltpu.VMEM(share.shape, share.dtype),
+        pltpu.VMEM((3, *quarter_shape(*share.shape)), share.dtype),
+    ]
+
+
+def reduce_kernel(*refs, whole, partly):
+    count = whole + partly
+    grads, outs, refs = refs[:count], refs[count : 2 * count], refs[2 * count :]
+    sems, group_sems, refs = refs[0], refs[1], refs[2:]
     jobs = [
-        Reduce(grads[i], outs[i], refs[5 * i : 5 * i + 5], sems.at[i]) for i in range(count)
+        Whole(grads[i], outs[i], refs[7 * i : 7 * i + 7], sems.at[i]) for i in range(whole)
+    ]
+    refs = refs[7 * whole :]
+    shares = [
+        GroupReduce(grads[whole + i], outs[whole + i], refs[2 * i : 2 * i + 2], group_sems.at[i])
+        for i in range(partly)
     ]
     greet()
-    run_stages(jobs, STAGES)
+    run_stages([*jobs, *shares], STAGES[:1])
+    run_stages(shares, STAGES[1:2])
+    run_stages(jobs, STAGES[1:3])
+    run_stages(shares, STAGES[3:4])
+    run_stages(jobs, STAGES[3:5])
+    run_stages([*shares, *jobs], STAGES[5:])
 
 
 def transfer_cost(size):
     return pl.CostEstimate(flops=4000 * size, bytes_accessed=2 * size, transcendentals=0)
 
 
-def reduce_call(grads, collective_id):
+def reduce_call(grads, shares, collective_id):
     in_vmem = pl.BlockSpec(memory_space=pltpu.VMEM)
-    scratch = [pltpu.SemaphoreType.DMA((len(grads), REDUCE_SEMS))]
+    whole, partly = len(grads), len(shares)
+    scratch = [
+        pltpu.SemaphoreType.DMA((whole, WHOLE_SEMS)),
+        pltpu.SemaphoreType.DMA((partly, GROUP_SEMS)),
+    ]
     for grad in grads:
-        scratch.extend(whole_scratch(grad))
+        scratch.extend(stepped_scratch(grad))
+    for share in shares:
+        scratch.extend(share_scratch(share))
+    out_shape = [jax.ShapeDtypeStruct(g.shape[1:], g.dtype) for g in grads]
+    out_shape += [jax.ShapeDtypeStruct(s.shape, s.dtype) for s in shares]
     return pl.pallas_call(
-        reduce_kernel,
-        in_specs=[ANYWHERE] * len(grads),
-        out_specs=[in_vmem] * len(grads),
-        out_shape=[jax.ShapeDtypeStruct(g.shape[1:], g.dtype) for g in grads],
+        functools.partial(reduce_kernel, whole=whole, partly=partly),
+        in_specs=[ANYWHERE] * (whole + partly),
+        out_specs=[in_vmem] * (whole + partly),
+        out_shape=out_shape,
         scratch_shapes=scratch,
         compiler_params=pltpu.CompilerParams(
             collective_id=collective_id, has_side_effects=True, vmem_limit_bytes=VMEM_LIMIT
         ),
         cost_estimate=NO_COST,
         name="reduce_gradients",
-    )(*grads)
+    )(*grads, *shares)
 
 
 def finish_kernel(*refs, done, partly):
@@ -587,9 +823,9 @@
         for i in range(partly)
     ]
     greet()
-    run_stages([job, *jobs], STAGES[:2])
+    run_stages([job, *jobs], STAGES[:3])
     total = sum(squares_in(out) for out in finished)
-    run_stages([*jobs, job], STAGES[2:5])
+    run_stages([*jobs, job], STAGES[3:6])
     total = total + sum(squares_in(out) for out in outs)
     _, level, core = place()
     mine = 2 * level + core
@@ -597,7 +833,7 @@
     full[mine] = small_out[...]
     full[mine, last : last + 1, :] = total
     Spread(full, spread_sems).run()
-    run_stages([job, *jobs], STAGES[5:])
+    run_stages([job, *jobs], STAGES[6:])
 
 
 def finish_call(finished, shares, small, collective_id):
@@ -610,8 +846,7 @@
         *whole_scratch(small),
     ]
     for share in shares:
-        scratch.append(pltpu.VMEM(share.shape, share.dtype))
-        scratch.append(pltpu.VMEM((3, *quarter_shape(*share.shape)), share.dtype))
+        scratch.extend(share_scratch(share))
     out_shape = [jax.ShapeDtypeStruct(s.shape, s.dtype) for s in shares]
     out_shape.append(jax.ShapeDtypeStruct(small.shape[1:], small.dtype))
     out_shape.append(jax.ShapeDtypeStruct(small.shape, small.dtype))
@@ -638,10 +873,14 @@
     return [lax.all_gather(shard, "fsdp", axis=0, tiled=True) for shard in shards]
 
 
-def reduce_all(grads, collective_id):
+def reduce_all(grads, shares, collective_id):
     if with_kernels():
-        return reduce_call(grads, collective_id)
-    return [lax.psum(scatter(grad), "dp") for grad in grads]
+        return reduce_call(grads, shares, collective_id)
+    return [lax.psum(scatter(grad), "dp") for grad in grads] + sum_shares(shares)
+
+
+def sum_shares(shares):
+    return [lax.psum(share, "dp") for share in shares]
 
 
 def finish_all(finished, shares, small, collective_id):
@@ -652,6 +891,14 @@
     total = sum(jnp.sum(jnp.square(out.astype(jnp.float32))) for out in (*finished, *outs))
     row = jnp.full((1, LANES), 1.0 / LANES, jnp.float32) * total
     return [*outs, own, lax.all_gather(own.at[-1:].set(row), "fsdp", axis=0)]
+
+
+def take(items, *counts):
+    cut = []
+    for count in counts:
+        cut.append(items[:count])
+        items = items[count:]
+    return cut
 
 
 def scatter(grad):
@@ -674,34 +921,32 @@
     rows = q_ref.shape[0]
     lower = lax.broadcasted_iota(jnp.int32, (block, PAIR), 1) < HD
     keys = k_ref[...]
-    values = v_ref[...]
+    values = jnp.concatenate([v_ref[...], jnp.ones((rows, PAIR), v_ref.dtype)], 1)
     seg_row = seg_row_ref[...]
-
-    def one_block(step, carry):
-        at = pl.ds(pl.multiple_of(step * block, block), block)
-        query = q_ref[at, :] * jnp.bfloat16(HD**-0.5)
-        same = seg_col_ref[at, :] == seg_row
-        outs, invs = [], []
-        for head in range(2):
-            keep = lower if head == 0 else jnp.logical_not(lower)
-            mine = jnp.where(keep, query, jnp.bfloat16(0))
-            scores = lax.dot_general(
-                mine, keys, (((1,), (1,)), ((), ())), preferred_element_type=jnp.float32
-            )
-            scores = jnp.where(same, scores, MASKED)
-            highest = jnp.max(scores, -1, keepdims=True)
-            exponent = jnp.exp(scores - highest)
-            total = jnp.sum(exponent, -1, keepdims=True)
-            low = exponent.astype(jnp.bfloat16)
-            expo_ref[head, at, :] = low
-            outs.append(jnp.dot(low, values, preferred_element_type=jnp.float32))
-            invs.append(1.0 / total)
-        inverse = jnp.where(lower, invs[0], invs[1])
-        out_ref[at, :] = (jnp.where(lower, outs[0], outs[1]) * inverse).astype(jnp.bfloat16)
-        inv_ref[at, :] = inverse
-        return carry
-
-    lax.fori_loop(0, rows // block, one_block, 0, unroll=True)
+    tasks = [(step, head) for step in range(rows // block) for head in range(2)]
+
+    def scores_of(step, head):
+        query = q_ref[step * block : (step + 1) * block, :] * jnp.bfloat16(HD**-0.5)
+        keep = lower if head == 0 else jnp.logical_not(lower)
+        return mul_nt(jnp.where(keep, query, jnp.bfloat16(0)), keys)
+
+    scores = scores_of(*tasks[0])
+    outs = []
+    for index, (step, head) in enumerate(tasks):
+        following = scores_of(*tasks[index + 1]) if index + 1 < len(tasks) else None
+        at = slice(step * block, (step + 1) * block)
+        scores = jnp.where(seg_col_ref[at, :] == seg_row, scores, MASKED)
+        highest = jnp.max(scores, -1, keepdims=True)
+        low = jnp.exp(scores - highest).astype(jnp.bfloat16)
+        expo_ref[head, at, :] = low
+        outs.append(mul(low, values))
+        if head:
+            inverse = 1.0 / jnp.where(lower, outs[0][:, PAIR:], outs[1][:, PAIR:])
+            sums = jnp.where(lower, outs[0][:, :PAIR], outs[1][:, :PAIR])
+            out_ref[at, :] = (sums * inverse).astype(jnp.bfloat16)
+            inv_ref[at, :] = inverse
+            outs = []
+        scores = following
     if jobs:
         beside(jobs, {pl.num_programs(0) - 1: ("fourth",)})
 
@@ -760,11 +1005,11 @@
     sources, refs = refs[7 : 7 + reduced], refs[7 + reduced :]
     dqkv_ref, sums, refs = refs[0], refs[1 : 1 + reduced], refs[1 + reduced :]
     jobs = [
-        Reduce(sources[i], refs[6 * i + 1], refs[6 * i + 2 : 6 * i + 7], refs[0].at[i])
+        GroupReduce(sources[i], refs[3 * i + 1], refs[3 * i + 2 : 3 * i + 4], refs[0].at[i])
         for i in range(reduced)
     ]
     if jobs:
-        beside(jobs, {0: ("greet", "first"), 1: ("second",)})
+        beside(jobs, {0: ("greet", "first", "second"), 3: ("third",)})
     rows = q_ref.shape[0]
     pair = pl.program_id(0)
     lower = lax.broadcasted_iota(jnp.int32, (block, PAIR), 1) < HD
@@ -778,32 +1023,41 @@
     product = scaled_grad.astype(jnp.float32) * out_ref[...].astype(jnp.float32)
     key_t = [None, None]
     value_t = [None, None]
-    for step in range(rows // block):
+    tasks = [(step, head) for step in range(rows // block) for head in range(2)]
+
+    def probs_grad_of(step, head):
+        keep = lower if head == 0 else jnp.logical_not(lower)
+        mine = scaled_grad[step * block : (step + 1) * block]
+        return mul_nt(jnp.where(keep, mine, jnp.bfloat16(0)), values)
+
+    probs_grad = probs_grad_of(*tasks[0])
+    query_parts = []
+    for index, (step, head) in enumerate(tasks):
+        following = probs_grad_of(*tasks[index + 1]) if index + 1 < len(tasks) else None
         at = slice(step * block, (step + 1) * block)
-        query_parts = []
-        for head in range(2):
-            lanes = slice(head * HD, (head + 1) * HD)
-            keep = lower if head == 0 else jnp.logical_not(lower)
-            mine = jnp.where(keep, scaled_grad[at], jnp.bfloat16(0))
-            inner = jnp.sum(jnp.where(keep, product[at], 0.0), -1, keepdims=True)
-            low = expo_ref[head, at, :]
-            probs_grad = lax.dot_general(
-                mine, values, (((1,), (1,)), ((), ())), preferred_element_type=jnp.float32
+        lanes = slice(head * HD, (head + 1) * HD)
+        keep = lower if head == 0 else jnp.logical_not(lower)
+        inner = jnp.sum(jnp.where(keep, product[at], 0.0), -1, keepdims=True)
+        low = expo_ref[head, at, :]
+        value_part = mul(grad_t[lanes, at], low)
+        scores_grad = (low.astype(jnp.float32) * (probs_grad - inner)).astype(jnp.bfloat16)
+        query_parts.append(mul(scores_grad, keys))
+        key_part = mul(query_t[lanes, at], scores_grad)
+        key_t[head] = key_part if step == 0 else key_t[head] + key_part
+        value_t[head] = value_part if step == 0 else value_t[head] + value_part
+        if head:
+            query_grad = jnp.where(lower, query_parts[0], query_parts[1]) * scale
+            dqkv_ref[at, pl.ds(pl.multiple_of(pair * PAIR, PAIR), PAIR)] = query_grad.astype(
+                jnp.bfloat16
             )
-            scores_grad = (low.astype(jnp.float32) * (probs_grad - inner)).astype(jnp.bfloat16)
-            query_parts.append(jnp.dot(scores_grad, keys, preferred_element_type=jnp.float32))
-            key_part = jnp.dot(query_t[lanes, at], scores_grad, preferred_element_type=jnp.float32)
-            value_part = jnp.dot(grad_t[lanes, at], low, preferred_element_type=jnp.float32)
-            key_t[head] = key_part if step == 0 else key_t[head] + key_part
-            value_t[head] = value_part if step == 0 else value_t[head] + value_part
-        query_grad = jnp.where(lower, query_parts[0], query_parts[1]) * scale
-        dqkv_ref[at, pl.ds(pl.multiple_of(pair * PAIR, PAIR), PAIR)] = query_grad.astype(jnp.bfloat16)
+            query_parts = []
+        probs_grad = following
     key_grad = (jnp.concatenate(key_t, 0) * scale).T
     value_grad = jnp.concatenate(value_t, 0).T
     dqkv_ref[:, pl.ds(pl.multiple_of(D + pair * PAIR, PAIR), PAIR)] = key_grad.astype(jnp.bfloat16)
     dqkv_ref[:, pl.ds(pl.multiple_of(2 * D + pair * PAIR, PAIR), PAIR)] = value_grad.astype(jnp.bfloat16)
     if jobs:
-        beside(jobs, {pl.num_programs(0) - 1: STAGES[2:]})
+        beside(jobs, {pl.num_programs(0) - 1: STAGES[5:]})
 
         @pl.when(pair == pl.num_programs(0) - 1)
         def _():
@@ -811,18 +1065,18 @@
                 total[...] = job.out[...]
 
 
-def attention_backward(qkv_rows, expo, inverse, attended, attended_grad, grads, collective_id):
+def attention_backward(qkv_rows, expo, inverse, attended, attended_grad, shares, collective_id):
     plain = []
     if not with_kernels():
-        plain, grads = reduce_all(grads, collective_id), []
-    reduced = len(grads)
+        plain, shares = sum_shares(shares), []
+    reduced = len(shares)
     transfer, scratch = {}, []
     if reduced:
         transfer = {"collective_id": collective_id, "has_side_effects": True}
-        scratch.append(pltpu.SemaphoreType.DMA((reduced, REDUCE_SEMS)))
-    for grad in grads:
-        scratch.append(pltpu.VMEM(grad.shape[1:], grad.dtype))
-        scratch.extend(whole_scratch(grad))
+        scratch.append(pltpu.SemaphoreType.DMA((reduced, GROUP_SEMS)))
+    for share in shares:
+        scratch.append(pltpu.VMEM(share.shape, share.dtype))
+        scratch.extend(share_scratch(share))
     rows = qkv_rows.shape[0]
     pairs = HEADS // 2
     block = min(256, rows)
@@ -840,16 +1094,16 @@
             wide(0),
             *[ANYWHERE] * reduced,
         ],
-        out_specs=[fixed(rows, 3 * D), *[fixed(*g.shape[1:]) for g in grads]],
+        out_specs=[fixed(rows, 3 * D), *[fixed(*s.shape) for s in shares]],
         out_shape=[
             jax.ShapeDtypeStruct((rows, 3 * D), jnp.bfloat16),
-            *[jax.ShapeDtypeStruct(g.shape[1:], g.dtype) for g in grads],
+            *[jax.ShapeDtypeStruct(s.shape, s.dtype) for s in shares],
         ],
         scratch_shapes=scratch,
         compiler_params=pltpu.CompilerParams(vmem_limit_bytes=VMEM_LIMIT, **transfer),
         cost_estimate=NO_COST,
         name="attention_backward",
-    )(qkv_rows, qkv_rows, qkv_rows, expo, inverse, attended, attended_grad, *grads)
+    )(qkv_rows, qkv_rows, qkv_rows, expo, inverse, attended, attended_grad, *shares)
     return qkv_grad, plain + sums
 
 
@@ -1002,17 +1256,23 @@
     normed = (unit * vector_ref[:, 2 * D : 3 * D] + vector_ref[:, 3 * D : 4 * D]).astype(jnp.bfloat16)
     normed_ref[...] = normed
     at_first(copies[1].wait)
-    part = 768
+    part = 512
+
+    def hidden_of(base):
+        bias = vector_ref[:, 9 * D + base : 9 * D + base + part]
+        return mul(normed, up_ref[:, base : base + part]) + bias
+
+    hidden = hidden_of(0)
     for base in range(0, width, part):
+        following = hidden_of(base + part) if base + part < width else None
         columns = slice(base, base + part)
-        bias = vector_ref[:, 9 * D + base : 9 * D + base + part]
-        hidden = mul(normed, up_ref[:, columns]) + bias
         square = hidden * hidden
-        bend = jnp.tanh(hidden * (ROOT + (ROOT * CUBE) * square))
-        half = 0.5 * (1.0 + bend)
-        active_ref[:, columns] = (hidden * half).astype(jnp.bfloat16)
-        rise = (0.5 * ROOT) + (1.5 * ROOT * CUBE) * square
-        slope_ref[:, columns] = (half + hidden * (1.0 - bend * bend) * rise).astype(jnp.bfloat16)
+        half = 0.5 + 0.5 * jnp.tanh(hidden * (ROOT + (ROOT * CUBE) * square))
+        active = hidden * half
+        active_ref[:, columns] = active.astype(jnp.bfloat16)
+        rise = (2.0 * ROOT) + (6.0 * ROOT * CUBE) * square
+        slope_ref[:, columns] = (half + active * (1.0 - half) * rise).astype(jnp.bfloat16)
+        hidden = following
     at_first(copies[2].wait)
     out_ref[...] = residual + mul(active_ref[...], down_ref[...]) + vector_ref[:, 8 * D : 9 * D]
 
@@ -1067,14 +1327,18 @@
     grad = grad_ref[...]
     grad_low = grad.astype(jnp.bfloat16)
     low_ref[...] = grad_low
-    part = 768
+    part = 512
     hidden_sums = []
+    active_grad = mul_nt(grad_low, down_ref[:part, :])
     for base in range(0, width, part):
+        following = None
+        if base + part < width:
+            following = mul_nt(grad_low, down_ref[base + part : base + 2 * part, :])
         columns = slice(base, base + part)
-        active_grad = mul_nt(grad_low, down_ref[columns, :])
         hidden_grad = (active_grad * slope_ref[:, columns].astype(jnp.float32)).astype(jnp.bfloat16)
         hidden_ref[:, columns] = hidden_grad
         hidden_sums.append(column_sum(hidden_grad))
+        active_grad = following
     at_first(copies[1].wait)
     second_grad = mul_nt(hidden_ref[...], up_ref[...])
     value_grad, gain_grad, shift_grad = norm_backward(
@@ -1150,7 +1414,7 @@
     )(grad, residual_grad, stream, weight, vector)
 
 
-def input_grad_kernel(first_ref, second_ref, qkv_ref, hidden_ref, out_ref, left_ref, *, cut):
+def input_grad_kernel(first_ref, second_ref, qkv_ref, hidden_ref, qkv_out, up_out, left_ref, *, cut):
     step = pl.program_id(0)
 
     @pl.when(step == 0)
@@ -1163,28 +1427,33 @@
 
     @pl.when(step < cut)
     def _():
-        out_ref[...] = mul(left_ref[...], qkv_ref[...]).astype(jnp.bfloat16)
+        qkv_out[...] = mul(left_ref[...], qkv_ref[...]).astype(jnp.bfloat16)
 
     @pl.when(step >= cut)
     def _():
-        out_ref[...] = mul(left_ref[...], hidden_ref[...]).astype(jnp.bfloat16)
+        up_out[...] = mul(left_ref[...], hidden_ref[...]).astype(jnp.bfloat16)
 
 
 def input_weight_grad(first, second, qkv_grad, hidden_grad):
     rows = first.shape[0]
     cut = qkv_grad.shape[1] // D
     steps = cut + hidden_grad.shape[1] // D
+    before = lambda i: (0, jnp.minimum(i, cut - 1))
+    after = lambda i: (0, jnp.maximum(i - cut, 0))
     return block_call(
         functools.partial(input_grad_kernel, cut=cut),
         steps,
         [
             fixed(rows, D),
             fixed(rows, D),
-            pl.BlockSpec((rows, D), lambda i: (0, jnp.minimum(i, cut - 1))),
-            pl.BlockSpec((rows, D), lambda i: (0, jnp.maximum(i - cut, 0))),
+            pl.BlockSpec((rows, D), before),
+            pl.BlockSpec((rows, D), after),
         ],
-        pl.BlockSpec((D, D), lambda i: (0, i)),
-        shape_of(D, steps * D, dtype=jnp.bfloat16),
+        [pl.BlockSpec((D, D), before), pl.BlockSpec((D, D), after)],
+        [
+            shape_of(D, qkv_grad.shape[1], dtype=jnp.bfloat16),
+            shape_of(D, hidden_grad.shape[1], dtype=jnp.bfloat16),
+        ],
         [pltpu.VMEM((D, rows), jnp.bfloat16)],
         2 * rows * D * D * steps,
         2 * rows * D * (steps + 2) + 2 * D * D * steps,
@@ -1372,7 +1641,7 @@
     final_grad = jnp.dot(member, pooled_grad / image_sizes[:, None], precision=HIGHEST)
     stream_grad, final_gain, final_shift = final_back(final_grad)
     vector_grads = [None] * LAYERS
-    parts = [head_part]
+    early_parts, late_parts = [head_part], []
     for index in reversed(range(LAYERS)):
         (qkv_weight, up, output, vector), first, second = saved_layers[index]
         entering, normed, qkv_rows, attended, expo, inverse = first
@@ -1382,19 +1651,21 @@
         )
         output_grad = output_weight_grad(attended, active, residual_low, grad_low)
         attended_grad, output_grad = lax.optimization_barrier((attended_grad, output_grad))
-        beside_attention = []
+        output_grad = by_owner(output_grad)
+        half = -(-output_grad.shape[1] // 64) * 32
         if index:
-            parts.append(scatter(by_owner(output_grad)))
+            early_parts.append(scatter(output_grad[:, :half]))
+            early_parts.append(scatter(output_grad[:, half:]))
         else:
-            beside_attention.append(by_owner(output_grad))
-        qkv_grad, output_sums = attention_backward(
-            qkv_rows, expo, inverse, attended, attended_grad, beside_attention, 6
+            last_part = scatter(output_grad)
+        qkv_grad, early_sums = attention_backward(
+            qkv_rows, expo, inverse, attended, attended_grad, [] if index else early_parts, 6
         )
         stream_grad, qkv_sums = qkv_backward(qkv_grad, residual_grad, entering, qkv_weight, vector)
-        input_grad = input_weight_grad(normed, normed_second, qkv_grad, hidden_grad)
+        input_grads = input_weight_grad(normed, normed_second, qkv_grad, hidden_grad)
         if index:
-            stream_grad, input_grad = lax.optimization_barrier((stream_grad, input_grad))
-            parts.append(scatter(by_owner(input_grad)))
+            stream_grad, *input_grads = lax.optimization_barrier((stream_grad, *input_grads))
+            late_parts.extend(scatter(by_owner(grad)) for grad in input_grads)
         vector_grads[index] = jnp.concatenate(
             [
                 qkv_sums[0, : 2 * D],
@@ -1426,20 +1697,26 @@
     used = vector_rows + rest_rows
     block_rows = (used // 64 + 1) * 64
     small = jnp.pad(small.reshape(owners, used, LANES), ((0, 0), (0, block_rows - used), (0, 0)))
-    summed = reduce_all([by_owner(input_grad), by_owner(kernel_grad)], 2)
-    (output_zero_sum,) = output_sums
-    head_sum, output_one_sum, input_one_sum, small_share, small_full = finish_all(
-        [*summed, output_zero_sum], parts, small, 3
-    )
+    input_zero_sums, kernel_sum, input_one_sums = take(
+        reduce_all([by_owner(grad) for grad in (*input_grads, kernel_grad)], late_parts, 2), 2, 1, 2
+    )
+    output_zero_sum, small_share, small_full = finish_all(
+        [*early_sums, *input_zero_sums, *kernel_sum, *input_one_sums], [last_part], small, 3
+    )
+    head_sum, output_one_sums = early_sums[0], early_sums[1:]
     rest_sum = small_full[:, vector_rows:used].reshape(-1)
     position_sum = rest_sum[: position_grad.size].reshape(position_grad.shape)
     global_sum = rest_sum[position_grad.size :][: global_vector.shape[0]]
     loss_sum = rest_sum[rest.shape[0] - 2]
     token_total = rest_sum[rest.shape[0] - 1]
-    kernel_sum = summed[1].astype(jnp.float32)
+    kernel_sum = kernel_sum[0].astype(jnp.float32)
     head_sum = head_sum[:, :CLS].astype(jnp.float32)
-    input_sum = jnp.stack([summed[0], input_one_sum]).astype(jnp.float32)
-    output_sum = jnp.stack([output_zero_sum, output_one_sum]).astype(jnp.float32)
+    input_sum = jnp.stack(
+        [jnp.concatenate(pair, 1) for pair in (input_zero_sums, input_one_sums)]
+    ).astype(jnp.float32)
+    output_sum = jnp.stack([output_zero_sum, jnp.concatenate(output_one_sums, 0)]).astype(
+        jnp.float32
+    )
     vector_sum = small_share[:vector_rows].reshape(-1)[:vector_size].reshape(layer_vector.shape)
     grad_norm = (
         jnp.sqrt(

time: 780 us -> 720 us (0.923)
  Pallas kernels: 671 us -> 601 us
  local copies, waits for them, and re-layouts: 24.7 us -> 33.6 us
    pallas_call x2, Pallas kernels: 101 us -> 63 us  [attention_backward(): pl.pallas_call(functools.partial(attention_backward_kernel, block=block,...]
    pallas_call x1, Pallas kernels: 60.3 us -> 37.6 us  [finish_call(): pl.pallas_call(functools.partial(finish_kernel, done=done, partly=partly)...]
    pallas_call x2, Pallas kernels: 126 us -> 108 us  [attention_forward(): pl.pallas_call(functools.partial(attention_forward_kernel, block=block, f...]
  transfers between devices with their start and end apart: 7 -> 10, of which waited for: 0 -> 1; matrix products, arithmetic and copies ran while one was open for 4% -> 6% of each run, Pallas kernels for 79% -> 79%
where the time goes in v5:
time: 720 us; the launch traced here: 716 us
  Pallas kernels  601 us (83%)
  other arithmetic  47.2 us (7%)
  local copies, waits for them, and re-layouts  33.6 us (5%)
  between operations  21.3 us (3%)
  matrix products  9.51 us (1%)
    pallas_call x2, Pallas kernels, attention_forward(): pl.pallas_call(functools.partial(attention_forward_kernel, block=block, f...  108 us
    pallas_call x1, Pallas kernels, reduce_call(): pl.pallas_call(functools.partial(reduce_kernel, whole=whole, partly=partl...  108 us
    pallas_call x1, Pallas kernels, gather_call(): pl.pallas_call(functools.partial(gather_kernel, split=split), in_specs=[A...  63.7 us
    pallas_call x2, Pallas kernels, attention_backward(): pl.pallas_call(functools.partial(attention_backward_kernel, block=block,...  63 us
    pallas_call x2, Pallas kernels, mlp_forward(): block_call(mlp_kernel, rows // block, [rows_of(block, D), rows_of(block,...  50.1 us
    pallas_call x2, Pallas kernels, mlp_backward(): block_call(mlp_back_kernel, rows // block, [narrow, rows_of(block, width)...  49.5 us
    pallas_call x1, Pallas kernels, finish_call(): pl.pallas_call(functools.partial(finish_kernel, done=done, partly=partly)...  37.6 us
    pallas_call x2, Pallas kernels, input_weight_grad(): block_call(functools.partial(input_grad_kernel, cut=cut), steps, [fixed(r...  32.8 us
  transfers between devices with their start and end apart: 10, of which 1 were waited for; matrix products, arithmetic and copies ran while one was open for 6% of the time, Pallas kernels for 79%

profile of v5, /device:TPU:0, one launch (start us, length us, event | category | flops | bytes accessed | tf_op | source)
XLA Modules:
  0.0 715.6 jit_solution(987947119258815934)
XLA Ops:
  7.2 2.0 convert.15
  9.2 1.2 slice_bitcast_fusion
  10.5 2.4 convert.14
  12.9 1.0 fusion.54
  14.0 1.1 fusion.53
  15.2 1.7 convert_element_type.168
  18.4 0.9 convert_element_type.147.refs_0_
  23.2 63.7 %gather_weights.1 = (bf16[8,384,768]{2,1,0:T(8,128)(2,1)}, bf16[8,32,128]{2,1,0:T(8,128)(2,1)}, bf16[8,96,2304]{2,1,0:T(8,128)(2,1)}) custom-call(bf16[384,768]{1,0:T(8,128)(2,1)} %convert_element_type.147.refs_0_, bf16[32,128]{1,0:T(8,128)(2,1)} %pad_bitcast_fusion.refs_1_, bf16[96,2304]{1,0:T(8,128)(2,1)} %get-tuple-element.197.refs_2_), custom_call_target="tpu_custom_call" | custom-call | flops 16646144000 | bytes 8323072 | tf_op jit(solution)/shard_map/gather_weights/pallas_call | solution.py:249
  86.9 0.9 copy.65
  88.2 0.7 squeeze.47.vector_ref
  88.9 1.0 copy.57.refs_3_
  89.9 0.7 squeeze.48.vector_ref
  90.6 0.8 pad.31.clone.pos_ref
  91.4 12.1 %embed.1.stream_ref = f32[1024,768]{1,0:T(8,128)} custom-call(bf16[1024,3072]{1,0:T(8,128)(2,1)} %pixel_ref.3, bf16[3072,768]{1,0:T(8,128)(2,1)} %bitcast.113, f32[1024,64]{1,0:T(8,128)} %pad.31.clone.pos_ref, f32[64,768]{1,0:T(8,128)} %pad_convert_fusion.table_ref, f32[1,768]{1,0:T(1,128)} %broadcast_in_dim.85.bias_ref), custom_call_target="tpu_custom_call" | custom-call | flops 4831838208 | bytes 14155776 | tf_op jit(solution)/shard_map/embed/pallas_call | solution.py:1197
  103.5 9.1 %qkv_forward.2 = (bf16[1024,768]{1,0:T(8,128)(2,1)}, bf16[1024,2304]{1,0:T(8,128)(2,1)}) custom-call(f32[1024,768]{1,0:T(8,128)} %embed.1.stream_ref, bf16[768,2304]{1,0:T(8,128)(2,1)} %bitcast.85, f32[1,9984]{1,0:T(1,128)} %squeeze.47.vector_ref), custom_call_target="tpu_custom_call" | custom-call | flops 3623878656 | bytes 14548992 | tf_op jit(solution)/shard_map/qkv_forward/pallas_call | solution.py:1222
  112.6 56.6 %attention_forward.2 = (bf16[1024,768]{1,0:T(8,128)(2,1)}, bf16[12,1024,1024]{2,1,0:T(8,128)(2,1)}, f32[1024,768]{1,0:T(8,128)}, bf16[8,96,3072]{2,1,0:T(8,128)(2,1)}) custom-call(bf16[1024,2304]{1,0:T(8,128)(2,1)} %get-tuple-element.94.refs_0_.refs_1_.refs_2_, bf16[1024,2304]{1,0:T(8,128)(2,1)} %get-tuple-element.94.refs_0_.refs_1_.refs_2_, ...), custom_call_target="tpu_custom_call" | custom-call | flops 12884901888 | bytes 34603008 | tf_op jit(solution)/shard_map/attention_forward/pallas_call | solution.py:967
  169.2 25.1 %mlp_forward.2 = (f32[1024,768]{1,0:T(8,128)}, bf16[1024,768]{1,0:T(8,128)(2,1)}, bf16[1024,3072]{1,0:T(8,128)(2,1)}, bf16[1024,3072]{1,0:T(8,128)(2,1)}, f32[1024,768]{1,0:T(8,128)}) custom-call(f32[1024,768]{1,0:T(8,128)} %embed.1.stream_ref, bf16[1024,768]{1,0:T(8,128)(2,1)} %get-tuple-element.97.attended_ref.refs_5_, bf16[768,3072]{1,0:T(8,128)(2,1)} %bitcast.80, ...), custom_call_target="tpu_custom_call" | custom-call | flops 10871635968 | bytes 35782656 | tf_op jit(solution)/shard_map/mlp_forward/pallas_call | solution.py:1285
  194.4 9.0 %qkv_forward.3 = (bf16[1024,768]{1,0:T(8,128)(2,1)}, bf16[1024,2304]{1,0:T(8,128)(2,1)}) custom-call(f32[1024,768]{1,0:T(8,128)} %get-tuple-element.99.stream_ref, bf16[768,2304]{1,0:T(8,128)(2,1)} %bitcast.87, f32[1,9984]{1,0:T(1,128)} %squeeze.48.vector_ref), custom_call_target="tpu_custom_call" | custom-call | flops 3623878656 | bytes 14548992 | tf_op jit(solution)/shard_map/qkv_forward/pallas_call | solution.py:1222
  203.3 51.8 %attention_forward.3 = (bf16[1024,768]{1,0:T(8,128)(2,1)}, bf16[12,1024,1024]{2,1,0:T(8,128)(2,1)}, f32[1024,768]{1,0:T(8,128)}, bf16[8,480,768]{2,1,0:T(8,128)(2,1)}) custom-call(bf16[1024,2304]{1,0:T(8,128)(2,1)} %get-tuple-element.100.refs_0_.refs_1_.refs_2_, bf16[1024,2304]{1,0:T(8,128)(2,1)} %get-tuple-element.100.refs_0_.refs_1_.refs_2_, ...), custom_call_target="tpu_custom_call" | custom-call | flops 12884901888 | bytes 34603008 | tf_op jit(solution)/shard_map/attention_forward/pallas_call | solution.py:967
  255.2 25.0 %mlp_forward.3 = (f32[1024,768]{1,0:T(8,128)}, bf16[1024,768]{1,0:T(8,128)(2,1)}, bf16[1024,3072]{1,0:T(8,128)(2,1)}, bf16[1024,3072]{1,0:T(8,128)(2,1)}, f32[1024,768]{1,0:T(8,128)}) custom-call(f32[1024,768]{1,0:T(8,128)} %get-tuple-element.99.stream_ref, bf16[1024,768]{1,0:T(8,128)(2,1)} %get-tuple-element.103.attended_ref.refs_5_, ...), custom_call_target="tpu_custom_call" | custom-call | flops 10871635968 | bytes 35782656 | tf_op jit(solution)/shard_map/mlp_forward/pallas_call | solution.py:1285
  280.2 2.3 reduce_sum.181
  283.6 1.7 fusion.15
  285.2 1.8 fusion.58
  287.4 1.8 convolution_convert_fusion
  289.2 2.6 copy.61
  291.8 2.7 pad.34.clone
  295.0 1.9 convolution_divide_fusion
  296.9 2.3 multiply_reduce_fusion
  299.2 1.5 fusion.52
  300.7 1.9 broadcast_add_fusion.grad_ref
  302.6 24.8 %mlp_backward.2 = (bf16[1024,768]{1,0:T(8,128)(2,1)}, bf16[1024,3072]{1,0:T(8,128)(2,1)}, f32[1024,768]{1,0:T(8,128)}, bf16[1024,768]{1,0:T(8,128)(2,1)}, bf16[1024,768]{1,0:T(8,128)(2,1)}, /*index=5*/f32[1,6144]{1,0:T(1,128)}) custom-call(f32[1024,768]{1,0:T(8,128)} %broadcast_add_fusion.grad_ref, bf16[1024,3072]{1,0:T(8,128)(2,1)} %get-tuple-element.106.slope_ref, ...), custom_call_target="tpu_custom_call" | custom-call | tf_op jit(solution)/shard_map/mlp_backward/pallas_call | solution.py:1365
  327.4 12.0 %output_weight_grad.2 = bf16[3840,768]{1,0:T(8,128)(2,1)} custom-call(bf16[1024,768]{1,0:T(8,128)(2,1)} %get-tuple-element.103.attended_ref.refs_5_, bf16[1024,3072]{1,0:T(8,128)(2,1)} %get-tuple-element.109.active_ref, bf16[1024,768]{1,0:T(8,128)(2,1)} %get-tuple-element.110.residual_ref, bf16[1024,768]{1,0:T(8,128)(2,1)} %get-tuple-element.111.grad_ref), custom_call_target="tpu_custom_call" | custom-call | tf_op jit(solution)/shard_map/output_weight_grad/pallas_call | solution.py:1482
  339.4 3.5 slice.160
  342.9 3.8 slice.159
  347.0 28.8 %attention_backward.2.grad_ref.qkv_ref = bf16[1024,2304]{1,0:T(8,128)(2,1)} custom-call(bf16[1024,2304]{1,0:T(8,128)(2,1)} %get-tuple-element.100.refs_0_.refs_1_.refs_2_, bf16[1024,2304]{1,0:T(8,128)(2,1)} %get-tuple-element.100.refs_0_.refs_1_.refs_2_, bf16[1024,2304]{1,0:T(8,128)(2,1)} %get-tuple-element.100.refs_0_.refs_1_.refs_2_, ...), custom_call_target="tpu_custom_call" | custom-call | tf_op jit(solution)/shard_map/attention_backward/pallas_call | solution.py:1084
  375.8 10.5 %qkv_backward.2 = (f32[1024,768]{1,0:T(8,128)}, f32[1,3840]{1,0:T(1,128)}) custom-call(bf16[1024,2304]{1,0:T(8,128)(2,1)} %attention_backward.2.grad_ref.qkv_ref, f32[1024,768]{1,0:T(8,128)} %get-tuple-element.113.residual_ref, f32[1024,768]{1,0:T(8,128)} %get-tuple-element.99.stream_ref, bf16[768,2304]{1,0:T(8,128)(2,1)} %bitcast.88, ...), custom_call_target="tpu_custom_call" | custom-call | tf_op jit(solution)/shard_map/qkv_backward/pallas_call | solution.py:1403
  386.2 16.5 %input_weight_grad.2 = (bf16[768,2304]{1,0:T(8,128)(2,1)}, bf16[768,3072]{1,0:T(8,128)(2,1)}) custom-call(bf16[1024,768]{1,0:T(8,128)(2,1)} %get-tuple-element.115.first_ref, bf16[1024,768]{1,0:T(8,128)(2,1)} %get-tuple-element.116.second_ref, bf16[1024,2304]{1,0:T(8,128)(2,1)} %attention_backward.2.grad_ref.qkv_ref, ...), custom_call_target="tpu_custom_call" | custom-call | tf_op jit(solution)/shard_map/input_weight_grad/pallas_call | solution.py:1443
  403.7 24.8 %mlp_backward.3 = (bf16[1024,768]{1,0:T(8,128)(2,1)}, bf16[1024,3072]{1,0:T(8,128)(2,1)}, f32[1024,768]{1,0:T(8,128)}, bf16[1024,768]{1,0:T(8,128)(2,1)}, bf16[1024,768]{1,0:T(8,128)(2,1)}, /*index=5*/f32[1,6144]{1,0:T(1,128)}) custom-call(f32[1024,768]{1,0:T(8,128)} %get-tuple-element.120.grad_ref, bf16[1024,3072]{1,0:T(8,128)(2,1)} %get-tuple-element.121.slope_ref, ...), custom_call_target="tpu_custom_call" | custom-call | tf_op jit(solution)/shard_map/mlp_backward/pallas_call | solution.py:1365
  428.5 12.3 %output_weight_grad.3 = bf16[3840,768]{1,0:T(8,128)(2,1)} custom-call(bf16[1024,768]{1,0:T(8,128)(2,1)} %get-tuple-element.97.attended_ref.refs_5_, bf16[1024,3072]{1,0:T(8,128)(2,1)} %get-tuple-element.124.active_ref, bf16[1024,768]{1,0:T(8,128)(2,1)} %get-tuple-element.125.residual_ref, bf16[1024,768]{1,0:T(8,128)(2,1)} %get-tuple-element.126.grad_ref), custom_call_target="tpu_custom_call" | custom-call | tf_op jit(solution)/shard_map/output_weight_grad/pallas_call | solution.py:1482
  440.8 0.7 pad_bitcast_fusion.1.pos_ref
  442.6 34.3 %attention_backward.3 = (bf16[1024,2304]{1,0:T(8,128)(2,1)}, bf16[96,1024]{1,0:T(8,128)(2,1)}, bf16[256,768]{1,0:T(8,128)(2,1)}, bf16[224,768]{1,0:T(8,128)(2,1)}) custom-call(bf16[1024,2304]{1,0:T(8,128)(2,1)} %get-tuple-element.94.refs_0_.refs_1_.refs_2_, bf16[1024,2304]{1,0:T(8,128)(2,1)} %get-tuple-element.94.refs_0_.refs_1_.refs_2_, ...), custom_call_target="tpu_custom_call" | custom-call | tf_op jit(solution)/shard_map/attention_backward/pallas_call | solution.py:1084
  476.8 10.4 %qkv_backward.3 = (f32[1024,768]{1,0:T(8,128)}, f32[1,3840]{1,0:T(1,128)}) custom-call(bf16[1024,2304]{1,0:T(8,128)(2,1)} %get-tuple-element.134.qkv_ref.grad_ref, f32[1024,768]{1,0:T(8,128)} %get-tuple-element.138.residual_ref, f32[1024,768]{1,0:T(8,128)} %embed.1.stream_ref, bf16[768,2304]{1,0:T(8,128)(2,1)} %bitcast.86, f32[1,9984]{1,0:T(1,128)} %squeeze.47.vector_ref), custom_call_target="tpu_custom_call" | custom-call | tf_op jit(solution)/shard_map/qkv_backward/pallas_call | solution.py:1403
  487.3 0.7 slice_reduce_fusion.5
  488.0 0.7 slice_reduce_fusion.8
  489.0 12.3 %embed_backward.1 = (bf16[3072,768]{1,0:T(8,128)(2,1)}, f32[64,768]{1,0:T(8,128)}, f32[1,768]{1,0:T(1,128)}) custom-call(bf16[1024,3072]{1,0:T(8,128)(2,1)} %pixel_ref.3, f32[1024,768]{1,0:T(8,128)} %get-tuple-element.139.grad_ref, f32[64,1024]{1,0:T(8,128)} %pad_bitcast_fusion.1.pos_ref), custom_call_target="tpu_custom_call" | custom-call | tf_op jit(solution)/shard_map/embed_backward/pallas_call | solution.py:1519
  501.3 0.9 slice.135
  503.0 1.4 concatenate.24
  504.5 0.7 pad.37.refs_9_
  505.2 16.4 %input_weight_grad.3 = (bf16[768,2304]{1,0:T(8,128)(2,1)}, bf16[768,3072]{1,0:T(8,128)(2,1)}) custom-call(bf16[1024,768]{1,0:T(8,128)(2,1)} %get-tuple-element.132.first_ref, bf16[1024,768]{1,0:T(8,128)(2,1)} %get-tuple-element.133.second_ref, bf16[1024,2304]{1,0:T(8,128)(2,1)} %get-tuple-element.134.qkv_ref.grad_ref, ...), custom_call_target="tpu_custom_call" | custom-call | tf_op jit(solution)/shard_map/input_weight_grad/pallas_call | solution.py:1443
  521.6 0.9 maximum_bitcast_fusion.2
  522.5 1.0 reduce-scatter.15.cloned.1.call-done
  523.5 108.1 %reduce_gradients.1 = (bf16[96,2304]{1,0:T(8,128)(2,1)}, bf16[96,3072]{1,0:T(8,128)(2,1)}, bf16[384,768]{1,0:T(8,128)(2,1)}, bf16[96,2304]{1,0:T(8,128)(2,1)}, bf16[96,3072]{1,0:T(8,128)(2,1)}) custom-call(bf16[8,96,2304]{2,1,0:T(8,128)(2,1)} %bitcast.90, bf16[8,96,3072]{2,1,0:T(8,128)(2,1)} %bitcast.84, bf16[8,384,768]{2,1,0:T(8,128)(2,1)} %bitcast.83, ...), custom_call_target="tpu_custom_call" | custom-call | tf_op jit(solution)/shard_map/reduce_gradients/pallas_call | solution.py:800
  631.7 1.6 maximum_bitcast_fusion
  633.4 37.6 %finish_gradients.1 = (bf16[480,768]{1,0:T(8,128)(2,1)}, f32[64,128]{1,0:T(8,128)}, f32[8,64,128]{2,1,0:T(8,128)}) custom-call(bf16[96,1024]{1,0:T(8,128)(2,1)} %get-tuple-element.129.refs_0_, bf16[256,768]{1,0:T(8,128)(2,1)} %get-tuple-element.130.refs_1_, bf16[224,768]{1,0:T(8,128)(2,1)} %get-tuple-element.131.refs_2_, ...), custom_call_target="tpu_custom_call" | custom-call | tf_op jit(solution)/shard_map/finish_gradients/pallas_call | solution.py:853
  671.0 0.9 slice.136
  671.9 1.4 slice_reduce_fusion.10
  673.3 1.5 multiply_reduce_fusion.4
  681.3 0.7 slice_bitcast_fusion.3
  682.8 1.6 mul.371
  684.6 4.5 multiply_subtract_fusion.2
  689.0 3.0 multiply_subtract_fusion.3
  693.3 0.9 multiply_subtract_fusion.4
  694.2 8.3 %multiply_subtract_fusion = (f32[2,96,5376]{2,1,0:T(8,128)}, f32[2,96,5376]{2,1,0:T(8,128)}, f32[2,96,5376]{2,1,0:T(8,128)}) fusion(f32[2,96,5376]{2,1,0:T(8,128)S(1)} %copy-done.1, f32[]{:T(128)S(6)} %div.163, bf16[1,96,5376]{2,1,0:T(8,128)(2,1)S(1)} %get-tuple-element.215, bf16[1,96,5376]{2,1,0:T(8,128)(2,1)S(1)} %get-tuple-element.214, ...), kind=kLoop, calls=%fused_computation.6 | loop fusion | flops 17547264 | bytes 26836996 | tf_op jit(solution)/shard_map/sub | solution.py:1542
  702.5 4.6 multiply_subtract_fusion.1
  (161 shorter events, 15.2 us)
Async XLA Ops:
  7.2 162.0 %all-gather.10.cloned.1.call-start = ((), (), s32[]{:S(2)}) async-start(), calls=%async_computation.13 | async-start | bytes 6635520 | tf_op jit(solution)/shard_map/all_gather | solution.py:1594
  10.4 183.9 %all-gather.12.cloned.1.call-start = ((), (), s32[]{:S(2)}) async-start(), calls=%async_computation.14 | async-start | bytes 3981312 | tf_op jit(solution)/shard_map/all_gather | solution.py:1594
  12.9 4.1 copy-start.17
  12.9 4.2 copy-start.19
  12.9 5.5 copy-start.3
  13.9 5.4 copy-start.21
  13.9 7.3 %copy-start.37 = (s32[1,8]{1,0:T(1,128)S(1)}, s32[1,8]{1,0:T(1,128)}, u32[]{:S(2)}) copy-start(s32[1,8]{1,0:T(1,128)} %param.27) | copy-start | bytes 100
  13.9 8.0 %copy-start.12 = (f32[49,768]{1,0:T(8,128)S(1)}, f32[49,768]{1,0:T(8,128)}, u32[]{:S(2)}) copy-start(f32[49,768]{1,0:T(8,128)} %param.34) | copy-start | bytes 451588
  13.9 241.2 %all-gather.14.cloned.1.call-start = ((), (), s32[]{:S(2)}) async-start(), calls=%async_computation.15 | async-start | bytes 5308416 | tf_op jit(solution)/shard_map/all_gather | solution.py:1594
  15.1 270.1 %all-gather.8.cloned.1.call-start = ((), (), s32[]{:S(2)}) async-start(), calls=%async_computation.6 | async-start | bytes 1769472 | tf_op jit(solution)/shard_map/all_gather | solution.py:1594
  16.9 425.6 %reduce-scatter.7.cloned.1.call-start = ((), (), s32[]{:S(2)}) async-start(), calls=%async_computation.7 | async-start | bytes 1769472 | tf_op jit(solution)/shard_map/reduce_scatter | solution.py:905
  17.1 4.5 copy-start.32
  280.2 2.8 copy-start
  280.2 3.4 copy-start.18
  280.2 3.3 copy-start.26
  280.2 3.3 copy-start.36
  283.0 2.2 copy-start.25
  283.5 3.6 copy-start.34
  283.5 3.8 copy-start.35
  294.5 148.0 %reduce-scatter.11.cloned.1.call-start = ((), (), s32[]{:S(2)}) async-start(), calls=%async_computation.9 | async-start | bytes 3096576 | tf_op jit(solution)/shard_map/reduce_scatter | solution.py:905
  342.9 99.7 %reduce-scatter.9.cloned.1.call-start = ((), (), s32[]{:S(2)}) async-start(), calls=%async_computation.8 | async-start | bytes 3538944 | tf_op jit(solution)/shard_map/reduce_scatter | solution.py:905
  346.8 175.7 %reduce-scatter.13.cloned.1.call-start = ((), (), s32[]{:S(2)}) async-start(), calls=%async_computation.10 | async-start | bytes 3981312 | tf_op jit(solution)/shard_map/reduce_scatter | solution.py:905
  402.7 120.8 %reduce-scatter.15.cloned.1.call-start = ((), (), s32[]{:S(2)}) async-start(), calls=%async_computation.11 | async-start | bytes 5308416 | tf_op jit(solution)/shard_map/reduce_scatter | solution.py:905
  403.5 229.9 %reduce-scatter.17.cloned.1.call-start = ((), (), s32[]{:S(2)}) async-start(), calls=%async_computation.12 | async-start | bytes 6635520 | tf_op jit(solution)/shard_map/reduce_scatter | solution.py:905
  440.8 0.8 copy-start.29
  440.8 0.8 copy-start.23
  440.8 1.0 copy-start.33
  440.8 1.7 copy-start.24
  505.2 16.4 %copy-start.9 = (bf16[256,768]{1,0:T(8,128)(2,1)S(1)}, bf16[256,768]{1,0:T(8,128)(2,1)}, u32[]{:S(2)}) copy-start(bf16[256,768]{1,0:T(8,128)(2,1)} %get-tuple-element.130.refs_1_) | copy-start | bytes 1179652
  505.2 16.4 %copy-start.10 = (bf16[224,768]{1,0:T(8,128)(2,1)S(1)}, bf16[224,768]{1,0:T(8,128)(2,1)}, u32[]{:S(2)}) copy-start(bf16[224,768]{1,0:T(8,128)(2,1)} %get-tuple-element.131.refs_2_) | copy-start | bytes 1032196
  633.3 51.1 %copy-start.4 = (f32[384,768]{1,0:T(8,128)S(1)}, f32[384,768]{1,0:T(8,128)}, u32[]{:S(2)}) copy-start(f32[384,768]{1,0:T(8,128)} %param.29) | copy-start | bytes 3538948
  684.4 7.5 %copy-start.20 = (f32[3304]{0:T(1024)S(1)}, f32[3304]{0:T(1024)}, u32[]{:S(2)}) copy-start(f32[3304]{0:T(1024)} %param.35) | copy-start | bytes 39652
  684.4 7.5 %copy-start.27 = (f32[3304]{0:T(1024)S(1)}, f32[3304]{0:T(1024)}, u32[]{:S(2)}) copy-start(f32[3304]{0:T(1024)} %param.49) | copy-start | bytes 39652
  684.4 7.5 %copy-start.28 = (f32[3304]{0:T(1024)S(1)}, f32[3304]{0:T(1024)}, u32[]{:S(2)}) copy-start(f32[3304]{0:T(1024)} %param.42) | copy-start | bytes 39652
  684.4 8.2 %copy-start.22 = (f32[2,1248]{1,0:T(2,128)S(1)}, f32[2,1248]{1,0:T(2,128)}, u32[]{:S(2)}) copy-start(f32[2,1248]{1,0:T(2,128)} %param.33) | copy-start | bytes 29956
  684.5 8.2 %copy-start.30 = (f32[2,1248]{1,0:T(2,128)S(1)}, f32[2,1248]{1,0:T(2,128)}, u32[]{:S(2)}) copy-start(f32[2,1248]{1,0:T(2,128)} %param.47) | copy-start | bytes 29956
  684.5 8.2 %copy-start.31 = (f32[2,1248]{1,0:T(2,128)S(1)}, f32[2,1248]{1,0:T(2,128)}, u32[]{:S(2)}) copy-start(f32[2,1248]{1,0:T(2,128)} %param.40) | copy-start | bytes 29956
  684.5 8.8 %copy-start.13 = (f32[49,768]{1,0:T(8,128)S(1)}, f32[49,768]{1,0:T(8,128)}, u32[]{:S(2)}) copy-start(f32[49,768]{1,0:T(8,128)} %param.34) | copy-start | bytes 451588
  684.5 8.8 %copy-start.14 = (f32[49,768]{1,0:T(8,128)S(1)}, f32[49,768]{1,0:T(8,128)}, u32[]{:S(2)}) copy-start(f32[49,768]{1,0:T(8,128)} %mul.371) | copy-start | bytes 451588
  684.5 8.8 %copy-start.15 = (f32[49,768]{1,0:T(8,128)S(1)}, f32[49,768]{1,0:T(8,128)}, u32[]{:S(2)}) copy-start(f32[49,768]{1,0:T(8,128)} %param.48) | copy-start | bytes 451588
  684.5 8.8 %copy-start.16 = (f32[49,768]{1,0:T(8,128)S(1)}, f32[49,768]{1,0:T(8,128)}, u32[]{:S(2)}) copy-start(f32[49,768]{1,0:T(8,128)} %param.41) | copy-start | bytes 451588
  684.5 9.6 %copy-start.1 = (f32[2,96,5376]{2,1,0:T(8,128)S(1)}, f32[2,96,5376]{2,1,0:T(8,128)}, u32[]{:S(2)}) copy-start(f32[2,96,5376]{2,1,0:T(8,128)} %param.31) | copy-start | bytes 12386308
  684.5 9.6 %copy-start.5 = (f32[2,96,5376]{2,1,0:T(8,128)S(1)}, f32[2,96,5376]{2,1,0:T(8,128)}, u32[]{:S(2)}) copy-start(f32[2,96,5376]{2,1,0:T(8,128)} %param.45) | copy-start | bytes 12386308
  694.2 8.3 %copy-start.2 = (f32[2,480,768]{2,1,0:T(8,128)S(1)}, f32[2,480,768]{2,1,0:T(8,128)}, u32[]{:S(2)}) copy-start(f32[2,480,768]{2,1,0:T(8,128)} %param.32) | copy-start | bytes 8847364
  694.2 8.3 %copy-start.6 = (f32[2,480,768]{2,1,0:T(8,128)S(1)}, f32[2,480,768]{2,1,0:T(8,128)}, u32[]{:S(2)}) copy-start(f32[2,480,768]{2,1,0:T(8,128)} %param.46) | copy-start | bytes 8847364
  694.2 8.3 %copy-start.7 = (f32[2,480,768]{2,1,0:T(8,128)S(1)}, f32[2,480,768]{2,1,0:T(8,128)}, u32[]{:S(2)}) copy-start(f32[2,480,768]{2,1,0:T(8,128)} %param.39) | copy-start | bytes 8847364
  694.2 8.3 %copy-start.8 = (bf16[1,480,768]{2,1,0:T(8,128)(2,1)S(1)}, bf16[1,480,768]{2,1,0:T(8,128)(2,1)}, u32[]{:S(2)}) copy-start(bf16[1,480,768]{2,1,0:T(8,128)(2,1)} %maximum_bitcast_fusion.2) | copy-start | bytes 2211844
  694.2 8.3 %copy-start.11 = (bf16[480,768]{1,0:T(8,128)(2,1)S(1)}, bf16[480,768]{1,0:T(8,128)(2,1)}, u32[]{:S(2)}) copy-start(bf16[480,768]{1,0:T(8,128)(2,1)} %get-tuple-element.156) | copy-start | bytes 2211844
Sparse Core Ops, SparseCore 0:
  10.6 86.6 all-gather.9
  98.9 52.7 all-gather.11
  153.9 50.4 all-gather.13
  206.5 32.3 all-gather.7
  294.6 33.0 reduce-scatter.6
  343.0 36.8 reduce-scatter.10
  382.3 39.4 reduce-scatter.8
  424.8 42.8 reduce-scatter.12
  470.0 53.4 reduce-scatter.14
  525.7 73.8 reduce-scatter.16

commit v6 on v5

--- a/solution.py
+++ b/solution.py
@@ -30,7 +30,8 @@
 
 PAIR = 2 * HD
 MASKED = -1e30
-VMEM_LIMIT = 56 * 1024 * 1024
+MIB = 1024 * 1024
+VMEM_LIMIT = 56 * MIB
 MESH = pl.DeviceIdType.MESH
 LANES = 128
 LOW = jnp.bfloat16
@@ -219,46 +220,349 @@
         self.own_copy().wait()
 
 
-def beside(jobs, plan):
-    for step, stages in plan.items():
-
-        @pl.when(pl.program_id(0) == step)
-        def _(stages=stages):
-            for stage in stages:
-                if stage == "greet":
-                    greet()
-                else:
-                    run_stages(jobs, (stage,))
-
-
-def gather_kernel(*refs, split):
-    count = len(split)
-    sems = refs[2 * count]
+class LevelGather:
+    def __init__(self, shard, out, sems):
+        self.shard, self.out, self.sems = shard, out, sems
+
+    def level_copy(self, turn):
+        group, level, core = place()
+        return remote(
+            self.shard.at[quarter(group, *self.shard.shape)],
+            self.out.at[level],
+            self.sems.at[turn],
+            self.sems.at[3 + turn],
+            (group, 2 * partner(level, turn) + core),
+        )
+
+    def first(self):
+        for turn in TURNS:
+            self.level_copy(turn).start()
+
+    def second(self):
+        pass
+
+    def third(self):
+        pass
+
+    def fourth(self):
+        for turn in TURNS:
+            self.level_copy(turn).wait_recv()
+            self.level_copy(turn).wait_send()
+
+
+GROUP_GATHER_SEMS = 30
+
+
+class GroupGather:
+    def __init__(self, shard, quarters, out, sems):
+        self.shard, self.quarters, self.out, self.sems = shard, quarters, out, sems
+
+    def part(self, turn):
+        group, level, core = place()
+        block = self.out.at[2 * partner(level, turn) + core]
+        return block.at[quarter(group, *self.shard.shape)]
+
+    def own_copy(self, turn):
+        _, level, core = place()
+        if turn == 0:
+            source, target = self.shard, self.out.at[2 * level + core]
+        else:
+            source, target = self.quarters.at[partner(level, turn)], self.part(turn)
+        return pltpu.make_async_copy(source, target, self.sems.at[turn])
+
+    def group_copy(self, turn, other):
+        group, level, core = place()
+        index = 3 * (turn - 1) + other - 1
+        return remote(
+            self.quarters.at[partner(level, turn)],
+            self.part(turn),
+            self.sems.at[4 + index],
+            self.sems.at[13 + index],
+            (partner(group, other), 2 * level + core),
+        )
+
+    def core_copy(self, turn):
+        group, level, core = place()
+        slot = 2 * partner(level, turn) + core
+        source = self.shard if turn == 0 else self.out.at[slot]
+        peer = (group, 2 * level + 1 - core)
+        return remote(source, self.out.at[slot], self.sems.at[22 + turn], self.sems.at[26 + turn], peer)
+
+    def first(self):
+        for turn in TURNS:
+            for other in TURNS:
+                self.group_copy(turn, other).start()
+        for turn in (0, *TURNS):
+            self.own_copy(turn).start()
+        self.core_copy(0).start()
+
+    def second(self):
+        for turn in TURNS:
+            for other in TURNS:
+                self.group_copy(turn, other).wait_recv()
+            self.own_copy(turn).wait()
+            self.core_copy(turn).start()
+
+    def third(self):
+        for turn in (0, *TURNS):
+            self.core_copy(turn).wait_recv()
+            self.core_copy(turn).wait_send()
+        for turn in TURNS:
+            for other in TURNS:
+                self.group_copy(turn, other).wait_send()
+        self.own_copy(0).wait()
+
+
+class GatherRide:
+    def __init__(self, shard, quarters):
+        owners = lax.axis_size("fsdp")
+        self.operands = [shard, quarters]
+        self.out_specs = [ANYWHERE]
+        self.out_shapes = [jax.ShapeDtypeStruct((owners, *shard.shape), shard.dtype)]
+        self.scratch = [pltpu.SemaphoreType.DMA((GROUP_GATHER_SEMS,))]
+
+    def job(self, sources, targets, scratch):
+        return GroupGather(*sources, *targets, *scratch)
+
+    def before(self, steps):
+        return {0: ("first",), max(1, 2 * steps // 3): ("second",)}
+
+    after = ("third",)
+
+    def result(self, outs):
+        return outs[0].reshape(-1, outs[0].shape[2])
+
+    def plain(self):
+        return lax.all_gather(self.operands[0], "fsdp", axis=0, tiled=True)
+
+
+class ShareRide:
+    def __init__(self, share):
+        self.operands = [share]
+        self.out_specs = [fixed(*share.shape)]
+        self.out_shapes = [jax.ShapeDtypeStruct(share.shape, share.dtype)]
+        self.scratch = [
+            pltpu.VMEM(share.shape, share.dtype),
+            *share_scratch(share),
+            pltpu.SemaphoreType.DMA((GROUP_SEMS,)),
+        ]
+
+    def job(self, sources, targets, scratch):
+        job = GroupReduce(sources[0], scratch[0], scratch[1:3], scratch[3])
+        job.target = targets[0]
+        return job
+
+    def before(self, steps):
+        return {0: ("first", "second"), max(1, steps // 2): ("third",)}
+
+    after = ("fifth", "sixth", "store")
+
+    def result(self, outs):
+        return outs[0]
+
+    def plain(self):
+        return lax.psum(self.operands[0], "dp")
+
+
+def riding(body, counts, rides, steps):
+    def kernel(*refs):
+        refs = list(refs)
+
+        def pop(count):
+            taken = refs[:count]
+            del refs[:count]
+            return taken
+
+        own = pop(counts[0])
+        sources = [pop(len(ride.operands)) for ride in rides]
+        own += pop(counts[1])
+        targets = [pop(len(ride.out_shapes)) for ride in rides]
+        own += pop(counts[2])
+        jobs = [
+            ride.job(source, target, pop(len(ride.scratch)))
+            for ride, source, target in zip(rides, sources, targets)
+        ]
+        for step in range(steps):
+            planned = [
+                (job, stages)
+                for ride, job in zip(rides, jobs)
+                for at, stages in ride.before(steps).items()
+                if at == step
+            ]
+            if planned:
+
+                @pl.when(pl.program_id(0) == step)
+                def _(planned=planned, step=step):
+                    if step == 0:
+                        greet()
+                    for job, stages in planned:
+                        run_stages([job], stages)
+
+        body(*own)
+
+        @pl.when(pl.program_id(0) == steps - 1)
+        def _():
+            for ride, job in zip(rides, jobs):
+                run_stages([job], ride.after)
+
+    return kernel
+
+
+def block_call(
+    body, grid, in_specs, operands, out_specs, out_shape, scratch, room, name,
+    cost=None, rides=(), collective_id=None,
+):
+    plain = []
+    if rides and not with_kernels():
+        plain, rides = [ride.plain() for ride in rides], ()
+    transfer = {}
+    kernel = body
+    if rides:
+        transfer = {"collective_id": collective_id, "has_side_effects": True}
+        kernel = riding(body, (len(operands), len(out_shape), len(scratch)), rides, grid)
+    count = len(out_shape)
+    for ride in rides:
+        operands, in_specs = [*operands, *ride.operands], [*in_specs, *[ANYWHERE] * len(ride.operands)]
+        out_specs, out_shape = [*out_specs, *ride.out_specs], [*out_shape, *ride.out_shapes]
+        scratch = [*scratch, *ride.scratch]
+    outs = pl.pallas_call(
+        kernel,
+        grid=(grid,),
+        in_specs=in_specs,
+        out_specs=out_specs,
+        out_shape=out_shape,
+        scratch_shapes=scratch,
+        compiler_params=pltpu.CompilerParams(vmem_limit_bytes=room * MIB, **transfer),
+        cost_estimate=cost or NO_COST,
+        name=name,
+    )(*operands)
+    brought, outs = list(outs[count:]), list(outs[:count])
+    for ride in rides:
+        plain.append(ride.result(brought[: len(ride.out_shapes)]))
+        brought = brought[len(ride.out_shapes) :]
+    return outs + plain
+
+
+def work(flops, size):
+    return pl.CostEstimate(flops=flops, bytes_accessed=size, transcendentals=0)
+
+
+def gather_kernel(*refs):
+    kernel, vectors, inputs, outputs, head = refs[:5]
+    kernel_full, vectors_full, qkv_full, up_level, qkv_level, output_level = refs[5:11]
+    up_zero, output_zero, qkv_one, up_one, output_one, head_low = refs[11:17]
+    wide_kernel, wide_inputs, wide_outputs, wide_head, kernel_low, qkv_zero = refs[17:23]
+    load_sems, sems = refs[23:]
+    pairs = [
+        (kernel, wide_kernel),
+        (inputs.at[0], wide_inputs.at[0]),
+        (outputs.at[1], wide_outputs.at[1]),
+        (inputs.at[1], wide_inputs.at[1]),
+        (outputs.at[0], wide_outputs.at[0]),
+        (head, wide_head),
+    ]
+    copies = [
+        pltpu.make_async_copy(source, target, load_sems.at[index])
+        for index, (source, target) in enumerate(pairs)
+    ]
+    for copy in copies:
+        copy.start()
     jobs = [
-        Gather(refs[i], refs[count + i], sems.at[i], split[i]) for i in range(count)
+        Gather(kernel_low, kernel_full, sems.at[0], True),
+        Gather(vectors, vectors_full, sems.at[1], False),
+        Gather(qkv_zero, qkv_full, sems.at[2], True),
+        LevelGather(up_zero, up_level, sems.at[3]),
+        LevelGather(qkv_one, qkv_level, sems.at[4]),
+        LevelGather(output_one, output_level, sems.at[5]),
     ]
     greet()
-    for stage in ("first", "second", "third", "fourth"):
-        for job in jobs:
-            getattr(job, stage)()
-
-
-def gather_call(shards, split, collective_id):
-    count = len(shards)
+    jobs[1].first()
+    copies[0].wait()
+    kernel_low[...] = wide_kernel[...].astype(LOW)
+    jobs[0].first()
+    copies[1].wait()
+    qkv_zero[...] = wide_inputs[0, :, : 3 * D].astype(LOW)
+    jobs[2].first()
+    up_zero[...] = wide_inputs[0, :, 3 * D :].astype(LOW)
+    jobs[3].first()
+    copies[3].wait()
+    qkv_one[...] = wide_inputs[1, :, : 3 * D].astype(LOW)
+    jobs[4].first()
+    copies[2].wait()
+    output_one[...] = wide_outputs[1].astype(LOW)
+    jobs[5].first()
+    run_stages(jobs[:3], ("second",))
+    up_one[...] = wide_inputs[1, :, 3 * D :].astype(LOW)
+    copies[4].wait()
+    output_zero[...] = wide_outputs[0].astype(LOW)
+    copies[5].wait()
+    head_low[...] = wide_head[...].astype(LOW)
+    run_stages(jobs[:3], ("third",))
+    run_stages(jobs, ("fourth",))
+
+
+def gather_first(patch_kernel, vectors, input_proj, output_proj, head_weight):
+    if not with_kernels():
+        inputs = [
+            (input_proj[index, :, : 3 * D].astype(LOW), input_proj[index, :, 3 * D :].astype(LOW))
+            for index in range(LAYERS)
+        ]
+        outputs = [output_proj[index].astype(LOW) for index in range(LAYERS)]
+        whole = [patch_kernel.astype(LOW), vectors, inputs[0][0]]
+        return (
+            [lax.all_gather(shard, "fsdp", axis=0, tiled=True) for shard in whole],
+            [GatherRide(shard, shard) for shard in (inputs[0][1], inputs[1][0], outputs[1])],
+            [outputs[0], inputs[1][1], head_weight.astype(LOW)],
+        )
     owners = lax.axis_size("fsdp")
-    full = pl.pallas_call(
-        functools.partial(gather_kernel, split=split),
-        in_specs=[ANYWHERE] * count,
-        out_specs=[ANYWHERE] * count,
-        out_shape=[jax.ShapeDtypeStruct((owners, *s.shape), s.dtype) for s in shards],
-        scratch_shapes=[pltpu.SemaphoreType.DMA((count, GATHER_SEMS))],
-        cost_estimate=transfer_cost(sum(shard.size for shard in shards) * owners),
+    depth = input_proj.shape[1]
+    up_shape = (depth, input_proj.shape[2] - 3 * D)
+    qkv_shape, out_shape = (depth, 3 * D), output_proj.shape[1:]
+    low = lambda *shape: jax.ShapeDtypeStruct(shape, LOW)
+    levels = lambda shape: low(4, *quarter_shape(*shape))
+    shapes = [
+        low(owners, *patch_kernel.shape),
+        low(owners, *vectors.shape),
+        low(owners, *qkv_shape),
+        levels(up_shape),
+        levels(qkv_shape),
+        levels(out_shape),
+        low(*up_shape),
+        low(*out_shape),
+        low(*qkv_shape),
+        low(*up_shape),
+        low(*out_shape),
+        low(*head_weight.shape),
+    ]
+    wide = (patch_kernel, input_proj, output_proj, head_weight)
+    results = pl.pallas_call(
+        gather_kernel,
+        in_specs=[ANYWHERE] * 5,
+        out_specs=[ANYWHERE] * 6 + [pl.BlockSpec(memory_space=pltpu.VMEM)] * 6,
+        out_shape=shapes,
+        scratch_shapes=[
+            *[pltpu.VMEM(array.shape, array.dtype) for array in wide],
+            pltpu.VMEM(patch_kernel.shape, LOW),
+            pltpu.VMEM(qkv_shape, LOW),
+            pltpu.SemaphoreType.DMA((6,)),
+            pltpu.SemaphoreType.DMA((6, GATHER_SEMS)),
+        ],
         compiler_params=pltpu.CompilerParams(
-            collective_id=collective_id, has_side_effects=True, vmem_limit_bytes=VMEM_LIMIT
+            collective_id=1, has_side_effects=True, vmem_limit_bytes=32 * MIB
         ),
+        cost_estimate=NO_COST,
         name="gather_weights",
-    )(*shards)
-    return [f.reshape(owners * f.shape[1], f.shape[2]) for f in full]
+    )(patch_kernel, vectors, input_proj, output_proj, head_weight)
+    up_zero, output_zero, qkv_one, up_one, output_one, head_low = results[6:]
+    return (
+        [full.reshape(owners * full.shape[1], full.shape[2]) for full in results[:3]],
+        [
+            GatherRide(up_zero, results[3]),
+            GatherRide(qkv_one, results[4]),
+            GatherRide(output_one, results[5]),
+        ],
+        [output_zero, up_one, head_low],
+    )
 
 
 REDUCE_SEMS = 48
@@ -671,6 +975,9 @@
     def fifth(self):
         for other in TURNS:
             self.share_copy(other).wait_recv()
+
+    def store(self):
+        self.target[...] = self.out[...]
 
     def sixth(self):
         for other in TURNS:
@@ -867,12 +1174,6 @@
     return lax.axis_size("dp") == 4 and lax.axis_size("fsdp") == 8
 
 
-def gather_all(shards, split, collective_id):
-    if with_kernels():
-        return gather_call(shards, split, collective_id)
-    return [lax.all_gather(shard, "fsdp", axis=0, tiled=True) for shard in shards]
-
-
 def reduce_all(grads, shares, collective_id):
     if with_kernels():
         return reduce_call(grads, shares, collective_id)
@@ -910,14 +1211,9 @@
     return grad.astype(low).reshape(owners, grad.shape[0] // owners, grad.shape[1])
 
 
-def attention_forward_kernel(*refs, block, fetched):
-    q_ref, k_ref, v_ref, seg_col_ref, seg_row_ref = refs[:5]
-    shards, refs = refs[5 : 5 + fetched], refs[5 + fetched :]
-    out_ref, expo_ref, inv_ref = refs[:3]
-    fulls, refs = refs[3 : 3 + fetched], refs[3 + fetched :]
-    jobs = [Gather(shards[i], fulls[i], refs[0].at[i], True) for i in range(fetched)]
-    if jobs:
-        beside(jobs, {0: ("greet", "first"), 1: ("second",), 3: ("third",)})
+def attention_forward_kernel(
+    q_ref, k_ref, v_ref, seg_col_ref, seg_row_ref, out_ref, expo_ref, inv_ref, *, block
+):
     rows = q_ref.shape[0]
     lower = lax.broadcasted_iota(jnp.int32, (block, PAIR), 1) < HD
     keys = k_ref[...]
@@ -947,69 +1243,35 @@
             inv_ref[at, :] = inverse
             outs = []
         scores = following
-    if jobs:
-        beside(jobs, {pl.num_programs(0) - 1: ("fourth",)})
-
-
-def attention_forward(qkv_rows, segment, shards, collective_id):
-    gathered = []
-    if not with_kernels():
-        gathered, shards = gather_all(shards, (True,) * len(shards), collective_id), []
+
+
+def attention_forward(qkv_rows, segment, rides, collective_id):
     rows = qkv_rows.shape[0]
-    fetched = len(shards)
-    owners = lax.axis_size("fsdp")
-    transfer = {}
-    if fetched:
-        transfer = {"collective_id": collective_id, "has_side_effects": True}
     pairs = HEADS // 2
-    block = min(256, rows)
     wide = lambda base: pl.BlockSpec((rows, PAIR), lambda j, base=base: (0, base + j))
-    attended, expo, inverse, *full = pl.pallas_call(
-        functools.partial(attention_forward_kernel, block=block, fetched=fetched),
-        grid=(pairs,),
-        in_specs=[
-            wide(0),
-            wide(pairs),
-            wide(2 * pairs),
-            pl.BlockSpec((rows, 1), lambda j: (0, 0)),
-            pl.BlockSpec((1, rows), lambda j: (0, 0)),
-            *[ANYWHERE] * fetched,
+    return block_call(
+        functools.partial(attention_forward_kernel, block=min(256, rows)),
+        pairs,
+        [wide(0), wide(pairs), wide(2 * pairs), fixed(rows, 1), fixed(1, rows)],
+        [qkv_rows, qkv_rows, qkv_rows, segment[:, None], segment[None, :]],
+        [wide(0), pl.BlockSpec((2, rows, rows), lambda j: (j, 0, 0)), wide(0)],
+        [
+            shape_of(rows, D, dtype=LOW),
+            shape_of(HEADS, rows, rows, dtype=LOW),
+            shape_of(rows, D),
         ],
-        out_specs=[
-            wide(0),
-            pl.BlockSpec((2, rows, rows), lambda j: (j, 0, 0)),
-            wide(0),
-            *[ANYWHERE] * fetched,
-        ],
-        out_shape=[
-            jax.ShapeDtypeStruct((rows, D), jnp.bfloat16),
-            jax.ShapeDtypeStruct((HEADS, rows, rows), jnp.bfloat16),
-            jax.ShapeDtypeStruct((rows, D), jnp.float32),
-            *[jax.ShapeDtypeStruct((owners, *s.shape), s.dtype) for s in shards],
-        ],
-        scratch_shapes=[pltpu.SemaphoreType.DMA((fetched, GATHER_SEMS))] * (fetched > 0),
-        compiler_params=pltpu.CompilerParams(vmem_limit_bytes=VMEM_LIMIT, **transfer),
-        cost_estimate=pl.CostEstimate(
-            flops=4 * HEADS * rows * rows * HD * 4,
-            bytes_accessed=2 * HEADS * rows * rows + 12 * rows * D,
-            transcendentals=HEADS * rows * rows,
-        ),
-        name="attention_forward",
-    )(qkv_rows, qkv_rows, qkv_rows, segment[:, None], segment[None, :], *shards)
-    gathered += [f.reshape(owners * f.shape[1], f.shape[2]) for f in full]
-    return attended, expo, inverse, gathered
-
-
-def attention_backward_kernel(*refs, block, reduced):
-    q_ref, k_ref, v_ref, expo_ref, inv_ref, out_ref, grad_ref = refs[:7]
-    sources, refs = refs[7 : 7 + reduced], refs[7 + reduced :]
-    dqkv_ref, sums, refs = refs[0], refs[1 : 1 + reduced], refs[1 + reduced :]
-    jobs = [
-        GroupReduce(sources[i], refs[3 * i + 1], refs[3 * i + 2 : 3 * i + 4], refs[0].at[i])
-        for i in range(reduced)
-    ]
-    if jobs:
-        beside(jobs, {0: ("greet", "first", "second"), 3: ("third",)})
+        [],
+        26,
+        "attention_forward",
+        work(16 * HEADS * rows * rows * HD, 2 * HEADS * rows * rows + 12 * rows * D),
+        rides,
+        collective_id,
+    )
+
+
+def attention_backward_kernel(
+    q_ref, k_ref, v_ref, expo_ref, inv_ref, out_ref, grad_ref, dqkv_ref, *, block
+):
     rows = q_ref.shape[0]
     pair = pl.program_id(0)
     lower = lax.broadcasted_iota(jnp.int32, (block, PAIR), 1) < HD
@@ -1056,35 +1318,16 @@
     value_grad = jnp.concatenate(value_t, 0).T
     dqkv_ref[:, pl.ds(pl.multiple_of(D + pair * PAIR, PAIR), PAIR)] = key_grad.astype(jnp.bfloat16)
     dqkv_ref[:, pl.ds(pl.multiple_of(2 * D + pair * PAIR, PAIR), PAIR)] = value_grad.astype(jnp.bfloat16)
-    if jobs:
-        beside(jobs, {pl.num_programs(0) - 1: STAGES[5:]})
-
-        @pl.when(pair == pl.num_programs(0) - 1)
-        def _():
-            for job, total in zip(jobs, sums):
-                total[...] = job.out[...]
-
-
-def attention_backward(qkv_rows, expo, inverse, attended, attended_grad, shares, collective_id):
-    plain = []
-    if not with_kernels():
-        plain, shares = sum_shares(shares), []
-    reduced = len(shares)
-    transfer, scratch = {}, []
-    if reduced:
-        transfer = {"collective_id": collective_id, "has_side_effects": True}
-        scratch.append(pltpu.SemaphoreType.DMA((reduced, GROUP_SEMS)))
-    for share in shares:
-        scratch.append(pltpu.VMEM(share.shape, share.dtype))
-        scratch.extend(share_scratch(share))
+
+
+def attention_backward(qkv_rows, expo, inverse, attended, attended_grad, rides, collective_id):
     rows = qkv_rows.shape[0]
     pairs = HEADS // 2
-    block = min(256, rows)
     wide = lambda base: pl.BlockSpec((rows, PAIR), lambda j, base=base: (0, base + j))
-    qkv_grad, *sums = pl.pallas_call(
-        functools.partial(attention_backward_kernel, block=block, reduced=reduced),
-        grid=(pairs,),
-        in_specs=[
+    return block_call(
+        functools.partial(attention_backward_kernel, block=min(256, rows)),
+        pairs,
+        [
             wide(0),
             wide(pairs),
             wide(2 * pairs),
@@ -1092,19 +1335,17 @@
             wide(0),
             wide(0),
             wide(0),
-            *[ANYWHERE] * reduced,
         ],
-        out_specs=[fixed(rows, 3 * D), *[fixed(*s.shape) for s in shares]],
-        out_shape=[
-            jax.ShapeDtypeStruct((rows, 3 * D), jnp.bfloat16),
-            *[jax.ShapeDtypeStruct(s.shape, s.dtype) for s in shares],
-        ],
-        scratch_shapes=scratch,
-        compiler_params=pltpu.CompilerParams(vmem_limit_bytes=VMEM_LIMIT, **transfer),
-        cost_estimate=NO_COST,
-        name="attention_backward",
-    )(qkv_rows, qkv_rows, qkv_rows, expo, inverse, attended, attended_grad, *shares)
-    return qkv_grad, plain + sums
+        [qkv_rows, qkv_rows, qkv_rows, expo, inverse, attended, attended_grad],
+        [fixed(rows, 3 * D)],
+        [shape_of(rows, 3 * D, dtype=LOW)],
+        [],
+        34,
+        "attention_backward",
+        None,
+        rides,
+        collective_id,
+    )
 
 
 def mul(left, right):
@@ -1155,7 +1396,7 @@
 
 
 def fixed(*shape):
-    return pl.BlockSpec(shape, lambda i: (0,) * len(shape))
+    return pl.BlockSpec(shape, lambda i: (0,) * len(shape), pipeline_mode=pl.Buffered(1))
 
 
 def loads(sources, targets, sems):
@@ -1167,20 +1408,6 @@
 
 def shape_of(*shape, dtype=jnp.float32):
     return jax.ShapeDtypeStruct(shape, dtype)
-
-
-def block_call(body, grid, in_specs, out_specs, out_shape, scratch, flops, size, name, early=False):
-    return pl.pallas_call(
-        body,
-        grid=(grid,),
-        in_specs=in_specs,
-        out_specs=out_specs,
-        out_shape=out_shape,
-        scratch_shapes=scratch,
-        compiler_params=pltpu.CompilerParams(vmem_limit_bytes=VMEM_LIMIT),
-        cost_estimate=NO_COST if early else pl.CostEstimate(flops=flops, bytes_accessed=size, transcendentals=0),
-        name=name,
-    )
 
 
 def embed_kernel(pixel_ref, weight_ref, pos_ref, table_ref, bias_ref, out_ref):
@@ -1198,13 +1425,14 @@
         embed_kernel,
         rows // block,
         [rows_of(block, depth), fixed(depth, D), rows_of(block, nodes), fixed(nodes, D), fixed(1, D)],
-        rows_of(block, D),
-        shape_of(rows, D),
+        [pixels, weight, pos_weights, table, bias],
+        [rows_of(block, D)],
+        [shape_of(rows, D)],
         [],
-        2 * rows * depth * D,
-        2 * rows * depth + 2 * depth * D + 4 * rows * D,
+        18,
         "embed",
-    )(pixels, weight, pos_weights, table, bias)
+        work(2 * rows * depth * D, 2 * rows * depth + 2 * depth * D + 4 * rows * D),
+    )[0]
 
 
 def qkv_kernel(stream_ref, weight_ref, vector_ref, normed_ref, qkv_ref):
@@ -1223,13 +1451,14 @@
         qkv_kernel,
         rows // block,
         [rows_of(block, D), fixed(D, 3 * D), fixed(1, vector.shape[1])],
+        [stream, weight, vector],
         [rows_of(block, D), rows_of(block, 3 * D)],
         [shape_of(rows, D, dtype=low), shape_of(rows, 3 * D, dtype=low)],
         [],
-        6 * rows * D * D,
-        14 * rows * D + 6 * D * D,
+        16,
         "qkv_forward",
-    )(stream, weight, vector)
+        work(6 * rows * D * D, 14 * rows * D + 6 * D * D),
+    )
 
 
 def mlp_kernel(
@@ -1277,7 +1506,7 @@
     out_ref[...] = residual + mul(active_ref[...], down_ref[...]) + vector_ref[:, 8 * D : 9 * D]
 
 
-def mlp_forward(stream, attended, up, proj_out, vector):
+def mlp_forward(stream, attended, up, proj_out, vector, rides, collective_id):
     rows = stream.shape[0]
     width = up.shape[1]
     block = 256
@@ -1286,6 +1515,7 @@
         mlp_kernel,
         rows // block,
         [rows_of(block, D), rows_of(block, D), ANYWHERE, ANYWHERE, fixed(1, vector.shape[1])],
+        [stream, attended, up, proj_out, vector],
         [rows_of(block, D), rows_of(block, D), rows_of(block, width), rows_of(block, width), rows_of(block, D)],
         [
             shape_of(rows, D),
@@ -1300,10 +1530,12 @@
             pltpu.VMEM((width, D), low),
             pltpu.SemaphoreType.DMA((3,)),
         ],
-        2 * rows * D * (D + 2 * width),
-        rows * (16 * D + 4 * width) + 2 * D * (D + 2 * width),
+        30,
         "mlp_forward",
-    )(stream, attended, up, proj_out, vector)
+        work(2 * rows * D * (D + 2 * width), rows * (16 * D + 4 * width) + 2 * D * (D + 2 * width)),
+        rides,
+        collective_id,
+    )
 
 
 def mlp_back_kernel(
@@ -1366,6 +1598,7 @@
         mlp_back_kernel,
         rows // block,
         [narrow, rows_of(block, width), narrow, ANYWHERE, ANYWHERE, fixed(1, vector.shape[1])],
+        [grad, slope, residual, up, proj_out, vector],
         [narrow, rows_of(block, width), narrow, narrow, narrow, fixed(1, 4 * D + width)],
         [
             shape_of(rows, D, dtype=low),
@@ -1381,11 +1614,10 @@
             pltpu.VMEM((width, D), low),
             pltpu.SemaphoreType.DMA((3,)),
         ],
-        2 * rows * D * (D + 2 * width),
-        rows * (18 * D + 4 * width) + 2 * D * (D + 2 * width),
+        30,
         "mlp_backward",
-        early=True,
-    )(grad, slope, residual, up, proj_out, vector)
+        None,
+    )
 
 
 def qkv_back_kernel(grad_ref, residual_ref, stream_ref, weight_ref, vector_ref, out_ref, sums_ref):
@@ -1404,14 +1636,14 @@
         qkv_back_kernel,
         rows // block,
         [rows_of(block, 3 * D), narrow, narrow, fixed(D, 3 * D), fixed(1, vector.shape[1])],
+        [grad, residual_grad, stream, weight, vector],
         [narrow, fixed(1, 5 * D)],
         [shape_of(rows, D), shape_of(1, 5 * D)],
         [],
-        6 * rows * D * D,
-        18 * rows * D + 6 * D * D,
+        16,
         "qkv_backward",
-        early=True,
-    )(grad, residual_grad, stream, weight, vector)
+        None,
+    )
 
 
 def input_grad_kernel(first_ref, second_ref, qkv_ref, hidden_ref, qkv_out, up_out, left_ref, *, cut):
@@ -1449,32 +1681,38 @@
             pl.BlockSpec((rows, D), before),
             pl.BlockSpec((rows, D), after),
         ],
+        [first, second, qkv_grad, hidden_grad],
         [pl.BlockSpec((D, D), before), pl.BlockSpec((D, D), after)],
         [
             shape_of(D, qkv_grad.shape[1], dtype=jnp.bfloat16),
             shape_of(D, hidden_grad.shape[1], dtype=jnp.bfloat16),
         ],
         [pltpu.VMEM((D, rows), jnp.bfloat16)],
-        2 * rows * D * D * steps,
-        2 * rows * D * (steps + 2) + 2 * D * D * steps,
+        24,
         "input_weight_grad",
-        early=True,
-    )(first, second, qkv_grad, hidden_grad)
-
-
-def output_grad_kernel(attended_ref, active_ref, residual_ref, grad_ref, out_ref, *, cut):
+        None,
+    )
+
+
+def output_grad_kernel(attended_ref, active_ref, residual_ref, grad_ref, *outs, cut):
     step = pl.program_id(0)
+
+    def store(product):
+        base = 0
+        for out in outs:
+            out[...] = product[:, base : base + out.shape[1]].astype(jnp.bfloat16)
+            base += out.shape[1]
 
     @pl.when(step < cut)
     def _():
-        out_ref[...] = mul(attended_ref[...].T, residual_ref[...]).astype(jnp.bfloat16)
+        store(mul(attended_ref[...].T, residual_ref[...]))
 
     @pl.when(step >= cut)
     def _():
-        out_ref[...] = mul(active_ref[...].T, grad_ref[...]).astype(jnp.bfloat16)
-
-
-def output_weight_grad(attended, active, residual_low, grad_low):
+        store(mul(active_ref[...].T, grad_ref[...]))
+
+
+def output_weight_grad(attended, active, residual_low, grad_low, parts):
     rows = attended.shape[0]
     block = 768
     cut = attended.shape[1] // block
@@ -1488,14 +1726,13 @@
             fixed(rows, D),
             fixed(rows, D),
         ],
-        rows_of(block, D),
-        shape_of(steps * block, D, dtype=jnp.bfloat16),
+        [attended, active, residual_low, grad_low],
+        [rows_of(block, part) for part in parts],
+        [shape_of(steps * block, part, dtype=LOW) for part in parts],
         [],
-        2 * rows * D * block * steps,
-        2 * rows * (block * steps + 2 * D) + 2 * D * block * steps,
+        24,
         "output_weight_grad",
-        early=True,
-    )(attended, active, residual_low, grad_low)
+    )
 
 
 def embed_back_kernel(pixel_ref, grad_ref, pos_ref, out_ref, table_ref, bias_ref, low_ref):
@@ -1520,14 +1757,14 @@
         embed_back_kernel,
         depth // block,
         [pl.BlockSpec((rows, block), lambda i: (0, i)), fixed(rows, D), fixed(nodes, rows)],
+        [pixels, grad, pos_weights_t],
         [rows_of(block, D), fixed(nodes, D), fixed(1, D)],
         [shape_of(depth, D, dtype=jnp.bfloat16), shape_of(nodes, D), shape_of(1, D)],
         [pltpu.VMEM((rows, D), jnp.bfloat16)],
-        2 * rows * depth * D,
-        2 * rows * depth + 2 * depth * D + 4 * rows * D,
+        20,
         "embed_backward",
-        early=True,
-    )(pixels, grad, pos_weights_t)
+        None,
+    )
 
 
 def adam_update(gradient, moment, square, weight, factor, learn_rate):
@@ -1574,40 +1811,32 @@
     nodes = pos_weights.shape[1]
     pos_weights = jnp.pad(pos_weights, ((0, 0), (0, -nodes % 64)))
     vector_size = layer_vector.size
-    inputs = [
-        (input_proj[index, :, : 3 * D].astype(LOW), input_proj[index, :, 3 * D :].astype(LOW))
-        for index in range(LAYERS)
-    ]
-    outputs = [output_proj[index].astype(LOW) for index in range(LAYERS)]
-    kernel_full, vectors, qkv_zero = gather_all(
-        [
-            patch_kernel.astype(LOW),
-            padded_rows(layer_vector.astype(LOW).reshape(-1), 32),
-            inputs[0][0],
-        ],
-        (True, False, True),
-        1,
+    (kernel_full, vectors, qkv_zero), rides, rest_shards = gather_first(
+        patch_kernel,
+        padded_rows(layer_vector.astype(LOW).reshape(-1), 32),
+        input_proj,
+        output_proj,
+        head_weight,
     )
     vectors = vectors.reshape(owners, -1)[:, :vector_size].reshape(owners, *layer_vector.shape)
     vectors = jnp.swapaxes(vectors, 0, 1).reshape(LAYERS, 1, -1).astype(jnp.float32)
-    output_zero, qkv_one, up_one, head_full = (
-        lax.all_gather(shard, "fsdp", axis=0, tiled=True)
-        for shard in (outputs[0], *inputs[1], head_weight.astype(LOW))
+    output_zero, up_one, head_full = (
+        lax.all_gather(shard, "fsdp", axis=0, tiled=True) for shard in rest_shards
     )
     global_low = rounded(global_vector)
     position_low = jnp.pad(rounded(position_table), ((0, -nodes % 64), (0, 0)))
     stream = embed(pixels, kernel_full, pos_weights, position_low, global_low[None, :D])
     saved_layers = []
-    for index, qkv_weight in enumerate((qkv_zero, qkv_one)):
+    qkv_weight = qkv_zero
+    for index in range(LAYERS):
         vector = vectors[index]
         normed, qkv_rows = qkv_forward(stream, qkv_weight, vector)
-        fetch = inputs[0][1] if index == 0 else outputs[1]
-        attended, expo, inverse, (fetched,) = attention_forward(
-            qkv_rows, segment, [fetch], 4 + index
+        attended, expo, inverse, fetched = attention_forward(
+            qkv_rows, segment, [rides[0] if index == 0 else rides[2]], 4 + index
         )
         up, output = (fetched, output_zero) if index == 0 else (up_one, fetched)
-        residual, normed_second, active, slope, following = mlp_forward(
-            stream, attended, up, output, vector
+        residual, normed_second, active, slope, following, *fetched = mlp_forward(
+            stream, attended, up, output, vector, rides[1:2] if index == 0 else (), 7
         )
         saved_layers.append(
             (
@@ -1617,6 +1846,8 @@
             )
         )
         stream = following
+        if fetched:
+            (qkv_weight,) = fetched
     final_norm, final_back = jax.vjp(
         layer_norm, stream, global_low[D : 2 * D], global_low[2 * D : 3 * D]
     )
@@ -1649,17 +1880,23 @@
         grad_low, hidden_grad, residual_grad, residual_low, attended_grad, mlp_sums = mlp_backward(
             stream_grad, slope, residual, up, output, vector
         )
-        output_grad = output_weight_grad(attended, active, residual_low, grad_low)
-        attended_grad, output_grad = lax.optimization_barrier((attended_grad, output_grad))
-        output_grad = by_owner(output_grad)
-        half = -(-output_grad.shape[1] // 64) * 32
+        output_grads = output_weight_grad(
+            attended, active, residual_low, grad_low, (D // 3,) * 3 if index else (D,)
+        )
+        attended_grad, *output_grads = lax.optimization_barrier((attended_grad, *output_grads))
+        output_parts = [scatter(by_owner(grad)) for grad in output_grads]
         if index:
-            early_parts.append(scatter(output_grad[:, :half]))
-            early_parts.append(scatter(output_grad[:, half:]))
+            early_parts.extend(output_parts)
         else:
-            last_part = scatter(output_grad)
-        qkv_grad, early_sums = attention_backward(
-            qkv_rows, expo, inverse, attended, attended_grad, [] if index else early_parts, 6
+            (last_part,) = output_parts
+        qkv_grad, *early_sums = attention_backward(
+            qkv_rows,
+            expo,
+            inverse,
+            attended,
+            attended_grad,
+            () if index else [ShareRide(part) for part in early_parts],
+            6,
         )
         stream_grad, qkv_sums = qkv_backward(qkv_grad, residual_grad, entering, qkv_weight, vector)
         input_grads = input_weight_grad(normed, normed_second, qkv_grad, hidden_grad)
@@ -1714,7 +1951,7 @@
     input_sum = jnp.stack(
         [jnp.concatenate(pair, 1) for pair in (input_zero_sums, input_one_sums)]
     ).astype(jnp.float32)
-    output_sum = jnp.stack([output_zero_sum, jnp.concatenate(output_one_sums, 0)]).astype(
+    output_sum = jnp.stack([output_zero_sum, jnp.concatenate(output_one_sums, 1)]).astype(
         jnp.float32
     )
     vector_sum = small_share[:vector_rows].reshape(-1)[:vector_size].reshape(layer_vector.shape)

time: 720 us -> 758 us (1.053)
  local copies, waits for them, and re-layouts: 33.6 us -> 132 us
  Pallas kernels: 601 us -> 521 us
  waiting for transfers between devices: 2.01 us -> 20.7 us
    unnamed x79 -> x287, local copies, waits for them, and re-layouts: 4.37 us -> 106 us
    pallas_call x19, Pallas kernels: 455 us -> 374 us  [the longest x18 306 us: block_call(): pl.pallas_call(kernel, grid=(grid,), in_specs=in_specs, out_specs=out_spe...]
    reduce_scatter x6 -> x7, waiting for transfers between devices: 1.12 us -> 17.3 us  [scatter(): return lax.psum_scatter(grad, 'fsdp', scatter_dimension=0)]
    slice x4 -> x0, local copies, waits for them, and re-layouts: 9.42 us -> none  [the longest x1 3.82 us: body(): early_parts.append(scatter(output_grad[:, :half]))]
  transfers between devices with their start and end apart: 10 -> 10, of which waited for: 1 -> 2; matrix products, arithmetic and copies ran while one was open for 6% -> 6% of each run, Pallas kernels for 79% -> 55%
where the time goes in v6:
time: 758 us; the launch traced here: 753 us
  Pallas kernels  521 us (69%)
  local copies, waits for them, and re-layouts  132 us (17%)
  other arithmetic  46.6 us (6%)
  between operations  21.8 us (3%)
  waiting for transfers between devices  20.7 us (3%)
  matrix products  10.1 us (1%)
    pallas_call x18, Pallas kernels, block_call(): pl.pallas_call(kernel, grid=(grid,), in_specs=in_specs, out_specs=out_spe...  306 us
    pallas_call x1, Pallas kernels, reduce_call(): pl.pallas_call(functools.partial(reduce_kernel, whole=whole, partly=partl...  108 us
    unnamed x287, local copies, waits for them, and re-layouts  106 us
    pallas_call x1, Pallas kernels, gather_first(): pl.pallas_call(gather_kernel, in_specs=[ANYWHERE] * 5, out_specs=[ANYWHER...  68.7 us
    pallas_call x1, Pallas kernels, finish_call(): pl.pallas_call(functools.partial(finish_kernel, done=done, partly=partly)...  38 us
    sub x7, other arithmetic, adam_update(): return (moment, square, weight - learn_rate * step_dir)  22.4 us
    reduce_scatter x7, waiting for transfers between devices, scatter(): return lax.psum_scatter(grad, 'fsdp', scatter_dimension=0)  17.3 us
  transfers between devices with their start and end apart: 10, of which 2 were waited for; matrix products, arithmetic and copies ran while one was open for 6% of the time, Pallas kernels for 55%

profile of v6, /device:TPU:0, one launch (start us, length us, event | category | flops | bytes accessed | tf_op | source)
XLA Modules:
  0.0 752.5 jit_solution(7940918475001839085)
XLA Ops:
  8.1 2.2 copy-done.7
  10.2 1.8 copy-done.9
  14.3 68.7 %gather_weights.1 = (bf16[8,384,768]{2,1,0:T(8,128)(2,1)S(1)}, bf16[8,32,128]{2,1,0:T(8,128)(2,1)S(1)}, bf16[8,96,2304]{2,1,0:T(8,128)(2,1)S(1)}, bf16[4,48,1536...) custom-call(f32[384,768]{1,0:T(8,128)S(1)} %copy-done.27, ...), custom_call_target="tpu_custom_call" | custom-call | tf_op jit(solution)/shard_map/gather_weights/pallas_call | solution.py:538
  86.0 2.2 copy-done.89
  104.4 1.9 copy.64
  118.8 2.9 copy-done.15
  122.6 2.4 copy-done.90
  125.0 8.1 %embed.1.stream_ref.refs_0_ = f32[1024,768]{1,0:T(8,128)S(1)} custom-call(bf16[1024,3072]{1,0:T(8,128)(2,1)S(1)} %copy-done.15, bf16[3072,768]{1,0:T(8,128)(2,1)S(1)} %bitcast.96, f32[1024,64]{1,0:T(8,128)S(1)} %pad.31.clone.pos_ref, f32[64,768]{1,0:T(8,128)S(1)} %copy-done.86, f32[1,768]{1,0:T(1,128)S(1)} %broadcast_in_dim.85.bias_ref), custom_call_target="tpu_custom_call" | custom-call | flops 4831838208 | bytes 14155776 | tf_op jit(solution)/shard_map/embed/pallas_call | solution.py:428
  133.2 5.2 qkv_forward.2
  139.7 33.4 %attention_forward.2 = (bf16[1024,768]{1,0:T(8,128)(2,1)S(1)}, bf16[12,1024,1024]{2,1,0:T(8,128)(2,1)}, f32[1024,768]{1,0:T(8,128)S(1)}, bf16[8,96,3072]{2,1,0:T(8,128)(2,1)S(1)}) custom-call(bf16[1024,2304]{1,0:T(8,128)(2,1)S(1)} %get-tuple-element.110.refs_0_.refs_1_.refs_2_, bf16[1024,2304]{1,0:T(8,128)(2,1)S(1)} %get-tuple-element.110.refs_0_.refs_1_.refs_2_, ...), custom_call_target="tpu_custom_call" | custom-call | flops 12884901888 | bytes 34603008 | tf_op jit(solution)/shard_map/attention_forward/pallas_call | solution.py:428
  173.1 2.1 copy-done.2
  175.3 2.3 copy-done.22
  179.3 2.9 copy-done.23
  182.2 1.9 copy-done.45
  184.2 28.9 %mlp_forward.2 = (f32[1024,768]{1,0:T(8,128)S(1)}, bf16[1024,768]{1,0:T(8,128)(2,1)S(1)}, bf16[1024,3072]{1,0:T(8,128)(2,1)}, bf16[1024,3072]{1,0:T(8,128)(2,1)}...) custom-call(f32[1024,768]{1,0:T(8,128)S(1)} %copy-done.45, ...), custom_call_target="tpu_custom_call" | custom-call | flops 10871635968 | bytes 35782656 | tf_op jit(solution)/shard_map/mlp_forward/pallas_call | solution.py:428
  213.2 5.4 qkv_forward.3
  219.8 36.7 %attention_forward.3 = (bf16[1024,768]{1,0:T(8,128)(2,1)S(1)}, bf16[12,1024,1024]{2,1,0:T(8,128)(2,1)}, f32[1024,768]{1,0:T(8,128)S(1)}, bf16[8,480,768]{2,1,0:T(8,128)(2,1)S(1)}) custom-call(bf16[1024,2304]{1,0:T(8,128)(2,1)S(1)} %get-tuple-element.122.refs_0_.refs_1_.refs_2_.q_ref.k_ref.v_ref, ...), custom_call_target="tpu_custom_call" | custom-call | flops 12884901888 | bytes 34603008 | tf_op jit(solution)/shard_map/attention_forward/pallas_call | solution.py:428
  256.5 2.1 copy-done
  259.8 2.6 copy-done.20
  265.5 2.7 copy-done.21
  268.1 2.3 copy-done.25
  270.5 1.9 copy-done.48
  272.4 22.8 %mlp_forward.3 = (f32[1024,768]{1,0:T(8,128)S(1)}, bf16[1024,768]{1,0:T(8,128)(2,1)S(1)}, bf16[1024,3072]{1,0:T(8,128)(2,1)}, bf16[1024,3072]{1,0:T(8,128)(2,1)}, f32[1024,768]{1,0:T(8,128)S(1)}) custom-call(f32[1024,768]{1,0:T(8,128)S(1)} %copy-done.48, bf16[1024,768]{1,0:T(8,128)(2,1)S(1)} %copy-done.12, bf16[768,3072]{1,0:T(8,128)(2,1)S(1)} %copy-done.25, ...), custom_call_target="tpu_custom_call" | custom-call | flops 10871635968 | bytes 35782656 | tf_op jit(solution)/shard_map/mlp_forward/pallas_call | solution.py:428
  300.5 1.8 fusion.56
  305.5 2.6 copy.61
  308.0 2.8 pad.34.clone
  310.9 1.9 convolution_divide_fusion
  312.8 2.9 multiply_reduce_fusion
  315.7 1.9 fusion.52
  319.5 21.7 %mlp_backward.2 = (bf16[1024,768]{1,0:T(8,128)(2,1)S(1)}, bf16[1024,3072]{1,0:T(8,128)(2,1)}, f32[1024,768]{1,0:T(8,128)S(1)}, bf16[1024,768]{1,0:T(8,128)(2,1)S...) custom-call(f32[1024,768]{1,0:T(8,128)S(1)} %broadcast_add_fusion.grad_ref, ...), custom_call_target="tpu_custom_call" | custom-call | tf_op jit(solution)/shard_map/mlp_backward/pallas_call | solution.py:428
  342.9 8.8 %output_weight_grad.2 = (bf16[3840,256]{1,0:T(8,128)(2,1)}, bf16[3840,256]{1,0:T(8,128)(2,1)}, bf16[3840,256]{1,0:T(8,128)(2,1)}) custom-call(bf16[1024,768]{1,0:T(8,128)(2,1)S(1)} %copy-done.13, bf16[1024,3072]{1,0:T(8,128)(2,1)S(1)} %bitcast.71, bf16[1024,768]{1,0:T(8,128)(2,1)S(1)} %get-tuple-element.136.residual_ref, ...), custom_call_target="tpu_custom_call" | custom-call | tf_op jit(solution)/shard_map/output_weight_grad/pallas_call | solution.py:428
  353.1 2.3 copy-done.1
  355.4 1.9 copy-done.39
  357.3 27.4 %attention_backward.2.grad_ref.qkv_ref = bf16[1024,2304]{1,0:T(8,128)(2,1)S(1)} custom-call(bf16[1024,2304]{1,0:T(8,128)(2,1)S(1)} %copy-done.1, bf16[1024,2304]{1,0:T(8,128)(2,1)S(1)} %copy-done.1, bf16[1024,2304]{1,0:T(8,128)(2,1)S(1)} %copy-done.1, bf16[12,1024,1024]{2,1,0:T(8,128)(2,1)} %get-tuple-element.125.expo_ref, f32[1024,768]{1,0:T(8,128)S(1)} %copy-done.39, ...), custom_call_target="tpu_custom_call" | custom-call | tf_op jit(solution)/shard_map/attention_backward/pallas_call | solution.py:428
  384.8 5.6 qkv_backward.2
  392.0 13.0 %input_weight_grad.2 = (bf16[768,2304]{1,0:T(8,128)(2,1)}, bf16[768,3072]{1,0:T(8,128)(2,1)S(1)}) custom-call(bf16[1024,768]{1,0:T(8,128)(2,1)S(1)} %copy-done.63, bf16[1024,768]{1,0:T(8,128)(2,1)S(1)} %copy-done.65, bf16[1024,2304]{1,0:T(8,128)(2,1)S(1)} %attention_backward.2.grad_ref.qkv_ref, bf16[1024,3072]{1,0:T(8,128)(2,1)S(1)} %bitcast.67), custom_call_target="tpu_custom_call" | custom-call | tf_op jit(solution)/shard_map/input_weight_grad/pallas_call | solution.py:428
  405.0 2.1 copy-done.26
  408.0 2.9 copy-done.19
  410.9 2.5 copy-done.24
  413.4 1.9 copy-done.37
  415.3 1.9 copy-done.43
  417.3 21.8 %mlp_backward.3 = (bf16[1024,768]{1,0:T(8,128)(2,1)S(1)}, bf16[1024,3072]{1,0:T(8,128)(2,1)}, f32[1024,768]{1,0:T(8,128)S(1)}, bf16[1024,768]{1,0:T(8,128)(2,1)S...) custom-call(f32[1024,768]{1,0:T(8,128)S(1)} %copy-done.43, bf16[1024,3072]{1,0:T(8,128)(2,1)} %get-tuple-element.150.slope_ref, ...), custom_call_target="tpu_custom_call" | custom-call | tf_op jit(solution)/shard_map/mlp_backward/pallas_call | solution.py:428
  439.1 7.7 %output_weight_grad.3 = bf16[3840,768]{1,0:T(8,128)(2,1)S(1)} custom-call(bf16[1024,768]{1,0:T(8,128)(2,1)S(1)} %copy-done.18, bf16[1024,3072]{1,0:T(8,128)(2,1)S(1)} %bitcast.69, bf16[1024,768]{1,0:T(8,128)(2,1)S(1)} %get-tuple-element.154.residual_ref, bf16[1024,768]{1,0:T(8,128)(2,1)S(1)} %get-tuple-element.155.grad_ref), custom_call_target="tpu_custom_call" | custom-call | tf_op jit(solution)/shard_map/output_weight_grad/pallas_call | solution.py:428
  446.8 2.6 copy-done.4
  453.4 5.8 reduce-scatter.14.cloned.1.call-done
  459.1 2.3 copy-done.3
  461.5 1.9 copy-done.55
  467.1 33.0 %attention_backward.3 = (bf16[1024,2304]{1,0:T(8,128)(2,1)S(1)}, bf16[96,1024]{1,0:T(8,128)(2,1)S(1)}, bf16[480,256]{1,0:T(8,128)(2,1)S(1)}, bf16[480,256]{1,0:T(8,128)(2,1)S(1)}, bf16[480,256]{1,0:T(8,128)(2,1)S(1)}) custom-call(bf16[1024,2304]{1,0:T(8,128)(2,1)S(1)} %copy-done.3, bf16[1024,2304]{1,0:T(8,128)(2,1)S(1)} %copy-done.3, ...), custom_call_target="tpu_custom_call" | custom-call | tf_op jit(solution)/shard_map/attention_backward/pallas_call | solution.py:428
  500.2 5.8 qkv_backward.3
  508.5 2.9 copy-done.16
  511.4 8.3 %embed_backward.1 = (bf16[3072,768]{1,0:T(8,128)(2,1)S(1)}, f32[64,768]{1,0:T(8,128)S(1)}, f32[1,768]{1,0:T(1,128)S(1)}) custom-call(bf16[1024,3072]{1,0:T(8,128)(2,1)S(1)} %copy-done.16, f32[1024,768]{1,0:T(8,128)S(1)} %get-tuple-element.171.grad_ref, f32[64,1024]{1,0:T(8,128)S(1)} %pad_bitcast_fusion.1.pos_ref), custom_call_target="tpu_custom_call" | custom-call | tf_op jit(solution)/shard_map/embed_backward/pallas_call | solution.py:428
  519.8 2.2 copy-done.29
  522.7 2.6 concatenate.24
  526.1 2.4 copy-done.6
  528.5 2.9 copy-done.14
  531.4 12.3 %input_weight_grad.3 = (bf16[768,2304]{1,0:T(8,128)(2,1)S(1)}, bf16[768,3072]{1,0:T(8,128)(2,1)S(1)}) custom-call(bf16[1024,768]{1,0:T(8,128)(2,1)S(1)} %copy-done.59, bf16[1024,768]{1,0:T(8,128)(2,1)S(1)} %copy-done.61, bf16[1024,2304]{1,0:T(8,128)(2,1)S(1)} %copy-done.6, bf16[1024,3072]{1,0:T(8,128)(2,1)S(1)} %copy-done.14), custom_call_target="tpu_custom_call" | custom-call | tf_op jit(solution)/shard_map/input_weight_grad/pallas_call | solution.py:428
  543.7 2.2 copy-done.30
  548.6 11.6 %reduce-scatter.18.cloned.1.call-done = bf16[1,96,3072]{2,1,0:T(8,128)(2,1)} async-done(((bf16[8,96,3072]{2,1,0:T(8,128)(2,1)}), bf16[1,96,3072]{2,1,0:T(8,128)(2,1)}) %reduce-scatter.18.cloned.1.call-update) | async-done | bytes 589840 | tf_op jit(solution)/shard_map/reduce_scatter | solution.py:1206
  560.2 108.1 %reduce_gradients.1 = (bf16[96,2304]{1,0:T(8,128)(2,1)}, bf16[96,3072]{1,0:T(8,128)(2,1)}, bf16[384,768]{1,0:T(8,128)(2,1)}, bf16[96,2304]{1,0:T(8,128)(2,1)}, bf16[96,3072]{1,0:T(8,128)(2,1)}) custom-call(bf16[8,96,2304]{2,1,0:T(8,128)(2,1)} %bitcast.87, bf16[8,96,3072]{2,1,0:T(8,128)(2,1)} %bitcast.82, bf16[8,384,768]{2,1,0:T(8,128)(2,1)} %bitcast.81, ...), custom_call_target="tpu_custom_call" | custom-call | tf_op jit(solution)/shard_map/reduce_gradients/pallas_call | solution.py:1107
  670.0 38.0 %finish_gradients.1 = (bf16[480,768]{1,0:T(8,128)(2,1)}, f32[64,128]{1,0:T(8,128)}, f32[8,64,128]{2,1,0:T(8,128)}) custom-call(bf16[96,1024]{1,0:T(8,128)(2,1)} %copy-done.72, bf16[480,256]{1,0:T(8,128)(2,1)} %copy-done.66, bf16[480,256]{1,0:T(8,128)(2,1)} %copy-done.68, bf16[480,256]{1,0:T(8,128)(2,1)} %copy-done.70, ...), custom_call_target="tpu_custom_call" | custom-call | tf_op jit(solution)/shard_map/finish_gradients/pallas_call | solution.py:1160
  721.6 4.5 multiply_subtract_fusion.2
  726.1 2.8 multiply_subtract_fusion.3
  731.1 8.3 %multiply_subtract_fusion = (f32[2,96,5376]{2,1,0:T(8,128)}, f32[2,96,5376]{2,1,0:T(8,128)}, f32[2,96,5376]{2,1,0:T(8,128)}) fusion(f32[2,96,5376]{2,1,0:T(8,128)S(1)} %copy-done.8, f32[]{:T(128)S(6)} %div.163, bf16[1,96,5376]{2,1,0:T(8,128)(2,1)S(1)} %get-tuple-element.241, bf16[1,96,5376]{2,1,0:T(8,128)(2,1)S(1)} %get-tuple-element.240, ...), kind=kLoop, calls=%fused_computation.6 | loop fusion | flops 17547264 | bytes 26836996 | tf_op jit(solution)/shard_map/sub | solution.py:1779
  739.4 4.6 multiply_subtract_fusion.1
  (365 shorter events, 86.7 us)
Async XLA Ops:
  7.2 172.1 %all-gather.4.cloned.1.call-start = ((), (), s32[]{:S(2)}) async-start(), calls=%async_computation.7 | async-start | bytes 6635520 | tf_op jit(solution)/shard_map/all_gather | solution.py:1824
  14.3 80.8 %copy-start.87 = (s32[1024]{0:T(1024)S(1)}, s32[1024]{0:T(1024)}, u32[]{:S(2)}) copy-start(s32[1024]{0:T(1024)} %param.26) | copy-start | bytes 12292
  93.0 40.1 %copy-start.31 = (bf16[8,96,2304]{2,1,0:T(8,128)(2,1)}, bf16[8,96,2304]{2,1,0:T(8,128)(2,1)S(1)}, u32[]{:S(2)}) copy-start(bf16[8,96,2304]{2,1,0:T(8,128)(2,1)S(1)} %get-tuple-element.108) | copy-start | bytes 10616836
  93.1 171.0 %all-gather.6.cloned.1.call-start = ((), (), s32[]{:S(2)}) async-start(), calls=%async_computation.8 | async-start | bytes 5308416 | tf_op jit(solution)/shard_map/all_gather | solution.py:1824
  93.8 206.6 %all-gather.8.cloned.1.call-start = ((), (), s32[]{:S(2)}) async-start(), calls=%async_computation.9 | async-start | bytes 1769472 | tf_op jit(solution)/shard_map/all_gather | solution.py:1824
  94.5 358.8 %reduce-scatter.8.cloned.1.call-start = ((), (), s32[]{:S(2)}) async-start(), calls=%async_computation.10 | async-start | bytes 1769472 | tf_op jit(solution)/shard_map/reduce_scatter | solution.py:1206
  125.0 8.1 %copy-start.78 = (f32[1,9984]{1,0:T(1,128)S(1)}, f32[1,9984]{1,0:T(1,128)}, u32[]{:S(2)}) copy-start(f32[1,9984]{1,0:T(1,128)} %squeeze.41.vector_ref.refs_4_) | copy-start | bytes 119812
  139.7 39.6 %copy-start.79 = (f32[1,9984]{1,0:T(1,128)S(1)}, f32[1,9984]{1,0:T(1,128)}, u32[]{:S(2)}) copy-start(f32[1,9984]{1,0:T(1,128)} %squeeze.41.vector_ref.refs_4_) | copy-start | bytes 119812
  139.7 39.6 %copy-start.100 = (bf16[4,48,1152]{2,1,0:T(8,128)(2,1)S(1)}, bf16[4,48,1152]{2,1,0:T(8,128)(2,1)}, u32[]{:S(2)}) copy-start(bf16[4,48,1152]{2,1,0:T(8,128)(2,1)} %copy-done.99) | copy-start | bytes 1327108
  139.7 39.6 %copy-start.102 = (bf16[96,2304]{1,0:T(8,128)(2,1)S(1)}, bf16[96,2304]{1,0:T(8,128)(2,1)}, u32[]{:S(2)}) copy-start(bf16[96,2304]{1,0:T(8,128)(2,1)} %copy-done.101) | copy-start | bytes 1327108
  179.3 33.8 %copy-start.17 = (bf16[1024,768]{1,0:T(8,128)(2,1)}, bf16[1024,768]{1,0:T(8,128)(2,1)S(1)}, u32[]{:S(2)}) copy-start(bf16[1024,768]{1,0:T(8,128)(2,1)S(1)} %get-tuple-element.115.refs_1_.attended_ref.refs_5_) | copy-start | bytes 4718596
  184.2 28.9 %copy-start.80 = (f32[1,9984]{1,0:T(1,128)S(1)}, f32[1,9984]{1,0:T(1,128)}, u32[]{:S(2)}) copy-start(f32[1,9984]{1,0:T(1,128)} %squeeze.42.vector_ref) | copy-start | bytes 119812
  213.1 6.6 copy-start.77
  213.1 6.6 copy-start.92
  213.1 6.6 copy-start.94
  302.3 8.5 %copy-start.124 = (f32[8]{0:T(128)}, f32[8]{0:T(128)S(1)}, u32[]{:S(2)}) copy-start(f32[8]{0:T(128)S(1)} %get-tuple-element.237) | copy-start | bytes 100
  310.8 142.5 %reduce-scatter.10.cloned.1.call-start = ((), (), s32[]{:S(2)}) async-start(), calls=%async_computation.11 | async-start | bytes 2211840 | tf_op jit(solution)/shard_map/reduce_scatter | solution.py:1206
  317.9 24.9 %slice-start.4 = ((s8[6291456]{0:T(1024)(128)(4,1)}), s8[4194304]{0:T(1024)(128)(4,1)S(1)}, s32[]{:S(2)}) async-start(s8[6291456]{0:T(1024)(128)(4,1)} %bitcast.70), calls=%async_computation.21 | async-start | bytes 8388608
  319.5 23.3 %copy-start.13 = (bf16[1024,768]{1,0:T(8,128)(2,1)S(1)}, bf16[1024,768]{1,0:T(8,128)(2,1)}, u32[]{:S(2)}) copy-start(bf16[1024,768]{1,0:T(8,128)(2,1)} %copy-done.11) | copy-start | bytes 4718596
  319.5 23.3 %slice-start.5 = ((s8[6291456]{0:T(1024)(128)(4,1)}), s8[2097152]{0:T(1024)(128)(4,1)S(1)}, s32[]{:S(2)}) async-start(s8[6291456]{0:T(1024)(128)(4,1)} %bitcast.70), calls=%async_computation.22 | async-start | bytes 4194304
  351.7 101.7 %reduce-scatter.12.cloned.1.call-start = ((), (), s32[]{:S(2)}) async-start(), calls=%async_computation.12 | async-start | bytes 2211840 | tf_op jit(solution)/shard_map/reduce_scatter | solution.py:1206
  352.3 106.9 %reduce-scatter.14.cloned.1.call-start = ((), (), s32[]{:S(2)}) async-start(), calls=%async_computation.13 | async-start | bytes 2211840 | tf_op jit(solution)/shard_map/reduce_scatter | solution.py:1206
  353.0 195.6 %reduce-scatter.16.cloned.1.call-start = ((), (), s32[]{:S(2)}) async-start(), calls=%async_computation.14 | async-start | bytes 3981312 | tf_op jit(solution)/shard_map/reduce_scatter | solution.py:1206
  357.3 27.4 %copy-start.34 = (bf16[8,96,2304]{2,1,0:T(8,128)(2,1)S(1)}, bf16[8,96,2304]{2,1,0:T(8,128)(2,1)}, u32[]{:S(2)}) copy-start(bf16[8,96,2304]{2,1,0:T(8,128)(2,1)} %copy-done.33) | copy-start | bytes 10616836
  357.3 27.4 %copy-start.49 = (f32[1024,768]{1,0:T(8,128)S(1)}, f32[1024,768]{1,0:T(8,128)}, u32[]{:S(2)}) copy-start(f32[1024,768]{1,0:T(8,128)} %copy-done.47) | copy-start | bytes 9437188
  357.3 27.4 %copy-start.53 = (f32[1024,768]{1,0:T(8,128)S(1)}, f32[1024,768]{1,0:T(8,128)}, u32[]{:S(2)}) copy-start(f32[1024,768]{1,0:T(8,128)} %copy-done.52) | copy-start | bytes 9437188
  384.7 7.3 slice-start
  384.7 7.3 slice-start.1
  384.8 7.3 copy-start.63
  384.8 7.3 copy-start.65
  407.2 153.0 %reduce-scatter.18.cloned.1.call-start = ((), (), s32[]{:S(2)}) async-start(), calls=%async_computation.15 | async-start | bytes 5308416 | tf_op jit(solution)/shard_map/reduce_scatter | solution.py:1206
  407.9 262.1 %reduce-scatter.20.cloned.1.call-start = ((), (), s32[]{:S(2)}) async-start(), calls=%async_computation.16 | async-start | bytes 6635520 | tf_op jit(solution)/shard_map/reduce_scatter | solution.py:1206
  408.0 31.1 %slice-start.2 = ((s8[6291456]{0:T(1024)(128)(4,1)}), s8[4194304]{0:T(1024)(128)(4,1)S(1)}, s32[]{:S(2)}) async-start(s8[6291456]{0:T(1024)(128)(4,1)} %bitcast.68), calls=%async_computation.19 | async-start | bytes 8388608
  417.3 21.8 %slice-start.3 = ((s8[6291456]{0:T(1024)(128)(4,1)}), s8[2097152]{0:T(1024)(128)(4,1)S(1)}, s32[]{:S(2)}) async-start(s8[6291456]{0:T(1024)(128)(4,1)} %bitcast.68), calls=%async_computation.20 | async-start | bytes 4194304
  417.3 21.8 %copy-start.18 = (bf16[1024,768]{1,0:T(8,128)(2,1)S(1)}, bf16[1024,768]{1,0:T(8,128)(2,1)}, u32[]{:S(2)}) copy-start(bf16[1024,768]{1,0:T(8,128)(2,1)} %copy-done.17) | copy-start | bytes 4718596
  439.0 7.8 %copy-start.50 = (f32[1024,768]{1,0:T(8,128)}, f32[1024,768]{1,0:T(8,128)S(1)}, u32[]{:S(2)}) copy-start(f32[1024,768]{1,0:T(8,128)S(1)} %get-tuple-element.170.residual_ref) | copy-start | bytes 9437188
  467.1 33.0 %copy-start.32 = (bf16[8,96,2304]{2,1,0:T(8,128)(2,1)S(1)}, bf16[8,96,2304]{2,1,0:T(8,128)(2,1)}, u32[]{:S(2)}) copy-start(bf16[8,96,2304]{2,1,0:T(8,128)(2,1)} %copy-done.31) | copy-start | bytes 10616836
  467.1 33.1 %copy-start.46 = (f32[1024,768]{1,0:T(8,128)S(1)}, f32[1024,768]{1,0:T(8,128)}, u32[]{:S(2)}) copy-start(f32[1024,768]{1,0:T(8,128)} %copy-done.44) | copy-start | bytes 9437188
  467.1 33.1 %copy-start.51 = (f32[1024,768]{1,0:T(8,128)S(1)}, f32[1024,768]{1,0:T(8,128)}, u32[]{:S(2)}) copy-start(f32[1024,768]{1,0:T(8,128)} %copy-done.50) | copy-start | bytes 9437188
  511.4 11.2 %copy-start.119 = (f32[1000]{0:T(1024)S(1)}, f32[1000]{0:T(1024)}, u32[]{:S(2)}) copy-start(f32[1000]{0:T(1024)} %get-tuple-element.222) | copy-start | bytes 12004
  511.4 11.2 %copy-start.120 = (f32[768]{0:T(1024)S(1)}, f32[768]{0:T(1024)}, u32[]{:S(2)}) copy-start(f32[768]{0:T(1024)} %get-tuple-element.190) | copy-start | bytes 9220
  511.4 11.2 %copy-start.121 = (f32[768]{0:T(1024)S(1)}, f32[768]{0:T(1024)}, u32[]{:S(2)}) copy-start(f32[768]{0:T(1024)} %get-tuple-element.192) | copy-start | bytes 9220
  511.4 13.9 %copy-start.110 = (f32[8,2496]{1,0:T(8,128)S(1)}, f32[8,2496]{1,0:T(8,128)}, u32[]{:S(2)}) copy-start(f32[8,2496]{1,0:T(8,128)} %reshape.372) | copy-start | bytes 239620
  531.4 16.3 %copy-start.67 = (bf16[480,256]{1,0:T(8,128)(2,1)S(1)}, bf16[480,256]{1,0:T(8,128)(2,1)}, u32[]{:S(2)}) copy-start(bf16[480,256]{1,0:T(8,128)(2,1)} %copy-done.66) | copy-start | bytes 737284
  531.4 16.3 %copy-start.69 = (bf16[480,256]{1,0:T(8,128)(2,1)S(1)}, bf16[480,256]{1,0:T(8,128)(2,1)}, u32[]{:S(2)}) copy-start(bf16[480,256]{1,0:T(8,128)(2,1)} %copy-done.68) | copy-start | bytes 737284
  531.4 16.3 %copy-start.71 = (bf16[480,256]{1,0:T(8,128)(2,1)S(1)}, bf16[480,256]{1,0:T(8,128)(2,1)}, u32[]{:S(2)}) copy-start(bf16[480,256]{1,0:T(8,128)(2,1)} %copy-done.70) | copy-start | bytes 737284
  670.0 51.4 %copy-start.28 = (f32[384,768]{1,0:T(8,128)S(1)}, f32[384,768]{1,0:T(8,128)}, u32[]{:S(2)}) copy-start(f32[384,768]{1,0:T(8,128)} %refs_0_.1) | copy-start | bytes 3538948
  721.4 7.4 copy-start.114
  721.4 7.4 copy-start.117
  721.4 7.4 copy-start.118
  721.5 8.0 %copy-start.115 = (f32[2,1248]{1,0:T(2,128)S(1)}, f32[2,1248]{1,0:T(2,128)}, u32[]{:S(2)}) copy-start(f32[2,1248]{1,0:T(2,128)} %param.33) | copy-start | bytes 29956
  721.5 8.0 %copy-start.122 = (f32[2,1248]{1,0:T(2,128)S(1)}, f32[2,1248]{1,0:T(2,128)}, u32[]{:S(2)}) copy-start(f32[2,1248]{1,0:T(2,128)} %param.47) | copy-start | bytes 29956
  721.5 8.0 %copy-start.123 = (f32[2,1248]{1,0:T(2,128)S(1)}, f32[2,1248]{1,0:T(2,128)}, u32[]{:S(2)}) copy-start(f32[2,1248]{1,0:T(2,128)} %param.40) | copy-start | bytes 29956
  721.5 8.7 %copy-start.108 = (f32[49,768]{1,0:T(8,128)S(1)}, f32[49,768]{1,0:T(8,128)}, u32[]{:S(2)}) copy-start(f32[49,768]{1,0:T(8,128)} %param.34) | copy-start | bytes 451588
  721.5 8.7 %copy-start.109 = (f32[49,768]{1,0:T(8,128)S(1)}, f32[49,768]{1,0:T(8,128)}, u32[]{:S(2)}) copy-start(f32[49,768]{1,0:T(8,128)} %mul.371) | copy-start | bytes 451588
  721.5 8.6 %copy-start.111 = (f32[49,768]{1,0:T(8,128)S(1)}, f32[49,768]{1,0:T(8,128)}, u32[]{:S(2)}) copy-start(f32[49,768]{1,0:T(8,128)} %param.48) | copy-start | bytes 451588
  721.5 8.6 %copy-start.112 = (f32[49,768]{1,0:T(8,128)S(1)}, f32[49,768]{1,0:T(8,128)}, u32[]{:S(2)}) copy-start(f32[49,768]{1,0:T(8,128)} %param.41) | copy-start | bytes 451588
  721.5 9.5 %copy-start.8 = (f32[2,96,5376]{2,1,0:T(8,128)S(1)}, f32[2,96,5376]{2,1,0:T(8,128)}, u32[]{:S(2)}) copy-start(f32[2,96,5376]{2,1,0:T(8,128)} %refs_2_.1) | copy-start | bytes 12386308
  721.6 9.5 %copy-start.103 = (f32[2,96,5376]{2,1,0:T(8,128)S(1)}, f32[2,96,5376]{2,1,0:T(8,128)}, u32[]{:S(2)}) copy-start(f32[2,96,5376]{2,1,0:T(8,128)} %param.45) | copy-start | bytes 12386308
  731.1 8.3 %copy-start.10 = (f32[2,480,768]{2,1,0:T(8,128)S(1)}, f32[2,480,768]{2,1,0:T(8,128)}, u32[]{:S(2)}) copy-start(f32[2,480,768]{2,1,0:T(8,128)} %refs_3_.1) | copy-start | bytes 8847364
  731.1 8.3 %copy-start.104 = (f32[2,480,768]{2,1,0:T(8,128)S(1)}, f32[2,480,768]{2,1,0:T(8,128)}, u32[]{:S(2)}) copy-start(f32[2,480,768]{2,1,0:T(8,128)} %param.46) | copy-start | bytes 8847364
  731.1 8.3 %copy-start.105 = (f32[2,480,768]{2,1,0:T(8,128)S(1)}, f32[2,480,768]{2,1,0:T(8,128)}, u32[]{:S(2)}) copy-start(f32[2,480,768]{2,1,0:T(8,128)} %param.39) | copy-start | bytes 8847364
  731.1 8.3 %copy-start.106 = (bf16[1,480,768]{2,1,0:T(8,128)(2,1)S(1)}, bf16[1,480,768]{2,1,0:T(8,128)(2,1)}, u32[]{:S(2)}) copy-start(bf16[1,480,768]{2,1,0:T(8,128)(2,1)} %maximum_bitcast_fusion.2) | copy-start | bytes 2211844
  731.1 8.3 %copy-start.107 = (bf16[480,768]{1,0:T(8,128)(2,1)S(1)}, bf16[480,768]{1,0:T(8,128)(2,1)}, u32[]{:S(2)}) copy-start(bf16[480,768]{1,0:T(8,128)(2,1)} %get-tuple-element.188) | copy-start | bytes 2211844
  (88 other events, 237.2 us)
Sparse Core Ops, SparseCore 0:
  93.2 62.5 all-gather.3
  158.0 50.3 all-gather.5
  210.6 23.8 all-gather.7
  310.9 32.2 reduce-scatter.7
  351.8 33.6 reduce-scatter.9
  388.3 33.9 reduce-scatter.11
  425.2 33.8 reduce-scatter.13
  462.1 42.2 reduce-scatter.15
  506.7 53.4 reduce-scatter.17
  562.3 73.8 reduce-scatter.19

commit v7 on v6

--- a/solution.py
+++ b/solution.py
@@ -150,8 +150,9 @@
 
 
 class Gather:
-    def __init__(self, shard, out, sems, split):
+    def __init__(self, shard, out, sems, split, in_place=False):
         self.shard, self.out, self.sems, self.split = shard, out, sems, split
+        self.in_place = in_place
         self.rows, self.columns = shard.shape
 
     def level_copy(self, turn):
@@ -188,7 +189,8 @@
         for turn in TURNS:
             self.level_copy(turn).start()
         self.core_copy(0).start()
-        self.own_copy().start()
+        if not self.in_place:
+            self.own_copy().start()
 
     def second(self):
         for turn in TURNS:
@@ -199,17 +201,19 @@
             else:
                 self.core_copy(turn).start()
 
-    def third(self):
-        if not self.split:
-            return
-        for turn in TURNS:
+    def third(self, use=None):
+        for turn in TURNS if self.split else ():
             for other in TURNS:
                 self.group_copy(turn, other).wait_recv()
             self.core_copy(turn).start()
-
-    def fourth(self):
-        for turn in (0, *TURNS):
+            if use is not None:
+                use(turn, True)
+
+    def fourth(self, use=None):
+        for turn in TURNS if use is not None else (0, *TURNS):
             self.core_copy(turn).wait_recv()
+            if use is not None:
+                use(turn, False)
         for turn in TURNS:
             self.level_copy(turn).wait_send()
             if self.split:
@@ -217,7 +221,8 @@
                     self.group_copy(turn, other).wait_send()
         for turn in (0, *TURNS):
             self.core_copy(turn).wait_send()
-        self.own_copy().wait()
+        if not self.in_place:
+            self.own_copy().wait()
 
 
 class LevelGather:
@@ -409,7 +414,7 @@
 
 
 def block_call(
-    body, grid, in_specs, operands, out_specs, out_shape, scratch, room, name,
+    body, grid, in_specs, operands, out_specs, out_shape, scratch, name,
     cost=None, rides=(), collective_id=None,
 ):
     plain = []
@@ -432,7 +437,7 @@
         out_specs=out_specs,
         out_shape=out_shape,
         scratch_shapes=scratch,
-        compiler_params=pltpu.CompilerParams(vmem_limit_bytes=room * MIB, **transfer),
+        compiler_params=pltpu.CompilerParams(vmem_limit_bytes=VMEM_LIMIT, **transfer),
         cost_estimate=cost or NO_COST,
         name=name,
     )(*operands)
@@ -447,17 +452,46 @@
     return pl.CostEstimate(flops=flops, bytes_accessed=size, transcendentals=0)
 
 
-def gather_kernel(*refs):
-    kernel, vectors, inputs, outputs, head = refs[:5]
-    kernel_full, vectors_full, qkv_full, up_level, qkv_level, output_level = refs[5:11]
-    up_zero, output_zero, qkv_one, up_one, output_one, head_low = refs[11:17]
-    wide_kernel, wide_inputs, wide_outputs, wide_head, kernel_low, qkv_zero = refs[17:23]
-    load_sems, sems = refs[23:]
+def position_weights(seg_col, patch_row, nodes):
+    rows = seg_col.shape[0]
+    slot = lax.broadcasted_iota(jnp.int32, (rows, IMGS), 1)
+    member = seg_col == slot
+    counts = jnp.sum(member.astype(jnp.float32), 0, keepdims=True)
+    start = jnp.sum(jnp.where(slot < seg_col, counts, 0.0), 1, keepdims=True)
+    token = lax.broadcasted_iota(jnp.int32, (rows, 1), 0).astype(jnp.float32)
+    inside = seg_col < IMGS
+    offset = jnp.where(inside, token - start, 0.0)
+    patch = jnp.sum(jnp.where(member, patch_row.astype(jnp.float32), 0.0), 1, keepdims=True)
+    side = jnp.where(inside, jnp.floor(IMG / jnp.where(inside, patch, 1.0) + 0.5), 1.0)
+    line = jnp.floor((offset + 0.5) / side)
+    column = offset - line * side
+
+    def spot(coord):
+        return jnp.clip((2.0 * coord + 1.0) * GRID / (2.0 * side) - 0.5, 0.0, GRID - 1.0)
+
+    node = lax.broadcasted_iota(jnp.int32, (rows, LANES), 1).astype(jnp.float32)
+    across = jnp.floor((node + 0.5) / GRID)
+    along = node - across * GRID
+    weights = jnp.maximum(1.0 - jnp.abs(spot(line) - across), 0.0)
+    weights = weights * jnp.maximum(1.0 - jnp.abs(spot(column) - along), 0.0)
+    return jnp.where(node < nodes, weights, 0.0)
+
+
+def first_kernel(*refs, spots):
+    kernel, vectors, inputs, outputs, head, pixels, seg_col, patch_row, table, biases = refs[:10]
+    stream, pos_t, vector_zero, vector_one = refs[10:14]
+    qkv_full, up_level, qkv_level, output_level = refs[14:18]
+    up_zero, output_zero, qkv_one, up_one, output_one, head_low = refs[18:24]
+    wide_kernel, wide_inputs, wide_outputs, wide_head, pixel_rows, table_low = refs[24:30]
+    kernel_full, qkv_zero, vectors_full, load_sems, sems = refs[30:]
+    _, level, core = place()
+    mine = 2 * level + core
     pairs = [
         (kernel, wide_kernel),
         (inputs.at[0], wide_inputs.at[0]),
         (outputs.at[1], wide_outputs.at[1]),
         (inputs.at[1], wide_inputs.at[1]),
+        (pixels, pixel_rows),
         (outputs.at[0], wide_outputs.at[0]),
         (head, wide_head),
     ]
@@ -467,62 +501,139 @@
     ]
     for copy in copies:
         copy.start()
-    jobs = [
-        Gather(kernel_low, kernel_full, sems.at[0], True),
-        Gather(vectors, vectors_full, sems.at[1], False),
-        Gather(qkv_zero, qkv_full, sems.at[2], True),
+    patch_job = Gather(kernel_full.at[mine], kernel_full, sems.at[0], True, in_place=True)
+    vector_job = Gather(vectors, vectors_full, sems.at[1], False)
+    qkv_job = Gather(qkv_zero, qkv_full, sems.at[2], True)
+    level_jobs = [
         LevelGather(up_zero, up_level, sems.at[3]),
         LevelGather(qkv_one, qkv_level, sems.at[4]),
         LevelGather(output_one, output_level, sems.at[5]),
     ]
+    copies[0].wait()
+    kernel_full[mine] = wide_kernel[...].astype(LOW)
     greet()
-    jobs[1].first()
-    copies[0].wait()
-    kernel_low[...] = wide_kernel[...].astype(LOW)
-    jobs[0].first()
+    patch_job.first()
+    vector_job.first()
     copies[1].wait()
     qkv_zero[...] = wide_inputs[0, :, : 3 * D].astype(LOW)
-    jobs[2].first()
+    qkv_job.first()
     up_zero[...] = wide_inputs[0, :, 3 * D :].astype(LOW)
-    jobs[3].first()
+    level_jobs[0].first()
     copies[3].wait()
     qkv_one[...] = wide_inputs[1, :, : 3 * D].astype(LOW)
-    jobs[4].first()
+    level_jobs[1].first()
     copies[2].wait()
     output_one[...] = wide_outputs[1].astype(LOW)
-    jobs[5].first()
-    run_stages(jobs[:3], ("second",))
+    level_jobs[2].first()
+
+    weights = position_weights(seg_col[...], patch_row[...], table.shape[0])
+    pos_t[...] = weights.T[: pos_t.shape[0], :]
+    table_low[...] = jnp.zeros_like(table_low)
+    table_low[: table.shape[0], :] = table[...].astype(LOW).astype(jnp.float32)
+    bias = biases[:, :D].astype(LOW).astype(jnp.float32)
+    stream[...] = bias + jnp.dot(
+        weights, table_low[...], precision=HIGHEST, preferred_element_type=jnp.float32
+    )
+    copies[4].wait()
+    depth = wide_kernel.shape[0]
+
+    def add_block(slot):
+        columns = pl.ds(pl.multiple_of(slot * depth, depth), depth)
+
+        def add(step, carry):
+            rows = pl.ds(pl.multiple_of(step * 256, 256), 256)
+            stream[rows, :] += mul(pixel_rows[rows, columns], kernel_full[slot])
+            return carry
+
+        lax.fori_loop(0, stream.shape[0] // 256, add, 0)
+
+    def use(turn, own_core):
+        add_block(2 * partner(level, turn) + (core if own_core else 1 - core))
+
+    add_block(mine)
+    patch_job.second()
+    vector_job.second()
+    qkv_job.second()
+    patch_job.core_copy(0).wait_recv()
+    use(0, False)
     up_one[...] = wide_inputs[1, :, 3 * D :].astype(LOW)
-    copies[4].wait()
+    copies[5].wait()
     output_zero[...] = wide_outputs[0].astype(LOW)
-    copies[5].wait()
-    head_low[...] = wide_head[...].astype(LOW)
-    run_stages(jobs[:3], ("third",))
-    run_stages(jobs, ("fourth",))
-
-
-def gather_first(patch_kernel, vectors, input_proj, output_proj, head_weight):
+    copies[6].wait()
+    head_low[...] = jnp.zeros_like(head_low)
+    head_low[:, : head.shape[1]] = wide_head[...].astype(LOW)
+    patch_job.third(use)
+    qkv_job.third()
+    patch_job.fourth(use)
+    vector_job.third()
+    vector_job.fourth()
+    blocks = [vectors_full[slot].astype(jnp.float32) for slot in range(vectors_full.shape[0])]
+    span = vectors.shape[0] // LAYERS
+    for layer, out in enumerate((vector_zero, vector_one)):
+        for row in range(out.shape[1] // LANES):
+            parts = [
+                block[layer * span + row - spot : layer * span + row - spot + 1, :]
+                for block, spot in zip(blocks, spots)
+                if 0 <= row - spot < span
+            ]
+            out[:, row * LANES : (row + 1) * LANES] = sum(parts)
+    run_stages([qkv_job, *level_jobs], ("fourth",))
+
+
+def padded_vectors(shard):
+    layers, width = shard.shape
+    owners = lax.axis_size("fsdp")
+    spots = [owner * width // LANES for owner in range(owners)]
+    span = max(-(-(owner + 1) * width // LANES) - spot for owner, spot in enumerate(spots))
+    span += -span % 16
+    shift = lax.rem(lax.axis_index("fsdp") * width, LANES)
+    padded = jnp.zeros((layers, span * LANES), LOW)
+    padded = lax.dynamic_update_slice(padded, shard.astype(LOW), (0, shift))
+    return padded.reshape(layers * span, LANES), spots
+
+
+def begin(
+    pixels, segment, patch_size, patch_kernel, layer_vector, input_proj, output_proj, head_weight,
+    position_table, global_vector,
+):
+    classes = head_weight.shape[1] + -head_weight.shape[1] % LANES
+    nodes = position_table.shape[0] + -position_table.shape[0] % 64
     if not with_kernels():
         inputs = [
             (input_proj[index, :, : 3 * D].astype(LOW), input_proj[index, :, 3 * D :].astype(LOW))
             for index in range(LAYERS)
         ]
         outputs = [output_proj[index].astype(LOW) for index in range(LAYERS)]
-        whole = [patch_kernel.astype(LOW), vectors, inputs[0][0]]
+        gather = lambda shard, axis: lax.all_gather(shard, "fsdp", axis=axis, tiled=True)
+        weights, _, _ = row_layout(segment, patch_size[0])
+        weights = jnp.pad(weights, ((0, 0), (0, nodes - weights.shape[1])))
+        table = jnp.pad(rounded(position_table), ((0, nodes - position_table.shape[0]), (0, 0)))
+        bias = rounded(global_vector)[None, :D]
+        stream = embed(pixels, gather(patch_kernel.astype(LOW), 0), weights, table, bias)
+        vectors = gather(layer_vector.astype(LOW), 1).astype(jnp.float32)
+        head = jnp.pad(head_weight.astype(LOW), ((0, 0), (0, classes - head_weight.shape[1])))
         return (
-            [lax.all_gather(shard, "fsdp", axis=0, tiled=True) for shard in whole],
+            stream,
+            weights.T,
+            [vectors[index : index + 1] for index in range(LAYERS)],
+            gather(inputs[0][0], 0),
             [GatherRide(shard, shard) for shard in (inputs[0][1], inputs[1][0], outputs[1])],
-            [outputs[0], inputs[1][1], head_weight.astype(LOW)],
-        )
+            [outputs[0], inputs[1][1], head],
+        )
+    rows = pixels.shape[0]
     owners = lax.axis_size("fsdp")
+    vectors, spots = padded_vectors(layer_vector)
     depth = input_proj.shape[1]
     up_shape = (depth, input_proj.shape[2] - 3 * D)
     qkv_shape, out_shape = (depth, 3 * D), output_proj.shape[1:]
     low = lambda *shape: jax.ShapeDtypeStruct(shape, LOW)
     levels = lambda shape: low(4, *quarter_shape(*shape))
+    width = layer_vector.shape[1] * owners
     shapes = [
-        low(owners, *patch_kernel.shape),
-        low(owners, *vectors.shape),
+        shape_of(rows, D),
+        shape_of(nodes, rows),
+        shape_of(1, width),
+        shape_of(1, width),
         low(owners, *qkv_shape),
         levels(up_shape),
         levels(qkv_shape),
@@ -532,34 +643,51 @@
         low(*qkv_shape),
         low(*up_shape),
         low(*out_shape),
-        low(*head_weight.shape),
+        low(head_weight.shape[0], classes),
     ]
-    wide = (patch_kernel, input_proj, output_proj, head_weight)
+    wide = (patch_kernel, input_proj, output_proj, head_weight, pixels)
+    in_vmem = pl.BlockSpec(memory_space=pltpu.VMEM)
     results = pl.pallas_call(
-        gather_kernel,
-        in_specs=[ANYWHERE] * 5,
-        out_specs=[ANYWHERE] * 6 + [pl.BlockSpec(memory_space=pltpu.VMEM)] * 6,
+        functools.partial(first_kernel, spots=spots),
+        in_specs=[ANYWHERE] * 6 + [in_vmem] * 4,
+        out_specs=[in_vmem] * 4 + [ANYWHERE] * 4 + [in_vmem] * 6,
         out_shape=shapes,
         scratch_shapes=[
             *[pltpu.VMEM(array.shape, array.dtype) for array in wide],
-            pltpu.VMEM(patch_kernel.shape, LOW),
+            pltpu.VMEM((LANES, D), jnp.float32),
+            pltpu.VMEM((owners, *patch_kernel.shape), LOW),
             pltpu.VMEM(qkv_shape, LOW),
-            pltpu.SemaphoreType.DMA((6,)),
+            pltpu.VMEM((owners, *vectors.shape), LOW),
+            pltpu.SemaphoreType.DMA((7,)),
             pltpu.SemaphoreType.DMA((6, GATHER_SEMS)),
         ],
         compiler_params=pltpu.CompilerParams(
-            collective_id=1, has_side_effects=True, vmem_limit_bytes=32 * MIB
+            collective_id=1, has_side_effects=True, vmem_limit_bytes=VMEM_LIMIT
         ),
         cost_estimate=NO_COST,
-        name="gather_weights",
-    )(patch_kernel, vectors, input_proj, output_proj, head_weight)
-    up_zero, output_zero, qkv_one, up_one, output_one, head_low = results[6:]
+        name="begin",
+    )(
+        patch_kernel,
+        vectors,
+        input_proj,
+        output_proj,
+        head_weight,
+        pixels,
+        segment[:, None],
+        patch_size,
+        position_table,
+        global_vector[None, :],
+    )
+    up_zero, output_zero, qkv_one, up_one, output_one, head_low = results[8:]
     return (
-        [full.reshape(owners * full.shape[1], full.shape[2]) for full in results[:3]],
+        results[0],
+        results[1],
+        results[2:4],
+        results[4].reshape(owners * depth, 3 * D),
         [
-            GatherRide(up_zero, results[3]),
-            GatherRide(qkv_one, results[4]),
-            GatherRide(output_one, results[5]),
+            GatherRide(up_zero, results[5]),
+            GatherRide(qkv_one, results[6]),
+            GatherRide(output_one, results[7]),
         ],
         [output_zero, up_one, head_low],
     )
@@ -1261,7 +1389,6 @@
             shape_of(rows, D),
         ],
         [],
-        26,
         "attention_forward",
         work(16 * HEADS * rows * rows * HD, 2 * HEADS * rows * rows + 12 * rows * D),
         rides,
@@ -1340,7 +1467,6 @@
         [fixed(rows, 3 * D)],
         [shape_of(rows, 3 * D, dtype=LOW)],
         [],
-        34,
         "attention_backward",
         None,
         rides,
@@ -1429,7 +1555,6 @@
         [rows_of(block, D)],
         [shape_of(rows, D)],
         [],
-        18,
         "embed",
         work(2 * rows * depth * D, 2 * rows * depth + 2 * depth * D + 4 * rows * D),
     )[0]
@@ -1455,7 +1580,6 @@
         [rows_of(block, D), rows_of(block, 3 * D)],
         [shape_of(rows, D, dtype=low), shape_of(rows, 3 * D, dtype=low)],
         [],
-        16,
         "qkv_forward",
         work(6 * rows * D * D, 14 * rows * D + 6 * D * D),
     )
@@ -1530,7 +1654,6 @@
             pltpu.VMEM((width, D), low),
             pltpu.SemaphoreType.DMA((3,)),
         ],
-        30,
         "mlp_forward",
         work(2 * rows * D * (D + 2 * width), rows * (16 * D + 4 * width) + 2 * D * (D + 2 * width)),
         rides,
@@ -1614,7 +1737,6 @@
             pltpu.VMEM((width, D), low),
             pltpu.SemaphoreType.DMA((3,)),
         ],
-        30,
         "mlp_backward",
         None,
     )
@@ -1640,7 +1762,6 @@
         [narrow, fixed(1, 5 * D)],
         [shape_of(rows, D), shape_of(1, 5 * D)],
         [],
-        16,
         "qkv_backward",
         None,
     )
@@ -1688,7 +1809,6 @@
             shape_of(D, hidden_grad.shape[1], dtype=jnp.bfloat16),
         ],
         [pltpu.VMEM((D, rows), jnp.bfloat16)],
-        24,
         "input_weight_grad",
         None,
     )
@@ -1730,7 +1850,6 @@
         [rows_of(block, part) for part in parts],
         [shape_of(steps * block, part, dtype=LOW) for part in parts],
         [],
-        24,
         "output_weight_grad",
     )
 
@@ -1761,10 +1880,68 @@
         [rows_of(block, D), fixed(nodes, D), fixed(1, D)],
         [shape_of(depth, D, dtype=jnp.bfloat16), shape_of(nodes, D), shape_of(1, D)],
         [pltpu.VMEM((rows, D), jnp.bfloat16)],
-        20,
         "embed_backward",
         None,
     )
+
+
+def head_kernel(
+    stream_ref, seg_col_ref, seg_row_ref, label_ref, weight_ref, vector_ref,
+    grad_ref, weight_grad_ref, sums_ref, bias_grad_ref, numbers_ref, *, classes,
+):
+    padded = weight_ref.shape[1]
+    vector = vector_ref[...].astype(LOW).astype(jnp.float32)
+    gain, shift = vector[:, D : 2 * D], vector[:, 2 * D : 3 * D]
+    slots = lax.broadcasted_iota(jnp.int32, (IMGS, 1), 0)
+    member = (seg_row_ref[...] == slots).astype(jnp.float32)
+    counts = jnp.sum(member, 1, keepdims=True)
+    sizes = jnp.maximum(counts, 1.0)
+    unit, inverse = normalized(stream_ref[...])
+    final = unit * gain + shift
+    pooled = jnp.dot(member, final, precision=HIGHEST, preferred_element_type=jnp.float32)
+    pooled = (pooled / sizes).astype(LOW)
+    class_at = lax.broadcasted_iota(jnp.int32, (IMGS, padded), 1)
+    logits = mul(pooled, weight_ref[...]) + vector[:, 3 * D :]
+    logits = jnp.where(class_at < classes, logits, MASKED)
+    highest = jnp.max(logits, -1, keepdims=True)
+    exponent = jnp.exp(logits - highest)
+    totals = jnp.sum(exponent, -1, keepdims=True)
+    onehot = class_at == label_ref[...]
+    picked = jnp.sum(jnp.where(onehot, logits, 0.0), 1, keepdims=True)
+    loss = jnp.sum(counts * (highest + jnp.log(totals) - picked), 0, keepdims=True)
+    numbers_ref[...] = jnp.concatenate([loss, jnp.sum(counts, 0, keepdims=True)], 1)
+    logits_grad = ((exponent / totals - onehot.astype(jnp.float32)) * counts).astype(LOW)
+    bias_grad_ref[...] = column_sum(logits_grad)
+    weight_grad_ref[...] = lax.dot_general(
+        pooled, logits_grad, (((0,), (0,)), ((), ())), preferred_element_type=jnp.float32
+    ).astype(LOW)
+    pooled_grad = mul_nt(logits_grad, weight_ref[...]) / sizes
+    own = (seg_col_ref[...] == lax.broadcasted_iota(jnp.int32, (1, IMGS), 1)).astype(jnp.float32)
+    final_grad = jnp.dot(own, pooled_grad, precision=HIGHEST, preferred_element_type=jnp.float32)
+    inner = final_grad * gain
+    mean_inner = jnp.mean(inner, -1, keepdims=True)
+    mean_cross = jnp.mean(inner * unit, -1, keepdims=True)
+    grad_ref[...] = inverse * (inner - mean_inner - unit * mean_cross)
+    sums_ref[...] = jnp.concatenate([column_sum(final_grad * unit), column_sum(final_grad)], 1)
+
+
+def head(stream, segment, labels, weight, global_vector, classes):
+    rows = stream.shape[0]
+    padded = weight.shape[1]
+    vector = jnp.pad(global_vector, (0, padded - classes))[None, :]
+    return pl.pallas_call(
+        functools.partial(head_kernel, classes=classes),
+        out_shape=[
+            shape_of(rows, D),
+            shape_of(D, padded, dtype=LOW),
+            shape_of(1, 2 * D),
+            shape_of(1, padded),
+            shape_of(1, 2),
+        ],
+        compiler_params=pltpu.CompilerParams(vmem_limit_bytes=VMEM_LIMIT),
+        cost_estimate=NO_COST,
+        name="head",
+    )(stream, segment[:, None], segment[None, :], labels.reshape(IMGS, 1), weight, vector)
 
 
 def adam_update(gradient, moment, square, weight, factor, learn_rate):
@@ -1806,28 +1983,25 @@
     position_square,
     global_square,
 ):
-    pos_weights, member, counts = row_layout(segment, patch_size[0])
     owners = lax.axis_size("fsdp")
-    nodes = pos_weights.shape[1]
-    pos_weights = jnp.pad(pos_weights, ((0, 0), (0, -nodes % 64)))
+    nodes = position_table.shape[0]
     vector_size = layer_vector.size
-    (kernel_full, vectors, qkv_zero), rides, rest_shards = gather_first(
+    stream, pos_weights_t, vectors, qkv_weight, rides, rest_shards = begin(
+        pixels,
+        segment,
+        patch_size,
         patch_kernel,
-        padded_rows(layer_vector.astype(LOW).reshape(-1), 32),
+        layer_vector,
         input_proj,
         output_proj,
         head_weight,
-    )
-    vectors = vectors.reshape(owners, -1)[:, :vector_size].reshape(owners, *layer_vector.shape)
-    vectors = jnp.swapaxes(vectors, 0, 1).reshape(LAYERS, 1, -1).astype(jnp.float32)
+        position_table,
+        global_vector,
+    )
     output_zero, up_one, head_full = (
         lax.all_gather(shard, "fsdp", axis=0, tiled=True) for shard in rest_shards
     )
-    global_low = rounded(global_vector)
-    position_low = jnp.pad(rounded(position_table), ((0, -nodes % 64), (0, 0)))
-    stream = embed(pixels, kernel_full, pos_weights, position_low, global_low[None, :D])
     saved_layers = []
-    qkv_weight = qkv_zero
     for index in range(LAYERS):
         vector = vectors[index]
         normed, qkv_rows = qkv_forward(stream, qkv_weight, vector)
@@ -1848,29 +2022,10 @@
         stream = following
         if fetched:
             (qkv_weight,) = fetched
-    final_norm, final_back = jax.vjp(
-        layer_norm, stream, global_low[D : 2 * D], global_low[2 * D : 3 * D]
-    )
-    image_sizes = jnp.maximum(counts, 1.0)
-    pooled = (jnp.dot(member.T, final_norm, precision=HIGHEST) / image_sizes[:, None]).astype(
-        jnp.bfloat16
-    )
-    logits = matmul(pooled, head_full) + global_low[3 * D :]
-    highest = jnp.max(logits, -1, keepdims=True)
-    exponent = jnp.exp(logits - highest)
-    totals = jnp.sum(exponent, -1, keepdims=True)
-    logsum = (highest + jnp.log(totals))[:, 0]
-    onehot = labels[0][:, None] == jnp.arange(CLS, dtype=jnp.int32)[None, :]
-    picked = jnp.sum(jnp.where(onehot, logits, 0.0), 1)
-    loss_local = jnp.sum(counts * (logsum - picked))
-    logits_grad = ((exponent / totals - onehot.astype(jnp.float32)) * counts[:, None]).astype(
-        jnp.bfloat16
-    )
-    head_grad = matmul(pooled.T, logits_grad).astype(LOW)
-    head_part = scatter(by_owner(jnp.pad(head_grad, ((0, 0), (0, -CLS % LANES)))))
-    pooled_grad = matmul(logits_grad, head_full.T)
-    final_grad = jnp.dot(member, pooled_grad / image_sizes[:, None], precision=HIGHEST)
-    stream_grad, final_gain, final_shift = final_back(final_grad)
+    stream_grad, head_grad, final_sums, head_bias_grad, numbers = head(
+        stream, segment, labels, head_full, global_vector, head_weight.shape[1]
+    )
+    head_part = scatter(by_owner(head_grad))
     vector_grads = [None] * LAYERS
     early_parts, late_parts = [head_part], []
     for index in reversed(range(LAYERS)):
@@ -1911,7 +2066,7 @@
                 mlp_sums[0, 2 * D :],
             ]
         )
-    kernel_grad, position_grad, bias_grad = embed_backward(pixels, stream_grad, pos_weights.T)
+    kernel_grad, position_grad, bias_grad = embed_backward(pixels, stream_grad, pos_weights_t)
     position_grad = position_grad[:nodes]
     vector_part = jnp.stack(vector_grads).reshape(LAYERS, owners, -1)
     vector_part = jnp.swapaxes(vector_part, 0, 1).reshape(owners, vector_size)
@@ -1921,11 +2076,9 @@
         [
             position_grad.reshape(-1),
             bias_grad[0],
-            final_gain,
-            final_shift,
-            jnp.sum(logits_grad.astype(jnp.float32), 0),
-            loss_local[None],
-            jnp.sum(counts)[None],
+            final_sums[0],
+            head_bias_grad[0, :CLS],
+            numbers[0],
         ]
     )
     rest_rows = -(-rest.shape[0] // (owners * LANES))

time: 758 us -> 733 us (0.967)
  local copies, waits for them, and re-layouts: 132 us -> 14.5 us
  Pallas kernels: 521 us -> 619 us
  waiting for transfers between devices: 20.7 us -> 39.2 us
  other arithmetic: 46.6 us -> 31.9 us
  matrix products: 10.1 us -> 0 us
    unnamed x287 -> x54, local copies, waits for them, and re-layouts: 106 us -> 1.57 us
    pallas_call x18 -> x17, Pallas kernels: 306 us -> 389 us  [block_call(): pl.pallas_call(kernel, grid=(grid,), in_specs=in_specs, out_specs=out_spe...]
    pallas_call x1 -> x2, Pallas kernels: 68.7 us -> 83.8 us  [the longest x1 72.2 us: begin(): pl.pallas_call(functools.partial(first_kernel, spots=spots), in_specs=[AN...]
    reduce_scatter x7, waiting for transfers between devices: 17.3 us -> 31.3 us  [scatter(): return lax.psum_scatter(grad, 'fsdp', scatter_dimension=0)]
    dot_general x5 -> x0, matrix products: 10.1 us -> none  [the longest x3 5.5 us: matmul(): return jnp.dot(left, right, preferred_element_type=jnp.float32)]
  transfers between devices with their start and end apart: 10 -> 10, of which waited for: 2 -> 3; matrix products, arithmetic and copies ran while one was open for 6% -> 1% of each run, Pallas kernels for 55% -> 69%
where the time goes in v7:
time: 733 us; the launch traced here: 726 us
  Pallas kernels  619 us (84%)
  waiting for transfers between devices  39.2 us (5%)
  other arithmetic  31.9 us (4%)
  between operations  21 us (3%)
  local copies, waits for them, and re-layouts  14.5 us (2%)
    pallas_call x17, Pallas kernels, block_call(): pl.pallas_call(kernel, grid=(grid,), in_specs=in_specs, out_specs=out_spe...  389 us
    pallas_call x1, Pallas kernels, reduce_call(): pl.pallas_call(functools.partial(reduce_kernel, whole=whole, partly=partl...  108 us
    pallas_call x1, Pallas kernels, begin(): pl.pallas_call(functools.partial(first_kernel, spots=spots), in_specs=[AN...  72.2 us
    pallas_call x1, Pallas kernels, finish_call(): pl.pallas_call(functools.partial(finish_kernel, done=done, partly=partly)...  37.6 us
    reduce_scatter x7, waiting for transfers between devices, scatter(): return lax.psum_scatter(grad, 'fsdp', scatter_dimension=0)  31.3 us
    sub x7, other arithmetic, adam_update(): return (moment, square, weight - learn_rate * step_dir)  22.8 us
  transfers between devices with their start and end apart: 10, of which 3 were waited for; matrix products, arithmetic and copies ran while one was open for 1% of the time, Pallas kernels for 69%

profile of v7, /device:TPU:0, one launch (start us, length us, event | category | flops | bytes accessed | tf_op | source)
XLA Modules:
  0.0 725.9 jit_solution(11584270452285393730)
XLA Ops:
  7.2 0.7 convert_element_type.23
  8.0 0.2 dynamic_update_slice.3
  8.2 0.6 reshape.125.refs_1_
  8.8 1.3 broadcast_in_dim.22.refs_9_
  10.2 1.7 copy.50.refs_6_.refs_3_.seg_col_ref
  11.9 72.2 %begin.1 = (f32[1024,768]{1,0:T(8,128)}, f32[64,1024]{1,0:T(8,128)}, f32[1,9984]{1,0:T(1,128)}, f32[1,9984]{1,0:T(1,128)}, bf16[8,96,2304]{2,1,0:T(8,128)(2,1)},...) custom-call(f32[384,768]{1,0:T(8,128)} %refs_0_.1, ...), custom_call_target="tpu_custom_call" | custom-call | tf_op jit(solution)/shard_map/begin/pallas_call | solution.py:650
  84.1 0.7 all-gather.6.cloned.1.call-update
  84.9 0.7 all-gather.8.cloned.1.call-update
  85.5 0.2 reduce-scatter.8.cloned.1.call-start
  85.8 0.7 copy.54.label_ref
  86.5 0.6 broadcast_in_dim.24.vector_ref
  87.1 8.9 %qkv_forward.2 = (bf16[1024,768]{1,0:T(8,128)(2,1)}, bf16[1024,2304]{1,0:T(8,128)(2,1)}) custom-call(f32[1024,768]{1,0:T(8,128)} %get-tuple-element.114.stream_ref.refs_0_, bf16[768,2304]{1,0:T(8,128)(2,1)} %bitcast.51, f32[1,9984]{1,0:T(1,128)} %get-tuple-element.116.vector_ref.refs_4_), custom_call_target="tpu_custom_call" | custom-call | flops 3623878656 | bytes 14548992 | tf_op jit(solution)/shard_map/qkv_forward/pallas_call | solution.py:433
  96.0 46.5 %attention_forward.2 = (bf16[1024,768]{1,0:T(8,128)(2,1)}, bf16[12,1024,1024]{2,1,0:T(8,128)(2,1)}, f32[1024,768]{1,0:T(8,128)}, bf16[8,96,3072]{2,1,0:T(8,128)(2,1)}) custom-call(bf16[1024,2304]{1,0:T(8,128)(2,1)} %get-tuple-element.117.refs_0_.refs_1_.refs_2_, bf16[1024,2304]{1,0:T(8,128)(2,1)} %get-tuple-element.117.refs_0_.refs_1_.refs_2_, ...), custom_call_target="tpu_custom_call" | custom-call | flops 12884901888 | bytes 34603008 | tf_op jit(solution)/shard_map/attention_forward/pallas_call | solution.py:433
  142.4 4.5 all-gather.4.cloned.1.call-done.refs_3_.proj_out
  147.0 41.4 %mlp_forward.2 = (f32[1024,768]{1,0:T(8,128)}, bf16[1024,768]{1,0:T(8,128)(2,1)}, bf16[1024,3072]{1,0:T(8,128)(2,1)}, bf16[1024,3072]{1,0:T(8,128)(2,1)}, f32[10...) custom-call(f32[1024,768]{1,0:T(8,128)} %get-tuple-element.114.stream_ref.refs_0_, ...), custom_call_target="tpu_custom_call" | custom-call | flops 10871635968 | bytes 35782656 | tf_op jit(solution)/shard_map/mlp_forward/pallas_call | solution.py:433
  188.4 9.0 %qkv_forward.3 = (bf16[1024,768]{1,0:T(8,128)(2,1)}, bf16[1024,2304]{1,0:T(8,128)(2,1)}) custom-call(f32[1024,768]{1,0:T(8,128)} %get-tuple-element.127.stream_ref, bf16[768,2304]{1,0:T(8,128)(2,1)} %bitcast.54, f32[1,9984]{1,0:T(1,128)} %get-tuple-element.129.vector_ref), custom_call_target="tpu_custom_call" | custom-call | flops 3623878656 | bytes 14548992 | tf_op jit(solution)/shard_map/qkv_forward/pallas_call | solution.py:433
  197.4 52.1 %attention_forward.3 = (bf16[1024,768]{1,0:T(8,128)(2,1)}, bf16[12,1024,1024]{2,1,0:T(8,128)(2,1)}, f32[1024,768]{1,0:T(8,128)}, bf16[8,480,768]{2,1,0:T(8,128)(2,1)}) custom-call(bf16[1024,2304]{1,0:T(8,128)(2,1)} %get-tuple-element.130.refs_0_.refs_1_.refs_2_.q_ref.k_ref.v_ref, ...), custom_call_target="tpu_custom_call" | custom-call | flops 12884901888 | bytes 34603008 | tf_op jit(solution)/shard_map/attention_forward/pallas_call | solution.py:433
  249.6 25.2 %mlp_forward.3 = (f32[1024,768]{1,0:T(8,128)}, bf16[1024,768]{1,0:T(8,128)(2,1)}, bf16[1024,3072]{1,0:T(8,128)(2,1)}, bf16[1024,3072]{1,0:T(8,128)(2,1)}, f32[1024,768]{1,0:T(8,128)}) custom-call(f32[1024,768]{1,0:T(8,128)} %get-tuple-element.127.stream_ref, bf16[1024,768]{1,0:T(8,128)(2,1)} %get-tuple-element.135.attended_ref.out_ref, ...), custom_call_target="tpu_custom_call" | custom-call | flops 10871635968 | bytes 35782656 | tf_op jit(solution)/shard_map/mlp_forward/pallas_call | solution.py:433
  274.8 11.7 %head.1 = (f32[1024,768]{1,0:T(8,128)}, bf16[768,1024]{1,0:T(8,128)(2,1)}, f32[1,1536]{1,0:T(1,128)}, f32[1,1024]{1,0:T(1,128)}, f32[1,2]{1,0:T(1,128)}) custom-call(f32[1024,768]{1,0:T(8,128)} %get-tuple-element.138.stream_ref, s32[1024,1]{1,0:T(8,128)} %copy.50.refs_6_.refs_3_.seg_col_ref, s32[1,1024]{1,0:T(1,128)} %bitcast.77, s32[8,1]{1,0:T(8,128)} %copy.54.label_ref, ...), custom_call_target="tpu_custom_call" | custom-call | tf_op jit(solution)/shard_map/head/pallas_call | solution.py:1932
  286.6 25.3 %mlp_backward.2 = (bf16[1024,768]{1,0:T(8,128)(2,1)}, bf16[1024,3072]{1,0:T(8,128)(2,1)}, f32[1024,768]{1,0:T(8,128)}, bf16[1024,768]{1,0:T(8,128)(2,1)}, bf16[1024,768]{1,0:T(8,128)(2,1)}, /*index=5*/f32[1,6144]{1,0:T(1,128)}) custom-call(f32[1024,768]{1,0:T(8,128)} %get-tuple-element.140.grad_ref, bf16[1024,3072]{1,0:T(8,128)(2,1)} %get-tuple-element.141.slope_ref, ...), custom_call_target="tpu_custom_call" | custom-call | tf_op jit(solution)/shard_map/mlp_backward/pallas_call | solution.py:433
  311.9 12.0 %output_weight_grad.2 = (bf16[3840,256]{1,0:T(8,128)(2,1)}, bf16[3840,256]{1,0:T(8,128)(2,1)}, bf16[3840,256]{1,0:T(8,128)(2,1)}) custom-call(bf16[1024,768]{1,0:T(8,128)(2,1)} %get-tuple-element.135.attended_ref.out_ref, bf16[1024,3072]{1,0:T(8,128)(2,1)} %get-tuple-element.144.active_ref, bf16[1024,768]{1,0:T(8,128)(2,1)} %get-tuple-element.145.residual_ref, ...), custom_call_target="tpu_custom_call" | custom-call | tf_op jit(solution)/shard_map/output_weight_grad/pallas_call | solution.py:433
  323.9 0.5 reduce-scatter.12.cloned.1.call-update
  324.5 0.7 reduce-scatter.14.cloned.1.call-update
  325.3 28.8 %attention_backward.2.grad_ref.qkv_ref = bf16[1024,2304]{1,0:T(8,128)(2,1)} custom-call(bf16[1024,2304]{1,0:T(8,128)(2,1)} %get-tuple-element.130.refs_0_.refs_1_.refs_2_.q_ref.k_ref.v_ref, bf16[1024,2304]{1,0:T(8,128)(2,1)} %get-tuple-element.130.refs_0_.refs_1_.refs_2_.q_ref.k_ref.v_ref, ...), custom_call_target="tpu_custom_call" | custom-call | tf_op jit(solution)/shard_map/attention_backward/pallas_call | solution.py:433
  354.0 10.4 %qkv_backward.2 = (f32[1024,768]{1,0:T(8,128)}, f32[1,3840]{1,0:T(1,128)}) custom-call(bf16[1024,2304]{1,0:T(8,128)(2,1)} %attention_backward.2.grad_ref.qkv_ref, f32[1024,768]{1,0:T(8,128)} %get-tuple-element.151.residual_ref, f32[1024,768]{1,0:T(8,128)} %get-tuple-element.127.stream_ref, bf16[768,2304]{1,0:T(8,128)(2,1)} %bitcast.55, ...), custom_call_target="tpu_custom_call" | custom-call | tf_op jit(solution)/shard_map/qkv_backward/pallas_call | solution.py:433
  364.4 16.5 %input_weight_grad.2 = (bf16[768,2304]{1,0:T(8,128)(2,1)}, bf16[768,3072]{1,0:T(8,128)(2,1)}) custom-call(bf16[1024,768]{1,0:T(8,128)(2,1)} %get-tuple-element.153.first_ref, bf16[1024,768]{1,0:T(8,128)(2,1)} %get-tuple-element.154.second_ref, bf16[1024,2304]{1,0:T(8,128)(2,1)} %attention_backward.2.grad_ref.qkv_ref, ...), custom_call_target="tpu_custom_call" | custom-call | tf_op jit(solution)/shard_map/input_weight_grad/pallas_call | solution.py:433
  381.0 0.7 reduce-scatter.18.cloned.1.call-update
  381.7 25.0 %mlp_backward.3 = (bf16[1024,768]{1,0:T(8,128)(2,1)}, bf16[1024,3072]{1,0:T(8,128)(2,1)}, f32[1024,768]{1,0:T(8,128)}, bf16[1024,768]{1,0:T(8,128)(2,1)}, bf16[1024,768]{1,0:T(8,128)(2,1)}, /*index=5*/f32[1,6144]{1,0:T(1,128)}) custom-call(f32[1024,768]{1,0:T(8,128)} %get-tuple-element.158.grad_ref, bf16[1024,3072]{1,0:T(8,128)(2,1)} %get-tuple-element.159.slope_ref, ...), custom_call_target="tpu_custom_call" | custom-call | tf_op jit(solution)/shard_map/mlp_backward/pallas_call | solution.py:433
  406.7 12.0 %output_weight_grad.3 = bf16[3840,768]{1,0:T(8,128)(2,1)} custom-call(bf16[1024,768]{1,0:T(8,128)(2,1)} %get-tuple-element.122.refs_1_.attended_ref.refs_5_, bf16[1024,3072]{1,0:T(8,128)(2,1)} %get-tuple-element.162.active_ref, bf16[1024,768]{1,0:T(8,128)(2,1)} %get-tuple-element.163.residual_ref, bf16[1024,768]{1,0:T(8,128)(2,1)} %get-tuple-element.164.grad_ref), custom_call_target="tpu_custom_call" | custom-call | tf_op jit(solution)/shard_map/output_weight_grad/pallas_call | solution.py:433
  418.8 0.7 copy-done.20
  419.6 0.1 stack.28
  419.9 11.7 %reduce-scatter.14.cloned.1.call-done = bf16[1,480,256]{2,1,0:T(8,128)(2,1)} async-done(((bf16[8,480,256]{2,1,0:T(8,128)(2,1)}), bf16[1,480,256]{2,1,0:T(8,128)(2,1)}) %reduce-scatter.14.cloned.1.call-update) | async-done | bytes 245776 | tf_op jit(solution)/shard_map/reduce_scatter | solution.py:1334
  431.6 37.0 %attention_backward.3 = (bf16[1024,2304]{1,0:T(8,128)(2,1)}, bf16[96,1024]{1,0:T(8,128)(2,1)}, bf16[480,256]{1,0:T(8,128)(2,1)}, bf16[480,256]{1,0:T(8,128)(2,1)}, bf16[480,256]{1,0:T(8,128)(2,1)}) custom-call(bf16[1024,2304]{1,0:T(8,128)(2,1)} %get-tuple-element.117.refs_0_.refs_1_.refs_2_, bf16[1024,2304]{1,0:T(8,128)(2,1)} %get-tuple-element.117.refs_0_.refs_1_.refs_2_, ...), custom_call_target="tpu_custom_call" | custom-call | tf_op jit(solution)/shard_map/attention_backward/pallas_call | solution.py:433
  468.6 10.5 %qkv_backward.3 = (f32[1024,768]{1,0:T(8,128)}, f32[1,3840]{1,0:T(1,128)}) custom-call(bf16[1024,2304]{1,0:T(8,128)(2,1)} %get-tuple-element.176.qkv_ref.grad_ref, f32[1024,768]{1,0:T(8,128)} %get-tuple-element.180.residual_ref, f32[1024,768]{1,0:T(8,128)} %get-tuple-element.114.stream_ref.refs_0_, bf16[768,2304]{1,0:T(8,128)(2,1)} %bitcast.52, ...), custom_call_target="tpu_custom_call" | custom-call | tf_op jit(solution)/shard_map/qkv_backward/pallas_call | solution.py:433
  479.1 0.7 slice_reduce_fusion.3
  479.8 0.7 slice_reduce_fusion.6
  480.8 0.1 reshape.141
  480.9 12.2 %embed_backward.1 = (bf16[3072,768]{1,0:T(8,128)(2,1)}, f32[64,768]{1,0:T(8,128)}, f32[1,768]{1,0:T(1,128)}) custom-call(bf16[1024,3072]{1,0:T(8,128)(2,1)} %pixel_ref.1, f32[1024,768]{1,0:T(8,128)} %get-tuple-element.181.grad_ref, f32[64,1024]{1,0:T(8,128)} %get-tuple-element.182.pos_ref), custom_call_target="tpu_custom_call" | custom-call | tf_op jit(solution)/shard_map/embed_backward/pallas_call | solution.py:433
  493.2 0.7 reduce.10
  493.9 0.9 slice.70
  495.1 0.7 pad.19.refs_10_
  495.8 16.3 %input_weight_grad.3 = (bf16[768,2304]{1,0:T(8,128)(2,1)}, bf16[768,3072]{1,0:T(8,128)(2,1)}) custom-call(bf16[1024,768]{1,0:T(8,128)(2,1)} %get-tuple-element.174.first_ref, bf16[1024,768]{1,0:T(8,128)(2,1)} %get-tuple-element.175.second_ref, bf16[1024,2304]{1,0:T(8,128)(2,1)} %get-tuple-element.176.qkv_ref.grad_ref, ...), custom_call_target="tpu_custom_call" | custom-call | tf_op jit(solution)/shard_map/input_weight_grad/pallas_call | solution.py:433
  512.2 0.9 maximum_bitcast_fusion.2
  513.1 19.5 %reduce-scatter.18.cloned.1.call-done = bf16[1,96,3072]{2,1,0:T(8,128)(2,1)} async-done(((bf16[8,96,3072]{2,1,0:T(8,128)(2,1)}), bf16[1,96,3072]{2,1,0:T(8,128)(2,1)}) %reduce-scatter.18.cloned.1.call-update) | async-done | bytes 589840 | tf_op jit(solution)/shard_map/reduce_scatter | solution.py:1334
  532.6 108.1 %reduce_gradients.1 = (bf16[96,2304]{1,0:T(8,128)(2,1)}, bf16[96,3072]{1,0:T(8,128)(2,1)}, bf16[384,768]{1,0:T(8,128)(2,1)}, bf16[96,2304]{1,0:T(8,128)(2,1)}, bf16[96,3072]{1,0:T(8,128)(2,1)}) custom-call(bf16[8,96,2304]{2,1,0:T(8,128)(2,1)} %bitcast.56, bf16[8,96,3072]{2,1,0:T(8,128)(2,1)} %bitcast.50, bf16[8,384,768]{2,1,0:T(8,128)(2,1)} %bitcast.49, ...), custom_call_target="tpu_custom_call" | custom-call | tf_op jit(solution)/shard_map/reduce_gradients/pallas_call | solution.py:1235
  640.7 1.6 maximum_bitcast_fusion
  642.4 37.6 %finish_gradients.1 = (bf16[480,768]{1,0:T(8,128)(2,1)}, f32[64,128]{1,0:T(8,128)}, f32[8,64,128]{2,1,0:T(8,128)}) custom-call(bf16[96,1024]{1,0:T(8,128)(2,1)} %get-tuple-element.170.refs_0_, bf16[480,256]{1,0:T(8,128)(2,1)} %get-tuple-element.171.refs_1_, bf16[480,256]{1,0:T(8,128)(2,1)} %get-tuple-element.172.refs_2_, ...), custom_call_target="tpu_custom_call" | custom-call | tf_op jit(solution)/shard_map/finish_gradients/pallas_call | solution.py:1288
  680.1 1.6 multiply_reduce_fusion.1
  681.7 1.4 slice_reduce_fusion.8
  683.1 0.9 slice.72
  684.0 0.6 multiply_reduce_fusion.2
  684.6 0.6 multiply_reduce_fusion
  685.3 0.6 fusion.15
  685.9 0.7 slice_bitcast_fusion
  691.3 0.7 slice_multiply_fusion
  692.0 1.6 mul.230
  693.6 0.6 multiply_subtract_fusion.5
  694.3 2.7 multiply_subtract_fusion.3
  697.0 3.9 multiply_subtract_fusion.2
  700.9 0.6 multiply_subtract_fusion.6
  701.6 1.9 multiply_subtract_fusion.4
  703.6 6.8 multiply_subtract_fusion.1
  710.4 0.8 copy-done.4
  711.2 6.2 multiply_subtract_fusion
  (92 shorter events, 1.4 us)
Async XLA Ops:
  7.2 139.8 %all-gather.4.cloned.1.call-start = ((), (), s32[]{:S(2)}) async-start(), calls=%async_computation.7 | async-start | bytes 6635520 | tf_op jit(solution)/shard_map/all_gather | solution.py:2002
  11.9 73.9 %copy-start.26 = (s32[1,8]{1,0:T(1,128)S(1)}, s32[1,8]{1,0:T(1,128)}, u32[]{:S(2)}) copy-start(s32[1,8]{1,0:T(1,128)} %param.28) | copy-start | bytes 100
  11.9 74.6 %copy-start.14 = (f32[3304]{0:T(1024)S(1)}, f32[3304]{0:T(1024)}, u32[]{:S(2)}) copy-start(f32[3304]{0:T(1024)} %param.35) | copy-start | bytes 39652
  84.1 165.5 %all-gather.6.cloned.1.call-start = ((), (), s32[]{:S(2)}) async-start(), calls=%async_computation.8 | async-start | bytes 5308416 | tf_op jit(solution)/shard_map/all_gather | solution.py:2002
  84.8 190.0 %all-gather.8.cloned.1.call-start = ((), (), s32[]{:S(2)}) async-start(), calls=%async_computation.9 | async-start | bytes 1769472 | tf_op jit(solution)/shard_map/all_gather | solution.py:2002
  85.5 334.3 %reduce-scatter.8.cloned.1.call-start = ((), (), s32[]{:S(2)}) async-start(), calls=%async_computation.10 | async-start | bytes 1769472 | tf_op jit(solution)/shard_map/reduce_scatter | solution.py:1334
  286.5 133.4 %reduce-scatter.10.cloned.1.call-start = ((), (), s32[]{:S(2)}) async-start(), calls=%async_computation.11 | async-start | bytes 2211840 | tf_op jit(solution)/shard_map/reduce_scatter | solution.py:1334
  323.9 96.0 %reduce-scatter.12.cloned.1.call-start = ((), (), s32[]{:S(2)}) async-start(), calls=%async_computation.12 | async-start | bytes 2211840 | tf_op jit(solution)/shard_map/reduce_scatter | solution.py:1334
  324.5 107.2 %reduce-scatter.14.cloned.1.call-start = ((), (), s32[]{:S(2)}) async-start(), calls=%async_computation.13 | async-start | bytes 2211840 | tf_op jit(solution)/shard_map/reduce_scatter | solution.py:1334
  325.2 187.9 %reduce-scatter.16.cloned.1.call-start = ((), (), s32[]{:S(2)}) async-start(), calls=%async_computation.14 | async-start | bytes 3981312 | tf_op jit(solution)/shard_map/reduce_scatter | solution.py:1334
  380.9 151.6 %reduce-scatter.18.cloned.1.call-start = ((), (), s32[]{:S(2)}) async-start(), calls=%async_computation.15 | async-start | bytes 5308416 | tf_op jit(solution)/shard_map/reduce_scatter | solution.py:1334
  381.7 260.7 %reduce-scatter.20.cloned.1.call-start = ((), (), s32[]{:S(2)}) async-start(), calls=%async_computation.16 | async-start | bytes 6635520 | tf_op jit(solution)/shard_map/reduce_scatter | solution.py:1334
  418.8 0.7 copy-start.20
  418.8 0.8 copy-start.16
  418.8 1.0 copy-start.23
  418.8 1.0 copy-start.17
  480.9 13.9 %copy-start.24 = (f32[1,1024]{1,0:T(1,128)S(1)}, f32[1,1024]{1,0:T(1,128)}, u32[]{:S(2)}) copy-start(f32[1,1024]{1,0:T(1,128)} %get-tuple-element.199) | copy-start | bytes 12292
  480.9 13.9 %copy-start.25 = (f32[1,2]{1,0:T(1,128)S(1)}, f32[1,2]{1,0:T(1,128)}, u32[]{:S(2)}) copy-start(f32[1,2]{1,0:T(1,128)} %get-tuple-element.200) | copy-start | bytes 28
  495.8 16.3 %copy-start.10 = (bf16[480,256]{1,0:T(8,128)(2,1)S(1)}, bf16[480,256]{1,0:T(8,128)(2,1)}, u32[]{:S(2)}) copy-start(bf16[480,256]{1,0:T(8,128)(2,1)} %get-tuple-element.171.refs_1_) | copy-start | bytes 737284
  495.8 16.3 %copy-start.11 = (bf16[480,256]{1,0:T(8,128)(2,1)S(1)}, bf16[480,256]{1,0:T(8,128)(2,1)}, u32[]{:S(2)}) copy-start(bf16[480,256]{1,0:T(8,128)(2,1)} %get-tuple-element.172.refs_2_) | copy-start | bytes 737284
  495.8 16.3 %copy-start.12 = (bf16[480,256]{1,0:T(8,128)(2,1)S(1)}, bf16[480,256]{1,0:T(8,128)(2,1)}, u32[]{:S(2)}) copy-start(bf16[480,256]{1,0:T(8,128)(2,1)} %get-tuple-element.173.refs_3_) | copy-start | bytes 737284
  642.4 51.3 %copy-start.18 = (f32[3304]{0:T(1024)S(1)}, f32[3304]{0:T(1024)}, u32[]{:S(2)}) copy-start(f32[3304]{0:T(1024)} %param.49) | copy-start | bytes 39652
  642.4 51.2 %copy-start.19 = (f32[3304]{0:T(1024)S(1)}, f32[3304]{0:T(1024)}, u32[]{:S(2)}) copy-start(f32[3304]{0:T(1024)} %param.42) | copy-start | bytes 39652
  642.4 58.5 %copy-start.15 = (f32[2,1248]{1,0:T(2,128)S(1)}, f32[2,1248]{1,0:T(2,128)}, u32[]{:S(2)}) copy-start(f32[2,1248]{1,0:T(2,128)} %param.33) | copy-start | bytes 29956
  642.4 58.5 %copy-start.21 = (f32[2,1248]{1,0:T(2,128)S(1)}, f32[2,1248]{1,0:T(2,128)}, u32[]{:S(2)}) copy-start(f32[2,1248]{1,0:T(2,128)} %param.47) | copy-start | bytes 29956
  642.4 58.5 %copy-start.22 = (f32[2,1248]{1,0:T(2,128)S(1)}, f32[2,1248]{1,0:T(2,128)}, u32[]{:S(2)}) copy-start(f32[2,1248]{1,0:T(2,128)} %param.40) | copy-start | bytes 29956
  680.1 16.9 %copy-start.2 = (f32[384,768]{1,0:T(8,128)S(1)}, f32[384,768]{1,0:T(8,128)}, u32[]{:S(2)}) copy-start(f32[384,768]{1,0:T(8,128)} %refs_0_.1) | copy-start | bytes 3538948
  693.6 3.3 copy-start.8
  693.6 3.3 copy-start.9
  694.3 7.3 %copy-start.13 = (f32[49,768]{1,0:T(8,128)S(1)}, f32[49,768]{1,0:T(8,128)}, u32[]{:S(2)}) copy-start(f32[49,768]{1,0:T(8,128)} %mul.230) | copy-start | bytes 451588
  694.3 9.2 %copy-start.7 = (bf16[1,480,768]{2,1,0:T(8,128)(2,1)S(1)}, bf16[1,480,768]{2,1,0:T(8,128)(2,1)}, u32[]{:S(2)}) copy-start(bf16[1,480,768]{2,1,0:T(8,128)(2,1)} %maximum_bitcast_fusion.2) | copy-start | bytes 2211844
  697.0 6.6 copy-start.1
  697.0 6.6 copy-start.5
  697.0 6.6 copy-start.6
  703.5 6.9 copy-start
  703.6 6.9 copy-start.3
  703.6 7.6 %copy-start.4 = (f32[2,96,5376]{2,1,0:T(8,128)S(1)}, f32[2,96,5376]{2,1,0:T(8,128)}, u32[]{:S(2)}) copy-start(f32[2,96,5376]{2,1,0:T(8,128)} %param.38) | copy-start | bytes 12386308
Sparse Core Ops, SparseCore 0:
  84.2 62.7 all-gather.3
  148.6 50.3 all-gather.5
  200.7 23.8 all-gather.7
  286.6 32.9 reduce-scatter.7
  324.0 34.1 reduce-scatter.9
  361.0 33.8 reduce-scatter.11
  397.8 33.7 reduce-scatter.13
  434.6 42.0 reduce-scatter.15
  479.0 53.4 reduce-scatter.17
  534.7 73.8 reduce-scatter.19

commit v8 on v7

--- a/solution.py
+++ b/solution.py
@@ -254,6 +254,11 @@
             self.level_copy(turn).wait_recv()
             self.level_copy(turn).wait_send()
 
+    def store(self):
+        _, level, _ = place()
+        self.out[level] = jnp.zeros(self.out.shape[1:], self.out.dtype)
+        self.target[...] = self.out[...]
+
 
 GROUP_GATHER_SEMS = 30
 
@@ -317,22 +322,58 @@
                 self.group_copy(turn, other).wait_send()
         self.own_copy(0).wait()
 
+    def store(self):
+        copy = pltpu.make_async_copy(self.out, self.target, self.sems.at[0])
+        copy.start()
+        copy.wait()
+
+
+class LevelRide:
+    def __init__(self, shard):
+        self.operands = [shard]
+        shape = (4, *quarter_shape(*shard.shape))
+        self.out_specs = [fixed(*shape)]
+        self.out_shapes = [jax.ShapeDtypeStruct(shape, shard.dtype)]
+        self.scratch = [pltpu.VMEM(shape, shard.dtype), pltpu.SemaphoreType.DMA((7,))]
+
+    def job(self, sources, targets, scratch):
+        job = LevelGather(sources[0], *scratch)
+        job.target = targets[0]
+        return job
+
+    def before(self, steps):
+        return {0: ("first",)}
+
+    after = ("fourth", "store")
+
+    def result(self, outs):
+        return GatherRide(self.operands[0], outs[0])
+
+    def plain(self):
+        return GatherRide(self.operands[0], self.operands[0])
+
 
 class GatherRide:
     def __init__(self, shard, quarters):
         owners = lax.axis_size("fsdp")
+        full = (owners, *shard.shape)
         self.operands = [shard, quarters]
         self.out_specs = [ANYWHERE]
-        self.out_shapes = [jax.ShapeDtypeStruct((owners, *shard.shape), shard.dtype)]
-        self.scratch = [pltpu.SemaphoreType.DMA((GROUP_GATHER_SEMS,))]
+        self.out_shapes = [jax.ShapeDtypeStruct(full, shard.dtype)]
+        self.scratch = [
+            pltpu.VMEM(full, shard.dtype),
+            pltpu.SemaphoreType.DMA((GROUP_GATHER_SEMS,)),
+        ]
 
     def job(self, sources, targets, scratch):
-        return GroupGather(*sources, *targets, *scratch)
+        job = GroupGather(*sources, *scratch)
+        job.target = targets[0]
+        return job
 
     def before(self, steps):
         return {0: ("first",), max(1, 2 * steps // 3): ("second",)}
 
-    after = ("third",)
+    after = ("third", "store")
 
     def result(self, outs):
         return outs[0].reshape(-1, outs[0].shape[2])
@@ -427,7 +468,8 @@
         kernel = riding(body, (len(operands), len(out_shape), len(scratch)), rides, grid)
     count = len(out_shape)
     for ride in rides:
-        operands, in_specs = [*operands, *ride.operands], [*in_specs, *[ANYWHERE] * len(ride.operands)]
+        operands = [*operands, *ride.operands]
+        in_specs = [*in_specs, *[fixed(*operand.shape) for operand in ride.operands]]
         out_specs, out_shape = [*out_specs, *ride.out_specs], [*out_shape, *ride.out_shapes]
         scratch = [*scratch, *ride.scratch]
     outs = pl.pallas_call(
@@ -480,19 +522,17 @@
 def first_kernel(*refs, spots):
     kernel, vectors, inputs, outputs, head, pixels, seg_col, patch_row, table, biases = refs[:10]
     stream, pos_t, vector_zero, vector_one = refs[10:14]
-    qkv_full, up_level, qkv_level, output_level = refs[14:18]
-    up_zero, output_zero, qkv_one, up_one, output_one, head_low = refs[18:24]
-    wide_kernel, wide_inputs, wide_outputs, wide_head, pixel_rows, table_low = refs[24:30]
-    kernel_full, qkv_zero, vectors_full, load_sems, sems = refs[30:]
+    qkv_full, up_level, up_zero, qkv_one, up_one, output_one, head_low = refs[14:21]
+    wide_kernel, wide_inputs, wide_outputs, wide_head, pixel_rows, table_low = refs[21:27]
+    kernel_full, qkv_zero, vectors_full, qkv_landing, up_landing, load_sems, sems = refs[27:]
     _, level, core = place()
     mine = 2 * level + core
     pairs = [
         (kernel, wide_kernel),
         (inputs.at[0], wide_inputs.at[0]),
-        (outputs.at[1], wide_outputs.at[1]),
+        (pixels, pixel_rows),
         (inputs.at[1], wide_inputs.at[1]),
-        (pixels, pixel_rows),
-        (outputs.at[0], wide_outputs.at[0]),
+        (outputs.at[1], wide_outputs),
         (head, wide_head),
     ]
     copies = [
@@ -503,12 +543,9 @@
         copy.start()
     patch_job = Gather(kernel_full.at[mine], kernel_full, sems.at[0], True, in_place=True)
     vector_job = Gather(vectors, vectors_full, sems.at[1], False)
-    qkv_job = Gather(qkv_zero, qkv_full, sems.at[2], True)
-    level_jobs = [
-        LevelGather(up_zero, up_level, sems.at[3]),
-        LevelGather(qkv_one, qkv_level, sems.at[4]),
-        LevelGather(output_one, output_level, sems.at[5]),
-    ]
+    qkv_job = Gather(qkv_zero, qkv_landing, sems.at[2], True)
+    up_job = LevelGather(up_zero, up_landing, sems.at[3])
+    up_job.target = up_level
     copies[0].wait()
     kernel_full[mine] = wide_kernel[...].astype(LOW)
     greet()
@@ -518,13 +555,7 @@
     qkv_zero[...] = wide_inputs[0, :, : 3 * D].astype(LOW)
     qkv_job.first()
     up_zero[...] = wide_inputs[0, :, 3 * D :].astype(LOW)
-    level_jobs[0].first()
-    copies[3].wait()
-    qkv_one[...] = wide_inputs[1, :, : 3 * D].astype(LOW)
-    level_jobs[1].first()
-    copies[2].wait()
-    output_one[...] = wide_outputs[1].astype(LOW)
-    level_jobs[2].first()
+    up_job.first()
 
     weights = position_weights(seg_col[...], patch_row[...], table.shape[0])
     pos_t[...] = weights.T[: pos_t.shape[0], :]
@@ -534,7 +565,7 @@
     stream[...] = bias + jnp.dot(
         weights, table_low[...], precision=HIGHEST, preferred_element_type=jnp.float32
     )
-    copies[4].wait()
+    copies[2].wait()
     depth = wide_kernel.shape[0]
 
     def add_block(slot):
@@ -556,10 +587,12 @@
     qkv_job.second()
     patch_job.core_copy(0).wait_recv()
     use(0, False)
+    copies[3].wait()
+    qkv_one[...] = wide_inputs[1, :, : 3 * D].astype(LOW)
     up_one[...] = wide_inputs[1, :, 3 * D :].astype(LOW)
+    copies[4].wait()
+    output_one[...] = wide_outputs[...].astype(LOW)
     copies[5].wait()
-    output_zero[...] = wide_outputs[0].astype(LOW)
-    copies[6].wait()
     head_low[...] = jnp.zeros_like(head_low)
     head_low[:, : head.shape[1]] = wide_head[...].astype(LOW)
     patch_job.third(use)
@@ -577,7 +610,12 @@
                 if 0 <= row - spot < span
             ]
             out[:, row * LANES : (row + 1) * LANES] = sum(parts)
-    run_stages([qkv_job, *level_jobs], ("fourth",))
+    qkv_job.fourth()
+    copy = pltpu.make_async_copy(qkv_landing, qkv_full, load_sems.at[0])
+    copy.start()
+    up_job.fourth()
+    up_job.store()
+    copy.wait()
 
 
 def padded_vectors(shard):
@@ -617,8 +655,8 @@
             weights.T,
             [vectors[index : index + 1] for index in range(LAYERS)],
             gather(inputs[0][0], 0),
-            [GatherRide(shard, shard) for shard in (inputs[0][1], inputs[1][0], outputs[1])],
-            [outputs[0], inputs[1][1], head],
+            [GatherRide(inputs[0][1], inputs[0][1]), LevelRide(inputs[1][0]), LevelRide(outputs[1])],
+            [inputs[1][1], head],
         )
     rows = pixels.shape[0]
     owners = lax.axis_size("fsdp")
@@ -636,21 +674,18 @@
         shape_of(1, width),
         low(owners, *qkv_shape),
         levels(up_shape),
-        levels(qkv_shape),
-        levels(out_shape),
         low(*up_shape),
-        low(*out_shape),
         low(*qkv_shape),
         low(*up_shape),
         low(*out_shape),
         low(head_weight.shape[0], classes),
     ]
-    wide = (patch_kernel, input_proj, output_proj, head_weight, pixels)
+    wide = (patch_kernel, input_proj, output_proj[0], head_weight, pixels)
     in_vmem = pl.BlockSpec(memory_space=pltpu.VMEM)
     results = pl.pallas_call(
         functools.partial(first_kernel, spots=spots),
         in_specs=[ANYWHERE] * 6 + [in_vmem] * 4,
-        out_specs=[in_vmem] * 4 + [ANYWHERE] * 4 + [in_vmem] * 6,
+        out_specs=[in_vmem] * 4 + [ANYWHERE] + [in_vmem] * 6,
         out_shape=shapes,
         scratch_shapes=[
             *[pltpu.VMEM(array.shape, array.dtype) for array in wide],
@@ -658,8 +693,10 @@
             pltpu.VMEM((owners, *patch_kernel.shape), LOW),
             pltpu.VMEM(qkv_shape, LOW),
             pltpu.VMEM((owners, *vectors.shape), LOW),
-            pltpu.SemaphoreType.DMA((7,)),
-            pltpu.SemaphoreType.DMA((6, GATHER_SEMS)),
+            pltpu.VMEM((owners, *qkv_shape), LOW),
+            pltpu.VMEM((4, *quarter_shape(*up_shape)), LOW),
+            pltpu.SemaphoreType.DMA((6,)),
+            pltpu.SemaphoreType.DMA((4, GATHER_SEMS)),
         ],
         compiler_params=pltpu.CompilerParams(
             collective_id=1, has_side_effects=True, vmem_limit_bytes=VMEM_LIMIT
@@ -678,18 +715,14 @@
         position_table,
         global_vector[None, :],
     )
-    up_zero, output_zero, qkv_one, up_one, output_one, head_low = results[8:]
+    up_zero, qkv_one, up_one, output_one, head_low = results[6:]
     return (
         results[0],
         results[1],
         results[2:4],
         results[4].reshape(owners * depth, 3 * D),
-        [
-            GatherRide(up_zero, results[5]),
-            GatherRide(qkv_one, results[6]),
-            GatherRide(output_one, results[7]),
-        ],
-        [output_zero, up_one, head_low],
+        [GatherRide(up_zero, results[5]), LevelRide(qkv_one), LevelRide(output_one)],
+        [up_one, head_low],
     )
 
 
@@ -1505,18 +1538,6 @@
     pl.when(pl.program_id(0) == 0)(action)
 
 
-def accumulate(out_ref, parts):
-    value = jnp.concatenate(parts, 1)
-
-    @pl.when(pl.program_id(0) == 0)
-    def _():
-        out_ref[...] = value
-
-    @pl.when(pl.program_id(0) > 0)
-    def _():
-        out_ref[...] += value
-
-
 def rows_of(block, columns):
     return pl.BlockSpec((block, columns), lambda i: (i, 0))
 
@@ -1560,99 +1581,125 @@
     )[0]
 
 
-def qkv_kernel(stream_ref, weight_ref, vector_ref, normed_ref, qkv_ref):
-    unit, _ = normalized(stream_ref[...])
-    normed = (unit * vector_ref[:, :D] + vector_ref[:, D : 2 * D]).astype(jnp.bfloat16)
-    normed_ref[...] = normed
-    bias = vector_ref[:, 4 * D : 7 * D]
-    qkv_ref[...] = (mul(normed, weight_ref[...]) + bias).astype(jnp.bfloat16)
+def chunk_at(base):
+    return pl.ds(pl.multiple_of(base + pl.program_id(0) * D, LANES), D)
+
+
+def columns_of(rows):
+    return pl.BlockSpec((rows, D), lambda i: (0, i))
+
+
+def halves_of(rows):
+    half = rows // 2
+    return [slice(start, start + half) for start in range(0, rows, half)]
+
+
+def at_last(action):
+    pl.when(pl.program_id(0) == pl.num_programs(0) - 1)(action)
+
+
+def qkv_kernel(stream_ref, weight_ref, vector_ref, normed_out, qkv_ref, normed_ref, sem):
+    copy = pltpu.make_async_copy(normed_ref, normed_out, sem)
+
+    @at_first
+    def _():
+        unit, _ = normalized(stream_ref[...])
+        normed_ref[...] = (unit * vector_ref[:, :D] + vector_ref[:, D : 2 * D]).astype(LOW)
+        copy.start()
+
+    bias = vector_ref[:, chunk_at(4 * D)]
+    for half in halves_of(stream_ref.shape[0]):
+        qkv_ref[half, :] = (mul(normed_ref[half, :], weight_ref[...]) + bias).astype(LOW)
+    at_last(copy.wait)
 
 
 def qkv_forward(stream, weight, vector):
     rows = stream.shape[0]
-    block = 256
-    low = jnp.bfloat16
     return block_call(
         qkv_kernel,
-        rows // block,
-        [rows_of(block, D), fixed(D, 3 * D), fixed(1, vector.shape[1])],
+        3,
+        [fixed(rows, D), columns_of(D), fixed(1, vector.shape[1])],
         [stream, weight, vector],
-        [rows_of(block, D), rows_of(block, 3 * D)],
-        [shape_of(rows, D, dtype=low), shape_of(rows, 3 * D, dtype=low)],
-        [],
+        [ANYWHERE, columns_of(rows)],
+        [shape_of(rows, D, dtype=LOW), shape_of(rows, 3 * D, dtype=LOW)],
+        [pltpu.VMEM((rows, D), LOW), pltpu.SemaphoreType.DMA],
         "qkv_forward",
         work(6 * rows * D * D, 14 * rows * D + 6 * D * D),
     )
 
 
 def mlp_kernel(
-    stream_ref, attended_ref, up_full, proj_out, vector_ref,
-    residual_ref, normed_ref, active_ref, slope_ref, out_ref,
-    mix_ref, up_ref, down_ref, sems,
+    stream_ref, attended_ref, mix_ref, up_ref, down_ref, vector_ref,
+    residual_out, normed_out, active_ref, slope_ref, out_ref,
+    residual_ref, normed_ref, sems,
 ):
-    width = up_ref.shape[1]
-    copies = loads(
-        (proj_out.at[pl.ds(0, D)], up_full, proj_out.at[pl.ds(D, width)]),
-        (mix_ref, up_ref, down_ref),
-        sems,
-    )
+    rows = stream_ref.shape[0]
+    copies = loads((residual_ref, normed_ref), (residual_out, normed_out), sems)
 
     @at_first
     def _():
+        for half in halves_of(rows):
+            residual = stream_ref[half, :] + mul(attended_ref[half, :], mix_ref[...])
+            residual = residual + vector_ref[:, 7 * D : 8 * D]
+            residual_ref[half, :] = residual
+            unit, _ = normalized(residual)
+            normed = unit * vector_ref[:, 2 * D : 3 * D] + vector_ref[:, 3 * D : 4 * D]
+            normed_ref[half, :] = normed.astype(LOW)
+            out_ref[half, :] = residual + vector_ref[:, 8 * D : 9 * D]
         for copy in copies:
             copy.start()
-        copies[0].wait()
-
-    residual = stream_ref[...] + mul(attended_ref[...], mix_ref[...]) + vector_ref[:, 7 * D : 8 * D]
-    residual_ref[...] = residual
-    unit, _ = normalized(residual)
-    normed = (unit * vector_ref[:, 2 * D : 3 * D] + vector_ref[:, 3 * D : 4 * D]).astype(jnp.bfloat16)
-    normed_ref[...] = normed
-    at_first(copies[1].wait)
-    part = 512
-
-    def hidden_of(base):
-        bias = vector_ref[:, 9 * D + base : 9 * D + base + part]
-        return mul(normed, up_ref[:, base : base + part]) + bias
-
-    hidden = hidden_of(0)
-    for base in range(0, width, part):
-        following = hidden_of(base + part) if base + part < width else None
-        columns = slice(base, base + part)
+
+    bias = vector_ref[:, chunk_at(9 * D)]
+    parts = halves_of(rows)
+    hidden = mul(normed_ref[parts[0], :], up_ref[...]) + bias
+    for index, half in enumerate(parts):
+        following = None
+        if index + 1 < len(parts):
+            following = mul(normed_ref[parts[index + 1], :], up_ref[...]) + bias
         square = hidden * hidden
-        half = 0.5 + 0.5 * jnp.tanh(hidden * (ROOT + (ROOT * CUBE) * square))
-        active = hidden * half
-        active_ref[:, columns] = active.astype(jnp.bfloat16)
-        rise = (2.0 * ROOT) + (6.0 * ROOT * CUBE) * square
-        slope_ref[:, columns] = (half + active * (1.0 - half) * rise).astype(jnp.bfloat16)
+        rise = 0.5 + 0.5 * jnp.tanh(hidden * (ROOT + (ROOT * CUBE) * square))
+        active = hidden * rise
+        active_low = active.astype(LOW)
+        active_ref[half, :] = active_low
+        bend = (2.0 * ROOT) + (6.0 * ROOT * CUBE) * square
+        slope_ref[half, :] = (rise + active * (1.0 - rise) * bend).astype(LOW)
+        out_ref[half, :] += mul(active_low, down_ref[...])
         hidden = following
-    at_first(copies[2].wait)
-    out_ref[...] = residual + mul(active_ref[...], down_ref[...]) + vector_ref[:, 8 * D : 9 * D]
+
+    @at_last
+    def _():
+        for copy in copies:
+            copy.wait()
+
+
+def mlp_specs(up, proj_out):
+    return (
+        [fixed(D, D), columns_of(D), pl.BlockSpec((D, D), lambda i: (i + 1, 0))],
+        [proj_out, up, proj_out],
+    )
 
 
 def mlp_forward(stream, attended, up, proj_out, vector, rides, collective_id):
     rows = stream.shape[0]
     width = up.shape[1]
-    block = 256
-    low = jnp.bfloat16
+    weight_specs, weights = mlp_specs(up, proj_out)
     return block_call(
         mlp_kernel,
-        rows // block,
-        [rows_of(block, D), rows_of(block, D), ANYWHERE, ANYWHERE, fixed(1, vector.shape[1])],
-        [stream, attended, up, proj_out, vector],
-        [rows_of(block, D), rows_of(block, D), rows_of(block, width), rows_of(block, width), rows_of(block, D)],
+        width // D,
+        [fixed(rows, D), fixed(rows, D), *weight_specs, fixed(1, vector.shape[1])],
+        [stream, attended, *weights, vector],
+        [ANYWHERE, ANYWHERE, columns_of(rows), columns_of(rows), fixed(rows, D)],
         [
             shape_of(rows, D),
-            shape_of(rows, D, dtype=low),
-            shape_of(rows, width, dtype=low),
-            shape_of(rows, width, dtype=low),
+            shape_of(rows, D, dtype=LOW),
+            shape_of(rows, width, dtype=LOW),
+            shape_of(rows, width, dtype=LOW),
             shape_of(rows, D),
         ],
         [
-            pltpu.VMEM((D, D), low),
-            pltpu.VMEM((D, width), low),
-            pltpu.VMEM((width, D), low),
-            pltpu.SemaphoreType.DMA((3,)),
+            pltpu.VMEM((rows, D), jnp.float32),
+            pltpu.VMEM((rows, D), LOW),
+            pltpu.SemaphoreType.DMA((2,)),
         ],
         "mlp_forward",
         work(2 * rows * D * (D + 2 * width), rows * (16 * D + 4 * width) + 2 * D * (D + 2 * width)),
@@ -1662,108 +1709,118 @@
 
 
 def mlp_back_kernel(
-    grad_ref, slope_ref, residual_ref, up_full, proj_out, vector_ref,
-    low_ref, hidden_ref, out_ref, out_low_ref, attended_ref, sums_ref,
-    mix_ref, up_ref, down_ref, sems,
+    grad_ref, slope_ref, residual_ref, mix_ref, up_ref, down_ref, vector_ref,
+    low_out, hidden_ref, out_ref, out_low_ref, attended_ref, sums_ref,
+    low_ref, second_ref, sem,
 ):
-    width = up_ref.shape[1]
-    copies = loads(
-        (proj_out.at[pl.ds(D, width)], up_full, proj_out.at[pl.ds(0, D)]),
-        (down_ref, up_ref, mix_ref),
-        sems,
-    )
+    rows = grad_ref.shape[0]
+    copy = pltpu.make_async_copy(low_ref, low_out, sem)
 
     @at_first
     def _():
-        for copy in copies:
-            copy.start()
-        copies[0].wait()
-
-    grad = grad_ref[...]
-    grad_low = grad.astype(jnp.bfloat16)
-    low_ref[...] = grad_low
-    part = 512
-    hidden_sums = []
-    active_grad = mul_nt(grad_low, down_ref[:part, :])
-    for base in range(0, width, part):
+        low_ref[...] = grad_ref[...].astype(LOW)
+        copy.start()
+        second_ref[...] = jnp.zeros_like(second_ref)
+
+    parts = halves_of(rows)
+    active_grad = mul_nt(low_ref[parts[0], :], down_ref[...])
+    hidden_sum = 0.0
+    for index, half in enumerate(parts):
         following = None
-        if base + part < width:
-            following = mul_nt(grad_low, down_ref[base + part : base + 2 * part, :])
-        columns = slice(base, base + part)
-        hidden_grad = (active_grad * slope_ref[:, columns].astype(jnp.float32)).astype(jnp.bfloat16)
-        hidden_ref[:, columns] = hidden_grad
-        hidden_sums.append(column_sum(hidden_grad))
+        if index + 1 < len(parts):
+            following = mul_nt(low_ref[parts[index + 1], :], down_ref[...])
+        hidden_grad = (active_grad * slope_ref[half, :].astype(jnp.float32)).astype(LOW)
+        hidden_ref[half, :] = hidden_grad
+        hidden_sum = hidden_sum + column_sum(hidden_grad)
+        second_ref[half, :] += mul_nt(hidden_grad, up_ref[...])
         active_grad = following
-    at_first(copies[1].wait)
-    second_grad = mul_nt(hidden_ref[...], up_ref[...])
-    value_grad, gain_grad, shift_grad = norm_backward(
-        second_grad, residual_ref[...], vector_ref[:, 2 * D : 3 * D]
-    )
-    total = value_grad + grad
-    out_ref[...] = total
-    total_low = total.astype(jnp.bfloat16)
-    out_low_ref[...] = total_low
-    at_first(copies[2].wait)
-    attended_ref[...] = mul_nt(total_low, mix_ref[...]).astype(jnp.bfloat16)
-    accumulate(
-        sums_ref,
-        [gain_grad, shift_grad, column_sum(total_low), column_sum(grad_low), *hidden_sums],
-    )
+    sums_ref[:, chunk_at(4 * D)] = hidden_sum
+
+    @at_last
+    def _():
+        gain = vector_ref[:, 2 * D : 3 * D]
+        totals = [0.0] * 4
+        for half in halves_of(rows):
+            grad = grad_ref[half, :]
+            value_grad, gain_grad, shift_grad = norm_backward(
+                second_ref[half, :], residual_ref[half, :], gain
+            )
+            total = value_grad + grad
+            out_ref[half, :] = total
+            total_low = total.astype(LOW)
+            out_low_ref[half, :] = total_low
+            attended_ref[half, :] = mul_nt(total_low, mix_ref[...]).astype(LOW)
+            new = (gain_grad, shift_grad, column_sum(total_low), column_sum(low_ref[half, :]))
+            totals = [old + part for old, part in zip(totals, new)]
+        sums_ref[:, : 4 * D] = jnp.concatenate(totals, 1)
+        copy.wait()
 
 
 def mlp_backward(grad, slope, residual, up, proj_out, vector):
     rows = grad.shape[0]
     width = up.shape[1]
-    block = 256
-    low = jnp.bfloat16
-    narrow = rows_of(block, D)
+    whole = fixed(rows, D)
+    weight_specs, weights = mlp_specs(up, proj_out)
     return block_call(
         mlp_back_kernel,
-        rows // block,
-        [narrow, rows_of(block, width), narrow, ANYWHERE, ANYWHERE, fixed(1, vector.shape[1])],
-        [grad, slope, residual, up, proj_out, vector],
-        [narrow, rows_of(block, width), narrow, narrow, narrow, fixed(1, 4 * D + width)],
+        width // D,
+        [whole, columns_of(rows), whole, *weight_specs, fixed(1, vector.shape[1])],
+        [grad, slope, residual, *weights, vector],
+        [ANYWHERE, columns_of(rows), whole, whole, whole, fixed(1, 4 * D + width)],
         [
-            shape_of(rows, D, dtype=low),
-            shape_of(rows, width, dtype=low),
+            shape_of(rows, D, dtype=LOW),
+            shape_of(rows, width, dtype=LOW),
             shape_of(rows, D),
-            shape_of(rows, D, dtype=low),
-            shape_of(rows, D, dtype=low),
+            shape_of(rows, D, dtype=LOW),
+            shape_of(rows, D, dtype=LOW),
             shape_of(1, 4 * D + width),
         ],
         [
-            pltpu.VMEM((D, D), low),
-            pltpu.VMEM((D, width), low),
-            pltpu.VMEM((width, D), low),
-            pltpu.SemaphoreType.DMA((3,)),
+            pltpu.VMEM((rows, D), LOW),
+            pltpu.VMEM((rows, D), jnp.float32),
+            pltpu.SemaphoreType.DMA,
         ],
         "mlp_backward",
-        None,
-    )
-
-
-def qkv_back_kernel(grad_ref, residual_ref, stream_ref, weight_ref, vector_ref, out_ref, sums_ref):
-    grad = grad_ref[...]
-    normed_grad = mul_nt(grad, weight_ref[...])
-    value_grad, gain_grad, shift_grad = norm_backward(normed_grad, stream_ref[...], vector_ref[:, :D])
-    out_ref[...] = residual_ref[...] + value_grad
-    accumulate(sums_ref, [gain_grad, shift_grad, column_sum(grad)])
+    )
+
+
+def qkv_back_kernel(
+    grad_ref, residual_ref, stream_ref, weight_ref, vector_ref, out_ref, sums_ref, normed_ref
+):
+    rows = stream_ref.shape[0]
+
+    @at_first
+    def _():
+        normed_ref[...] = jnp.zeros_like(normed_ref)
+
+    for half in halves_of(rows):
+        normed_ref[half, :] += mul_nt(grad_ref[half, :], weight_ref[...])
+    sums_ref[:, chunk_at(2 * D)] = column_sum(grad_ref[...])
+
+    @at_last
+    def _():
+        totals = [0.0] * 2
+        for half in halves_of(rows):
+            value_grad, gain_grad, shift_grad = norm_backward(
+                normed_ref[half, :], stream_ref[half, :], vector_ref[:, :D]
+            )
+            out_ref[half, :] = residual_ref[half, :] + value_grad
+            totals = [totals[0] + gain_grad, totals[1] + shift_grad]
+        sums_ref[:, : 2 * D] = jnp.concatenate(totals, 1)
 
 
 def qkv_backward(grad, residual_grad, stream, weight, vector):
     rows = stream.shape[0]
-    block = 256
-    narrow = rows_of(block, D)
+    whole = fixed(rows, D)
     return block_call(
         qkv_back_kernel,
-        rows // block,
-        [rows_of(block, 3 * D), narrow, narrow, fixed(D, 3 * D), fixed(1, vector.shape[1])],
+        3,
+        [columns_of(rows), whole, whole, columns_of(D), fixed(1, vector.shape[1])],
         [grad, residual_grad, stream, weight, vector],
-        [narrow, fixed(1, 5 * D)],
+        [whole, fixed(1, 5 * D)],
         [shape_of(rows, D), shape_of(1, 5 * D)],
-        [],
+        [pltpu.VMEM((rows, D), jnp.float32)],
         "qkv_backward",
-        None,
     )
 
 
@@ -1986,6 +2043,7 @@
     owners = lax.axis_size("fsdp")
     nodes = position_table.shape[0]
     vector_size = layer_vector.size
+    output_zero = lax.all_gather(output_proj[0].astype(LOW), "fsdp", axis=0, tiled=True)
     stream, pos_weights_t, vectors, qkv_weight, rides, rest_shards = begin(
         pixels,
         segment,
@@ -1998,19 +2056,24 @@
         position_table,
         global_vector,
     )
-    output_zero, up_one, head_full = (
+    up_one, head_full = (
         lax.all_gather(shard, "fsdp", axis=0, tiled=True) for shard in rest_shards
     )
+    up_ride, qkv_ride, output_ride = rides
     saved_layers = []
     for index in range(LAYERS):
         vector = vectors[index]
         normed, qkv_rows = qkv_forward(stream, qkv_weight, vector)
-        attended, expo, inverse, fetched = attention_forward(
-            qkv_rows, segment, [rides[0] if index == 0 else rides[2]], 4 + index
-        )
-        up, output = (fetched, output_zero) if index == 0 else (up_one, fetched)
+        if index == 0:
+            attended, expo, inverse, up, qkv_ride = attention_forward(
+                qkv_rows, segment, [up_ride, qkv_ride], 4
+            )
+            output, mlp_rides = output_zero, [qkv_ride, output_ride]
+        else:
+            attended, expo, inverse, output = attention_forward(qkv_rows, segment, [output_ride], 5)
+            up, mlp_rides = up_one, ()
         residual, normed_second, active, slope, following, *fetched = mlp_forward(
-            stream, attended, up, output, vector, rides[1:2] if index == 0 else (), 7
+            stream, attended, up, output, vector, mlp_rides, 7
         )
         saved_layers.append(
             (
@@ -2021,7 +2084,7 @@
         )
         stream = following
         if fetched:
-            (qkv_weight,) = fetched
+            qkv_weight, output_ride = fetched
     stream_grad, head_grad, final_sums, head_bias_grad, numbers = head(
         stream, segment, labels, head_full, global_vector, head_weight.shape[1]
     )
@@ -2036,7 +2099,7 @@
             stream_grad, slope, residual, up, output, vector
         )
         output_grads = output_weight_grad(
-            attended, active, residual_low, grad_low, (D // 3,) * 3 if index else (D,)
+            attended, active, residual_low, grad_low, (D // 2,) * 2 if index else (D,)
         )
         attended_grad, *output_grads = lax.optimization_barrier((attended_grad, *output_grads))
         output_parts = [scatter(by_owner(grad)) for grad in output_grads]
@@ -2050,7 +2113,7 @@
             inverse,
             attended,
             attended_grad,
-            () if index else [ShareRide(part) for part in early_parts],
+            () if index else [ShareRide(early_parts[0]), ShareRide(jnp.concatenate(early_parts[1:], 1))],
             6,
         )
         stream_grad, qkv_sums = qkv_backward(qkv_grad, residual_grad, entering, qkv_weight, vector)
@@ -2093,7 +2156,7 @@
     output_zero_sum, small_share, small_full = finish_all(
         [*early_sums, *input_zero_sums, *kernel_sum, *input_one_sums], [last_part], small, 3
     )
-    head_sum, output_one_sums = early_sums[0], early_sums[1:]
+    head_sum, output_one_sum = early_sums
     rest_sum = small_full[:, vector_rows:used].reshape(-1)
     position_sum = rest_sum[: position_grad.size].reshape(position_grad.shape)
     global_sum = rest_sum[position_grad.size :][: global_vector.shape[0]]
@@ -2104,7 +2167,7 @@
     input_sum = jnp.stack(
         [jnp.concatenate(pair, 1) for pair in (input_zero_sums, input_one_sums)]
     ).astype(jnp.float32)
-    output_sum = jnp.stack([output_zero_sum, jnp.concatenate(output_one_sums, 1)]).astype(
+    output_sum = jnp.stack([output_zero_sum, output_one_sum]).astype(
         jnp.float32
     )
     vector_sum = small_share[:vector_rows].reshape(-1)[:vector_size].reshape(layer_vector.shape)

time: 733 us -> 721 us (0.984)
  Pallas kernels: 619 us -> 602 us
    pallas_call x17, Pallas kernels: 389 us -> 362 us  [block_call(): pl.pallas_call(kernel, grid=(grid,), in_specs=in_specs, out_specs=out_spe...]
    pallas_call x1, Pallas kernels: 72.2 us -> 83 us  [begin(): pl.pallas_call(functools.partial(first_kernel, spots=spots), in_specs=[AN...]
    reduce_scatter x7 -> x6, waiting for transfers between devices: 31.3 us -> 37.6 us  [scatter(): return lax.psum_scatter(grad, 'fsdp', scatter_dimension=0)]
  transfers between devices with their start and end apart: 10 -> 9, of which waited for: 3 -> 2; matrix products, arithmetic and copies ran while one was open for 1% -> 2% of each run, Pallas kernels for 69% -> 73%
where the time goes in v8:
time: 721 us; the launch traced here: 713 us
  Pallas kernels  602 us (83%)
  waiting for transfers between devices  40.2 us (6%)
  other arithmetic  32.8 us (5%)
  between operations  20.4 us (3%)
  local copies, waits for them, and re-layouts  17.2 us (2%)
    pallas_call x17, Pallas kernels, block_call(): pl.pallas_call(kernel, grid=(grid,), in_specs=in_specs, out_specs=out_spe...  362 us
    pallas_call x1, Pallas kernels, reduce_call(): pl.pallas_call(functools.partial(reduce_kernel, whole=whole, partly=partl...  108 us
    pallas_call x1, Pallas kernels, begin(): pl.pallas_call(functools.partial(first_kernel, spots=spots), in_specs=[AN...  83 us
    reduce_scatter x6, waiting for transfers between devices, scatter(): return lax.psum_scatter(grad, 'fsdp', scatter_dimension=0)  37.6 us
    pallas_call x1, Pallas kernels, finish_call(): pl.pallas_call(functools.partial(finish_kernel, done=done, partly=partly)...  37.5 us
    sub x7, other arithmetic, adam_update(): return (moment, square, weight - learn_rate * step_dir)  22.7 us
  transfers between devices with their start and end apart: 9, of which 2 were waited for; matrix products, arithmetic and copies ran while one was open for 2% of the time, Pallas kernels for 73%

profile of v8, /device:TPU:0, one launch (start us, length us, event | category | flops | bytes accessed | tf_op | source)
XLA Modules:
  0.0 713.5 jit_solution(9868995167902436531)
XLA Ops:
  7.2 2.3 slice.116
  9.6 0.7 convert_element_type.27
  10.4 0.2 dynamic_update_slice.3
  10.6 0.6 reshape.123.refs_1_
  11.2 1.3 broadcast_in_dim.22.refs_9_
  12.5 1.7 copy.50.refs_6_.refs_3_.seg_col_ref
  14.3 83.0 %begin.1 = (f32[1024,768]{1,0:T(8,128)}, f32[64,1024]{1,0:T(8,128)}, f32[1,9984]{1,0:T(1,128)}, f32[1,9984]{1,0:T(1,128)}, bf16[8,96,2304]{2,1,0:T(8,128)(2,1)},...) custom-call(f32[384,768]{1,0:T(8,128)} %refs_0_.1, ...), custom_call_target="tpu_custom_call" | custom-call | tf_op jit(solution)/shard_map/begin/pallas_call | solution.py:685
  97.4 0.7 all-gather.7.cloned.1.call-update
  98.0 0.2 reduce-scatter.9.cloned.1.call-start
  98.3 0.7 copy.54.label_ref
  99.0 0.6 broadcast_in_dim.24.vector_ref
  99.6 9.2 %qkv_forward.2 = (bf16[1024,768]{1,0:T(8,128)(2,1)}, bf16[1024,2304]{1,0:T(8,128)(2,1)}) custom-call(f32[1024,768]{1,0:T(8,128)} %get-tuple-element.109.stream_ref.refs_0_, bf16[768,2304]{1,0:T(8,128)(2,1)} %bitcast.55, f32[1,9984]{1,0:T(1,128)} %get-tuple-element.111.vector_ref.refs_5_), custom_call_target="tpu_custom_call" | custom-call | flops 3623878656 | bytes 14548992 | tf_op jit(solution)/shard_map/qkv_forward/pallas_call | solution.py:475
  108.7 40.3 %attention_forward.2 = (bf16[1024,768]{1,0:T(8,128)(2,1)}, bf16[12,1024,1024]{2,1,0:T(8,128)(2,1)}, f32[1024,768]{1,0:T(8,128)}, bf16[8,96,3072]{2,1,0:T(8,128)(2,1)}, bf16[4,48,1152]{2,1,0:T(8,128)(2,1)}) custom-call(bf16[1024,2304]{1,0:T(8,128)(2,1)} %get-tuple-element.112.refs_0_.refs_1_.refs_2_, ...), custom_call_target="tpu_custom_call" | custom-call | flops 12884901888 | bytes 34603008 | tf_op jit(solution)/shard_map/attention_forward/pallas_call | solution.py:475
  149.1 34.4 %mlp_forward.2 = (f32[1024,768]{1,0:T(8,128)}, bf16[1024,768]{1,0:T(8,128)(2,1)}, bf16[1024,3072]{1,0:T(8,128)(2,1)}, bf16[1024,3072]{1,0:T(8,128)(2,1)}, f32[10...) custom-call(f32[1024,768]{1,0:T(8,128)} %get-tuple-element.109.stream_ref.refs_0_, ...), custom_call_target="tpu_custom_call" | custom-call | flops 10871635968 | bytes 35782656 | tf_op jit(solution)/shard_map/mlp_forward/pallas_call | solution.py:475
  183.5 9.4 %qkv_forward.3 = (bf16[1024,768]{1,0:T(8,128)(2,1)}, bf16[1024,2304]{1,0:T(8,128)(2,1)}) custom-call(f32[1024,768]{1,0:T(8,128)} %get-tuple-element.122.stream_ref, bf16[768,2304]{1,0:T(8,128)(2,1)} %bitcast.58, f32[1,9984]{1,0:T(1,128)} %get-tuple-element.124.vector_ref), custom_call_target="tpu_custom_call" | custom-call | flops 3623878656 | bytes 14548992 | tf_op jit(solution)/shard_map/qkv_forward/pallas_call | solution.py:475
  192.9 43.2 %attention_forward.3 = (bf16[1024,768]{1,0:T(8,128)(2,1)}, bf16[12,1024,1024]{2,1,0:T(8,128)(2,1)}, f32[1024,768]{1,0:T(8,128)}, bf16[8,480,768]{2,1,0:T(8,128)(2,1)}) custom-call(bf16[1024,2304]{1,0:T(8,128)(2,1)} %get-tuple-element.125.refs_0_.refs_1_.refs_2_.q_ref.k_ref.v_ref, ...), custom_call_target="tpu_custom_call" | custom-call | flops 12884901888 | bytes 34603008 | tf_op jit(solution)/shard_map/attention_forward/pallas_call | solution.py:475
  236.1 21.4 %mlp_forward.3 = (f32[1024,768]{1,0:T(8,128)}, bf16[1024,768]{1,0:T(8,128)(2,1)}, bf16[1024,3072]{1,0:T(8,128)(2,1)}, bf16[1024,3072]{1,0:T(8,128)(2,1)}, f32[1024,768]{1,0:T(8,128)}) custom-call(f32[1024,768]{1,0:T(8,128)} %get-tuple-element.122.stream_ref, bf16[1024,768]{1,0:T(8,128)(2,1)} %get-tuple-element.129.attended_ref.out_ref, ...), custom_call_target="tpu_custom_call" | custom-call | flops 10871635968 | bytes 35782656 | tf_op jit(solution)/shard_map/mlp_forward/pallas_call | solution.py:475
  257.5 11.7 %head.1 = (f32[1024,768]{1,0:T(8,128)}, bf16[768,1024]{1,0:T(8,128)(2,1)}, f32[1,1536]{1,0:T(1,128)}, f32[1,1024]{1,0:T(1,128)}, f32[1,2]{1,0:T(1,128)}) custom-call(f32[1024,768]{1,0:T(8,128)} %get-tuple-element.132.stream_ref, s32[1024,1]{1,0:T(8,128)} %copy.50.refs_6_.refs_3_.seg_col_ref, s32[1,1024]{1,0:T(1,128)} %bitcast.80, s32[8,1]{1,0:T(8,128)} %copy.54.label_ref, ...), custom_call_target="tpu_custom_call" | custom-call | tf_op jit(solution)/shard_map/head/pallas_call | solution.py:1989
  269.2 22.7 %mlp_backward.2 = (bf16[1024,768]{1,0:T(8,128)(2,1)}, bf16[1024,3072]{1,0:T(8,128)(2,1)}, f32[1024,768]{1,0:T(8,128)}, bf16[1024,768]{1,0:T(8,128)(2,1)}, bf16[1024,768]{1,0:T(8,128)(2,1)}, /*index=5*/f32[1,6144]{1,0:T(1,128)}) custom-call(f32[1024,768]{1,0:T(8,128)} %get-tuple-element.134.grad_ref, bf16[1024,3072]{1,0:T(8,128)(2,1)} %get-tuple-element.135.slope_ref, ...), custom_call_target="tpu_custom_call" | custom-call | tf_op jit(solution)/shard_map/mlp_backward/pallas_call | solution.py:475
  291.9 11.9 %output_weight_grad.2 = (bf16[3840,384]{1,0:T(8,128)(2,1)}, bf16[3840,384]{1,0:T(8,128)(2,1)}) custom-call(bf16[1024,768]{1,0:T(8,128)(2,1)} %get-tuple-element.129.attended_ref.out_ref, bf16[1024,3072]{1,0:T(8,128)(2,1)} %get-tuple-element.138.active_ref, bf16[1024,768]{1,0:T(8,128)(2,1)} %get-tuple-element.139.residual_ref, ...), custom_call_target="tpu_custom_call" | custom-call | tf_op jit(solution)/shard_map/output_weight_grad/pallas_call | solution.py:475
  303.9 0.5 reduce-scatter.11.cloned.1.call-update
  304.5 0.5 reduce-scatter.7.cloned.1.call-update
  305.1 28.8 %attention_backward.2.grad_ref.qkv_ref = bf16[1024,2304]{1,0:T(8,128)(2,1)} custom-call(bf16[1024,2304]{1,0:T(8,128)(2,1)} %get-tuple-element.125.refs_0_.refs_1_.refs_2_.q_ref.k_ref.v_ref, bf16[1024,2304]{1,0:T(8,128)(2,1)} %get-tuple-element.125.refs_0_.refs_1_.refs_2_.q_ref.k_ref.v_ref, ...), custom_call_target="tpu_custom_call" | custom-call | tf_op jit(solution)/shard_map/attention_backward/pallas_call | solution.py:475
  333.9 12.7 %qkv_backward.2 = (f32[1024,768]{1,0:T(8,128)}, f32[1,3840]{1,0:T(1,128)}) custom-call(bf16[1024,2304]{1,0:T(8,128)(2,1)} %attention_backward.2.grad_ref.qkv_ref, f32[1024,768]{1,0:T(8,128)} %get-tuple-element.144.residual_ref, f32[1024,768]{1,0:T(8,128)} %get-tuple-element.122.stream_ref, bf16[768,2304]{1,0:T(8,128)(2,1)} %bitcast.59, ...), custom_call_target="tpu_custom_call" | custom-call | tf_op jit(solution)/shard_map/qkv_backward/pallas_call | solution.py:475
  346.6 16.3 %input_weight_grad.2 = (bf16[768,2304]{1,0:T(8,128)(2,1)}, bf16[768,3072]{1,0:T(8,128)(2,1)}) custom-call(bf16[1024,768]{1,0:T(8,128)(2,1)} %get-tuple-element.146.first_ref, bf16[1024,768]{1,0:T(8,128)(2,1)} %get-tuple-element.147.second_ref, bf16[1024,2304]{1,0:T(8,128)(2,1)} %attention_backward.2.grad_ref.qkv_ref, ...), custom_call_target="tpu_custom_call" | custom-call | tf_op jit(solution)/shard_map/input_weight_grad/pallas_call | solution.py:475
  363.0 0.7 reduce-scatter.15.cloned.1.call-update
  363.7 23.1 %mlp_backward.3 = (bf16[1024,768]{1,0:T(8,128)(2,1)}, bf16[1024,3072]{1,0:T(8,128)(2,1)}, f32[1024,768]{1,0:T(8,128)}, bf16[1024,768]{1,0:T(8,128)(2,1)}, bf16[1024,768]{1,0:T(8,128)(2,1)}, /*index=5*/f32[1,6144]{1,0:T(1,128)}) custom-call(f32[1024,768]{1,0:T(8,128)} %get-tuple-element.151.grad_ref, bf16[1024,3072]{1,0:T(8,128)(2,1)} %get-tuple-element.152.slope_ref, ...), custom_call_target="tpu_custom_call" | custom-call | tf_op jit(solution)/shard_map/mlp_backward/pallas_call | solution.py:475
  386.9 12.0 %output_weight_grad.3 = bf16[3840,768]{1,0:T(8,128)(2,1)} custom-call(bf16[1024,768]{1,0:T(8,128)(2,1)} %get-tuple-element.118.refs_1_.attended_ref.refs_5_, bf16[1024,3072]{1,0:T(8,128)(2,1)} %get-tuple-element.155.active_ref, bf16[1024,768]{1,0:T(8,128)(2,1)} %get-tuple-element.156.residual_ref, bf16[1024,768]{1,0:T(8,128)(2,1)} %get-tuple-element.157.grad_ref), custom_call_target="tpu_custom_call" | custom-call | tf_op jit(solution)/shard_map/output_weight_grad/pallas_call | solution.py:475
  398.9 0.7 copy-done.17
  399.7 0.1 stack.28
  400.0 2.0 pad_maximum_fusion.2.refs_8_
  402.0 17.5 %reduce-scatter.7.cloned.1.call-done = bf16[1,96,1024]{2,1,0:T(8,128)(2,1)} async-done(((bf16[8,96,1024]{2,1,0:T(8,128)(2,1)}), bf16[1,96,1024]{2,1,0:T(8,128)(2,1)}) %reduce-scatter.7.cloned.1.call-update) | async-done | bytes 196624 | tf_op jit(solution)/shard_map/reduce_scatter | solution.py:1367
  419.5 35.0 %attention_backward.3 = (bf16[1024,2304]{1,0:T(8,128)(2,1)}, bf16[96,1024]{1,0:T(8,128)(2,1)}, bf16[480,768]{1,0:T(8,128)(2,1)}) custom-call(bf16[1024,2304]{1,0:T(8,128)(2,1)} %get-tuple-element.112.refs_0_.refs_1_.refs_2_, bf16[1024,2304]{1,0:T(8,128)(2,1)} %get-tuple-element.112.refs_0_.refs_1_.refs_2_, ...), custom_call_target="tpu_custom_call" | custom-call | tf_op jit(solution)/shard_map/attention_backward/pallas_call | solution.py:475
  454.6 12.7 %qkv_backward.3 = (f32[1024,768]{1,0:T(8,128)}, f32[1,3840]{1,0:T(1,128)}) custom-call(bf16[1024,2304]{1,0:T(8,128)(2,1)} %get-tuple-element.166.qkv_ref.grad_ref, f32[1024,768]{1,0:T(8,128)} %get-tuple-element.170.residual_ref, f32[1024,768]{1,0:T(8,128)} %get-tuple-element.109.stream_ref.refs_0_, bf16[768,2304]{1,0:T(8,128)(2,1)} %bitcast.56, ...), custom_call_target="tpu_custom_call" | custom-call | tf_op jit(solution)/shard_map/qkv_backward/pallas_call | solution.py:475
  467.3 0.7 slice_reduce_fusion.3
  468.0 0.7 slice_reduce_fusion.6
  468.8 0.1 stack.27
  469.0 0.1 reshape.138
  469.1 12.1 %embed_backward.1 = (bf16[3072,768]{1,0:T(8,128)(2,1)}, f32[64,768]{1,0:T(8,128)}, f32[1,768]{1,0:T(1,128)}) custom-call(bf16[1024,3072]{1,0:T(8,128)(2,1)} %pixel_ref.1, f32[1024,768]{1,0:T(8,128)} %get-tuple-element.171.grad_ref, f32[64,1024]{1,0:T(8,128)} %get-tuple-element.172.pos_ref), custom_call_target="tpu_custom_call" | custom-call | tf_op jit(solution)/shard_map/embed_backward/pallas_call | solution.py:475
  481.3 0.7 reduce.10
  482.0 0.9 slice.75
  483.2 0.7 pad.19.refs_8_
  483.9 16.5 %input_weight_grad.3 = (bf16[768,2304]{1,0:T(8,128)(2,1)}, bf16[768,3072]{1,0:T(8,128)(2,1)}) custom-call(bf16[1024,768]{1,0:T(8,128)(2,1)} %get-tuple-element.164.first_ref, bf16[1024,768]{1,0:T(8,128)(2,1)} %get-tuple-element.165.second_ref, bf16[1024,2304]{1,0:T(8,128)(2,1)} %get-tuple-element.166.qkv_ref.grad_ref, ...), custom_call_target="tpu_custom_call" | custom-call | tf_op jit(solution)/shard_map/input_weight_grad/pallas_call | solution.py:475
  500.4 20.0 %reduce-scatter.15.cloned.1.call-done = bf16[1,96,3072]{2,1,0:T(8,128)(2,1)} async-done(((bf16[8,96,3072]{2,1,0:T(8,128)(2,1)}), bf16[1,96,3072]{2,1,0:T(8,128)(2,1)}) %reduce-scatter.15.cloned.1.call-update) | async-done | bytes 589840 | tf_op jit(solution)/shard_map/reduce_scatter | solution.py:1367
  520.4 108.4 %reduce_gradients.1 = (bf16[96,2304]{1,0:T(8,128)(2,1)}, bf16[96,3072]{1,0:T(8,128)(2,1)}, bf16[384,768]{1,0:T(8,128)(2,1)}, bf16[96,2304]{1,0:T(8,128)(2,1)}, bf16[96,3072]{1,0:T(8,128)(2,1)}) custom-call(bf16[8,96,2304]{2,1,0:T(8,128)(2,1)} %bitcast.60, bf16[8,96,3072]{2,1,0:T(8,128)(2,1)} %bitcast.54, bf16[8,384,768]{2,1,0:T(8,128)(2,1)} %bitcast.53, ...), custom_call_target="tpu_custom_call" | custom-call | tf_op jit(solution)/shard_map/reduce_gradients/pallas_call | solution.py:1268
  628.8 1.6 maximum_bitcast_fusion
  630.5 37.5 %finish_gradients.1 = (bf16[480,768]{1,0:T(8,128)(2,1)}, f32[64,128]{1,0:T(8,128)}, f32[8,64,128]{2,1,0:T(8,128)}) custom-call(bf16[96,1024]{1,0:T(8,128)(2,1)} %get-tuple-element.162.refs_0_, bf16[480,768]{1,0:T(8,128)(2,1)} %get-tuple-element.163.refs_1_, bf16[96,2304]{1,0:T(8,128)(2,1)} %get-tuple-element.176.refs_2_, ...), custom_call_target="tpu_custom_call" | custom-call | tf_op jit(solution)/shard_map/finish_gradients/pallas_call | solution.py:1321
  668.0 1.6 multiply_reduce_fusion.1
  669.7 1.4 slice_reduce_fusion.8
  671.0 0.9 slice.77
  672.0 0.6 multiply_reduce_fusion.2
  672.6 0.6 multiply_reduce_fusion
  673.2 0.6 fusion.15
  673.8 0.7 slice_bitcast_fusion
  679.2 0.7 slice_multiply_fusion
  680.0 1.6 mul.230
  681.6 0.6 multiply_subtract_fusion.5
  682.2 2.7 multiply_subtract_fusion.3
  684.9 3.9 multiply_subtract_fusion.2
  688.9 0.6 multiply_subtract_fusion.6
  689.5 1.9 multiply_subtract_fusion.4
  691.5 6.7 multiply_subtract_fusion.1
  698.2 1.2 copy-done.4
  699.4 6.2 multiply_subtract_fusion
  (84 shorter events, 1.3 us)
Async XLA Ops:
  7.2 141.9 %all-gather.9.cloned.1.call-start = ((), (), s32[]{:S(2)}) async-start(), calls=%async_computation.14 | async-start | bytes 6635520 | tf_op jit(solution)/shard_map/all_gather | solution.py:2046
  9.6 226.5 %all-gather.5.cloned.1.call-start = ((), (), s32[]{:S(2)}) async-start(), calls=%async_computation.6 | async-start | bytes 5308416 | tf_op jit(solution)/shard_map/all_gather | solution.py:2060
  14.3 84.0 %copy-start.23 = (s32[1,8]{1,0:T(1,128)S(1)}, s32[1,8]{1,0:T(1,128)}, u32[]{:S(2)}) copy-start(s32[1,8]{1,0:T(1,128)} %param.28) | copy-start | bytes 100
  14.3 84.7 %copy-start.11 = (f32[3304]{0:T(1024)S(1)}, f32[3304]{0:T(1024)}, u32[]{:S(2)}) copy-start(f32[3304]{0:T(1024)} %param.35) | copy-start | bytes 39652
  97.3 160.2 %all-gather.7.cloned.1.call-start = ((), (), s32[]{:S(2)}) async-start(), calls=%async_computation.7 | async-start | bytes 1769472 | tf_op jit(solution)/shard_map/all_gather | solution.py:2060
  98.0 301.9 %reduce-scatter.9.cloned.1.call-start = ((), (), s32[]{:S(2)}) async-start(), calls=%async_computation.9 | async-start | bytes 3317760 | tf_op jit(solution)/shard_map/reduce_scatter | solution.py:1367
  303.8 96.1 %reduce-scatter.11.cloned.1.call-start = ((), (), s32[]{:S(2)}) async-start(), calls=%async_computation.10 | async-start | bytes 3317760 | tf_op jit(solution)/shard_map/reduce_scatter | solution.py:1367
  304.4 115.1 %reduce-scatter.7.cloned.1.call-start = ((), (), s32[]{:S(2)}) async-start(), calls=%async_computation.8 | async-start | bytes 1769472 | tf_op jit(solution)/shard_map/reduce_scatter | solution.py:1367
  305.0 195.4 %reduce-scatter.13.cloned.1.call-start = ((), (), s32[]{:S(2)}) async-start(), calls=%async_computation.11 | async-start | bytes 3981312 | tf_op jit(solution)/shard_map/reduce_scatter | solution.py:1367
  362.9 157.4 %reduce-scatter.15.cloned.1.call-start = ((), (), s32[]{:S(2)}) async-start(), calls=%async_computation.12 | async-start | bytes 5308416 | tf_op jit(solution)/shard_map/reduce_scatter | solution.py:1367
  363.7 266.7 %reduce-scatter.17.cloned.1.call-start = ((), (), s32[]{:S(2)}) async-start(), calls=%async_computation.13 | async-start | bytes 6635520 | tf_op jit(solution)/shard_map/reduce_scatter | solution.py:1367
  398.8 0.7 copy-start.17
  398.8 0.8 copy-start.13
  398.8 1.0 copy-start.20
  398.9 1.0 copy-start.14
  469.1 13.8 %copy-start.21 = (f32[1,1024]{1,0:T(1,128)S(1)}, f32[1,1024]{1,0:T(1,128)}, u32[]{:S(2)}) copy-start(f32[1,1024]{1,0:T(1,128)} %get-tuple-element.189) | copy-start | bytes 12292
  469.1 13.8 %copy-start.22 = (f32[1,2]{1,0:T(1,128)S(1)}, f32[1,2]{1,0:T(1,128)}, u32[]{:S(2)}) copy-start(f32[1,2]{1,0:T(1,128)} %get-tuple-element.190) | copy-start | bytes 28
  630.4 51.2 %copy-start.15 = (f32[3304]{0:T(1024)S(1)}, f32[3304]{0:T(1024)}, u32[]{:S(2)}) copy-start(f32[3304]{0:T(1024)} %param.49) | copy-start | bytes 39652
  630.4 51.1 %copy-start.16 = (f32[3304]{0:T(1024)S(1)}, f32[3304]{0:T(1024)}, u32[]{:S(2)}) copy-start(f32[3304]{0:T(1024)} %param.42) | copy-start | bytes 39652
  630.4 58.4 %copy-start.12 = (f32[2,1248]{1,0:T(2,128)S(1)}, f32[2,1248]{1,0:T(2,128)}, u32[]{:S(2)}) copy-start(f32[2,1248]{1,0:T(2,128)} %param.33) | copy-start | bytes 29956
  630.5 58.4 %copy-start.18 = (f32[2,1248]{1,0:T(2,128)S(1)}, f32[2,1248]{1,0:T(2,128)}, u32[]{:S(2)}) copy-start(f32[2,1248]{1,0:T(2,128)} %param.47) | copy-start | bytes 29956
  630.5 58.4 %copy-start.19 = (f32[2,1248]{1,0:T(2,128)S(1)}, f32[2,1248]{1,0:T(2,128)}, u32[]{:S(2)}) copy-start(f32[2,1248]{1,0:T(2,128)} %param.40) | copy-start | bytes 29956
  668.0 16.9 %copy-start.2 = (f32[384,768]{1,0:T(8,128)S(1)}, f32[384,768]{1,0:T(8,128)}, u32[]{:S(2)}) copy-start(f32[384,768]{1,0:T(8,128)} %refs_0_.1) | copy-start | bytes 3538948
  681.6 3.3 copy-start.8
  681.6 3.3 copy-start.9
  682.2 7.3 %copy-start.10 = (f32[49,768]{1,0:T(8,128)S(1)}, f32[49,768]{1,0:T(8,128)}, u32[]{:S(2)}) copy-start(f32[49,768]{1,0:T(8,128)} %mul.230) | copy-start | bytes 451588
  682.2 9.2 %copy-start.7 = (bf16[480,768]{1,0:T(8,128)(2,1)S(1)}, bf16[480,768]{1,0:T(8,128)(2,1)}, u32[]{:S(2)}) copy-start(bf16[480,768]{1,0:T(8,128)(2,1)} %get-tuple-element.163.refs_1_) | copy-start | bytes 2211844
  684.9 6.6 copy-start.1
  684.9 6.6 copy-start.5
  684.9 6.6 copy-start.6
  691.5 6.7 copy-start
  691.5 6.7 copy-start.3
  691.5 7.9 %copy-start.4 = (f32[2,96,5376]{2,1,0:T(8,128)S(1)}, f32[2,96,5376]{2,1,0:T(8,128)}, u32[]{:S(2)}) copy-start(f32[2,96,5376]{2,1,0:T(8,128)} %param.38) | copy-start | bytes 12386308
Sparse Core Ops, SparseCore 0:
  10.2 98.0 all-gather.8
  110.0 73.7 all-gather.4
  185.4 22.8 all-gather.6
  304.0 38.4 reduce-scatter.8
  345.3 38.4 reduce-scatter.10
  386.0 33.5 reduce-scatter.6
  422.4 41.9 reduce-scatter.12
  466.9 53.4 reduce-scatter.14
  522.8 74.0 reduce-scatter.16

commit v9 on v8

--- a/solution.py
+++ b/solution.py
@@ -146,14 +146,63 @@
     )
 
 
-GATHER_SEMS = 33
-
-
-class Gather:
+GATHER_SEMS = 39
+
+
+def relay_rows(part, rows):
+    cut = -(-rows // 32) * 16
+    return (0, cut) if part == 0 else (cut, rows - cut)
+
+
+class Relay:
+    def region(self, turn, index):
+        _, level, core = place()
+        block = self.out.at[2 * partner(level, turn) + core]
+        return block.at[quarter(index, *self.shard.shape)]
+
+    def group_copy(self, turn, other):
+        group, level, core = place()
+        index = self.group_at + 2 * (turn - 1) + other - 1
+        peer = (partner(group, other), 2 * level + core)
+        target = self.region(turn, group)
+        source = self.quarter_source(turn, target)
+        return remote(source, target, self.sems.at[index], self.sems.at[index + 6], peer)
+
+    def relay_copy(self, turn, part):
+        group, level, core = place()
+        first, count = relay_rows(part, quarter_shape(*self.shard.shape)[0])
+        block = self.region(turn, partner(group, 1 + part)).at[pl.ds(first, count)]
+        index = self.relay_at + 2 * (turn - 1) + part
+        peer = (partner(group, 2 - part), 2 * level + core)
+        return remote(block, block, self.sems.at[index], self.sems.at[index + 6], peer)
+
+    def relay(self):
+        for turn in TURNS:
+            for part in range(2):
+                self.group_copy(turn, 1 + part).wait_recv()
+                self.relay_copy(turn, part).start()
+
+    def wait_quarters(self, turn):
+        for part in range(2):
+            self.relay_copy(turn, part).wait_recv()
+
+    def wait_passed(self):
+        for turn in TURNS:
+            for part in range(2):
+                self.group_copy(turn, 1 + part).wait_send()
+                self.relay_copy(turn, part).wait_send()
+
+
+class Gather(Relay):
+    group_at, relay_at = 7, 19
+
     def __init__(self, shard, out, sems, split, in_place=False):
         self.shard, self.out, self.sems, self.split = shard, out, sems, split
         self.in_place = in_place
         self.rows, self.columns = shard.shape
+
+    def quarter_source(self, turn, target):
+        return target
 
     def level_copy(self, turn):
         group, level, core = place()
@@ -162,24 +211,15 @@
         if self.split:
             part = quarter(group, self.rows, self.columns)
             source, block = source.at[part], block.at[part]
-        sems = self.sems
         peer = (group, 2 * partner(level, turn) + core)
-        return remote(source, block, sems.at[turn], sems.at[3 + turn], peer)
-
-    def group_copy(self, turn, other):
-        group, level, core = place()
-        part = quarter(group, self.rows, self.columns)
-        block = self.out.at[2 * partner(level, turn) + core].at[part]
-        index = 3 * (turn - 1) + other - 1
-        peer = (partner(group, other), 2 * level + core)
-        return remote(block, block, self.sems.at[7 + index], self.sems.at[16 + index], peer)
+        return remote(source, block, self.sems.at[turn], self.sems.at[3 + turn], peer)
 
     def core_copy(self, turn):
         group, level, core = place()
         slot = 2 * partner(level, turn) + core
         source = self.shard if turn == 0 else self.out.at[slot]
         peer = (group, 2 * level + 1 - core)
-        return remote(source, self.out.at[slot], self.sems.at[25 + turn], self.sems.at[29 + turn], peer)
+        return remote(source, self.out.at[slot], self.sems.at[31 + turn], self.sems.at[35 + turn], peer)
 
     def own_copy(self):
         _, level, core = place()
@@ -196,15 +236,14 @@
         for turn in TURNS:
             self.level_copy(turn).wait_recv()
             if self.split:
-                for other in TURNS:
+                for other in (1, 2):
                     self.group_copy(turn, other).start()
             else:
                 self.core_copy(turn).start()
 
     def third(self, use=None):
         for turn in TURNS if self.split else ():
-            for other in TURNS:
-                self.group_copy(turn, other).wait_recv()
+            self.wait_quarters(turn)
             self.core_copy(turn).start()
             if use is not None:
                 use(turn, True)
@@ -216,9 +255,8 @@
                 use(turn, False)
         for turn in TURNS:
             self.level_copy(turn).wait_send()
-            if self.split:
-                for other in TURNS:
-                    self.group_copy(turn, other).wait_send()
+        if self.split:
+            self.wait_passed()
         for turn in (0, *TURNS):
             self.core_copy(turn).wait_send()
         if not self.in_place:
@@ -260,66 +298,53 @@
         self.target[...] = self.out[...]
 
 
-GROUP_GATHER_SEMS = 30
-
-
-class GroupGather:
+GROUP_GATHER_SEMS = 36
+
+
+class GroupGather(Relay):
+    group_at, relay_at = 4, 16
+
     def __init__(self, shard, quarters, out, sems):
         self.shard, self.quarters, self.out, self.sems = shard, quarters, out, sems
 
-    def part(self, turn):
+    def quarter_source(self, turn, target):
+        _, level, _ = place()
+        return self.quarters.at[partner(level, turn)]
+
+    def own_copy(self, turn):
         group, level, core = place()
-        block = self.out.at[2 * partner(level, turn) + core]
-        return block.at[quarter(group, *self.shard.shape)]
-
-    def own_copy(self, turn):
-        _, level, core = place()
         if turn == 0:
             source, target = self.shard, self.out.at[2 * level + core]
         else:
-            source, target = self.quarters.at[partner(level, turn)], self.part(turn)
+            source, target = self.quarters.at[partner(level, turn)], self.region(turn, group)
         return pltpu.make_async_copy(source, target, self.sems.at[turn])
-
-    def group_copy(self, turn, other):
-        group, level, core = place()
-        index = 3 * (turn - 1) + other - 1
-        return remote(
-            self.quarters.at[partner(level, turn)],
-            self.part(turn),
-            self.sems.at[4 + index],
-            self.sems.at[13 + index],
-            (partner(group, other), 2 * level + core),
-        )
 
     def core_copy(self, turn):
         group, level, core = place()
         slot = 2 * partner(level, turn) + core
         source = self.shard if turn == 0 else self.out.at[slot]
         peer = (group, 2 * level + 1 - core)
-        return remote(source, self.out.at[slot], self.sems.at[22 + turn], self.sems.at[26 + turn], peer)
+        return remote(source, self.out.at[slot], self.sems.at[28 + turn], self.sems.at[32 + turn], peer)
 
     def first(self):
         for turn in TURNS:
-            for other in TURNS:
+            for other in (1, 2):
                 self.group_copy(turn, other).start()
         for turn in (0, *TURNS):
             self.own_copy(turn).start()
         self.core_copy(0).start()
 
-    def second(self):
+    def third(self):
         for turn in TURNS:
-            for other in TURNS:
-                self.group_copy(turn, other).wait_recv()
+            self.wait_quarters(turn)
             self.own_copy(turn).wait()
             self.core_copy(turn).start()
 
-    def third(self):
+    def fourth(self):
         for turn in (0, *TURNS):
             self.core_copy(turn).wait_recv()
             self.core_copy(turn).wait_send()
-        for turn in TURNS:
-            for other in TURNS:
-                self.group_copy(turn, other).wait_send()
+        self.wait_passed()
         self.own_copy(0).wait()
 
     def store(self):
@@ -331,6 +356,7 @@
 class LevelRide:
     def __init__(self, shard):
         self.operands = [shard]
+        self.in_specs = [fixed(*shard.shape)]
         shape = (4, *quarter_shape(*shard.shape))
         self.out_specs = [fixed(*shape)]
         self.out_shapes = [jax.ShapeDtypeStruct(shape, shard.dtype)]
@@ -358,6 +384,7 @@
         owners = lax.axis_size("fsdp")
         full = (owners, *shard.shape)
         self.operands = [shard, quarters]
+        self.in_specs = [fixed(*shard.shape), fixed(*quarters.shape)]
         self.out_specs = [ANYWHERE]
         self.out_shapes = [jax.ShapeDtypeStruct(full, shard.dtype)]
         self.scratch = [
@@ -371,9 +398,9 @@
         return job
 
     def before(self, steps):
-        return {0: ("first",), max(1, 2 * steps // 3): ("second",)}
-
-    after = ("third", "store")
+        return {0: ("first",), steps // 2: ("relay",), steps - 1: ("third",)}
+
+    after = ("fourth", "store")
 
     def result(self, outs):
         return outs[0].reshape(-1, outs[0].shape[2])
@@ -385,6 +412,7 @@
 class ShareRide:
     def __init__(self, share):
         self.operands = [share]
+        self.in_specs = [ANYWHERE]
         self.out_specs = [fixed(*share.shape)]
         self.out_shapes = [jax.ShapeDtypeStruct(share.shape, share.dtype)]
         self.scratch = [
@@ -408,6 +436,39 @@
 
     def plain(self):
         return lax.psum(self.operands[0], "dp")
+
+
+class SumRide:
+    def __init__(self, grad, large):
+        block = grad.shape[1:]
+        self.large = large
+        self.operands = [grad]
+        self.in_specs = [ANYWHERE]
+        self.out_specs = [fixed(*block)]
+        self.out_shapes = [jax.ShapeDtypeStruct(block, grad.dtype)]
+        buffers = stepped_scratch(grad) if large else whole_scratch(grad)
+        sems = WHOLE_SEMS if large else REDUCE_SEMS
+        self.scratch = [pltpu.VMEM(block, grad.dtype), *buffers, pltpu.SemaphoreType.DMA((sems,))]
+
+    def job(self, sources, targets, scratch):
+        job = (Whole if self.large else Reduce)(sources[0], scratch[0], scratch[1:-1], scratch[-1])
+        job.target = targets[0]
+        return job
+
+    def before(self, steps):
+        if self.large:
+            return {0: ("first",), 1: ("second",), steps - 2: ("between",), steps - 1: ("third",)}
+        return {0: ("first",), 1: ("second",), steps // 2: ("third",), steps - 1: ("fourth",)}
+
+    @property
+    def after(self):
+        return (("fourth",) if self.large else ()) + ("fifth", "sixth", "store")
+
+    def result(self, outs):
+        return outs[0]
+
+    def plain(self):
+        return lax.psum(scatter(self.operands[0]), "dp")
 
 
 def riding(body, counts, rides, steps):
@@ -469,7 +530,7 @@
     count = len(out_shape)
     for ride in rides:
         operands = [*operands, *ride.operands]
-        in_specs = [*in_specs, *[fixed(*operand.shape) for operand in ride.operands]]
+        in_specs = [*in_specs, *ride.in_specs]
         out_specs, out_shape = [*out_specs, *ride.out_specs], [*out_shape, *ride.out_shapes]
         scratch = [*scratch, *ride.scratch]
     outs = pl.pallas_call(
@@ -522,9 +583,11 @@
 def first_kernel(*refs, spots):
     kernel, vectors, inputs, outputs, head, pixels, seg_col, patch_row, table, biases = refs[:10]
     stream, pos_t, vector_zero, vector_one = refs[10:14]
-    qkv_full, up_level, up_zero, qkv_one, up_one, output_one, head_low = refs[14:21]
-    wide_kernel, wide_inputs, wide_outputs, wide_head, pixel_rows, table_low = refs[21:27]
-    kernel_full, qkv_zero, vectors_full, qkv_landing, up_landing, load_sems, sems = refs[27:]
+    qkv_full, up_level, output_level = refs[14:17]
+    up_zero, output_zero, qkv_one, up_one, output_one, head_low = refs[17:23]
+    wide_kernel, wide_inputs, wide_outputs, wide_head, pixel_rows, table_low = refs[23:29]
+    kernel_full, qkv_zero, vectors_full, qkv_landing, up_landing, output_landing = refs[29:35]
+    load_sems, sems = refs[35:]
     _, level, core = place()
     mine = 2 * level + core
     pairs = [
@@ -532,7 +595,8 @@
         (inputs.at[0], wide_inputs.at[0]),
         (pixels, pixel_rows),
         (inputs.at[1], wide_inputs.at[1]),
-        (outputs.at[1], wide_outputs),
+        (outputs.at[0], wide_outputs.at[0]),
+        (outputs.at[1], wide_outputs.at[1]),
         (head, wide_head),
     ]
     copies = [
@@ -546,6 +610,8 @@
     qkv_job = Gather(qkv_zero, qkv_landing, sems.at[2], True)
     up_job = LevelGather(up_zero, up_landing, sems.at[3])
     up_job.target = up_level
+    output_job = LevelGather(output_zero, output_landing, sems.at[4])
+    output_job.target = output_level
     copies[0].wait()
     kernel_full[mine] = wide_kernel[...].astype(LOW)
     greet()
@@ -556,6 +622,9 @@
     qkv_job.first()
     up_zero[...] = wide_inputs[0, :, 3 * D :].astype(LOW)
     up_job.first()
+    copies[4].wait()
+    output_zero[...] = wide_outputs[0].astype(LOW)
+    output_job.first()
 
     weights = position_weights(seg_col[...], patch_row[...], table.shape[0])
     pos_t[...] = weights.T[: pos_t.shape[0], :]
@@ -590,11 +659,13 @@
     copies[3].wait()
     qkv_one[...] = wide_inputs[1, :, : 3 * D].astype(LOW)
     up_one[...] = wide_inputs[1, :, 3 * D :].astype(LOW)
-    copies[4].wait()
-    output_one[...] = wide_outputs[...].astype(LOW)
     copies[5].wait()
+    output_one[...] = wide_outputs[1].astype(LOW)
+    copies[6].wait()
     head_low[...] = jnp.zeros_like(head_low)
     head_low[:, : head.shape[1]] = wide_head[...].astype(LOW)
+    patch_job.relay()
+    qkv_job.relay()
     patch_job.third(use)
     qkv_job.third()
     patch_job.fourth(use)
@@ -613,8 +684,7 @@
     qkv_job.fourth()
     copy = pltpu.make_async_copy(qkv_landing, qkv_full, load_sems.at[0])
     copy.start()
-    up_job.fourth()
-    up_job.store()
+    run_stages([up_job, output_job], ("fourth", "store"))
     copy.wait()
 
 
@@ -655,8 +725,8 @@
             weights.T,
             [vectors[index : index + 1] for index in range(LAYERS)],
             gather(inputs[0][0], 0),
-            [GatherRide(inputs[0][1], inputs[0][1]), LevelRide(inputs[1][0]), LevelRide(outputs[1])],
-            [inputs[1][1], head],
+            [*[GatherRide(shard, shard) for shard in (inputs[0][1], outputs[0])], LevelRide(outputs[1])],
+            [*inputs[1], head],
         )
     rows = pixels.shape[0]
     owners = lax.axis_size("fsdp")
@@ -674,18 +744,20 @@
         shape_of(1, width),
         low(owners, *qkv_shape),
         levels(up_shape),
+        levels(out_shape),
         low(*up_shape),
+        low(*out_shape),
         low(*qkv_shape),
         low(*up_shape),
         low(*out_shape),
         low(head_weight.shape[0], classes),
     ]
-    wide = (patch_kernel, input_proj, output_proj[0], head_weight, pixels)
+    wide = (patch_kernel, input_proj, output_proj, head_weight, pixels)
     in_vmem = pl.BlockSpec(memory_space=pltpu.VMEM)
     results = pl.pallas_call(
         functools.partial(first_kernel, spots=spots),
         in_specs=[ANYWHERE] * 6 + [in_vmem] * 4,
-        out_specs=[in_vmem] * 4 + [ANYWHERE] + [in_vmem] * 6,
+        out_specs=[in_vmem] * 4 + [ANYWHERE] + [in_vmem] * 8,
         out_shape=shapes,
         scratch_shapes=[
             *[pltpu.VMEM(array.shape, array.dtype) for array in wide],
@@ -695,8 +767,9 @@
             pltpu.VMEM((owners, *vectors.shape), LOW),
             pltpu.VMEM((owners, *qkv_shape), LOW),
             pltpu.VMEM((4, *quarter_shape(*up_shape)), LOW),
-            pltpu.SemaphoreType.DMA((6,)),
-            pltpu.SemaphoreType.DMA((4, GATHER_SEMS)),
+            pltpu.VMEM((4, *quarter_shape(*out_shape)), LOW),
+            pltpu.SemaphoreType.DMA((7,)),
+            pltpu.SemaphoreType.DMA((5, GATHER_SEMS)),
         ],
         compiler_params=pltpu.CompilerParams(
             collective_id=1, has_side_effects=True, vmem_limit_bytes=VMEM_LIMIT
@@ -715,14 +788,14 @@
         position_table,
         global_vector[None, :],
     )
-    up_zero, qkv_one, up_one, output_one, head_low = results[6:]
+    up_zero, output_zero, qkv_one, up_one, output_one, head_low = results[7:]
     return (
         results[0],
         results[1],
         results[2:4],
         results[4].reshape(owners * depth, 3 * D),
-        [GatherRide(up_zero, results[5]), LevelRide(qkv_one), LevelRide(output_one)],
-        [up_one, head_low],
+        [GatherRide(up_zero, results[5]), GatherRide(output_zero, results[6]), LevelRide(output_one)],
+        [qkv_one, up_one, head_low],
     )
 
 
@@ -858,6 +931,9 @@
         lax.fori_loop(0, high // self.chunk, add, 0)
         for other in TURNS:
             self.share_copy(other).start()
+
+    def store(self):
+        self.target[...] = self.out[...]
 
     def fifth(self):
         for other in TURNS:
@@ -1047,6 +1123,9 @@
         lax.fori_loop(0, self.high // chunk, add, 0)
         for other in TURNS:
             self.share_copy(other).start()
+
+    def store(self):
+        self.target[...] = self.out[...]
 
     def fifth(self):
         for other in TURNS:
@@ -1353,14 +1432,6 @@
     total = sum(jnp.sum(jnp.square(out.astype(jnp.float32))) for out in (*finished, *outs))
     row = jnp.full((1, LANES), 1.0 / LANES, jnp.float32) * total
     return [*outs, own, lax.all_gather(own.at[-1:].set(row), "fsdp", axis=0)]
-
-
-def take(items, *counts):
-    cut = []
-    for count in counts:
-        cut.append(items[:count])
-        items = items[count:]
-    return cut
 
 
 def scatter(grad):
@@ -1784,91 +1855,56 @@
     )
 
 
-def qkv_back_kernel(
-    grad_ref, residual_ref, stream_ref, weight_ref, vector_ref, out_ref, sums_ref, normed_ref
-):
-    rows = stream_ref.shape[0]
+def qkv_back_kernel(grad_ref, residual_ref, stream_ref, weight_ref, vector_ref, out_ref, sums_ref):
+    grad = grad_ref[...]
+    normed_grad = mul_nt(grad, weight_ref[...])
+    value_grad, gain_grad, shift_grad = norm_backward(normed_grad, stream_ref[...], vector_ref[:, :D])
+    out_ref[...] = residual_ref[...] + value_grad
+    sums = jnp.concatenate([gain_grad, shift_grad, column_sum(grad)], 1)
 
     @at_first
     def _():
-        normed_ref[...] = jnp.zeros_like(normed_ref)
-
-    for half in halves_of(rows):
-        normed_ref[half, :] += mul_nt(grad_ref[half, :], weight_ref[...])
-    sums_ref[:, chunk_at(2 * D)] = column_sum(grad_ref[...])
-
-    @at_last
-    def _():
-        totals = [0.0] * 2
-        for half in halves_of(rows):
-            value_grad, gain_grad, shift_grad = norm_backward(
-                normed_ref[half, :], stream_ref[half, :], vector_ref[:, :D]
-            )
-            out_ref[half, :] = residual_ref[half, :] + value_grad
-            totals = [totals[0] + gain_grad, totals[1] + shift_grad]
-        sums_ref[:, : 2 * D] = jnp.concatenate(totals, 1)
+        sums_ref[...] = jnp.zeros_like(sums_ref)
+
+    sums_ref[...] += sums
 
 
 def qkv_backward(grad, residual_grad, stream, weight, vector):
     rows = stream.shape[0]
-    whole = fixed(rows, D)
+    block = 256
+    narrow = rows_of(block, D)
     return block_call(
         qkv_back_kernel,
-        3,
-        [columns_of(rows), whole, whole, columns_of(D), fixed(1, vector.shape[1])],
+        rows // block,
+        [rows_of(block, 3 * D), narrow, narrow, fixed(D, 3 * D), fixed(1, vector.shape[1])],
         [grad, residual_grad, stream, weight, vector],
-        [whole, fixed(1, 5 * D)],
+        [narrow, fixed(1, 5 * D)],
         [shape_of(rows, D), shape_of(1, 5 * D)],
-        [pltpu.VMEM((rows, D), jnp.float32)],
+        [],
         "qkv_backward",
     )
 
 
-def input_grad_kernel(first_ref, second_ref, qkv_ref, hidden_ref, qkv_out, up_out, left_ref, *, cut):
-    step = pl.program_id(0)
-
-    @pl.when(step == 0)
+def input_grad_kernel(left_ref, right_ref, out_ref, turned_ref):
+    @at_first
     def _():
-        left_ref[...] = first_ref[...].T
-
-    @pl.when(step == cut)
-    def _():
-        left_ref[...] = second_ref[...].T
-
-    @pl.when(step < cut)
-    def _():
-        qkv_out[...] = mul(left_ref[...], qkv_ref[...]).astype(jnp.bfloat16)
-
-    @pl.when(step >= cut)
-    def _():
-        up_out[...] = mul(left_ref[...], hidden_ref[...]).astype(jnp.bfloat16)
-
-
-def input_weight_grad(first, second, qkv_grad, hidden_grad):
-    rows = first.shape[0]
-    cut = qkv_grad.shape[1] // D
-    steps = cut + hidden_grad.shape[1] // D
-    before = lambda i: (0, jnp.minimum(i, cut - 1))
-    after = lambda i: (0, jnp.maximum(i - cut, 0))
+        turned_ref[...] = left_ref[...].T
+
+    out_ref[...] = mul(turned_ref[...], right_ref[...]).astype(LOW)
+
+
+def input_weight_grad(left, right):
+    rows, width = right.shape
     return block_call(
-        functools.partial(input_grad_kernel, cut=cut),
-        steps,
-        [
-            fixed(rows, D),
-            fixed(rows, D),
-            pl.BlockSpec((rows, D), before),
-            pl.BlockSpec((rows, D), after),
-        ],
-        [first, second, qkv_grad, hidden_grad],
-        [pl.BlockSpec((D, D), before), pl.BlockSpec((D, D), after)],
-        [
-            shape_of(D, qkv_grad.shape[1], dtype=jnp.bfloat16),
-            shape_of(D, hidden_grad.shape[1], dtype=jnp.bfloat16),
-        ],
-        [pltpu.VMEM((D, rows), jnp.bfloat16)],
+        input_grad_kernel,
+        width // D,
+        [fixed(rows, D), columns_of(rows)],
+        [left, right],
+        [columns_of(D)],
+        [shape_of(D, width, dtype=LOW)],
+        [pltpu.VMEM((D, rows), LOW)],
         "input_weight_grad",
-        None,
-    )
+    )[0]
 
 
 def output_grad_kernel(attended_ref, active_ref, residual_ref, grad_ref, *outs, cut):
@@ -2043,7 +2079,6 @@
     owners = lax.axis_size("fsdp")
     nodes = position_table.shape[0]
     vector_size = layer_vector.size
-    output_zero = lax.all_gather(output_proj[0].astype(LOW), "fsdp", axis=0, tiled=True)
     stream, pos_weights_t, vectors, qkv_weight, rides, rest_shards = begin(
         pixels,
         segment,
@@ -2056,24 +2091,20 @@
         position_table,
         global_vector,
     )
-    up_one, head_full = (
+    qkv_one, up_one, head_full = (
         lax.all_gather(shard, "fsdp", axis=0, tiled=True) for shard in rest_shards
     )
-    up_ride, qkv_ride, output_ride = rides
     saved_layers = []
     for index in range(LAYERS):
         vector = vectors[index]
         normed, qkv_rows = qkv_forward(stream, qkv_weight, vector)
         if index == 0:
-            attended, expo, inverse, up, qkv_ride = attention_forward(
-                qkv_rows, segment, [up_ride, qkv_ride], 4
-            )
-            output, mlp_rides = output_zero, [qkv_ride, output_ride]
+            attended, expo, inverse, up, output = attention_forward(qkv_rows, segment, rides[:2], 4)
         else:
             attended, expo, inverse, output = attention_forward(qkv_rows, segment, [output_ride], 5)
-            up, mlp_rides = up_one, ()
+            up = up_one
         residual, normed_second, active, slope, following, *fetched = mlp_forward(
-            stream, attended, up, output, vector, mlp_rides, 7
+            stream, attended, up, output, vector, () if index else rides[2:], 7
         )
         saved_layers.append(
             (
@@ -2084,13 +2115,12 @@
         )
         stream = following
         if fetched:
-            qkv_weight, output_ride = fetched
+            qkv_weight, (output_ride,) = qkv_one, fetched
     stream_grad, head_grad, final_sums, head_bias_grad, numbers = head(
         stream, segment, labels, head_full, global_vector, head_weight.shape[1]
     )
-    head_part = scatter(by_owner(head_grad))
     vector_grads = [None] * LAYERS
-    early_parts, late_parts = [head_part], []
+    early_parts, late_parts = [], []
     for index in reversed(range(LAYERS)):
         (qkv_weight, up, output, vector), first, second = saved_layers[index]
         entering, normed, qkv_rows, attended, expo, inverse = first
@@ -2102,25 +2132,27 @@
             attended, active, residual_low, grad_low, (D // 2,) * 2 if index else (D,)
         )
         attended_grad, *output_grads = lax.optimization_barrier((attended_grad, *output_grads))
+        up_grad = input_weight_grad(normed_second, hidden_grad)
         output_parts = [scatter(by_owner(grad)) for grad in output_grads]
         if index:
             early_parts.extend(output_parts)
+            beside = [SumRide(by_owner(head_grad), False)]
         else:
             (last_part,) = output_parts
-        qkv_grad, *early_sums = attention_backward(
-            qkv_rows,
-            expo,
-            inverse,
-            attended,
-            attended_grad,
-            () if index else [ShareRide(early_parts[0]), ShareRide(jnp.concatenate(early_parts[1:], 1))],
-            6,
+            beside = [ShareRide(jnp.concatenate(early_parts, 1)), SumRide(by_owner(up_grad), True)]
+        qkv_grad, *beside_sums = attention_backward(
+            qkv_rows, expo, inverse, attended, attended_grad, beside, 6 if index else 8
         )
         stream_grad, qkv_sums = qkv_backward(qkv_grad, residual_grad, entering, qkv_weight, vector)
-        input_grads = input_weight_grad(normed, normed_second, qkv_grad, hidden_grad)
+        qkv_weight_grad = input_weight_grad(normed, qkv_grad)
         if index:
-            stream_grad, *input_grads = lax.optimization_barrier((stream_grad, *input_grads))
-            late_parts.extend(scatter(by_owner(grad)) for grad in input_grads)
+            (head_sum,) = beside_sums
+            stream_grad, qkv_weight_grad, up_grad = lax.optimization_barrier(
+                (stream_grad, qkv_weight_grad, up_grad)
+            )
+            late_parts.extend(scatter(by_owner(grad)) for grad in (qkv_weight_grad, up_grad))
+        else:
+            output_one_sum, up_zero_sum = beside_sums
         vector_grads[index] = jnp.concatenate(
             [
                 qkv_sums[0, : 2 * D],
@@ -2150,22 +2182,24 @@
     used = vector_rows + rest_rows
     block_rows = (used // 64 + 1) * 64
     small = jnp.pad(small.reshape(owners, used, LANES), ((0, 0), (0, block_rows - used), (0, 0)))
-    input_zero_sums, kernel_sum, input_one_sums = take(
-        reduce_all([by_owner(grad) for grad in (*input_grads, kernel_grad)], late_parts, 2), 2, 1, 2
+    qkv_zero_sum, kernel_sum, *input_one_sums = reduce_all(
+        [by_owner(qkv_weight_grad), by_owner(kernel_grad)], late_parts, 2
     )
     output_zero_sum, small_share, small_full = finish_all(
-        [*early_sums, *input_zero_sums, *kernel_sum, *input_one_sums], [last_part], small, 3
-    )
-    head_sum, output_one_sum = early_sums
+        [head_sum, output_one_sum, up_zero_sum, qkv_zero_sum, kernel_sum, *input_one_sums],
+        [last_part],
+        small,
+        3,
+    )
     rest_sum = small_full[:, vector_rows:used].reshape(-1)
     position_sum = rest_sum[: position_grad.size].reshape(position_grad.shape)
     global_sum = rest_sum[position_grad.size :][: global_vector.shape[0]]
     loss_sum = rest_sum[rest.shape[0] - 2]
     token_total = rest_sum[rest.shape[0] - 1]
-    kernel_sum = kernel_sum[0].astype(jnp.float32)
+    kernel_sum = kernel_sum.astype(jnp.float32)
     head_sum = head_sum[:, :CLS].astype(jnp.float32)
     input_sum = jnp.stack(
-        [jnp.concatenate(pair, 1) for pair in (input_zero_sums, input_one_sums)]
+        [jnp.concatenate(pair, 1) for pair in ((qkv_zero_sum, up_zero_sum), input_one_sums)]
     ).astype(jnp.float32)
     output_sum = jnp.stack([output_zero_sum, output_one_sum]).astype(
         jnp.float32

time: 721 us -> 680 us (0.943)
  waiting for transfers between devices: 40.2 us -> 2.78 us
    pallas_call x17 -> x19, Pallas kernels: 362 us -> 416 us  [block_call(): pl.pallas_call(kernel, grid=(grid,), in_specs=in_specs, out_specs=out_spe...]
    reduce_scatter x6 -> x5, waiting for transfers between devices: 37.6 us -> 0.06 us  [scatter(): return lax.psum_scatter(grad, 'fsdp', scatter_dimension=0)]
    pallas_call x1, Pallas kernels: 108 us -> 74.1 us  [reduce_call(): pl.pallas_call(functools.partial(reduce_kernel, whole=whole, partly=partl...]
    pallas_call x1, Pallas kernels: 83 us -> 63.3 us  [begin(): pl.pallas_call(functools.partial(first_kernel, spots=spots), in_specs=[AN...]
  transfers between devices with their start and end apart: 9 -> 8, of which waited for: 2 -> 0; matrix products, arithmetic and copies ran while one was open for 2% -> 1% of each run, Pallas kernels for 73% -> 68%
where the time goes in v9:
time: 680 us; the launch traced here: 673 us
  Pallas kernels  601 us (88%)
  other arithmetic  32.6 us (5%)
  between operations  20.7 us (3%)
  local copies, waits for them, and re-layouts  14.9 us (2%)
    pallas_call x19, Pallas kernels, block_call(): pl.pallas_call(kernel, grid=(grid,), in_specs=in_specs, out_specs=out_spe...  416 us
    pallas_call x1, Pallas kernels, reduce_call(): pl.pallas_call(functools.partial(reduce_kernel, whole=whole, partly=partl...  74.1 us
    pallas_call x1, Pallas kernels, begin(): pl.pallas_call(functools.partial(first_kernel, spots=spots), in_specs=[AN...  63.3 us
    pallas_call x1, Pallas kernels, finish_call(): pl.pallas_call(functools.partial(finish_kernel, done=done, partly=partly)...  35.6 us
    sub x7, other arithmetic, adam_update(): return (moment, square, weight - learn_rate * step_dir)  22.7 us
  transfers between devices with their start and end apart: 8, of which 0 were waited for; matrix products, arithmetic and copies ran while one was open for 1% of the time, Pallas kernels for 68%

profile of v9, /device:TPU:0, one launch (start us, length us, event | category | flops | bytes accessed | tf_op | source)
XLA Modules:
  0.0 672.5 jit_solution(281925228125091536)
XLA Ops:
  7.2 0.7 convert_element_type.23
  8.0 0.2 dynamic_update_slice.3
  8.2 0.6 reshape.122.refs_1_
  8.8 1.3 broadcast_in_dim.22.refs_9_
  10.2 1.7 copy.50.refs_6_.refs_3_.seg_col_ref
  11.9 63.3 %begin.1 = (f32[1024,768]{1,0:T(8,128)}, f32[64,1024]{1,0:T(8,128)}, f32[1,9984]{1,0:T(1,128)}, f32[1,9984]{1,0:T(1,128)}, bf16[8,96,2304]{2,1,0:T(8,128)(2,1)},...) custom-call(f32[384,768]{1,0:T(8,128)} %refs_0_.1, ...), custom_call_target="tpu_custom_call" | custom-call | tf_op jit(solution)/shard_map/begin/pallas_call | solution.py:757
  75.2 0.7 all-gather.6.cloned.1.call-update
  76.0 0.7 all-gather.8.cloned.1.call-update
  76.6 0.2 reduce-scatter.6.cloned.1.call-start
  76.9 9.2 %qkv_forward.2 = (bf16[1024,768]{1,0:T(8,128)(2,1)}, bf16[1024,2304]{1,0:T(8,128)(2,1)}) custom-call(f32[1024,768]{1,0:T(8,128)} %get-tuple-element.107.stream_ref.refs_0_, bf16[768,2304]{1,0:T(8,128)(2,1)} %bitcast.55, f32[1,9984]{1,0:T(1,128)} %get-tuple-element.109.vector_ref.refs_5_), custom_call_target="tpu_custom_call" | custom-call | flops 3623878656 | bytes 14548992 | tf_op jit(solution)/shard_map/qkv_forward/pallas_call | solution.py:536
  86.0 51.8 %attention_forward.2 = (bf16[1024,768]{1,0:T(8,128)(2,1)}, bf16[12,1024,1024]{2,1,0:T(8,128)(2,1)}, f32[1024,768]{1,0:T(8,128)}, bf16[8,96,3072]{2,1,0:T(8,128)(2,1)}, bf16[8,480,768]{2,1,0:T(8,128)(2,1)}) custom-call(bf16[1024,2304]{1,0:T(8,128)(2,1)} %get-tuple-element.110.refs_0_.refs_1_.refs_2_, ...), custom_call_target="tpu_custom_call" | custom-call | flops 12884901888 | bytes 34603008 | tf_op jit(solution)/shard_map/attention_forward/pallas_call | solution.py:536
  137.9 35.1 %mlp_forward.2 = (f32[1024,768]{1,0:T(8,128)}, bf16[1024,768]{1,0:T(8,128)(2,1)}, bf16[1024,3072]{1,0:T(8,128)(2,1)}, bf16[1024,3072]{1,0:T(8,128)(2,1)}, f32[10...) custom-call(f32[1024,768]{1,0:T(8,128)} %get-tuple-element.107.stream_ref.refs_0_, ...), custom_call_target="tpu_custom_call" | custom-call | flops 10871635968 | bytes 35782656 | tf_op jit(solution)/shard_map/mlp_forward/pallas_call | solution.py:536
  173.0 0.7 copy.54.label_ref
  173.6 0.6 broadcast_in_dim.24.vector_ref
  174.2 9.4 %qkv_forward.3 = (bf16[1024,768]{1,0:T(8,128)(2,1)}, bf16[1024,2304]{1,0:T(8,128)(2,1)}) custom-call(f32[1024,768]{1,0:T(8,128)} %get-tuple-element.119.stream_ref, bf16[768,2304]{1,0:T(8,128)(2,1)} %all-gather.4.cloned.1.call-done.weight_ref, f32[1,9984]{1,0:T(1,128)} %get-tuple-element.121.vector_ref), custom_call_target="tpu_custom_call" | custom-call | flops 3623878656 | bytes 14548992 | tf_op jit(solution)/shard_map/qkv_forward/pallas_call | solution.py:536
  183.6 43.8 %attention_forward.3 = (bf16[1024,768]{1,0:T(8,128)(2,1)}, bf16[12,1024,1024]{2,1,0:T(8,128)(2,1)}, f32[1024,768]{1,0:T(8,128)}, bf16[8,480,768]{2,1,0:T(8,128)(2,1)}) custom-call(bf16[1024,2304]{1,0:T(8,128)(2,1)} %get-tuple-element.122.refs_0_.refs_1_.refs_2_, bf16[1024,2304]{1,0:T(8,128)(2,1)} %get-tuple-element.122.refs_0_.refs_1_.refs_2_, ...), custom_call_target="tpu_custom_call" | custom-call | flops 12884901888 | bytes 34603008 | tf_op jit(solution)/shard_map/attention_forward/pallas_call | solution.py:536
  227.5 21.4 %mlp_forward.3 = (f32[1024,768]{1,0:T(8,128)}, bf16[1024,768]{1,0:T(8,128)(2,1)}, bf16[1024,3072]{1,0:T(8,128)(2,1)}, bf16[1024,3072]{1,0:T(8,128)(2,1)}, f32[1024,768]{1,0:T(8,128)}) custom-call(f32[1024,768]{1,0:T(8,128)} %get-tuple-element.119.stream_ref, bf16[1024,768]{1,0:T(8,128)(2,1)} %get-tuple-element.126.attended_ref.refs_5_, ...), custom_call_target="tpu_custom_call" | custom-call | flops 10871635968 | bytes 35782656 | tf_op jit(solution)/shard_map/mlp_forward/pallas_call | solution.py:536
  248.9 11.7 %head.1 = (f32[1024,768]{1,0:T(8,128)}, bf16[768,1024]{1,0:T(8,128)(2,1)}, f32[1,1536]{1,0:T(1,128)}, f32[1,1024]{1,0:T(1,128)}, f32[1,2]{1,0:T(1,128)}) custom-call(f32[1024,768]{1,0:T(8,128)} %get-tuple-element.129.stream_ref, s32[1024,1]{1,0:T(8,128)} %copy.50.refs_6_.refs_3_.seg_col_ref, s32[1,1024]{1,0:T(1,128)} %bitcast.75, s32[8,1]{1,0:T(8,128)} %copy.54.label_ref, ...), custom_call_target="tpu_custom_call" | custom-call | tf_op jit(solution)/shard_map/head/pallas_call | solution.py:2025
  260.6 22.6 %mlp_backward.2 = (bf16[1024,768]{1,0:T(8,128)(2,1)}, bf16[1024,3072]{1,0:T(8,128)(2,1)}, f32[1024,768]{1,0:T(8,128)}, bf16[1024,768]{1,0:T(8,128)(2,1)}, bf16[1024,768]{1,0:T(8,128)(2,1)}, /*index=5*/f32[1,6144]{1,0:T(1,128)}) custom-call(f32[1024,768]{1,0:T(8,128)} %get-tuple-element.131.grad_ref, bf16[1024,3072]{1,0:T(8,128)(2,1)} %get-tuple-element.132.slope_ref, ...), custom_call_target="tpu_custom_call" | custom-call | tf_op jit(solution)/shard_map/mlp_backward/pallas_call | solution.py:536
  283.2 11.9 %output_weight_grad.2 = (bf16[3840,384]{1,0:T(8,128)(2,1)}, bf16[3840,384]{1,0:T(8,128)(2,1)}) custom-call(bf16[1024,768]{1,0:T(8,128)(2,1)} %get-tuple-element.126.attended_ref.refs_5_, bf16[1024,3072]{1,0:T(8,128)(2,1)} %get-tuple-element.135.active_ref, bf16[1024,768]{1,0:T(8,128)(2,1)} %get-tuple-element.136.residual_ref, ...), custom_call_target="tpu_custom_call" | custom-call | tf_op jit(solution)/shard_map/output_weight_grad/pallas_call | solution.py:536
  295.2 0.5 reduce-scatter.8.cloned.1.call-update
  295.8 35.2 %attention_backward.2 = (bf16[1024,2304]{1,0:T(8,128)(2,1)}, bf16[96,1024]{1,0:T(8,128)(2,1)}) custom-call(bf16[1024,2304]{1,0:T(8,128)(2,1)} %get-tuple-element.122.refs_0_.refs_1_.refs_2_, bf16[1024,2304]{1,0:T(8,128)(2,1)} %get-tuple-element.122.refs_0_.refs_1_.refs_2_, bf16[1024,2304]{1,0:T(8,128)(2,1)} %get-tuple-element.122.refs_0_.refs_1_.refs_2_, ...), custom_call_target="tpu_custom_call" | custom-call | tf_op jit(solution)/shard_map/attention_backward/pallas_call | solution.py:536
  331.0 8.1 %input_weight_grad.4 = bf16[768,2304]{1,0:T(8,128)(2,1)} custom-call(bf16[1024,768]{1,0:T(8,128)(2,1)} %get-tuple-element.148.left_ref, bf16[1024,2304]{1,0:T(8,128)(2,1)} %get-tuple-element.145.grad_ref.right_ref), custom_call_target="tpu_custom_call" | custom-call | tf_op jit(solution)/shard_map/input_weight_grad/pallas_call | solution.py:536
  339.1 9.7 %input_weight_grad.5 = bf16[768,3072]{1,0:T(8,128)(2,1)} custom-call(bf16[1024,768]{1,0:T(8,128)(2,1)} %get-tuple-element.149.left_ref, bf16[1024,3072]{1,0:T(8,128)(2,1)} %get-tuple-element.150.right_ref), custom_call_target="tpu_custom_call" | custom-call | tf_op jit(solution)/shard_map/input_weight_grad/pallas_call | solution.py:536
  348.8 10.4 %qkv_backward.2 = (f32[1024,768]{1,0:T(8,128)}, f32[1,3840]{1,0:T(1,128)}) custom-call(bf16[1024,2304]{1,0:T(8,128)(2,1)} %get-tuple-element.145.grad_ref.right_ref, f32[1024,768]{1,0:T(8,128)} %get-tuple-element.146.residual_ref, f32[1024,768]{1,0:T(8,128)} %get-tuple-element.119.stream_ref, bf16[768,2304]{1,0:T(8,128)(2,1)} %all-gather.4.cloned.1.call-done.weight_ref, ...), custom_call_target="tpu_custom_call" | custom-call | tf_op jit(solution)/shard_map/qkv_backward/pallas_call | solution.py:536
  359.3 0.7 reduce-scatter.12.cloned.1.call-update
  360.0 23.1 %mlp_backward.3 = (bf16[1024,768]{1,0:T(8,128)(2,1)}, bf16[1024,3072]{1,0:T(8,128)(2,1)}, f32[1024,768]{1,0:T(8,128)}, bf16[1024,768]{1,0:T(8,128)(2,1)}, bf16[1024,768]{1,0:T(8,128)(2,1)}, /*index=5*/f32[1,6144]{1,0:T(1,128)}) custom-call(f32[1024,768]{1,0:T(8,128)} %get-tuple-element.151.grad_ref, bf16[1024,3072]{1,0:T(8,128)(2,1)} %get-tuple-element.152.slope_ref, ...), custom_call_target="tpu_custom_call" | custom-call | tf_op jit(solution)/shard_map/mlp_backward/pallas_call | solution.py:536
  383.2 12.0 %output_weight_grad.3 = bf16[3840,768]{1,0:T(8,128)(2,1)} custom-call(bf16[1024,768]{1,0:T(8,128)(2,1)} %get-tuple-element.115.refs_1_.attended_ref.refs_5_, bf16[1024,3072]{1,0:T(8,128)(2,1)} %get-tuple-element.155.active_ref, bf16[1024,768]{1,0:T(8,128)(2,1)} %get-tuple-element.156.residual_ref, bf16[1024,768]{1,0:T(8,128)(2,1)} %get-tuple-element.157.grad_ref), custom_call_target="tpu_custom_call" | custom-call | tf_op jit(solution)/shard_map/output_weight_grad/pallas_call | solution.py:536
  395.2 0.7 copy-done.18
  396.0 0.1 stack.28
  396.2 9.7 %input_weight_grad.6 = bf16[768,3072]{1,0:T(8,128)(2,1)} custom-call(bf16[1024,768]{1,0:T(8,128)(2,1)} %get-tuple-element.161.left_ref, bf16[1024,3072]{1,0:T(8,128)(2,1)} %get-tuple-element.162.right_ref), custom_call_target="tpu_custom_call" | custom-call | tf_op jit(solution)/shard_map/input_weight_grad/pallas_call | solution.py:536
  406.0 2.0 pad_maximum_fusion.2.refs_7_
  408.0 72.7 %attention_backward.3 = (bf16[1024,2304]{1,0:T(8,128)(2,1)}, bf16[480,768]{1,0:T(8,128)(2,1)}, bf16[96,3072]{1,0:T(8,128)(2,1)}) custom-call(bf16[1024,2304]{1,0:T(8,128)(2,1)} %get-tuple-element.110.refs_0_.refs_1_.refs_2_, bf16[1024,2304]{1,0:T(8,128)(2,1)} %get-tuple-element.110.refs_0_.refs_1_.refs_2_, ...), custom_call_target="tpu_custom_call" | custom-call | tf_op jit(solution)/shard_map/attention_backward/pallas_call | solution.py:536
  480.8 10.4 %qkv_backward.3 = (f32[1024,768]{1,0:T(8,128)}, f32[1,3840]{1,0:T(1,128)}) custom-call(bf16[1024,2304]{1,0:T(8,128)(2,1)} %get-tuple-element.166.right_ref.grad_ref, f32[1024,768]{1,0:T(8,128)} %get-tuple-element.167.residual_ref, f32[1024,768]{1,0:T(8,128)} %get-tuple-element.107.stream_ref.refs_0_, bf16[768,2304]{1,0:T(8,128)(2,1)} %bitcast.56, ...), custom_call_target="tpu_custom_call" | custom-call | tf_op jit(solution)/shard_map/qkv_backward/pallas_call | solution.py:536
  491.2 0.7 slice_reduce_fusion.3
  491.9 0.7 slice_reduce_fusion.6
  492.6 0.1 stack.27
  492.8 0.1 reshape.137
  493.0 11.9 %embed_backward.1 = (bf16[3072,768]{1,0:T(8,128)(2,1)}, f32[64,768]{1,0:T(8,128)}, f32[1,768]{1,0:T(1,128)}) custom-call(bf16[1024,3072]{1,0:T(8,128)(2,1)} %pixel_ref.1, f32[1024,768]{1,0:T(8,128)} %get-tuple-element.168.grad_ref, f32[64,1024]{1,0:T(8,128)} %get-tuple-element.169.pos_ref), custom_call_target="tpu_custom_call" | custom-call | tf_op jit(solution)/shard_map/embed_backward/pallas_call | solution.py:536
  504.8 0.7 reduce.10
  505.5 0.9 slice.70
  506.5 0.1 concatenate.25
  506.8 0.7 pad.19.refs_8_
  507.5 8.0 %input_weight_grad.7 = bf16[768,2304]{1,0:T(8,128)(2,1)} custom-call(bf16[1024,768]{1,0:T(8,128)(2,1)} %get-tuple-element.165.left_ref, bf16[1024,2304]{1,0:T(8,128)(2,1)} %get-tuple-element.166.right_ref.grad_ref), custom_call_target="tpu_custom_call" | custom-call | tf_op jit(solution)/shard_map/input_weight_grad/pallas_call | solution.py:536
  515.5 74.1 %reduce_gradients.1 = (bf16[96,2304]{1,0:T(8,128)(2,1)}, bf16[384,768]{1,0:T(8,128)(2,1)}, bf16[96,2304]{1,0:T(8,128)(2,1)}, bf16[96,3072]{1,0:T(8,128)(2,1)}) custom-call(bf16[8,96,2304]{2,1,0:T(8,128)(2,1)} %bitcast.51, bf16[8,384,768]{2,1,0:T(8,128)(2,1)} %bitcast.52, bf16[96,2304]{1,0:T(8,128)(2,1)} %bitcast.69, bf16[96,3072]{1,0:T(8,128)(2,1)} %bitcast.68), custom_call_target="tpu_custom_call" | custom-call | tf_op jit(solution)/shard_map/reduce_gradients/pallas_call | solution.py:1347
  589.7 1.5 maximum_bitcast_fusion
  591.2 35.6 %finish_gradients.1 = (bf16[480,768]{1,0:T(8,128)(2,1)}, f32[64,128]{1,0:T(8,128)}, f32[8,64,128]{2,1,0:T(8,128)}) custom-call(bf16[96,1024]{1,0:T(8,128)(2,1)} %get-tuple-element.142.refs_0_, bf16[480,768]{1,0:T(8,128)(2,1)} %get-tuple-element.163.refs_1_, bf16[96,3072]{1,0:T(8,128)(2,1)} %get-tuple-element.164.refs_2_, ...), custom_call_target="tpu_custom_call" | custom-call | tf_op jit(solution)/shard_map/finish_gradients/pallas_call | solution.py:1400
  626.8 1.6 multiply_reduce_fusion.1
  628.4 1.4 slice_reduce_fusion.8
  629.8 0.9 slice.72
  630.7 0.6 multiply_reduce_fusion.2
  631.3 0.6 multiply_reduce_fusion
  632.0 0.6 fusion.15
  632.6 0.7 slice_bitcast_fusion
  638.0 0.7 slice_multiply_fusion
  638.7 1.6 mul.230
  640.3 0.6 multiply_subtract_fusion.5
  641.0 2.7 multiply_subtract_fusion.3
  643.7 3.9 multiply_subtract_fusion.2
  647.6 0.6 multiply_subtract_fusion.6
  648.3 1.9 multiply_subtract_fusion.4
  650.3 6.7 multiply_subtract_fusion.1
  656.9 1.2 copy-done.4
  658.1 6.2 multiply_subtract_fusion
  (84 shorter events, 1.1 us)
Async XLA Ops:
  7.2 167.1 %all-gather.4.cloned.1.call-start = ((), (), s32[]{:S(2)}) async-start(), calls=%async_computation.5 | async-start | bytes 3981312 | tf_op jit(solution)/shard_map/all_gather | solution.py:2095
  75.2 152.3 %all-gather.6.cloned.1.call-start = ((), (), s32[]{:S(2)}) async-start(), calls=%async_computation.6 | async-start | bytes 5308416 | tf_op jit(solution)/shard_map/all_gather | solution.py:2095
  75.9 173.0 %all-gather.8.cloned.1.call-start = ((), (), s32[]{:S(2)}) async-start(), calls=%async_computation.7 | async-start | bytes 1769472 | tf_op jit(solution)/shard_map/all_gather | solution.py:2095
  76.6 329.3 %reduce-scatter.6.cloned.1.call-start = ((), (), s32[]{:S(2)}) async-start(), calls=%async_computation.8 | async-start | bytes 3317760 | tf_op jit(solution)/shard_map/reduce_scatter | solution.py:1438
  137.8 35.1 %copy-start.24 = (s32[1,8]{1,0:T(1,128)S(1)}, s32[1,8]{1,0:T(1,128)}, u32[]{:S(2)}) copy-start(s32[1,8]{1,0:T(1,128)} %param.28) | copy-start | bytes 100
  137.8 35.8 %copy-start.12 = (f32[3304]{0:T(1024)S(1)}, f32[3304]{0:T(1024)}, u32[]{:S(2)}) copy-start(f32[3304]{0:T(1024)} %param.35) | copy-start | bytes 39652
  295.2 110.8 %reduce-scatter.8.cloned.1.call-start = ((), (), s32[]{:S(2)}) async-start(), calls=%async_computation.9 | async-start | bytes 3317760 | tf_op jit(solution)/shard_map/reduce_scatter | solution.py:1438
  295.8 219.7 %reduce-scatter.10.cloned.1.call-start = ((), (), s32[]{:S(2)}) async-start(), calls=%async_computation.10 | async-start | bytes 3981312 | tf_op jit(solution)/shard_map/reduce_scatter | solution.py:1438
  359.2 156.3 %reduce-scatter.12.cloned.1.call-start = ((), (), s32[]{:S(2)}) async-start(), calls=%async_computation.11 | async-start | bytes 5308416 | tf_op jit(solution)/shard_map/reduce_scatter | solution.py:1438
  360.0 231.2 %reduce-scatter.14.cloned.1.call-start = ((), (), s32[]{:S(2)}) async-start(), calls=%async_computation.12 | async-start | bytes 6635520 | tf_op jit(solution)/shard_map/reduce_scatter | solution.py:1438
  395.2 0.7 copy-start.18
  395.2 0.8 copy-start.14
  395.2 1.0 copy-start.21
  396.2 9.7 %copy-start.15 = (f32[1,6144]{1,0:T(1,128)S(1)}, f32[1,6144]{1,0:T(1,128)}, u32[]{:S(2)}) copy-start(f32[1,6144]{1,0:T(1,128)} %get-tuple-element.179) | copy-start | bytes 73732
  493.0 13.5 %copy-start.22 = (f32[1,1024]{1,0:T(1,128)S(1)}, f32[1,1024]{1,0:T(1,128)}, u32[]{:S(2)}) copy-start(f32[1,1024]{1,0:T(1,128)} %get-tuple-element.185) | copy-start | bytes 12292
  493.0 13.6 %copy-start.23 = (f32[1,2]{1,0:T(1,128)S(1)}, f32[1,2]{1,0:T(1,128)}, u32[]{:S(2)}) copy-start(f32[1,2]{1,0:T(1,128)} %get-tuple-element.186) | copy-start | bytes 28
  515.5 74.1 %copy-start.8 = (bf16[96,3072]{1,0:T(8,128)(2,1)S(1)}, bf16[96,3072]{1,0:T(8,128)(2,1)}, u32[]{:S(2)}) copy-start(bf16[96,3072]{1,0:T(8,128)(2,1)} %get-tuple-element.164.refs_2_) | copy-start | bytes 1769476
  591.2 49.2 %copy-start.16 = (f32[3304]{0:T(1024)S(1)}, f32[3304]{0:T(1024)}, u32[]{:S(2)}) copy-start(f32[3304]{0:T(1024)} %param.49) | copy-start | bytes 39652
  591.2 49.2 %copy-start.17 = (f32[3304]{0:T(1024)S(1)}, f32[3304]{0:T(1024)}, u32[]{:S(2)}) copy-start(f32[3304]{0:T(1024)} %param.42) | copy-start | bytes 39652
  591.2 56.4 %copy-start.13 = (f32[2,1248]{1,0:T(2,128)S(1)}, f32[2,1248]{1,0:T(2,128)}, u32[]{:S(2)}) copy-start(f32[2,1248]{1,0:T(2,128)} %param.33) | copy-start | bytes 29956
  591.2 56.4 %copy-start.19 = (f32[2,1248]{1,0:T(2,128)S(1)}, f32[2,1248]{1,0:T(2,128)}, u32[]{:S(2)}) copy-start(f32[2,1248]{1,0:T(2,128)} %param.47) | copy-start | bytes 29956
  591.2 56.4 %copy-start.20 = (f32[2,1248]{1,0:T(2,128)S(1)}, f32[2,1248]{1,0:T(2,128)}, u32[]{:S(2)}) copy-start(f32[2,1248]{1,0:T(2,128)} %param.40) | copy-start | bytes 29956
  626.8 16.9 %copy-start.2 = (f32[384,768]{1,0:T(8,128)S(1)}, f32[384,768]{1,0:T(8,128)}, u32[]{:S(2)}) copy-start(f32[384,768]{1,0:T(8,128)} %refs_0_.1) | copy-start | bytes 3538948
  640.3 3.3 copy-start.9
  640.3 3.3 copy-start.10
  641.0 7.3 %copy-start.11 = (f32[49,768]{1,0:T(8,128)S(1)}, f32[49,768]{1,0:T(8,128)}, u32[]{:S(2)}) copy-start(f32[49,768]{1,0:T(8,128)} %mul.230) | copy-start | bytes 451588
  641.0 9.2 %copy-start.7 = (bf16[480,768]{1,0:T(8,128)(2,1)S(1)}, bf16[480,768]{1,0:T(8,128)(2,1)}, u32[]{:S(2)}) copy-start(bf16[480,768]{1,0:T(8,128)(2,1)} %get-tuple-element.163.refs_1_) | copy-start | bytes 2211844
  643.7 6.6 copy-start.1
  643.7 6.6 copy-start.5
  643.7 6.6 copy-start.6
  650.2 6.7 copy-start
  650.3 6.7 copy-start.3
  650.3 7.9 %copy-start.4 = (f32[2,96,5376]{2,1,0:T(8,128)S(1)}, f32[2,96,5376]{2,1,0:T(8,128)}, u32[]{:S(2)}) copy-start(f32[2,96,5376]{2,1,0:T(8,128)} %param.38) | copy-start | bytes 12386308
Sparse Core Ops, SparseCore 0:
  75.3 42.7 all-gather.3
  119.7 66.0 all-gather.5
  187.5 23.7 all-gather.7
  295.3 41.1 reduce-scatter.5
  339.4 38.4 reduce-scatter.7
  380.6 43.2 reduce-scatter.9
  426.3 62.9 reduce-scatter.11
  491.7 67.4 reduce-scatter.13

commit v10 on v9

--- a/solution.py
+++ b/solution.py
@@ -799,13 +799,13 @@
     )
 
 
-REDUCE_SEMS = 48
+REDUCE_SEMS = 52
 
 
 class Reduce:
     def __init__(self, grad, out, scratch, sems):
         self.grad, self.out, self.sems = grad, out, sems
-        self.own, self.got_core, self.got_group, self.part, self.got_level = scratch
+        self.own, self.away, self.got_core, self.got_group, self.part, self.got_level = scratch
         self.rows, self.columns = out.shape
         self.chunk = 16
 
@@ -815,10 +815,16 @@
             self.grad.at[2 * level + core], self.own.at[level], self.sems.at[level]
         )
 
+    def load_away(self, level):
+        _, _, core = place()
+        return pltpu.make_async_copy(
+            self.grad.at[2 * level + 1 - core], self.away.at[level], self.sems.at[48 + level]
+        )
+
     def core_copy(self, target_level):
         group, level, core = place()
         return remote(
-            self.grad.at[2 * target_level + 1 - core],
+            self.away.at[target_level],
             self.got_core.at[target_level],
             self.sems.at[4 + target_level],
             self.sems.at[8 + target_level],
@@ -864,8 +870,12 @@
     def first(self):
         _, level, _ = place()
         for turn in (*TURNS, 0):
+            self.load_away(partner(level, turn)).start()
+        for turn in (*TURNS, 0):
+            self.load(partner(level, turn)).start()
+        for turn in (*TURNS, 0):
+            self.load_away(partner(level, turn)).wait()
             self.core_copy(partner(level, turn)).start()
-            self.load(partner(level, turn)).start()
 
     def second(self):
         _, level, _ = place()
@@ -950,7 +960,7 @@
                 self.share_copy(turn).wait_send()
 
 
-WHOLE_SEMS = 40
+WHOLE_SEMS = 44
 
 
 def add_rows(target, row, columns, source, count, wide):
@@ -972,7 +982,7 @@
 
     def __init__(self, grad, out, scratch, sems):
         self.grad, self.out, self.sems = grad, out, sems
-        self.own, self.got_core, self.got_x, self.got_y, self.got_last, self.part, self.got_level = scratch
+        self.own, self.away, self.got_core, self.got_x, self.got_y, self.got_last, self.part, self.got_level = scratch
         self.rows, self.columns = out.shape
         self.high, self.wide = self.rows // 2, self.columns // 2
 
@@ -988,10 +998,16 @@
             self.grad.at[2 * level + core], self.own.at[level], self.sems.at[level]
         )
 
+    def load_away(self, level):
+        _, _, core = place()
+        return pltpu.make_async_copy(
+            self.grad.at[2 * level + 1 - core], self.away.at[level], self.sems.at[40 + level]
+        )
+
     def core_copy(self, target_level):
         group, level, core = place()
         return remote(
-            self.grad.at[2 * target_level + 1 - core],
+            self.away.at[target_level],
             self.got_core.at[target_level],
             self.sems.at[4 + target_level],
             self.sems.at[8 + target_level],
@@ -1052,8 +1068,12 @@
     def first(self):
         _, level, _ = place()
         for turn in (*TURNS, 0):
+            self.load_away(partner(level, turn)).start()
+        for turn in (*TURNS, 0):
+            self.load(partner(level, turn)).start()
+        for turn in (*TURNS, 0):
+            self.load_away(partner(level, turn)).wait()
             self.core_copy(partner(level, turn)).start()
-            self.load(partner(level, turn)).start()
 
     def second(self):
         _, level, _ = place()
@@ -1280,7 +1300,7 @@
 def whole_scratch(grad):
     _, rows, columns = grad.shape
     high, wide = quarter_shape(rows, columns)
-    shapes = ((4, rows, columns), (4, rows, columns), (3, 4, high, wide), (4, high, wide))
+    shapes = (*[(4, rows, columns)] * 3, (3, 4, high, wide), (4, high, wide))
     return [pltpu.VMEM(shape, grad.dtype) for shape in (*shapes, (3, high, wide))]
 
 
@@ -1288,8 +1308,7 @@
     _, rows, columns = grad.shape
     high, wide = rows // 2, columns // 2
     shapes = (
-        (4, rows, columns),
-        (4, rows, columns),
+        *[(4, rows, columns)] * 3,
         (2, rows, wide),
         (2, high, columns),
         (4, high, wide),
@@ -1307,99 +1326,126 @@
 
 
 def reduce_kernel(*refs, whole, partly):
-    count = whole + partly
+    count = whole + 1 + partly
     grads, outs, refs = refs[:count], refs[count : 2 * count], refs[2 * count :]
-    sems, group_sems, refs = refs[0], refs[1], refs[2:]
+    sems, small_sems, group_sems, refs = refs[0], refs[1], refs[2], refs[3:]
     jobs = [
-        Whole(grads[i], outs[i], refs[7 * i : 7 * i + 7], sems.at[i]) for i in range(whole)
+        Whole(grads[i], outs[i], refs[8 * i : 8 * i + 8], sems.at[i]) for i in range(whole)
     ]
-    refs = refs[7 * whole :]
+    refs = refs[8 * whole :]
+    small = Reduce(grads[whole], outs[whole], refs[:6], small_sems)
+    refs = refs[6:]
     shares = [
-        GroupReduce(grads[whole + i], outs[whole + i], refs[2 * i : 2 * i + 2], group_sems.at[i])
+        GroupReduce(
+            grads[whole + 1 + i], outs[whole + 1 + i], refs[2 * i : 2 * i + 2], group_sems.at[i]
+        )
         for i in range(partly)
     ]
     greet()
-    run_stages([*jobs, *shares], STAGES[:1])
-    run_stages(shares, STAGES[1:2])
+    run_stages([*jobs, small, *shares], STAGES[:1])
+    run_stages([small, *shares], STAGES[1:2])
     run_stages(jobs, STAGES[1:3])
-    run_stages(shares, STAGES[3:4])
-    run_stages(jobs, STAGES[3:5])
-    run_stages([*shares, *jobs], STAGES[5:])
-
-
-def transfer_cost(size):
-    return pl.CostEstimate(flops=4000 * size, bytes_accessed=2 * size, transcendentals=0)
-
-
-def reduce_call(grads, shares, collective_id):
+    run_stages([small, *shares], STAGES[3:4])
+    run_stages(jobs, STAGES[3:4])
+    run_stages([small, *jobs], STAGES[4:5])
+    run_stages([*shares, small, *jobs], STAGES[5:])
+
+
+def transfer_outs(arrays):
+    return [jax.ShapeDtypeStruct(array.shape[-2:], array.dtype) for array in arrays]
+
+
+def reduce_call(grads, small, shares, collective_id):
     in_vmem = pl.BlockSpec(memory_space=pltpu.VMEM)
     whole, partly = len(grads), len(shares)
+    operands = [*grads, small, *shares]
     scratch = [
         pltpu.SemaphoreType.DMA((whole, WHOLE_SEMS)),
+        pltpu.SemaphoreType.DMA((REDUCE_SEMS,)),
         pltpu.SemaphoreType.DMA((partly, GROUP_SEMS)),
     ]
     for grad in grads:
         scratch.extend(stepped_scratch(grad))
+    scratch.extend(whole_scratch(small))
     for share in shares:
         scratch.extend(share_scratch(share))
-    out_shape = [jax.ShapeDtypeStruct(g.shape[1:], g.dtype) for g in grads]
-    out_shape += [jax.ShapeDtypeStruct(s.shape, s.dtype) for s in shares]
     return pl.pallas_call(
         functools.partial(reduce_kernel, whole=whole, partly=partly),
-        in_specs=[ANYWHERE] * (whole + partly),
-        out_specs=[in_vmem] * (whole + partly),
-        out_shape=out_shape,
+        in_specs=[ANYWHERE] * len(operands),
+        out_specs=[in_vmem] * len(operands),
+        out_shape=transfer_outs(operands),
         scratch_shapes=scratch,
         compiler_params=pltpu.CompilerParams(
             collective_id=collective_id, has_side_effects=True, vmem_limit_bytes=VMEM_LIMIT
         ),
         cost_estimate=NO_COST,
         name="reduce_gradients",
-    )(*grads, *shares)
-
-
-def finish_kernel(*refs, done, partly):
-    finished, refs = refs[:done], refs[done:]
-    shares, small, refs = refs[:partly], refs[partly], refs[partly + 1 :]
-    outs, small_out, full, refs = refs[:partly], refs[partly], refs[partly + 1], refs[partly + 2 :]
-    sems, group_sems, spread_sems, refs = refs[0], refs[1], refs[2], refs[3:]
-    job = Reduce(small, small_out, refs[:5], sems)
-    refs = refs[5:]
+    )(*operands)
+
+
+def totals(full, vector_rows, rest_size):
+    owners, rows, _ = full.shape
+    rest_rows = -(-rest_size // (owners * LANES))
+    row = lax.broadcasted_iota(jnp.int32, full.shape, 1)
+    spot = row - vector_rows + rest_rows * lax.broadcasted_iota(jnp.int32, full.shape, 0)
+    spot = spot * LANES + lax.broadcasted_iota(jnp.int32, full.shape, 2)
+    in_rest = (row >= vector_rows) & (row < vector_rows + rest_rows)
+
+    def summed(values):
+        return jnp.sum(jnp.sum(jnp.sum(values, 0), 0, keepdims=True), 1, keepdims=True)
+
+    tokens = summed(jnp.where(in_rest & (spot == rest_size - 1), full, 0.0))
+    loss = summed(jnp.where(in_rest & (spot == rest_size - 2), full, 0.0))
+    kept = (row < vector_rows) | (in_rest & (spot < rest_size - 2))
+    squares = jnp.where(kept, full * full, jnp.where(row == rows - 1, full, 0.0))
+    norm = jnp.sqrt(summed(squares)) / tokens
+    factor = jnp.minimum(1.0, CLIP_NORM / norm) / tokens
+    lane = lax.broadcasted_iota(jnp.int32, (1, LANES), 1)
+    return jnp.where(
+        lane == 0, factor, jnp.where(lane == 1, norm, jnp.where(lane == 2, loss, tokens))
+    )
+
+
+def finish_kernel(*refs, done, partly, vector_rows, rest_size):
+    finished, small, refs = refs[:done], refs[done], refs[done + 1 :]
+    shares, refs = refs[:partly], refs[partly:]
+    outs, full, numbers, refs = refs[:partly], refs[partly], refs[partly + 1], refs[partly + 2 :]
+    group_sems, spread_sems, refs = refs[0], refs[1], refs[2:]
     jobs = [
         GroupReduce(shares[i], outs[i], refs[2 * i : 2 * i + 2], group_sems.at[i])
         for i in range(partly)
     ]
     greet()
-    run_stages([job, *jobs], STAGES[:3])
+    run_stages(jobs, STAGES[:2])
     total = sum(squares_in(out) for out in finished)
-    run_stages([*jobs, job], STAGES[3:6])
+    run_stages(jobs, STAGES[3:6])
     total = total + sum(squares_in(out) for out in outs)
     _, level, core = place()
     mine = 2 * level + core
-    last = small_out.shape[0] - 1
-    full[mine] = small_out[...]
+    last = small.shape[0] - 1
+    full[mine] = small[...]
     full[mine, last : last + 1, :] = total
     Spread(full, spread_sems).run()
-    run_stages([job, *jobs], STAGES[6:])
-
-
-def finish_call(finished, shares, small, collective_id):
+    numbers[...] = totals(full[...], vector_rows, rest_size)
+    run_stages(jobs, STAGES[6:])
+
+
+def finish_call(finished, small, shares, vector_rows, rest_size, collective_id):
     done, partly = len(finished), len(shares)
     in_vmem = pl.BlockSpec(memory_space=pltpu.VMEM)
     scratch = [
-        pltpu.SemaphoreType.DMA((REDUCE_SEMS,)),
         pltpu.SemaphoreType.DMA((partly, GROUP_SEMS)),
         pltpu.SemaphoreType.DMA((14,)),
-        *whole_scratch(small),
     ]
     for share in shares:
         scratch.extend(share_scratch(share))
-    out_shape = [jax.ShapeDtypeStruct(s.shape, s.dtype) for s in shares]
-    out_shape.append(jax.ShapeDtypeStruct(small.shape[1:], small.dtype))
-    out_shape.append(jax.ShapeDtypeStruct(small.shape, small.dtype))
+    full = (lax.axis_size("fsdp"), *small.shape)
+    out_shape = [*transfer_outs(shares), jax.ShapeDtypeStruct(full, small.dtype), shape_of(1, LANES)]
     return pl.pallas_call(
-        functools.partial(finish_kernel, done=done, partly=partly),
-        in_specs=[in_vmem] * done + [ANYWHERE] * (partly + 1),
+        functools.partial(
+            finish_kernel, done=done, partly=partly, vector_rows=vector_rows, rest_size=rest_size
+        ),
+        in_specs=[in_vmem] * (done + 1) + [ANYWHERE] * partly,
         out_specs=[in_vmem] * len(out_shape),
         out_shape=out_shape,
         scratch_shapes=scratch,
@@ -1407,31 +1453,29 @@
             collective_id=collective_id, has_side_effects=True, vmem_limit_bytes=VMEM_LIMIT
         ),
         name="finish_gradients",
-    )(*finished, *shares, small)
+    )(*finished, small, *shares)
 
 
 def with_kernels():
     return lax.axis_size("dp") == 4 and lax.axis_size("fsdp") == 8
 
 
-def reduce_all(grads, shares, collective_id):
+def reduce_all(grads, small, shares, collective_id):
     if with_kernels():
-        return reduce_call(grads, shares, collective_id)
-    return [lax.psum(scatter(grad), "dp") for grad in grads] + sum_shares(shares)
-
-
-def sum_shares(shares):
-    return [lax.psum(share, "dp") for share in shares]
-
-
-def finish_all(finished, shares, small, collective_id):
+        return reduce_call(grads, small, shares, collective_id)
+    return [lax.psum(scatter(grad), "dp") for grad in (*grads, small)] + [
+        lax.psum(share, "dp") for share in shares
+    ]
+
+
+def finish_all(finished, small, shares, vector_rows, rest_size, collective_id):
     if with_kernels():
-        return finish_call(finished, shares, small, collective_id)
+        return finish_call(finished, small, shares, vector_rows, rest_size, collective_id)
     outs = [lax.psum(share, "dp") for share in shares]
-    own = lax.psum(scatter(small), "dp")
     total = sum(jnp.sum(jnp.square(out.astype(jnp.float32))) for out in (*finished, *outs))
     row = jnp.full((1, LANES), 1.0 / LANES, jnp.float32) * total
-    return [*outs, own, lax.all_gather(own.at[-1:].set(row), "fsdp", axis=0)]
+    full = lax.all_gather(small.at[-1:].set(row), "fsdp", axis=0)
+    return [*outs, full, totals(full, vector_rows, rest_size)]
 
 
 def scatter(grad):
@@ -1750,7 +1794,7 @@
     )
 
 
-def mlp_forward(stream, attended, up, proj_out, vector, rides, collective_id):
+def mlp_forward(stream, attended, up, proj_out, vector):
     rows = stream.shape[0]
     width = up.shape[1]
     weight_specs, weights = mlp_specs(up, proj_out)
@@ -1774,8 +1818,6 @@
         ],
         "mlp_forward",
         work(2 * rows * D * (D + 2 * width), rows * (16 * D + 4 * width) + 2 * D * (D + 2 * width)),
-        rides,
-        collective_id,
     )
 
 
@@ -1991,8 +2033,9 @@
     sizes = jnp.maximum(counts, 1.0)
     unit, inverse = normalized(stream_ref[...])
     final = unit * gain + shift
-    pooled = jnp.dot(member, final, precision=HIGHEST, preferred_element_type=jnp.float32)
-    pooled = (pooled / sizes).astype(LOW)
+    owner = jnp.broadcast_to(seg_col_ref[...], final.shape)
+    pooled = [jnp.sum(jnp.where(owner == k, final, 0.0), 0, keepdims=True) for k in range(IMGS)]
+    pooled = (jnp.concatenate(pooled, 0) / sizes).astype(LOW)
     class_at = lax.broadcasted_iota(jnp.int32, (IMGS, padded), 1)
     logits = mul(pooled, weight_ref[...]) + vector[:, 3 * D :]
     logits = jnp.where(class_at < classes, logits, MASKED)
@@ -2009,8 +2052,12 @@
         pooled, logits_grad, (((0,), (0,)), ((), ())), preferred_element_type=jnp.float32
     ).astype(LOW)
     pooled_grad = mul_nt(logits_grad, weight_ref[...]) / sizes
-    own = (seg_col_ref[...] == lax.broadcasted_iota(jnp.int32, (1, IMGS), 1)).astype(jnp.float32)
-    final_grad = jnp.dot(own, pooled_grad, precision=HIGHEST, preferred_element_type=jnp.float32)
+    own = (seg_col_ref[...] == lax.broadcasted_iota(jnp.int32, (1, IMGS), 1)).astype(LOW)
+    final_grad, left = 0.0, pooled_grad
+    for _ in range(3):
+        term = left.astype(LOW)
+        final_grad = final_grad + mul(own, term)
+        left = left - term.astype(jnp.float32)
     inner = final_grad * gain
     mean_inner = jnp.mean(inner, -1, keepdims=True)
     mean_cross = jnp.mean(inner * unit, -1, keepdims=True)
@@ -2099,12 +2146,14 @@
         vector = vectors[index]
         normed, qkv_rows = qkv_forward(stream, qkv_weight, vector)
         if index == 0:
-            attended, expo, inverse, up, output = attention_forward(qkv_rows, segment, rides[:2], 4)
+            attended, expo, inverse, up, output, output_ride = attention_forward(
+                qkv_rows, segment, rides, 4
+            )
         else:
             attended, expo, inverse, output = attention_forward(qkv_rows, segment, [output_ride], 5)
             up = up_one
-        residual, normed_second, active, slope, following, *fetched = mlp_forward(
-            stream, attended, up, output, vector, () if index else rides[2:], 7
+        residual, normed_second, active, slope, following = mlp_forward(
+            stream, attended, up, output, vector
         )
         saved_layers.append(
             (
@@ -2113,9 +2162,7 @@
                 (residual, normed_second, active, slope),
             )
         )
-        stream = following
-        if fetched:
-            qkv_weight, (output_ride,) = qkv_one, fetched
+        stream, qkv_weight = following, qkv_one
     stream_grad, head_grad, final_sums, head_bias_grad, numbers = head(
         stream, segment, labels, head_full, global_vector, head_weight.shape[1]
     )
@@ -2182,20 +2229,21 @@
     used = vector_rows + rest_rows
     block_rows = (used // 64 + 1) * 64
     small = jnp.pad(small.reshape(owners, used, LANES), ((0, 0), (0, block_rows - used), (0, 0)))
-    qkv_zero_sum, kernel_sum, *input_one_sums = reduce_all(
-        [by_owner(qkv_weight_grad), by_owner(kernel_grad)], late_parts, 2
-    )
-    output_zero_sum, small_share, small_full = finish_all(
+    qkv_zero_sum, kernel_sum, small_share, *input_one_sums = reduce_all(
+        [by_owner(qkv_weight_grad), by_owner(kernel_grad)], small, late_parts, 2
+    )
+    output_zero_sum, small_full, numbers = finish_all(
         [head_sum, output_one_sum, up_zero_sum, qkv_zero_sum, kernel_sum, *input_one_sums],
+        small_share,
         [last_part],
-        small,
+        vector_rows,
+        rest.shape[0],
         3,
     )
+    factor, grad_norm, loss_sum, token_total = (numbers[0, index] for index in range(4))
     rest_sum = small_full[:, vector_rows:used].reshape(-1)
     position_sum = rest_sum[: position_grad.size].reshape(position_grad.shape)
     global_sum = rest_sum[position_grad.size :][: global_vector.shape[0]]
-    loss_sum = rest_sum[rest.shape[0] - 2]
-    token_total = rest_sum[rest.shape[0] - 1]
     kernel_sum = kernel_sum.astype(jnp.float32)
     head_sum = head_sum[:, :CLS].astype(jnp.float32)
     input_sum = jnp.stack(
@@ -2205,16 +2253,6 @@
         jnp.float32
     )
     vector_sum = small_share[:vector_rows].reshape(-1)[:vector_size].reshape(layer_vector.shape)
-    grad_norm = (
-        jnp.sqrt(
-            jnp.sum(small_full[:, -1])
-            + jnp.sum(jnp.square(small_full[:, :vector_rows]))
-            + jnp.sum(position_sum * position_sum)
-            + jnp.sum(global_sum * global_sum)
-        )
-        / token_total
-    )
-    factor = jnp.minimum(1.0, CLIP_NORM / grad_norm) / token_total
     patch_next = adam_update(
         kernel_sum, patch_moment, patch_square, patch_kernel, factor, LEARN_RATE
     )

time: 680 us -> 659 us (0.969)
  Pallas kernels: 601 us -> 584 us
    pallas_call x19, Pallas kernels: 416 us -> 394 us  [block_call(): pl.pallas_call(kernel, grid=(grid,), in_specs=in_specs, out_specs=out_spe...]
    pallas_call x1, Pallas kernels: 74.1 us -> 83.2 us  [reduce_call(): pl.pallas_call(functools.partial(reduce_kernel, whole=whole, partly=partl...]
  transfers between devices with their start and end apart: 8 -> 8, of which waited for: 0 -> 0; matrix products, arithmetic and copies ran while one was open for 1% -> 2% of each run, Pallas kernels for 68% -> 68%
where the time goes in v10:
time: 659 us; the launch traced here: 652 us
  Pallas kernels  584 us (89%)
  other arithmetic  34.3 us (5%)
  local copies, waits for them, and re-layouts  15.2 us (2%)
  between operations  14.9 us (2%)
    pallas_call x19, Pallas kernels, block_call(): pl.pallas_call(kernel, grid=(grid,), in_specs=in_specs, out_specs=out_spe...  394 us
    pallas_call x1, Pallas kernels, reduce_call(): pl.pallas_call(functools.partial(reduce_kernel, whole=whole, partly=partl...  83.2 us
    pallas_call x1, Pallas kernels, begin(): pl.pallas_call(functools.partial(first_kernel, spots=spots), in_specs=[AN...  63 us
    pallas_call x1, Pallas kernels, finish_call(): pl.pallas_call(functools.partial(finish_kernel, done=done, partly=partly,...  32.9 us
    sub x7, other arithmetic, adam_update(): return (moment, square, weight - learn_rate * step_dir)  26.4 us
  transfers between devices with their start and end apart: 8, of which 0 were waited for; matrix products, arithmetic and copies ran while one was open for 2% of the time, Pallas kernels for 68%

profile of v10, /device:TPU:0, one launch (start us, length us, event | category | flops | bytes accessed | tf_op | source)
XLA Modules:
  0.0 651.7 jit_solution(6895593444072358008)
XLA Ops:
  7.2 0.7 convert_element_type.23
  8.0 0.2 dynamic_update_slice.3
  8.2 0.6 reshape.122.refs_1_
  8.8 1.3 broadcast_in_dim.22.refs_9_
  10.2 1.7 copy.50.refs_6_.refs_3_.seg_col_ref
  11.9 63.0 %begin.1 = (f32[1024,768]{1,0:T(8,128)}, f32[64,1024]{1,0:T(8,128)}, f32[1,9984]{1,0:T(1,128)}, f32[1,9984]{1,0:T(1,128)}, bf16[8,96,2304]{2,1,0:T(8,128)(2,1)},...) custom-call(f32[384,768]{1,0:T(8,128)} %refs_0_.1, ...), custom_call_target="tpu_custom_call" | custom-call | tf_op jit(solution)/shard_map/begin/pallas_call | solution.py:757
  74.9 0.7 all-gather.6.cloned.1.call-update
  75.7 0.7 all-gather.8.cloned.1.call-update
  76.4 0.3 reduce-scatter.6.cloned.1.call-start
  76.7 9.1 %qkv_forward.2 = (bf16[1024,768]{1,0:T(8,128)(2,1)}, bf16[1024,2304]{1,0:T(8,128)(2,1)}) custom-call(f32[1024,768]{1,0:T(8,128)} %get-tuple-element.108.stream_ref, bf16[768,2304]{1,0:T(8,128)(2,1)} %bitcast.57, f32[1,9984]{1,0:T(1,128)} %get-tuple-element.110.vector_ref), custom_call_target="tpu_custom_call" | custom-call | flops 3623878656 | bytes 14548992 | tf_op jit(solution)/shard_map/qkv_forward/pallas_call | solution.py:536
  85.8 52.4 %attention_forward.2 = (bf16[1024,768]{1,0:T(8,128)(2,1)}, bf16[12,1024,1024]{2,1,0:T(8,128)(2,1)}, f32[1024,768]{1,0:T(8,128)}, bf16[8,96,3072]{2,1,0:T(8,128)(...) custom-call(bf16[1024,2304]{1,0:T(8,128)(2,1)} %get-tuple-element.111.refs_0_.refs_1_.refs_2_, ...), custom_call_target="tpu_custom_call" | custom-call | flops 12884901888 | bytes 34603008 | tf_op jit(solution)/shard_map/attention_forward/pallas_call | solution.py:536
  138.3 21.3 %mlp_forward.2 = (f32[1024,768]{1,0:T(8,128)}, bf16[1024,768]{1,0:T(8,128)(2,1)}, bf16[1024,3072]{1,0:T(8,128)(2,1)}, bf16[1024,3072]{1,0:T(8,128)(2,1)}, f32[1024,768]{1,0:T(8,128)}) custom-call(f32[1024,768]{1,0:T(8,128)} %get-tuple-element.108.stream_ref, bf16[1024,768]{1,0:T(8,128)(2,1)} %get-tuple-element.117.attended_ref.refs_5_, ...), custom_call_target="tpu_custom_call" | custom-call | flops 10871635968 | bytes 35782656 | tf_op jit(solution)/shard_map/mlp_forward/pallas_call | solution.py:536
  159.6 0.7 copy.54.label_ref
  160.2 0.6 broadcast_in_dim.24.vector_ref
  160.9 9.7 %qkv_forward.3 = (bf16[1024,768]{1,0:T(8,128)(2,1)}, bf16[1024,2304]{1,0:T(8,128)(2,1)}) custom-call(f32[1024,768]{1,0:T(8,128)} %get-tuple-element.120.stream_ref, bf16[768,2304]{1,0:T(8,128)(2,1)} %all-gather.4.cloned.1.call-done.weight_ref, f32[1,9984]{1,0:T(1,128)} %get-tuple-element.122.vector_ref), custom_call_target="tpu_custom_call" | custom-call | flops 3623878656 | bytes 14548992 | tf_op jit(solution)/shard_map/qkv_forward/pallas_call | solution.py:536
  170.5 33.9 %attention_forward.3 = (bf16[1024,768]{1,0:T(8,128)(2,1)}, bf16[12,1024,1024]{2,1,0:T(8,128)(2,1)}, f32[1024,768]{1,0:T(8,128)}, bf16[8,480,768]{2,1,0:T(8,128)(2,1)}) custom-call(bf16[1024,2304]{1,0:T(8,128)(2,1)} %get-tuple-element.123.refs_0_.refs_1_.refs_2_, bf16[1024,2304]{1,0:T(8,128)(2,1)} %get-tuple-element.123.refs_0_.refs_1_.refs_2_, ...), custom_call_target="tpu_custom_call" | custom-call | flops 12884901888 | bytes 34603008 | tf_op jit(solution)/shard_map/attention_forward/pallas_call | solution.py:536
  204.4 21.3 %mlp_forward.3 = (f32[1024,768]{1,0:T(8,128)}, bf16[1024,768]{1,0:T(8,128)(2,1)}, bf16[1024,3072]{1,0:T(8,128)(2,1)}, bf16[1024,3072]{1,0:T(8,128)(2,1)}, f32[1024,768]{1,0:T(8,128)}) custom-call(f32[1024,768]{1,0:T(8,128)} %get-tuple-element.120.stream_ref, bf16[1024,768]{1,0:T(8,128)(2,1)} %get-tuple-element.127.attended_ref.refs_5_, ...), custom_call_target="tpu_custom_call" | custom-call | flops 10871635968 | bytes 35782656 | tf_op jit(solution)/shard_map/mlp_forward/pallas_call | solution.py:536
  225.7 10.7 %head.1 = (f32[1024,768]{1,0:T(8,128)}, bf16[768,1024]{1,0:T(8,128)(2,1)}, f32[1,1536]{1,0:T(1,128)}, f32[1,1024]{1,0:T(1,128)}, f32[1,2]{1,0:T(1,128)}) custom-call(f32[1024,768]{1,0:T(8,128)} %get-tuple-element.130.stream_ref, s32[1024,1]{1,0:T(8,128)} %copy.50.refs_6_.refs_3_.seg_col_ref, s32[1,1024]{1,0:T(1,128)} %bitcast.74, s32[8,1]{1,0:T(8,128)} %copy.54.label_ref, ...), custom_call_target="tpu_custom_call" | custom-call | tf_op jit(solution)/shard_map/head/pallas_call | solution.py:2072
  236.5 22.5 %mlp_backward.2 = (bf16[1024,768]{1,0:T(8,128)(2,1)}, bf16[1024,3072]{1,0:T(8,128)(2,1)}, f32[1024,768]{1,0:T(8,128)}, bf16[1024,768]{1,0:T(8,128)(2,1)}, bf16[1024,768]{1,0:T(8,128)(2,1)}, /*index=5*/f32[1,6144]{1,0:T(1,128)}) custom-call(f32[1024,768]{1,0:T(8,128)} %get-tuple-element.132.grad_ref, bf16[1024,3072]{1,0:T(8,128)(2,1)} %get-tuple-element.133.slope_ref, ...), custom_call_target="tpu_custom_call" | custom-call | tf_op jit(solution)/shard_map/mlp_backward/pallas_call | solution.py:536
  258.9 12.2 %output_weight_grad.2 = (bf16[3840,384]{1,0:T(8,128)(2,1)}, bf16[3840,384]{1,0:T(8,128)(2,1)}) custom-call(bf16[1024,768]{1,0:T(8,128)(2,1)} %get-tuple-element.127.attended_ref.refs_5_, bf16[1024,3072]{1,0:T(8,128)(2,1)} %get-tuple-element.136.active_ref, bf16[1024,768]{1,0:T(8,128)(2,1)} %get-tuple-element.137.residual_ref, ...), custom_call_target="tpu_custom_call" | custom-call | tf_op jit(solution)/shard_map/output_weight_grad/pallas_call | solution.py:536
  271.2 0.5 reduce-scatter.8.cloned.1.call-update
  271.8 35.7 %attention_backward.2 = (bf16[1024,2304]{1,0:T(8,128)(2,1)}, bf16[96,1024]{1,0:T(8,128)(2,1)}) custom-call(bf16[1024,2304]{1,0:T(8,128)(2,1)} %get-tuple-element.123.refs_0_.refs_1_.refs_2_, bf16[1024,2304]{1,0:T(8,128)(2,1)} %get-tuple-element.123.refs_0_.refs_1_.refs_2_, bf16[1024,2304]{1,0:T(8,128)(2,1)} %get-tuple-element.123.refs_0_.refs_1_.refs_2_, ...), custom_call_target="tpu_custom_call" | custom-call | tf_op jit(solution)/shard_map/attention_backward/pallas_call | solution.py:536
  307.5 8.0 %input_weight_grad.4 = bf16[768,2304]{1,0:T(8,128)(2,1)} custom-call(bf16[1024,768]{1,0:T(8,128)(2,1)} %get-tuple-element.149.left_ref, bf16[1024,2304]{1,0:T(8,128)(2,1)} %get-tuple-element.146.grad_ref.right_ref), custom_call_target="tpu_custom_call" | custom-call | tf_op jit(solution)/shard_map/input_weight_grad/pallas_call | solution.py:536
  315.5 9.6 %input_weight_grad.5 = bf16[768,3072]{1,0:T(8,128)(2,1)} custom-call(bf16[1024,768]{1,0:T(8,128)(2,1)} %get-tuple-element.150.left_ref, bf16[1024,3072]{1,0:T(8,128)(2,1)} %get-tuple-element.151.right_ref), custom_call_target="tpu_custom_call" | custom-call | tf_op jit(solution)/shard_map/input_weight_grad/pallas_call | solution.py:536
  325.1 10.4 %qkv_backward.2 = (f32[1024,768]{1,0:T(8,128)}, f32[1,3840]{1,0:T(1,128)}) custom-call(bf16[1024,2304]{1,0:T(8,128)(2,1)} %get-tuple-element.146.grad_ref.right_ref, f32[1024,768]{1,0:T(8,128)} %get-tuple-element.147.residual_ref, f32[1024,768]{1,0:T(8,128)} %get-tuple-element.120.stream_ref, bf16[768,2304]{1,0:T(8,128)(2,1)} %all-gather.4.cloned.1.call-done.weight_ref, ...), custom_call_target="tpu_custom_call" | custom-call | tf_op jit(solution)/shard_map/qkv_backward/pallas_call | solution.py:536
  335.6 0.7 reduce-scatter.12.cloned.1.call-update
  336.3 23.1 %mlp_backward.3 = (bf16[1024,768]{1,0:T(8,128)(2,1)}, bf16[1024,3072]{1,0:T(8,128)(2,1)}, f32[1024,768]{1,0:T(8,128)}, bf16[1024,768]{1,0:T(8,128)(2,1)}, bf16[1024,768]{1,0:T(8,128)(2,1)}, /*index=5*/f32[1,6144]{1,0:T(1,128)}) custom-call(f32[1024,768]{1,0:T(8,128)} %get-tuple-element.152.grad_ref, bf16[1024,3072]{1,0:T(8,128)(2,1)} %get-tuple-element.153.slope_ref, ...), custom_call_target="tpu_custom_call" | custom-call | tf_op jit(solution)/shard_map/mlp_backward/pallas_call | solution.py:536
  359.5 12.3 %output_weight_grad.3 = bf16[3840,768]{1,0:T(8,128)(2,1)} custom-call(bf16[1024,768]{1,0:T(8,128)(2,1)} %get-tuple-element.117.attended_ref.refs_5_, bf16[1024,3072]{1,0:T(8,128)(2,1)} %get-tuple-element.156.active_ref, bf16[1024,768]{1,0:T(8,128)(2,1)} %get-tuple-element.157.residual_ref, bf16[1024,768]{1,0:T(8,128)(2,1)} %get-tuple-element.158.grad_ref), custom_call_target="tpu_custom_call" | custom-call | tf_op jit(solution)/shard_map/output_weight_grad/pallas_call | solution.py:536
  371.8 0.7 copy-done.20
  372.7 0.1 stack.28
  372.8 9.7 %input_weight_grad.6 = bf16[768,3072]{1,0:T(8,128)(2,1)} custom-call(bf16[1024,768]{1,0:T(8,128)(2,1)} %get-tuple-element.162.left_ref, bf16[1024,3072]{1,0:T(8,128)(2,1)} %get-tuple-element.163.right_ref), custom_call_target="tpu_custom_call" | custom-call | tf_op jit(solution)/shard_map/input_weight_grad/pallas_call | solution.py:536
  382.7 2.0 pad_maximum_fusion.2.refs_7_
  384.7 72.5 %attention_backward.3 = (bf16[1024,2304]{1,0:T(8,128)(2,1)}, bf16[480,768]{1,0:T(8,128)(2,1)}, bf16[96,3072]{1,0:T(8,128)(2,1)}) custom-call(bf16[1024,2304]{1,0:T(8,128)(2,1)} %get-tuple-element.111.refs_0_.refs_1_.refs_2_, bf16[1024,2304]{1,0:T(8,128)(2,1)} %get-tuple-element.111.refs_0_.refs_1_.refs_2_, ...), custom_call_target="tpu_custom_call" | custom-call | tf_op jit(solution)/shard_map/attention_backward/pallas_call | solution.py:536
  457.2 10.4 %qkv_backward.3 = (f32[1024,768]{1,0:T(8,128)}, f32[1,3840]{1,0:T(1,128)}) custom-call(bf16[1024,2304]{1,0:T(8,128)(2,1)} %get-tuple-element.167.right_ref.grad_ref, f32[1024,768]{1,0:T(8,128)} %get-tuple-element.168.residual_ref, f32[1024,768]{1,0:T(8,128)} %get-tuple-element.108.stream_ref, bf16[768,2304]{1,0:T(8,128)(2,1)} %bitcast.58, ...), custom_call_target="tpu_custom_call" | custom-call | tf_op jit(solution)/shard_map/qkv_backward/pallas_call | solution.py:536
  467.6 0.7 slice_reduce_fusion.3
  468.4 0.7 slice_reduce_fusion.6
  469.1 0.1 stack.27
  469.2 0.1 maximum_bitcast_fusion.2
  469.3 0.1 reshape.134
  469.4 11.9 %embed_backward.1 = (bf16[3072,768]{1,0:T(8,128)(2,1)}, f32[64,768]{1,0:T(8,128)}, f32[1,768]{1,0:T(1,128)}) custom-call(bf16[1024,3072]{1,0:T(8,128)(2,1)} %pixel_ref.1, f32[1024,768]{1,0:T(8,128)} %get-tuple-element.169.grad_ref, f32[64,1024]{1,0:T(8,128)} %get-tuple-element.170.pos_ref), custom_call_target="tpu_custom_call" | custom-call | tf_op jit(solution)/shard_map/embed_backward/pallas_call | solution.py:536
  481.3 0.7 reduce.8
  482.0 0.9 slice.70
  483.0 0.1 concatenate.25
  483.2 0.7 pad.19.refs_2_
  483.9 8.1 %input_weight_grad.7 = bf16[768,2304]{1,0:T(8,128)(2,1)} custom-call(bf16[1024,768]{1,0:T(8,128)(2,1)} %get-tuple-element.166.left_ref, bf16[1024,2304]{1,0:T(8,128)(2,1)} %get-tuple-element.167.right_ref.grad_ref), custom_call_target="tpu_custom_call" | custom-call | tf_op jit(solution)/shard_map/input_weight_grad/pallas_call | solution.py:536
  492.1 83.2 %reduce_gradients.1 = (bf16[96,2304]{1,0:T(8,128)(2,1)}, bf16[384,768]{1,0:T(8,128)(2,1)}, f32[64,128]{1,0:T(8,128)}, bf16[96,2304]{1,0:T(8,128)(2,1)}, bf16[96,3072]{1,0:T(8,128)(2,1)}) custom-call(bf16[8,96,2304]{2,1,0:T(8,128)(2,1)} %bitcast.53, bf16[8,384,768]{2,1,0:T(8,128)(2,1)} %bitcast.54, f32[8,64,128]{2,1,0:T(8,128)} %pad.19.refs_2_, ...), custom_call_target="tpu_custom_call" | custom-call | tf_op jit(solution)/shard_map/reduce_gradients/pallas_call | solution.py:1372
  575.3 0.7 slice_bitcast_fusion
  576.0 1.3 maximum_bitcast_fusion.1
  577.3 1.1 maximum_bitcast_fusion
  578.5 32.9 %finish_gradients.1 = (bf16[480,768]{1,0:T(8,128)(2,1)}, f32[8,64,128]{2,1,0:T(8,128)}, f32[1,128]{1,0:T(1,128)}) custom-call(bf16[96,1024]{1,0:T(8,128)(2,1)} %get-tuple-element.143.refs_0_, bf16[480,768]{1,0:T(8,128)(2,1)} %get-tuple-element.164.refs_1_, bf16[96,3072]{1,0:T(8,128)(2,1)} %get-tuple-element.165.refs_2_, ...), custom_call_target="tpu_custom_call" | custom-call | tf_op jit(solution)/shard_map/finish_gradients/pallas_call | solution.py:1444
  611.4 1.4 fusion.15
  612.8 0.6 slice_multiply_fusion.2
  613.5 0.1 mul.216
  613.5 0.9 slice.79
  614.5 0.7 copy-done.13
  615.1 1.3 slice_multiply_fusion
  616.4 1.6 mul.221
  618.1 2.1 multiply_subtract_fusion.5
  620.2 3.2 multiply_subtract_fusion.3
  623.4 4.9 multiply_subtract_fusion.2
  628.3 0.6 multiply_subtract_fusion.6
  629.0 1.9 multiply_subtract_fusion.4
  631.0 6.8 %multiply_subtract_fusion.1 = (f32[2,480,768]{2,1,0:T(8,128)}, f32[2,480,768]{2,1,0:T(8,128)}, f32[2,480,768]{2,1,0:T(8,128)}) fusion(f32[2,480,768]{2,1,0:T(8,128)S(1)} %copy-done.1, f32[]{:T(128)} %bitcast.28, bf16[1,480,768]{2,1,0:T(8,128)(2,1)S(1)} %bitcast.61, bf16[1,480,768]{2,1,0:T(8,128)(2,1)} %bitcast.64, f32[2,480,768]{2,1,0:T(8,128)S(1)} %copy-done.5, ...), kind=kLoop, calls=%fused_computation.8 | loop fusion | flops 12533760 | bytes 19169284 | tf_op jit(solution)/shard_map/sub | solution.py:2096
  637.8 6.9 %multiply_subtract_fusion = (f32[2,96,5376]{2,1,0:T(8,128)}, f32[2,96,5376]{2,1,0:T(8,128)}, f32[2,96,5376]{2,1,0:T(8,128)}) fusion(f32[2,96,5376]{2,1,0:T(8,128)S(1)} %copy-done, f32[]{:T(128)} %bitcast.28, bf16[1,96,5376]{2,1,0:T(8,128)(2,1)S(1)} %maximum_bitcast_fusion.1, bf16[1,96,5376]{2,1,0:T(8,128)(2,1)S(1)} %maximum_bitcast_fusion, ...), kind=kLoop, calls=%fused_computation.5 | loop fusion | flops 17547264 | bytes 26836996 | tf_op jit(solution)/shard_map/sub | solution.py:2096
  (85 shorter events, 0.9 us)
Async XLA Ops:
  7.2 153.7 %all-gather.4.cloned.1.call-start = ((), (), s32[]{:S(2)}) async-start(), calls=%async_computation.5 | async-start | bytes 3981312 | tf_op jit(solution)/shard_map/all_gather | solution.py:2142
  74.9 129.5 %all-gather.6.cloned.1.call-start = ((), (), s32[]{:S(2)}) async-start(), calls=%async_computation.6 | async-start | bytes 5308416 | tf_op jit(solution)/shard_map/all_gather | solution.py:2142
  75.6 150.1 %all-gather.8.cloned.1.call-start = ((), (), s32[]{:S(2)}) async-start(), calls=%async_computation.7 | async-start | bytes 1769472 | tf_op jit(solution)/shard_map/all_gather | solution.py:2142
  76.4 306.3 %reduce-scatter.6.cloned.1.call-start = ((), (), s32[]{:S(2)}) async-start(), calls=%async_computation.8 | async-start | bytes 3317760 | tf_op jit(solution)/shard_map/reduce_scatter | solution.py:1482
  138.2 21.3 %copy-start.26 = (s32[1,8]{1,0:T(1,128)S(1)}, s32[1,8]{1,0:T(1,128)}, u32[]{:S(2)}) copy-start(s32[1,8]{1,0:T(1,128)} %param.28) | copy-start | bytes 100
  138.3 22.0 %copy-start.14 = (f32[3304]{0:T(1024)S(1)}, f32[3304]{0:T(1024)}, u32[]{:S(2)}) copy-start(f32[3304]{0:T(1024)} %param.35) | copy-start | bytes 39652
  271.1 111.5 %reduce-scatter.8.cloned.1.call-start = ((), (), s32[]{:S(2)}) async-start(), calls=%async_computation.9 | async-start | bytes 3317760 | tf_op jit(solution)/shard_map/reduce_scatter | solution.py:1482
  271.7 220.3 %reduce-scatter.10.cloned.1.call-start = ((), (), s32[]{:S(2)}) async-start(), calls=%async_computation.10 | async-start | bytes 3981312 | tf_op jit(solution)/shard_map/reduce_scatter | solution.py:1482
  335.5 156.5 %reduce-scatter.12.cloned.1.call-start = ((), (), s32[]{:S(2)}) async-start(), calls=%async_computation.11 | async-start | bytes 5308416 | tf_op jit(solution)/shard_map/reduce_scatter | solution.py:1482
  336.3 242.1 %reduce-scatter.14.cloned.1.call-start = ((), (), s32[]{:S(2)}) async-start(), calls=%async_computation.12 | async-start | bytes 6635520 | tf_op jit(solution)/shard_map/reduce_scatter | solution.py:1482
  371.8 0.7 copy-start.20
  371.8 0.8 copy-start.16
  371.8 1.0 copy-start.23
  372.8 9.8 %copy-start.17 = (f32[1,6144]{1,0:T(1,128)S(1)}, f32[1,6144]{1,0:T(1,128)}, u32[]{:S(2)}) copy-start(f32[1,6144]{1,0:T(1,128)} %get-tuple-element.173) | copy-start | bytes 73732
  469.4 13.5 %copy-start.24 = (f32[1,1024]{1,0:T(1,128)S(1)}, f32[1,1024]{1,0:T(1,128)}, u32[]{:S(2)}) copy-start(f32[1,1024]{1,0:T(1,128)} %get-tuple-element.179) | copy-start | bytes 12292
  469.4 13.5 %copy-start.25 = (f32[1,2]{1,0:T(1,128)S(1)}, f32[1,2]{1,0:T(1,128)}, u32[]{:S(2)}) copy-start(f32[1,2]{1,0:T(1,128)} %get-tuple-element.180) | copy-start | bytes 28
  492.1 85.2 %copy-start.8 = (bf16[96,3072]{1,0:T(8,128)(2,1)S(1)}, bf16[96,3072]{1,0:T(8,128)(2,1)}, u32[]{:S(2)}) copy-start(bf16[96,3072]{1,0:T(8,128)(2,1)} %get-tuple-element.165.refs_2_) | copy-start | bytes 1769476
  578.4 39.7 %copy-start.18 = (f32[3304]{0:T(1024)S(1)}, f32[3304]{0:T(1024)}, u32[]{:S(2)}) copy-start(f32[3304]{0:T(1024)} %param.49) | copy-start | bytes 39652
  578.4 39.7 %copy-start.19 = (f32[3304]{0:T(1024)S(1)}, f32[3304]{0:T(1024)}, u32[]{:S(2)}) copy-start(f32[3304]{0:T(1024)} %param.42) | copy-start | bytes 39652
  578.4 41.8 %copy-start.11 = (bf16[96,1024]{1,0:T(8,128)(2,1)S(1)}, bf16[96,1024]{1,0:T(8,128)(2,1)}, u32[]{:S(2)}) copy-start(bf16[96,1024]{1,0:T(8,128)(2,1)} %get-tuple-element.143.refs_0_) | copy-start | bytes 589828
  578.4 44.9 %copy-start.2 = (f32[384,768]{1,0:T(8,128)S(1)}, f32[384,768]{1,0:T(8,128)}, u32[]{:S(2)}) copy-start(f32[384,768]{1,0:T(8,128)} %refs_0_.1) | copy-start | bytes 3538948
  578.4 49.9 %copy-start.15 = (f32[2,1248]{1,0:T(2,128)S(1)}, f32[2,1248]{1,0:T(2,128)}, u32[]{:S(2)}) copy-start(f32[2,1248]{1,0:T(2,128)} %param.33) | copy-start | bytes 29956
  578.5 49.9 %copy-start.21 = (f32[2,1248]{1,0:T(2,128)S(1)}, f32[2,1248]{1,0:T(2,128)}, u32[]{:S(2)}) copy-start(f32[2,1248]{1,0:T(2,128)} %param.47) | copy-start | bytes 29956
  578.5 49.9 %copy-start.22 = (f32[2,1248]{1,0:T(2,128)S(1)}, f32[2,1248]{1,0:T(2,128)}, u32[]{:S(2)}) copy-start(f32[2,1248]{1,0:T(2,128)} %param.40) | copy-start | bytes 29956
  614.5 0.7 copy-start.13
  618.1 5.3 copy-start.9
  618.1 5.3 copy-start.10
  620.2 8.8 %copy-start.12 = (f32[49,768]{1,0:T(8,128)S(1)}, f32[49,768]{1,0:T(8,128)}, u32[]{:S(2)}) copy-start(f32[49,768]{1,0:T(8,128)} %mul.221) | copy-start | bytes 451588
  620.2 10.8 %copy-start.7 = (bf16[480,768]{1,0:T(8,128)(2,1)S(1)}, bf16[480,768]{1,0:T(8,128)(2,1)}, u32[]{:S(2)}) copy-start(bf16[480,768]{1,0:T(8,128)(2,1)} %get-tuple-element.164.refs_1_) | copy-start | bytes 2211844
  623.4 7.6 %copy-start.1 = (f32[2,480,768]{2,1,0:T(8,128)S(1)}, f32[2,480,768]{2,1,0:T(8,128)}, u32[]{:S(2)}) copy-start(f32[2,480,768]{2,1,0:T(8,128)} %refs_3_.1) | copy-start | bytes 8847364
  623.4 7.6 %copy-start.5 = (f32[2,480,768]{2,1,0:T(8,128)S(1)}, f32[2,480,768]{2,1,0:T(8,128)}, u32[]{:S(2)}) copy-start(f32[2,480,768]{2,1,0:T(8,128)} %param.46) | copy-start | bytes 8847364
  623.4 7.6 %copy-start.6 = (f32[2,480,768]{2,1,0:T(8,128)S(1)}, f32[2,480,768]{2,1,0:T(8,128)}, u32[]{:S(2)}) copy-start(f32[2,480,768]{2,1,0:T(8,128)} %param.39) | copy-start | bytes 8847364
  631.0 6.8 %copy-start = (f32[2,96,5376]{2,1,0:T(8,128)S(1)}, f32[2,96,5376]{2,1,0:T(8,128)}, u32[]{:S(2)}) copy-start(f32[2,96,5376]{2,1,0:T(8,128)} %refs_2_.1) | copy-start | bytes 12386308
  631.0 6.8 %copy-start.3 = (f32[2,96,5376]{2,1,0:T(8,128)S(1)}, f32[2,96,5376]{2,1,0:T(8,128)}, u32[]{:S(2)}) copy-start(f32[2,96,5376]{2,1,0:T(8,128)} %param.45) | copy-start | bytes 12386308
  631.0 6.8 %copy-start.4 = (f32[2,96,5376]{2,1,0:T(8,128)S(1)}, f32[2,96,5376]{2,1,0:T(8,128)}, u32[]{:S(2)}) copy-start(f32[2,96,5376]{2,1,0:T(8,128)} %param.38) | copy-start | bytes 12386308
Sparse Core Ops, SparseCore 0:
  75.0 58.5 all-gather.3
  135.2 50.4 all-gather.5
  187.4 23.8 all-gather.7
  271.3 40.4 reduce-scatter.5
  314.6 38.5 reduce-scatter.7
  356.0 43.2 reduce-scatter.9
  401.7 62.9 reduce-scatter.11
  467.1 66.9 reduce-scatter.13

commit v11 on v10

--- a/solution.py
+++ b/solution.py
@@ -583,11 +583,11 @@
 def first_kernel(*refs, spots):
     kernel, vectors, inputs, outputs, head, pixels, seg_col, patch_row, table, biases = refs[:10]
     stream, pos_t, vector_zero, vector_one = refs[10:14]
-    qkv_full, up_level, output_level = refs[14:17]
-    up_zero, output_zero, qkv_one, up_one, output_one, head_low = refs[17:23]
-    wide_kernel, wide_inputs, wide_outputs, wide_head, pixel_rows, table_low = refs[23:29]
-    kernel_full, qkv_zero, vectors_full, qkv_landing, up_landing, output_landing = refs[29:35]
-    load_sems, sems = refs[35:]
+    qkv_full, up_full, output_level = refs[14:17]
+    output_zero, qkv_one, up_one, output_one, head_low = refs[17:22]
+    wide_kernel, wide_inputs, wide_outputs, wide_head, pixel_rows, table_low = refs[22:28]
+    kernel_full, qkv_zero, vectors_full, qkv_landing, up_landing, output_landing = refs[28:34]
+    up_zero, load_sems, sems = refs[34:]
     _, level, core = place()
     mine = 2 * level + core
     pairs = [
@@ -608,8 +608,7 @@
     patch_job = Gather(kernel_full.at[mine], kernel_full, sems.at[0], True, in_place=True)
     vector_job = Gather(vectors, vectors_full, sems.at[1], False)
     qkv_job = Gather(qkv_zero, qkv_landing, sems.at[2], True)
-    up_job = LevelGather(up_zero, up_landing, sems.at[3])
-    up_job.target = up_level
+    up_job = Gather(up_zero, up_landing, sems.at[3], True)
     output_job = LevelGather(output_zero, output_landing, sems.at[4])
     output_job.target = output_level
     copies[0].wait()
@@ -654,6 +653,7 @@
     patch_job.second()
     vector_job.second()
     qkv_job.second()
+    up_job.second()
     patch_job.core_copy(0).wait_recv()
     use(0, False)
     copies[3].wait()
@@ -667,6 +667,7 @@
     patch_job.relay()
     qkv_job.relay()
     patch_job.third(use)
+    up_job.relay()
     qkv_job.third()
     patch_job.fourth(use)
     vector_job.third()
@@ -681,11 +682,16 @@
                 if 0 <= row - spot < span
             ]
             out[:, row * LANES : (row + 1) * LANES] = sum(parts)
+    up_job.third()
     qkv_job.fourth()
     copy = pltpu.make_async_copy(qkv_landing, qkv_full, load_sems.at[0])
     copy.start()
-    run_stages([up_job, output_job], ("fourth", "store"))
+    up_job.fourth()
+    up_copy = pltpu.make_async_copy(up_landing, up_full, load_sems.at[1])
+    up_copy.start()
+    run_stages([output_job], ("fourth", "store"))
     copy.wait()
+    up_copy.wait()
 
 
 def padded_vectors(shard):
@@ -725,7 +731,8 @@
             weights.T,
             [vectors[index : index + 1] for index in range(LAYERS)],
             gather(inputs[0][0], 0),
-            [*[GatherRide(shard, shard) for shard in (inputs[0][1], outputs[0])], LevelRide(outputs[1])],
+            gather(inputs[0][1], 0),
+            [GatherRide(outputs[0], outputs[0]), LevelRide(outputs[1])],
             [*inputs[1], head],
         )
     rows = pixels.shape[0]
@@ -743,9 +750,8 @@
         shape_of(1, width),
         shape_of(1, width),
         low(owners, *qkv_shape),
-        levels(up_shape),
+        low(owners, *up_shape),
         levels(out_shape),
-        low(*up_shape),
         low(*out_shape),
         low(*qkv_shape),
         low(*up_shape),
@@ -757,7 +763,7 @@
     results = pl.pallas_call(
         functools.partial(first_kernel, spots=spots),
         in_specs=[ANYWHERE] * 6 + [in_vmem] * 4,
-        out_specs=[in_vmem] * 4 + [ANYWHERE] + [in_vmem] * 8,
+        out_specs=[in_vmem] * 4 + [ANYWHERE] * 2 + [in_vmem] * 6,
         out_shape=shapes,
         scratch_shapes=[
             *[pltpu.VMEM(array.shape, array.dtype) for array in wide],
@@ -766,8 +772,9 @@
             pltpu.VMEM(qkv_shape, LOW),
             pltpu.VMEM((owners, *vectors.shape), LOW),
             pltpu.VMEM((owners, *qkv_shape), LOW),
-            pltpu.VMEM((4, *quarter_shape(*up_shape)), LOW),
+            pltpu.VMEM((owners, *up_shape), LOW),
             pltpu.VMEM((4, *quarter_shape(*out_shape)), LOW),
+            pltpu.VMEM(up_shape, LOW),
             pltpu.SemaphoreType.DMA((7,)),
             pltpu.SemaphoreType.DMA((5, GATHER_SEMS)),
         ],
@@ -788,13 +795,14 @@
         position_table,
         global_vector[None, :],
     )
-    up_zero, output_zero, qkv_one, up_one, output_one, head_low = results[7:]
+    output_zero, qkv_one, up_one, output_one, head_low = results[7:]
     return (
         results[0],
         results[1],
         results[2:4],
         results[4].reshape(owners * depth, 3 * D),
-        [GatherRide(up_zero, results[5]), GatherRide(output_zero, results[6]), LevelRide(output_one)],
+        results[5].reshape(owners * depth, up_shape[1]),
+        [GatherRide(output_zero, results[6]), LevelRide(output_one)],
         [qkv_one, up_one, head_low],
     )
 
@@ -1822,17 +1830,35 @@
 
 
 def mlp_back_kernel(
-    grad_ref, slope_ref, residual_ref, mix_ref, up_ref, down_ref, vector_ref,
-    low_out, hidden_ref, out_ref, out_low_ref, attended_ref, sums_ref,
-    low_ref, second_ref, sem,
+    grad_ref, slope_ref, residual_in, normed_ref, active_ref, attended_ref, mix_ref, up_ref, down_ref, vector_ref,
+    out_ref, attended_grad_ref, sums_ref, up_grad_ref, *refs,
 ):
+    outs, scratch = refs[:-7], refs[-7:]
+    residual_ref, low_ref, second_ref, turned_ref, hidden_ref, product_ref, sems = scratch
     rows = grad_ref.shape[0]
-    copy = pltpu.make_async_copy(low_ref, low_out, sem)
+    step = pl.program_id(0)
+    load = pltpu.make_async_copy(residual_in, residual_ref, sems.at[0, 0])
+
+    def stores(slot):
+        copies, base = [], 0
+        for index, out in enumerate(outs):
+            width = out.shape[1]
+            source = product_ref.at[slot, :, pl.ds(base, width)]
+            target = out.at[pl.ds(pl.multiple_of(slot * D, D), D)]
+            copies.append(pltpu.make_async_copy(source, target, sems.at[1 + index, slot]))
+            base += width
+        return copies
+
+    def store(slot, product):
+        product_ref[slot] = product.astype(LOW)
+        for copy in stores(slot):
+            copy.start()
 
     @at_first
     def _():
+        load.start()
         low_ref[...] = grad_ref[...].astype(LOW)
-        copy.start()
+        turned_ref[...] = normed_ref[...].T
         second_ref[...] = jnp.zeros_like(second_ref)
 
     parts = halves_of(rows)
@@ -1848,9 +1874,12 @@
         second_ref[half, :] += mul_nt(hidden_grad, up_ref[...])
         active_grad = following
     sums_ref[:, chunk_at(4 * D)] = hidden_sum
+    store(step + 1, mul(active_ref[...].T, low_ref[...]))
+    up_grad_ref[...] = mul(turned_ref[...], hidden_ref[...]).astype(LOW)
 
     @at_last
     def _():
+        load.wait()
         gain = vector_ref[:, 2 * D : 3 * D]
         totals = [0.0] * 4
         for half in halves_of(rows):
@@ -1861,131 +1890,113 @@
             total = value_grad + grad
             out_ref[half, :] = total
             total_low = total.astype(LOW)
-            out_low_ref[half, :] = total_low
-            attended_ref[half, :] = mul_nt(total_low, mix_ref[...]).astype(LOW)
+            hidden_ref[half, :] = total_low
+            attended_grad_ref[half, :] = mul_nt(total_low, mix_ref[...]).astype(LOW)
             new = (gain_grad, shift_grad, column_sum(total_low), column_sum(low_ref[half, :]))
             totals = [old + part for old, part in zip(totals, new)]
         sums_ref[:, : 4 * D] = jnp.concatenate(totals, 1)
-        copy.wait()
-
-
-def mlp_backward(grad, slope, residual, up, proj_out, vector):
+        store(0, mul(attended_ref[...].T, hidden_ref[...]))
+        for slot in range(product_ref.shape[0]):
+            for copy in stores(slot):
+                copy.wait()
+
+
+def mlp_backward(grad, slope, residual, normed, active, attended, up, proj_out, vector, parts):
     rows = grad.shape[0]
     width = up.shape[1]
+    steps = width // D
     whole = fixed(rows, D)
     weight_specs, weights = mlp_specs(up, proj_out)
     return block_call(
         mlp_back_kernel,
-        width // D,
-        [whole, columns_of(rows), whole, *weight_specs, fixed(1, vector.shape[1])],
-        [grad, slope, residual, *weights, vector],
-        [ANYWHERE, columns_of(rows), whole, whole, whole, fixed(1, 4 * D + width)],
+        steps,
         [
-            shape_of(rows, D, dtype=LOW),
-            shape_of(rows, width, dtype=LOW),
+            whole,
+            columns_of(rows),
+            ANYWHERE,
+            whole,
+            columns_of(rows),
+            whole,
+            *weight_specs,
+            fixed(1, vector.shape[1]),
+        ],
+        [grad, slope, residual, normed, active, attended, *weights, vector],
+        [whole, whole, fixed(1, 4 * D + width), columns_of(D), *[ANYWHERE] * len(parts)],
+        [
             shape_of(rows, D),
             shape_of(rows, D, dtype=LOW),
-            shape_of(rows, D, dtype=LOW),
             shape_of(1, 4 * D + width),
+            shape_of(D, width, dtype=LOW),
+            *[shape_of(D + width, part, dtype=LOW) for part in parts],
         ],
         [
+            pltpu.VMEM((rows, D), jnp.float32),
             pltpu.VMEM((rows, D), LOW),
             pltpu.VMEM((rows, D), jnp.float32),
-            pltpu.SemaphoreType.DMA,
+            pltpu.VMEM((D, rows), LOW),
+            pltpu.VMEM((rows, D), LOW),
+            pltpu.VMEM((steps + 1, D, D), LOW),
+            pltpu.SemaphoreType.DMA((1 + len(parts), steps + 1)),
         ],
         "mlp_backward",
     )
 
 
-def qkv_back_kernel(grad_ref, residual_ref, stream_ref, weight_ref, vector_ref, out_ref, sums_ref):
-    grad = grad_ref[...]
-    normed_grad = mul_nt(grad, weight_ref[...])
-    value_grad, gain_grad, shift_grad = norm_backward(normed_grad, stream_ref[...], vector_ref[:, :D])
-    out_ref[...] = residual_ref[...] + value_grad
-    sums = jnp.concatenate([gain_grad, shift_grad, column_sum(grad)], 1)
+def qkv_back_kernel(
+    grad_ref, residual_in, stream_in, normed_ref, weight_ref, vector_ref,
+    out_ref, sums_ref, weight_grad_ref,
+    residual_ref, stream_ref, sum_ref, turned_ref, sems,
+):
+    rows = out_ref.shape[0]
+    copies = loads((residual_in, stream_in), (residual_ref, stream_ref), sems)
 
     @at_first
     def _():
-        sums_ref[...] = jnp.zeros_like(sums_ref)
-
-    sums_ref[...] += sums
-
-
-def qkv_backward(grad, residual_grad, stream, weight, vector):
+        for copy in copies:
+            copy.start()
+        turned_ref[...] = normed_ref[...].T
+        sum_ref[...] = jnp.zeros_like(sum_ref)
+
+    for half in halves_of(rows):
+        sum_ref[half, :] += mul_nt(grad_ref[half, :], weight_ref[...])
+    sums_ref[:, chunk_at(2 * D)] = column_sum(grad_ref[...])
+    weight_grad_ref[...] = mul(turned_ref[...], grad_ref[...]).astype(LOW)
+
+    @at_last
+    def _():
+        for copy in copies:
+            copy.wait()
+        totals = [0.0] * 2
+        for half in halves_of(rows):
+            value_grad, gain_grad, shift_grad = norm_backward(
+                sum_ref[half, :], stream_ref[half, :], vector_ref[:, :D]
+            )
+            out_ref[half, :] = residual_ref[half, :] + value_grad
+            totals = [totals[0] + gain_grad, totals[1] + shift_grad]
+        sums_ref[:, : 2 * D] = jnp.concatenate(totals, 1)
+
+
+def qkv_backward(grad, residual_grad, stream, normed, weight, vector, rides, collective_id):
     rows = stream.shape[0]
-    block = 256
-    narrow = rows_of(block, D)
+    whole = fixed(rows, D)
     return block_call(
         qkv_back_kernel,
-        rows // block,
-        [rows_of(block, 3 * D), narrow, narrow, fixed(D, 3 * D), fixed(1, vector.shape[1])],
-        [grad, residual_grad, stream, weight, vector],
-        [narrow, fixed(1, 5 * D)],
-        [shape_of(rows, D), shape_of(1, 5 * D)],
-        [],
+        3,
+        [columns_of(rows), ANYWHERE, ANYWHERE, whole, columns_of(D), fixed(1, vector.shape[1])],
+        [grad, residual_grad, stream, normed, weight, vector],
+        [whole, fixed(1, 5 * D), columns_of(D)],
+        [shape_of(rows, D), shape_of(1, 5 * D), shape_of(D, 3 * D, dtype=LOW)],
+        [
+            pltpu.VMEM((rows, D), jnp.float32),
+            pltpu.VMEM((rows, D), jnp.float32),
+            pltpu.VMEM((rows, D), jnp.float32),
+            pltpu.VMEM((D, rows), LOW),
+            pltpu.SemaphoreType.DMA((2,)),
+        ],
         "qkv_backward",
-    )
-
-
-def input_grad_kernel(left_ref, right_ref, out_ref, turned_ref):
-    @at_first
-    def _():
-        turned_ref[...] = left_ref[...].T
-
-    out_ref[...] = mul(turned_ref[...], right_ref[...]).astype(LOW)
-
-
-def input_weight_grad(left, right):
-    rows, width = right.shape
-    return block_call(
-        input_grad_kernel,
-        width // D,
-        [fixed(rows, D), columns_of(rows)],
-        [left, right],
-        [columns_of(D)],
-        [shape_of(D, width, dtype=LOW)],
-        [pltpu.VMEM((D, rows), LOW)],
-        "input_weight_grad",
-    )[0]
-
-
-def output_grad_kernel(attended_ref, active_ref, residual_ref, grad_ref, *outs, cut):
-    step = pl.program_id(0)
-
-    def store(product):
-        base = 0
-        for out in outs:
-            out[...] = product[:, base : base + out.shape[1]].astype(jnp.bfloat16)
-            base += out.shape[1]
-
-    @pl.when(step < cut)
-    def _():
-        store(mul(attended_ref[...].T, residual_ref[...]))
-
-    @pl.when(step >= cut)
-    def _():
-        store(mul(active_ref[...].T, grad_ref[...]))
-
-
-def output_weight_grad(attended, active, residual_low, grad_low, parts):
-    rows = attended.shape[0]
-    block = 768
-    cut = attended.shape[1] // block
-    steps = cut + active.shape[1] // block
-    return block_call(
-        functools.partial(output_grad_kernel, cut=cut),
-        steps,
-        [
-            pl.BlockSpec((rows, block), lambda i: (0, jnp.minimum(i, cut - 1))),
-            pl.BlockSpec((rows, block), lambda i: (0, jnp.maximum(i - cut, 0))),
-            fixed(rows, D),
-            fixed(rows, D),
-        ],
-        [attended, active, residual_low, grad_low],
-        [rows_of(block, part) for part in parts],
-        [shape_of(steps * block, part, dtype=LOW) for part in parts],
-        [],
-        "output_weight_grad",
+        None,
+        rides,
+        collective_id,
     )
 
 
@@ -2126,7 +2137,7 @@
     owners = lax.axis_size("fsdp")
     nodes = position_table.shape[0]
     vector_size = layer_vector.size
-    stream, pos_weights_t, vectors, qkv_weight, rides, rest_shards = begin(
+    stream, pos_weights_t, vectors, qkv_weight, up_zero, rides, rest_shards = begin(
         pixels,
         segment,
         patch_size,
@@ -2146,9 +2157,10 @@
         vector = vectors[index]
         normed, qkv_rows = qkv_forward(stream, qkv_weight, vector)
         if index == 0:
-            attended, expo, inverse, up, output, output_ride = attention_forward(
+            attended, expo, inverse, output, output_ride = attention_forward(
                 qkv_rows, segment, rides, 4
             )
+            up = up_zero
         else:
             attended, expo, inverse, output = attention_forward(qkv_rows, segment, [output_ride], 5)
             up = up_one
@@ -2167,39 +2179,52 @@
         stream, segment, labels, head_full, global_vector, head_weight.shape[1]
     )
     vector_grads = [None] * LAYERS
-    early_parts, late_parts = [], []
     for index in reversed(range(LAYERS)):
         (qkv_weight, up, output, vector), first, second = saved_layers[index]
         entering, normed, qkv_rows, attended, expo, inverse = first
         residual, normed_second, active, slope = second
-        grad_low, hidden_grad, residual_grad, residual_low, attended_grad, mlp_sums = mlp_backward(
-            stream_grad, slope, residual, up, output, vector
-        )
-        output_grads = output_weight_grad(
-            attended, active, residual_low, grad_low, (D // 2,) * 2 if index else (D,)
+        residual_grad, attended_grad, mlp_sums, up_grad, *output_grads = mlp_backward(
+            stream_grad,
+            slope,
+            residual,
+            normed_second,
+            active,
+            attended,
+            up,
+            output,
+            vector,
+            (D // 2,) * 2 if index else (D,),
         )
         attended_grad, *output_grads = lax.optimization_barrier((attended_grad, *output_grads))
-        up_grad = input_weight_grad(normed_second, hidden_grad)
         output_parts = [scatter(by_owner(grad)) for grad in output_grads]
+        qkv_grad, beside_sum = attention_backward(
+            qkv_rows,
+            expo,
+            inverse,
+            attended,
+            attended_grad,
+            [SumRide(by_owner(head_grad), False) if index else SumRide(by_owner(up_grad), True)],
+            6 if index else 8,
+        )
+        stream_grad, qkv_sums, qkv_weight_grad, *output_one_sum = qkv_backward(
+            qkv_grad,
+            residual_grad,
+            entering,
+            normed,
+            qkv_weight,
+            vector,
+            () if index else [ShareRide(jnp.concatenate(early_parts, 1))],
+            7,
+        )
         if index:
-            early_parts.extend(output_parts)
-            beside = [SumRide(by_owner(head_grad), False)]
-        else:
-            (last_part,) = output_parts
-            beside = [ShareRide(jnp.concatenate(early_parts, 1)), SumRide(by_owner(up_grad), True)]
-        qkv_grad, *beside_sums = attention_backward(
-            qkv_rows, expo, inverse, attended, attended_grad, beside, 6 if index else 8
-        )
-        stream_grad, qkv_sums = qkv_backward(qkv_grad, residual_grad, entering, qkv_weight, vector)
-        qkv_weight_grad = input_weight_grad(normed, qkv_grad)
-        if index:
-            (head_sum,) = beside_sums
+            head_sum = beside_sum
+            early_parts = output_parts
             stream_grad, qkv_weight_grad, up_grad = lax.optimization_barrier(
                 (stream_grad, qkv_weight_grad, up_grad)
             )
-            late_parts.extend(scatter(by_owner(grad)) for grad in (qkv_weight_grad, up_grad))
+            late_parts = [scatter(by_owner(grad)) for grad in (qkv_weight_grad, up_grad)]
         else:
-            output_one_sum, up_zero_sum = beside_sums
+            up_zero_sum, (output_one_sum,), (last_part,) = beside_sum, output_one_sum, output_parts
         vector_grads[index] = jnp.concatenate(
             [
                 qkv_sums[0, : 2 * D],

time: 659 us -> 658 us (level)
    pallas_call x19 -> x13, Pallas kernels: 394 us -> 361 us  [block_call(): pl.pallas_call(kernel, grid=(grid,), in_specs=in_specs, out_specs=out_spe...]
    pallas_call x1, Pallas kernels: 63 us -> 80.3 us  [begin(): pl.pallas_call(functools.partial(first_kernel, spots=spots), in_specs=[AN...]
    pallas_call x1, Pallas kernels: 83.2 us -> 94.6 us  [reduce_call(): pl.pallas_call(functools.partial(reduce_kernel, whole=whole, partly=partl...]
  transfers between devices with their start and end apart: 8 -> 8, of which waited for: 0 -> 1; matrix products, arithmetic and copies ran while one was open for 2% -> 2% of each run, Pallas kernels for 68% -> 65%
where the time goes in v11:
time: 658 us; the launch traced here: 651 us
  Pallas kernels  581 us (88%)
  other arithmetic  33.7 us (5%)
  local copies, waits for them, and re-layouts  15.2 us (2%)
  between operations  15 us (2%)
    pallas_call x13, Pallas kernels, block_call(): pl.pallas_call(kernel, grid=(grid,), in_specs=in_specs, out_specs=out_spe...  361 us
    pallas_call x1, Pallas kernels, reduce_call(): pl.pallas_call(functools.partial(reduce_kernel, whole=whole, partly=partl...  94.6 us
    pallas_call x1, Pallas kernels, begin(): pl.pallas_call(functools.partial(first_kernel, spots=spots), in_specs=[AN...  80.3 us
    pallas_call x1, Pallas kernels, finish_call(): pl.pallas_call(functools.partial(finish_kernel, done=done, partly=partly,...  34.7 us
    sub x7, other arithmetic, adam_update(): return (moment, square, weight - learn_rate * step_dir)  26 us
  transfers between devices with their start and end apart: 8, of which 1 were waited for; matrix products, arithmetic and copies ran while one was open for 2% of the time, Pallas kernels for 65%

profile of v11, /device:TPU:0, one launch (start us, length us, event | category | flops | bytes accessed | tf_op | source)
XLA Modules:
  0.0 651.2 jit_solution(647773772157616483)
XLA Ops:
  7.2 0.0 all-gather.4.cloned.1.call-start
  7.2 0.7 convert_element_type.23
  8.0 0.2 dynamic_update_slice.3
  8.2 0.6 reshape.122.refs_1_
  8.8 1.3 broadcast_in_dim.22.refs_9_
  10.2 1.7 copy.50.refs_6_.refs_3_.seg_col_ref
  11.9 80.3 %begin.1 = (f32[1024,768]{1,0:T(8,128)}, f32[64,1024]{1,0:T(8,128)}, f32[1,9984]{1,0:T(1,128)}, f32[1,9984]{1,0:T(1,128)}, bf16[8,96,2304]{2,1,0:T(8,128)(2,1)},...) custom-call(f32[384,768]{1,0:T(8,128)} %refs_0_.1, ...), custom_call_target="tpu_custom_call" | custom-call | tf_op jit(solution)/shard_map/begin/pallas_call | solution.py:763
  92.2 0.0 all-gather.6.cloned.1.call-start
  92.3 0.7 all-gather.6.cloned.1.call-update
  93.0 0.7 all-gather.8.cloned.1.call-update
  93.7 0.2 reduce-scatter.6.cloned.1.call-start
  93.9 9.1 %qkv_forward.2 = (bf16[1024,768]{1,0:T(8,128)(2,1)}, bf16[1024,2304]{1,0:T(8,128)(2,1)}) custom-call(f32[1024,768]{1,0:T(8,128)} %get-tuple-element.105.stream_ref.refs_2_, bf16[768,2304]{1,0:T(8,128)(2,1)} %bitcast.55, f32[1,9984]{1,0:T(1,128)} %get-tuple-element.107.vector_ref.refs_5_), custom_call_target="tpu_custom_call" | custom-call | flops 3623878656 | bytes 14548992 | tf_op jit(solution)/shard_map/qkv_forward/pallas_call | solution.py:536
  103.0 38.2 %attention_forward.2 = (bf16[1024,768]{1,0:T(8,128)(2,1)}, bf16[12,1024,1024]{2,1,0:T(8,128)(2,1)}, f32[1024,768]{1,0:T(8,128)}, bf16[8,480,768]{2,1,0:T(8,128)(2,1)}, bf16[4,240,384]{2,1,0:T(8,128)(2,1)}) custom-call(bf16[1024,2304]{1,0:T(8,128)(2,1)} %get-tuple-element.108.refs_0_.refs_1_.refs_2_, ...), custom_call_target="tpu_custom_call" | custom-call | flops 12884901888 | bytes 34603008 | tf_op jit(solution)/shard_map/attention_forward/pallas_call | solution.py:536
  141.3 21.0 %mlp_forward.2 = (f32[1024,768]{1,0:T(8,128)}, bf16[1024,768]{1,0:T(8,128)(2,1)}, bf16[1024,3072]{1,0:T(8,128)(2,1)}, bf16[1024,3072]{1,0:T(8,128)(2,1)}, f32[1024,768]{1,0:T(8,128)}) custom-call(f32[1024,768]{1,0:T(8,128)} %get-tuple-element.105.stream_ref.refs_2_, bf16[1024,768]{1,0:T(8,128)(2,1)} %get-tuple-element.112.attended_ref.refs_5_, ...), custom_call_target="tpu_custom_call" | custom-call | flops 10871635968 | bytes 35782656 | tf_op jit(solution)/shard_map/mlp_forward/pallas_call | solution.py:536
  162.3 0.7 copy.54.label_ref
  163.0 0.6 broadcast_in_dim.24.vector_ref
  163.6 9.4 %qkv_forward.3 = (bf16[1024,768]{1,0:T(8,128)(2,1)}, bf16[1024,2304]{1,0:T(8,128)(2,1)}) custom-call(f32[1024,768]{1,0:T(8,128)} %get-tuple-element.115.stream_ref.stream_in, bf16[768,2304]{1,0:T(8,128)(2,1)} %all-gather.4.cloned.1.call-done.weight_ref, f32[1,9984]{1,0:T(1,128)} %get-tuple-element.117.vector_ref), custom_call_target="tpu_custom_call" | custom-call | flops 3623878656 | bytes 14548992 | tf_op jit(solution)/shard_map/qkv_forward/pallas_call | solution.py:536
  173.0 42.3 %attention_forward.3 = (bf16[1024,768]{1,0:T(8,128)(2,1)}, bf16[12,1024,1024]{2,1,0:T(8,128)(2,1)}, f32[1024,768]{1,0:T(8,128)}, bf16[8,480,768]{2,1,0:T(8,128)(2,1)}) custom-call(bf16[1024,2304]{1,0:T(8,128)(2,1)} %get-tuple-element.118.refs_0_.refs_1_.refs_2_, bf16[1024,2304]{1,0:T(8,128)(2,1)} %get-tuple-element.118.refs_0_.refs_1_.refs_2_, ...), custom_call_target="tpu_custom_call" | custom-call | flops 12884901888 | bytes 34603008 | tf_op jit(solution)/shard_map/attention_forward/pallas_call | solution.py:536
  215.3 21.4 %mlp_forward.3 = (f32[1024,768]{1,0:T(8,128)}, bf16[1024,768]{1,0:T(8,128)(2,1)}, bf16[1024,3072]{1,0:T(8,128)(2,1)}, bf16[1024,3072]{1,0:T(8,128)(2,1)}, f32[1024,768]{1,0:T(8,128)}) custom-call(f32[1024,768]{1,0:T(8,128)} %get-tuple-element.115.stream_ref.stream_in, bf16[1024,768]{1,0:T(8,128)(2,1)} %get-tuple-element.122.attended_ref.refs_5_, ...), custom_call_target="tpu_custom_call" | custom-call | flops 10871635968 | bytes 35782656 | tf_op jit(solution)/shard_map/mlp_forward/pallas_call | solution.py:536
  236.7 10.7 %head.1 = (f32[1024,768]{1,0:T(8,128)}, bf16[768,1024]{1,0:T(8,128)(2,1)}, f32[1,1536]{1,0:T(1,128)}, f32[1,1024]{1,0:T(1,128)}, f32[1,2]{1,0:T(1,128)}) custom-call(f32[1024,768]{1,0:T(8,128)} %get-tuple-element.125.stream_ref, s32[1024,1]{1,0:T(8,128)} %copy.50.refs_6_.refs_3_.seg_col_ref, s32[1,1024]{1,0:T(1,128)} %bitcast.74, s32[8,1]{1,0:T(8,128)} %copy.54.label_ref, ...), custom_call_target="tpu_custom_call" | custom-call | tf_op jit(solution)/shard_map/head/pallas_call | solution.py:2083
  247.4 35.3 %mlp_backward.2 = (f32[1024,768]{1,0:T(8,128)}, bf16[1024,768]{1,0:T(8,128)(2,1)}, f32[1,6144]{1,0:T(1,128)}, bf16[768,3072]{1,0:T(8,128)(2,1)}, bf16[3840,384]{1,0:T(8,128)(2,1)}, /*index=5*/bf16[3840,384]{1,0:T(8,128)(2,1)}) custom-call(f32[1024,768]{1,0:T(8,128)} %get-tuple-element.127.grad_ref, bf16[1024,3072]{1,0:T(8,128)(2,1)} %get-tuple-element.128.slope_ref, ...), custom_call_target="tpu_custom_call" | custom-call | tf_op jit(solution)/shard_map/mlp_backward/pallas_call | solution.py:536
  282.8 0.0 reduce-scatter.8.cloned.1.call-start
  282.8 0.5 reduce-scatter.8.cloned.1.call-update
  283.4 36.4 %attention_backward.2 = (bf16[1024,2304]{1,0:T(8,128)(2,1)}, bf16[96,1024]{1,0:T(8,128)(2,1)}) custom-call(bf16[1024,2304]{1,0:T(8,128)(2,1)} %get-tuple-element.118.refs_0_.refs_1_.refs_2_, bf16[1024,2304]{1,0:T(8,128)(2,1)} %get-tuple-element.118.refs_0_.refs_1_.refs_2_, bf16[1024,2304]{1,0:T(8,128)(2,1)} %get-tuple-element.118.refs_0_.refs_1_.refs_2_, ...), custom_call_target="tpu_custom_call" | custom-call | tf_op jit(solution)/shard_map/attention_backward/pallas_call | solution.py:536
  319.9 15.2 %qkv_backward.2 = (f32[1024,768]{1,0:T(8,128)}, f32[1,3840]{1,0:T(1,128)}, bf16[768,2304]{1,0:T(8,128)(2,1)}) custom-call(bf16[1024,2304]{1,0:T(8,128)(2,1)} %get-tuple-element.140.grad_ref, f32[1024,768]{1,0:T(8,128)} %get-tuple-element.141.residual_in, f32[1024,768]{1,0:T(8,128)} %get-tuple-element.115.stream_ref.stream_in, ...), custom_call_target="tpu_custom_call" | custom-call | tf_op jit(solution)/shard_map/qkv_backward/pallas_call | solution.py:536
  335.1 0.0 reduce-scatter.12.cloned.1.call-start
  335.2 0.7 reduce-scatter.12.cloned.1.call-update
  335.9 0.0 reduce-scatter.14.cloned.1.call-start
  335.9 35.7 %mlp_backward.3 = (f32[1024,768]{1,0:T(8,128)}, bf16[1024,768]{1,0:T(8,128)(2,1)}, f32[1,6144]{1,0:T(1,128)}, bf16[768,3072]{1,0:T(8,128)(2,1)}, bf16[3840,768]{1,0:T(8,128)(2,1)}) custom-call(f32[1024,768]{1,0:T(8,128)} %get-tuple-element.146.grad_ref, bf16[1024,3072]{1,0:T(8,128)(2,1)} %get-tuple-element.147.slope_ref, ...), custom_call_target="tpu_custom_call" | custom-call | tf_op jit(solution)/shard_map/mlp_backward/pallas_call | solution.py:536
  371.7 0.7 copy-done.20
  372.5 0.1 stack.28
  372.7 59.2 %attention_backward.3 = (bf16[1024,2304]{1,0:T(8,128)(2,1)}, bf16[96,3072]{1,0:T(8,128)(2,1)}) custom-call(bf16[1024,2304]{1,0:T(8,128)(2,1)} %get-tuple-element.108.refs_0_.refs_1_.refs_2_, bf16[1024,2304]{1,0:T(8,128)(2,1)} %get-tuple-element.108.refs_0_.refs_1_.refs_2_, bf16[1024,2304]{1,0:T(8,128)(2,1)} %get-tuple-element.108.refs_0_.refs_1_.refs_2_, ...), custom_call_target="tpu_custom_call" | custom-call | tf_op jit(solution)/shard_map/attention_backward/pallas_call | solution.py:536
  432.1 2.0 pad_maximum_fusion.2.refs_6_
  434.1 25.5 %qkv_backward.3 = (f32[1024,768]{1,0:T(8,128)}, f32[1,3840]{1,0:T(1,128)}, bf16[768,2304]{1,0:T(8,128)(2,1)}, bf16[480,768]{1,0:T(8,128)(2,1)}) custom-call(bf16[1024,2304]{1,0:T(8,128)(2,1)} %get-tuple-element.155.refs_0_, f32[1024,768]{1,0:T(8,128)} %get-tuple-element.156.refs_1_, f32[1024,768]{1,0:T(8,128)} %get-tuple-element.105.stream_ref.refs_2_, ...), custom_call_target="tpu_custom_call" | custom-call | tf_op jit(solution)/shard_map/qkv_backward/pallas_call | solution.py:536
  459.6 0.7 slice_reduce_fusion.3
  460.4 0.7 slice_reduce_fusion.6
  461.1 0.1 stack.27
  461.2 0.1 maximum_bitcast_fusion.2
  461.3 0.1 reshape.134
  461.4 12.1 %embed_backward.1 = (bf16[3072,768]{1,0:T(8,128)(2,1)}, f32[64,768]{1,0:T(8,128)}, f32[1,768]{1,0:T(1,128)}) custom-call(bf16[1024,3072]{1,0:T(8,128)(2,1)} %pixel_ref.1, f32[1024,768]{1,0:T(8,128)} %get-tuple-element.163.grad_ref, f32[64,1024]{1,0:T(8,128)} %get-tuple-element.164.pos_ref), custom_call_target="tpu_custom_call" | custom-call | tf_op jit(solution)/shard_map/embed_backward/pallas_call | solution.py:536
  473.6 0.7 reduce.8
  474.3 0.9 slice.70
  475.2 0.1 concatenate.25
  475.5 0.7 pad.19.refs_2_
  476.2 2.7 reduce-scatter.12.cloned.1.call-done
  478.9 94.6 %reduce_gradients.1 = (bf16[96,2304]{1,0:T(8,128)(2,1)}, bf16[384,768]{1,0:T(8,128)(2,1)}, f32[64,128]{1,0:T(8,128)}, bf16[96,2304]{1,0:T(8,128)(2,1)}, bf16[96,3072]{1,0:T(8,128)(2,1)}) custom-call(bf16[8,96,2304]{2,1,0:T(8,128)(2,1)} %bitcast.58, bf16[8,384,768]{2,1,0:T(8,128)(2,1)} %bitcast.52, f32[8,64,128]{2,1,0:T(8,128)} %pad.19.refs_2_, ...), custom_call_target="tpu_custom_call" | custom-call | tf_op jit(solution)/shard_map/reduce_gradients/pallas_call | solution.py:1380
  573.5 0.7 slice_bitcast_fusion
  574.3 1.3 maximum_bitcast_fusion.1
  575.5 1.1 maximum_bitcast_fusion
  576.7 34.7 %finish_gradients.1 = (bf16[480,768]{1,0:T(8,128)(2,1)}, f32[8,64,128]{2,1,0:T(8,128)}, f32[1,128]{1,0:T(1,128)}) custom-call(bf16[96,1024]{1,0:T(8,128)(2,1)} %get-tuple-element.137.refs_0_, bf16[480,768]{1,0:T(8,128)(2,1)} %get-tuple-element.160.refs_1_, bf16[96,3072]{1,0:T(8,128)(2,1)} %get-tuple-element.161.refs_2_, ...), custom_call_target="tpu_custom_call" | custom-call | tf_op jit(solution)/shard_map/finish_gradients/pallas_call | solution.py:1452
  611.4 1.4 fusion.15
  612.9 0.5 slice_multiply_fusion.2
  613.4 0.1 mul.216
  613.5 0.9 slice.79
  614.5 0.7 copy-done.13
  615.1 1.2 slice_multiply_fusion
  616.3 1.6 mul.221
  618.0 2.0 multiply_subtract_fusion.5
  620.0 3.1 multiply_subtract_fusion.3
  623.1 4.8 multiply_subtract_fusion.2
  628.0 0.6 multiply_subtract_fusion.6
  628.6 1.9 multiply_subtract_fusion.4
  630.6 6.7 %multiply_subtract_fusion.1 = (f32[2,480,768]{2,1,0:T(8,128)}, f32[2,480,768]{2,1,0:T(8,128)}, f32[2,480,768]{2,1,0:T(8,128)}) fusion(f32[2,480,768]{2,1,0:T(8,128)S(1)} %copy-done.1, f32[]{:T(128)} %bitcast.28, bf16[1,480,768]{2,1,0:T(8,128)(2,1)S(1)} %bitcast.61, bf16[1,480,768]{2,1,0:T(8,128)(2,1)} %bitcast.64, f32[2,480,768]{2,1,0:T(8,128)S(1)} %copy-done.5, ...), kind=kLoop, calls=%fused_computation.8 | loop fusion | flops 12533760 | bytes 19169284 | tf_op jit(solution)/shard_map/sub | solution.py:2107
  637.3 6.8 %multiply_subtract_fusion = (f32[2,96,5376]{2,1,0:T(8,128)}, f32[2,96,5376]{2,1,0:T(8,128)}, f32[2,96,5376]{2,1,0:T(8,128)}) fusion(f32[2,96,5376]{2,1,0:T(8,128)S(1)} %copy-done, f32[]{:T(128)} %bitcast.28, bf16[1,96,5376]{2,1,0:T(8,128)(2,1)S(1)} %maximum_bitcast_fusion.1, bf16[1,96,5376]{2,1,0:T(8,128)(2,1)S(1)} %maximum_bitcast_fusion, ...), kind=kLoop, calls=%fused_computation.5 | loop fusion | flops 17547264 | bytes 26836996 | tf_op jit(solution)/shard_map/sub | solution.py:2107
  (79 shorter events, 0.7 us)
Async XLA Ops:
  7.2 156.4 %all-gather.4.cloned.1.call-start = ((), (), s32[]{:S(2)}) async-start(), calls=%async_computation.5 | async-start | bytes 3981312 | tf_op jit(solution)/shard_map/all_gather | solution.py:2153
  92.2 123.1 %all-gather.6.cloned.1.call-start = ((), (), s32[]{:S(2)}) async-start(), calls=%async_computation.6 | async-start | bytes 5308416 | tf_op jit(solution)/shard_map/all_gather | solution.py:2153
  93.0 143.8 %all-gather.8.cloned.1.call-start = ((), (), s32[]{:S(2)}) async-start(), calls=%async_computation.7 | async-start | bytes 1769472 | tf_op jit(solution)/shard_map/all_gather | solution.py:2153
  93.7 338.3 %reduce-scatter.6.cloned.1.call-start = ((), (), s32[]{:S(2)}) async-start(), calls=%async_computation.8 | async-start | bytes 3317760 | tf_op jit(solution)/shard_map/reduce_scatter | solution.py:1490
  141.3 21.0 %copy-start.26 = (s32[1,8]{1,0:T(1,128)S(1)}, s32[1,8]{1,0:T(1,128)}, u32[]{:S(2)}) copy-start(s32[1,8]{1,0:T(1,128)} %param.28) | copy-start | bytes 100
  141.3 21.7 %copy-start.14 = (f32[3304]{0:T(1024)S(1)}, f32[3304]{0:T(1024)}, u32[]{:S(2)}) copy-start(f32[3304]{0:T(1024)} %param.35) | copy-start | bytes 39652
  282.8 149.3 %reduce-scatter.8.cloned.1.call-start = ((), (), s32[]{:S(2)}) async-start(), calls=%async_computation.9 | async-start | bytes 3317760 | tf_op jit(solution)/shard_map/reduce_scatter | solution.py:1490
  283.4 192.8 %reduce-scatter.10.cloned.1.call-start = ((), (), s32[]{:S(2)}) async-start(), calls=%async_computation.10 | async-start | bytes 3981312 | tf_op jit(solution)/shard_map/reduce_scatter | solution.py:1490
  335.1 143.8 %reduce-scatter.12.cloned.1.call-start = ((), (), s32[]{:S(2)}) async-start(), calls=%async_computation.11 | async-start | bytes 5308416 | tf_op jit(solution)/shard_map/reduce_scatter | solution.py:1490
  335.9 240.8 %reduce-scatter.14.cloned.1.call-start = ((), (), s32[]{:S(2)}) async-start(), calls=%async_computation.12 | async-start | bytes 6635520 | tf_op jit(solution)/shard_map/reduce_scatter | solution.py:1490
  371.7 0.7 copy-start.20
  371.7 0.7 copy-start.16
  371.7 1.0 copy-start.23
  372.7 59.3 %copy-start.17 = (f32[1,6144]{1,0:T(1,128)S(1)}, f32[1,6144]{1,0:T(1,128)}, u32[]{:S(2)}) copy-start(f32[1,6144]{1,0:T(1,128)} %get-tuple-element.167) | copy-start | bytes 73732
  461.4 13.8 %copy-start.24 = (f32[1,1024]{1,0:T(1,128)S(1)}, f32[1,1024]{1,0:T(1,128)}, u32[]{:S(2)}) copy-start(f32[1,1024]{1,0:T(1,128)} %get-tuple-element.173) | copy-start | bytes 12292
  461.4 13.8 %copy-start.25 = (f32[1,2]{1,0:T(1,128)S(1)}, f32[1,2]{1,0:T(1,128)}, u32[]{:S(2)}) copy-start(f32[1,2]{1,0:T(1,128)} %get-tuple-element.174) | copy-start | bytes 28
  478.9 96.6 %copy-start.8 = (bf16[96,3072]{1,0:T(8,128)(2,1)S(1)}, bf16[96,3072]{1,0:T(8,128)(2,1)}, u32[]{:S(2)}) copy-start(bf16[96,3072]{1,0:T(8,128)(2,1)} %get-tuple-element.161.refs_2_) | copy-start | bytes 1769476
  576.6 41.3 %copy-start.18 = (f32[3304]{0:T(1024)S(1)}, f32[3304]{0:T(1024)}, u32[]{:S(2)}) copy-start(f32[3304]{0:T(1024)} %param.49) | copy-start | bytes 39652
  576.6 41.3 %copy-start.19 = (f32[3304]{0:T(1024)S(1)}, f32[3304]{0:T(1024)}, u32[]{:S(2)}) copy-start(f32[3304]{0:T(1024)} %param.42) | copy-start | bytes 39652
  576.6 43.4 %copy-start.11 = (bf16[96,1024]{1,0:T(8,128)(2,1)S(1)}, bf16[96,1024]{1,0:T(8,128)(2,1)}, u32[]{:S(2)}) copy-start(bf16[96,1024]{1,0:T(8,128)(2,1)} %get-tuple-element.137.refs_0_) | copy-start | bytes 589828
  576.7 46.4 %copy-start.2 = (f32[384,768]{1,0:T(8,128)S(1)}, f32[384,768]{1,0:T(8,128)}, u32[]{:S(2)}) copy-start(f32[384,768]{1,0:T(8,128)} %refs_0_.1) | copy-start | bytes 3538948
  576.7 51.3 %copy-start.15 = (f32[2,1248]{1,0:T(2,128)S(1)}, f32[2,1248]{1,0:T(2,128)}, u32[]{:S(2)}) copy-start(f32[2,1248]{1,0:T(2,128)} %param.33) | copy-start | bytes 29956
  576.7 51.3 %copy-start.21 = (f32[2,1248]{1,0:T(2,128)S(1)}, f32[2,1248]{1,0:T(2,128)}, u32[]{:S(2)}) copy-start(f32[2,1248]{1,0:T(2,128)} %param.47) | copy-start | bytes 29956
  576.7 51.3 %copy-start.22 = (f32[2,1248]{1,0:T(2,128)S(1)}, f32[2,1248]{1,0:T(2,128)}, u32[]{:S(2)}) copy-start(f32[2,1248]{1,0:T(2,128)} %param.40) | copy-start | bytes 29956
  614.4 0.7 copy-start.13
  617.9 5.2 copy-start.9
  617.9 5.2 copy-start.10
  620.0 8.6 %copy-start.12 = (f32[49,768]{1,0:T(8,128)S(1)}, f32[49,768]{1,0:T(8,128)}, u32[]{:S(2)}) copy-start(f32[49,768]{1,0:T(8,128)} %mul.221) | copy-start | bytes 451588
  620.0 10.6 %copy-start.7 = (bf16[480,768]{1,0:T(8,128)(2,1)S(1)}, bf16[480,768]{1,0:T(8,128)(2,1)}, u32[]{:S(2)}) copy-start(bf16[480,768]{1,0:T(8,128)(2,1)} %get-tuple-element.160.refs_1_) | copy-start | bytes 2211844
  623.1 7.5 %copy-start.1 = (f32[2,480,768]{2,1,0:T(8,128)S(1)}, f32[2,480,768]{2,1,0:T(8,128)}, u32[]{:S(2)}) copy-start(f32[2,480,768]{2,1,0:T(8,128)} %refs_3_.1) | copy-start | bytes 8847364
  623.1 7.5 %copy-start.5 = (f32[2,480,768]{2,1,0:T(8,128)S(1)}, f32[2,480,768]{2,1,0:T(8,128)}, u32[]{:S(2)}) copy-start(f32[2,480,768]{2,1,0:T(8,128)} %param.46) | copy-start | bytes 8847364
  623.1 7.5 %copy-start.6 = (f32[2,480,768]{2,1,0:T(8,128)S(1)}, f32[2,480,768]{2,1,0:T(8,128)}, u32[]{:S(2)}) copy-start(f32[2,480,768]{2,1,0:T(8,128)} %param.39) | copy-start | bytes 8847364
  630.6 6.7 %copy-start = (f32[2,96,5376]{2,1,0:T(8,128)S(1)}, f32[2,96,5376]{2,1,0:T(8,128)}, u32[]{:S(2)}) copy-start(f32[2,96,5376]{2,1,0:T(8,128)} %refs_2_.1) | copy-start | bytes 12386308
  630.6 6.7 %copy-start.3 = (f32[2,96,5376]{2,1,0:T(8,128)S(1)}, f32[2,96,5376]{2,1,0:T(8,128)}, u32[]{:S(2)}) copy-start(f32[2,96,5376]{2,1,0:T(8,128)} %param.45) | copy-start | bytes 12386308
  630.6 6.7 %copy-start.4 = (f32[2,96,5376]{2,1,0:T(8,128)S(1)}, f32[2,96,5376]{2,1,0:T(8,128)}, u32[]{:S(2)}) copy-start(f32[2,96,5376]{2,1,0:T(8,128)} %param.38) | copy-start | bytes 12386308
Sparse Core Ops, SparseCore 0:
  92.3 58.7 all-gather.3
  152.7 50.5 all-gather.5
  204.9 23.8 all-gather.7
  282.9 41.1 reduce-scatter.5
  326.9 38.2 reduce-scatter.7
  368.0 49.6 reduce-scatter.9
  420.1 58.7 reduce-scatter.11
  481.3 80.5 reduce-scatter.13

commit v12 on v11

--- a/solution.py
+++ b/solution.py
@@ -463,6 +463,64 @@
     @property
     def after(self):
         return (("fourth",) if self.large else ()) + ("fifth", "sixth", "store")
+
+    def result(self, outs):
+        return outs[0]
+
+    def plain(self):
+        return lax.psum(scatter(self.operands[0]), "dp")
+
+
+class LeadRide:
+    after = ("third", "sixth", "store")
+
+    def __init__(self, grad):
+        _, rows, columns = grad.shape
+        shape = (4, rows // 2, columns // 2)
+        self.operands = [grad]
+        self.in_specs = [ANYWHERE]
+        self.out_specs = [fixed(*shape)]
+        self.out_shapes = [jax.ShapeDtypeStruct(shape, grad.dtype)]
+        self.scratch = [*stepped_scratch(grad), pltpu.SemaphoreType.DMA((WHOLE_SEMS,))]
+
+    def job(self, sources, targets, scratch):
+        job = Lead(sources[0], None, scratch[:-1], scratch[-1])
+        job.target = targets[0]
+        return job
+
+    def before(self, steps):
+        return {0: ("first",), 1: ("second",), steps - 2: ("between",)}
+
+    def result(self, outs):
+        return RestRide(outs[0])
+
+    def plain(self):
+        return RestRide(self.operands[0])
+
+
+class RestRide:
+    after = ("fifth", "sixth", "store")
+
+    def __init__(self, part):
+        _, high, wide = part.shape
+        block = (2 * high, 2 * wide)
+        self.operands = [part]
+        self.in_specs = [fixed(*part.shape)]
+        self.out_specs = [fixed(*block)]
+        self.out_shapes = [jax.ShapeDtypeStruct(block, part.dtype)]
+        self.scratch = [
+            pltpu.VMEM(block, part.dtype),
+            pltpu.VMEM((3, high, wide), part.dtype),
+            pltpu.SemaphoreType.DMA((WHOLE_SEMS,)),
+        ]
+
+    def job(self, sources, targets, scratch):
+        job = Rest(sources[0], *scratch)
+        job.target = targets[0]
+        return job
+
+    def before(self, steps):
+        return {0: ("first",), steps - 1: ("fourth",)}
 
     def result(self, outs):
         return outs[0]
@@ -584,10 +642,10 @@
     kernel, vectors, inputs, outputs, head, pixels, seg_col, patch_row, table, biases = refs[:10]
     stream, pos_t, vector_zero, vector_one = refs[10:14]
     qkv_full, up_full, output_level = refs[14:17]
-    output_zero, qkv_one, up_one, output_one, head_low = refs[17:22]
-    wide_kernel, wide_inputs, wide_outputs, wide_head, pixel_rows, table_low = refs[22:28]
-    kernel_full, qkv_zero, vectors_full, qkv_landing, up_landing, output_landing = refs[28:34]
-    up_zero, load_sems, sems = refs[34:]
+    output_zero, qkv_one, up_one, output_one, head_low, normed, qkv_rows = refs[17:24]
+    wide_kernel, wide_inputs, wide_outputs, wide_head, pixel_rows, table_low = refs[24:30]
+    kernel_full, qkv_zero, vectors_full, qkv_landing, up_landing, output_landing = refs[30:36]
+    up_zero, load_sems, sems = refs[36:]
     _, level, core = place()
     mine = 2 * level + core
     pairs = [
@@ -686,6 +744,14 @@
     qkv_job.fourth()
     copy = pltpu.make_async_copy(qkv_landing, qkv_full, load_sems.at[0])
     copy.start()
+    weight = qkv_landing[...].reshape(-1, qkv_landing.shape[2])
+    for half in halves_of(stream.shape[0]):
+        unit, _ = normalized(stream[half, :])
+        low = (unit * vector_zero[:, :D] + vector_zero[:, D : 2 * D]).astype(LOW)
+        normed[half, :] = low
+        for base in range(0, 3 * D, D):
+            bias = vector_zero[:, 4 * D + base : 5 * D + base]
+            qkv_rows[half, base : base + D] = (mul(low, weight[:, base : base + D]) + bias).astype(LOW)
     up_job.fourth()
     up_copy = pltpu.make_async_copy(up_landing, up_full, load_sems.at[1])
     up_copy.start()
@@ -734,6 +800,7 @@
             gather(inputs[0][1], 0),
             [GatherRide(outputs[0], outputs[0]), LevelRide(outputs[1])],
             [*inputs[1], head],
+            qkv_forward(stream, gather(inputs[0][0], 0), vectors[:1]),
         )
     rows = pixels.shape[0]
     owners = lax.axis_size("fsdp")
@@ -757,13 +824,15 @@
         low(*up_shape),
         low(*out_shape),
         low(head_weight.shape[0], classes),
+        low(rows, D),
+        low(rows, 3 * D),
     ]
     wide = (patch_kernel, input_proj, output_proj, head_weight, pixels)
     in_vmem = pl.BlockSpec(memory_space=pltpu.VMEM)
     results = pl.pallas_call(
         functools.partial(first_kernel, spots=spots),
         in_specs=[ANYWHERE] * 6 + [in_vmem] * 4,
-        out_specs=[in_vmem] * 4 + [ANYWHERE] * 2 + [in_vmem] * 6,
+        out_specs=[in_vmem] * 4 + [ANYWHERE] * 2 + [in_vmem] * 8,
         out_shape=shapes,
         scratch_shapes=[
             *[pltpu.VMEM(array.shape, array.dtype) for array in wide],
@@ -795,7 +864,7 @@
         position_table,
         global_vector[None, :],
     )
-    output_zero, qkv_one, up_one, output_one, head_low = results[7:]
+    output_zero, qkv_one, up_one, output_one, head_low, normed, qkv_rows = results[7:]
     return (
         results[0],
         results[1],
@@ -804,6 +873,7 @@
         results[5].reshape(owners * depth, up_shape[1]),
         [GatherRide(output_zero, results[6]), LevelRide(output_one)],
         [qkv_one, up_one, head_low],
+        (normed, qkv_rows),
     )
 
 
@@ -988,10 +1058,12 @@
 class Whole:
     FIRST_X = (1, 0)
 
+    lead = False
+
     def __init__(self, grad, out, scratch, sems):
         self.grad, self.out, self.sems = grad, out, sems
         self.own, self.away, self.got_core, self.got_x, self.got_y, self.got_last, self.part, self.got_level = scratch
-        self.rows, self.columns = out.shape
+        self.rows, self.columns = grad.shape[1:]
         self.high, self.wide = self.rows // 2, self.columns // 2
 
     def row_half(self, index):
@@ -1127,7 +1199,7 @@
                 return carry
 
             lax.fori_loop(0, self.high // chunk, add, 0)
-            if turn:
+            if turn and not self.lead:
                 self.level_copy(turn).start()
 
     def fourth(self):
@@ -1165,9 +1237,32 @@
             self.core_copy(partner(level, turn)).wait_send()
             self.step_copy(turn).wait_send()
             self.last_copy(turn).wait_send()
-            if turn:
+            if turn and not self.lead:
                 self.level_copy(turn).wait_send()
                 self.share_copy(turn).wait_send()
+
+
+class Lead(Whole):
+    lead = True
+
+    def store(self):
+        self.target[...] = self.part[...]
+
+
+class Rest(Whole):
+    def __init__(self, part, out, got_level, sems):
+        self.part, self.out, self.got_level, self.sems = part, out, got_level, sems
+        self.rows, self.columns = out.shape
+        self.high, self.wide = self.rows // 2, self.columns // 2
+
+    def first(self):
+        for turn in TURNS:
+            self.level_copy(turn).start()
+
+    def sixth(self):
+        for turn in TURNS:
+            self.level_copy(turn).wait_send()
+            self.share_copy(turn).wait_send()
 
 
 GROUP_SEMS = 13
@@ -1831,28 +1926,22 @@
 
 def mlp_back_kernel(
     grad_ref, slope_ref, residual_in, normed_ref, active_ref, attended_ref, mix_ref, up_ref, down_ref, vector_ref,
-    out_ref, attended_grad_ref, sums_ref, up_grad_ref, *refs,
+    out_ref, attended_grad_ref, sums_ref, up_grad_ref, output_grad,
+    residual_ref, low_ref, second_ref, turned_ref, hidden_ref, product_ref, sems,
 ):
-    outs, scratch = refs[:-7], refs[-7:]
-    residual_ref, low_ref, second_ref, turned_ref, hidden_ref, product_ref, sems = scratch
     rows = grad_ref.shape[0]
     step = pl.program_id(0)
-    load = pltpu.make_async_copy(residual_in, residual_ref, sems.at[0, 0])
-
-    def stores(slot):
-        copies, base = [], 0
-        for index, out in enumerate(outs):
-            width = out.shape[1]
-            source = product_ref.at[slot, :, pl.ds(base, width)]
-            target = out.at[pl.ds(pl.multiple_of(slot * D, D), D)]
-            copies.append(pltpu.make_async_copy(source, target, sems.at[1 + index, slot]))
-            base += width
-        return copies
+    load = pltpu.make_async_copy(residual_in, residual_ref, sems.at[0])
+
+    def store_copy(slot):
+        rows_at = pl.ds(pl.multiple_of(slot * D, D), D)
+        return pltpu.make_async_copy(
+            product_ref.at[slot], output_grad.at[rows_at], sems.at[1 + slot]
+        )
 
     def store(slot, product):
         product_ref[slot] = product.astype(LOW)
-        for copy in stores(slot):
-            copy.start()
+        store_copy(slot).start()
 
     @at_first
     def _():
@@ -1897,11 +1986,12 @@
         sums_ref[:, : 4 * D] = jnp.concatenate(totals, 1)
         store(0, mul(attended_ref[...].T, hidden_ref[...]))
         for slot in range(product_ref.shape[0]):
-            for copy in stores(slot):
-                copy.wait()
-
-
-def mlp_backward(grad, slope, residual, normed, active, attended, up, proj_out, vector, parts):
+            store_copy(slot).wait()
+
+
+def mlp_backward(
+    grad, slope, residual, normed, active, attended, up, proj_out, vector, rides, collective_id
+):
     rows = grad.shape[0]
     width = up.shape[1]
     steps = width // D
@@ -1921,13 +2011,13 @@
             fixed(1, vector.shape[1]),
         ],
         [grad, slope, residual, normed, active, attended, *weights, vector],
-        [whole, whole, fixed(1, 4 * D + width), columns_of(D), *[ANYWHERE] * len(parts)],
+        [whole, whole, fixed(1, 4 * D + width), columns_of(D), ANYWHERE],
         [
             shape_of(rows, D),
             shape_of(rows, D, dtype=LOW),
             shape_of(1, 4 * D + width),
             shape_of(D, width, dtype=LOW),
-            *[shape_of(D + width, part, dtype=LOW) for part in parts],
+            shape_of(D + width, D, dtype=LOW),
         ],
         [
             pltpu.VMEM((rows, D), jnp.float32),
@@ -1936,9 +2026,12 @@
             pltpu.VMEM((D, rows), LOW),
             pltpu.VMEM((rows, D), LOW),
             pltpu.VMEM((steps + 1, D, D), LOW),
-            pltpu.SemaphoreType.DMA((1 + len(parts), steps + 1)),
+            pltpu.SemaphoreType.DMA((steps + 2,)),
         ],
         "mlp_backward",
+        None,
+        rides,
+        collective_id,
     )
 
 
@@ -2137,7 +2230,7 @@
     owners = lax.axis_size("fsdp")
     nodes = position_table.shape[0]
     vector_size = layer_vector.size
-    stream, pos_weights_t, vectors, qkv_weight, up_zero, rides, rest_shards = begin(
+    stream, pos_weights_t, vectors, qkv_weight, up_zero, rides, rest_shards, first_rows = begin(
         pixels,
         segment,
         patch_size,
@@ -2155,7 +2248,10 @@
     saved_layers = []
     for index in range(LAYERS):
         vector = vectors[index]
-        normed, qkv_rows = qkv_forward(stream, qkv_weight, vector)
+        if index:
+            normed, qkv_rows = qkv_forward(stream, qkv_weight, vector)
+        else:
+            normed, qkv_rows = first_rows
         if index == 0:
             attended, expo, inverse, output, output_ride = attention_forward(
                 qkv_rows, segment, rides, 4
@@ -2183,7 +2279,7 @@
         (qkv_weight, up, output, vector), first, second = saved_layers[index]
         entering, normed, qkv_rows, attended, expo, inverse = first
         residual, normed_second, active, slope = second
-        residual_grad, attended_grad, mlp_sums, up_grad, *output_grads = mlp_backward(
+        residual_grad, attended_grad, mlp_sums, up_grad, output_grad, *brought = mlp_backward(
             stream_grad,
             slope,
             residual,
@@ -2193,38 +2289,40 @@
             up,
             output,
             vector,
-            (D // 2,) * 2 if index else (D,),
-        )
-        attended_grad, *output_grads = lax.optimization_barrier((attended_grad, *output_grads))
-        output_parts = [scatter(by_owner(grad)) for grad in output_grads]
-        qkv_grad, beside_sum = attention_backward(
+            () if index else [output_rest, SumRide(by_owner(head_grad), False)],
+            9,
+        )
+        if index == 0:
+            output_one_sum, head_sum = brought
+            attended_grad, output_grad = lax.optimization_barrier((attended_grad, output_grad))
+            last_part = scatter(by_owner(output_grad))
+        qkv_grad, rest = attention_backward(
             qkv_rows,
             expo,
             inverse,
             attended,
             attended_grad,
-            [SumRide(by_owner(head_grad), False) if index else SumRide(by_owner(up_grad), True)],
+            [LeadRide(by_owner(output_grad if index else up_grad))],
             6 if index else 8,
         )
-        stream_grad, qkv_sums, qkv_weight_grad, *output_one_sum = qkv_backward(
+        stream_grad, qkv_sums, qkv_weight_grad, *brought = qkv_backward(
             qkv_grad,
             residual_grad,
             entering,
             normed,
             qkv_weight,
             vector,
-            () if index else [ShareRide(jnp.concatenate(early_parts, 1))],
+            () if index else [rest],
             7,
         )
         if index:
-            head_sum = beside_sum
-            early_parts = output_parts
+            output_rest = rest
             stream_grad, qkv_weight_grad, up_grad = lax.optimization_barrier(
                 (stream_grad, qkv_weight_grad, up_grad)
             )
             late_parts = [scatter(by_owner(grad)) for grad in (qkv_weight_grad, up_grad)]
         else:
-            up_zero_sum, (output_one_sum,), (last_part,) = beside_sum, output_one_sum, output_parts
+            (up_zero_sum,) = brought
         vector_grads[index] = jnp.concatenate(
             [
                 qkv_sums[0, : 2 * D],

time: 658 us -> 648 us (0.985)
  Pallas kernels: 581 us -> 574 us
    pallas_call x1, Pallas kernels: 94.6 us -> 82.9 us  [reduce_call(): pl.pallas_call(functools.partial(reduce_kernel, whole=whole, partly=partl...]
    pallas_call x13 -> x12, Pallas kernels: 361 us -> 361 us  [block_call(): pl.pallas_call(kernel, grid=(grid,), in_specs=in_specs, out_specs=out_spe...]
  transfers between devices with their start and end apart: 8 -> 6, of which waited for: 1 -> 1; matrix products, arithmetic and copies ran while one was open for 2% -> 1% of each run, Pallas kernels for 65% -> 55%
where the time goes in v12:
time: 648 us; the launch traced here: 639 us
  Pallas kernels  574 us (89%)
  other arithmetic  31.7 us (5%)
  between operations  15.1 us (2%)
  local copies, waits for them, and re-layouts  14.5 us (2%)
    pallas_call x12, Pallas kernels, block_call(): pl.pallas_call(kernel, grid=(grid,), in_specs=in_specs, out_specs=out_spe...  361 us
    pallas_call x1, Pallas kernels, begin(): pl.pallas_call(functools.partial(first_kernel, spots=spots), in_specs=[AN...  85.1 us
    pallas_call x1, Pallas kernels, reduce_call(): pl.pallas_call(functools.partial(reduce_kernel, whole=whole, partly=partl...  82.9 us
    pallas_call x1, Pallas kernels, finish_call(): pl.pallas_call(functools.partial(finish_kernel, done=done, partly=partly,...  33.7 us
    sub x7, other arithmetic, adam_update(): return (moment, square, weight - learn_rate * step_dir)  26 us
  transfers between devices with their start and end apart: 6, of which 1 were waited for; matrix products, arithmetic and copies ran while one was open for 1% of the time, Pallas kernels for 55%

profile of v12, /device:TPU:0, one launch (start us, length us, event | category | flops | bytes accessed | tf_op | source)
XLA Modules:
  0.0 639.5 jit_solution(1765171450640371512)
XLA Ops:
  7.2 0.0 all-gather.4.cloned.1.call-start
  7.2 0.7 convert_element_type.23
  8.0 0.2 dynamic_update_slice.3
  8.2 0.6 reshape.119.refs_1_
  8.8 1.3 broadcast_in_dim.22.refs_9_
  10.2 1.7 copy.50.refs_6_.refs_3_.seg_col_ref
  11.9 85.1 %begin.1 = (f32[1024,768]{1,0:T(8,128)}, f32[64,1024]{1,0:T(8,128)}, f32[1,9984]{1,0:T(1,128)}, f32[1,9984]{1,0:T(1,128)}, bf16[8,96,2304]{2,1,0:T(8,128)(2,1)},...) custom-call(f32[384,768]{1,0:T(8,128)} %refs_0_.1, ...), custom_call_target="tpu_custom_call" | custom-call | tf_op jit(solution)/shard_map/begin/pallas_call | solution.py:832
  97.0 0.0 all-gather.4.cloned.1.call-update
  97.0 0.0 all-gather.6.cloned.1.call-start
  97.0 0.7 all-gather.6.cloned.1.call-update
  97.7 0.0 all-gather.8.cloned.1.call-start
  97.8 0.7 all-gather.8.cloned.1.call-update
  98.5 0.5 reduce-scatter.4.cloned.1.call-start
  99.0 36.4 %attention_forward.2 = (bf16[1024,768]{1,0:T(8,128)(2,1)}, bf16[12,1024,1024]{2,1,0:T(8,128)(2,1)}, f32[1024,768]{1,0:T(8,128)}, bf16[8,480,768]{2,1,0:T(8,128)(2,1)}, bf16[4,240,384]{2,1,0:T(8,128)(2,1)}) custom-call(bf16[1024,2304]{1,0:T(8,128)(2,1)} %get-tuple-element.104.refs_0_.refs_1_.refs_2_, ...), custom_call_target="tpu_custom_call" | custom-call | flops 12884901888 | bytes 34603008 | tf_op jit(solution)/shard_map/attention_forward/pallas_call | solution.py:594
  135.4 21.1 %mlp_forward.2 = (f32[1024,768]{1,0:T(8,128)}, bf16[1024,768]{1,0:T(8,128)(2,1)}, bf16[1024,3072]{1,0:T(8,128)(2,1)}, bf16[1024,3072]{1,0:T(8,128)(2,1)}, f32[1024,768]{1,0:T(8,128)}) custom-call(f32[1024,768]{1,0:T(8,128)} %get-tuple-element.103.stream_ref.refs_2_, bf16[1024,768]{1,0:T(8,128)(2,1)} %get-tuple-element.108.attended_ref.refs_5_, ...), custom_call_target="tpu_custom_call" | custom-call | flops 10871635968 | bytes 35782656 | tf_op jit(solution)/shard_map/mlp_forward/pallas_call | solution.py:594
  156.5 0.7 copy.54.label_ref
  157.1 0.6 broadcast_in_dim.24.vector_ref
  157.8 9.4 %qkv_forward.1 = (bf16[1024,768]{1,0:T(8,128)(2,1)}, bf16[1024,2304]{1,0:T(8,128)(2,1)}) custom-call(f32[1024,768]{1,0:T(8,128)} %get-tuple-element.112.stream_ref.stream_in, bf16[768,2304]{1,0:T(8,128)(2,1)} %all-gather.4.cloned.1.call-done.weight_ref, f32[1,9984]{1,0:T(1,128)} %get-tuple-element.114.vector_ref), custom_call_target="tpu_custom_call" | custom-call | flops 3623878656 | bytes 14548992 | tf_op jit(solution)/shard_map/qkv_forward/pallas_call | solution.py:594
  167.1 39.0 %attention_forward.3 = (bf16[1024,768]{1,0:T(8,128)(2,1)}, bf16[12,1024,1024]{2,1,0:T(8,128)(2,1)}, f32[1024,768]{1,0:T(8,128)}, bf16[8,480,768]{2,1,0:T(8,128)(2,1)}) custom-call(bf16[1024,2304]{1,0:T(8,128)(2,1)} %get-tuple-element.115.refs_0_.refs_1_.refs_2_, bf16[1024,2304]{1,0:T(8,128)(2,1)} %get-tuple-element.115.refs_0_.refs_1_.refs_2_, ...), custom_call_target="tpu_custom_call" | custom-call | flops 12884901888 | bytes 34603008 | tf_op jit(solution)/shard_map/attention_forward/pallas_call | solution.py:594
  206.1 0.0 all-gather.6.cloned.1.call-done.up_ref
  206.1 21.2 %mlp_forward.3 = (f32[1024,768]{1,0:T(8,128)}, bf16[1024,768]{1,0:T(8,128)(2,1)}, bf16[1024,3072]{1,0:T(8,128)(2,1)}, bf16[1024,3072]{1,0:T(8,128)(2,1)}, f32[1024,768]{1,0:T(8,128)}) custom-call(f32[1024,768]{1,0:T(8,128)} %get-tuple-element.112.stream_ref.stream_in, bf16[1024,768]{1,0:T(8,128)(2,1)} %get-tuple-element.119.attended_ref.refs_5_, ...), custom_call_target="tpu_custom_call" | custom-call | flops 10871635968 | bytes 35782656 | tf_op jit(solution)/shard_map/mlp_forward/pallas_call | solution.py:594
  227.4 1.8 all-gather.8.cloned.1.call-done.weight_ref
  229.2 10.8 %head.1 = (f32[1024,768]{1,0:T(8,128)}, bf16[768,1024]{1,0:T(8,128)(2,1)}, f32[1,1536]{1,0:T(1,128)}, f32[1,1024]{1,0:T(1,128)}, f32[1,2]{1,0:T(1,128)}) custom-call(f32[1024,768]{1,0:T(8,128)} %get-tuple-element.122.stream_ref, s32[1024,1]{1,0:T(8,128)} %copy.50.refs_6_.refs_3_.seg_col_ref, s32[1,1024]{1,0:T(1,128)} %bitcast.67, s32[8,1]{1,0:T(8,128)} %copy.54.label_ref, ...), custom_call_target="tpu_custom_call" | custom-call | tf_op jit(solution)/shard_map/head/pallas_call | solution.py:2176
  239.9 35.3 %mlp_backward.2 = (f32[1024,768]{1,0:T(8,128)}, bf16[1024,768]{1,0:T(8,128)(2,1)}, f32[1,6144]{1,0:T(1,128)}, bf16[768,3072]{1,0:T(8,128)(2,1)}, bf16[3840,768]{1,0:T(8,128)(2,1)}) custom-call(f32[1024,768]{1,0:T(8,128)} %get-tuple-element.124.grad_ref, bf16[1024,3072]{1,0:T(8,128)(2,1)} %get-tuple-element.125.slope_ref, ...), custom_call_target="tpu_custom_call" | custom-call | tf_op jit(solution)/shard_map/mlp_backward/pallas_call | solution.py:594
  275.3 41.6 %attention_backward.2 = (bf16[1024,2304]{1,0:T(8,128)(2,1)}, bf16[4,240,384]{2,1,0:T(8,128)(2,1)}) custom-call(bf16[1024,2304]{1,0:T(8,128)(2,1)} %get-tuple-element.115.refs_0_.refs_1_.refs_2_, bf16[1024,2304]{1,0:T(8,128)(2,1)} %get-tuple-element.115.refs_0_.refs_1_.refs_2_, bf16[1024,2304]{1,0:T(8,128)(2,1)} %get-tuple-element.115.refs_0_.refs_1_.refs_2_, ...), custom_call_target="tpu_custom_call" | custom-call | tf_op jit(solution)/shard_map/attention_backward/pallas_call | solution.py:594
  316.9 15.2 %qkv_backward.2 = (f32[1024,768]{1,0:T(8,128)}, f32[1,3840]{1,0:T(1,128)}, bf16[768,2304]{1,0:T(8,128)(2,1)}) custom-call(bf16[1024,2304]{1,0:T(8,128)(2,1)} %get-tuple-element.131.grad_ref, f32[1024,768]{1,0:T(8,128)} %get-tuple-element.132.residual_in, f32[1024,768]{1,0:T(8,128)} %get-tuple-element.112.stream_ref.stream_in, ...), custom_call_target="tpu_custom_call" | custom-call | tf_op jit(solution)/shard_map/qkv_backward/pallas_call | solution.py:594
  332.1 0.0 reduce-scatter.4.cloned.1.call-update
  332.1 0.0 reduce-scatter.6.cloned.1.call-start
  332.2 0.5 reduce-scatter.6.cloned.1.call-update
  332.7 0.0 reduce-scatter.8.cloned.1.call-start
  332.8 57.7 %mlp_backward.3 = (f32[1024,768]{1,0:T(8,128)}, bf16[1024,768]{1,0:T(8,128)(2,1)}, f32[1,6144]{1,0:T(1,128)}, bf16[768,3072]{1,0:T(8,128)(2,1)}, bf16[3840,768]{...) custom-call(f32[1024,768]{1,0:T(8,128)} %get-tuple-element.137.refs_0_, ...), custom_call_target="tpu_custom_call" | custom-call | tf_op jit(solution)/shard_map/mlp_backward/pallas_call | solution.py:594
  390.5 35.6 %attention_backward.3 = (bf16[1024,2304]{1,0:T(8,128)(2,1)}, bf16[4,48,1536]{2,1,0:T(8,128)(2,1)}) custom-call(bf16[1024,2304]{1,0:T(8,128)(2,1)} %get-tuple-element.104.refs_0_.refs_1_.refs_2_, bf16[1024,2304]{1,0:T(8,128)(2,1)} %get-tuple-element.104.refs_0_.refs_1_.refs_2_, bf16[1024,2304]{1,0:T(8,128)(2,1)} %get-tuple-element.104.refs_0_.refs_1_.refs_2_, ...), custom_call_target="tpu_custom_call" | custom-call | tf_op jit(solution)/shard_map/attention_backward/pallas_call | solution.py:594
  426.1 36.7 %qkv_backward.3 = (f32[1024,768]{1,0:T(8,128)}, f32[1,3840]{1,0:T(1,128)}, bf16[768,2304]{1,0:T(8,128)(2,1)}, bf16[96,3072]{1,0:T(8,128)(2,1)}) custom-call(bf16[1024,2304]{1,0:T(8,128)(2,1)} %get-tuple-element.152.refs_0_, f32[1024,768]{1,0:T(8,128)} %get-tuple-element.153.refs_1_, f32[1024,768]{1,0:T(8,128)} %get-tuple-element.103.stream_ref.refs_2_, ...), custom_call_target="tpu_custom_call" | custom-call | tf_op jit(solution)/shard_map/qkv_backward/pallas_call | solution.py:594
  462.8 0.7 slice_reduce_fusion.3
  463.5 0.7 slice_reduce_fusion.6
  464.3 0.1 stack.27
  464.6 0.1 stack.28
  464.8 0.1 maximum_bitcast_fusion.2
  464.8 0.1 reshape.130
  465.0 12.1 %embed_backward.1 = (bf16[3072,768]{1,0:T(8,128)(2,1)}, f32[64,768]{1,0:T(8,128)}, f32[1,768]{1,0:T(1,128)}) custom-call(bf16[1024,3072]{1,0:T(8,128)(2,1)} %pixel_ref.1, f32[1024,768]{1,0:T(8,128)} %get-tuple-element.159.grad_ref, f32[64,1024]{1,0:T(8,128)} %get-tuple-element.160.pos_ref), custom_call_target="tpu_custom_call" | custom-call | tf_op jit(solution)/shard_map/embed_backward/pallas_call | solution.py:594
  477.1 0.7 reduce.8
  477.8 0.9 slice.70
  478.8 0.1 concatenate.21
  479.0 0.7 pad.19.refs_2_
  479.8 82.9 %reduce_gradients.1 = (bf16[96,2304]{1,0:T(8,128)(2,1)}, bf16[384,768]{1,0:T(8,128)(2,1)}, f32[64,128]{1,0:T(8,128)}, bf16[96,2304]{1,0:T(8,128)(2,1)}, bf16[96,3072]{1,0:T(8,128)(2,1)}) custom-call(bf16[8,96,2304]{2,1,0:T(8,128)(2,1)} %bitcast.55, bf16[8,384,768]{2,1,0:T(8,128)(2,1)} %bitcast.52, f32[8,64,128]{2,1,0:T(8,128)} %pad.19.refs_2_, ...), custom_call_target="tpu_custom_call" | custom-call | tf_op jit(solution)/shard_map/reduce_gradients/pallas_call | solution.py:1475
  562.6 0.7 slice_bitcast_fusion
  563.3 1.3 maximum_bitcast_fusion.1
  564.6 1.1 maximum_bitcast_fusion
  565.7 0.0 reduce-scatter.8.cloned.1.call-done
  565.8 33.7 %finish_gradients.1 = (bf16[480,768]{1,0:T(8,128)(2,1)}, f32[8,64,128]{2,1,0:T(8,128)}, f32[1,128]{1,0:T(1,128)}) custom-call(bf16[96,1024]{1,0:T(8,128)(2,1)} %get-tuple-element.144.refs_0_, bf16[480,768]{1,0:T(8,128)(2,1)} %get-tuple-element.145.refs_1_, bf16[96,3072]{1,0:T(8,128)(2,1)} %get-tuple-element.157.refs_2_, ...), custom_call_target="tpu_custom_call" | custom-call | tf_op jit(solution)/shard_map/finish_gradients/pallas_call | solution.py:1547
  599.5 1.4 fusion.15
  600.9 0.5 slice_multiply_fusion.2
  601.5 0.1 mul.216
  601.6 0.9 slice.79
  602.5 0.7 copy-done.13
  603.2 1.2 slice_multiply_fusion
  604.4 1.6 mul.221
  606.0 2.0 multiply_subtract_fusion.5
  608.1 3.1 multiply_subtract_fusion.3
  611.2 4.8 multiply_subtract_fusion.2
  616.0 0.6 multiply_subtract_fusion.6
  616.7 1.9 multiply_subtract_fusion.4
  618.7 6.7 %multiply_subtract_fusion.1 = (f32[2,480,768]{2,1,0:T(8,128)}, f32[2,480,768]{2,1,0:T(8,128)}, f32[2,480,768]{2,1,0:T(8,128)}) fusion(f32[2,480,768]{2,1,0:T(8,128)S(1)} %copy-done.1, f32[]{:T(128)} %bitcast.25, bf16[1,480,768]{2,1,0:T(8,128)(2,1)S(1)} %bitcast.56, bf16[1,480,768]{2,1,0:T(8,128)(2,1)} %bitcast.59, f32[2,480,768]{2,1,0:T(8,128)S(1)} %copy-done.5, ...), kind=kLoop, calls=%fused_computation.8 | loop fusion | flops 12533760 | bytes 19169284 | tf_op jit(solution)/shard_map/sub | solution.py:2200
  625.4 6.8 %multiply_subtract_fusion = (f32[2,96,5376]{2,1,0:T(8,128)}, f32[2,96,5376]{2,1,0:T(8,128)}, f32[2,96,5376]{2,1,0:T(8,128)}) fusion(f32[2,96,5376]{2,1,0:T(8,128)S(1)} %copy-done, f32[]{:T(128)} %bitcast.25, bf16[1,96,5376]{2,1,0:T(8,128)(2,1)S(1)} %maximum_bitcast_fusion.1, bf16[1,96,5376]{2,1,0:T(8,128)(2,1)S(1)} %maximum_bitcast_fusion, ...), kind=kLoop, calls=%fused_computation.5 | loop fusion | flops 17547264 | bytes 26836996 | tf_op jit(solution)/shard_map/sub | solution.py:2200
  (71 shorter events, 0.5 us)
Async XLA Ops:
  7.2 150.6 %all-gather.4.cloned.1.call-start = ((), (), s32[]{:S(2)}) async-start(), calls=%async_computation.3 | async-start | bytes 3981312 | tf_op jit(solution)/shard_map/all_gather | solution.py:2246
  97.0 109.2 %all-gather.6.cloned.1.call-start = ((), (), s32[]{:S(2)}) async-start(), calls=%async_computation.4 | async-start | bytes 5308416 | tf_op jit(solution)/shard_map/all_gather | solution.py:2246
  97.7 131.5 %all-gather.8.cloned.1.call-start = ((), (), s32[]{:S(2)}) async-start(), calls=%async_computation.5 | async-start | bytes 1769472 | tf_op jit(solution)/shard_map/all_gather | solution.py:2246
  98.5 381.3 %reduce-scatter.4.cloned.1.call-start = ((), (), s32[]{:S(2)}) async-start(), calls=%async_computation.6 | async-start | bytes 3981312 | tf_op jit(solution)/shard_map/reduce_scatter | solution.py:1585
  135.4 21.1 %copy-start.26 = (s32[1,8]{1,0:T(1,128)S(1)}, s32[1,8]{1,0:T(1,128)}, u32[]{:S(2)}) copy-start(s32[1,8]{1,0:T(1,128)} %param.28) | copy-start | bytes 100
  135.4 21.8 %copy-start.14 = (f32[3304]{0:T(1024)S(1)}, f32[3304]{0:T(1024)}, u32[]{:S(2)}) copy-start(f32[3304]{0:T(1024)} %param.35) | copy-start | bytes 39652
  332.1 147.6 %reduce-scatter.6.cloned.1.call-start = ((), (), s32[]{:S(2)}) async-start(), calls=%async_computation.7 | async-start | bytes 5308416 | tf_op jit(solution)/shard_map/reduce_scatter | solution.py:1585
  332.7 233.0 %reduce-scatter.8.cloned.1.call-start = ((), (), s32[]{:S(2)}) async-start(), calls=%async_computation.8 | async-start | bytes 6635520 | tf_op jit(solution)/shard_map/reduce_scatter | solution.py:1585
  426.0 37.5 %copy-start.17 = (f32[1,6144]{1,0:T(1,128)S(1)}, f32[1,6144]{1,0:T(1,128)}, u32[]{:S(2)}) copy-start(f32[1,6144]{1,0:T(1,128)} %get-tuple-element.163) | copy-start | bytes 73732
  426.0 38.4 %copy-start.20 = (f32[1,3840]{1,0:T(1,128)S(1)}, f32[1,3840]{1,0:T(1,128)}, u32[]{:S(2)}) copy-start(f32[1,3840]{1,0:T(1,128)} %get-tuple-element.164) | copy-start | bytes 46084
  426.0 38.5 %copy-start.16 = (f32[1,6144]{1,0:T(1,128)S(1)}, f32[1,6144]{1,0:T(1,128)}, u32[]{:S(2)}) copy-start(f32[1,6144]{1,0:T(1,128)} %get-tuple-element.165) | copy-start | bytes 73732
  426.1 38.9 %copy-start.23 = (f32[1,1536]{1,0:T(1,128)S(1)}, f32[1,1536]{1,0:T(1,128)}, u32[]{:S(2)}) copy-start(f32[1,1536]{1,0:T(1,128)} %get-tuple-element.168) | copy-start | bytes 18436
  465.0 13.8 %copy-start.24 = (f32[1,1024]{1,0:T(1,128)S(1)}, f32[1,1024]{1,0:T(1,128)}, u32[]{:S(2)}) copy-start(f32[1,1024]{1,0:T(1,128)} %get-tuple-element.169) | copy-start | bytes 12292
  465.0 13.8 %copy-start.25 = (f32[1,2]{1,0:T(1,128)S(1)}, f32[1,2]{1,0:T(1,128)}, u32[]{:S(2)}) copy-start(f32[1,2]{1,0:T(1,128)} %get-tuple-element.170) | copy-start | bytes 28
  479.8 84.8 %copy-start.8 = (bf16[96,3072]{1,0:T(8,128)(2,1)S(1)}, bf16[96,3072]{1,0:T(8,128)(2,1)}, u32[]{:S(2)}) copy-start(bf16[96,3072]{1,0:T(8,128)(2,1)} %get-tuple-element.157.refs_2_) | copy-start | bytes 1769476
  565.7 40.3 %copy-start.18 = (f32[3304]{0:T(1024)S(1)}, f32[3304]{0:T(1024)}, u32[]{:S(2)}) copy-start(f32[3304]{0:T(1024)} %param.49) | copy-start | bytes 39652
  565.7 40.3 %copy-start.19 = (f32[3304]{0:T(1024)S(1)}, f32[3304]{0:T(1024)}, u32[]{:S(2)}) copy-start(f32[3304]{0:T(1024)} %param.42) | copy-start | bytes 39652
  565.7 42.3 %copy-start.11 = (bf16[96,1024]{1,0:T(8,128)(2,1)S(1)}, bf16[96,1024]{1,0:T(8,128)(2,1)}, u32[]{:S(2)}) copy-start(bf16[96,1024]{1,0:T(8,128)(2,1)} %get-tuple-element.144.refs_0_) | copy-start | bytes 589828
  565.8 45.4 %copy-start.2 = (f32[384,768]{1,0:T(8,128)S(1)}, f32[384,768]{1,0:T(8,128)}, u32[]{:S(2)}) copy-start(f32[384,768]{1,0:T(8,128)} %refs_0_.1) | copy-start | bytes 3538948
  565.8 50.3 %copy-start.15 = (f32[2,1248]{1,0:T(2,128)S(1)}, f32[2,1248]{1,0:T(2,128)}, u32[]{:S(2)}) copy-start(f32[2,1248]{1,0:T(2,128)} %param.33) | copy-start | bytes 29956
  565.8 50.3 %copy-start.21 = (f32[2,1248]{1,0:T(2,128)S(1)}, f32[2,1248]{1,0:T(2,128)}, u32[]{:S(2)}) copy-start(f32[2,1248]{1,0:T(2,128)} %param.47) | copy-start | bytes 29956
  565.8 50.2 %copy-start.22 = (f32[2,1248]{1,0:T(2,128)S(1)}, f32[2,1248]{1,0:T(2,128)}, u32[]{:S(2)}) copy-start(f32[2,1248]{1,0:T(2,128)} %param.40) | copy-start | bytes 29956
  602.5 0.7 copy-start.13
  606.0 5.1 copy-start.9
  606.0 5.1 copy-start.10
  608.1 8.6 %copy-start.12 = (f32[49,768]{1,0:T(8,128)S(1)}, f32[49,768]{1,0:T(8,128)}, u32[]{:S(2)}) copy-start(f32[49,768]{1,0:T(8,128)} %mul.221) | copy-start | bytes 451588
  608.1 10.6 %copy-start.7 = (bf16[480,768]{1,0:T(8,128)(2,1)S(1)}, bf16[480,768]{1,0:T(8,128)(2,1)}, u32[]{:S(2)}) copy-start(bf16[480,768]{1,0:T(8,128)(2,1)} %get-tuple-element.145.refs_1_) | copy-start | bytes 2211844
  611.2 7.5 %copy-start.1 = (f32[2,480,768]{2,1,0:T(8,128)S(1)}, f32[2,480,768]{2,1,0:T(8,128)}, u32[]{:S(2)}) copy-start(f32[2,480,768]{2,1,0:T(8,128)} %refs_3_.1) | copy-start | bytes 8847364
  611.2 7.5 %copy-start.5 = (f32[2,480,768]{2,1,0:T(8,128)S(1)}, f32[2,480,768]{2,1,0:T(8,128)}, u32[]{:S(2)}) copy-start(f32[2,480,768]{2,1,0:T(8,128)} %param.46) | copy-start | bytes 8847364
  611.2 7.4 %copy-start.6 = (f32[2,480,768]{2,1,0:T(8,128)S(1)}, f32[2,480,768]{2,1,0:T(8,128)}, u32[]{:S(2)}) copy-start(f32[2,480,768]{2,1,0:T(8,128)} %param.39) | copy-start | bytes 8847364
  618.7 6.7 %copy-start = (f32[2,96,5376]{2,1,0:T(8,128)S(1)}, f32[2,96,5376]{2,1,0:T(8,128)}, u32[]{:S(2)}) copy-start(f32[2,96,5376]{2,1,0:T(8,128)} %refs_2_.1) | copy-start | bytes 12386308
  618.7 6.7 %copy-start.3 = (f32[2,96,5376]{2,1,0:T(8,128)S(1)}, f32[2,96,5376]{2,1,0:T(8,128)}, u32[]{:S(2)}) copy-start(f32[2,96,5376]{2,1,0:T(8,128)} %param.45) | copy-start | bytes 12386308
  618.7 6.7 %copy-start.4 = (f32[2,96,5376]{2,1,0:T(8,128)S(1)}, f32[2,96,5376]{2,1,0:T(8,128)}, u32[]{:S(2)}) copy-start(f32[2,96,5376]{2,1,0:T(8,128)} %param.38) | copy-start | bytes 12386308
Sparse Core Ops, SparseCore 0:
  97.1 54.8 all-gather.3
  153.6 49.9 all-gather.5
  205.3 23.8 all-gather.7
  332.2 58.4 reduce-scatter.3
  393.0 67.7 reduce-scatter.5
  463.0 67.2 reduce-scatter.7

commit v13 on v12

--- a/solution.py
+++ b/solution.py
@@ -709,25 +709,24 @@
 
     add_block(mine)
     patch_job.second()
+    qkv_job.second()
     vector_job.second()
-    qkv_job.second()
-    up_job.second()
     patch_job.core_copy(0).wait_recv()
     use(0, False)
     copies[3].wait()
     qkv_one[...] = wide_inputs[1, :, : 3 * D].astype(LOW)
     up_one[...] = wide_inputs[1, :, 3 * D :].astype(LOW)
+    patch_job.relay()
     copies[5].wait()
     output_one[...] = wide_outputs[1].astype(LOW)
     copies[6].wait()
     head_low[...] = jnp.zeros_like(head_low)
     head_low[:, : head.shape[1]] = wide_head[...].astype(LOW)
-    patch_job.relay()
+    patch_job.third(use)
     qkv_job.relay()
-    patch_job.third(use)
-    up_job.relay()
+    up_job.second()
+    patch_job.fourth(use)
     qkv_job.third()
-    patch_job.fourth(use)
     vector_job.third()
     vector_job.fourth()
     blocks = [vectors_full[slot].astype(jnp.float32) for slot in range(vectors_full.shape[0])]
@@ -740,6 +739,7 @@
                 if 0 <= row - spot < span
             ]
             out[:, row * LANES : (row + 1) * LANES] = sum(parts)
+    up_job.relay()
     up_job.third()
     qkv_job.fourth()
     copy = pltpu.make_async_copy(qkv_landing, qkv_full, load_sems.at[0])
@@ -1428,10 +1428,11 @@
     ]
 
 
-def reduce_kernel(*refs, whole, partly):
+def reduce_kernel(*refs, whole, partly, done, vector_rows, rest_size):
     count = whole + 1 + partly
-    grads, outs, refs = refs[:count], refs[count : 2 * count], refs[2 * count :]
-    sems, small_sems, group_sems, refs = refs[0], refs[1], refs[2], refs[3:]
+    finished, grads, refs = refs[:done], refs[done : done + count], refs[done + count :]
+    outs, full, numbers, refs = refs[:count], refs[count], refs[count + 1], refs[count + 2 :]
+    sems, small_sems, group_sems, spread_sems, refs = *refs[:4], refs[4:]
     jobs = [
         Whole(grads[i], outs[i], refs[8 * i : 8 * i + 8], sems.at[i]) for i in range(whole)
     ]
@@ -1451,39 +1452,58 @@
     run_stages([small, *shares], STAGES[3:4])
     run_stages(jobs, STAGES[3:4])
     run_stages([small, *jobs], STAGES[4:5])
-    run_stages([*shares, small, *jobs], STAGES[5:])
+    run_stages([*shares, small, *jobs], STAGES[5:6])
+    total = sum(squares_in(out) for out in (*finished, *outs[:whole], *outs[whole + 1 :]))
+    _, level, core = place()
+    mine = 2 * level + core
+    block = outs[whole]
+    last = block.shape[0] - 1
+    full[mine] = block[...]
+    full[mine, last : last + 1, :] = total
+    Spread(full, spread_sems).run()
+    numbers[...] = totals(full[...], vector_rows, rest_size)
+    run_stages([*shares, small, *jobs], STAGES[6:])
 
 
 def transfer_outs(arrays):
     return [jax.ShapeDtypeStruct(array.shape[-2:], array.dtype) for array in arrays]
 
 
-def reduce_call(grads, small, shares, collective_id):
+def reduce_call(grads, small, shares, finished, vector_rows, rest_size, collective_id):
     in_vmem = pl.BlockSpec(memory_space=pltpu.VMEM)
-    whole, partly = len(grads), len(shares)
+    whole, partly, done = len(grads), len(shares), len(finished)
     operands = [*grads, small, *shares]
     scratch = [
         pltpu.SemaphoreType.DMA((whole, WHOLE_SEMS)),
         pltpu.SemaphoreType.DMA((REDUCE_SEMS,)),
         pltpu.SemaphoreType.DMA((partly, GROUP_SEMS)),
+        pltpu.SemaphoreType.DMA((14,)),
     ]
     for grad in grads:
         scratch.extend(stepped_scratch(grad))
     scratch.extend(whole_scratch(small))
     for share in shares:
         scratch.extend(share_scratch(share))
+    out_shape = [*transfer_outs(operands), shape_of(*small.shape), shape_of(1, LANES)]
     return pl.pallas_call(
-        functools.partial(reduce_kernel, whole=whole, partly=partly),
-        in_specs=[ANYWHERE] * len(operands),
-        out_specs=[in_vmem] * len(operands),
-        out_shape=transfer_outs(operands),
+        functools.partial(
+            reduce_kernel,
+            whole=whole,
+            partly=partly,
+            done=done,
+            vector_rows=vector_rows,
+            rest_size=rest_size,
+        ),
+        in_specs=[in_vmem] * done + [ANYWHERE] * len(operands),
+        out_specs=[in_vmem] * len(out_shape),
+        out_shape=out_shape,
         scratch_shapes=scratch,
         compiler_params=pltpu.CompilerParams(
             collective_id=collective_id, has_side_effects=True, vmem_limit_bytes=VMEM_LIMIT
         ),
         cost_estimate=NO_COST,
         name="reduce_gradients",
-    )(*operands)
+    )(*finished, *operands)
 
 
 def totals(full, vector_rows, rest_size):
@@ -1509,76 +1529,20 @@
     )
 
 
-def finish_kernel(*refs, done, partly, vector_rows, rest_size):
-    finished, small, refs = refs[:done], refs[done], refs[done + 1 :]
-    shares, refs = refs[:partly], refs[partly:]
-    outs, full, numbers, refs = refs[:partly], refs[partly], refs[partly + 1], refs[partly + 2 :]
-    group_sems, spread_sems, refs = refs[0], refs[1], refs[2:]
-    jobs = [
-        GroupReduce(shares[i], outs[i], refs[2 * i : 2 * i + 2], group_sems.at[i])
-        for i in range(partly)
-    ]
-    greet()
-    run_stages(jobs, STAGES[:2])
-    total = sum(squares_in(out) for out in finished)
-    run_stages(jobs, STAGES[3:6])
-    total = total + sum(squares_in(out) for out in outs)
-    _, level, core = place()
-    mine = 2 * level + core
-    last = small.shape[0] - 1
-    full[mine] = small[...]
-    full[mine, last : last + 1, :] = total
-    Spread(full, spread_sems).run()
-    numbers[...] = totals(full[...], vector_rows, rest_size)
-    run_stages(jobs, STAGES[6:])
-
-
-def finish_call(finished, small, shares, vector_rows, rest_size, collective_id):
-    done, partly = len(finished), len(shares)
-    in_vmem = pl.BlockSpec(memory_space=pltpu.VMEM)
-    scratch = [
-        pltpu.SemaphoreType.DMA((partly, GROUP_SEMS)),
-        pltpu.SemaphoreType.DMA((14,)),
-    ]
-    for share in shares:
-        scratch.extend(share_scratch(share))
-    full = (lax.axis_size("fsdp"), *small.shape)
-    out_shape = [*transfer_outs(shares), jax.ShapeDtypeStruct(full, small.dtype), shape_of(1, LANES)]
-    return pl.pallas_call(
-        functools.partial(
-            finish_kernel, done=done, partly=partly, vector_rows=vector_rows, rest_size=rest_size
-        ),
-        in_specs=[in_vmem] * (done + 1) + [ANYWHERE] * partly,
-        out_specs=[in_vmem] * len(out_shape),
-        out_shape=out_shape,
-        scratch_shapes=scratch,
-        compiler_params=pltpu.CompilerParams(
-            collective_id=collective_id, has_side_effects=True, vmem_limit_bytes=VMEM_LIMIT
-        ),
-        name="finish_gradients",
-    )(*finished, small, *shares)
-
-
 def with_kernels():
     return lax.axis_size("dp") == 4 and lax.axis_size("fsdp") == 8
 
 
-def reduce_all(grads, small, shares, collective_id):
+def reduce_all(grads, small, shares, finished, vector_rows, rest_size, collective_id):
     if with_kernels():
-        return reduce_call(grads, small, shares, collective_id)
-    return [lax.psum(scatter(grad), "dp") for grad in (*grads, small)] + [
-        lax.psum(share, "dp") for share in shares
-    ]
-
-
-def finish_all(finished, small, shares, vector_rows, rest_size, collective_id):
-    if with_kernels():
-        return finish_call(finished, small, shares, vector_rows, rest_size, collective_id)
+        return reduce_call(grads, small, shares, finished, vector_rows, rest_size, collective_id)
+    sums = [lax.psum(scatter(grad), "dp") for grad in grads]
+    block = lax.psum(scatter(small), "dp")
     outs = [lax.psum(share, "dp") for share in shares]
-    total = sum(jnp.sum(jnp.square(out.astype(jnp.float32))) for out in (*finished, *outs))
+    total = sum(jnp.sum(jnp.square(out.astype(jnp.float32))) for out in (*finished, *sums, *outs))
     row = jnp.full((1, LANES), 1.0 / LANES, jnp.float32) * total
-    full = lax.all_gather(small.at[-1:].set(row), "fsdp", axis=0)
-    return [*outs, full, totals(full, vector_rows, rest_size)]
+    full = lax.all_gather(block.at[-1:].set(row), "fsdp", axis=0)
+    return [*sums, block, *outs, full, totals(full, vector_rows, rest_size)]
 
 
 def scatter(grad):
@@ -1926,9 +1890,10 @@
 
 def mlp_back_kernel(
     grad_ref, slope_ref, residual_in, normed_ref, active_ref, attended_ref, mix_ref, up_ref, down_ref, vector_ref,
-    out_ref, attended_grad_ref, sums_ref, up_grad_ref, output_grad,
-    residual_ref, low_ref, second_ref, turned_ref, hidden_ref, product_ref, sems,
+    out_ref, attended_grad_ref, sums_ref, output_grad, *refs,
 ):
+    up_grads, scratch = refs[:-7], refs[-7:]
+    residual_ref, low_ref, second_ref, turned_ref, hidden_ref, product_ref, sems = scratch
     rows = grad_ref.shape[0]
     step = pl.program_id(0)
     load = pltpu.make_async_copy(residual_in, residual_ref, sems.at[0])
@@ -1964,7 +1929,13 @@
         active_grad = following
     sums_ref[:, chunk_at(4 * D)] = hidden_sum
     store(step + 1, mul(active_ref[...].T, low_ref[...]))
-    up_grad_ref[...] = mul(turned_ref[...], hidden_ref[...]).astype(LOW)
+    up_grad = mul(turned_ref[...], hidden_ref[...]).astype(LOW)
+    share = pl.num_programs(0) // len(up_grads)
+    for index, part in enumerate(up_grads):
+
+        @pl.when(lax.div(step, share) == index)
+        def _(part=part):
+            part[...] = up_grad
 
     @at_last
     def _():
@@ -1990,11 +1961,13 @@
 
 
 def mlp_backward(
-    grad, slope, residual, normed, active, attended, up, proj_out, vector, rides, collective_id
+    grad, slope, residual, normed, active, attended, up, proj_out, vector, parts, rides, collective_id
 ):
     rows = grad.shape[0]
     width = up.shape[1]
     steps = width // D
+    share = steps // parts
+    part_of = lambda index: lambda i: (0, jnp.clip(i - index * share, 0, share - 1))
     whole = fixed(rows, D)
     weight_specs, weights = mlp_specs(up, proj_out)
     return block_call(
@@ -2011,13 +1984,13 @@
             fixed(1, vector.shape[1]),
         ],
         [grad, slope, residual, normed, active, attended, *weights, vector],
-        [whole, whole, fixed(1, 4 * D + width), columns_of(D), ANYWHERE],
+        [whole, whole, fixed(1, 4 * D + width), ANYWHERE, *[pl.BlockSpec((D, D), part_of(index)) for index in range(parts)]],
         [
             shape_of(rows, D),
             shape_of(rows, D, dtype=LOW),
             shape_of(1, 4 * D + width),
-            shape_of(D, width, dtype=LOW),
             shape_of(D + width, D, dtype=LOW),
+            *[shape_of(D, width // parts, dtype=LOW)] * parts,
         ],
         [
             pltpu.VMEM((rows, D), jnp.float32),
@@ -2279,7 +2252,7 @@
         (qkv_weight, up, output, vector), first, second = saved_layers[index]
         entering, normed, qkv_rows, attended, expo, inverse = first
         residual, normed_second, active, slope = second
-        residual_grad, attended_grad, mlp_sums, up_grad, output_grad, *brought = mlp_backward(
+        residual_grad, attended_grad, mlp_sums, output_grad, *brought = mlp_backward(
             stream_grad,
             slope,
             residual,
@@ -2289,13 +2262,17 @@
             up,
             output,
             vector,
+            2 if index else 1,
             () if index else [output_rest, SumRide(by_owner(head_grad), False)],
             9,
         )
-        if index == 0:
-            output_one_sum, head_sum = brought
+        if index:
+            attended_grad, *up_parts = lax.optimization_barrier((attended_grad, *brought))
+            late_parts = [scatter(by_owner(part)) for part in up_parts]
+        else:
+            up_grad, output_one_sum, head_sum = brought
             attended_grad, output_grad = lax.optimization_barrier((attended_grad, output_grad))
-            last_part = scatter(by_owner(output_grad))
+            late_parts.append(scatter(by_owner(output_grad)))
         qkv_grad, rest = attention_backward(
             qkv_rows,
             expo,
@@ -2317,10 +2294,8 @@
         )
         if index:
             output_rest = rest
-            stream_grad, qkv_weight_grad, up_grad = lax.optimization_barrier(
-                (stream_grad, qkv_weight_grad, up_grad)
-            )
-            late_parts = [scatter(by_owner(grad)) for grad in (qkv_weight_grad, up_grad)]
+            stream_grad, qkv_weight_grad = lax.optimization_barrier((stream_grad, qkv_weight_grad))
+            late_parts.append(scatter(by_owner(qkv_weight_grad)))
         else:
             (up_zero_sum,) = brought
         vector_grads[index] = jnp.concatenate(
@@ -2352,16 +2327,23 @@
     used = vector_rows + rest_rows
     block_rows = (used // 64 + 1) * 64
     small = jnp.pad(small.reshape(owners, used, LANES), ((0, 0), (0, block_rows - used), (0, 0)))
-    qkv_zero_sum, kernel_sum, small_share, *input_one_sums = reduce_all(
-        [by_owner(qkv_weight_grad), by_owner(kernel_grad)], small, late_parts, 2
-    )
-    output_zero_sum, small_full, numbers = finish_all(
-        [head_sum, output_one_sum, up_zero_sum, qkv_zero_sum, kernel_sum, *input_one_sums],
+    (
+        qkv_zero_sum,
+        kernel_sum,
         small_share,
-        [last_part],
+        *up_one_sums,
+        qkv_one_sum,
+        output_zero_sum,
+        small_full,
+        numbers,
+    ) = reduce_all(
+        [by_owner(qkv_weight_grad), by_owner(kernel_grad)],
+        small,
+        late_parts,
+        [head_sum, output_one_sum, up_zero_sum],
         vector_rows,
         rest.shape[0],
-        3,
+        2,
     )
     factor, grad_norm, loss_sum, token_total = (numbers[0, index] for index in range(4))
     rest_sum = small_full[:, vector_rows:used].reshape(-1)
@@ -2370,7 +2352,10 @@
     kernel_sum = kernel_sum.astype(jnp.float32)
     head_sum = head_sum[:, :CLS].astype(jnp.float32)
     input_sum = jnp.stack(
-        [jnp.concatenate(pair, 1) for pair in ((qkv_zero_sum, up_zero_sum), input_one_sums)]
+        [
+            jnp.concatenate(parts, 1)
+            for parts in ((qkv_zero_sum, up_zero_sum), (qkv_one_sum, *up_one_sums))
+        ]
     ).astype(jnp.float32)
     output_sum = jnp.stack([output_zero_sum, output_one_sum]).astype(
         jnp.float32

time: 648 us -> 640 us (0.988)
  Pallas kernels: 574 us -> 567 us
    pallas_call x1 -> x0, Pallas kernels: 33.7 us -> none  [finish_call(): pl.pallas_call(functools.partial(finish_kernel, done=done, partly=partly,...]
    pallas_call x1, Pallas kernels: 82.9 us -> 110 us  [reduce_call(): pl.pallas_call(functools.partial(reduce_kernel, whole=whole, partly=partl...]
  transfers between devices with their start and end apart: 6 -> 7, of which waited for: 1 -> 1; matrix products, arithmetic and copies ran while one was open for 1% -> 1% of each run, Pallas kernels for 55% -> 52%
where the time goes in v13:
time: 640 us; the launch traced here: 631 us
  Pallas kernels  567 us (89%)
  other arithmetic  26.9 us (4%)
  between operations  15.2 us (2%)
  local copies, waits for them, and re-layouts  14.5 us (2%)
  waiting for transfers between devices  7.15 us (1%)
    pallas_call x12, Pallas kernels, block_call(): pl.pallas_call(kernel, grid=(grid,), in_specs=in_specs, out_specs=out_spe...  366 us
    pallas_call x1, Pallas kernels, reduce_call(): pl.pallas_call(functools.partial(reduce_kernel, whole=whole, partly=partl...  110 us
    pallas_call x1, Pallas kernels, begin(): pl.pallas_call(functools.partial(first_kernel, spots=spots), in_specs=[AN...  80.1 us
    sub x7, other arithmetic, adam_update(): return (moment, square, weight - learn_rate * step_dir)  21.6 us
  transfers between devices with their start and end apart: 7, of which 1 were waited for; matrix products, arithmetic and copies ran while one was open for 1% of the time, Pallas kernels for 52%

profile of v13, /device:TPU:0, one launch (start us, length us, event | category | flops | bytes accessed | tf_op | source)
XLA Modules:
  0.0 631.0 jit_solution(14397225399653748314)
XLA Ops:
  7.2 0.0 all-gather.4.cloned.1.call-start
  7.2 0.7 convert_element_type.23
  8.0 0.2 dynamic_update_slice.3
  8.2 0.6 reshape.122.refs_1_
  8.8 1.3 broadcast_in_dim.22.refs_9_
  10.2 1.7 copy.50.refs_6_.refs_3_.seg_col_ref
  11.9 80.1 %begin.1 = (f32[1024,768]{1,0:T(8,128)}, f32[64,1024]{1,0:T(8,128)}, f32[1,9984]{1,0:T(1,128)}, f32[1,9984]{1,0:T(1,128)}, bf16[8,96,2304]{2,1,0:T(8,128)(2,1)},...) custom-call(f32[384,768]{1,0:T(8,128)} %refs_0_.1, ...), custom_call_target="tpu_custom_call" | custom-call | tf_op jit(solution)/shard_map/begin/pallas_call | solution.py:832
  92.0 0.0 all-gather.6.cloned.1.call-start
  92.1 0.7 all-gather.6.cloned.1.call-update
  92.8 0.0 all-gather.8.cloned.1.call-start
  92.8 0.7 all-gather.8.cloned.1.call-update
  93.5 0.3 reduce-scatter.5.cloned.1.call-start
  93.8 34.1 %attention_forward.2 = (bf16[1024,768]{1,0:T(8,128)(2,1)}, bf16[12,1024,1024]{2,1,0:T(8,128)(2,1)}, f32[1024,768]{1,0:T(8,128)}, bf16[8,480,768]{2,1,0:T(8,128)(2,1)}, bf16[4,240,384]{2,1,0:T(8,128)(2,1)}) custom-call(bf16[1024,2304]{1,0:T(8,128)(2,1)} %get-tuple-element.108.refs_0_.refs_1_.refs_2_, ...), custom_call_target="tpu_custom_call" | custom-call | flops 12884901888 | bytes 34603008 | tf_op jit(solution)/shard_map/attention_forward/pallas_call | solution.py:594
  127.9 21.0 %mlp_forward.2 = (f32[1024,768]{1,0:T(8,128)}, bf16[1024,768]{1,0:T(8,128)(2,1)}, bf16[1024,3072]{1,0:T(8,128)(2,1)}, bf16[1024,3072]{1,0:T(8,128)(2,1)}, f32[1024,768]{1,0:T(8,128)}) custom-call(f32[1024,768]{1,0:T(8,128)} %get-tuple-element.107.stream_ref.refs_2_, bf16[1024,768]{1,0:T(8,128)(2,1)} %get-tuple-element.112.attended_ref.refs_5_, ...), custom_call_target="tpu_custom_call" | custom-call | flops 10871635968 | bytes 35782656 | tf_op jit(solution)/shard_map/mlp_forward/pallas_call | solution.py:594
  149.0 0.7 copy.54.label_ref
  149.7 0.6 broadcast_in_dim.24.vector_ref
  150.3 9.1 %qkv_forward.1 = (bf16[1024,768]{1,0:T(8,128)(2,1)}, bf16[1024,2304]{1,0:T(8,128)(2,1)}) custom-call(f32[1024,768]{1,0:T(8,128)} %get-tuple-element.116.stream_ref.stream_in, bf16[768,2304]{1,0:T(8,128)(2,1)} %all-gather.4.cloned.1.call-done.weight_ref, f32[1,9984]{1,0:T(1,128)} %get-tuple-element.118.vector_ref), custom_call_target="tpu_custom_call" | custom-call | flops 3623878656 | bytes 14548992 | tf_op jit(solution)/shard_map/qkv_forward/pallas_call | solution.py:594
  159.4 50.9 %attention_forward.3 = (bf16[1024,768]{1,0:T(8,128)(2,1)}, bf16[12,1024,1024]{2,1,0:T(8,128)(2,1)}, f32[1024,768]{1,0:T(8,128)}, bf16[8,480,768]{2,1,0:T(8,128)(2,1)}) custom-call(bf16[1024,2304]{1,0:T(8,128)(2,1)} %get-tuple-element.119.refs_0_.refs_1_.refs_2_, bf16[1024,2304]{1,0:T(8,128)(2,1)} %get-tuple-element.119.refs_0_.refs_1_.refs_2_, ...), custom_call_target="tpu_custom_call" | custom-call | flops 12884901888 | bytes 34603008 | tf_op jit(solution)/shard_map/attention_forward/pallas_call | solution.py:594
  210.3 0.0 all-gather.6.cloned.1.call-done.up_ref
  210.3 21.1 %mlp_forward.3 = (f32[1024,768]{1,0:T(8,128)}, bf16[1024,768]{1,0:T(8,128)(2,1)}, bf16[1024,3072]{1,0:T(8,128)(2,1)}, bf16[1024,3072]{1,0:T(8,128)(2,1)}, f32[1024,768]{1,0:T(8,128)}) custom-call(f32[1024,768]{1,0:T(8,128)} %get-tuple-element.116.stream_ref.stream_in, bf16[1024,768]{1,0:T(8,128)(2,1)} %get-tuple-element.123.attended_ref.refs_5_, ...), custom_call_target="tpu_custom_call" | custom-call | flops 10871635968 | bytes 35782656 | tf_op jit(solution)/shard_map/mlp_forward/pallas_call | solution.py:594
  231.5 0.0 all-gather.8.cloned.1.call-done.weight_ref
  231.5 10.7 %head.1 = (f32[1024,768]{1,0:T(8,128)}, bf16[768,1024]{1,0:T(8,128)(2,1)}, f32[1,1536]{1,0:T(1,128)}, f32[1,1024]{1,0:T(1,128)}, f32[1,2]{1,0:T(1,128)}) custom-call(f32[1024,768]{1,0:T(8,128)} %get-tuple-element.126.stream_ref, s32[1024,1]{1,0:T(8,128)} %copy.50.refs_6_.refs_3_.seg_col_ref, s32[1,1024]{1,0:T(1,128)} %bitcast.71, s32[8,1]{1,0:T(8,128)} %copy.54.label_ref, ...), custom_call_target="tpu_custom_call" | custom-call | tf_op jit(solution)/shard_map/head/pallas_call | solution.py:2149
  242.2 36.1 %mlp_backward.2 = (f32[1024,768]{1,0:T(8,128)}, bf16[1024,768]{1,0:T(8,128)(2,1)}, f32[1,6144]{1,0:T(1,128)}, bf16[3840,768]{1,0:T(8,128)(2,1)}, bf16[768,1536]{1,0:T(8,128)(2,1)}, /*index=5*/bf16[768,1536]{1,0:T(8,128)(2,1)}) custom-call(f32[1024,768]{1,0:T(8,128)} %get-tuple-element.128.grad_ref, bf16[1024,3072]{1,0:T(8,128)(2,1)} %get-tuple-element.129.slope_ref, ...), custom_call_target="tpu_custom_call" | custom-call | tf_op jit(solution)/shard_map/mlp_backward/pallas_call | solution.py:594
  278.4 0.0 reduce-scatter.7.cloned.1.call-start
  278.4 0.5 reduce-scatter.7.cloned.1.call-update
  279.0 0.0 reduce-scatter.9.cloned.1.call-start
  279.0 43.9 %attention_backward.2 = (bf16[1024,2304]{1,0:T(8,128)(2,1)}, bf16[4,240,384]{2,1,0:T(8,128)(2,1)}) custom-call(bf16[1024,2304]{1,0:T(8,128)(2,1)} %get-tuple-element.119.refs_0_.refs_1_.refs_2_, bf16[1024,2304]{1,0:T(8,128)(2,1)} %get-tuple-element.119.refs_0_.refs_1_.refs_2_, bf16[1024,2304]{1,0:T(8,128)(2,1)} %get-tuple-element.119.refs_0_.refs_1_.refs_2_, ...), custom_call_target="tpu_custom_call" | custom-call | tf_op jit(solution)/shard_map/attention_backward/pallas_call | solution.py:594
  323.0 15.4 %qkv_backward.2 = (f32[1024,768]{1,0:T(8,128)}, f32[1,3840]{1,0:T(1,128)}, bf16[768,2304]{1,0:T(8,128)(2,1)}) custom-call(bf16[1024,2304]{1,0:T(8,128)(2,1)} %get-tuple-element.138.grad_ref, f32[1024,768]{1,0:T(8,128)} %get-tuple-element.139.residual_in, f32[1024,768]{1,0:T(8,128)} %get-tuple-element.116.stream_ref.stream_in, ...), custom_call_target="tpu_custom_call" | custom-call | tf_op jit(solution)/shard_map/qkv_backward/pallas_call | solution.py:594
  338.4 0.0 reduce-scatter.11.cloned.1.call-start
  338.5 47.9 %mlp_backward.3 = (f32[1024,768]{1,0:T(8,128)}, bf16[1024,768]{1,0:T(8,128)(2,1)}, f32[1,6144]{1,0:T(1,128)}, bf16[3840,768]{1,0:T(8,128)(2,1)}, bf16[768,3072]{...) custom-call(f32[1024,768]{1,0:T(8,128)} %get-tuple-element.143.refs_0_, ...), custom_call_target="tpu_custom_call" | custom-call | tf_op jit(solution)/shard_map/mlp_backward/pallas_call | solution.py:594
  386.4 36.8 %attention_backward.3 = (bf16[1024,2304]{1,0:T(8,128)(2,1)}, bf16[4,48,1536]{2,1,0:T(8,128)(2,1)}) custom-call(bf16[1024,2304]{1,0:T(8,128)(2,1)} %get-tuple-element.108.refs_0_.refs_1_.refs_2_, bf16[1024,2304]{1,0:T(8,128)(2,1)} %get-tuple-element.108.refs_0_.refs_1_.refs_2_, bf16[1024,2304]{1,0:T(8,128)(2,1)} %get-tuple-element.108.refs_0_.refs_1_.refs_2_, ...), custom_call_target="tpu_custom_call" | custom-call | tf_op jit(solution)/shard_map/attention_backward/pallas_call | solution.py:594
  423.2 37.0 %qkv_backward.3 = (f32[1024,768]{1,0:T(8,128)}, f32[1,3840]{1,0:T(1,128)}, bf16[768,2304]{1,0:T(8,128)(2,1)}, bf16[96,3072]{1,0:T(8,128)(2,1)}) custom-call(bf16[1024,2304]{1,0:T(8,128)(2,1)} %get-tuple-element.158.refs_0_, f32[1024,768]{1,0:T(8,128)} %get-tuple-element.159.refs_1_, f32[1024,768]{1,0:T(8,128)} %get-tuple-element.107.stream_ref.refs_2_, ...), custom_call_target="tpu_custom_call" | custom-call | tf_op jit(solution)/shard_map/qkv_backward/pallas_call | solution.py:594
  460.2 0.7 slice_reduce_fusion.3
  461.0 0.7 slice_reduce_fusion.6
  461.8 0.1 stack.27
  462.1 0.1 stack.28
  462.2 0.1 maximum_bitcast_fusion.2
  462.3 0.1 reshape.133
  462.4 12.1 %embed_backward.1 = (bf16[3072,768]{1,0:T(8,128)(2,1)}, f32[64,768]{1,0:T(8,128)}, f32[1,768]{1,0:T(1,128)}) custom-call(bf16[1024,3072]{1,0:T(8,128)(2,1)} %pixel_ref.1, f32[1024,768]{1,0:T(8,128)} %get-tuple-element.165.grad_ref, f32[64,1024]{1,0:T(8,128)} %get-tuple-element.166.pos_ref), custom_call_target="tpu_custom_call" | custom-call | tf_op jit(solution)/shard_map/embed_backward/pallas_call | solution.py:594
  474.6 0.7 reduce.8
  475.3 0.9 slice.70
  476.3 0.1 concatenate.21
  476.5 0.7 pad.19.refs_5_
  477.2 5.1 reduce-scatter.11.cloned.1.call-done
  482.3 110.4 %reduce_gradients.1 = (bf16[96,2304]{1,0:T(8,128)(2,1)}, bf16[384,768]{1,0:T(8,128)(2,1)}, f32[64,128]{1,0:T(8,128)}, bf16[96,1536]{1,0:T(8,128)(2,1)}, bf16[96,...) custom-call(bf16[96,1024]{1,0:T(8,128)(2,1)} %get-tuple-element.150., ...), custom_call_target="tpu_custom_call" | custom-call | tf_op jit(solution)/shard_map/reduce_gradients/pallas_call | solution.py:1488
  592.8 1.3 fusion.15
  594.2 0.7 slice_bitcast_fusion
  594.9 0.7 slice_multiply_fusion.2
  595.6 0.1 mul.216
  595.7 0.9 slice.79
  596.6 0.7 slice_multiply_fusion
  597.4 1.2 maximum_bitcast_fusion
  598.6 1.3 multiply_subtract_fusion.5
  600.0 2.1 multiply_subtract_fusion.3
  602.1 0.6 multiply_subtract_fusion.6
  602.7 0.9 multiply_subtract_fusion.4
  603.6 1.1 maximum_bitcast_fusion.1
  604.8 3.4 multiply_subtract_fusion.2
  608.2 0.1 copy-done.5
  608.3 0.6 copy-done.7
  608.9 0.2 copy-done.13
  609.1 6.4 %multiply_subtract_fusion.1 = (f32[2,480,768]{2,1,0:T(8,128)}, f32[2,480,768]{2,1,0:T(8,128)}, f32[2,480,768]{2,1,0:T(8,128)}) fusion(f32[2,480,768]{2,1,0:T(8,128)S(1)} %copy-done.1, f32[]{:T(128)} %bitcast.27, bf16[1,480,768]{2,1,0:T(8,128)(2,1)S(1)} %bitcast.57, bf16[1,480,768]{2,1,0:T(8,128)(2,1)S(1)} %bitcast.62, f32[2,480,768]{2,1,0:T(8,128)S(1)} %copy-done.5, ...), kind=kLoop, calls=%fused_computation.8 | loop fusion | flops 12533760 | bytes 19169284 | tf_op jit(solution)/shard_map/sub | solution.py:2173
  615.6 1.3 copy-done.4
  616.8 6.9 %multiply_subtract_fusion = (f32[2,96,5376]{2,1,0:T(8,128)}, f32[2,96,5376]{2,1,0:T(8,128)}, f32[2,96,5376]{2,1,0:T(8,128)}) fusion(f32[2,96,5376]{2,1,0:T(8,128)S(1)} %copy-done, f32[]{:T(128)} %bitcast.27, bf16[1,96,5376]{2,1,0:T(8,128)(2,1)S(1)} %maximum_bitcast_fusion.1, bf16[1,96,5376]{2,1,0:T(8,128)(2,1)S(1)} %maximum_bitcast_fusion, ...), kind=kLoop, calls=%fused_computation.5 | loop fusion | flops 17547264 | bytes 26836996 | tf_op jit(solution)/shard_map/sub | solution.py:2173
  (87 shorter events, 0.6 us)
Async XLA Ops:
  7.2 143.1 %all-gather.4.cloned.1.call-start = ((), (), s32[]{:S(2)}) async-start(), calls=%async_computation.4 | async-start | bytes 3981312 | tf_op jit(solution)/shard_map/all_gather | solution.py:2219
  92.0 118.3 %all-gather.6.cloned.1.call-start = ((), (), s32[]{:S(2)}) async-start(), calls=%async_computation.5 | async-start | bytes 5308416 | tf_op jit(solution)/shard_map/all_gather | solution.py:2219
  92.8 138.7 %all-gather.8.cloned.1.call-start = ((), (), s32[]{:S(2)}) async-start(), calls=%async_computation.6 | async-start | bytes 1769472 | tf_op jit(solution)/shard_map/all_gather | solution.py:2219
  93.5 383.7 %reduce-scatter.5.cloned.1.call-start = ((), (), s32[]{:S(2)}) async-start(), calls=%async_computation.7 | async-start | bytes 2654208 | tf_op jit(solution)/shard_map/reduce_scatter | solution.py:1549
  127.9 21.1 %copy-start.33 = (s32[1,8]{1,0:T(1,128)S(1)}, s32[1,8]{1,0:T(1,128)}, u32[]{:S(2)}) copy-start(s32[1,8]{1,0:T(1,128)} %param.28) | copy-start | bytes 100
  127.9 21.7 %copy-start.21 = (f32[3304]{0:T(1024)S(1)}, f32[3304]{0:T(1024)}, u32[]{:S(2)}) copy-start(f32[3304]{0:T(1024)} %param.35) | copy-start | bytes 39652
  278.4 198.8 %reduce-scatter.7.cloned.1.call-start = ((), (), s32[]{:S(2)}) async-start(), calls=%async_computation.8 | async-start | bytes 2654208 | tf_op jit(solution)/shard_map/reduce_scatter | solution.py:1549
  279.0 198.3 %reduce-scatter.9.cloned.1.call-start = ((), (), s32[]{:S(2)}) async-start(), calls=%async_computation.9 | async-start | bytes 3981312 | tf_op jit(solution)/shard_map/reduce_scatter | solution.py:1549
  338.4 143.9 %reduce-scatter.11.cloned.1.call-start = ((), (), s32[]{:S(2)}) async-start(), calls=%async_computation.10 | async-start | bytes 6635520 | tf_op jit(solution)/shard_map/reduce_scatter | solution.py:1549
  423.2 37.8 %copy-start.24 = (f32[1,6144]{1,0:T(1,128)S(1)}, f32[1,6144]{1,0:T(1,128)}, u32[]{:S(2)}) copy-start(f32[1,6144]{1,0:T(1,128)} %get-tuple-element.169) | copy-start | bytes 73732
  423.2 38.7 %copy-start.27 = (f32[1,3840]{1,0:T(1,128)S(1)}, f32[1,3840]{1,0:T(1,128)}, u32[]{:S(2)}) copy-start(f32[1,3840]{1,0:T(1,128)} %get-tuple-element.170) | copy-start | bytes 46084
  423.2 38.7 %copy-start.23 = (f32[1,6144]{1,0:T(1,128)S(1)}, f32[1,6144]{1,0:T(1,128)}, u32[]{:S(2)}) copy-start(f32[1,6144]{1,0:T(1,128)} %get-tuple-element.171) | copy-start | bytes 73732
  423.2 39.2 %copy-start.30 = (f32[1,1536]{1,0:T(1,128)S(1)}, f32[1,1536]{1,0:T(1,128)}, u32[]{:S(2)}) copy-start(f32[1,1536]{1,0:T(1,128)} %get-tuple-element.174) | copy-start | bytes 18436
  462.4 13.8 %copy-start.31 = (f32[1,1024]{1,0:T(1,128)S(1)}, f32[1,1024]{1,0:T(1,128)}, u32[]{:S(2)}) copy-start(f32[1,1024]{1,0:T(1,128)} %get-tuple-element.175) | copy-start | bytes 12292
  462.4 13.8 %copy-start.32 = (f32[1,2]{1,0:T(1,128)S(1)}, f32[1,2]{1,0:T(1,128)}, u32[]{:S(2)}) copy-start(f32[1,2]{1,0:T(1,128)} %get-tuple-element.176) | copy-start | bytes 28
  482.3 115.0 %copy-start.8 = (bf16[96,3072]{1,0:T(8,128)(2,1)S(1)}, bf16[96,3072]{1,0:T(8,128)(2,1)}, u32[]{:S(2)}) copy-start(bf16[96,3072]{1,0:T(8,128)(2,1)} %get-tuple-element.163.refs_2_) | copy-start | bytes 1769476
  482.3 119.7 %copy-start.29 = (f32[2,1248]{1,0:T(2,128)S(1)}, f32[2,1248]{1,0:T(2,128)}, u32[]{:S(2)}) copy-start(f32[2,1248]{1,0:T(2,128)} %param.40) | copy-start | bytes 29956
  482.3 120.4 %copy-start.19 = (f32[49,768]{1,0:T(8,128)S(1)}, f32[49,768]{1,0:T(8,128)}, u32[]{:S(2)}) copy-start(f32[49,768]{1,0:T(8,128)} %param.48) | copy-start | bytes 451588
  482.3 120.4 %copy-start.20 = (f32[49,768]{1,0:T(8,128)S(1)}, f32[49,768]{1,0:T(8,128)}, u32[]{:S(2)}) copy-start(f32[49,768]{1,0:T(8,128)} %param.41) | copy-start | bytes 451588
  592.7 5.9 copy-start.25
  592.7 5.9 copy-start.26
  592.7 7.2 %copy-start.9 = (f32[96,1000]{1,0:T(8,128)S(1)}, f32[96,1000]{1,0:T(8,128)}, u32[]{:S(2)}) copy-start(f32[96,1000]{1,0:T(8,128)} %refs_4_.1) | copy-start | bytes 1152004
  592.8 7.2 %copy-start.12 = (bf16[96,1024]{1,0:T(8,128)(2,1)S(1)}, bf16[96,1024]{1,0:T(8,128)(2,1)}, u32[]{:S(2)}) copy-start(bf16[96,1024]{1,0:T(8,128)(2,1)} %get-tuple-element.150.refs_0_) | copy-start | bytes 589828
  592.8 7.2 %copy-start.17 = (f32[96,1000]{1,0:T(8,128)S(1)}, f32[96,1000]{1,0:T(8,128)}, u32[]{:S(2)}) copy-start(f32[96,1000]{1,0:T(8,128)} %param.44) | copy-start | bytes 1152004
  592.8 7.2 %copy-start.18 = (f32[96,1000]{1,0:T(8,128)S(1)}, f32[96,1000]{1,0:T(8,128)}, u32[]{:S(2)}) copy-start(f32[96,1000]{1,0:T(8,128)} %param.37) | copy-start | bytes 1152004
  592.8 9.3 %copy-start.22 = (f32[2,1248]{1,0:T(2,128)S(1)}, f32[2,1248]{1,0:T(2,128)}, u32[]{:S(2)}) copy-start(f32[2,1248]{1,0:T(2,128)} %param.33) | copy-start | bytes 29956
  592.8 9.3 %copy-start.28 = (f32[2,1248]{1,0:T(2,128)S(1)}, f32[2,1248]{1,0:T(2,128)}, u32[]{:S(2)}) copy-start(f32[2,1248]{1,0:T(2,128)} %param.47) | copy-start | bytes 29956
  592.8 9.9 %copy-start.14 = (f32[49,768]{1,0:T(8,128)S(1)}, f32[49,768]{1,0:T(8,128)}, u32[]{:S(2)}) copy-start(f32[49,768]{1,0:T(8,128)} %refs_8_.1) | copy-start | bytes 451588
  597.4 6.3 copy-start.16
  597.4 7.4 %copy-start.11 = (f32[384,768]{1,0:T(8,128)S(1)}, f32[384,768]{1,0:T(8,128)}, u32[]{:S(2)}) copy-start(f32[384,768]{1,0:T(8,128)} %param.36) | copy-start | bytes 3538948
  599.9 4.8 copy-start.2
  600.0 4.8 copy-start.10
  600.0 4.8 copy-start.15
  600.0 8.2 %copy-start.6 = (f32[2,480,768]{2,1,0:T(8,128)S(1)}, f32[2,480,768]{2,1,0:T(8,128)}, u32[]{:S(2)}) copy-start(f32[2,480,768]{2,1,0:T(8,128)} %param.39) | copy-start | bytes 8847364
  604.8 3.4 copy-start.1
  604.8 3.5 copy-start.5
  604.8 4.1 copy-start.7
  604.8 4.3 copy-start.13
  609.1 6.4 %copy-start = (f32[2,96,5376]{2,1,0:T(8,128)S(1)}, f32[2,96,5376]{2,1,0:T(8,128)}, u32[]{:S(2)}) copy-start(f32[2,96,5376]{2,1,0:T(8,128)} %refs_2_.1) | copy-start | bytes 12386308
  609.1 6.4 %copy-start.3 = (f32[2,96,5376]{2,1,0:T(8,128)S(1)}, f32[2,96,5376]{2,1,0:T(8,128)}, u32[]{:S(2)}) copy-start(f32[2,96,5376]{2,1,0:T(8,128)} %param.45) | copy-start | bytes 12386308
  609.1 7.7 %copy-start.4 = (f32[2,96,5376]{2,1,0:T(8,128)S(1)}, f32[2,96,5376]{2,1,0:T(8,128)}, u32[]{:S(2)}) copy-start(f32[2,96,5376]{2,1,0:T(8,128)} %param.38) | copy-start | bytes 12386308
Sparse Core Ops, SparseCore 0:
  92.1 53.8 all-gather.3
  147.7 51.3 all-gather.5
  200.8 23.2 all-gather.7
  278.5 38.0 reduce-scatter.4
  319.4 38.8 reduce-scatter.6
  361.1 44.5 reduce-scatter.8
  408.1 74.1 reduce-scatter.10

commit v14 on v13

--- a/solution.py
+++ b/solution.py
@@ -2263,16 +2263,17 @@
             output,
             vector,
             2 if index else 1,
-            () if index else [output_rest, SumRide(by_owner(head_grad), False)],
-            9,
+            [SumRide(by_owner(head_grad), False) if index else output_rest],
+            10 if index else 9,
         )
         if index:
-            attended_grad, *up_parts = lax.optimization_barrier((attended_grad, *brought))
-            late_parts = [scatter(by_owner(part)) for part in up_parts]
+            *up_parts, head_sum = brought
+            attended_grad, *up_parts = lax.optimization_barrier((attended_grad, *up_parts))
+            one_parts = [scatter(by_owner(part)) for part in up_parts]
         else:
-            up_grad, output_one_sum, head_sum = brought
+            up_grad, output_one_sum = brought
             attended_grad, output_grad = lax.optimization_barrier((attended_grad, output_grad))
-            late_parts.append(scatter(by_owner(output_grad)))
+            output_zero_part = scatter(by_owner(output_grad))
         qkv_grad, rest = attention_backward(
             qkv_rows,
             expo,
@@ -2289,15 +2290,15 @@
             normed,
             qkv_weight,
             vector,
-            () if index else [rest],
+            () if index else [rest, *[ShareRide(part) for part in one_parts]],
             7,
         )
         if index:
             output_rest = rest
             stream_grad, qkv_weight_grad = lax.optimization_barrier((stream_grad, qkv_weight_grad))
-            late_parts.append(scatter(by_owner(qkv_weight_grad)))
+            one_parts.append(scatter(by_owner(qkv_weight_grad)))
         else:
-            (up_zero_sum,) = brought
+            up_zero_sum, *up_one_sums, qkv_one_sum = brought
         vector_grads[index] = jnp.concatenate(
             [
                 qkv_sums[0, : 2 * D],
@@ -2331,16 +2332,14 @@
         qkv_zero_sum,
         kernel_sum,
         small_share,
-        *up_one_sums,
-        qkv_one_sum,
         output_zero_sum,
         small_full,
         numbers,
     ) = reduce_all(
         [by_owner(qkv_weight_grad), by_owner(kernel_grad)],
         small,
-        late_parts,
-        [head_sum, output_one_sum, up_zero_sum],
+        [output_zero_part],
+        [head_sum, output_one_sum, up_zero_sum, *up_one_sums, qkv_one_sum],
         vector_rows,
         rest.shape[0],
         2,

time: 640 us -> 627 us (0.980)
  Pallas kernels: 567 us -> 551 us
    pallas_call x1, Pallas kernels: 110 us -> 90.6 us  [reduce_call(): pl.pallas_call(functools.partial(reduce_kernel, whole=whole, partly=partl...]
where the time goes in v14:
time: 627 us; the launch traced here: 618 us
  Pallas kernels  551 us (88%)
  other arithmetic  25.7 us (4%)
  local copies, waits for them, and re-layouts  15.3 us (2%)
  between operations  15.3 us (2%)
  waiting for transfers between devices  10.3 us (2%)
    pallas_call x12, Pallas kernels, block_call(): pl.pallas_call(kernel, grid=(grid,), in_specs=in_specs, out_specs=out_spe...  370 us
    pallas_call x1, Pallas kernels, reduce_call(): pl.pallas_call(functools.partial(reduce_kernel, whole=whole, partly=partl...  90.6 us
    pallas_call x1, Pallas kernels, begin(): pl.pallas_call(functools.partial(first_kernel, spots=spots), in_specs=[AN...  80.1 us
    sub x7, other arithmetic, adam_update(): return (moment, square, weight - learn_rate * step_dir)  21.5 us
  transfers between devices with their start and end apart: 7, of which 1 were waited for; matrix products, arithmetic and copies ran while one was open for 1% of the time, Pallas kernels for 52%

profile of v14, /device:TPU:0, one launch (start us, length us, event | category | flops | bytes accessed | tf_op | source)
XLA Modules:
  0.0 618.1 jit_solution(10173247968942839481)
XLA Ops:
  7.2 0.0 all-gather.4.cloned.1.call-start
  7.2 0.7 convert_element_type.23
  8.0 0.2 dynamic_update_slice.3
  8.2 0.6 reshape.122.refs_1_
  8.8 1.3 broadcast_in_dim.22.refs_9_
  10.2 1.7 copy.50.refs_6_.refs_3_.seg_col_ref
  11.9 80.1 %begin.1 = (f32[1024,768]{1,0:T(8,128)}, f32[64,1024]{1,0:T(8,128)}, f32[1,9984]{1,0:T(1,128)}, f32[1,9984]{1,0:T(1,128)}, bf16[8,96,2304]{2,1,0:T(8,128)(2,1)},...) custom-call(f32[384,768]{1,0:T(8,128)} %refs_0_.1, ...), custom_call_target="tpu_custom_call" | custom-call | tf_op jit(solution)/shard_map/begin/pallas_call | solution.py:832
  92.0 0.0 all-gather.6.cloned.1.call-start
  92.0 0.7 all-gather.6.cloned.1.call-update
  92.7 0.0 all-gather.8.cloned.1.call-start
  92.8 0.7 all-gather.8.cloned.1.call-update
  93.5 0.3 reduce-scatter.5.cloned.1.call-start
  93.8 34.1 %attention_forward.2 = (bf16[1024,768]{1,0:T(8,128)(2,1)}, bf16[12,1024,1024]{2,1,0:T(8,128)(2,1)}, f32[1024,768]{1,0:T(8,128)}, bf16[8,480,768]{2,1,0:T(8,128)(2,1)}, bf16[4,240,384]{2,1,0:T(8,128)(2,1)}) custom-call(bf16[1024,2304]{1,0:T(8,128)(2,1)} %get-tuple-element.108.refs_0_.refs_1_.refs_2_, ...), custom_call_target="tpu_custom_call" | custom-call | flops 12884901888 | bytes 34603008 | tf_op jit(solution)/shard_map/attention_forward/pallas_call | solution.py:594
  127.9 21.0 %mlp_forward.2 = (f32[1024,768]{1,0:T(8,128)}, bf16[1024,768]{1,0:T(8,128)(2,1)}, bf16[1024,3072]{1,0:T(8,128)(2,1)}, bf16[1024,3072]{1,0:T(8,128)(2,1)}, f32[1024,768]{1,0:T(8,128)}) custom-call(f32[1024,768]{1,0:T(8,128)} %get-tuple-element.107.stream_ref.refs_2_, bf16[1024,768]{1,0:T(8,128)(2,1)} %get-tuple-element.112.attended_ref.refs_5_, ...), custom_call_target="tpu_custom_call" | custom-call | flops 10871635968 | bytes 35782656 | tf_op jit(solution)/shard_map/mlp_forward/pallas_call | solution.py:594
  148.9 0.7 copy.54.label_ref
  149.6 0.6 broadcast_in_dim.24.vector_ref
  150.2 9.1 %qkv_forward.1 = (bf16[1024,768]{1,0:T(8,128)(2,1)}, bf16[1024,2304]{1,0:T(8,128)(2,1)}) custom-call(f32[1024,768]{1,0:T(8,128)} %get-tuple-element.116.stream_ref.stream_in, bf16[768,2304]{1,0:T(8,128)(2,1)} %all-gather.4.cloned.1.call-done.weight_ref, f32[1,9984]{1,0:T(1,128)} %get-tuple-element.118.vector_ref.refs_9_), custom_call_target="tpu_custom_call" | custom-call | flops 3623878656 | bytes 14548992 | tf_op jit(solution)/shard_map/qkv_forward/pallas_call | solution.py:594
  159.4 50.9 %attention_forward.3 = (bf16[1024,768]{1,0:T(8,128)(2,1)}, bf16[12,1024,1024]{2,1,0:T(8,128)(2,1)}, f32[1024,768]{1,0:T(8,128)}, bf16[8,480,768]{2,1,0:T(8,128)(2,1)}) custom-call(bf16[1024,2304]{1,0:T(8,128)(2,1)} %get-tuple-element.119.refs_0_.refs_1_.refs_2_, bf16[1024,2304]{1,0:T(8,128)(2,1)} %get-tuple-element.119.refs_0_.refs_1_.refs_2_, ...), custom_call_target="tpu_custom_call" | custom-call | flops 12884901888 | bytes 34603008 | tf_op jit(solution)/shard_map/attention_forward/pallas_call | solution.py:594
  210.3 0.0 all-gather.6.cloned.1.call-done.up_ref.refs_7_
  210.3 21.1 %mlp_forward.3 = (f32[1024,768]{1,0:T(8,128)}, bf16[1024,768]{1,0:T(8,128)(2,1)}, bf16[1024,3072]{1,0:T(8,128)(2,1)}, bf16[1024,3072]{1,0:T(8,128)(2,1)}, f32[1024,768]{1,0:T(8,128)}) custom-call(f32[1024,768]{1,0:T(8,128)} %get-tuple-element.116.stream_ref.stream_in, bf16[1024,768]{1,0:T(8,128)(2,1)} %get-tuple-element.121.attended_ref.refs_5_, ...), custom_call_target="tpu_custom_call" | custom-call | flops 10871635968 | bytes 35782656 | tf_op jit(solution)/shard_map/mlp_forward/pallas_call | solution.py:594
  231.4 0.0 all-gather.8.cloned.1.call-done.weight_ref
  231.5 10.7 %head.1 = (f32[1024,768]{1,0:T(8,128)}, bf16[768,1024]{1,0:T(8,128)(2,1)}, f32[1,1536]{1,0:T(1,128)}, f32[1,1024]{1,0:T(1,128)}, f32[1,2]{1,0:T(1,128)}) custom-call(f32[1024,768]{1,0:T(8,128)} %get-tuple-element.124.stream_ref, s32[1024,1]{1,0:T(8,128)} %copy.50.refs_6_.refs_3_.seg_col_ref, s32[1,1024]{1,0:T(1,128)} %bitcast.71, s32[8,1]{1,0:T(8,128)} %copy.54.label_ref, ...), custom_call_target="tpu_custom_call" | custom-call | tf_op jit(solution)/shard_map/head/pallas_call | solution.py:2149
  242.2 48.7 %mlp_backward.2 = (f32[1024,768]{1,0:T(8,128)}, bf16[1024,768]{1,0:T(8,128)(2,1)}, f32[1,6144]{1,0:T(1,128)}, bf16[3840,768]{1,0:T(8,128)(2,1)}, bf16[768,1536]{...) custom-call(f32[1024,768]{1,0:T(8,128)} %get-tuple-element.126.refs_0_, ...), custom_call_target="tpu_custom_call" | custom-call | tf_op jit(solution)/shard_map/mlp_backward/pallas_call | solution.py:594
  290.9 0.0 reduce-scatter.7.cloned.1.call-start
  291.0 0.5 reduce-scatter.7.cloned.1.call-update
  291.5 0.0 reduce-scatter.9.cloned.1.call-start
  291.6 40.5 %attention_backward.2 = (bf16[1024,2304]{1,0:T(8,128)(2,1)}, bf16[4,240,384]{2,1,0:T(8,128)(2,1)}) custom-call(bf16[1024,2304]{1,0:T(8,128)(2,1)} %get-tuple-element.119.refs_0_.refs_1_.refs_2_, bf16[1024,2304]{1,0:T(8,128)(2,1)} %get-tuple-element.119.refs_0_.refs_1_.refs_2_, bf16[1024,2304]{1,0:T(8,128)(2,1)} %get-tuple-element.119.refs_0_.refs_1_.refs_2_, ...), custom_call_target="tpu_custom_call" | custom-call | tf_op jit(solution)/shard_map/attention_backward/pallas_call | solution.py:594
  332.1 15.4 %qkv_backward.2 = (f32[1024,768]{1,0:T(8,128)}, f32[1,3840]{1,0:T(1,128)}, bf16[768,2304]{1,0:T(8,128)(2,1)}) custom-call(bf16[1024,2304]{1,0:T(8,128)(2,1)} %get-tuple-element.140.grad_ref, f32[1024,768]{1,0:T(8,128)} %get-tuple-element.141.residual_in, f32[1024,768]{1,0:T(8,128)} %get-tuple-element.116.stream_ref.stream_in, ...), custom_call_target="tpu_custom_call" | custom-call | tf_op jit(solution)/shard_map/qkv_backward/pallas_call | solution.py:594
  347.5 0.0 reduce-scatter.11.cloned.1.call-start
  347.6 39.6 %mlp_backward.3 = (f32[1024,768]{1,0:T(8,128)}, bf16[1024,768]{1,0:T(8,128)(2,1)}, f32[1,6144]{1,0:T(1,128)}, bf16[3840,768]{1,0:T(8,128)(2,1)}, bf16[768,3072]{1,0:T(8,128)(2,1)}, /*index=5*/bf16[480,768]{1,0:T(8,128)(2,1)}) custom-call(f32[1024,768]{1,0:T(8,128)} %get-tuple-element.145.refs_0_, bf16[1024,3072]{1,0:T(8,128)(2,1)} %get-tuple-element.146.refs_1_, ...), custom_call_target="tpu_custom_call" | custom-call | tf_op jit(solution)/shard_map/mlp_backward/pallas_call | solution.py:594
  387.2 0.7 copy-done.29
  388.0 0.1 stack.28
  388.2 38.0 %attention_backward.3 = (bf16[1024,2304]{1,0:T(8,128)(2,1)}, bf16[4,48,1536]{2,1,0:T(8,128)(2,1)}) custom-call(bf16[1024,2304]{1,0:T(8,128)(2,1)} %get-tuple-element.108.refs_0_.refs_1_.refs_2_, bf16[1024,2304]{1,0:T(8,128)(2,1)} %get-tuple-element.108.refs_0_.refs_1_.refs_2_, bf16[1024,2304]{1,0:T(8,128)(2,1)} %get-tuple-element.108.refs_0_.refs_1_.refs_2_, ...), custom_call_target="tpu_custom_call" | custom-call | tf_op jit(solution)/shard_map/attention_backward/pallas_call | solution.py:594
  426.4 39.0 %qkv_backward.3 = (f32[1024,768]{1,0:T(8,128)}, f32[1,3840]{1,0:T(1,128)}, bf16[768,2304]{1,0:T(8,128)(2,1)}, bf16[96,3072]{1,0:T(8,128)(2,1)}, bf16[96,1536]{1,...) custom-call(bf16[1024,2304]{1,0:T(8,128)(2,1)} %get-tuple-element.158.refs_0_, ...), custom_call_target="tpu_custom_call" | custom-call | tf_op jit(solution)/shard_map/qkv_backward/pallas_call | solution.py:594
  465.3 0.7 slice_reduce_fusion.7
  466.1 0.7 slice_reduce_fusion.3
  466.8 0.1 stack.27
  466.9 0.1 maximum_bitcast_fusion.2
  467.0 0.1 reshape.136
  467.1 12.2 %embed_backward.1 = (bf16[3072,768]{1,0:T(8,128)(2,1)}, f32[64,768]{1,0:T(8,128)}, f32[1,768]{1,0:T(1,128)}) custom-call(bf16[1024,3072]{1,0:T(8,128)(2,1)} %pixel_ref.1, f32[1024,768]{1,0:T(8,128)} %get-tuple-element.171.grad_ref, f32[64,1024]{1,0:T(8,128)} %get-tuple-element.172.pos_ref), custom_call_target="tpu_custom_call" | custom-call | tf_op jit(solution)/shard_map/embed_backward/pallas_call | solution.py:594
  479.3 0.7 reduce.8
  480.0 0.9 slice.70
  481.0 0.1 concatenate.21
  481.3 0.7 pad.19.refs_8_
  482.0 8.2 %reduce-scatter.11.cloned.1.call-done = bf16[1,480,768]{2,1,0:T(8,128)(2,1)} async-done(((bf16[8,480,768]{2,1,0:T(8,128)(2,1)}), bf16[1,480,768]{2,1,0:T(8,128)(2,1)}) %reduce-scatter.11.cloned.1.call-update) | async-done | bytes 737296 | tf_op jit(solution)/shard_map/reduce_scatter | solution.py:1549
  490.2 90.6 %reduce_gradients.1 = (bf16[96,2304]{1,0:T(8,128)(2,1)}, bf16[384,768]{1,0:T(8,128)(2,1)}, f32[64,128]{1,0:T(8,128)}, bf16[480,768]{1,0:T(8,128)(2,1)}, f32[8,64,128]{2,1,0:T(8,128)}, /*index=5*/f32[1,128]{1,0:T(1,128)}) custom-call(bf16[96,1024]{1,0:T(8,128)(2,1)} %get-tuple-element.132.refs_0_, bf16[480,768]{1,0:T(8,128)(2,1)} %get-tuple-element.151.refs_1_, ...), custom_call_target="tpu_custom_call" | custom-call | tf_op jit(solution)/shard_map/reduce_gradients/pallas_call | solution.py:1488
  580.9 1.4 fusion.15
  582.3 0.7 slice_bitcast_fusion
  583.0 0.7 slice_multiply_fusion.2
  583.7 0.1 mul.216
  583.8 0.9 slice.79
  584.7 0.7 slice_multiply_fusion
  585.6 1.3 maximum_bitcast_fusion
  587.0 1.5 multiply_subtract_fusion.5
  588.4 1.9 multiply_subtract_fusion.3
  590.4 0.6 multiply_subtract_fusion.6
  591.0 0.9 multiply_subtract_fusion.4
  592.0 3.4 multiply_subtract_fusion.2
  595.3 0.1 copy-done.5
  595.5 0.6 copy-done.7
  596.1 0.2 copy-done.16
  596.3 6.4 %multiply_subtract_fusion.1 = (f32[2,480,768]{2,1,0:T(8,128)}, f32[2,480,768]{2,1,0:T(8,128)}, f32[2,480,768]{2,1,0:T(8,128)}) fusion(f32[2,480,768]{2,1,0:T(8,128)S(1)} %copy-done.1, f32[]{:T(128)} %bitcast.27, bf16[1,480,768]{2,1,0:T(8,128)(2,1)S(1)} %bitcast.57, bf16[1,480,768]{2,1,0:T(8,128)(2,1)S(1)} %bitcast.62, f32[2,480,768]{2,1,0:T(8,128)S(1)} %copy-done.5, ...), kind=kLoop, calls=%fused_computation.8 | loop fusion | flops 12533760 | bytes 19169284 | tf_op jit(solution)/shard_map/sub | solution.py:2173
  602.7 1.3 copy-done.4
  603.9 6.9 %multiply_subtract_fusion = (f32[2,96,5376]{2,1,0:T(8,128)}, f32[2,96,5376]{2,1,0:T(8,128)}, f32[2,96,5376]{2,1,0:T(8,128)}) fusion(f32[2,96,5376]{2,1,0:T(8,128)S(1)} %copy-done, f32[]{:T(128)} %bitcast.27, bf16[1,96,5376]{2,1,0:T(8,128)(2,1)S(1)} %get-tuple-element.216, bf16[1,96,5376]{2,1,0:T(8,128)(2,1)S(1)} %get-tuple-element.215, ...), kind=kLoop, calls=%fused_computation.5 | loop fusion | flops 17547264 | bytes 26836996 | tf_op jit(solution)/shard_map/sub | solution.py:2173
  (92 shorter events, 0.7 us)
Async XLA Ops:
  7.2 143.0 %all-gather.4.cloned.1.call-start = ((), (), s32[]{:S(2)}) async-start(), calls=%async_computation.4 | async-start | bytes 3981312 | tf_op jit(solution)/shard_map/all_gather | solution.py:2219
  92.0 118.3 %all-gather.6.cloned.1.call-start = ((), (), s32[]{:S(2)}) async-start(), calls=%async_computation.5 | async-start | bytes 5308416 | tf_op jit(solution)/shard_map/all_gather | solution.py:2219
  92.7 138.7 %all-gather.8.cloned.1.call-start = ((), (), s32[]{:S(2)}) async-start(), calls=%async_computation.6 | async-start | bytes 1769472 | tf_op jit(solution)/shard_map/all_gather | solution.py:2219
  93.5 332.8 %reduce-scatter.5.cloned.1.call-start = ((), (), s32[]{:S(2)}) async-start(), calls=%async_computation.7 | async-start | bytes 2654208 | tf_op jit(solution)/shard_map/reduce_scatter | solution.py:1549
  127.9 21.1 %copy-start.35 = (s32[1,8]{1,0:T(1,128)S(1)}, s32[1,8]{1,0:T(1,128)}, u32[]{:S(2)}) copy-start(s32[1,8]{1,0:T(1,128)} %param.28) | copy-start | bytes 100
  127.9 21.7 %copy-start.23 = (f32[3304]{0:T(1024)S(1)}, f32[3304]{0:T(1024)}, u32[]{:S(2)}) copy-start(f32[3304]{0:T(1024)} %param.35) | copy-start | bytes 39652
  290.9 135.4 %reduce-scatter.7.cloned.1.call-start = ((), (), s32[]{:S(2)}) async-start(), calls=%async_computation.8 | async-start | bytes 2654208 | tf_op jit(solution)/shard_map/reduce_scatter | solution.py:1549
  291.5 134.8 %reduce-scatter.9.cloned.1.call-start = ((), (), s32[]{:S(2)}) async-start(), calls=%async_computation.9 | async-start | bytes 3981312 | tf_op jit(solution)/shard_map/reduce_scatter | solution.py:1549
  347.5 142.7 %reduce-scatter.11.cloned.1.call-start = ((), (), s32[]{:S(2)}) async-start(), calls=%async_computation.10 | async-start | bytes 6635520 | tf_op jit(solution)/shard_map/reduce_scatter | solution.py:1549
  387.1 0.7 copy-start.29
  387.2 0.7 copy-start.25
  387.2 1.0 copy-start.32
  388.2 38.0 %copy-start.26 = (f32[1,6144]{1,0:T(1,128)S(1)}, f32[1,6144]{1,0:T(1,128)}, u32[]{:S(2)}) copy-start(f32[1,6144]{1,0:T(1,128)} %get-tuple-element.175) | copy-start | bytes 73732
  467.1 13.9 %copy-start.33 = (f32[1,1024]{1,0:T(1,128)S(1)}, f32[1,1024]{1,0:T(1,128)}, u32[]{:S(2)}) copy-start(f32[1,1024]{1,0:T(1,128)} %get-tuple-element.181) | copy-start | bytes 12292
  467.1 13.9 %copy-start.34 = (f32[1,2]{1,0:T(1,128)S(1)}, f32[1,2]{1,0:T(1,128)}, u32[]{:S(2)}) copy-start(f32[1,2]{1,0:T(1,128)} %get-tuple-element.182) | copy-start | bytes 28
  490.2 95.3 %copy-start.8 = (bf16[96,3072]{1,0:T(8,128)(2,1)S(1)}, bf16[96,3072]{1,0:T(8,128)(2,1)}, u32[]{:S(2)}) copy-start(bf16[96,3072]{1,0:T(8,128)(2,1)} %get-tuple-element.166.refs_2_) | copy-start | bytes 1769476
  490.2 95.3 %copy-start.9 = (bf16[96,2304]{1,0:T(8,128)(2,1)S(1)}, bf16[96,2304]{1,0:T(8,128)(2,1)}, u32[]{:S(2)}) copy-start(bf16[96,2304]{1,0:T(8,128)(2,1)} %get-tuple-element.169.refs_5_) | copy-start | bytes 1327108
  490.2 95.3 %copy-start.11 = (bf16[96,1536]{1,0:T(8,128)(2,1)S(1)}, bf16[96,1536]{1,0:T(8,128)(2,1)}, u32[]{:S(2)}) copy-start(bf16[96,1536]{1,0:T(8,128)(2,1)} %get-tuple-element.167.refs_3_) | copy-start | bytes 884740
  490.2 95.3 %copy-start.12 = (bf16[96,1536]{1,0:T(8,128)(2,1)S(1)}, bf16[96,1536]{1,0:T(8,128)(2,1)}, u32[]{:S(2)}) copy-start(bf16[96,1536]{1,0:T(8,128)(2,1)} %get-tuple-element.168.refs_4_) | copy-start | bytes 884740
  580.8 6.1 copy-start.27
  580.9 6.1 copy-start.28
  580.9 7.6 %copy-start.10 = (f32[96,1000]{1,0:T(8,128)S(1)}, f32[96,1000]{1,0:T(8,128)}, u32[]{:S(2)}) copy-start(f32[96,1000]{1,0:T(8,128)} %refs_4_.1) | copy-start | bytes 1152004
  580.9 7.5 %copy-start.15 = (bf16[96,1024]{1,0:T(8,128)(2,1)S(1)}, bf16[96,1024]{1,0:T(8,128)(2,1)}, u32[]{:S(2)}) copy-start(bf16[96,1024]{1,0:T(8,128)(2,1)} %get-tuple-element.132.refs_0_) | copy-start | bytes 589828
  580.9 7.5 %copy-start.19 = (f32[96,1000]{1,0:T(8,128)S(1)}, f32[96,1000]{1,0:T(8,128)}, u32[]{:S(2)}) copy-start(f32[96,1000]{1,0:T(8,128)} %param.44) | copy-start | bytes 1152004
  580.9 7.5 %copy-start.20 = (f32[96,1000]{1,0:T(8,128)S(1)}, f32[96,1000]{1,0:T(8,128)}, u32[]{:S(2)}) copy-start(f32[96,1000]{1,0:T(8,128)} %param.37) | copy-start | bytes 1152004
  585.5 4.9 copy-start.24
  585.5 4.8 copy-start.30
  585.5 4.8 copy-start.31
  585.5 5.5 copy-start.17
  585.5 5.5 copy-start.21
  585.6 5.5 copy-start.22
  585.6 6.3 %copy-start.18 = (bf16[384,768]{1,0:T(8,128)(2,1)S(1)}, bf16[384,768]{1,0:T(8,128)(2,1)}, u32[]{:S(2)}) copy-start(bf16[384,768]{1,0:T(8,128)(2,1)} %get-tuple-element.185) | copy-start | bytes 1769476
  585.6 9.7 %copy-start.6 = (f32[2,480,768]{2,1,0:T(8,128)S(1)}, f32[2,480,768]{2,1,0:T(8,128)}, u32[]{:S(2)}) copy-start(f32[2,480,768]{2,1,0:T(8,128)} %param.39) | copy-start | bytes 8847364
  586.9 5.0 copy-start.2
  586.9 5.0 copy-start.13
  586.9 5.0 copy-start.14
  591.9 3.4 copy-start.1
  591.9 3.5 copy-start.5
  591.9 4.1 copy-start.7
  591.9 4.3 copy-start.16
  596.3 6.4 %copy-start = (f32[2,96,5376]{2,1,0:T(8,128)S(1)}, f32[2,96,5376]{2,1,0:T(8,128)}, u32[]{:S(2)}) copy-start(f32[2,96,5376]{2,1,0:T(8,128)} %refs_2_.1) | copy-start | bytes 12386308
  596.3 6.4 %copy-start.3 = (f32[2,96,5376]{2,1,0:T(8,128)S(1)}, f32[2,96,5376]{2,1,0:T(8,128)}, u32[]{:S(2)}) copy-start(f32[2,96,5376]{2,1,0:T(8,128)} %param.45) | copy-start | bytes 12386308
  596.3 7.7 %copy-start.4 = (f32[2,96,5376]{2,1,0:T(8,128)S(1)}, f32[2,96,5376]{2,1,0:T(8,128)}, u32[]{:S(2)}) copy-start(f32[2,96,5376]{2,1,0:T(8,128)} %param.38) | copy-start | bytes 12386308
Sparse Core Ops, SparseCore 0:
  92.1 53.8 all-gather.3
  147.6 50.7 all-gather.5
  200.1 23.8 all-gather.7
  291.1 34.5 reduce-scatter.4
  327.8 38.2 reduce-scatter.6
  368.8 44.8 reduce-scatter.8
  416.1 74.0 reduce-scatter.10

commit v15 on v14

--- a/solution.py
+++ b/solution.py
@@ -1861,7 +1861,7 @@
     )
 
 
-def mlp_forward(stream, attended, up, proj_out, vector):
+def mlp_forward(stream, attended, up, proj_out, vector, rides, collective_id):
     rows = stream.shape[0]
     width = up.shape[1]
     weight_specs, weights = mlp_specs(up, proj_out)
@@ -1885,6 +1885,8 @@
         ],
         "mlp_forward",
         work(2 * rows * D * (D + 2 * width), rows * (16 * D + 4 * width) + 2 * D * (D + 2 * width)),
+        rides,
+        collective_id,
     )
 
 
@@ -2231,10 +2233,10 @@
             )
             up = up_zero
         else:
-            attended, expo, inverse, output = attention_forward(qkv_rows, segment, [output_ride], 5)
-            up = up_one
-        residual, normed_second, active, slope, following = mlp_forward(
-            stream, attended, up, output, vector
+            attended, expo, inverse = attention_forward(qkv_rows, segment, (), 5)
+            up, output = up_one, output_one
+        residual, normed_second, active, slope, following, *fetched = mlp_forward(
+            stream, attended, up, output, vector, () if index else [output_ride], 5
         )
         saved_layers.append(
             (
@@ -2244,6 +2246,8 @@
             )
         )
         stream, qkv_weight = following, qkv_one
+        if fetched:
+            (output_one,) = fetched
     stream_grad, head_grad, final_sums, head_bias_grad, numbers = head(
         stream, segment, labels, head_full, global_vector, head_weight.shape[1]
     )
@@ -2263,24 +2267,26 @@
             output,
             vector,
             2 if index else 1,
-            [SumRide(by_owner(head_grad), False) if index else output_rest],
-            10 if index else 9,
+            () if index else [output_rest],
+            9,
         )
         if index:
-            *up_parts, head_sum = brought
-            attended_grad, *up_parts = lax.optimization_barrier((attended_grad, *up_parts))
+            attended_grad, *up_parts = lax.optimization_barrier((attended_grad, *brought))
             one_parts = [scatter(by_owner(part)) for part in up_parts]
         else:
             up_grad, output_one_sum = brought
             attended_grad, output_grad = lax.optimization_barrier((attended_grad, output_grad))
             output_zero_part = scatter(by_owner(output_grad))
-        qkv_grad, rest = attention_backward(
+        qkv_grad, rest, *head_sums = attention_backward(
             qkv_rows,
             expo,
             inverse,
             attended,
             attended_grad,
-            [LeadRide(by_owner(output_grad if index else up_grad))],
+            [
+                LeadRide(by_owner(output_grad if index else up_grad)),
+                *([SumRide(by_owner(head_grad), False)] if index else []),
+            ],
             6 if index else 8,
         )
         stream_grad, qkv_sums, qkv_weight_grad, *brought = qkv_backward(
@@ -2294,7 +2300,7 @@
             7,
         )
         if index:
-            output_rest = rest
+            output_rest, (head_sum,) = rest, head_sums
             stream_grad, qkv_weight_grad = lax.optimization_barrier((stream_grad, qkv_weight_grad))
             one_parts.append(scatter(by_owner(qkv_weight_grad)))
         else:

time: 627 us -> 633 us (level)
  Pallas kernels: 551 us -> 565 us
  waiting for transfers between devices: 10.3 us -> 2.07 us
    pallas_call x12, Pallas kernels: 370 us -> 385 us  [block_call(): pl.pallas_call(kernel, grid=(grid,), in_specs=in_specs, out_specs=out_spe...]
    reduce_scatter x4, waiting for transfers between devices: 8.29 us -> 0.06 us  [scatter(): return lax.psum_scatter(grad, 'fsdp', scatter_dimension=0)]
  transfers between devices with their start and end apart: 7 -> 7, of which waited for: 1 -> 0; matrix products, arithmetic and copies ran while one was open for 1% -> 1% of each run, Pallas kernels for 52% -> 56%
where the time goes in v15:
time: 633 us; the launch traced here: 624 us
  Pallas kernels  565 us (89%)
  other arithmetic  25.7 us (4%)
  local copies, waits for them, and re-layouts  15.3 us (2%)
  between operations  15.3 us (2%)
    pallas_call x12, Pallas kernels, block_call(): pl.pallas_call(kernel, grid=(grid,), in_specs=in_specs, out_specs=out_spe...  385 us
    pallas_call x1, Pallas kernels, reduce_call(): pl.pallas_call(functools.partial(reduce_kernel, whole=whole, partly=partl...  89 us
    pallas_call x1, Pallas kernels, begin(): pl.pallas_call(functools.partial(first_kernel, spots=spots), in_specs=[AN...  80.1 us
    sub x7, other arithmetic, adam_update(): return (moment, square, weight - learn_rate * step_dir)  21.5 us
  transfers between devices with their start and end apart: 7, of which 0 were waited for; matrix products, arithmetic and copies ran while one was open for 1% of the time, Pallas kernels for 56%

profile of v15, /device:TPU:0, one launch (start us, length us, event | category | flops | bytes accessed | tf_op | source)
XLA Modules:
  0.0 624.0 jit_solution(10876243649110539396)
XLA Ops:
  7.2 0.0 all-gather.4.cloned.1.call-start
  7.2 0.7 convert_element_type.23
  8.0 0.2 dynamic_update_slice.3
  8.2 0.6 reshape.122.refs_1_
  8.8 1.3 broadcast_in_dim.22.refs_9_
  10.2 1.7 copy.50.refs_6_.refs_3_.seg_col_ref
  11.9 80.1 %begin.1 = (f32[1024,768]{1,0:T(8,128)}, f32[64,1024]{1,0:T(8,128)}, f32[1,9984]{1,0:T(1,128)}, f32[1,9984]{1,0:T(1,128)}, bf16[8,96,2304]{2,1,0:T(8,128)(2,1)},...) custom-call(f32[384,768]{1,0:T(8,128)} %refs_0_.1, ...), custom_call_target="tpu_custom_call" | custom-call | tf_op jit(solution)/shard_map/begin/pallas_call | solution.py:832
  92.0 0.0 all-gather.6.cloned.1.call-start
  92.0 0.7 all-gather.6.cloned.1.call-update
  92.7 0.0 all-gather.8.cloned.1.call-start
  92.8 0.7 all-gather.8.cloned.1.call-update
  93.4 0.3 reduce-scatter.5.cloned.1.call-start
  93.8 34.1 %attention_forward.2 = (bf16[1024,768]{1,0:T(8,128)(2,1)}, bf16[12,1024,1024]{2,1,0:T(8,128)(2,1)}, f32[1024,768]{1,0:T(8,128)}, bf16[8,480,768]{2,1,0:T(8,128)(2,1)}, bf16[4,240,384]{2,1,0:T(8,128)(2,1)}) custom-call(bf16[1024,2304]{1,0:T(8,128)(2,1)} %get-tuple-element.108.refs_0_.refs_1_.refs_2_, ...), custom_call_target="tpu_custom_call" | custom-call | flops 12884901888 | bytes 34603008 | tf_op jit(solution)/shard_map/attention_forward/pallas_call | solution.py:594
  127.9 40.5 %mlp_forward.2 = (f32[1024,768]{1,0:T(8,128)}, bf16[1024,768]{1,0:T(8,128)(2,1)}, bf16[1024,3072]{1,0:T(8,128)(2,1)}, bf16[1024,3072]{1,0:T(8,128)(2,1)}, f32[10...) custom-call(f32[1024,768]{1,0:T(8,128)} %get-tuple-element.107.refs_0_.refs_2_, ...), custom_call_target="tpu_custom_call" | custom-call | flops 10871635968 | bytes 35782656 | tf_op jit(solution)/shard_map/mlp_forward/pallas_call | solution.py:594
  168.3 0.7 copy.54.label_ref
  169.0 0.6 broadcast_in_dim.24.vector_ref
  169.6 9.1 %qkv_forward.1 = (bf16[1024,768]{1,0:T(8,128)(2,1)}, bf16[1024,2304]{1,0:T(8,128)(2,1)}) custom-call(f32[1024,768]{1,0:T(8,128)} %get-tuple-element.117.stream_ref.stream_in, bf16[768,2304]{1,0:T(8,128)(2,1)} %all-gather.4.cloned.1.call-done.weight_ref, f32[1,9984]{1,0:T(1,128)} %get-tuple-element.119.vector_ref), custom_call_target="tpu_custom_call" | custom-call | flops 3623878656 | bytes 14548992 | tf_op jit(solution)/shard_map/qkv_forward/pallas_call | solution.py:594
  178.8 32.7 %attention_forward.3 = (bf16[1024,768]{1,0:T(8,128)(2,1)}, bf16[12,1024,1024]{2,1,0:T(8,128)(2,1)}, f32[1024,768]{1,0:T(8,128)}) custom-call(bf16[1024,2304]{1,0:T(8,128)(2,1)} %get-tuple-element.120.q_ref.k_ref.v_ref.refs_0_.refs_1_.refs_2_, bf16[1024,2304]{1,0:T(8,128)(2,1)} %get-tuple-element.120.q_ref.k_ref.v_ref.refs_0_.refs_1_.refs_2_, ...), custom_call_target="tpu_custom_call" | custom-call | flops 12884901888 | bytes 34603008 | tf_op jit(solution)/shard_map/attention_forward/pallas_call | solution.py:594
  211.5 21.1 %mlp_forward.3 = (f32[1024,768]{1,0:T(8,128)}, bf16[1024,768]{1,0:T(8,128)(2,1)}, bf16[1024,3072]{1,0:T(8,128)(2,1)}, bf16[1024,3072]{1,0:T(8,128)(2,1)}, f32[1024,768]{1,0:T(8,128)}) custom-call(f32[1024,768]{1,0:T(8,128)} %get-tuple-element.117.stream_ref.stream_in, bf16[1024,768]{1,0:T(8,128)(2,1)} %get-tuple-element.123.attended_ref.refs_5_, ...), custom_call_target="tpu_custom_call" | custom-call | flops 10871635968 | bytes 35782656 | tf_op jit(solution)/shard_map/mlp_forward/pallas_call | solution.py:594
  232.6 0.0 all-gather.8.cloned.1.call-done.weight_ref
  232.6 10.7 %head.1 = (f32[1024,768]{1,0:T(8,128)}, bf16[768,1024]{1,0:T(8,128)(2,1)}, f32[1,1536]{1,0:T(1,128)}, f32[1,1024]{1,0:T(1,128)}, f32[1,2]{1,0:T(1,128)}) custom-call(f32[1024,768]{1,0:T(8,128)} %get-tuple-element.126.stream_ref, s32[1024,1]{1,0:T(8,128)} %copy.50.refs_6_.refs_3_.seg_col_ref, s32[1,1024]{1,0:T(1,128)} %bitcast.71, s32[8,1]{1,0:T(8,128)} %copy.54.label_ref, ...), custom_call_target="tpu_custom_call" | custom-call | tf_op jit(solution)/shard_map/head/pallas_call | solution.py:2151
  243.3 36.3 %mlp_backward.2 = (f32[1024,768]{1,0:T(8,128)}, bf16[1024,768]{1,0:T(8,128)(2,1)}, f32[1,6144]{1,0:T(1,128)}, bf16[3840,768]{1,0:T(8,128)(2,1)}, bf16[768,1536]{1,0:T(8,128)(2,1)}, /*index=5*/bf16[768,1536]{1,0:T(8,128)(2,1)}) custom-call(f32[1024,768]{1,0:T(8,128)} %get-tuple-element.128.grad_ref, bf16[1024,3072]{1,0:T(8,128)(2,1)} %get-tuple-element.129.slope_ref, ...), custom_call_target="tpu_custom_call" | custom-call | tf_op jit(solution)/shard_map/mlp_backward/pallas_call | solution.py:594
  279.7 0.0 reduce-scatter.7.cloned.1.call-start
  279.7 0.5 reduce-scatter.7.cloned.1.call-update
  280.3 0.0 reduce-scatter.9.cloned.1.call-start
  280.3 61.0 %attention_backward.2 = (bf16[1024,2304]{1,0:T(8,128)(2,1)}, bf16[4,240,384]{2,1,0:T(8,128)(2,1)}, bf16[96,1024]{1,0:T(8,128)(2,1)}) custom-call(bf16[1024,2304]{1,0:T(8,128)(2,1)} %get-tuple-element.120.q_ref.k_ref.v_ref.refs_0_.refs_1_.refs_2_, bf16[1024,2304]{1,0:T(8,128)(2,1)} %get-tuple-element.120.q_ref.k_ref.v_ref.refs_0_.refs_1_.refs_2_, ...), custom_call_target="tpu_custom_call" | custom-call | tf_op jit(solution)/shard_map/attention_backward/pallas_call | solution.py:594
  341.3 15.3 %qkv_backward.2 = (f32[1024,768]{1,0:T(8,128)}, f32[1,3840]{1,0:T(1,128)}, bf16[768,2304]{1,0:T(8,128)(2,1)}) custom-call(bf16[1024,2304]{1,0:T(8,128)(2,1)} %get-tuple-element.140.grad_ref, f32[1024,768]{1,0:T(8,128)} %get-tuple-element.141.residual_in, f32[1024,768]{1,0:T(8,128)} %get-tuple-element.117.stream_ref.stream_in, ...), custom_call_target="tpu_custom_call" | custom-call | tf_op jit(solution)/shard_map/qkv_backward/pallas_call | solution.py:594
  356.6 0.0 reduce-scatter.11.cloned.1.call-start
  356.7 46.3 %mlp_backward.3 = (f32[1024,768]{1,0:T(8,128)}, bf16[1024,768]{1,0:T(8,128)(2,1)}, f32[1,6144]{1,0:T(1,128)}, bf16[3840,768]{1,0:T(8,128)(2,1)}, bf16[768,3072]{1,0:T(8,128)(2,1)}, /*index=5*/bf16[480,768]{1,0:T(8,128)(2,1)}) custom-call(f32[1024,768]{1,0:T(8,128)} %get-tuple-element.145.refs_0_, bf16[1024,3072]{1,0:T(8,128)(2,1)} %get-tuple-element.146.refs_1_, ...), custom_call_target="tpu_custom_call" | custom-call | tf_op jit(solution)/shard_map/mlp_backward/pallas_call | solution.py:594
  403.1 0.7 copy-done.29
  403.9 0.1 stack.28
  404.1 37.6 %attention_backward.3 = (bf16[1024,2304]{1,0:T(8,128)(2,1)}, bf16[4,48,1536]{2,1,0:T(8,128)(2,1)}) custom-call(bf16[1024,2304]{1,0:T(8,128)(2,1)} %get-tuple-element.108.refs_0_.refs_1_.refs_2_, bf16[1024,2304]{1,0:T(8,128)(2,1)} %get-tuple-element.108.refs_0_.refs_1_.refs_2_, bf16[1024,2304]{1,0:T(8,128)(2,1)} %get-tuple-element.108.refs_0_.refs_1_.refs_2_, ...), custom_call_target="tpu_custom_call" | custom-call | tf_op jit(solution)/shard_map/attention_backward/pallas_call | solution.py:594
  441.8 0.0 reduce-scatter.5.cloned.1.call-done
  441.8 0.0 reduce-scatter.7.cloned.1.call-done
  441.9 39.3 %qkv_backward.3 = (f32[1024,768]{1,0:T(8,128)}, f32[1,3840]{1,0:T(1,128)}, bf16[768,2304]{1,0:T(8,128)(2,1)}, bf16[96,3072]{1,0:T(8,128)(2,1)}, bf16[96,1536]{1,...) custom-call(bf16[1024,2304]{1,0:T(8,128)(2,1)} %get-tuple-element.158.refs_0_, ...), custom_call_target="tpu_custom_call" | custom-call | tf_op jit(solution)/shard_map/qkv_backward/pallas_call | solution.py:594
  481.2 0.7 slice_reduce_fusion.7
  481.9 0.7 slice_reduce_fusion.3
  482.7 0.1 stack.27
  482.8 0.1 maximum_bitcast_fusion.2
  482.9 0.1 reshape.136
  483.0 12.1 %embed_backward.1 = (bf16[3072,768]{1,0:T(8,128)(2,1)}, f32[64,768]{1,0:T(8,128)}, f32[1,768]{1,0:T(1,128)}) custom-call(bf16[1024,3072]{1,0:T(8,128)(2,1)} %pixel_ref.1, f32[1024,768]{1,0:T(8,128)} %get-tuple-element.171.grad_ref, f32[64,1024]{1,0:T(8,128)} %get-tuple-element.172.pos_ref), custom_call_target="tpu_custom_call" | custom-call | tf_op jit(solution)/shard_map/embed_backward/pallas_call | solution.py:594
  495.1 0.7 reduce.8
  495.8 0.9 slice.70
  496.8 0.1 concatenate.21
  497.0 0.7 pad.19.refs_8_
  497.8 89.0 %reduce_gradients.1 = (bf16[96,2304]{1,0:T(8,128)(2,1)}, bf16[384,768]{1,0:T(8,128)(2,1)}, f32[64,128]{1,0:T(8,128)}, bf16[480,768]{1,0:T(8,128)(2,1)}, f32[8,64,128]{2,1,0:T(8,128)}, /*index=5*/f32[1,128]{1,0:T(1,128)}) custom-call(bf16[96,1024]{1,0:T(8,128)(2,1)} %get-tuple-element.139.refs_0_, bf16[480,768]{1,0:T(8,128)(2,1)} %get-tuple-element.151.refs_1_, ...), custom_call_target="tpu_custom_call" | custom-call | tf_op jit(solution)/shard_map/reduce_gradients/pallas_call | solution.py:1488
  586.8 1.4 fusion.15
  588.2 0.7 slice_bitcast_fusion
  588.9 0.7 slice_multiply_fusion.2
  589.6 0.1 mul.216
  589.7 0.9 slice.79
  590.6 0.7 slice_multiply_fusion
  591.5 1.3 maximum_bitcast_fusion
  592.9 1.5 multiply_subtract_fusion.5
  594.3 1.9 multiply_subtract_fusion.3
  596.3 0.6 multiply_subtract_fusion.6
  596.9 0.9 multiply_subtract_fusion.4
  597.9 3.4 multiply_subtract_fusion.2
  601.2 0.1 copy-done.5
  601.4 0.6 copy-done.7
  602.0 0.2 copy-done.16
  602.2 6.4 %multiply_subtract_fusion.1 = (f32[2,480,768]{2,1,0:T(8,128)}, f32[2,480,768]{2,1,0:T(8,128)}, f32[2,480,768]{2,1,0:T(8,128)}) fusion(f32[2,480,768]{2,1,0:T(8,128)S(1)} %copy-done.1, f32[]{:T(128)} %bitcast.27, bf16[1,480,768]{2,1,0:T(8,128)(2,1)S(1)} %bitcast.57, bf16[1,480,768]{2,1,0:T(8,128)(2,1)S(1)} %bitcast.62, f32[2,480,768]{2,1,0:T(8,128)S(1)} %copy-done.5, ...), kind=kLoop, calls=%fused_computation.8 | loop fusion | flops 12533760 | bytes 19169284 | tf_op jit(solution)/shard_map/sub | solution.py:2175
  608.6 1.3 copy-done.4
  609.8 6.9 %multiply_subtract_fusion = (f32[2,96,5376]{2,1,0:T(8,128)}, f32[2,96,5376]{2,1,0:T(8,128)}, f32[2,96,5376]{2,1,0:T(8,128)}) fusion(f32[2,96,5376]{2,1,0:T(8,128)S(1)} %copy-done, f32[]{:T(128)} %bitcast.27, bf16[1,96,5376]{2,1,0:T(8,128)(2,1)S(1)} %get-tuple-element.216, bf16[1,96,5376]{2,1,0:T(8,128)(2,1)S(1)} %get-tuple-element.215, ...), kind=kLoop, calls=%fused_computation.5 | loop fusion | flops 17547264 | bytes 26836996 | tf_op jit(solution)/shard_map/sub | solution.py:2175
  (92 shorter events, 0.7 us)
Async XLA Ops:
  7.2 162.4 %all-gather.4.cloned.1.call-start = ((), (), s32[]{:S(2)}) async-start(), calls=%async_computation.4 | async-start | bytes 3981312 | tf_op jit(solution)/shard_map/all_gather | solution.py:2221
  92.0 119.5 %all-gather.6.cloned.1.call-start = ((), (), s32[]{:S(2)}) async-start(), calls=%async_computation.5 | async-start | bytes 5308416 | tf_op jit(solution)/shard_map/all_gather | solution.py:2221
  92.7 139.9 %all-gather.8.cloned.1.call-start = ((), (), s32[]{:S(2)}) async-start(), calls=%async_computation.6 | async-start | bytes 1769472 | tf_op jit(solution)/shard_map/all_gather | solution.py:2221
  93.4 348.4 %reduce-scatter.5.cloned.1.call-start = ((), (), s32[]{:S(2)}) async-start(), calls=%async_computation.7 | async-start | bytes 2654208 | tf_op jit(solution)/shard_map/reduce_scatter | solution.py:1549
  127.8 40.5 %copy-start.35 = (s32[1,8]{1,0:T(1,128)S(1)}, s32[1,8]{1,0:T(1,128)}, u32[]{:S(2)}) copy-start(s32[1,8]{1,0:T(1,128)} %param.28) | copy-start | bytes 100
  127.8 41.2 %copy-start.23 = (f32[3304]{0:T(1024)S(1)}, f32[3304]{0:T(1024)}, u32[]{:S(2)}) copy-start(f32[3304]{0:T(1024)} %param.35) | copy-start | bytes 39652
  279.7 162.2 %reduce-scatter.7.cloned.1.call-start = ((), (), s32[]{:S(2)}) async-start(), calls=%async_computation.8 | async-start | bytes 2654208 | tf_op jit(solution)/shard_map/reduce_scatter | solution.py:1549
  280.3 161.6 %reduce-scatter.9.cloned.1.call-start = ((), (), s32[]{:S(2)}) async-start(), calls=%async_computation.9 | async-start | bytes 3981312 | tf_op jit(solution)/shard_map/reduce_scatter | solution.py:1549
  356.6 141.1 %reduce-scatter.11.cloned.1.call-start = ((), (), s32[]{:S(2)}) async-start(), calls=%async_computation.10 | async-start | bytes 6635520 | tf_op jit(solution)/shard_map/reduce_scatter | solution.py:1549
  403.0 0.7 copy-start.29
  403.0 0.7 copy-start.25
  403.0 1.0 copy-start.32
  404.1 37.7 %copy-start.26 = (f32[1,6144]{1,0:T(1,128)S(1)}, f32[1,6144]{1,0:T(1,128)}, u32[]{:S(2)}) copy-start(f32[1,6144]{1,0:T(1,128)} %get-tuple-element.175) | copy-start | bytes 73732
  483.0 13.8 %copy-start.33 = (f32[1,1024]{1,0:T(1,128)S(1)}, f32[1,1024]{1,0:T(1,128)}, u32[]{:S(2)}) copy-start(f32[1,1024]{1,0:T(1,128)} %get-tuple-element.181) | copy-start | bytes 12292
  483.0 13.8 %copy-start.34 = (f32[1,2]{1,0:T(1,128)S(1)}, f32[1,2]{1,0:T(1,128)}, u32[]{:S(2)}) copy-start(f32[1,2]{1,0:T(1,128)} %get-tuple-element.182) | copy-start | bytes 28
  497.8 93.6 %copy-start.8 = (bf16[96,3072]{1,0:T(8,128)(2,1)S(1)}, bf16[96,3072]{1,0:T(8,128)(2,1)}, u32[]{:S(2)}) copy-start(bf16[96,3072]{1,0:T(8,128)(2,1)} %get-tuple-element.166.refs_2_) | copy-start | bytes 1769476
  497.8 93.6 %copy-start.9 = (bf16[96,2304]{1,0:T(8,128)(2,1)S(1)}, bf16[96,2304]{1,0:T(8,128)(2,1)}, u32[]{:S(2)}) copy-start(bf16[96,2304]{1,0:T(8,128)(2,1)} %get-tuple-element.169.refs_5_) | copy-start | bytes 1327108
  497.8 93.6 %copy-start.11 = (bf16[96,1536]{1,0:T(8,128)(2,1)S(1)}, bf16[96,1536]{1,0:T(8,128)(2,1)}, u32[]{:S(2)}) copy-start(bf16[96,1536]{1,0:T(8,128)(2,1)} %get-tuple-element.167.refs_3_) | copy-start | bytes 884740
  497.8 93.6 %copy-start.12 = (bf16[96,1536]{1,0:T(8,128)(2,1)S(1)}, bf16[96,1536]{1,0:T(8,128)(2,1)}, u32[]{:S(2)}) copy-start(bf16[96,1536]{1,0:T(8,128)(2,1)} %get-tuple-element.168.refs_4_) | copy-start | bytes 884740
  586.7 6.1 copy-start.27
  586.8 6.1 copy-start.28
  586.8 7.6 %copy-start.10 = (f32[96,1000]{1,0:T(8,128)S(1)}, f32[96,1000]{1,0:T(8,128)}, u32[]{:S(2)}) copy-start(f32[96,1000]{1,0:T(8,128)} %refs_4_.1) | copy-start | bytes 1152004
  586.8 7.6 %copy-start.15 = (bf16[96,1024]{1,0:T(8,128)(2,1)S(1)}, bf16[96,1024]{1,0:T(8,128)(2,1)}, u32[]{:S(2)}) copy-start(bf16[96,1024]{1,0:T(8,128)(2,1)} %get-tuple-element.139.refs_0_) | copy-start | bytes 589828
  586.8 7.5 %copy-start.19 = (f32[96,1000]{1,0:T(8,128)S(1)}, f32[96,1000]{1,0:T(8,128)}, u32[]{:S(2)}) copy-start(f32[96,1000]{1,0:T(8,128)} %param.44) | copy-start | bytes 1152004
  586.8 7.5 %copy-start.20 = (f32[96,1000]{1,0:T(8,128)S(1)}, f32[96,1000]{1,0:T(8,128)}, u32[]{:S(2)}) copy-start(f32[96,1000]{1,0:T(8,128)} %param.37) | copy-start | bytes 1152004
  591.4 4.8 copy-start.24
  591.4 4.8 copy-start.30
  591.4 4.8 copy-start.31
  591.5 5.5 copy-start.17
  591.5 5.5 copy-start.21
  591.5 5.4 copy-start.22
  591.5 6.3 %copy-start.18 = (bf16[384,768]{1,0:T(8,128)(2,1)S(1)}, bf16[384,768]{1,0:T(8,128)(2,1)}, u32[]{:S(2)}) copy-start(bf16[384,768]{1,0:T(8,128)(2,1)} %get-tuple-element.185) | copy-start | bytes 1769476
  591.5 9.7 %copy-start.6 = (f32[2,480,768]{2,1,0:T(8,128)S(1)}, f32[2,480,768]{2,1,0:T(8,128)}, u32[]{:S(2)}) copy-start(f32[2,480,768]{2,1,0:T(8,128)} %param.39) | copy-start | bytes 8847364
  592.8 5.0 copy-start.2
  592.8 5.0 copy-start.13
  592.9 4.9 copy-start.14
  597.8 3.4 copy-start.1
  597.8 3.5 copy-start.5
  597.8 4.1 copy-start.7
  597.8 4.3 copy-start.16
  602.2 6.4 %copy-start = (f32[2,96,5376]{2,1,0:T(8,128)S(1)}, f32[2,96,5376]{2,1,0:T(8,128)}, u32[]{:S(2)}) copy-start(f32[2,96,5376]{2,1,0:T(8,128)} %refs_2_.1) | copy-start | bytes 12386308
  602.2 6.4 %copy-start.3 = (f32[2,96,5376]{2,1,0:T(8,128)S(1)}, f32[2,96,5376]{2,1,0:T(8,128)}, u32[]{:S(2)}) copy-start(f32[2,96,5376]{2,1,0:T(8,128)} %param.45) | copy-start | bytes 12386308
  602.2 7.7 %copy-start.4 = (f32[2,96,5376]{2,1,0:T(8,128)S(1)}, f32[2,96,5376]{2,1,0:T(8,128)}, u32[]{:S(2)}) copy-start(f32[2,96,5376]{2,1,0:T(8,128)} %param.38) | copy-start | bytes 12386308
Sparse Core Ops, SparseCore 0:
  92.1 54.5 all-gather.3
  148.3 50.0 all-gather.5
  200.1 23.8 all-gather.7
  279.8 38.2 reduce-scatter.4
  320.9 35.4 reduce-scatter.6
  359.1 53.1 reduce-scatter.8
  414.7 77.3 reduce-scatter.10

commit v16 on v14

--- a/solution.py
+++ b/solution.py
@@ -2263,15 +2263,14 @@
             output,
             vector,
             2 if index else 1,
-            [SumRide(by_owner(head_grad), False) if index else output_rest],
-            10 if index else 9,
+            () if index else [output_rest, SumRide(by_owner(head_grad), False)],
+            9,
         )
         if index:
-            *up_parts, head_sum = brought
-            attended_grad, *up_parts = lax.optimization_barrier((attended_grad, *up_parts))
+            attended_grad, *up_parts = lax.optimization_barrier((attended_grad, *brought))
             one_parts = [scatter(by_owner(part)) for part in up_parts]
         else:
-            up_grad, output_one_sum = brought
+            up_grad, output_one_sum, head_sum = brought
             attended_grad, output_grad = lax.optimization_barrier((attended_grad, output_grad))
             output_zero_part = scatter(by_owner(output_grad))
         qkv_grad, rest = attention_backward(

time: 627 us -> 619 us (0.987)
  transfers between devices with their start and end apart: 7 -> 7, of which waited for: 1 -> 1; matrix products, arithmetic and copies ran while one was open for 1% -> 1% of each run, Pallas kernels for 52% -> 54%
where the time goes in v16:
time: 619 us; the launch traced here: 610 us
  Pallas kernels  549 us (89%)
  other arithmetic  25.7 us (4%)
  local copies, waits for them, and re-layouts  15.3 us (2%)
  between operations  15.3 us (2%)
    pallas_call x12, Pallas kernels, block_call(): pl.pallas_call(kernel, grid=(grid,), in_specs=in_specs, out_specs=out_spe...  368 us
    pallas_call x1, Pallas kernels, reduce_call(): pl.pallas_call(functools.partial(reduce_kernel, whole=whole, partly=partl...  90.6 us
    pallas_call x1, Pallas kernels, begin(): pl.pallas_call(functools.partial(first_kernel, spots=spots), in_specs=[AN...  80.1 us
    sub x7, other arithmetic, adam_update(): return (moment, square, weight - learn_rate * step_dir)  21.5 us
  transfers between devices with their start and end apart: 7, of which 1 were waited for; matrix products, arithmetic and copies ran while one was open for 1% of the time, Pallas kernels for 54%

profile of v16, /device:TPU:0, one launch (start us, length us, event | category | flops | bytes accessed | tf_op | source)
XLA Modules:
  0.0 610.1 jit_solution(12798676831916447134)
XLA Ops:
  7.2 0.0 all-gather.4.cloned.1.call-start
  7.2 0.7 convert_element_type.23
  8.0 0.2 dynamic_update_slice.3
  8.2 0.6 reshape.122.refs_1_
  8.8 1.3 broadcast_in_dim.22.refs_9_
  10.2 1.7 copy.50.refs_6_.refs_3_.seg_col_ref
  11.9 80.1 %begin.1 = (f32[1024,768]{1,0:T(8,128)}, f32[64,1024]{1,0:T(8,128)}, f32[1,9984]{1,0:T(1,128)}, f32[1,9984]{1,0:T(1,128)}, bf16[8,96,2304]{2,1,0:T(8,128)(2,1)},...) custom-call(f32[384,768]{1,0:T(8,128)} %refs_0_.1, ...), custom_call_target="tpu_custom_call" | custom-call | tf_op jit(solution)/shard_map/begin/pallas_call | solution.py:832
  92.0 0.0 all-gather.6.cloned.1.call-start
  92.0 0.7 all-gather.6.cloned.1.call-update
  92.7 0.0 all-gather.8.cloned.1.call-start
  92.8 0.7 all-gather.8.cloned.1.call-update
  93.5 0.3 reduce-scatter.5.cloned.1.call-start
  93.8 34.1 %attention_forward.2 = (bf16[1024,768]{1,0:T(8,128)(2,1)}, bf16[12,1024,1024]{2,1,0:T(8,128)(2,1)}, f32[1024,768]{1,0:T(8,128)}, bf16[8,480,768]{2,1,0:T(8,128)(2,1)}, bf16[4,240,384]{2,1,0:T(8,128)(2,1)}) custom-call(bf16[1024,2304]{1,0:T(8,128)(2,1)} %get-tuple-element.108.refs_0_.refs_1_.refs_2_, ...), custom_call_target="tpu_custom_call" | custom-call | flops 12884901888 | bytes 34603008 | tf_op jit(solution)/shard_map/attention_forward/pallas_call | solution.py:594
  127.9 21.0 %mlp_forward.2 = (f32[1024,768]{1,0:T(8,128)}, bf16[1024,768]{1,0:T(8,128)(2,1)}, bf16[1024,3072]{1,0:T(8,128)(2,1)}, bf16[1024,3072]{1,0:T(8,128)(2,1)}, f32[1024,768]{1,0:T(8,128)}) custom-call(f32[1024,768]{1,0:T(8,128)} %get-tuple-element.107.stream_ref.refs_2_, bf16[1024,768]{1,0:T(8,128)(2,1)} %get-tuple-element.112.attended_ref.refs_5_, ...), custom_call_target="tpu_custom_call" | custom-call | flops 10871635968 | bytes 35782656 | tf_op jit(solution)/shard_map/mlp_forward/pallas_call | solution.py:594
  148.9 0.7 copy.54.label_ref
  149.6 0.6 broadcast_in_dim.24.vector_ref
  150.2 9.1 %qkv_forward.1 = (bf16[1024,768]{1,0:T(8,128)(2,1)}, bf16[1024,2304]{1,0:T(8,128)(2,1)}) custom-call(f32[1024,768]{1,0:T(8,128)} %get-tuple-element.116.stream_ref.stream_in, bf16[768,2304]{1,0:T(8,128)(2,1)} %all-gather.4.cloned.1.call-done.weight_ref, f32[1,9984]{1,0:T(1,128)} %get-tuple-element.118.vector_ref), custom_call_target="tpu_custom_call" | custom-call | flops 3623878656 | bytes 14548992 | tf_op jit(solution)/shard_map/qkv_forward/pallas_call | solution.py:594
  159.4 50.9 %attention_forward.3 = (bf16[1024,768]{1,0:T(8,128)(2,1)}, bf16[12,1024,1024]{2,1,0:T(8,128)(2,1)}, f32[1024,768]{1,0:T(8,128)}, bf16[8,480,768]{2,1,0:T(8,128)(2,1)}) custom-call(bf16[1024,2304]{1,0:T(8,128)(2,1)} %get-tuple-element.119.refs_0_.refs_1_.refs_2_, bf16[1024,2304]{1,0:T(8,128)(2,1)} %get-tuple-element.119.refs_0_.refs_1_.refs_2_, ...), custom_call_target="tpu_custom_call" | custom-call | flops 12884901888 | bytes 34603008 | tf_op jit(solution)/shard_map/attention_forward/pallas_call | solution.py:594
  210.3 0.0 all-gather.6.cloned.1.call-done.up_ref
  210.3 21.1 %mlp_forward.3 = (f32[1024,768]{1,0:T(8,128)}, bf16[1024,768]{1,0:T(8,128)(2,1)}, bf16[1024,3072]{1,0:T(8,128)(2,1)}, bf16[1024,3072]{1,0:T(8,128)(2,1)}, f32[1024,768]{1,0:T(8,128)}) custom-call(f32[1024,768]{1,0:T(8,128)} %get-tuple-element.116.stream_ref.stream_in, bf16[1024,768]{1,0:T(8,128)(2,1)} %get-tuple-element.123.attended_ref.refs_5_, ...), custom_call_target="tpu_custom_call" | custom-call | flops 10871635968 | bytes 35782656 | tf_op jit(solution)/shard_map/mlp_forward/pallas_call | solution.py:594
  231.4 0.0 all-gather.8.cloned.1.call-done.weight_ref
  231.5 10.7 %head.1 = (f32[1024,768]{1,0:T(8,128)}, bf16[768,1024]{1,0:T(8,128)(2,1)}, f32[1,1536]{1,0:T(1,128)}, f32[1,1024]{1,0:T(1,128)}, f32[1,2]{1,0:T(1,128)}) custom-call(f32[1024,768]{1,0:T(8,128)} %get-tuple-element.126.stream_ref, s32[1024,1]{1,0:T(8,128)} %copy.50.refs_6_.refs_3_.seg_col_ref, s32[1,1024]{1,0:T(1,128)} %bitcast.71, s32[8,1]{1,0:T(8,128)} %copy.54.label_ref, ...), custom_call_target="tpu_custom_call" | custom-call | tf_op jit(solution)/shard_map/head/pallas_call | solution.py:2149
  242.2 36.2 %mlp_backward.2 = (f32[1024,768]{1,0:T(8,128)}, bf16[1024,768]{1,0:T(8,128)(2,1)}, f32[1,6144]{1,0:T(1,128)}, bf16[3840,768]{1,0:T(8,128)(2,1)}, bf16[768,1536]{1,0:T(8,128)(2,1)}, /*index=5*/bf16[768,1536]{1,0:T(8,128)(2,1)}) custom-call(f32[1024,768]{1,0:T(8,128)} %get-tuple-element.128.grad_ref, bf16[1024,3072]{1,0:T(8,128)(2,1)} %get-tuple-element.129.slope_ref, ...), custom_call_target="tpu_custom_call" | custom-call | tf_op jit(solution)/shard_map/mlp_backward/pallas_call | solution.py:594
  278.4 0.0 reduce-scatter.7.cloned.1.call-start
  278.4 0.5 reduce-scatter.7.cloned.1.call-update
  279.0 0.0 reduce-scatter.9.cloned.1.call-start
  279.0 43.9 %attention_backward.2 = (bf16[1024,2304]{1,0:T(8,128)(2,1)}, bf16[4,240,384]{2,1,0:T(8,128)(2,1)}) custom-call(bf16[1024,2304]{1,0:T(8,128)(2,1)} %get-tuple-element.119.refs_0_.refs_1_.refs_2_, bf16[1024,2304]{1,0:T(8,128)(2,1)} %get-tuple-element.119.refs_0_.refs_1_.refs_2_, bf16[1024,2304]{1,0:T(8,128)(2,1)} %get-tuple-element.119.refs_0_.refs_1_.refs_2_, ...), custom_call_target="tpu_custom_call" | custom-call | tf_op jit(solution)/shard_map/attention_backward/pallas_call | solution.py:594
  322.9 15.4 %qkv_backward.2 = (f32[1024,768]{1,0:T(8,128)}, f32[1,3840]{1,0:T(1,128)}, bf16[768,2304]{1,0:T(8,128)(2,1)}) custom-call(bf16[1024,2304]{1,0:T(8,128)(2,1)} %get-tuple-element.138.grad_ref, f32[1024,768]{1,0:T(8,128)} %get-tuple-element.139.residual_in, f32[1024,768]{1,0:T(8,128)} %get-tuple-element.116.stream_ref.stream_in, ...), custom_call_target="tpu_custom_call" | custom-call | tf_op jit(solution)/shard_map/qkv_backward/pallas_call | solution.py:594
  338.3 0.0 reduce-scatter.11.cloned.1.call-start
  338.4 47.8 %mlp_backward.3 = (f32[1024,768]{1,0:T(8,128)}, bf16[1024,768]{1,0:T(8,128)(2,1)}, f32[1,6144]{1,0:T(1,128)}, bf16[3840,768]{1,0:T(8,128)(2,1)}, bf16[768,3072]{...) custom-call(f32[1024,768]{1,0:T(8,128)} %get-tuple-element.143.refs_0_, ...), custom_call_target="tpu_custom_call" | custom-call | tf_op jit(solution)/shard_map/mlp_backward/pallas_call | solution.py:594
  386.2 0.7 copy-done.29
  387.1 0.1 stack.28
  387.2 36.8 %attention_backward.3 = (bf16[1024,2304]{1,0:T(8,128)(2,1)}, bf16[4,48,1536]{2,1,0:T(8,128)(2,1)}) custom-call(bf16[1024,2304]{1,0:T(8,128)(2,1)} %get-tuple-element.108.refs_0_.refs_1_.refs_2_, bf16[1024,2304]{1,0:T(8,128)(2,1)} %get-tuple-element.108.refs_0_.refs_1_.refs_2_, bf16[1024,2304]{1,0:T(8,128)(2,1)} %get-tuple-element.108.refs_0_.refs_1_.refs_2_, ...), custom_call_target="tpu_custom_call" | custom-call | tf_op jit(solution)/shard_map/attention_backward/pallas_call | solution.py:594
  424.2 39.1 %qkv_backward.3 = (f32[1024,768]{1,0:T(8,128)}, f32[1,3840]{1,0:T(1,128)}, bf16[768,2304]{1,0:T(8,128)(2,1)}, bf16[96,3072]{1,0:T(8,128)(2,1)}, bf16[96,1536]{1,...) custom-call(bf16[1024,2304]{1,0:T(8,128)(2,1)} %get-tuple-element.158.refs_0_, ...), custom_call_target="tpu_custom_call" | custom-call | tf_op jit(solution)/shard_map/qkv_backward/pallas_call | solution.py:594
  463.3 0.7 slice_reduce_fusion.7
  464.0 0.7 slice_reduce_fusion.3
  464.8 0.1 stack.27
  464.9 0.1 maximum_bitcast_fusion.2
  465.0 0.1 reshape.136
  465.1 12.2 %embed_backward.1 = (bf16[3072,768]{1,0:T(8,128)(2,1)}, f32[64,768]{1,0:T(8,128)}, f32[1,768]{1,0:T(1,128)}) custom-call(bf16[1024,3072]{1,0:T(8,128)(2,1)} %pixel_ref.1, f32[1024,768]{1,0:T(8,128)} %get-tuple-element.171.grad_ref, f32[64,1024]{1,0:T(8,128)} %get-tuple-element.172.pos_ref), custom_call_target="tpu_custom_call" | custom-call | tf_op jit(solution)/shard_map/embed_backward/pallas_call | solution.py:594
  477.3 0.7 reduce.8
  478.0 0.9 slice.70
  479.0 0.1 concatenate.21
  479.2 0.7 pad.19.refs_8_
  479.9 2.3 reduce-scatter.11.cloned.1.call-done
  482.3 90.6 %reduce_gradients.1 = (bf16[96,2304]{1,0:T(8,128)(2,1)}, bf16[384,768]{1,0:T(8,128)(2,1)}, f32[64,128]{1,0:T(8,128)}, bf16[480,768]{1,0:T(8,128)(2,1)}, f32[8,64,128]{2,1,0:T(8,128)}, /*index=5*/f32[1,128]{1,0:T(1,128)}) custom-call(bf16[96,1024]{1,0:T(8,128)(2,1)} %get-tuple-element.150.refs_0_, bf16[480,768]{1,0:T(8,128)(2,1)} %get-tuple-element.151.refs_1_, ...), custom_call_target="tpu_custom_call" | custom-call | tf_op jit(solution)/shard_map/reduce_gradients/pallas_call | solution.py:1488
  572.9 1.4 fusion.15
  574.3 0.7 slice_bitcast_fusion
  575.0 0.7 slice_multiply_fusion.2
  575.7 0.1 mul.216
  575.8 0.9 slice.79
  576.7 0.7 slice_multiply_fusion
  577.6 1.3 maximum_bitcast_fusion
  579.0 1.5 multiply_subtract_fusion.5
  580.4 1.9 multiply_subtract_fusion.3
  582.3 0.6 multiply_subtract_fusion.6
  583.0 0.9 multiply_subtract_fusion.4
  583.9 3.4 multiply_subtract_fusion.2
  587.3 0.1 copy-done.5
  587.4 0.6 copy-done.7
  588.0 0.2 copy-done.16
  588.3 6.4 %multiply_subtract_fusion.1 = (f32[2,480,768]{2,1,0:T(8,128)}, f32[2,480,768]{2,1,0:T(8,128)}, f32[2,480,768]{2,1,0:T(8,128)}) fusion(f32[2,480,768]{2,1,0:T(8,128)S(1)} %copy-done.1, f32[]{:T(128)} %bitcast.27, bf16[1,480,768]{2,1,0:T(8,128)(2,1)S(1)} %bitcast.57, bf16[1,480,768]{2,1,0:T(8,128)(2,1)S(1)} %bitcast.62, f32[2,480,768]{2,1,0:T(8,128)S(1)} %copy-done.5, ...), kind=kLoop, calls=%fused_computation.8 | loop fusion | flops 12533760 | bytes 19169284 | tf_op jit(solution)/shard_map/sub | solution.py:2173
  594.6 1.3 copy-done.4
  595.9 6.9 %multiply_subtract_fusion = (f32[2,96,5376]{2,1,0:T(8,128)}, f32[2,96,5376]{2,1,0:T(8,128)}, f32[2,96,5376]{2,1,0:T(8,128)}) fusion(f32[2,96,5376]{2,1,0:T(8,128)S(1)} %copy-done, f32[]{:T(128)} %bitcast.27, bf16[1,96,5376]{2,1,0:T(8,128)(2,1)S(1)} %get-tuple-element.216, bf16[1,96,5376]{2,1,0:T(8,128)(2,1)S(1)} %get-tuple-element.215, ...), kind=kLoop, calls=%fused_computation.5 | loop fusion | flops 17547264 | bytes 26836996 | tf_op jit(solution)/shard_map/sub | solution.py:2173
  (92 shorter events, 0.7 us)
Async XLA Ops:
  7.2 143.0 %all-gather.4.cloned.1.call-start = ((), (), s32[]{:S(2)}) async-start(), calls=%async_computation.4 | async-start | bytes 3981312 | tf_op jit(solution)/shard_map/all_gather | solution.py:2219
  92.0 118.3 %all-gather.6.cloned.1.call-start = ((), (), s32[]{:S(2)}) async-start(), calls=%async_computation.5 | async-start | bytes 5308416 | tf_op jit(solution)/shard_map/all_gather | solution.py:2219
  92.7 138.7 %all-gather.8.cloned.1.call-start = ((), (), s32[]{:S(2)}) async-start(), calls=%async_computation.6 | async-start | bytes 1769472 | tf_op jit(solution)/shard_map/all_gather | solution.py:2219
  93.5 330.6 %reduce-scatter.5.cloned.1.call-start = ((), (), s32[]{:S(2)}) async-start(), calls=%async_computation.7 | async-start | bytes 2654208 | tf_op jit(solution)/shard_map/reduce_scatter | solution.py:1549
  127.9 21.1 %copy-start.35 = (s32[1,8]{1,0:T(1,128)S(1)}, s32[1,8]{1,0:T(1,128)}, u32[]{:S(2)}) copy-start(s32[1,8]{1,0:T(1,128)} %param.28) | copy-start | bytes 100
  127.9 21.7 %copy-start.23 = (f32[3304]{0:T(1024)S(1)}, f32[3304]{0:T(1024)}, u32[]{:S(2)}) copy-start(f32[3304]{0:T(1024)} %param.35) | copy-start | bytes 39652
  278.4 145.8 %reduce-scatter.7.cloned.1.call-start = ((), (), s32[]{:S(2)}) async-start(), calls=%async_computation.8 | async-start | bytes 2654208 | tf_op jit(solution)/shard_map/reduce_scatter | solution.py:1549
  279.0 145.2 %reduce-scatter.9.cloned.1.call-start = ((), (), s32[]{:S(2)}) async-start(), calls=%async_computation.9 | async-start | bytes 3981312 | tf_op jit(solution)/shard_map/reduce_scatter | solution.py:1549
  338.3 143.9 %reduce-scatter.11.cloned.1.call-start = ((), (), s32[]{:S(2)}) async-start(), calls=%async_computation.10 | async-start | bytes 6635520 | tf_op jit(solution)/shard_map/reduce_scatter | solution.py:1549
  386.2 0.7 copy-start.29
  386.2 0.7 copy-start.25
  386.2 1.0 copy-start.32
  387.2 36.8 %copy-start.26 = (f32[1,6144]{1,0:T(1,128)S(1)}, f32[1,6144]{1,0:T(1,128)}, u32[]{:S(2)}) copy-start(f32[1,6144]{1,0:T(1,128)} %get-tuple-element.175) | copy-start | bytes 73732
  465.1 13.9 %copy-start.33 = (f32[1,1024]{1,0:T(1,128)S(1)}, f32[1,1024]{1,0:T(1,128)}, u32[]{:S(2)}) copy-start(f32[1,1024]{1,0:T(1,128)} %get-tuple-element.181) | copy-start | bytes 12292
  465.1 13.9 %copy-start.34 = (f32[1,2]{1,0:T(1,128)S(1)}, f32[1,2]{1,0:T(1,128)}, u32[]{:S(2)}) copy-start(f32[1,2]{1,0:T(1,128)} %get-tuple-element.182) | copy-start | bytes 28
  482.2 95.2 %copy-start.8 = (bf16[96,3072]{1,0:T(8,128)(2,1)S(1)}, bf16[96,3072]{1,0:T(8,128)(2,1)}, u32[]{:S(2)}) copy-start(bf16[96,3072]{1,0:T(8,128)(2,1)} %get-tuple-element.166.refs_2_) | copy-start | bytes 1769476
  482.2 95.2 %copy-start.9 = (bf16[96,2304]{1,0:T(8,128)(2,1)S(1)}, bf16[96,2304]{1,0:T(8,128)(2,1)}, u32[]{:S(2)}) copy-start(bf16[96,2304]{1,0:T(8,128)(2,1)} %get-tuple-element.169.refs_5_) | copy-start | bytes 1327108
  482.2 95.2 %copy-start.11 = (bf16[96,1536]{1,0:T(8,128)(2,1)S(1)}, bf16[96,1536]{1,0:T(8,128)(2,1)}, u32[]{:S(2)}) copy-start(bf16[96,1536]{1,0:T(8,128)(2,1)} %get-tuple-element.167.refs_3_) | copy-start | bytes 884740
  482.3 95.2 %copy-start.12 = (bf16[96,1536]{1,0:T(8,128)(2,1)S(1)}, bf16[96,1536]{1,0:T(8,128)(2,1)}, u32[]{:S(2)}) copy-start(bf16[96,1536]{1,0:T(8,128)(2,1)} %get-tuple-element.168.refs_4_) | copy-start | bytes 884740
  572.8 6.1 copy-start.27
  572.8 6.1 copy-start.28
  572.8 7.6 %copy-start.10 = (f32[96,1000]{1,0:T(8,128)S(1)}, f32[96,1000]{1,0:T(8,128)}, u32[]{:S(2)}) copy-start(f32[96,1000]{1,0:T(8,128)} %refs_4_.1) | copy-start | bytes 1152004
  572.9 7.6 %copy-start.15 = (bf16[96,1024]{1,0:T(8,128)(2,1)S(1)}, bf16[96,1024]{1,0:T(8,128)(2,1)}, u32[]{:S(2)}) copy-start(bf16[96,1024]{1,0:T(8,128)(2,1)} %get-tuple-element.150.refs_0_) | copy-start | bytes 589828
  572.9 7.5 %copy-start.19 = (f32[96,1000]{1,0:T(8,128)S(1)}, f32[96,1000]{1,0:T(8,128)}, u32[]{:S(2)}) copy-start(f32[96,1000]{1,0:T(8,128)} %param.44) | copy-start | bytes 1152004
  572.9 7.5 %copy-start.20 = (f32[96,1000]{1,0:T(8,128)S(1)}, f32[96,1000]{1,0:T(8,128)}, u32[]{:S(2)}) copy-start(f32[96,1000]{1,0:T(8,128)} %param.37) | copy-start | bytes 1152004
  577.5 4.8 copy-start.24
  577.5 4.8 copy-start.30
  577.5 4.8 copy-start.31
  577.5 5.5 copy-start.17
  577.5 5.5 copy-start.21
  577.6 5.4 copy-start.22
  577.6 6.3 %copy-start.18 = (bf16[384,768]{1,0:T(8,128)(2,1)S(1)}, bf16[384,768]{1,0:T(8,128)(2,1)}, u32[]{:S(2)}) copy-start(bf16[384,768]{1,0:T(8,128)(2,1)} %get-tuple-element.185) | copy-start | bytes 1769476
  577.6 9.7 %copy-start.6 = (f32[2,480,768]{2,1,0:T(8,128)S(1)}, f32[2,480,768]{2,1,0:T(8,128)}, u32[]{:S(2)}) copy-start(f32[2,480,768]{2,1,0:T(8,128)} %param.39) | copy-start | bytes 8847364
  578.9 5.0 copy-start.2
  578.9 5.0 copy-start.13
  578.9 4.9 copy-start.14
  583.9 3.4 copy-start.1
  583.9 3.5 copy-start.5
  583.9 4.1 copy-start.7
  583.9 4.3 copy-start.16
  588.3 6.4 %copy-start = (f32[2,96,5376]{2,1,0:T(8,128)S(1)}, f32[2,96,5376]{2,1,0:T(8,128)}, u32[]{:S(2)}) copy-start(f32[2,96,5376]{2,1,0:T(8,128)} %refs_2_.1) | copy-start | bytes 12386308
  588.3 6.4 %copy-start.3 = (f32[2,96,5376]{2,1,0:T(8,128)S(1)}, f32[2,96,5376]{2,1,0:T(8,128)}, u32[]{:S(2)}) copy-start(f32[2,96,5376]{2,1,0:T(8,128)} %param.45) | copy-start | bytes 12386308
  588.3 7.7 %copy-start.4 = (f32[2,96,5376]{2,1,0:T(8,128)S(1)}, f32[2,96,5376]{2,1,0:T(8,128)}, u32[]{:S(2)}) copy-start(f32[2,96,5376]{2,1,0:T(8,128)} %param.38) | copy-start | bytes 12386308
Sparse Core Ops, SparseCore 0:
  92.1 53.8 all-gather.3
  147.7 51.3 all-gather.5
  200.7 23.2 all-gather.7
  278.5 37.9 reduce-scatter.4
  319.2 38.8 reduce-scatter.6
  360.9 44.6 reduce-scatter.8
  408.0 74.1 reduce-scatter.10
